TPU v7x, 32 devices: a whole 2x2x4 slice. The times are simulated.
32 devices in a mesh: groups: 2 (over y), patient: 4 (over x, core), feature: 4 (over z).
Axes of the slice: x: 2, y: 2, z: 4, core: 2. Of those that a mesh axis runs over, the one named last changes fastest.
Arguments:
- visits: bfloat16 [256, 256, 4096], P(('groups', 'patient'), None, 'feature'), parts along dimension 0, may hold values from -6 to 6
- visit_counts: int32 [256], P(('groups', 'patient')), parts along dimension 0, may hold values from 16 to 256, as said below
- h_start: float32 [64, 64], replicated, may hold values from -0.75 to 0.75
- v_start: bfloat16 [4096, 64], P('feature'), may hold values from -0.09375 to 0.09375
- w_start: float32 [256, 64], P(('groups', 'patient')), parts along dimension 0, may hold values from -5 to 5
Outputs:
- h_next: float32 [64, 128], P(None, 'groups'), parts along dimension 1
- v_next: float32 [4096, 128], P('feature', 'groups'), parts along dimension 1
- w_next: float32 [128, 128], P('patient', 'groups'), parts along dimension 1
There are 2 independent parts, one for each index of `groups`. A program takes and returns all parts, laid end to end along the dimension named above; an argument that names none is the same for every part. Nothing has to cross between parts.
Inputs may be any that keep to these rules, and one draw needn't show every extreme that they name: `visit_counts`: in each block of 32 patients that lie on one index of patient, one patient has exactly 256 visits.
All inputs are finite; a program needn't handle non-finite values.
Results may differ from a plain program's by a relative error of at most 0.0015.
Values may be sent and summed in bfloat16 or wider, within the bound.
No kernel may reach another device: no remote copies, remote signals or barrier semaphores. Data moves between devices by JAX's collectives and lax.ppermute only.
A program may use at most 128 MiB of HBM per device.

v0:
```python
import jax
import jax.numpy as jnp
from jax import lax
from jax.sharding import PartitionSpec as P

NS_STEPS = 12


epsilon = 1e-06
HIGH = lax.Precision.HIGHEST


def project(piece, v_start):
    return jnp.einsum("kmj,jr->krm", piece, v_start, preferred_element_type=jnp.float32)


def polar_factor(proj, weights, counts, h_start):
    slots = jnp.arange(proj.shape[2], dtype=jnp.int32)
    keep = (slots[None, :] < counts[:, None]).astype(jnp.float32)
    mixed = (
        jnp.einsum("rc,kcm->krm", h_start, proj * weights[:, :, None], precision=HIGH)
        * keep[:, None, :]
    )
    scale = lax.rsqrt(jnp.sum(mixed * mixed, axis=(1, 2)) + epsilon)
    frames = mixed * scale[:, None, None]

    def sweep(step, frames):
        gram = jnp.einsum("krm,ksm->krs", frames, frames, precision=HIGH)
        return 1.5 * frames - 0.5 * jnp.einsum("ksr,ksm->krm", gram, frames, precision=HIGH)

    frames = lax.fori_loop(0, NS_STEPS, sweep, frames)
    return frames.astype(jnp.bfloat16)


def solve_right(terms, gram):
    lower = jnp.linalg.cholesky(gram)
    first = lax.linalg.triangular_solve(lower, terms.T, left_side=True, lower=True)
    second = lax.linalg.triangular_solve(lower, first, left_side=True, lower=True, transpose_a=True)
    return second.T


def on_device(visits, visit_counts, h_start, v_start, w_start):
    share = visits.shape[0] // lax.axis_size("feature")
    proj = lax.psum_scatter(project(visits, v_start), "feature", scatter_dimension=0, tiled=True)
    first_row = lax.axis_index("feature") * share
    weights = lax.dynamic_slice_in_dim(w_start, first_row, share, 0)
    counts = lax.dynamic_slice_in_dim(visit_counts, first_row, share, 0)
    own_frames = polar_factor(proj, weights, counts, h_start)
    projected = jnp.einsum(
        "krm,kmj->krj",
        lax.all_gather(own_frames, "feature", axis=0, tiled=True),
        visits,
        preferred_element_type=jnp.float32,
    )
    v_full = v_start.astype(jnp.float32)
    v_local = jnp.dot(v_full.T, v_full, precision=HIGH)
    w_local = jnp.dot(w_start.T, w_start, precision=HIGH)
    inner = jnp.einsum("krj,jc->krc", projected, v_full, precision=HIGH)
    h_local = jnp.einsum("krc,kc->rc", inner, w_start, precision=HIGH)
    v_gram = lax.psum(v_local, "feature")
    w_gram = lax.psum(w_local, "patient")
    h_terms = lax.psum(h_local, ("patient", "feature"))
    h_next = solve_right(h_terms, w_gram * v_gram)
    h_gram = jnp.dot(h_next.T, h_next, precision=HIGH)
    factor = h_next[None, :, :] * w_start[:, None, :]
    v_local_terms = jnp.einsum("krj,krc->jc", projected, factor, precision=HIGH)
    v_terms = lax.psum(v_local_terms, "patient")
    v_next = solve_right(v_terms, h_gram * w_gram)
    second = jnp.einsum("krj,jc->krc", projected, v_next, precision=HIGH)
    w_local_terms = jnp.einsum("krc,rc->kc", second, h_next, precision=HIGH)
    v_local_next = jnp.dot(v_next.T, v_next, precision=HIGH)
    w_terms, v_gram_next = lax.psum((w_local_terms, v_local_next), "feature")
    w_next = solve_right(w_terms, h_gram * v_gram_next)
    return (h_next, v_next, w_next)


def solution(mesh):
    return jax.shard_map(
        on_device,
        mesh=mesh,
        in_specs=(
            P(("groups", "patient"), None, "feature"),
            P(("groups", "patient")),
            P(),
            P("feature", None),
            P(("groups", "patient"), None),
        ),
        out_specs=(P(None, "groups"), P("feature", "groups"), P("patient", "groups")),
        check_vma=False,
    )
```

profile of v0, /device:TPU:0, one launch (start us, length us, event | category | flops | bytes accessed | tf_op | source)
XLA Modules:
  0.0 310.8 jit_solution(6929437406793777465)
XLA Ops:
  8.1 12.3 %convolution_bitcast_fusion = f32[32,64,256]{2,1,0:T(8,128)} fusion(bf16[32,256,1024]{2,1,0:T(8,128)(2,1)} %param.8, bf16[1024,64]{0,1:T(8,128)(2,1)S(1)} %copy-done), kind=kOutput, calls=%fused_computation.2 | convolution fusion | flops 1073741824 | bytes 19005440 | tf_op jit(solution)/shard_map/kmj,jr->krm/dot_general | solution.py:14
  20.6 46.5 %reduce-scatter.2.cloned.1.call-done = f32[8,64,256]{2,1,0:T(8,128)} async-done(((f32[32,64,256]{2,1,0:T(8,128)}), f32[8,64,256]{2,1,0:T(8,128)}) %reduce-scatter.2.cloned.1.call-update) | async-done | bytes 524304 | tf_op jit(solution)/shard_map/reduce_scatter | solution.py:44
  67.1 1.8 multiply_reduce_fusion
  69.1 15.8 %while.10 = (s32[]{:T(128)}, f32[8,64,256]{2,1,0:T(8,128)S(1)}, s32[]{:T(128)}) while((s32[]{:T(128)}, f32[8,64,256]{2,1,0:T(8,128)S(1)}, s32[]{:T(128)}) %tuple.27), condition=%wide.region_7.0_spmd, body=%wide.region_6.8_spmd.sunk | while | flops 201719808 | bytes 2883629 | solution.py:31
  85.9 17.7 %psum.43 = f32[64,64]{0,1:T(8,128)S(1)} all-reduce(f32[64,64]{0,1:T(8,128)S(1)} %fusion.35), channel_id=1, replica_groups=mesh['groups'=2,'patient'=4,'feature'=4] {'feature'}, use_global_device_ids=true, to_apply=%region_1.0 | all-reduce | flops 4096 | bytes 32768 | tf_op jit(solution)/shard_map/psum | solution.py:60
  103.8 11.2 %psum.42 = f32[64,64]{0,1:T(8,128)S(1)} all-reduce(f32[64,64]{0,1:T(8,128)S(1)} %fusion.34), channel_id=1, replica_groups=mesh['groups'=2,'patient'=4,'feature'=4] {'patient'}, use_global_device_ids=true, to_apply=%region_0.0 | all-reduce | flops 4096 | bytes 32768 | tf_op jit(solution)/shard_map/psum | solution.py:61
  115.2 5.8 %cholesky.59 = f32[64,64]{1,0:T(8,128)S(1)} custom-call(f32[64,64]{1,0:T(8,128)S(1)} %fusion.30), custom_call_target="Cholesky" | custom-call | tf_op jit(solution)/shard_map/jit(cholesky)/cholesky | solution.py:36
  122.4 4.9 %custom-call.17 = f32[1,64,64]{1,2,0:T(8,128)S(1)} custom-call(f32[1,64,64]{2,1,0:T(8,128)S(1)} %fusion.12), custom_call_target="InvertDiagBlocksLowerTriangular" | custom-call | tf_op jit(solution)/shard_map/triangular_solve | solution.py:38
  127.3 9.1 %fusion.36 = f32[32,64,1024]{2,1,0:T(8,128)S(1)} fusion(bf16[32,64,256]{2,1,0:T(8,128)(2,1)} %all-gather.2.cloned.1.call-done, bf16[32,256,1024]{2,1,0:T(8,128)(2,1)} %param.8), kind=kOutput, calls=%fused_computation.60 | convolution fusion | flops 1073741824 | bytes 26214400 | tf_op jit(solution)/shard_map/krm,kmj->krj/dot_general | solution.py:49
  136.4 3.2 %copy-done.1 = f32[32,64,1024]{2,1,0:T(8,128)} copy-done((f32[32,64,1024]{2,1,0:T(8,128)}, f32[32,64,1024]{2,1,0:T(8,128)S(1)}, u32[]{:S(2)}) %copy-start.1) | copy-done | bytes 8388632
  139.7 3.9 %fusion.2 = f32[64,64]{0,1:T(8,128)S(1)} fusion(f32[32,64,1024]{2,1,0:T(8,128)S(1)} %fusion.36, f32[64,32]{0,1:T(8,128)S(1)} %bitcast.107, bf16[1024,64]{0,1:T(8,128)(2,1)S(1)} %copy-done), kind=kOutput, calls=%fused_computation.5 | convolution fusion | flops 1610870784 | bytes 8544256 | tf_op jit(solution)/shard_map/krj,jc->krc/dot_general | solution.py:58
  143.7 58.3 %psum.44 = f32[64,64]{0,1:T(8,128)S(1)} all-reduce(f32[64,64]{0,1:T(8,128)S(1)} %bitcast.109), channel_id=1, replica_groups=mesh['groups'=2,'patient'=4,'feature'=4] {'patient','feature'}, use_global_device_ids=true, to_apply=%region_8.0 | all-reduce | flops 4096 | bytes 32768 | tf_op jit(solution)/shard_map/psum | solution.py:62
  202.8 5.8 %cholesky.70 = f32[64,64]{1,0:T(8,128)S(1)} custom-call(f32[64,64]{1,0:T(8,128)S(1)} %fusion.24), custom_call_target="Cholesky" | custom-call | tf_op jit(solution)/shard_map/jit(cholesky)/cholesky | solution.py:36
  209.3 16.2 %convolution_bitcast_fusion.2 = f32[1024,64]{1,0:T(8,128)} fusion(f32[32,64,1024]{2,1,0:T(8,128)} %copy-done.1, f32[32,64]{1,0:T(8,128)S(1)} %copy-done.3, f32[64,64]{1,0:T(8,128)S(1)} %copy.27), kind=kOutput, calls=%fused_computation.6 | convolution fusion | flops 1610743808 | bytes 8675328 | tf_op jit(solution)/shard_map/krj,krc->jc/dot_general | solution.py:66
  226.2 4.9 %custom-call.18 = f32[1,64,64]{1,2,0:T(8,128)S(1)} custom-call(f32[1,64,64]{2,1,0:T(8,128)S(1)} %fusion.13), custom_call_target="InvertDiagBlocksLowerTriangular" | custom-call | tf_op jit(solution)/shard_map/triangular_solve | solution.py:38
  231.1 25.5 %all-reduce.3.cloned.1.call-done = f32[1024,64]{1,0:T(8,128)} async-done(((f32[1024,64]{1,0:T(8,128)}), f32[1024,64]{1,0:T(8,128)}) %all-reduce.3.cloned.1.call-update) | async-done | bytes 262160 | tf_op jit(solution)/shard_map/psum | solution.py:67
  256.6 1.7 fusion.22
  258.7 9.5 %fusion.7 = f32[32,64,64]{2,1,0:T(8,128)S(1)} fusion(f32[32,64,1024]{2,1,0:T(8,128)} %copy-done.1, f32[64,1024]{1,0:T(8,128)S(1)} %fusion.20), kind=kOutput, calls=%fused_computation.14 | convolution fusion | flops 1610612736 | bytes 9175040 | tf_op jit(solution)/shard_map/krj,jc->krc/dot_general | solution.py:69
  268.7 0.9 copy.40
  269.6 1.8 fusion.38
  271.3 19.6 %all-reduce = (f32[32,64]{0,1:T(8,128)S(1)}, f32[64,64]{0,1:T(8,128)S(1)}) all-reduce(f32[32,64]{0,1:T(8,128)S(1)} %bitcast.108, f32[64,64]{0,1:T(8,128)S(1)} %fusion.37), channel_id=1, replica_groups=mesh['groups'=2,'patient'=4,'feature'=4] {'feature'}, use_global_device_ids=true, to_apply=%region_11.13 | all-reduce | flops 6144 | bytes 49152 | tf_op jit(solution)/shard_map/psum | solution.py:72
  291.1 5.8 %cholesky.81 = f32[64,64]{1,0:T(8,128)S(1)} custom-call(f32[64,64]{1,0:T(8,128)S(1)} %fusion.19), custom_call_target="Cholesky" | custom-call | tf_op jit(solution)/shard_map/jit(cholesky)/cholesky | solution.py:36
  298.3 4.9 %custom-call.19 = f32[1,64,64]{1,2,0:T(8,128)S(1)} custom-call(f32[1,64,64]{2,1,0:T(8,128)S(1)} %fusion.14), custom_call_target="InvertDiagBlocksLowerTriangular" | custom-call | tf_op jit(solution)/shard_map/triangular_solve | solution.py:38
  303.5 0.8 fusion.15
  (89 shorter events, 23.7 us)
Async XLA Ops:
  7.2 0.9 copy-start
  7.2 13.3 %copy-start.6 = (s32[32]{0:T(128)S(1)}, s32[32]{0:T(128)}, u32[]{:S(2)}) copy-start(s32[32]{0:T(128)} %param.9) | copy-start | bytes 388
  7.2 13.4 %copy-start.3 = (f32[32,64]{1,0:T(8,128)S(1)}, f32[32,64]{1,0:T(8,128)}, u32[]{:S(2)}) copy-start(f32[32,64]{1,0:T(8,128)} %param.12) | copy-start | bytes 24580
  7.2 59.9 %copy-start.5 = (f32[64,64]{1,0:T(8,128)S(1)}, f32[64,64]{1,0:T(8,128)}, u32[]{:S(2)}) copy-start(f32[64,64]{1,0:T(8,128)} %param.10) | copy-start | bytes 49156
  7.2 59.9 %reduce-scatter.2.cloned.1.call-start = ((), (), s32[]{:S(2)}) async-start(), calls=%async_computation.1 | async-start | bytes 2621440 | tf_op jit(solution)/shard_map/reduce_scatter | solution.py:44
  20.4 106.9 %all-gather.2.cloned.1.call-start = ((), (), s32[]{:S(2)}) async-start(), calls=%async_computation.2 | async-start | bytes 1310720 | tf_op jit(solution)/shard_map/all_gather | solution.py:51
  85.6 171.0 %all-reduce.3.cloned.1.call-start = ((), (), s32[]{:S(2)}) async-start(), calls=%async_computation.3 | async-start | bytes 1048576 | tf_op jit(solution)/shard_map/psum | solution.py:67
  136.4 3.2 %copy-start.1 = (f32[32,64,1024]{2,1,0:T(8,128)}, f32[32,64,1024]{2,1,0:T(8,128)S(1)}, u32[]{:S(2)}) copy-start(f32[32,64,1024]{2,1,0:T(8,128)S(1)} %fusion.36) | copy-start | bytes 25165828
  202.7 55.7 %copy-start.4 = (f32[64,64]{1,0:T(8,128)}, f32[64,64]{1,0:T(8,128)S(1)}, u32[]{:S(2)}) copy-start(f32[64,64]{1,0:T(8,128)S(1)} %copy.27) | copy-start | bytes 49156
  258.7 45.6 %copy-start.2 = (f32[64,1024]{1,0:T(8,128)}, f32[64,1024]{1,0:T(8,128)S(1)}, u32[]{:S(2)}) copy-start(f32[64,1024]{1,0:T(8,128)S(1)} %fusion.20) | copy-start | bytes 786436
Sparse Core Ops, SparseCore 0:
  20.5 46.5 reduce-scatter.1
  85.8 27.5 all-gather.1
  225.7 30.8 all-reduce.2
where the time goes:
time: 311 us
  blocking collectives  107 us (34%)
  matrix products  74.2 us (24%)
  waiting for transfers between devices  72.1 us (23%)
  other arithmetic  37.2 us (12%)
  between operations  14.1 us (5%)
  local copies, waits for them, and re-layouts  5.86 us (2%)
    psum x1, blocking collectives, on_device(): h_terms = lax.psum(h_local, ('patient', 'feature'))  58.3 us
    reduce_scatter x1, waiting for transfers between devices, on_device(): lax.psum_scatter(project(visits, v_start), 'feature', scatter_dimension=0...  46.5 us
    psum x1, waiting for transfers between devices, on_device(): v_terms = lax.psum(v_local_terms, 'patient')  25.5 us
    psum x1, blocking collectives, on_device(): w_terms, v_gram_next = lax.psum((w_local_terms, v_local_next), 'feature')  19.6 us
    another operation x9, other arithmetic, solve_right(): lower = jnp.linalg.cholesky(gram)  19.6 us
    psum x1, blocking collectives, on_device(): v_gram = lax.psum(v_local, 'feature')  17.7 us
    another operation x6, other arithmetic, solve_right(): lax.linalg.triangular_solve(lower, first, left_side=True, lower=True, tra...  16.6 us
    dot_general x1, matrix products, on_device(): v_local_terms = jnp.einsum('krj,krc->jc', projected, factor, precision=HIGH)  16.2 us
  transfers between devices with their start and end apart: 3, of which 2 were waited for; matrix products, arithmetic and copies ran while one was open for 6% of the time, Pallas kernels for 0%

commit v1 on v0

v1 whole, which is shorter than its diff:
```python
import functools

import jax
import jax.numpy as jnp
from jax import lax
from jax.experimental import pallas as pl
from jax.experimental.pallas import tpu as pltpu
from jax.sharding import PartitionSpec as P

NS_STEPS = 12
LANES = 128
LEVELS = 32000.0

epsilon = 1e-06
HIGH = lax.Precision.HIGHEST
F32 = jnp.float32
BF16 = jnp.bfloat16
MIB = 1024 * 1024

ROWS_BY_COLS = (((1,), (0,)), ((), ()))
ROWS_BY_ROWS = (((1,), (1,)), ((), ()))
COLS_BY_COLS = (((0,), (0,)), ((), ()))


def low_dot(a, b, dims=ROWS_BY_COLS):
    return lax.dot_general(a, b, dims, preferred_element_type=F32)


def high_dot(a, b, dims=ROWS_BY_COLS):
    return lax.dot_general(a, b, dims, precision=HIGH, preferred_element_type=F32)


def two_parts(x):
    first = x.astype(BF16)
    return first, (x - first.astype(F32)).astype(BF16)


def three_parts(x):
    first = x.astype(BF16)
    rest = x - first.astype(F32)
    second = rest.astype(BF16)
    return first, second, (rest - second.astype(F32)).astype(BF16)


def lane_numbers(shape):
    return lax.broadcasted_iota(jnp.int32, shape, len(shape) - 1)


def project_piece(visits, frame):
    return low_dot(frame, visits, ROWS_BY_ROWS)


def send_projection_kernel(slot, batch, place, v_ref, visits_ref, coded_ref, scale_ref, frame):
    step = pl.program_id(0)

    @pl.when(step == 0)
    def _():
        frame[...] = v_ref[...].astype(F32).T.astype(BF16)
        scale_ref[...] = jnp.zeros_like(scale_ref)

    scales = scale_ref[...].astype(F32)
    lanes = lane_numbers(scales.shape)
    for p in range(batch):
        proj = project_piece(visits_ref[0, p], frame[...])
        top = jnp.max(jnp.abs(proj), axis=1, keepdims=True)
        scale = (jnp.maximum(top, 1e-30) * 1.0078125).astype(BF16).astype(F32)
        coded = jnp.floor(proj * (LEVELS / scale) + 0.5)
        coded_ref[p] = coded.astype(jnp.int32).astype(jnp.int16)
        scales = jnp.where(lanes == step * batch + p, scale, scales)
    scale_ref[...] = scales.astype(BF16)


def own_projection_kernel(batch, place, v_ref, w_ref, visits_ref, proj_ref, v_gram_ref, w_gram_ref, frame):
    step = pl.program_id(0)

    @pl.when(step == 0)
    def _():
        frame[...] = v_ref[...].astype(F32).T.astype(BF16)
        v_gram_ref[...] = low_dot(frame[...], frame[...], ROWS_BY_ROWS)
        w_gram_ref[...] = high_dot(w_ref[...], w_ref[...], COLS_BY_COLS)

    for p in range(batch):
        proj_ref[p] = project_piece(visits_ref[0, p], frame[...])


def batch_of(share):
    return 2 if share % 2 == 0 else 1


def visits_spec(slot, batch, slots, width):
    return pl.BlockSpec((1, batch, slots, width), lambda i, place: (place[0] ^ slot, i, 0, 0))


def whole(shape):
    return pl.BlockSpec(shape, lambda i, place: (0,) * len(shape))


def cost(flops, size):
    return pl.CostEstimate(flops=int(flops), bytes_accessed=int(size), transcendentals=0)


def project_for(slot, place, visits, v_start):
    _, share, slots, width = visits.shape
    rank = v_start.shape[1]
    batch = batch_of(share)
    return pl.pallas_call(
        functools.partial(send_projection_kernel, slot, batch),
        grid_spec=pltpu.PrefetchScalarGridSpec(
            num_scalar_prefetch=1,
            grid=(share // batch,),
            in_specs=[whole(v_start.shape), visits_spec(slot, batch, slots, width)],
            out_specs=[
                pl.BlockSpec((batch, rank, slots), lambda i, place: (i, 0, 0)),
                whole((rank, LANES)),
            ],
            scratch_shapes=[pltpu.VMEM((rank, width), BF16)],
        ),
        out_shape=[
            jax.ShapeDtypeStruct((share, rank, slots), jnp.int16),
            jax.ShapeDtypeStruct((rank, LANES), BF16),
        ],
        cost_estimate=cost(2 * share * rank * slots * width, 2 * share * slots * width),
        name="project_send",
    )(place, v_start, visits)


def project_own(place, visits, v_start, w_start):
    _, share, slots, width = visits.shape
    rank = v_start.shape[1]
    batch = batch_of(share)
    gram = (rank, rank)
    return pl.pallas_call(
        functools.partial(own_projection_kernel, batch),
        grid_spec=pltpu.PrefetchScalarGridSpec(
            num_scalar_prefetch=1,
            grid=(share // batch,),
            in_specs=[whole(v_start.shape), whole(w_start.shape), visits_spec(0, batch, slots, width)],
            out_specs=[
                pl.BlockSpec((batch, rank, slots), lambda i, place: (i, 0, 0)),
                whole(gram),
                whole(gram),
            ],
            scratch_shapes=[pltpu.VMEM((rank, width), BF16)],
        ),
        out_shape=[
            jax.ShapeDtypeStruct((share, rank, slots), F32),
            jax.ShapeDtypeStruct(gram, F32),
            jax.ShapeDtypeStruct(gram, F32),
        ],
        cost_estimate=cost(2 * share * rank * slots * width, 2 * share * slots * width),
        name="project_own",
    )(place, v_start, w_start, visits)


def eliminate(table, rank):
    rows = lax.broadcasted_iota(jnp.int32, table.shape, 0)
    for i in range(rank):
        pivot_row = table[i : i + 1, :] / table[i : i + 1, i : i + 1]
        column = table[:, i : i + 1]
        table = jnp.where(rows == i, pivot_row, table - column * pivot_row)
    return table


def inverse_of(gram):
    rank = gram.shape[0]
    eye = (lax.broadcasted_iota(jnp.int32, gram.shape, 0) == lane_numbers(gram.shape)).astype(F32)
    return eliminate(jnp.concatenate([gram, eye], axis=1), rank)[:, rank:]


def total(refs):
    out = refs[0][...]
    for ref in refs[1:]:
        out = out + ref[...]
    return out


def first_inverse_kernel(n_v, n_w, *refs):
    v_refs, w_refs = refs[:n_v], refs[n_v : n_v + n_w]
    w_gram_ref, inverse_ref = refs[n_v + n_w :]
    w_gram = total(w_refs)
    w_gram_ref[...] = w_gram
    inverse_ref[...] = inverse_of(w_gram * total(v_refs))


def first_inverse(v_grams, w_grams):
    out = jax.ShapeDtypeStruct(w_grams[0].shape, F32)
    return pl.pallas_call(
        functools.partial(first_inverse_kernel, len(v_grams), len(w_grams)),
        out_shape=[out, out],
        cost_estimate=cost(12_000_000_000, 64),
        name="first_inverse",
    )(*v_grams, *w_grams)


def frames_kernel(share, n_slots, place, counts_ref, h_ref, w_ref, own_ref, *refs):
    coded, scales = refs[: n_slots - 1], refs[n_slots - 1 : 2 * n_slots - 2]
    frames_ref, terms_ref, proj, frames = refs[2 * n_slots - 2 :]
    first = place[0] * share
    rank, slots = frames.shape[1:]
    for p in range(share):
        piece = own_ref[p]
        for code, scale in zip(coded, scales):
            step = scale[:, p : p + 1].astype(F32) * (1.0 / LEVELS)
            piece = piece + code[p].astype(jnp.int32).astype(F32) * step
        proj[p] = piece
        weights = w_ref[pl.ds(first + p, 1), :]
        mixed = high_dot(h_ref[...] * weights, piece)
        mixed = jnp.where(lane_numbers((rank, slots)) < counts_ref[first + p], mixed, 0.0)
        energy = jnp.sum(jnp.sum(mixed * mixed, axis=1, keepdims=True), axis=0, keepdims=True)
        frames[p] = mixed * lax.rsqrt(energy + epsilon)

    def sweep(step, carry):
        for p in range(share):
            frame = frames[p]
            first_part, second_part = two_parts(frame)
            both = low_dot(jnp.concatenate([first_part, second_part], axis=0), first_part, ROWS_BY_ROWS)
            gram = both[:rank] + both[rank:] + low_dot(first_part, second_part, ROWS_BY_ROWS)
            gram_first, gram_second = two_parts(gram)
            moved = low_dot(jnp.concatenate([gram_first, gram_second], axis=0), first_part)
            moved = moved[:rank] + moved[rank:] + low_dot(gram_first, second_part)
            frames[p] = 1.5 * frame - 0.5 * moved
        return carry

    lax.fori_loop(0, NS_STEPS, sweep, 0)
    terms = jnp.zeros((rank, rank), F32)
    for p in range(share):
        low = frames[p].astype(BF16)
        frames_ref[p] = low
        parts = three_parts(proj[p])
        product = low_dot(low, parts[0], ROWS_BY_ROWS)
        for part in parts[1:]:
            product = product + low_dot(low, part, ROWS_BY_ROWS)
        terms = terms + product * w_ref[pl.ds(first + p, 1), :]
    terms_ref[...] = terms


VMEM_SPEC = pl.BlockSpec(memory_space=pltpu.VMEM)
SMEM_SPEC = pl.BlockSpec(memory_space=pltpu.SMEM)


def own_frames(place, counts, h_start, w_start, own, coded, scales):
    share, rank, slots = own.shape
    return pl.pallas_call(
        functools.partial(frames_kernel, share, len(coded) + 1),
        in_specs=[SMEM_SPEC] * 2 + [VMEM_SPEC] * (3 + len(coded) + len(scales)),
        out_specs=[VMEM_SPEC] * 2,
        out_shape=[
            jax.ShapeDtypeStruct(own.shape, BF16),
            jax.ShapeDtypeStruct((rank, rank), F32),
        ],
        scratch_shapes=[pltpu.VMEM(own.shape, F32)] * 2,
        compiler_params=pltpu.CompilerParams(vmem_limit_bytes=32 * MIB),
        cost_estimate=cost(10_000_000_000, 4 * share * rank * slots),
        name="own_frames",
    )(place, counts, h_start, w_start, own, *coded, *scales)


def next_h_kernel(n_terms, *refs):
    inverse_ref, w_gram_ref, h_ref, gram_ref, product_ref = refs[n_terms:]
    h_next = high_dot(total(refs[:n_terms]), inverse_ref[...])
    gram = high_dot(h_next, h_next, COLS_BY_COLS)
    h_ref[...] = h_next
    gram_ref[...] = gram
    product_ref[...] = gram * w_gram_ref[...]


def next_h(terms, inverse, w_gram):
    out = jax.ShapeDtypeStruct(w_gram.shape, F32)
    return pl.pallas_call(
        functools.partial(next_h_kernel, len(terms)),
        out_shape=[out] * 3,
        cost_estimate=cost(2_000_000_000, 64),
        name="next_h",
    )(*terms, inverse, w_gram)


def inverse_kernel(gram_ref, inverse_ref):
    inverse_ref[...] = inverse_of(gram_ref[...])


def inverse(gram):
    return pl.pallas_call(
        inverse_kernel,
        out_shape=jax.ShapeDtypeStruct(gram.shape, F32),
        cost_estimate=cost(12_000_000_000, 64),
        name="inverse",
    )(gram)


def v_terms_kernel(slot, batch, share, resumed, place, h_ref, w_ref, frames_ref, visits_ref, *refs):
    if resumed:
        before_ref, _, terms_ref, mixed_ref, h_parts = refs
    else:
        terms_ref, mixed_ref, h_parts = refs
    step = pl.program_id(0)
    rank, slots = frames_ref.shape[1:]

    @pl.when(step == 0)
    def _():
        h_parts[...] = jnp.concatenate(three_parts(h_ref[...].T), axis=0)
        terms_ref[...] = before_ref[...] if resumed else jnp.zeros_like(terms_ref)

    joined = jnp.concatenate([frames_ref[p] for p in range(batch)], axis=1)
    mixed = low_dot(h_parts[...], joined)
    mixed = mixed[:rank] + mixed[rank : 2 * rank] + mixed[2 * rank :]
    first = (place[0] ^ slot) * share + step * batch
    w_columns = w_ref[...]
    patients = lane_numbers(w_columns.shape)
    weighted = []
    for p in range(batch):
        piece = mixed[:, p * slots : (p + 1) * slots]
        mixed_ref[0, p] = piece
        weight = jnp.sum(jnp.where(patients == first + p, w_columns, 0.0), axis=1, keepdims=True)
        weighted.append(piece * weight)
    parts = jnp.concatenate(three_parts(jnp.concatenate(weighted, axis=1)), axis=0)
    pieces = visits_ref[0].reshape(batch * slots, visits_ref.shape[3])
    terms = low_dot(parts, pieces)
    terms_ref[...] += terms[:rank] + terms[rank : 2 * rank] + terms[2 * rank :]


def add_v_terms(slot, place, h_next, w_columns, frames, visits, before):
    n_slots, share, slots, width = visits.shape
    rank = h_next.shape[0]
    batch = batch_of(share)
    terms_shape = (rank, width)
    mixed_shape = (n_slots, share, rank, slots)
    in_specs = [
        whole(h_next.shape),
        whole(w_columns.shape),
        pl.BlockSpec((batch, rank, slots), lambda i, place: (i, 0, 0)),
        visits_spec(slot, batch, slots, width),
    ]
    operands = [h_next, w_columns, frames, visits]
    aliases = {}
    if before is not None:
        in_specs += [whole(terms_shape), pl.BlockSpec(memory_space=pl.ANY)]
        operands += before
        aliases = {6: 1}
    return pl.pallas_call(
        functools.partial(v_terms_kernel, slot, batch, share, before is not None),
        grid_spec=pltpu.PrefetchScalarGridSpec(
            num_scalar_prefetch=1,
            grid=(share // batch,),
            in_specs=in_specs,
            out_specs=[
                whole(terms_shape),
                pl.BlockSpec((1, batch, rank, slots), lambda i, place: (slot, i, 0, 0)),
            ],
            scratch_shapes=[pltpu.VMEM((3 * rank, rank), BF16)],
        ),
        out_shape=[
            jax.ShapeDtypeStruct(terms_shape, F32),
            jax.ShapeDtypeStruct(mixed_shape, F32),
        ],
        input_output_aliases=aliases,
        cost_estimate=cost(8 * share * rank * slots * width, 2 * share * slots * width),
        name="v_terms",
    )(place, *operands)


def next_v_kernel(n_terms, batch, share, place, *refs):
    terms_refs, (inverse_ref, mixed_ref, visits_ref, v_ref, sums_ref, v_parts) = refs[:n_terms], refs[n_terms:]
    step = pl.program_id(0)
    rank = inverse_ref.shape[0]

    @pl.when(step == 0)
    def _():
        v_columns = high_dot(inverse_ref[...], total(terms_refs))
        v_ref[...] = v_columns.T
        v_parts[...] = jnp.concatenate(three_parts(v_columns), axis=0)
        gram = high_dot(v_columns, v_columns, ROWS_BY_ROWS)
        sums_ref[...] = jnp.concatenate([gram, jnp.zeros((rank, LANES - rank), F32)], axis=1)

    sums = sums_ref[...]
    lanes = lane_numbers(sums.shape)
    for p in range(batch):
        seen = low_dot(v_parts[...], visits_ref[p], ROWS_BY_ROWS)
        seen = seen[:rank] + seen[rank : 2 * rank] + seen[2 * rank :]
        column = jnp.sum(seen * mixed_ref[0, p], axis=1, keepdims=True)
        sums = jnp.where(lanes == rank + step * batch + p, column, sums)
    sums_ref[...] = sums


def next_v(place, terms, inverse, mixed, visits):
    patients, slots, width = visits.shape
    _, share, rank, _ = mixed.shape
    batch = batch_of(share)
    per_owner = share // batch
    return pl.pallas_call(
        functools.partial(next_v_kernel, len(terms), batch, share),
        grid_spec=pltpu.PrefetchScalarGridSpec(
            num_scalar_prefetch=1,
            grid=(patients // batch,),
            in_specs=[whole((rank, width))] * len(terms)
            + [
                whole((rank, rank)),
                pl.BlockSpec(
                    (1, batch, rank, slots),
                    lambda i, place: (place[0] ^ (i // per_owner), i % per_owner, 0, 0),
                ),
                pl.BlockSpec((batch, slots, width), lambda i, place: (i, 0, 0)),
            ],
            out_specs=[whole((width, rank)), whole((rank, LANES))],
            scratch_shapes=[pltpu.VMEM((3 * rank, width), BF16)],
        ),
        out_shape=[
            jax.ShapeDtypeStruct((width, rank), F32),
            jax.ShapeDtypeStruct((rank, LANES), F32),
        ],
        compiler_params=pltpu.CompilerParams(vmem_limit_bytes=32 * MIB),
        cost_estimate=cost(8 * patients * rank * slots * width, 2 * patients * slots * width),
        name="next_v",
    )(place, *terms, inverse, mixed, visits)


def next_w_kernel(n_sums, *refs):
    gram_ref, w_ref = refs[n_sums:]
    patients, rank = w_ref.shape
    sums = total(refs[:n_sums])
    table = jnp.concatenate([sums[:, :rank] * gram_ref[...], sums[:, rank:]], axis=1)
    solved = eliminate(table, rank)
    w_ref[...] = solved.T[rank : rank + patients]


def next_w(sums, h_gram, patients):
    rank = h_gram.shape[0]
    return pl.pallas_call(
        functools.partial(next_w_kernel, len(sums)),
        out_shape=jax.ShapeDtypeStruct((patients, rank), F32),
        cost_estimate=cost(12_000_000_000, 64),
        name="next_w",
    )(*sums, h_gram)


def swap(x, axis, slot):
    pairs = [(i, i ^ slot) for i in range(lax.axis_size(axis))]
    return lax.ppermute(x, axis, pairs)


def all_terms(x, axis):
    n = lax.axis_size(axis)
    if n > 4:
        return [lax.psum(x, axis)]
    return [x] + [swap(x, axis, s) for s in range(1, n)]


def staged_terms(x, axis):
    n = lax.axis_size(axis)
    step = 1
    while 2 * step < n:
        x = x + swap(x, axis, step)
        step *= 2
    return [x, swap(x, axis, step)]


def on_device(visits, visit_counts, h_start, v_start, w_start):
    n = lax.axis_size("feature")
    patients, slots, width = visits.shape
    share = patients // n
    place = lax.axis_index("feature").astype(jnp.int32).reshape(1)
    by_owner = visits.reshape(n, share, slots, width)

    coded, scales = [], []
    for slot in range(n - 1, 0, -1):
        code, scale = project_for(slot, place, by_owner, v_start)
        coded.append(swap(code, "feature", slot))
        scales.append(swap(scale, "feature", slot))
    own, v_local, w_local = project_own(place, by_owner, v_start, w_start)
    w_gram, first = first_inverse(all_terms(v_local, "feature"), all_terms(w_local, "patient"))

    frames, h_local = own_frames(place, visit_counts, h_start, w_start, own, coded, scales)
    h_terms = all_terms(sum(all_terms(h_local, "feature")), "patient")
    all_frames = [frames] + [swap(frames, "feature", slot) for slot in range(1, n)]
    h_next, h_gram, product = next_h(h_terms, first, w_gram)

    w_columns = w_start.T
    before = None
    for slot in range(n):
        before = add_v_terms(slot, place, h_next, w_columns, all_frames[slot], by_owner, before)
    terms, mixed = before
    v_terms = staged_terms(terms, "patient")
    v_next, sums = next_v(place, v_terms, inverse(product), mixed, visits)
    w_next = next_w(all_terms(sums, "feature"), h_gram, patients)
    return (h_next, v_next, w_next)


def solution(mesh):
    return jax.shard_map(
        on_device,
        mesh=mesh,
        in_specs=(
            P(("groups", "patient"), None, "feature"),
            P(("groups", "patient")),
            P(),
            P("feature", None),
            P(("groups", "patient"), None),
        ),
        out_specs=(P(None, "groups"), P("feature", "groups"), P("patient", "groups")),
        check_vma=False,
    )
```

time: 311 us -> 155 us (0.50)
  blocking collectives: 107 us -> 0 us
  Pallas kernels: 0 us -> 85.8 us
  matrix products: 74.2 us -> 0 us
  waiting for transfers between devices: 72.1 us -> 15.6 us
  other arithmetic: 37.2 us -> 1 us
  starting transfers between devices: 0.12 us -> 35.3 us
  between operations: 14.1 us -> 0.91 us
  local copies, waits for them, and re-layouts: 5.86 us -> 15.4 us
    psum x4 -> x0, blocking collectives: 107 us -> none  [the longest x1 58.3 us: on_device(): h_terms = lax.psum(h_local, ('patient', 'feature'))]
    pallas_call x0 -> x14, Pallas kernels: none -> 85.8 us  [the longest x4 20.4 us: add_v_terms(): pl.pallas_call(functools.partial(v_terms_kernel, slot, batch, share, befo...]
    dot_general x35 -> x0, matrix products: 70.6 us -> none  [the longest x1 16.2 us: on_device(): v_local_terms = jnp.einsum('krj,krc->jc', projected, factor, precision=HIGH)]
    reduce_scatter x1 -> x0, waiting for transfers between devices: 46.5 us -> none  [on_device(): lax.psum_scatter(project(visits, v_start), 'feature', scatter_dimension=0...]
    another operation x15 -> x0, other arithmetic: 36.2 us -> none  [the longest x9 19.6 us: solve_right(): lower = jnp.linalg.cholesky(gram)]
    ppermute x0 -> x26, starting transfers between devices: none -> 35.3 us  [swap(): return lax.ppermute(x, axis, pairs)]
    psum x1 -> x0, waiting for transfers between devices: 25.5 us -> none  [on_device(): v_terms = lax.psum(v_local_terms, 'patient')]
    ppermute x0 -> x26, waiting for transfers between devices: none -> 15.6 us  [swap(): return lax.ppermute(x, axis, pairs)]
  transfers between devices with their start and end apart: 3 -> 26, of which waited for: 2 -> 7; matrix products, arithmetic and copies ran while one was open for 6% -> 1% of each run, Pallas kernels for 0% -> 38%
where the time goes in v1:
time: 155 us; the launch traced here: 154 us
  Pallas kernels  85.8 us (55%)
  starting transfers between devices  35.3 us (23%)
  waiting for transfers between devices  15.6 us (10%)
  local copies, waits for them, and re-layouts  15.4 us (10%)
    ppermute x26, starting transfers between devices, swap(): return lax.ppermute(x, axis, pairs)  35.3 us
    pallas_call x4, Pallas kernels, add_v_terms(): pl.pallas_call(functools.partial(v_terms_kernel, slot, batch, share, befo...  20.4 us
    ppermute x26, waiting for transfers between devices, swap(): return lax.ppermute(x, axis, pairs)  15.6 us
    unnamed x61, local copies, waits for them, and re-layouts  15.4 us
    pallas_call x3, Pallas kernels, project_for(): pl.pallas_call(functools.partial(send_projection_kernel, slot, batch), gr...  15.2 us
    pallas_call x1, Pallas kernels, own_frames(): pl.pallas_call(functools.partial(frames_kernel, share, len(coded) + 1), i...  11.8 us
    pallas_call x1, Pallas kernels, next_v(): pl.pallas_call(functools.partial(next_v_kernel, len(terms), batch, share)...  10.3 us
    pallas_call x1, Pallas kernels, inverse(): pl.pallas_call(inverse_kernel, out_shape=jax.ShapeDtypeStruct(gram.shape,...  7.08 us
  transfers between devices with their start and end apart: 26, of which 7 were waited for; matrix products, arithmetic and copies ran while one was open for 1% of the time, Pallas kernels for 38%

profile of v1, /device:TPU:0, one launch (start us, length us, event | category | flops | bytes accessed | tf_op | source)
XLA Modules:
  0.0 154.1 jit_solution(12463221557337475155)
XLA Ops:
  2.4 5.1 %project_send.3 = (s16[8,64,256]{2,1,0:T(8,128)(2,1)}, bf16[64,128]{1,0:T(8,128)(2,1)}) custom-call(s32[1]{0:T(128)} %bitcast.place, bf16[1024,64]{1,0:T(8,128)(2,1)} %copy.11.v_ref, bf16[4,8,256,1024]{3,2,1,0:T(8,128)(2,1)} %bitcast.3), custom_call_target="tpu_custom_call" | custom-call | flops 268435456 | bytes 4194304 | tf_op jit(solution)/shard_map/project_send/pallas_call | solution.py:106
  7.5 5.1 %collective-permute-start = (s16[8,64,256]{2,1,0:T(8,128)(2,1)}, s16[8,64,256]{2,1,0:T(8,128)(2,1)S(1)}, u32[]{:S(2)}, u32[]{:S(2)}) collective-permute-start(s16[8,64,256]{2,1,0:T(8,128)(2,1)} %get-tuple-element.30), channel_id=1, source_target_pairs={{0,3},{1,2},{2,1},{3,0},{4,7},{5,6},{6,5},{7,4},{8,11},{9,10},{10,... | collective-permute-start | bytes 786440 | tf_op jit(solution)/shard_map/ppermute | solution.py:437
  12.5 5.1 %project_send.4 = (s16[8,64,256]{2,1,0:T(8,128)(2,1)}, bf16[64,128]{1,0:T(8,128)(2,1)}) custom-call(s32[1]{0:T(128)} %bitcast.place, bf16[1024,64]{1,0:T(8,128)(2,1)} %copy.11.v_ref, bf16[4,8,256,1024]{3,2,1,0:T(8,128)(2,1)} %bitcast.4), custom_call_target="tpu_custom_call" | custom-call | flops 268435456 | bytes 4194304 | tf_op jit(solution)/shard_map/project_send/pallas_call | solution.py:106
  17.6 5.1 %project_send.5 = (s16[8,64,256]{2,1,0:T(8,128)(2,1)}, bf16[64,128]{1,0:T(8,128)(2,1)}) custom-call(s32[1]{0:T(128)} %bitcast.place, bf16[1024,64]{1,0:T(8,128)(2,1)} %copy.11.v_ref, bf16[4,8,256,1024]{3,2,1,0:T(8,128)(2,1)} %bitcast.5), custom_call_target="tpu_custom_call" | custom-call | flops 268435456 | bytes 4194304 | tf_op jit(solution)/shard_map/project_send/pallas_call | solution.py:106
  23.3 3.8 %collective-permute-start.3 = (bf16[64,128]{1,0:T(8,128)(2,1)S(1)}, bf16[64,128]{1,0:T(8,128)(2,1)S(1)}, u32[]{:S(2)}, u32[]{:S(2)}) collective-permute-start(bf16[64,128]{1,0:T(8,128)(2,1)S(1)} %copy-done.28), channel_id=1, source_target_pairs={{0,3},{1,2},{2,1},{3,0},{4,7},{5,6},{6,5},{7,4},{8,11},{9,10},{10,... | collective-permute-start | bytes 49160 | tf_op jit(solution)/shard_map/ppermute | solution.py:437
  27.1 6.3 %collective-permute-done.3.refs_3_ = bf16[64,128]{1,0:T(8,128)(2,1)S(1)} collective-permute-done((bf16[64,128]{1,0:T(8,128)(2,1)S(1)}, bf16[64,128]{1,0:T(8,128)(2,1)S(1)}, u32[]{:S(2)}, u32[]{:S(2)}) %collective-permute-start.3) | collective-permute-done | bytes 16416 | tf_op jit(solution)/shard_map/ppermute | solution.py:437
  33.4 3.4 %collective-permute-start.5 = (bf16[64,128]{1,0:T(8,128)(2,1)}, bf16[64,128]{1,0:T(8,128)(2,1)S(1)}, u32[]{:S(2)}, u32[]{:S(2)}) collective-permute-start(bf16[64,128]{1,0:T(8,128)(2,1)} %get-tuple-element.35), channel_id=1, source_target_pairs={{0,1},{1,0},{2,3},{3,2},{4,5},{5,4},{6,7},{7,6},{8,9},{9,8},{10,11... | collective-permute-start | bytes 49160 | tf_op jit(solution)/shard_map/ppermute | solution.py:437
  36.9 5.1 %project_own.1 = (f32[8,64,256]{2,1,0:T(8,128)}, f32[64,64]{1,0:T(8,128)}, f32[64,64]{1,0:T(8,128)}) custom-call(s32[1]{0:T(128)} %bitcast.place, bf16[1024,64]{1,0:T(8,128)(2,1)} %copy.11.v_ref, f32[32,64]{1,0:T(8,128)} %w_ref.3, bf16[4,8,256,1024]{3,2,1,0:T(8,128)(2,1)} %bitcast.6), custom_call_target="tpu_custom_call" | custom-call | flops 268435456 | bytes 4194304 | tf_op jit(solution)/shard_map/project_own/pallas_call | solution.py:132
  43.1 11.8 %own_frames.1 = (bf16[8,64,256]{2,1,0:T(8,128)(2,1)S(1)}, f32[64,64]{1,0:T(8,128)S(1)}) custom-call(s32[1]{0:T(128)} %bitcast.place, s32[32]{0:T(128)S(1)} %copy-done.8, f32[64,64]{1,0:T(8,128)S(1)} %copy-done.6, f32[32,64]{1,0:T(8,128)S(1)} %copy-done.3, f32[8,64,256]{2,1,0:T(8,128)S(1)} %copy-done.5, s16[8,64,256]{2,1,0:T(8,128)(2,1)S(1)} %collective-permute-done.refs_0_, ...), custom_call_target="tpu_custom_call" | custom-call | flops 10000000000 | bytes 524288 | tf_op jit(solution)/shard_map/own_frames/pallas_call | solution.py:243
  55.0 2.0 %collective-permute-start.6 = (f32[64,64]{1,0:T(8,128)S(1)}, f32[64,64]{1,0:T(8,128)S(1)}, u32[]{:S(2)}, u32[]{:S(2)}) collective-permute-start(f32[64,64]{1,0:T(8,128)S(1)} %get-tuple-element.36), channel_id=1, source_target_pairs={{0,1},{1,0},{2,3},{3,2},{4,5},{5,4},{6,7},{7,6},{8,9},{9,8},{10,11... | collective-permute-start | bytes 49160 | tf_op jit(solution)/shard_map/ppermute | solution.py:437
  59.5 2.0 %collective-permute-start.13 = (f32[64,64]{1,0:T(8,128)S(1)}, f32[64,64]{1,0:T(8,128)S(1)}, u32[]{:S(2)}, u32[]{:S(2)}) collective-permute-start(f32[64,64]{1,0:T(8,128)S(1)} %copy-done.13), channel_id=1, source_target_pairs={{0,2},{1,3},{2,0},{3,1},{4,6},{5,7},{6,4},{7,5},{8,10},{9,11},{10,... | collective-permute-start | bytes 49160 | tf_op jit(solution)/shard_map/ppermute | solution.py:437
  70.7 7.1 %first_inverse.1 = (f32[64,64]{1,0:T(8,128)}, f32[64,64]{1,0:T(8,128)}) custom-call(f32[64,64]{1,0:T(8,128)} %get-tuple-element.37.refs_0_, f32[64,64]{1,0:T(8,128)} %copy-done.15, f32[64,64]{1,0:T(8,128)} %copy-done.16, f32[64,64]{1,0:T(8,128)} %copy-done.17, f32[64,64]{1,0:T(8,128)} %get-tuple-element.38.refs_4_, f32[64,64]{1,0:T(8,128)} %copy-done.19, ...), custom_call_target="tpu_custom_call" | custom-call | flops 12000000000 | bytes 64 | tf_op jit(solution)/shard_map/first_inverse/pallas_call | solution.py:187
  79.7 2.5 %collective-permute-start.18 = (bf16[8,64,256]{2,1,0:T(8,128)(2,1)S(1)}, bf16[8,64,256]{2,1,0:T(8,128)(2,1)S(1)}, u32[]{:S(2)}, u32[]{:S(2)}) collective-permute-start(bf16[8,64,256]{2,1,0:T(8,128)(2,1)S(1)} %get-tuple-element.42.frames_ref), channel_id=1, source_target_pairs={{0,3},{1,2},{2,1},{3,0},{4,7},{5,6},{6,5},{7,4},{8,11},{9,10},{10,... | collective-permute-start | bytes 786440 | tf_op jit(solution)/shard_map/ppermute | solution.py:437
  84.7 5.0 %v_terms.4 = (f32[64,1024]{1,0:T(8,128)}, f32[4,8,64,256]{3,2,1,0:T(8,128)}) custom-call(s32[1]{0:T(128)} %bitcast.place, f32[64,64]{1,0:T(8,128)} %get-tuple-element.55.h_ref, f32[64,32]{1,0:T(8,128)} %bitcast.11, bf16[8,64,256]{2,1,0:T(8,128)(2,1)} %copy-done.2, bf16[4,8,256,1024]{3,2,1,0:T(8,128)(2,1)} %bitcast.7), custom_call_target="tpu_custom_call" | custom-call | flops 1073741824 | bytes 4194304 | tf_op jit(solution)/shard_map/v_terms/pallas_call | solution.py:339
  91.0 5.1 %v_terms.5 = (f32[64,1024]{1,0:T(8,128)}, f32[4,8,64,256]{3,2,1,0:T(8,128)}) custom-call(s32[1]{0:T(128)} %bitcast.place, f32[64,64]{1,0:T(8,128)} %get-tuple-element.55.h_ref, f32[64,32]{1,0:T(8,128)} %bitcast.12, bf16[8,64,256]{2,1,0:T(8,128)(2,1)} %copy-done.11, bf16[4,8,256,1024]{3,2,1,0:T(8,128)(2,1)} %bitcast.8, ...), custom_call_target="tpu_custom_call", output_to_operand_aliasing={{1}: (6, {})} | custom-call | flops 1073741824 | bytes 4194304 | tf_op jit(solution)/shard_map/v_terms/pallas_call | solution.py:339
  96.2 3.0 %collective-permute-done.19.frames_ref = bf16[8,64,256]{2,1,0:T(8,128)(2,1)S(1)} collective-permute-done((bf16[8,64,256]{2,1,0:T(8,128)(2,1)S(1)}, bf16[8,64,256]{2,1,0:T(8,128)(2,1)S(1)}, u32[]{:S(2)}, u32[]{:S(2)}) %collective-permute-start.19) | collective-permute-done | bytes 262176 | tf_op jit(solution)/shard_map/ppermute | solution.py:437
  99.9 5.1 %v_terms.6 = (f32[64,1024]{1,0:T(8,128)}, f32[4,8,64,256]{3,2,1,0:T(8,128)}) custom-call(s32[1]{0:T(128)} %bitcast.place, f32[64,64]{1,0:T(8,128)} %get-tuple-element.55.h_ref, f32[64,32]{1,0:T(8,128)} %bitcast.13, bf16[8,64,256]{2,1,0:T(8,128)(2,1)} %copy-done.10, bf16[4,8,256,1024]{3,2,1,0:T(8,128)(2,1)} %bitcast.9, ...), custom_call_target="tpu_custom_call", output_to_operand_aliasing={{1}: (6, {})} | custom-call | flops 1073741824 | bytes 4194304 | tf_op jit(solution)/shard_map/v_terms/pallas_call | solution.py:339
  105.7 5.1 %v_terms.7 = (f32[64,1024]{1,0:T(8,128)}, f32[4,8,64,256]{3,2,1,0:T(8,128)}) custom-call(s32[1]{0:T(128)} %bitcast.place, f32[64,64]{1,0:T(8,128)} %get-tuple-element.55.h_ref, f32[64,32]{1,0:T(8,128)} %bitcast.14, bf16[8,64,256]{2,1,0:T(8,128)(2,1)} %copy-done.9, bf16[4,8,256,1024]{3,2,1,0:T(8,128)(2,1)} %bitcast.10, ...), custom_call_target="tpu_custom_call", output_to_operand_aliasing={{1}: (6, {})} | custom-call | flops 1073741824 | bytes 4194304 | tf_op jit(solution)/shard_map/v_terms/pallas_call | solution.py:339
  114.2 7.1 %inverse.1.refs_2_ = f32[64,64]{1,0:T(8,128)} custom-call(f32[64,64]{1,0:T(8,128)} %get-tuple-element.50.gram_ref), custom_call_target="tpu_custom_call" | custom-call | flops 12000000000 | bytes 64 | tf_op jit(solution)/shard_map/inverse/pallas_call | solution.py:282
  122.0 5.8 %copy-done = bf16[32,256,1024]{2,1,0:T(8,128)(2,1)S(1)} copy-done((bf16[32,256,1024]{2,1,0:T(8,128)(2,1)S(1)}, bf16[32,256,1024]{2,1,0:T(8,128)(2,1)}, u32[]{:S(2)}) %copy-start) | copy-done | bytes 16777240
  128.5 10.3 %next_v.1 = (f32[1024,64]{1,0:T(8,128)S(1)}, f32[64,128]{1,0:T(8,128)S(1)}) custom-call(s32[1]{0:T(128)} %bitcast.place, f32[64,1024]{1,0:T(8,128)S(1)} %add.15.refs_0_, f32[64,1024]{1,0:T(8,128)S(1)} %collective-permute-done.22.refs_1_, f32[64,64]{1,0:T(8,128)S(1)} %copy-done.4, f32[4,8,64,256]{3,2,1,0:T(8,128)S(1)} %copy-done.1, ...), custom_call_target="tpu_custom_call" | custom-call | flops 4294967296 | bytes 16777216 | tf_op jit(solution)/shard_map/next_v/pallas_call | solution.py:389
  140.9 2.4 %collective-permute-start.25 = (f32[64,128]{1,0:T(8,128)S(1)}, f32[64,128]{1,0:T(8,128)S(1)}, u32[]{:S(2)}, u32[]{:S(2)}) collective-permute-start(f32[64,128]{1,0:T(8,128)S(1)} %get-tuple-element.53.refs_0_), channel_id=1, source_target_pairs={{0,3},{1,2},{2,1},{3,0},{4,7},{5,6},{6,5},{7,4},{8,11},{9,10},{10,... | collective-permute-start | bytes 98312 | tf_op jit(solution)/shard_map/ppermute | solution.py:437
  144.2 2.4 %collective-permute-done.25.refs_3_ = f32[64,128]{1,0:T(8,128)S(1)} collective-permute-done((f32[64,128]{1,0:T(8,128)S(1)}, f32[64,128]{1,0:T(8,128)S(1)}, u32[]{:S(2)}, u32[]{:S(2)}) %collective-permute-start.25) | collective-permute-done | bytes 32800 | tf_op jit(solution)/shard_map/ppermute | solution.py:437
  147.2 6.9 %next_w.1 = f32[32,64]{1,0:T(8,128)} custom-call(f32[64,128]{1,0:T(8,128)} %copy-done.7, f32[64,128]{1,0:T(8,128)} %copy-done.24, f32[64,128]{1,0:T(8,128)} %copy-done.25, f32[64,128]{1,0:T(8,128)} %copy-done.26, f32[64,64]{1,0:T(8,128)} %get-tuple-element.54.refs_4_), custom_call_target="tpu_custom_call" | custom-call | flops 12000000000 | bytes 64 | tf_op jit(solution)/shard_map/next_w/pallas_call | solution.py:427
  (105 shorter events, 30.6 us)
Async XLA Ops:
  7.5 34.6 %collective-permute-start = (s16[8,64,256]{2,1,0:T(8,128)(2,1)}, s16[8,64,256]{2,1,0:T(8,128)(2,1)S(1)}, u32[]{:S(2)}, u32[]{:S(2)}) collective-permute-start(s16[8,64,256]{2,1,0:T(8,128)(2,1)} %get-tuple-element.30), channel_id=1, source_target_pairs={{0,3},{1,2},{2,1},{3,0},{4,7},{5,6},{6,5},{7,4},{8,11},{9,10},{10,... | collective-permute-start | bytes 786440 | tf_op jit(solution)/shard_map/ppermute | solution.py:437
  17.6 24.5 %collective-permute-start.1 = (s16[8,64,256]{2,1,0:T(8,128)(2,1)}, s16[8,64,256]{2,1,0:T(8,128)(2,1)S(1)}, u32[]{:S(2)}, u32[]{:S(2)}) collective-permute-start(s16[8,64,256]{2,1,0:T(8,128)(2,1)} %get-tuple-element.31), channel_id=1, source_target_pairs={{0,2},{1,3},{2,0},{3,1},{4,6},{5,7},{6,4},{7,5},{8,10},{9,11},{10,... | collective-permute-start | bytes 786440 | tf_op jit(solution)/shard_map/ppermute | solution.py:437
  22.7 19.3 %collective-permute-start.2 = (s16[8,64,256]{2,1,0:T(8,128)(2,1)}, s16[8,64,256]{2,1,0:T(8,128)(2,1)S(1)}, u32[]{:S(2)}, u32[]{:S(2)}) collective-permute-start(s16[8,64,256]{2,1,0:T(8,128)(2,1)} %get-tuple-element.32), channel_id=1, source_target_pairs={{0,1},{1,0},{2,3},{3,2},{4,5},{5,4},{6,7},{7,6},{8,9},{9,8},{10,11... | collective-permute-start | bytes 786440 | tf_op jit(solution)/shard_map/ppermute | solution.py:437
  23.3 10.2 %collective-permute-start.3 = (bf16[64,128]{1,0:T(8,128)(2,1)S(1)}, bf16[64,128]{1,0:T(8,128)(2,1)S(1)}, u32[]{:S(2)}, u32[]{:S(2)}) collective-permute-start(bf16[64,128]{1,0:T(8,128)(2,1)S(1)} %copy-done.28), channel_id=1, source_target_pairs={{0,3},{1,2},{2,1},{3,0},{4,7},{5,6},{6,5},{7,4},{8,11},{9,10},{10,... | collective-permute-start | bytes 49160 | tf_op jit(solution)/shard_map/ppermute | solution.py:437
  27.1 14.8 %collective-permute-start.4 = (bf16[64,128]{1,0:T(8,128)(2,1)S(1)}, bf16[64,128]{1,0:T(8,128)(2,1)S(1)}, u32[]{:S(2)}, u32[]{:S(2)}) collective-permute-start(bf16[64,128]{1,0:T(8,128)(2,1)S(1)} %copy-done.27), channel_id=1, source_target_pairs={{0,2},{1,3},{2,0},{3,1},{4,6},{5,7},{6,4},{7,5},{8,10},{9,11},{10,... | collective-permute-start | bytes 49160 | tf_op jit(solution)/shard_map/ppermute | solution.py:437
  33.4 8.6 %collective-permute-start.5 = (bf16[64,128]{1,0:T(8,128)(2,1)}, bf16[64,128]{1,0:T(8,128)(2,1)S(1)}, u32[]{:S(2)}, u32[]{:S(2)}) collective-permute-start(bf16[64,128]{1,0:T(8,128)(2,1)} %get-tuple-element.35), channel_id=1, source_target_pairs={{0,1},{1,0},{2,3},{3,2},{4,5},{5,4},{6,7},{7,6},{8,9},{9,8},{10,11... | collective-permute-start | bytes 49160 | tf_op jit(solution)/shard_map/ppermute | solution.py:437
  41.9 20.2 %collective-permute-start.12 = (f32[64,64]{1,0:T(8,128)}, f32[64,64]{1,0:T(8,128)S(1)}, u32[]{:S(2)}, u32[]{:S(2)}) collective-permute-start(f32[64,64]{1,0:T(8,128)} %get-tuple-element.37.refs_0_), channel_id=1, source_target_pairs={{0,1},{1,0},{2,3},{3,2},{4,5},{5,4},{6,7},{7,6},{8,9},{9,8},{10,11... | collective-permute-start | bytes 49160 | tf_op jit(solution)/shard_map/ppermute | solution.py:437
  55.0 8.5 %collective-permute-start.6 = (f32[64,64]{1,0:T(8,128)S(1)}, f32[64,64]{1,0:T(8,128)S(1)}, u32[]{:S(2)}, u32[]{:S(2)}) collective-permute-start(f32[64,64]{1,0:T(8,128)S(1)} %get-tuple-element.36), channel_id=1, source_target_pairs={{0,1},{1,0},{2,3},{3,2},{4,5},{5,4},{6,7},{7,6},{8,9},{9,8},{10,11... | collective-permute-start | bytes 49160 | tf_op jit(solution)/shard_map/ppermute | solution.py:437
  57.0 6.6 %collective-permute-start.7 = (f32[64,64]{1,0:T(8,128)S(1)}, f32[64,64]{1,0:T(8,128)S(1)}, u32[]{:S(2)}, u32[]{:S(2)}) collective-permute-start(f32[64,64]{1,0:T(8,128)S(1)} %get-tuple-element.36), channel_id=1, source_target_pairs={{0,2},{1,3},{2,0},{3,1},{4,6},{5,7},{6,4},{7,5},{8,10},{9,11},{10,... | collective-permute-start | bytes 49160 | tf_op jit(solution)/shard_map/ppermute | solution.py:437
  58.1 7.0 %collective-permute-start.8 = (f32[64,64]{1,0:T(8,128)S(1)}, f32[64,64]{1,0:T(8,128)S(1)}, u32[]{:S(2)}, u32[]{:S(2)}) collective-permute-start(f32[64,64]{1,0:T(8,128)S(1)} %get-tuple-element.36), channel_id=1, source_target_pairs={{0,3},{1,2},{2,1},{3,0},{4,7},{5,6},{6,5},{7,4},{8,11},{9,10},{10,... | collective-permute-start | bytes 49160 | tf_op jit(solution)/shard_map/ppermute | solution.py:437
  59.5 6.0 %collective-permute-start.13 = (f32[64,64]{1,0:T(8,128)S(1)}, f32[64,64]{1,0:T(8,128)S(1)}, u32[]{:S(2)}, u32[]{:S(2)}) collective-permute-start(f32[64,64]{1,0:T(8,128)S(1)} %copy-done.13), channel_id=1, source_target_pairs={{0,2},{1,3},{2,0},{3,1},{4,6},{5,7},{6,4},{7,5},{8,10},{9,11},{10,... | collective-permute-start | bytes 49160 | tf_op jit(solution)/shard_map/ppermute | solution.py:437
  62.1 5.7 %collective-permute-start.14 = (f32[64,64]{1,0:T(8,128)S(1)}, f32[64,64]{1,0:T(8,128)S(1)}, u32[]{:S(2)}, u32[]{:S(2)}) collective-permute-start(f32[64,64]{1,0:T(8,128)S(1)} %copy-done.13), channel_id=1, source_target_pairs={{0,3},{1,2},{2,1},{3,0},{4,7},{5,6},{6,5},{7,4},{8,11},{9,10},{10,... | collective-permute-start | bytes 49160 | tf_op jit(solution)/shard_map/ppermute | solution.py:437
  63.6 5.9 %collective-permute-start.16 = (f32[64,64]{1,0:T(8,128)S(1)}, f32[64,64]{1,0:T(8,128)S(1)}, u32[]{:S(2)}, u32[]{:S(2)}) collective-permute-start(f32[64,64]{1,0:T(8,128)S(1)} %copy-done.14), channel_id=1, source_target_pairs={{0,8},{4,12},{8,0},{12,4},{1,9},{5,13},{9,1},{13,5},{2,10},{6,14},... | collective-permute-start | bytes 49160 | tf_op jit(solution)/shard_map/ppermute | solution.py:437
  65.1 4.4 %collective-permute-start.17 = (f32[64,64]{1,0:T(8,128)S(1)}, f32[64,64]{1,0:T(8,128)S(1)}, u32[]{:S(2)}, u32[]{:S(2)}) collective-permute-start(f32[64,64]{1,0:T(8,128)S(1)} %copy-done.14), channel_id=1, source_target_pairs={{0,12},{4,8},{8,4},{12,0},{1,13},{5,9},{9,5},{13,1},{2,14},{6,10},... | collective-permute-start | bytes 49160 | tf_op jit(solution)/shard_map/ppermute | solution.py:437
  65.5 14.2 %collective-permute-start.10 = (f32[64,64]{1,0:T(8,128)S(1)}, f32[64,64]{1,0:T(8,128)S(1)}, u32[]{:S(2)}, u32[]{:S(2)}) collective-permute-start(f32[64,64]{1,0:T(8,128)S(1)} %add_add_fusion.refs_0_), channel_id=1, source_target_pairs={{0,8},{4,12},{8,0},{12,4},{1,9},{5,13},{9,1},{13,5},{2,10},{6,14},... | collective-permute-start | bytes 49160 | tf_op jit(solution)/shard_map/ppermute | solution.py:437
  67.9 14.3 %collective-permute-start.11 = (f32[64,64]{1,0:T(8,128)S(1)}, f32[64,64]{1,0:T(8,128)S(1)}, u32[]{:S(2)}, u32[]{:S(2)}) collective-permute-start(f32[64,64]{1,0:T(8,128)S(1)} %add_add_fusion.refs_0_), channel_id=1, source_target_pairs={{0,12},{4,8},{8,4},{12,0},{1,13},{5,9},{9,5},{13,1},{2,14},{6,10},... | collective-permute-start | bytes 49160 | tf_op jit(solution)/shard_map/ppermute | solution.py:437
  67.9 14.3 %collective-permute-start.9 = (f32[64,64]{1,0:T(8,128)S(1)}, f32[64,64]{1,0:T(8,128)S(1)}, u32[]{:S(2)}, u32[]{:S(2)}) collective-permute-start(f32[64,64]{1,0:T(8,128)S(1)} %add_add_fusion.refs_0_), channel_id=1, source_target_pairs={{0,4},{4,0},{8,12},{12,8},{1,5},{5,1},{9,13},{13,9},{2,6},{6,2},{1... | collective-permute-start | bytes 49160 | tf_op jit(solution)/shard_map/ppermute | solution.py:437
  77.8 12.6 %collective-permute-start.20 = (bf16[8,64,256]{2,1,0:T(8,128)(2,1)S(1)}, bf16[8,64,256]{2,1,0:T(8,128)(2,1)S(1)}, u32[]{:S(2)}, u32[]{:S(2)}) collective-permute-start(bf16[8,64,256]{2,1,0:T(8,128)(2,1)S(1)} %get-tuple-element.42.frames_ref), channel_id=1, source_target_pairs={{0,1},{1,0},{2,3},{3,2},{4,5},{5,4},{6,7},{7,6},{8,9},{9,8},{10,11... | collective-permute-start | bytes 786440 | tf_op jit(solution)/shard_map/ppermute | solution.py:437
  77.8 21.4 %collective-permute-start.19 = (bf16[8,64,256]{2,1,0:T(8,128)(2,1)S(1)}, bf16[8,64,256]{2,1,0:T(8,128)(2,1)S(1)}, u32[]{:S(2)}, u32[]{:S(2)}) collective-permute-start(bf16[8,64,256]{2,1,0:T(8,128)(2,1)S(1)} %get-tuple-element.42.frames_ref), channel_id=1, source_target_pairs={{0,2},{1,3},{2,0},{3,1},{4,6},{5,7},{6,4},{7,5},{8,10},{9,11},{10,... | collective-permute-start | bytes 786440 | tf_op jit(solution)/shard_map/ppermute | solution.py:437
  79.7 25.3 %collective-permute-start.18 = (bf16[8,64,256]{2,1,0:T(8,128)(2,1)S(1)}, bf16[8,64,256]{2,1,0:T(8,128)(2,1)S(1)}, u32[]{:S(2)}, u32[]{:S(2)}) collective-permute-start(bf16[8,64,256]{2,1,0:T(8,128)(2,1)S(1)} %get-tuple-element.42.frames_ref), channel_id=1, source_target_pairs={{0,3},{1,2},{2,1},{3,0},{4,7},{5,6},{6,5},{7,4},{8,11},{9,10},{10,... | collective-permute-start | bytes 786440 | tf_op jit(solution)/shard_map/ppermute | solution.py:437
  113.6 8.4 %collective-permute-start.22 = (f32[64,1024]{1,0:T(8,128)S(1)}, f32[64,1024]{1,0:T(8,128)S(1)}, u32[]{:S(2)}, u32[]{:S(2)}) collective-permute-start(f32[64,1024]{1,0:T(8,128)S(1)} %add.15.refs_0_), channel_id=1, source_target_pairs={{0,8},{4,12},{8,0},{12,4},{1,9},{5,13},{9,1},{13,5},{2,10},{6,14},... | collective-permute-start | bytes 786440 | tf_op jit(solution)/shard_map/ppermute | solution.py:437
  138.9 5.3 %collective-permute-start.23 = (f32[64,128]{1,0:T(8,128)S(1)}, f32[64,128]{1,0:T(8,128)S(1)}, u32[]{:S(2)}, u32[]{:S(2)}) collective-permute-start(f32[64,128]{1,0:T(8,128)S(1)} %get-tuple-element.53.refs_0_), channel_id=1, source_target_pairs={{0,1},{1,0},{2,3},{3,2},{4,5},{5,4},{6,7},{7,6},{8,9},{9,8},{10,11... | collective-permute-start | bytes 98312 | tf_op jit(solution)/shard_map/ppermute | solution.py:437
  139.0 5.3 %collective-permute-start.24 = (f32[64,128]{1,0:T(8,128)S(1)}, f32[64,128]{1,0:T(8,128)S(1)}, u32[]{:S(2)}, u32[]{:S(2)}) collective-permute-start(f32[64,128]{1,0:T(8,128)S(1)} %get-tuple-element.53.refs_0_), channel_id=1, source_target_pairs={{0,2},{1,3},{2,0},{3,1},{4,6},{5,7},{6,4},{7,5},{8,10},{9,11},{10,... | collective-permute-start | bytes 98312 | tf_op jit(solution)/shard_map/ppermute | solution.py:437
  140.9 5.7 %collective-permute-start.25 = (f32[64,128]{1,0:T(8,128)S(1)}, f32[64,128]{1,0:T(8,128)S(1)}, u32[]{:S(2)}, u32[]{:S(2)}) collective-permute-start(f32[64,128]{1,0:T(8,128)S(1)} %get-tuple-element.53.refs_0_), channel_id=1, source_target_pairs={{0,3},{1,2},{2,1},{3,0},{4,7},{5,6},{6,5},{7,4},{8,11},{9,10},{10,... | collective-permute-start | bytes 98312 | tf_op jit(solution)/shard_map/ppermute | solution.py:437
  (31 other events, 171.2 us)

commit v2 on v0

v2 whole, which is shorter than its diff:
```python
import functools

import jax
import jax.numpy as jnp
from jax import lax
from jax.experimental import pallas as pl
from jax.experimental.pallas import tpu as pltpu
from jax.sharding import PartitionSpec as P

NS_STEPS = 12
LANES = 128
LEVELS = 32000.0
COARSE_STEPS = 3
SHORT = pl.CostEstimate(flops=1000, bytes_accessed=1000, transcendentals=0)

epsilon = 1e-06
HIGH = lax.Precision.HIGHEST
F32 = jnp.float32
BF16 = jnp.bfloat16
MIB = 1024 * 1024

ROWS_BY_COLS = (((1,), (0,)), ((), ()))
ROWS_BY_ROWS = (((1,), (1,)), ((), ()))
COLS_BY_COLS = (((0,), (0,)), ((), ()))


def low_dot(a, b, dims=ROWS_BY_COLS):
    return lax.dot_general(a, b, dims, preferred_element_type=F32)


def high_dot(a, b, dims=ROWS_BY_COLS):
    return lax.dot_general(a, b, dims, precision=HIGH, preferred_element_type=F32)


def two_parts(x):
    first = x.astype(BF16)
    return first, (x - first.astype(F32)).astype(BF16)


def three_parts(x):
    first = x.astype(BF16)
    rest = x - first.astype(F32)
    second = rest.astype(BF16)
    return first, second, (rest - second.astype(F32)).astype(BF16)


def lane_numbers(shape):
    return lax.broadcasted_iota(jnp.int32, shape, len(shape) - 1)


def batch_of(share):
    return 2 if share % 2 == 0 else 1


def whole(shape):
    return pl.BlockSpec(shape, lambda *place: (0,) * len(shape))


def parameters(mib):
    return pltpu.CompilerParams(vmem_limit_bytes=mib * MIB)


STREAM = 50
SMALL = 16
VMEM_SPEC = pl.BlockSpec(memory_space=pltpu.VMEM)
SMEM_SPEC = pl.BlockSpec(memory_space=pltpu.SMEM)


def exponent_rows(share):
    return -(-share // 16) * 16


def encode(proj, coded_ref, first_row, exponents, patient):
    top = jnp.max(jnp.abs(proj), axis=1, keepdims=True)
    exponent = jnp.ceil(jnp.log2(jnp.maximum(top, 1e-30)))
    coded = jnp.floor(proj * (LEVELS / jnp.exp2(exponent)) + 0.5)
    coded_ref[pl.ds(first_row, proj.shape[0]), :] = coded.astype(jnp.int32).astype(jnp.int16)
    return jnp.where(lane_numbers(exponents.shape) == patient, exponent, exponents)


def encode_batch(step, batch, share, v_ref, visits_ref, coded_ref, exponents_ref):
    rank = v_ref.shape[0]
    exponents = exponents_ref[...]
    for p in range(batch):
        proj = low_dot(v_ref[...], visits_ref[0, p], ROWS_BY_ROWS)
        row = pl.multiple_of((step * batch + p) * rank, rank)
        exponents = encode(proj, coded_ref, row, exponents, step * batch + p)
    exponents_ref[...] = exponents

    @pl.when(step == share // batch - 1)
    def _():
        rows = exponent_rows(share)
        last = exponents.T[:rows]
        last = jnp.concatenate([last, jnp.zeros((rows, coded_ref.shape[1] - rank), F32)], axis=1)
        coded_ref[pl.ds(share * rank, rows), :] = last.astype(jnp.int32).astype(jnp.int16)


def decode(coded_ref, share, rank):
    rows = exponent_rows(share)
    exponents = coded_ref[pl.ds(share * rank, rows), :LANES].astype(jnp.int32).astype(F32).T
    steps = jnp.exp2(exponents[:rank]) * (1.0 / LEVELS)
    return [
        coded_ref[pl.ds(p * rank, rank), :].astype(jnp.int32).astype(F32) * steps[:, p : p + 1]
        for p in range(share)
    ]


def send_projection_kernel(batch, share, place, v_ref, visits_ref, coded_ref, exponents_ref):
    step = pl.program_id(0)

    @pl.when(step == 0)
    def _():
        exponents_ref[...] = jnp.zeros_like(exponents_ref)

    encode_batch(step, batch, share, v_ref, visits_ref, coded_ref, exponents_ref)


def last_projection_kernel(
    batch, share, place, v_ref, w_ref, visits_ref, coded_ref, proj_ref, v_gram_ref, w_gram_ref, exponents_ref
):
    own = pl.program_id(0)
    step = pl.program_id(1)

    @pl.when((own == 0) & (step == 0))
    def _():
        exponents_ref[...] = jnp.zeros_like(exponents_ref)
        v_gram_ref[...] = low_dot(v_ref[...], v_ref[...], ROWS_BY_ROWS)
        w_gram_ref[...] = high_dot(w_ref[...], w_ref[...], COLS_BY_COLS)

    @pl.when(own == 0)
    def _():
        encode_batch(step, batch, share, v_ref, visits_ref, coded_ref, exponents_ref)

    @pl.when(own == 1)
    def _():
        for p in range(batch):
            proj_ref[p] = low_dot(v_ref[...], visits_ref[0, p], ROWS_BY_ROWS)


def project_for(slot, place, visits, v_rows):
    _, share, slots, width = visits.shape
    rank = v_rows.shape[0]
    batch = batch_of(share)
    coded = (share * rank + exponent_rows(share), slots)
    return pl.pallas_call(
        functools.partial(send_projection_kernel, batch, share),
        grid_spec=pltpu.PrefetchScalarGridSpec(
            num_scalar_prefetch=1,
            grid=(share // batch,),
            in_specs=[
                whole(v_rows.shape),
                pl.BlockSpec((1, batch, slots, width), lambda i, place: (place[0] ^ slot, i, 0, 0)),
            ],
            out_specs=whole(coded),
            scratch_shapes=[pltpu.VMEM((rank, LANES), F32)],
        ),
        out_shape=jax.ShapeDtypeStruct(coded, jnp.int16),
        compiler_params=parameters(STREAM),
        cost_estimate=SHORT,
        name="project_send",
    )(place, v_rows, visits)


def project_last(place, visits, v_rows, w_start):
    _, share, slots, width = visits.shape
    rank = v_rows.shape[0]
    batch = batch_of(share)
    coded = (share * rank + exponent_rows(share), slots)
    gram = (rank, rank)
    return pl.pallas_call(
        functools.partial(last_projection_kernel, batch, share),
        grid_spec=pltpu.PrefetchScalarGridSpec(
            num_scalar_prefetch=1,
            grid=(2, share // batch),
            in_specs=[
                whole(v_rows.shape),
                whole(w_start.shape),
                pl.BlockSpec((1, batch, slots, width), lambda own, i, place: (place[0] ^ (1 - own), i, 0, 0)),
            ],
            out_specs=[
                whole(coded),
                pl.BlockSpec((batch, rank, slots), lambda own, i, place: (i * own, 0, 0)),
                whole(gram),
                whole(gram),
            ],
            scratch_shapes=[pltpu.VMEM((rank, LANES), F32)],
        ),
        out_shape=[
            jax.ShapeDtypeStruct(coded, jnp.int16),
            jax.ShapeDtypeStruct((share, rank, slots), F32),
            jax.ShapeDtypeStruct(gram, F32),
            jax.ShapeDtypeStruct(gram, F32),
        ],
        compiler_params=parameters(STREAM),
        cost_estimate=SHORT,
        name="project_last",
    )(place, v_rows, w_start, visits)


def eliminate(table, rank):
    rows = lax.broadcasted_iota(jnp.int32, table.shape, 0)
    for i in range(0, rank, 2):
        first = jnp.broadcast_to(table[:, i : i + 1], table.shape)
        second = jnp.broadcast_to(table[:, i + 1 : i + 2], table.shape)
        row_first, row_second = table[i : i + 1], table[i + 1 : i + 2]
        a, b = first[i : i + 1], second[i : i + 1]
        c, d = first[i + 1 : i + 2], second[i + 1 : i + 2]
        scale = 1.0 / (a * d - b * c)
        new_first = (d * row_first - b * row_second) * scale
        new_second = (a * row_second - c * row_first) * scale
        table = table - first * new_first - second * new_second
        table = jnp.where(rows == i, new_first, jnp.where(rows == i + 1, new_second, table))
    return table


def inverse_of(gram):
    rank = gram.shape[0]
    eye = (lax.broadcasted_iota(jnp.int32, gram.shape, 0) == lane_numbers(gram.shape)).astype(F32)
    return eliminate(jnp.concatenate([gram, eye], axis=1), rank)[:, rank:]


def total(refs):
    out = refs[0][...]
    for ref in refs[1:]:
        out = out + ref[...]
    return out


def first_inverse_kernel(n_v, *refs):
    w_gram_ref, inverse_ref = refs[-2:]
    w_gram = total(refs[n_v:-2])
    w_gram_ref[...] = w_gram
    inverse_ref[...] = inverse_of(w_gram * total(refs[:n_v]))


def first_inverse(v_grams, w_grams):
    out = jax.ShapeDtypeStruct(w_grams[0].shape, F32)
    return pl.pallas_call(
        functools.partial(first_inverse_kernel, len(v_grams)),
        out_shape=[out, out],
        compiler_params=parameters(SMALL),
        cost_estimate=SHORT,
        name="first_inverse",
    )(*v_grams, *w_grams)


def sweep_once(frames, p, rank, fine):
    frame = frames[p]
    first, second = two_parts(frame)
    if fine:
        both = low_dot(jnp.concatenate([first, second], axis=0), first, ROWS_BY_ROWS)
        gram = both[:rank] + both[rank:] + low_dot(first, second, ROWS_BY_ROWS)
        gram_first, gram_second = two_parts(gram)
        moved = low_dot(jnp.concatenate([gram_first, gram_second], axis=0), first)
        moved = moved[:rank] + moved[rank:] + low_dot(gram_first, second)
    else:
        moved = low_dot(low_dot(first, first, ROWS_BY_ROWS).astype(BF16), first)
    frames[p] = 1.5 * frame - 0.5 * moved


def frames_kernel(share, n_slots, place, counts_ref, h_ref, w_ref, own_ref, *refs):
    coded = refs[: n_slots - 1]
    frames_ref, terms_ref, proj, frames = refs[n_slots - 1 :]
    first = place[0] * share
    rank, slots = frames.shape[1:]
    pieces = [own_ref[p] for p in range(share)]
    for code in coded:
        pieces = [a + b for a, b in zip(pieces, decode(code, share, rank))]
    for p, piece in enumerate(pieces):
        proj[p] = piece
        mixed = high_dot(h_ref[...] * w_ref[pl.ds(first + p, 1), :], piece)
        mixed = jnp.where(lane_numbers((rank, slots)) < counts_ref[first + p], mixed, 0.0)
        energy = jnp.sum(jnp.sum(mixed * mixed, axis=1, keepdims=True), axis=0, keepdims=True)
        frames[p] = mixed * lax.rsqrt(energy + epsilon)

    def sweep(fine, step, carry):
        for p in range(share):
            sweep_once(frames, p, rank, fine)
        return carry

    lax.fori_loop(0, COARSE_STEPS, functools.partial(sweep, False), 0)
    lax.fori_loop(COARSE_STEPS, NS_STEPS, functools.partial(sweep, True), 0)
    terms = jnp.zeros((rank, rank), F32)
    for p in range(share):
        low = frames[p].astype(BF16)
        frames_ref[p] = low
        parts = three_parts(proj[p])
        product = low_dot(low, parts[0], ROWS_BY_ROWS)
        for part in parts[1:]:
            product = product + low_dot(low, part, ROWS_BY_ROWS)
        terms = terms + product * w_ref[pl.ds(first + p, 1), :]
    terms_ref[...] = terms


def own_frames(place, counts, h_start, w_start, own, coded):
    share, rank, slots = own.shape
    return pl.pallas_call(
        functools.partial(frames_kernel, share, len(coded) + 1),
        in_specs=[SMEM_SPEC] * 2 + [VMEM_SPEC] * (3 + len(coded)),
        out_specs=[VMEM_SPEC] * 2,
        out_shape=[
            jax.ShapeDtypeStruct(own.shape, BF16),
            jax.ShapeDtypeStruct((rank, rank), F32),
        ],
        scratch_shapes=[pltpu.VMEM(own.shape, F32)] * 2,
        compiler_params=parameters(SMALL),
        cost_estimate=SHORT,
        name="own_frames",
    )(place, counts, h_start, w_start, own, *coded)


def projected_kernel(batch, place, frames_ref, visits_ref, *refs):
    first_ref, second_ref = refs[-2:]
    rank = frames_ref.shape[1]
    for p in range(batch):
        rows = slice(p * rank, (p + 1) * rank)
        first_ref[0, rows], second_ref[0, rows] = two_parts(low_dot(frames_ref[p], visits_ref[0, p]))


def project_frames(slot, place, frames, visits, before):
    n_slots, share, slots, width = visits.shape
    rank = frames.shape[1]
    batch = batch_of(share)
    out = jax.ShapeDtypeStruct((n_slots, share * rank, width), BF16)
    return pl.pallas_call(
        functools.partial(projected_kernel, batch),
        grid_spec=pltpu.PrefetchScalarGridSpec(
            num_scalar_prefetch=1,
            grid=(share // batch,),
            in_specs=[
                pl.BlockSpec((batch, rank, slots), lambda i, place: (i, 0, 0)),
                pl.BlockSpec((1, batch, slots, width), lambda i, place: (place[0] ^ slot, i, 0, 0)),
            ]
            + [pl.BlockSpec(memory_space=pl.ANY)] * len(before),
            out_specs=[pl.BlockSpec((1, batch * rank, width), lambda i, place: (slot, i, 0))] * 2,
        ),
        out_shape=[out] * 2,
        input_output_aliases={3: 0, 4: 1} if before else {},
        compiler_params=parameters(STREAM),
        cost_estimate=SHORT,
        name="project_frames",
    )(place, frames, visits, *before)


def next_h_kernel(n_terms, n_slots, place, *refs):
    inverse_ref, w_ref, h_ref, factor_ref = refs[n_terms:]
    h_next = high_dot(total(refs[:n_terms]), inverse_ref[...])
    h_ref[...] = h_next
    rank = h_next.shape[0]
    patients = w_ref.shape[0]
    share = patients // n_slots
    h_rows = h_next.T
    w_rows = jnp.concatenate([w_ref[...], jnp.zeros((LANES - patients, rank), F32)], axis=0)
    w_columns = w_rows.T
    for slot in range(n_slots):
        first = (place[0] ^ slot) * share
        columns = pltpu.roll(w_columns, jnp.where(first == 0, 0, LANES - first), 1)
        factor = jnp.concatenate([h_rows * columns[:, p : p + 1] for p in range(share)], axis=1)
        factor_ref[slot] = jnp.concatenate(three_parts(factor), axis=0)


def next_h(place, terms, inverse, w_start, n_slots):
    patients, rank = w_start.shape
    share = patients // n_slots
    return pl.pallas_call(
        functools.partial(next_h_kernel, len(terms), n_slots),
        in_specs=[SMEM_SPEC] + [VMEM_SPEC] * (len(terms) + 2),
        out_specs=[VMEM_SPEC] * 2,
        out_shape=[
            jax.ShapeDtypeStruct(inverse.shape, F32),
            jax.ShapeDtypeStruct((n_slots, 3 * rank, share * rank), BF16),
        ],
        compiler_params=parameters(SMALL),
        cost_estimate=SHORT,
        name="next_h",
    )(place, *terms, inverse, w_start)


def second_inverse_kernel(h_ref, w_gram_ref, gram_ref, inverse_ref):
    gram = high_dot(h_ref[...], h_ref[...], COLS_BY_COLS)
    gram_ref[...] = gram
    inverse_ref[...] = inverse_of(gram * w_gram_ref[...])


def second_inverse(h_next, w_gram):
    out = jax.ShapeDtypeStruct(w_gram.shape, F32)
    return pl.pallas_call(
        second_inverse_kernel,
        out_shape=[out, out],
        compiler_params=parameters(SMALL),
        cost_estimate=SHORT,
        name="second_inverse",
    )(h_next, w_gram)


def v_terms_kernel(factor_ref, first_ref, second_ref, terms_ref):
    step = pl.program_id(0)
    rank = terms_ref.shape[0]
    large = low_dot(factor_ref[0], first_ref[0])
    small = low_dot(factor_ref[0, : 2 * rank], second_ref[0])
    terms = large[:rank] + (large[rank : 2 * rank] + small[:rank]) + (large[2 * rank :] + small[rank:])

    @pl.when(step == 0)
    def _():
        terms_ref[...] = terms

    @pl.when(step > 0)
    def _():
        terms_ref[...] += terms


def all_v_terms(factor, first, second):
    n_slots, rows, width = first.shape
    rank = factor.shape[1] // 3
    return pl.pallas_call(
        v_terms_kernel,
        grid=(n_slots,),
        in_specs=[
            pl.BlockSpec((1, 3 * rank, rows), lambda i: (i, 0, 0)),
            pl.BlockSpec((1, rows, width), lambda i: (i, 0, 0)),
            pl.BlockSpec((1, rows, width), lambda i: (i, 0, 0)),
        ],
        out_specs=whole((rank, width)),
        out_shape=jax.ShapeDtypeStruct((rank, width), F32),
        compiler_params=parameters(STREAM),
        cost_estimate=SHORT,
        name="v_terms",
    )(factor, first, second)


def next_v_kernel(n_terms, share, place, *refs):
    inverse_ref, h_ref, first_ref, second_ref, v_ref, sums_ref, v_parts, weights = refs[n_terms:]
    slot = pl.program_id(0)
    rank = inverse_ref.shape[0]

    @pl.when(slot == 0)
    def _():
        v_rows = high_dot(inverse_ref[...], total(refs[:n_terms]))
        v_ref[...] = v_rows
        v_parts[...] = jnp.concatenate(two_parts(v_rows), axis=0)
        weights[...] = jnp.concatenate([h_ref[...]] * 2, axis=1)
        gram = high_dot(v_rows, v_rows, ROWS_BY_ROWS)
        sums_ref[...] = jnp.concatenate([jnp.zeros((rank, rank), F32), gram], axis=1)

    seen = low_dot(first_ref[0], v_parts[...], ROWS_BY_ROWS) + low_dot(second_ref[0], v_parts[...], ROWS_BY_ROWS)
    first = (place[0] ^ slot) * share
    for p in range(share):
        row = jnp.sum(seen[p * rank : (p + 1) * rank] * weights[...], axis=0, keepdims=True)
        sums_ref[pl.ds(first + p, 1), :rank] = row[:, :rank] + row[:, rank:]


def next_v(place, terms, inverse, h_next, first, second):
    n_slots, rows, width = first.shape
    rank = inverse.shape[0]
    return pl.pallas_call(
        functools.partial(next_v_kernel, len(terms), rows // rank),
        grid_spec=pltpu.PrefetchScalarGridSpec(
            num_scalar_prefetch=1,
            grid=(n_slots,),
            in_specs=[whole((rank, width))] * len(terms)
            + [whole((rank, rank))] * 2
            + [pl.BlockSpec((1, rows, width), lambda i, place: (i, 0, 0))] * 2,
            out_specs=[whole((rank, width)), whole((rank, 2 * rank))],
            scratch_shapes=[pltpu.VMEM((2 * rank, width), BF16), pltpu.VMEM((rank, 2 * rank), F32)],
        ),
        out_shape=[
            jax.ShapeDtypeStruct((rank, width), F32),
            jax.ShapeDtypeStruct((rank, 2 * rank), F32),
        ],
        compiler_params=parameters(STREAM),
        cost_estimate=SHORT,
        name="next_v",
    )(place, *terms, inverse, h_next, first, second)


def next_w_kernel(n_sums, *refs):
    gram_ref, w_ref = refs[n_sums:]
    patients, rank = w_ref.shape
    sums = total(refs[:n_sums])
    table = jnp.concatenate([sums[:, rank:] * gram_ref[...], sums.T[:rank]], axis=1)
    w_ref[...] = eliminate(table, rank).T[rank : rank + patients]


def next_w(sums, h_gram, patients):
    rank = h_gram.shape[0]
    return pl.pallas_call(
        functools.partial(next_w_kernel, len(sums)),
        out_shape=jax.ShapeDtypeStruct((patients, rank), F32),
        compiler_params=parameters(SMALL),
        cost_estimate=SHORT,
        name="next_w",
    )(*sums, h_gram)


def swap(x, axis, slot):
    pairs = [(i, i ^ slot) for i in range(lax.axis_size(axis))]
    return lax.ppermute(x, axis, pairs)


def all_terms(x, axis):
    n = lax.axis_size(axis)
    if n > 4:
        return [lax.psum(x, axis)]
    return [x] + [swap(x, axis, s) for s in range(1, n)]


def staged_terms(x, axis):
    n = lax.axis_size(axis)
    step = 1
    while 2 * step < n:
        x = x + swap(x, axis, step)
        step *= 2
    return [x, swap(x, axis, step)]


def on_device(visits, visit_counts, h_start, v_start, w_start):
    n = lax.axis_size("feature")
    patients, slots, width = visits.shape
    share = patients // n
    place = lax.axis_index("feature").astype(jnp.int32).reshape(1)
    by_owner = visits.reshape(n, share, slots, width)
    v_rows = v_start.T

    coded = [swap(project_for(slot, place, by_owner, v_rows), "feature", slot) for slot in range(n - 1, 1, -1)]
    code, own, v_local, w_local = project_last(place, by_owner, v_rows, w_start)
    coded.append(swap(code, "feature", 1))
    w_gram, first = first_inverse(all_terms(v_local, "feature"), all_terms(w_local, "patient"))

    frames, h_local = own_frames(place, visit_counts, h_start, w_start, own, coded)
    order = list(range(n - 1, 0, -1))
    all_frames = {0: frames} | {slot: swap(frames, "feature", slot) for slot in order}
    h_terms = all_terms(sum(all_terms(h_local, "feature")), "patient")
    h_next, factor = next_h(place, h_terms, first, w_start, n)

    before = []
    for slot in [0, 1] + order[:-1]:
        before = project_frames(slot, place, all_frames[slot], by_owner, before)
    v_terms = staged_terms(all_v_terms(factor, *before), "patient")
    h_gram, second = second_inverse(h_next, w_gram)
    v_next, sums = next_v(place, v_terms, second, h_next, *before)
    w_next = next_w(all_terms(sums, "feature"), h_gram, patients)
    return (h_next, v_next.T, w_next)


def solution(mesh):
    return jax.shard_map(
        on_device,
        mesh=mesh,
        in_specs=(
            P(("groups", "patient"), None, "feature"),
            P(("groups", "patient")),
            P(),
            P("feature", None),
            P(("groups", "patient"), None),
        ),
        out_specs=(P(None, "groups"), P("feature", "groups"), P("patient", "groups")),
        check_vma=False,
    )
```

time: 311 us -> 140 us (0.45)
  blocking collectives: 107 us -> 0 us
  matrix products: 74.2 us -> 0 us
  Pallas kernels: 0 us -> 70.3 us
  other arithmetic: 37.2 us -> 0.04 us
  waiting for transfers between devices: 72.1 us -> 36.6 us
  starting transfers between devices: 0.12 us -> 29.5 us
  between operations: 14.1 us -> 0.74 us
  local copies, waits for them, and re-layouts: 5.86 us -> 1.63 us
    psum x4 -> x0, blocking collectives: 107 us -> none  [the longest x1 58.3 us: on_device(): h_terms = lax.psum(h_local, ('patient', 'feature'))]
    dot_general x35 -> x0, matrix products: 70.6 us -> none  [the longest x1 16.2 us: on_device(): v_local_terms = jnp.einsum('krj,krc->jc', projected, factor, precision=HIGH)]
    pallas_call x0 -> x14, Pallas kernels: none -> 70.3 us  [the longest x4 18.9 us: project_frames(): pl.pallas_call(functools.partial(projected_kernel, batch), grid_spec=pltp...]
    reduce_scatter x1 -> x0, waiting for transfers between devices: 46.5 us -> none  [on_device(): lax.psum_scatter(project(visits, v_start), 'feature', scatter_dimension=0...]
    ppermute x0 -> x23, waiting for transfers between devices: none -> 36.6 us  [swap(): return lax.ppermute(x, axis, pairs)]
    another operation x15 -> x0, other arithmetic: 36.2 us -> none  [the longest x9 19.6 us: solve_right(): lower = jnp.linalg.cholesky(gram)]
    ppermute x0 -> x23, starting transfers between devices: none -> 29.5 us  [swap(): return lax.ppermute(x, axis, pairs)]
    psum x1 -> x0, waiting for transfers between devices: 25.5 us -> none  [on_device(): v_terms = lax.psum(v_local_terms, 'patient')]
  transfers between devices with their start and end apart: 3 -> 23, of which waited for: 2 -> 8; matrix products, arithmetic and copies ran while one was open for 6% -> 0% of each run, Pallas kernels for 0% -> 30%
where the time goes in v2:
time: 140 us; the launch traced here: 139 us
  Pallas kernels  70.3 us (50%)
  waiting for transfers between devices  36.6 us (26%)
  starting transfers between devices  29.5 us (21%)
  local copies, waits for them, and re-layouts  1.63 us (1%)
    ppermute x23, waiting for transfers between devices, swap(): return lax.ppermute(x, axis, pairs)  36.6 us
    ppermute x23, starting transfers between devices, swap(): return lax.ppermute(x, axis, pairs)  29.5 us
    pallas_call x4, Pallas kernels, project_frames(): pl.pallas_call(functools.partial(projected_kernel, batch), grid_spec=pltp...  18.9 us
    pallas_call x1, Pallas kernels, own_frames(): pl.pallas_call(functools.partial(frames_kernel, share, len(coded) + 1), i...  10.9 us
    pallas_call x2, Pallas kernels, project_for(): pl.pallas_call(functools.partial(send_projection_kernel, batch, share), g...  8.61 us
    pallas_call x1, Pallas kernels, project_last(): pl.pallas_call(functools.partial(last_projection_kernel, batch, share), g...  8.1 us
    pallas_call x1, Pallas kernels, next_v(): pl.pallas_call(functools.partial(next_v_kernel, len(terms), rows // rank)...  6.93 us
    pallas_call x1, Pallas kernels, all_v_terms(): pl.pallas_call(v_terms_kernel, grid=(n_slots,), in_specs=[pl.BlockSpec((1...  5 us
  transfers between devices with their start and end apart: 23, of which 8 were waited for; matrix products, arithmetic and copies ran while one was open for 0% of the time, Pallas kernels for 30%

profile of v2, /device:TPU:0, one launch (start us, length us, event | category | flops | bytes accessed | tf_op | source)
XLA Modules:
  0.0 138.9 jit_solution(12111662640248561070)
XLA Ops:
  2.3 8.1 %project_last.1 = (s16[528,256]{1,0:T(8,128)(2,1)S(1)}, f32[8,64,256]{2,1,0:T(8,128)S(1)}, f32[64,64]{1,0:T(8,128)S(1)}, f32[64,64]{1,0:T(8,128)S(1)}) custom-call(s32[1]{0:T(128)} %bitcast.place, bf16[64,1024]{1,0:T(8,128)(2,1)S(1)} %bitcast.4, f32[32,64]{1,0:T(8,128)S(1)} %copy-done.1, bf16[4,8,256,1024]{3,2,1,0:T(8,128)(2,1)} %bitcast.7), custom_call_target="tpu_custom_call" | custom-call | flops 1000 | bytes 1000 | tf_op jit(solution)/shard_map/project_last/pallas_call | solution.py:170
  10.4 3.1 %collective-permute-start.2 = (s16[528,256]{1,0:T(8,128)(2,1)S(1)}, s16[528,256]{1,0:T(8,128)(2,1)S(1)}, u32[]{:S(2)}, u32[]{:S(2)}) collective-permute-start(s16[528,256]{1,0:T(8,128)(2,1)S(1)} %get-tuple-element.26), channel_id=1, source_target_pairs={{0,1},{1,0},{2,3},{3,2},{4,5},{5,4},{6,7},{7,6},{8,9},{9,8},{10,11... | collective-permute-start | bytes 811016 | tf_op jit(solution)/shard_map/ppermute | solution.py:497
  13.4 4.3 %project_send.2 = s16[528,256]{1,0:T(8,128)(2,1)S(1)} custom-call(s32[1]{0:T(128)} %bitcast.place, bf16[64,1024]{1,0:T(8,128)(2,1)S(1)} %bitcast.5, bf16[4,8,256,1024]{3,2,1,0:T(8,128)(2,1)} %bitcast.8), custom_call_target="tpu_custom_call" | custom-call | flops 1000 | bytes 1000 | tf_op jit(solution)/shard_map/project_send/pallas_call | solution.py:145
  17.8 2.5 %collective-permute-start = (s16[528,256]{1,0:T(8,128)(2,1)S(1)}, s16[528,256]{1,0:T(8,128)(2,1)S(1)}, u32[]{:S(2)}, u32[]{:S(2)}) collective-permute-start(s16[528,256]{1,0:T(8,128)(2,1)S(1)} %project_send.2), channel_id=1, source_target_pairs={{0,3},{1,2},{2,1},{3,0},{4,7},{5,6},{6,5},{7,4},{8,11},{9,10},{10,... | collective-permute-start | bytes 811016 | tf_op jit(solution)/shard_map/ppermute | solution.py:497
  20.3 4.3 %project_send.3 = s16[528,256]{1,0:T(8,128)(2,1)S(1)} custom-call(s32[1]{0:T(128)} %bitcast.place, bf16[64,1024]{1,0:T(8,128)(2,1)S(1)} %bitcast.6, bf16[4,8,256,1024]{3,2,1,0:T(8,128)(2,1)} %bitcast.9), custom_call_target="tpu_custom_call" | custom-call | flops 1000 | bytes 1000 | tf_op jit(solution)/shard_map/project_send/pallas_call | solution.py:145
  24.8 2.8 %collective-permute-start.10 = (f32[64,64]{1,0:T(8,128)S(1)}, f32[64,64]{1,0:T(8,128)S(1)}, u32[]{:S(2)}, u32[]{:S(2)}) collective-permute-start(f32[64,64]{1,0:T(8,128)S(1)} %get-tuple-element.28.refs_0_), channel_id=1, source_target_pairs={{0,2},{1,3},{2,0},{3,1},{4,6},{5,7},{6,4},{7,5},{8,10},{9,11},{10,... | collective-permute-start | bytes 49160 | tf_op jit(solution)/shard_map/ppermute | solution.py:497
  29.0 17.2 %collective-permute-done.1.refs_1_ = s16[528,256]{1,0:T(8,128)(2,1)S(1)} collective-permute-done((s16[528,256]{1,0:T(8,128)(2,1)S(1)}, s16[528,256]{1,0:T(8,128)(2,1)S(1)}, u32[]{:S(2)}, u32[]{:S(2)}) %collective-permute-start.1) | collective-permute-done | bytes 270368 | tf_op jit(solution)/shard_map/ppermute | solution.py:497
  46.1 10.9 %own_frames.1 = (bf16[8,64,256]{2,1,0:T(8,128)(2,1)S(1)}, f32[64,64]{1,0:T(8,128)S(1)}) custom-call(s32[1]{0:T(128)} %bitcast.place, s32[32]{0:T(128)S(1)} %copy-done.5, f32[64,64]{1,0:T(8,128)S(1)} %copy-done.4, f32[32,64]{1,0:T(8,128)S(1)} %copy-done.2, f32[8,64,256]{2,1,0:T(8,128)S(1)} %get-tuple-element.25.own_ref, ...), custom_call_target="tpu_custom_call" | custom-call | flops 1000 | bytes 1000 | tf_op jit(solution)/shard_map/own_frames/pallas_call | solution.py:297
  57.2 3.2 %collective-permute-start.4 = (f32[64,64]{1,0:T(8,128)S(1)}, f32[64,64]{1,0:T(8,128)S(1)}, u32[]{:S(2)}, u32[]{:S(2)}) collective-permute-start(f32[64,64]{1,0:T(8,128)S(1)} %get-tuple-element.27), channel_id=1, source_target_pairs={{0,2},{1,3},{2,0},{3,1},{4,6},{5,7},{6,4},{7,5},{8,10},{9,11},{10,... | collective-permute-start | bytes 49160 | tf_op jit(solution)/shard_map/ppermute | solution.py:497
  61.6 2.7 %collective-permute-start.16 = (bf16[8,64,256]{2,1,0:T(8,128)(2,1)S(1)}, bf16[8,64,256]{2,1,0:T(8,128)(2,1)S(1)}, u32[]{:S(2)}, u32[]{:S(2)}) collective-permute-start(bf16[8,64,256]{2,1,0:T(8,128)(2,1)S(1)} %get-tuple-element.33.frames_ref), channel_id=1, source_target_pairs={{0,3},{1,2},{2,1},{3,0},{4,7},{5,6},{6,5},{7,4},{8,11},{9,10},{10,... | collective-permute-start | bytes 786440 | tf_op jit(solution)/shard_map/ppermute | solution.py:497
  66.6 2.4 %collective-permute-done.13.refs_6_ = f32[64,64]{1,0:T(8,128)S(1)} collective-permute-done((f32[64,64]{1,0:T(8,128)S(1)}, f32[64,64]{1,0:T(8,128)S(1)}, u32[]{:S(2)}, u32[]{:S(2)}) %collective-permute-start.13) | collective-permute-done | bytes 16416 | tf_op jit(solution)/shard_map/ppermute | solution.py:497
  70.3 7.7 %collective-permute-done.9.refs_1_ = f32[64,64]{1,0:T(8,128)S(1)} collective-permute-done((f32[64,64]{1,0:T(8,128)S(1)}, f32[64,64]{1,0:T(8,128)S(1)}, u32[]{:S(2)}, u32[]{:S(2)}) %collective-permute-start.9) | collective-permute-done | bytes 16416 | tf_op jit(solution)/shard_map/ppermute | solution.py:497
  79.5 3.3 %first_inverse.1 = (f32[64,64]{1,0:T(8,128)S(1)}, f32[64,64]{1,0:T(8,128)S(1)}) custom-call(f32[64,64]{1,0:T(8,128)S(1)} %get-tuple-element.28.refs_0_, f32[64,64]{1,0:T(8,128)S(1)} %collective-permute-done.9.refs_1_, f32[64,64]{1,0:T(8,128)S(1)} %collective-permute-done.10.refs_2_, f32[64,64]{1,0:T(8,128)S(1)} %collective-permute-done.11.refs_3_, ...), custom_call_target="tpu_custom_call" | custom-call | flops 1000 | bytes 1000 | tf_op jit(solution)/shard_map/first_inverse/pallas_call | solution.py:238
  82.8 4.7 %project_frames.4 = (bf16[4,512,1024]{2,1,0:T(8,128)(2,1)}, bf16[4,512,1024]{2,1,0:T(8,128)(2,1)}) custom-call(s32[1]{0:T(128)} %bitcast.place, bf16[8,64,256]{2,1,0:T(8,128)(2,1)S(1)} %get-tuple-element.33.frames_ref, bf16[4,8,256,1024]{3,2,1,0:T(8,128)(2,1)} %bitcast.10), custom_call_target="tpu_custom_call" | custom-call | flops 1000 | bytes 1000 | tf_op jit(solution)/shard_map/project_frames/pallas_call | solution.py:325
  88.6 4.7 %project_frames.5 = (bf16[4,512,1024]{2,1,0:T(8,128)(2,1)}, bf16[4,512,1024]{2,1,0:T(8,128)(2,1)}) custom-call(s32[1]{0:T(128)} %bitcast.place, bf16[8,64,256]{2,1,0:T(8,128)(2,1)S(1)} %collective-permute-done.17.frames_ref, bf16[4,8,256,1024]{3,2,1,0:T(8,128)(2,1)} %bitcast.11, ...), custom_call_target="tpu_custom_call", output_to_operand_aliasing={{0}: (3, {}), {1}: (4, {})} | custom-call | flops 1000 | bytes 1000 | tf_op jit(solution)/shard_map/project_frames/pallas_call | solution.py:325
  93.4 4.8 %project_frames.6 = (bf16[4,512,1024]{2,1,0:T(8,128)(2,1)}, bf16[4,512,1024]{2,1,0:T(8,128)(2,1)}) custom-call(s32[1]{0:T(128)} %bitcast.place, bf16[8,64,256]{2,1,0:T(8,128)(2,1)S(1)} %collective-permute-done.16.frames_ref, bf16[4,8,256,1024]{3,2,1,0:T(8,128)(2,1)} %bitcast.12, ...), custom_call_target="tpu_custom_call", output_to_operand_aliasing={{0}: (3, {}), {1}: (4, {})} | custom-call | flops 1000 | bytes 1000 | tf_op jit(solution)/shard_map/project_frames/pallas_call | solution.py:325
  98.1 4.7 %project_frames.7 = (bf16[4,512,1024]{2,1,0:T(8,128)(2,1)}, bf16[4,512,1024]{2,1,0:T(8,128)(2,1)}) custom-call(s32[1]{0:T(128)} %bitcast.place, bf16[8,64,256]{2,1,0:T(8,128)(2,1)S(1)} %collective-permute-done.15.frames_ref, bf16[4,8,256,1024]{3,2,1,0:T(8,128)(2,1)} %bitcast.13, ...), custom_call_target="tpu_custom_call", output_to_operand_aliasing={{0}: (3, {}), {1}: (4, {})} | custom-call | flops 1000 | bytes 1000 | tf_op jit(solution)/shard_map/project_frames/pallas_call | solution.py:325
  102.8 5.0 %v_terms.1 = f32[64,1024]{1,0:T(8,128)S(1)} custom-call(bf16[4,192,512]{2,1,0:T(8,128)(2,1)S(1)} %get-tuple-element.32.factor_ref, bf16[4,512,1024]{2,1,0:T(8,128)(2,1)} %get-tuple-element.40.first_ref.refs_4_, bf16[4,512,1024]{2,1,0:T(8,128)(2,1)} %get-tuple-element.41.second_ref.refs_5_), custom_call_target="tpu_custom_call" | custom-call | flops 1000 | bytes 1000 | tf_op jit(solution)/shard_map/v_terms/pallas_call | solution.py:415
  111.3 3.5 %second_inverse.1 = (f32[64,64]{1,0:T(8,128)S(1)}, f32[64,64]{1,0:T(8,128)S(1)}) custom-call(f32[64,64]{1,0:T(8,128)S(1)} %copy-done.3, f32[64,64]{1,0:T(8,128)S(1)} %get-tuple-element.42.w_gram_ref), custom_call_target="tpu_custom_call" | custom-call | flops 1000 | bytes 1000 | tf_op jit(solution)/shard_map/second_inverse/pallas_call | solution.py:387
  114.8 3.6 %collective-permute-done.19.refs_1_ = f32[64,1024]{1,0:T(8,128)S(1)} collective-permute-done((f32[64,1024]{1,0:T(8,128)S(1)}, f32[64,1024]{1,0:T(8,128)S(1)}, u32[]{:S(2)}, u32[]{:S(2)}) %collective-permute-start.19) | collective-permute-done | bytes 262176 | tf_op jit(solution)/shard_map/ppermute | solution.py:497
  118.4 6.9 %next_v.1 = (f32[64,1024]{1,0:T(8,128)}, f32[64,128]{1,0:T(8,128)S(1)}) custom-call(s32[1]{0:T(128)} %bitcast.place, f32[64,1024]{1,0:T(8,128)S(1)} %add.15.refs_0_, f32[64,1024]{1,0:T(8,128)S(1)} %collective-permute-done.19.refs_1_, f32[64,64]{1,0:T(8,128)S(1)} %get-tuple-element.43.refs_2_, f32[64,64]{1,0:T(8,128)S(1)} %copy-done.3, ...), custom_call_target="tpu_custom_call" | custom-call | flops 1000 | bytes 1000 | tf_op jit(solution)/shard_map/next_v/pallas_call | solution.py:455
  125.3 2.5 %collective-permute-start.20 = (f32[64,128]{1,0:T(8,128)S(1)}, f32[64,128]{1,0:T(8,128)S(1)}, u32[]{:S(2)}, u32[]{:S(2)}) collective-permute-start(f32[64,128]{1,0:T(8,128)S(1)} %get-tuple-element.45.refs_0_), channel_id=1, source_target_pairs={{0,1},{1,0},{2,3},{3,2},{4,5},{5,4},{6,7},{7,6},{8,9},{9,8},{10,11... | collective-permute-start | bytes 98312 | tf_op jit(solution)/shard_map/ppermute | solution.py:497
  130.7 3.0 %collective-permute-done.21.refs_2_ = f32[64,128]{1,0:T(8,128)S(1)} collective-permute-done((f32[64,128]{1,0:T(8,128)S(1)}, f32[64,128]{1,0:T(8,128)S(1)}, u32[]{:S(2)}, u32[]{:S(2)}) %collective-permute-start.21) | collective-permute-done | bytes 32800 | tf_op jit(solution)/shard_map/ppermute | solution.py:497
  134.9 4.0 %next_w.1 = f32[32,64]{1,0:T(8,128)} custom-call(f32[64,128]{1,0:T(8,128)S(1)} %get-tuple-element.45.refs_0_, f32[64,128]{1,0:T(8,128)S(1)} %collective-permute-done.20.refs_1_, f32[64,128]{1,0:T(8,128)S(1)} %collective-permute-done.21.refs_2_, f32[64,128]{1,0:T(8,128)S(1)} %collective-permute-done.22.refs_3_, f32[64,64]{1,0:T(8,128)S(1)} %get-tuple-element.46.refs_4_), custom_call_target="tpu_custom_call" | custom-call | flops 1000 | bytes 1000 | tf_op jit(solution)/shard_map/next_w/pallas_call | solution.py:486
  (50 shorter events, 18.3 us)
Async XLA Ops:
  10.4 18.6 %collective-permute-start.2 = (s16[528,256]{1,0:T(8,128)(2,1)S(1)}, s16[528,256]{1,0:T(8,128)(2,1)S(1)}, u32[]{:S(2)}, u32[]{:S(2)}) collective-permute-start(s16[528,256]{1,0:T(8,128)(2,1)S(1)} %get-tuple-element.26), channel_id=1, source_target_pairs={{0,1},{1,0},{2,3},{3,2},{4,5},{5,4},{6,7},{7,6},{8,9},{9,8},{10,11... | collective-permute-start | bytes 811016 | tf_op jit(solution)/shard_map/ppermute | solution.py:497
  17.8 28.4 %copy-start.2 = (f32[32,64]{1,0:T(8,128)S(1)}, f32[32,64]{1,0:T(8,128)}, u32[]{:S(2)}) copy-start(f32[32,64]{1,0:T(8,128)} %refs_5_.1) | copy-start | bytes 24580
  17.8 11.2 %collective-permute-start = (s16[528,256]{1,0:T(8,128)(2,1)S(1)}, s16[528,256]{1,0:T(8,128)(2,1)S(1)}, u32[]{:S(2)}, u32[]{:S(2)}) collective-permute-start(s16[528,256]{1,0:T(8,128)(2,1)S(1)} %project_send.2), channel_id=1, source_target_pairs={{0,3},{1,2},{2,1},{3,0},{4,7},{5,6},{6,5},{7,4},{8,11},{9,10},{10,... | collective-permute-start | bytes 811016 | tf_op jit(solution)/shard_map/ppermute | solution.py:497
  24.6 21.5 %collective-permute-start.1 = (s16[528,256]{1,0:T(8,128)(2,1)S(1)}, s16[528,256]{1,0:T(8,128)(2,1)S(1)}, u32[]{:S(2)}, u32[]{:S(2)}) collective-permute-start(s16[528,256]{1,0:T(8,128)(2,1)S(1)} %project_send.3), channel_id=1, source_target_pairs={{0,2},{1,3},{2,0},{3,1},{4,6},{5,7},{6,4},{7,5},{8,10},{9,11},{10,... | collective-permute-start | bytes 811016 | tf_op jit(solution)/shard_map/ppermute | solution.py:497
  24.8 35.5 %collective-permute-start.10 = (f32[64,64]{1,0:T(8,128)S(1)}, f32[64,64]{1,0:T(8,128)S(1)}, u32[]{:S(2)}, u32[]{:S(2)}) collective-permute-start(f32[64,64]{1,0:T(8,128)S(1)} %get-tuple-element.28.refs_0_), channel_id=1, source_target_pairs={{0,2},{1,3},{2,0},{3,1},{4,6},{5,7},{6,4},{7,5},{8,10},{9,11},{10,... | collective-permute-start | bytes 49160 | tf_op jit(solution)/shard_map/ppermute | solution.py:497
  27.6 33.9 %collective-permute-start.11 = (f32[64,64]{1,0:T(8,128)S(1)}, f32[64,64]{1,0:T(8,128)S(1)}, u32[]{:S(2)}, u32[]{:S(2)}) collective-permute-start(f32[64,64]{1,0:T(8,128)S(1)} %get-tuple-element.28.refs_0_), channel_id=1, source_target_pairs={{0,3},{1,2},{2,1},{3,0},{4,7},{5,6},{6,5},{7,4},{8,11},{9,10},{10,... | collective-permute-start | bytes 49160 | tf_op jit(solution)/shard_map/ppermute | solution.py:497
  29.0 32.6 %collective-permute-start.12 = (f32[64,64]{1,0:T(8,128)S(1)}, f32[64,64]{1,0:T(8,128)S(1)}, u32[]{:S(2)}, u32[]{:S(2)}) collective-permute-start(f32[64,64]{1,0:T(8,128)S(1)} %get-tuple-element.29.refs_4_), channel_id=1, source_target_pairs={{0,4},{4,0},{8,12},{12,8},{1,5},{5,1},{9,13},{13,9},{2,6},{6,2},{1... | collective-permute-start | bytes 49160 | tf_op jit(solution)/shard_map/ppermute | solution.py:497
  57.1 7.2 %collective-permute-start.3 = (f32[64,64]{1,0:T(8,128)S(1)}, f32[64,64]{1,0:T(8,128)S(1)}, u32[]{:S(2)}, u32[]{:S(2)}) collective-permute-start(f32[64,64]{1,0:T(8,128)S(1)} %get-tuple-element.27), channel_id=1, source_target_pairs={{0,1},{1,0},{2,3},{3,2},{4,5},{5,4},{6,7},{7,6},{8,9},{9,8},{10,11... | collective-permute-start | bytes 49160 | tf_op jit(solution)/shard_map/ppermute | solution.py:497
  57.2 7.9 %collective-permute-start.4 = (f32[64,64]{1,0:T(8,128)S(1)}, f32[64,64]{1,0:T(8,128)S(1)}, u32[]{:S(2)}, u32[]{:S(2)}) collective-permute-start(f32[64,64]{1,0:T(8,128)S(1)} %get-tuple-element.27), channel_id=1, source_target_pairs={{0,2},{1,3},{2,0},{3,1},{4,6},{5,7},{6,4},{7,5},{8,10},{9,11},{10,... | collective-permute-start | bytes 49160 | tf_op jit(solution)/shard_map/ppermute | solution.py:497
  60.4 6.2 %collective-permute-start.5 = (f32[64,64]{1,0:T(8,128)S(1)}, f32[64,64]{1,0:T(8,128)S(1)}, u32[]{:S(2)}, u32[]{:S(2)}) collective-permute-start(f32[64,64]{1,0:T(8,128)S(1)} %get-tuple-element.27), channel_id=1, source_target_pairs={{0,3},{1,2},{2,1},{3,0},{4,7},{5,6},{6,5},{7,4},{8,11},{9,10},{10,... | collective-permute-start | bytes 49160 | tf_op jit(solution)/shard_map/ppermute | solution.py:497
  61.6 27.1 %collective-permute-start.17 = (bf16[8,64,256]{2,1,0:T(8,128)(2,1)S(1)}, bf16[8,64,256]{2,1,0:T(8,128)(2,1)S(1)}, u32[]{:S(2)}, u32[]{:S(2)}) collective-permute-start(bf16[8,64,256]{2,1,0:T(8,128)(2,1)S(1)} %get-tuple-element.33.frames_ref), channel_id=1, source_target_pairs={{0,1},{1,0},{2,3},{3,2},{4,5},{5,4},{6,7},{7,6},{8,9},{9,8},{10,11... | collective-permute-start | bytes 786440 | tf_op jit(solution)/shard_map/ppermute | solution.py:497
  61.6 31.8 %collective-permute-start.16 = (bf16[8,64,256]{2,1,0:T(8,128)(2,1)S(1)}, bf16[8,64,256]{2,1,0:T(8,128)(2,1)S(1)}, u32[]{:S(2)}, u32[]{:S(2)}) collective-permute-start(bf16[8,64,256]{2,1,0:T(8,128)(2,1)S(1)} %get-tuple-element.33.frames_ref), channel_id=1, source_target_pairs={{0,3},{1,2},{2,1},{3,0},{4,7},{5,6},{6,5},{7,4},{8,11},{9,10},{10,... | collective-permute-start | bytes 786440 | tf_op jit(solution)/shard_map/ppermute | solution.py:497
  64.3 33.9 %collective-permute-start.15 = (bf16[8,64,256]{2,1,0:T(8,128)(2,1)S(1)}, bf16[8,64,256]{2,1,0:T(8,128)(2,1)S(1)}, u32[]{:S(2)}, u32[]{:S(2)}) collective-permute-start(bf16[8,64,256]{2,1,0:T(8,128)(2,1)S(1)} %get-tuple-element.33.frames_ref), channel_id=1, source_target_pairs={{0,2},{1,3},{2,0},{3,1},{4,6},{5,7},{6,4},{7,5},{8,10},{9,11},{10,... | collective-permute-start | bytes 786440 | tf_op jit(solution)/shard_map/ppermute | solution.py:497
  65.1 3.9 %collective-permute-start.13 = (f32[64,64]{1,0:T(8,128)S(1)}, f32[64,64]{1,0:T(8,128)S(1)}, u32[]{:S(2)}, u32[]{:S(2)}) collective-permute-start(f32[64,64]{1,0:T(8,128)S(1)} %get-tuple-element.29.refs_4_), channel_id=1, source_target_pairs={{0,8},{4,12},{8,0},{12,4},{1,9},{5,13},{9,1},{13,5},{2,10},{6,14},... | collective-permute-start | bytes 49160 | tf_op jit(solution)/shard_map/ppermute | solution.py:497
  66.6 3.7 %collective-permute-start.14 = (f32[64,64]{1,0:T(8,128)S(1)}, f32[64,64]{1,0:T(8,128)S(1)}, u32[]{:S(2)}, u32[]{:S(2)}) collective-permute-start(f32[64,64]{1,0:T(8,128)S(1)} %get-tuple-element.29.refs_4_), channel_id=1, source_target_pairs={{0,12},{4,8},{8,4},{12,0},{1,13},{5,9},{9,5},{13,1},{2,14},{6,10},... | collective-permute-start | bytes 49160 | tf_op jit(solution)/shard_map/ppermute | solution.py:497
  69.0 9.0 %collective-permute-start.9 = (f32[64,64]{1,0:T(8,128)S(1)}, f32[64,64]{1,0:T(8,128)S(1)}, u32[]{:S(2)}, u32[]{:S(2)}) collective-permute-start(f32[64,64]{1,0:T(8,128)S(1)} %get-tuple-element.28.refs_0_), channel_id=1, source_target_pairs={{0,1},{1,0},{2,3},{3,2},{4,5},{5,4},{6,7},{7,6},{8,9},{9,8},{10,11... | collective-permute-start | bytes 49160 | tf_op jit(solution)/shard_map/ppermute | solution.py:497
  70.2 9.3 %collective-permute-start.6 = (f32[64,64]{1,0:T(8,128)S(1)}, f32[64,64]{1,0:T(8,128)S(1)}, u32[]{:S(2)}, u32[]{:S(2)}) collective-permute-start(f32[64,64]{1,0:T(8,128)S(1)} %add_add_fusion.refs_0_), channel_id=1, source_target_pairs={{0,4},{4,0},{8,12},{12,8},{1,5},{5,1},{9,13},{13,9},{2,6},{6,2},{1... | collective-permute-start | bytes 49160 | tf_op jit(solution)/shard_map/ppermute | solution.py:497
  78.0 9.5 %collective-permute-start.7 = (f32[64,64]{1,0:T(8,128)S(1)}, f32[64,64]{1,0:T(8,128)S(1)}, u32[]{:S(2)}, u32[]{:S(2)}) collective-permute-start(f32[64,64]{1,0:T(8,128)S(1)} %add_add_fusion.refs_0_), channel_id=1, source_target_pairs={{0,8},{4,12},{8,0},{12,4},{1,9},{5,13},{9,1},{13,5},{2,10},{6,14},... | collective-permute-start | bytes 49160 | tf_op jit(solution)/shard_map/ppermute | solution.py:497
  79.5 8.0 %collective-permute-start.8 = (f32[64,64]{1,0:T(8,128)S(1)}, f32[64,64]{1,0:T(8,128)S(1)}, u32[]{:S(2)}, u32[]{:S(2)}) collective-permute-start(f32[64,64]{1,0:T(8,128)S(1)} %add_add_fusion.refs_0_), channel_id=1, source_target_pairs={{0,12},{4,8},{8,4},{12,0},{1,13},{5,9},{9,5},{13,1},{2,14},{6,10},... | collective-permute-start | bytes 49160 | tf_op jit(solution)/shard_map/ppermute | solution.py:497
  107.8 1.9 %collective-permute-start.18 = (f32[64,1024]{1,0:T(8,128)S(1)}, f32[64,1024]{1,0:T(8,128)S(1)}, u32[]{:S(2)}, u32[]{:S(2)}) collective-permute-start(f32[64,1024]{1,0:T(8,128)S(1)} %v_terms.1), channel_id=1, source_target_pairs={{0,4},{4,0},{8,12},{12,8},{1,5},{5,1},{9,13},{13,9},{2,6},{6,2},{1... | collective-permute-start | bytes 786440 | tf_op jit(solution)/shard_map/ppermute | solution.py:497
  109.7 8.7 %collective-permute-start.19 = (f32[64,1024]{1,0:T(8,128)S(1)}, f32[64,1024]{1,0:T(8,128)S(1)}, u32[]{:S(2)}, u32[]{:S(2)}) collective-permute-start(f32[64,1024]{1,0:T(8,128)S(1)} %add.15.refs_0_), channel_id=1, source_target_pairs={{0,8},{4,12},{8,0},{12,4},{1,9},{5,13},{9,1},{13,5},{2,10},{6,14},... | collective-permute-start | bytes 786440 | tf_op jit(solution)/shard_map/ppermute | solution.py:497
  125.3 5.3 %collective-permute-start.20 = (f32[64,128]{1,0:T(8,128)S(1)}, f32[64,128]{1,0:T(8,128)S(1)}, u32[]{:S(2)}, u32[]{:S(2)}) collective-permute-start(f32[64,128]{1,0:T(8,128)S(1)} %get-tuple-element.45.refs_0_), channel_id=1, source_target_pairs={{0,1},{1,0},{2,3},{3,2},{4,5},{5,4},{6,7},{7,6},{8,9},{9,8},{10,11... | collective-permute-start | bytes 98312 | tf_op jit(solution)/shard_map/ppermute | solution.py:497
  127.8 5.8 %collective-permute-start.21 = (f32[64,128]{1,0:T(8,128)S(1)}, f32[64,128]{1,0:T(8,128)S(1)}, u32[]{:S(2)}, u32[]{:S(2)}) collective-permute-start(f32[64,128]{1,0:T(8,128)S(1)} %get-tuple-element.45.refs_0_), channel_id=1, source_target_pairs={{0,2},{1,3},{2,0},{3,1},{4,6},{5,7},{6,4},{7,5},{8,10},{9,11},{10,... | collective-permute-start | bytes 98312 | tf_op jit(solution)/shard_map/ppermute | solution.py:497
  129.2 5.7 %collective-permute-start.22 = (f32[64,128]{1,0:T(8,128)S(1)}, f32[64,128]{1,0:T(8,128)S(1)}, u32[]{:S(2)}, u32[]{:S(2)}) collective-permute-start(f32[64,128]{1,0:T(8,128)S(1)} %get-tuple-element.45.refs_0_), channel_id=1, source_target_pairs={{0,3},{1,2},{2,1},{3,0},{4,7},{5,6},{6,5},{7,4},{8,11},{9,10},{10,... | collective-permute-start | bytes 98312 | tf_op jit(solution)/shard_map/ppermute | solution.py:497
  (5 other events, 66.8 us)

commit v3 on v2

v3 whole, which is shorter than its diff:
```python
import functools

import jax
import jax.numpy as jnp
from jax import lax
from jax.experimental import pallas as pl
from jax.experimental.pallas import tpu as pltpu
from jax.sharding import PartitionSpec as P

NS_STEPS = 12
LANES = 128
LEVELS = 32000.0
COARSE_STEPS = 3
SHORT = pl.CostEstimate(flops=1000, bytes_accessed=1000, transcendentals=0)

epsilon = 1e-06
HIGH = lax.Precision.HIGHEST
F32 = jnp.float32
BF16 = jnp.bfloat16
MIB = 1024 * 1024

ROWS_BY_COLS = (((1,), (0,)), ((), ()))
ROWS_BY_ROWS = (((1,), (1,)), ((), ()))
COLS_BY_COLS = (((0,), (0,)), ((), ()))


def low_dot(a, b, dims=ROWS_BY_COLS):
    return lax.dot_general(a, b, dims, preferred_element_type=F32)


def high_dot(a, b, dims=ROWS_BY_COLS):
    return lax.dot_general(a, b, dims, precision=HIGH, preferred_element_type=F32)


def two_parts(x):
    first = x.astype(BF16)
    return first, (x - first.astype(F32)).astype(BF16)


def three_parts(x):
    first = x.astype(BF16)
    rest = x - first.astype(F32)
    second = rest.astype(BF16)
    return first, second, (rest - second.astype(F32)).astype(BF16)


def lane_numbers(shape):
    return lax.broadcasted_iota(jnp.int32, shape, len(shape) - 1)


def batch_of(share):
    return 4 if share % 4 == 0 else share


ANY_SPEC = pl.BlockSpec(memory_space=pl.ANY)


def whole(shape):
    return pl.BlockSpec(shape, lambda *place: (0,) * len(shape))


def parameters(mib):
    return pltpu.CompilerParams(vmem_limit_bytes=mib * MIB)


STREAM = 50
SMALL = 16
VMEM_SPEC = pl.BlockSpec(memory_space=pltpu.VMEM)
SMEM_SPEC = pl.BlockSpec(memory_space=pltpu.SMEM)


def exponent_rows(share):
    return -(-(share + 1) // 16) * 16


def payload_shape(share, rank, slots):
    return (share * rank + rank // 2 + exponent_rows(share), slots)


def row_exponent(x):
    top = jnp.max(jnp.abs(x), axis=1, keepdims=True)
    return jnp.ceil(jnp.log2(jnp.maximum(top, 1e-30)))


def encode_batch(step, batch, v_ref, visits_refs, coded_ref, exponents_ref):
    rank = v_ref.shape[0]
    exponents = exponents_ref[...]
    lanes = lane_numbers(exponents.shape)
    for p in range(batch):
        proj = low_dot(v_ref[...], visits_refs[p][0, 0], ROWS_BY_ROWS)
        exponent = row_exponent(proj)
        coded = jnp.floor(proj * (LEVELS / jnp.exp2(exponent)) + 0.5)
        row = pl.multiple_of((step * batch + p) * rank, rank)
        coded_ref[pl.ds(row, rank), :] = coded.astype(jnp.int32).astype(jnp.int16)
        exponents = jnp.where(lanes == step * batch + p, exponent, exponents)
    exponents_ref[...] = exponents


def encode_rest(share, v_ref, coded_ref, exponents_ref):
    rank = v_ref.shape[0]
    gram = low_dot(v_ref[...], v_ref[...], ROWS_BY_ROWS)
    exponent = row_exponent(gram)
    scaled = gram * (LEVELS / jnp.exp2(exponent))
    first = jnp.floor(scaled + 0.5)
    second = jnp.floor((scaled - first) * (2 * LEVELS) + 0.5)
    digits = jnp.concatenate([first, second], axis=1)
    digits = jnp.concatenate([digits[: rank // 2], digits[rank // 2 :]], axis=1)
    coded_ref[pl.ds(share * rank, rank // 2), :] = digits.astype(jnp.int32).astype(jnp.int16)
    exponents = exponents_ref[...]
    exponents = jnp.where(lane_numbers(exponents.shape) == share, exponent, exponents)
    rows = exponent_rows(share)
    last = exponents.T[:rows]
    last = jnp.concatenate([last, jnp.zeros((rows, coded_ref.shape[1] - rank), F32)], axis=1)
    coded_ref[pl.ds(share * rank + rank // 2, rows), :] = last.astype(jnp.int32).astype(jnp.int16)


def decode(coded_ref, share, rank):
    def rows(first, count):
        return coded_ref[pl.ds(first, count), :].astype(jnp.int32).astype(F32)

    exponents = rows(share * rank + rank // 2, exponent_rows(share))[:, :LANES].T
    steps = jnp.exp2(exponents[:rank]) * (1.0 / LEVELS)
    digits = rows(share * rank, rank // 2)
    digits = jnp.concatenate([digits[:, : 2 * rank], digits[:, 2 * rank :]], axis=0)
    gram = (digits[:, :rank] + digits[:, rank:] * (0.5 / LEVELS)) * steps[:, share : share + 1]
    return [rows(p * rank, rank) * steps[:, p : p + 1] for p in range(share)], gram


def send_projection_kernel(batch, share, place, v_ref, *refs):
    visits_refs = refs[:batch]
    coded_ref, exponents_ref = refs[batch:]
    step = pl.program_id(0)

    @pl.when(step == 0)
    def _():
        exponents_ref[...] = jnp.zeros_like(exponents_ref)

    encode_batch(step, batch, v_ref, visits_refs, coded_ref, exponents_ref)

    @pl.when(step == share // batch - 1)
    def _():
        encode_rest(share, v_ref, coded_ref, exponents_ref)


def own_projection_kernel(batch, place, v_ref, w_ref, *refs):
    visits_refs = refs[:batch]
    proj_ref, v_gram_ref, w_gram_ref = refs[batch:]

    @pl.when(pl.program_id(0) == 0)
    def _():
        v_gram_ref[...] = low_dot(v_ref[...], v_ref[...], ROWS_BY_ROWS)
        w_gram_ref[...] = high_dot(w_ref[...], w_ref[...], COLS_BY_COLS)

    for p in range(batch):
        proj_ref[p] = low_dot(v_ref[...], visits_refs[p][0, 0], ROWS_BY_ROWS)


def visits_specs(slot, batch, slots, width):
    return [
        pl.BlockSpec((1, 1, slots, width), lambda i, place, p=p: (place[0] ^ slot, i * batch + p, 0, 0))
        for p in range(batch)
    ]


def project_for(slot, place, visits, v_rows):
    _, share, slots, width = visits.shape
    rank = v_rows.shape[0]
    batch = batch_of(share)
    coded = payload_shape(share, rank, slots)
    return pl.pallas_call(
        functools.partial(send_projection_kernel, batch, share),
        grid_spec=pltpu.PrefetchScalarGridSpec(
            num_scalar_prefetch=1,
            grid=(share // batch,),
            in_specs=[whole(v_rows.shape)] + visits_specs(slot, batch, slots, width),
            out_specs=whole(coded),
            scratch_shapes=[pltpu.VMEM((rank, LANES), F32)],
        ),
        out_shape=jax.ShapeDtypeStruct(coded, jnp.int16),
        compiler_params=parameters(STREAM),
        cost_estimate=SHORT,
        name="project_send",
    )(place, v_rows, *[visits] * batch)


def project_own(place, visits, v_rows, w_start):
    _, share, slots, width = visits.shape
    rank = v_rows.shape[0]
    batch = batch_of(share)
    gram = (rank, rank)
    return pl.pallas_call(
        functools.partial(own_projection_kernel, batch),
        grid_spec=pltpu.PrefetchScalarGridSpec(
            num_scalar_prefetch=1,
            grid=(share // batch,),
            in_specs=[whole(v_rows.shape), whole(w_start.shape)] + visits_specs(0, batch, slots, width),
            out_specs=[
                pl.BlockSpec((batch, rank, slots), lambda i, place: (i, 0, 0)),
                whole(gram),
                whole(gram),
            ],
        ),
        out_shape=[
            jax.ShapeDtypeStruct((share, rank, slots), F32),
            jax.ShapeDtypeStruct(gram, F32),
            jax.ShapeDtypeStruct(gram, F32),
        ],
        compiler_params=parameters(STREAM),
        cost_estimate=SHORT,
        name="project_own",
    )(place, v_rows, w_start, *[visits] * batch)


def eliminate(table, rank):
    rows = lax.broadcasted_iota(jnp.int32, table.shape, 0)
    for i in range(0, rank, 2):
        first = jnp.broadcast_to(table[:, i : i + 1], table.shape)
        second = jnp.broadcast_to(table[:, i + 1 : i + 2], table.shape)
        row_first, row_second = table[i : i + 1], table[i + 1 : i + 2]
        a, b = first[i : i + 1], second[i : i + 1]
        c, d = first[i + 1 : i + 2], second[i + 1 : i + 2]
        scale = 1.0 / (a * d - b * c)
        new_first = (d * row_first - b * row_second) * scale
        new_second = (a * row_second - c * row_first) * scale
        table = table - first * new_first - second * new_second
        table = jnp.where(rows == i, new_first, jnp.where(rows == i + 1, new_second, table))
    return table


def inverse_of(gram):
    rank = gram.shape[0]
    eye = (lax.broadcasted_iota(jnp.int32, gram.shape, 0) == lane_numbers(gram.shape)).astype(F32)
    return eliminate(jnp.concatenate([gram, eye], axis=1), rank)[:, rank:]


def total(refs):
    out = refs[0][...]
    for ref in refs[1:]:
        out = out + ref[...]
    return out


def first_inverse_kernel(v_gram_ref, w_gram_ref, after_ref, inverse_ref):
    inverse_ref[...] = inverse_of(w_gram_ref[...] * v_gram_ref[...])


def first_inverse(v_gram, w_gram, after):
    return pl.pallas_call(
        first_inverse_kernel,
        in_specs=[VMEM_SPEC] * 2 + [ANY_SPEC],
        out_specs=VMEM_SPEC,
        out_shape=jax.ShapeDtypeStruct(w_gram.shape, F32),
        compiler_params=parameters(SMALL),
        cost_estimate=SHORT,
        name="first_inverse",
    )(v_gram, w_gram, after)


def sum_h_kernel(n_terms, *refs):
    h_ref, w_gram_ref = refs[n_terms + 1 :]
    rank = h_ref.shape[0]
    both = total(refs[:n_terms])
    h_ref[...] = both[:, :rank]
    w_gram_ref[...] = both[:, rank:]


def sum_h(terms, after):
    rank = terms[0].shape[0]
    return pl.pallas_call(
        functools.partial(sum_h_kernel, len(terms)),
        in_specs=[VMEM_SPEC] * len(terms) + [ANY_SPEC],
        out_specs=[VMEM_SPEC] * 2,
        out_shape=[jax.ShapeDtypeStruct((rank, rank), F32)] * 2,
        compiler_params=parameters(SMALL),
        cost_estimate=SHORT,
        name="sum_h",
    )(*terms, after)


def sweep_once(frames, p, rank, fine):
    frame = frames[p]
    first, second = two_parts(frame)
    if fine:
        both = low_dot(jnp.concatenate([first, second], axis=0), first, ROWS_BY_ROWS)
        gram = both[:rank] + both[rank:] + low_dot(first, second, ROWS_BY_ROWS)
        gram_first, gram_second = two_parts(gram)
        moved = low_dot(jnp.concatenate([gram_first, gram_second], axis=0), first)
        moved = moved[:rank] + moved[rank:] + low_dot(gram_first, second)
    else:
        moved = low_dot(low_dot(first, first, ROWS_BY_ROWS).astype(BF16), first)
    frames[p] = 1.5 * frame - 0.5 * moved


def frames_kernel(share, n_coded, place, counts_ref, h_ref, w_ref, v_gram_ref, w_gram_ref, own_ref, *refs):
    coded = refs[:n_coded]
    frames_ref, terms_ref, v_total_ref, proj, frames = refs[n_coded:]
    first = place[0] * share
    rank, slots = frames.shape[1:]
    pieces = [own_ref[p] for p in range(share)]
    v_gram = v_gram_ref[...]
    for code in coded:
        arrived, gram = decode(code, share, rank)
        pieces = [a + b for a, b in zip(pieces, arrived)]
        v_gram = v_gram + gram
    v_total_ref[...] = v_gram
    for p, piece in enumerate(pieces):
        proj[p] = piece
        mixed = high_dot(h_ref[...] * w_ref[pl.ds(first + p, 1), :], piece)
        mixed = jnp.where(lane_numbers((rank, slots)) < counts_ref[first + p], mixed, 0.0)
        energy = jnp.sum(jnp.sum(mixed * mixed, axis=1, keepdims=True), axis=0, keepdims=True)
        frames[p] = mixed * lax.rsqrt(energy + epsilon)

    def sweep(fine, step, carry):
        for p in range(share):
            sweep_once(frames, p, rank, fine)
        return carry

    lax.fori_loop(0, COARSE_STEPS, functools.partial(sweep, False), 0)
    lax.fori_loop(COARSE_STEPS, NS_STEPS, functools.partial(sweep, True), 0)
    terms = jnp.zeros((rank, rank), F32)
    for p in range(share):
        low = frames[p].astype(BF16)
        frames_ref[p] = low
        parts = three_parts(proj[p])
        product = low_dot(low, parts[0], ROWS_BY_ROWS)
        for part in parts[1:]:
            product = product + low_dot(low, part, ROWS_BY_ROWS)
        terms = terms + product * w_ref[pl.ds(first + p, 1), :]
    terms_ref[...] = jnp.concatenate([terms, w_gram_ref[...]], axis=1)


def own_frames(place, counts, h_start, w_start, v_gram, w_gram, own, coded):
    share, rank, slots = own.shape
    return pl.pallas_call(
        functools.partial(frames_kernel, share, len(coded)),
        in_specs=[SMEM_SPEC] * 2 + [VMEM_SPEC] * (5 + len(coded)),
        out_specs=[VMEM_SPEC] * 3,
        out_shape=[
            jax.ShapeDtypeStruct(own.shape, BF16),
            jax.ShapeDtypeStruct((rank, 2 * rank), F32),
            jax.ShapeDtypeStruct((rank, rank), F32),
        ],
        scratch_shapes=[pltpu.VMEM(own.shape, F32)] * 2,
        compiler_params=parameters(SMALL),
        cost_estimate=SHORT,
        name="own_frames",
    )(place, counts, h_start, w_start, v_gram, w_gram, own, *coded)


def projected_kernel(batch, place, frames_ref, *refs):
    first_ref, second_ref, token_ref = refs[-3:]
    rank = frames_ref.shape[1]
    token_ref[...] = jnp.zeros_like(token_ref)
    for p in range(batch):
        rows = slice(p * rank, (p + 1) * rank)
        first_ref[0, rows], second_ref[0, rows] = two_parts(low_dot(frames_ref[p], refs[p][0, 0]))


def project_frames(slot, place, frames, visits, before):
    n_slots, share, slots, width = visits.shape
    rank = frames.shape[1]
    batch = batch_of(share)
    out = jax.ShapeDtypeStruct((n_slots, share * rank, width), BF16)
    aliases = {batch + 2: 0, batch + 3: 1} if before else {}
    *before, token = pl.pallas_call(
        functools.partial(projected_kernel, batch),
        grid_spec=pltpu.PrefetchScalarGridSpec(
            num_scalar_prefetch=1,
            grid=(share // batch,),
            in_specs=[pl.BlockSpec((batch, rank, slots), lambda i, place: (i, 0, 0))]
            + visits_specs(slot, batch, slots, width)
            + [ANY_SPEC] * len(before),
            out_specs=[pl.BlockSpec((1, batch * rank, width), lambda i, place: (slot, i, 0))] * 2 + [whole((8, LANES))],
        ),
        out_shape=[out, out, jax.ShapeDtypeStruct((8, LANES), F32)],
        input_output_aliases=aliases,
        compiler_params=parameters(STREAM),
        cost_estimate=SHORT,
        name="project_frames",
    )(place, frames, *[visits] * batch, *before)
    return before, token


def next_h_kernel(n_terms, n_slots, place, *refs):
    inverse_ref, w_ref, _, h_ref, factor_ref = refs[n_terms:]
    h_next = high_dot(total(refs[:n_terms]), inverse_ref[...])
    h_ref[...] = h_next
    rank = h_next.shape[0]
    patients = w_ref.shape[0]
    share = patients // n_slots
    h_rows = h_next.T
    w_rows = jnp.concatenate([w_ref[...], jnp.zeros((LANES - patients, rank), F32)], axis=0)
    w_columns = w_rows.T
    for slot in range(n_slots):
        first = (place[0] ^ slot) * share
        columns = pltpu.roll(w_columns, jnp.where(first == 0, 0, LANES - first), 1)
        factor = jnp.concatenate([h_rows * columns[:, p : p + 1] for p in range(share)], axis=1)
        factor_ref[slot] = jnp.concatenate(three_parts(factor), axis=0)


def next_h(place, terms, inverse, w_start, n_slots, after):
    patients, rank = w_start.shape
    share = patients // n_slots
    return pl.pallas_call(
        functools.partial(next_h_kernel, len(terms), n_slots),
        in_specs=[SMEM_SPEC] + [VMEM_SPEC] * (len(terms) + 2) + [ANY_SPEC],
        out_specs=[VMEM_SPEC] * 2,
        out_shape=[
            jax.ShapeDtypeStruct(inverse.shape, F32),
            jax.ShapeDtypeStruct((n_slots, 3 * rank, share * rank), BF16),
        ],
        compiler_params=parameters(SMALL),
        cost_estimate=SHORT,
        name="next_h",
    )(place, *terms, inverse, w_start, after)


def second_inverse_kernel(h_ref, w_gram_ref, gram_ref, inverse_ref):
    gram = high_dot(h_ref[...], h_ref[...], COLS_BY_COLS)
    gram_ref[...] = gram
    inverse_ref[...] = inverse_of(gram * w_gram_ref[...])


def second_inverse(h_next, w_gram):
    out = jax.ShapeDtypeStruct(w_gram.shape, F32)
    return pl.pallas_call(
        second_inverse_kernel,
        out_shape=[out, out],
        compiler_params=parameters(SMALL),
        cost_estimate=SHORT,
        name="second_inverse",
    )(h_next, w_gram)


def v_terms_kernel(core, factor_ref, first_ref, second_ref, keep_ref, send_ref, terms_ref):
    step = pl.program_id(0)
    rank, width = terms_ref.shape
    half = width // 2
    large = low_dot(factor_ref[0], first_ref[0])
    small = low_dot(factor_ref[0, : 2 * rank], second_ref[0])
    terms = large[:rank] + (large[rank : 2 * rank] + small[:rank]) + (large[2 * rank :] + small[rank:])

    @pl.when(step == 0)
    def _():
        terms_ref[...] = terms

    @pl.when(step > 0)
    def _():
        terms_ref[...] += terms

    @pl.when(step == pl.num_programs(0) - 1)
    def _():
        keep_ref[...] = terms_ref[:, pl.ds(pl.multiple_of(core[0] * half, half), half)]
        send_ref[...] = terms_ref[:, pl.ds(pl.multiple_of((1 - core[0]) * half, half), half)]


def all_v_terms(core, factor, first, second):
    n_slots, rows, width = first.shape
    rank = factor.shape[1] // 3
    half = (rank, width // 2)
    return pl.pallas_call(
        v_terms_kernel,
        grid_spec=pltpu.PrefetchScalarGridSpec(
            num_scalar_prefetch=1,
            grid=(n_slots,),
            in_specs=[
                pl.BlockSpec((1, 3 * rank, rows), lambda i, core: (i, 0, 0)),
                pl.BlockSpec((1, rows, width), lambda i, core: (i, 0, 0)),
                pl.BlockSpec((1, rows, width), lambda i, core: (i, 0, 0)),
            ],
            out_specs=[whole(half)] * 2,
            scratch_shapes=[pltpu.VMEM((rank, width), F32)],
        ),
        out_shape=[jax.ShapeDtypeStruct(half, F32)] * 2,
        compiler_params=parameters(STREAM),
        cost_estimate=SHORT,
        name="v_terms",
    )(core, factor, first, second)


def next_v_kernel(share, place, core, own_ref, other_ref, *refs):
    inverse_ref, h_ref, first_ref, second_ref, v_ref, sums_ref, v_parts, weights = refs
    slot = pl.program_id(0)
    rank = inverse_ref.shape[0]

    @pl.when(slot == 0)
    def _():
        upper = core[0] == 1
        left = jnp.where(upper, other_ref[...], own_ref[...])
        right = jnp.where(upper, own_ref[...], other_ref[...])
        v_rows = high_dot(inverse_ref[...], jnp.concatenate([left, right], axis=1))
        v_ref[...] = v_rows
        v_parts[...] = jnp.concatenate(two_parts(v_rows), axis=0)
        weights[...] = jnp.concatenate([h_ref[...]] * 2, axis=1)
        gram = low_dot(v_parts[...], v_parts[...], ROWS_BY_ROWS)
        gram = gram[:rank, :rank] + (gram[:rank, rank:] + gram[rank:, :rank])
        sums_ref[...] = jnp.concatenate([jnp.zeros((rank, rank), F32), gram], axis=1)

    seen = low_dot(first_ref[0], v_parts[...], ROWS_BY_ROWS) + low_dot(second_ref[0], v_parts[...], ROWS_BY_ROWS)
    first = (place[0] ^ slot) * share
    for p in range(share):
        row = jnp.sum(seen[p * rank : (p + 1) * rank] * weights[...], axis=0, keepdims=True)
        sums_ref[pl.ds(first + p, 1), :rank] = row[:, :rank] + row[:, rank:]


def next_v(place, core, own, other, inverse, h_next, first, second):
    n_slots, rows, width = first.shape
    rank = inverse.shape[0]
    return pl.pallas_call(
        functools.partial(next_v_kernel, rows // rank),
        grid_spec=pltpu.PrefetchScalarGridSpec(
            num_scalar_prefetch=2,
            grid=(n_slots,),
            in_specs=[whole(own.shape)] * 2
            + [whole((rank, rank))] * 2
            + [pl.BlockSpec((1, rows, width), lambda i, place, core: (i, 0, 0))] * 2,
            out_specs=[whole((rank, width)), whole((rank, 2 * rank))],
            scratch_shapes=[pltpu.VMEM((2 * rank, width), BF16), pltpu.VMEM((rank, 2 * rank), F32)],
        ),
        out_shape=[
            jax.ShapeDtypeStruct((rank, width), F32),
            jax.ShapeDtypeStruct((rank, 2 * rank), F32),
        ],
        compiler_params=parameters(STREAM),
        cost_estimate=SHORT,
        name="next_v",
    )(place, core, own, other, inverse, h_next, first, second)


def next_w_kernel(n_sums, *refs):
    gram_ref, w_ref = refs[n_sums:]
    patients, rank = w_ref.shape
    sums = total(refs[:n_sums])
    table = jnp.concatenate([sums[:, rank:] * gram_ref[...], sums.T[:rank]], axis=1)
    w_ref[...] = eliminate(table, rank).T[rank : rank + patients]


def next_w(sums, h_gram, patients):
    rank = h_gram.shape[0]
    return pl.pallas_call(
        functools.partial(next_w_kernel, len(sums)),
        out_shape=jax.ShapeDtypeStruct((patients, rank), F32),
        compiler_params=parameters(SMALL),
        cost_estimate=SHORT,
        name="next_w",
    )(*sums, h_gram)


def swap(x, axis, slot):
    pairs = [(i, i ^ slot) for i in range(lax.axis_size(axis))]
    return lax.ppermute(x, axis, pairs)


def all_terms(x, axis):
    n = lax.axis_size(axis)
    if n > 4:
        return [lax.psum(x, axis)]
    return [x] + [swap(x, axis, s) for s in range(1, n)]


def add_kernel(a_ref, b_ref, after_ref, sum_ref):
    sum_ref[...] = a_ref[...] + b_ref[...]


def add(a, b, after):
    return pl.pallas_call(
        add_kernel,
        in_specs=[VMEM_SPEC] * 2 + [ANY_SPEC],
        out_specs=VMEM_SPEC,
        out_shape=jax.ShapeDtypeStruct(a.shape, a.dtype),
        compiler_params=parameters(SMALL),
        cost_estimate=SHORT,
        name="add_terms",
    )(a, b, after)


def patient_halves(keep, send, after):
    own = keep + swap(send, "patient", 1)
    step = 2
    while step < lax.axis_size("patient"):
        own = add(own, swap(own, "patient", step), after)
        step *= 2
    return own, swap(own, "patient", 1)


def on_device(visits, visit_counts, h_start, v_start, w_start):
    n = lax.axis_size("feature")
    patients, slots, width = visits.shape
    share = patients // n
    place = lax.axis_index("feature").astype(jnp.int32).reshape(1)
    core = lax.rem(lax.axis_index("patient").astype(jnp.int32), 2).reshape(1)
    by_owner = visits.reshape(n, share, slots, width)
    v_rows = v_start.T

    coded = [swap(project_for(slot, place, by_owner, v_rows), "feature", slot) for slot in range(n - 1, 0, -1)]
    own, v_local, w_local = project_own(place, by_owner, v_rows, w_start)

    frames, h_local, v_gram = own_frames(place, visit_counts, h_start, w_start, v_local, w_local, own, coded)
    far = list(range(n - 1, 1, -1))
    all_frames = {0: frames} | {slot: swap(frames, "feature", slot) for slot in far + [1]}
    h_sums = all_terms(h_local, "patient")

    projected, token = project_frames(0, place, frames, by_owner, [])
    h_sum, w_gram = sum_h(h_sums, token)
    h_terms = all_terms(h_sum, "feature")
    projected, token = project_frames(1, place, all_frames[1], by_owner, projected)
    first = first_inverse(v_gram, w_gram, token)
    for slot in far:
        projected, token = project_frames(slot, place, all_frames[slot], by_owner, projected)
    h_next, factor = next_h(place, h_terms, first, w_start, n, token)

    keep, send = all_v_terms(core, factor, *projected)
    h_gram, second = second_inverse(h_next, w_gram)
    own_terms, other_terms = patient_halves(keep, send, second)
    v_next, sums = next_v(place, core, own_terms, other_terms, second, h_next, *projected)
    w_next = next_w(all_terms(sums, "feature"), h_gram, patients)
    return (h_next, v_next.T, w_next)


def solution(mesh):
    return jax.shard_map(
        on_device,
        mesh=mesh,
        in_specs=(
            P(("groups", "patient"), None, "feature"),
            P(("groups", "patient")),
            P(),
            P("feature", None),
            P(("groups", "patient"), None),
        ),
        out_specs=(P(None, "groups"), P("feature", "groups"), P("patient", "groups")),
        check_vma=False,
    )
```

time: 140 us -> 111 us (0.79)
  waiting for transfers between devices: 36.6 us -> 22.3 us
  Pallas kernels: 70.3 us -> 63.9 us
  starting transfers between devices: 29.5 us -> 23.1 us
    ppermute x23 -> x18, waiting for transfers between devices: 36.6 us -> 22.3 us  [swap(): return lax.ppermute(x, axis, pairs)]
    ppermute x23 -> x18, starting transfers between devices: 29.5 us -> 23.1 us  [swap(): return lax.ppermute(x, axis, pairs)]
    pallas_call x5 -> x7, Pallas kernels: 34.3 us -> 29.6 us  [the longest x1 11 us: own_frames(): pl.pallas_call(functools.partial(frames_kernel, share, len(coded)), in_sp...]
    pallas_call x4, Pallas kernels: 18.9 us -> 14.5 us  [project_frames(): pl.pallas_call(functools.partial(projected_kernel, batch), grid_spec=pltp...]
    pallas_call x2 -> x3, Pallas kernels: 8.61 us -> 11.3 us  [project_for(): pl.pallas_call(functools.partial(send_projection_kernel, batch, share), g...]
  transfers between devices with their start and end apart: 23 -> 18, of which waited for: 8 -> 7; matrix products, arithmetic and copies ran while one was open for 0% -> 0% of each run, Pallas kernels for 30% -> 29%
where the time goes in v3:
time: 111 us
  Pallas kernels  63.9 us (58%)
  starting transfers between devices  23.1 us (21%)
  waiting for transfers between devices  22.3 us (20%)
    ppermute x18, starting transfers between devices, swap(): return lax.ppermute(x, axis, pairs)  23.1 us
    ppermute x18, waiting for transfers between devices, swap(): return lax.ppermute(x, axis, pairs)  22.3 us
    pallas_call x4, Pallas kernels, project_frames(): pl.pallas_call(functools.partial(projected_kernel, batch), grid_spec=pltp...  14.5 us
    pallas_call x3, Pallas kernels, project_for(): pl.pallas_call(functools.partial(send_projection_kernel, batch, share), g...  11.3 us
    pallas_call x1, Pallas kernels, own_frames(): pl.pallas_call(functools.partial(frames_kernel, share, len(coded)), in_sp...  11 us
    pallas_call x1, Pallas kernels, next_v(): pl.pallas_call(functools.partial(next_v_kernel, rows // rank), grid_spec=...  6.86 us
    pallas_call x1, Pallas kernels, all_v_terms(): pl.pallas_call(v_terms_kernel, grid_spec=pltpu.PrefetchScalarGridSpec(num...  5.01 us
    pallas_call x1, Pallas kernels, next_w(): pl.pallas_call(functools.partial(next_w_kernel, len(sums)), out_shape=jax...  3.96 us
  transfers between devices with their start and end apart: 18, of which 7 were waited for; matrix products, arithmetic and copies ran while one was open for 0% of the time, Pallas kernels for 29%

profile of v3, /device:TPU:0, one launch (start us, length us, event | category | flops | bytes accessed | tf_op | source)
XLA Modules:
  0.0 110.9 jit_solution(5543883695543804042)
XLA Ops:
  1.5 3.7 %project_send.3 = s16[560,256]{1,0:T(8,128)(2,1)S(1)} custom-call(s32[1]{0:T(128)} %bitcast.place, bf16[64,1024]{1,0:T(8,128)(2,1)S(1)} %bitcast.5, bf16[4,8,256,1024]{3,2,1,0:T(8,128)(2,1)} %bitcast.9, bf16[4,8,256,1024]{3,2,1,0:T(8,128)(2,1)} %bitcast.10, bf16[4,8,256,1024]{3,2,1,0:T(8,128)(2,1)} %bitcast.11, bf16[4,8,256,1024]{3,2,1,0:T(8,128)(2,1)} %bitcast.12), custom_call_target="tpu_custom_call" | custom-call | flops 1000 | bytes 1000 | tf_op jit(solution)/shard_map/project_send/pallas_call | solution.py:170
  5.3 5.1 %collective-permute-start = (s16[560,256]{1,0:T(8,128)(2,1)S(1)}, s16[560,256]{1,0:T(8,128)(2,1)S(1)}, u32[]{:S(2)}, u32[]{:S(2)}) collective-permute-start(s16[560,256]{1,0:T(8,128)(2,1)S(1)} %project_send.3), channel_id=1, source_target_pairs={{0,3},{1,2},{2,1},{3,0},{4,7},{5,6},{6,5},{7,4},{8,11},{9,10},{10,... | collective-permute-start | bytes 860168 | tf_op jit(solution)/shard_map/ppermute | solution.py:551
  10.4 3.7 %project_send.4 = s16[560,256]{1,0:T(8,128)(2,1)S(1)} custom-call(s32[1]{0:T(128)} %bitcast.place, bf16[64,1024]{1,0:T(8,128)(2,1)S(1)} %bitcast.6, bf16[4,8,256,1024]{3,2,1,0:T(8,128)(2,1)} %bitcast.13, bf16[4,8,256,1024]{3,2,1,0:T(8,128)(2,1)} %bitcast.14, bf16[4,8,256,1024]{3,2,1,0:T(8,128)(2,1)} %bitcast.15, bf16[4,8,256,1024]{3,2,1,0:T(8,128)(2,1)} %bitcast.16), custom_call_target="tpu_custom_call" | custom-call | flops 1000 | bytes 1000 | tf_op jit(solution)/shard_map/project_send/pallas_call | solution.py:170
  14.3 3.8 %project_send.5 = s16[560,256]{1,0:T(8,128)(2,1)S(1)} custom-call(s32[1]{0:T(128)} %bitcast.place, bf16[64,1024]{1,0:T(8,128)(2,1)S(1)} %bitcast.7, bf16[4,8,256,1024]{3,2,1,0:T(8,128)(2,1)} %bitcast.17, bf16[4,8,256,1024]{3,2,1,0:T(8,128)(2,1)} %bitcast.18, bf16[4,8,256,1024]{3,2,1,0:T(8,128)(2,1)} %bitcast.19, bf16[4,8,256,1024]{3,2,1,0:T(8,128)(2,1)} %bitcast.20), custom_call_target="tpu_custom_call" | custom-call | flops 1000 | bytes 1000 | tf_op jit(solution)/shard_map/project_send/pallas_call | solution.py:170
  18.7 3.4 %project_own.1 = (f32[8,64,256]{2,1,0:T(8,128)S(1)}, f32[64,64]{1,0:T(8,128)S(1)}, f32[64,64]{1,0:T(8,128)S(1)}) custom-call(s32[1]{0:T(128)} %bitcast.place, bf16[64,1024]{1,0:T(8,128)(2,1)S(1)} %bitcast.8, f32[32,64]{1,0:T(8,128)S(1)} %copy-done.1, bf16[4,8,256,1024]{3,2,1,0:T(8,128)(2,1)} %bitcast.24, bf16[4,8,256,1024]{3,2,1,0:T(8,128)(2,1)} %bitcast.22, ...), custom_call_target="tpu_custom_call" | custom-call | flops 1000 | bytes 1000 | tf_op jit(solution)/shard_map/project_own/pallas_call | solution.py:191
  22.1 12.7 %collective-permute-done.1.refs_1_ = s16[560,256]{1,0:T(8,128)(2,1)S(1)} collective-permute-done((s16[560,256]{1,0:T(8,128)(2,1)S(1)}, s16[560,256]{1,0:T(8,128)(2,1)S(1)}, u32[]{:S(2)}, u32[]{:S(2)}) %collective-permute-start.1) | collective-permute-done | bytes 286752 | tf_op jit(solution)/shard_map/ppermute | solution.py:551
  34.8 11.0 %own_frames.1 = (bf16[8,64,256]{2,1,0:T(8,128)(2,1)S(1)}, f32[64,128]{1,0:T(8,128)S(1)}, f32[64,64]{1,0:T(8,128)S(1)}) custom-call(s32[1]{0:T(128)} %bitcast.place, s32[32]{0:T(128)S(1)} %copy-done.4, f32[64,64]{1,0:T(8,128)S(1)} %copy-done.3, f32[32,64]{1,0:T(8,128)S(1)} %copy-done.1, f32[64,64]{1,0:T(8,128)S(1)} %get-tuple-element.30.v_gram_ref, ...), custom_call_target="tpu_custom_call" | custom-call | flops 1000 | bytes 1000 | tf_op jit(solution)/shard_map/own_frames/pallas_call | solution.py:334
  45.9 2.5 %collective-permute-start.11 = (bf16[8,64,256]{2,1,0:T(8,128)(2,1)S(1)}, bf16[8,64,256]{2,1,0:T(8,128)(2,1)S(1)}, u32[]{:S(2)}, u32[]{:S(2)}) collective-permute-start(bf16[8,64,256]{2,1,0:T(8,128)(2,1)S(1)} %get-tuple-element.34.frames_ref), channel_id=1, source_target_pairs={{0,3},{1,2},{2,1},{3,0},{4,7},{5,6},{6,5},{7,4},{8,11},{9,10},{10,... | collective-permute-start | bytes 786440 | tf_op jit(solution)/shard_map/ppermute | solution.py:551
  51.8 3.6 %project_frames.4 = (bf16[4,512,1024]{2,1,0:T(8,128)(2,1)}, bf16[4,512,1024]{2,1,0:T(8,128)(2,1)}, f32[8,128]{1,0:T(8,128)S(1)}) custom-call(s32[1]{0:T(128)} %bitcast.place, bf16[8,64,256]{2,1,0:T(8,128)(2,1)S(1)} %get-tuple-element.34.frames_ref, bf16[4,8,256,1024]{3,2,1,0:T(8,128)(2,1)} %bitcast.25, bf16[4,8,256,1024]{3,2,1,0:T(8,128)(2,1)} %bitcast.26, ...), custom_call_target="tpu_custom_call" | custom-call | flops 1000 | bytes 1000 | tf_op jit(solution)/shard_map/project_frames/pallas_call | solution.py:365
  56.5 2.1 %collective-permute-start.7 = (f32[64,64]{1,0:T(8,128)S(1)}, f32[64,64]{1,0:T(8,128)S(1)}, u32[]{:S(2)}, u32[]{:S(2)}) collective-permute-start(f32[64,64]{1,0:T(8,128)S(1)} %get-tuple-element.36.refs_0_), channel_id=1, source_target_pairs={{0,2},{1,3},{2,0},{3,1},{4,6},{5,7},{6,4},{7,5},{8,10},{9,11},{10,... | collective-permute-start | bytes 49160 | tf_op jit(solution)/shard_map/ppermute | solution.py:551
  58.6 2.1 %collective-permute-start.8 = (f32[64,64]{1,0:T(8,128)S(1)}, f32[64,64]{1,0:T(8,128)S(1)}, u32[]{:S(2)}, u32[]{:S(2)}) collective-permute-start(f32[64,64]{1,0:T(8,128)S(1)} %get-tuple-element.36.refs_0_), channel_id=1, source_target_pairs={{0,3},{1,2},{2,1},{3,0},{4,7},{5,6},{6,5},{7,4},{8,11},{9,10},{10,... | collective-permute-start | bytes 49160 | tf_op jit(solution)/shard_map/ppermute | solution.py:551
  60.7 3.6 %project_frames.5 = (bf16[4,512,1024]{2,1,0:T(8,128)(2,1)}, bf16[4,512,1024]{2,1,0:T(8,128)(2,1)}, f32[8,128]{1,0:T(8,128)S(1)}) custom-call(s32[1]{0:T(128)} %bitcast.place, bf16[8,64,256]{2,1,0:T(8,128)(2,1)S(1)} %collective-permute-done.9.frames_ref, bf16[4,8,256,1024]{3,2,1,0:T(8,128)(2,1)} %bitcast.29, ...), custom_call_target="tpu_custom_call", output_to_operand_aliasing={{0}: (6, {}), {1}: (7, {})} | custom-call | flops 1000 | bytes 1000 | tf_op jit(solution)/shard_map/project_frames/pallas_call | solution.py:365
  64.3 3.3 %first_inverse.1.refs_4_ = f32[64,64]{1,0:T(8,128)S(1)} custom-call(f32[64,64]{1,0:T(8,128)S(1)} %get-tuple-element.37.v_gram_ref, f32[64,64]{1,0:T(8,128)S(1)} %get-tuple-element.38.w_gram_ref, f32[8,128]{1,0:T(8,128)S(1)} %get-tuple-element.41.after_ref), custom_call_target="tpu_custom_call" | custom-call | flops 1000 | bytes 1000 | tf_op jit(solution)/shard_map/first_inverse/pallas_call | solution.py:248
  67.6 3.7 %project_frames.6 = (bf16[4,512,1024]{2,1,0:T(8,128)(2,1)}, bf16[4,512,1024]{2,1,0:T(8,128)(2,1)}, f32[8,128]{1,0:T(8,128)}) custom-call(s32[1]{0:T(128)} %bitcast.place, bf16[8,64,256]{2,1,0:T(8,128)(2,1)S(1)} %collective-permute-done.11.frames_ref, bf16[4,8,256,1024]{3,2,1,0:T(8,128)(2,1)} %bitcast.33, ...), custom_call_target="tpu_custom_call", output_to_operand_aliasing={{0}: (6, {}), {1}: (7, {})} | custom-call | flops 1000 | bytes 1000 | tf_op jit(solution)/shard_map/project_frames/pallas_call | solution.py:365
  71.3 2.1 %collective-permute-done.10.frames_ref = bf16[8,64,256]{2,1,0:T(8,128)(2,1)S(1)} collective-permute-done((bf16[8,64,256]{2,1,0:T(8,128)(2,1)S(1)}, bf16[8,64,256]{2,1,0:T(8,128)(2,1)S(1)}, u32[]{:S(2)}, u32[]{:S(2)}) %collective-permute-start.10) | collective-permute-done | bytes 262176 | tf_op jit(solution)/shard_map/ppermute | solution.py:551
  73.4 3.6 %project_frames.7 = (bf16[4,512,1024]{2,1,0:T(8,128)(2,1)}, bf16[4,512,1024]{2,1,0:T(8,128)(2,1)}, f32[8,128]{1,0:T(8,128)S(1)}) custom-call(s32[1]{0:T(128)} %bitcast.place, bf16[8,64,256]{2,1,0:T(8,128)(2,1)S(1)} %collective-permute-done.10.frames_ref, bf16[4,8,256,1024]{3,2,1,0:T(8,128)(2,1)} %bitcast.37, ...), custom_call_target="tpu_custom_call", output_to_operand_aliasing={{0}: (6, {}), {1}: (7, {})} | custom-call | flops 1000 | bytes 1000 | tf_op jit(solution)/shard_map/project_frames/pallas_call | solution.py:365
  78.0 5.0 %v_terms.1 = (f32[64,512]{1,0:T(8,128)S(1)}, f32[64,512]{1,0:T(8,128)S(1)}) custom-call(s32[1]{0:T(128)} %bitcast.3.core, bf16[4,192,512]{2,1,0:T(8,128)(2,1)S(1)} %get-tuple-element.48.factor_ref, bf16[4,512,1024]{2,1,0:T(8,128)(2,1)} %get-tuple-element.49.first_ref.refs_2_, bf16[4,512,1024]{2,1,0:T(8,128)(2,1)} %get-tuple-element.50.second_ref.refs_3_), custom_call_target="tpu_custom_call" | custom-call | flops 1000 | bytes 1000 | tf_op jit(solution)/shard_map/v_terms/pallas_call | solution.py:461
  84.5 1.5 %collective-permute-start.13 = (f32[64,512]{1,0:T(8,128)S(1)}, f32[64,512]{1,0:T(8,128)S(1)}, u32[]{:S(2)}, u32[]{:S(2)}) collective-permute-start(f32[64,512]{1,0:T(8,128)S(1)} %add.3.a_ref), channel_id=1, source_target_pairs={{0,8},{4,12},{8,0},{12,4},{1,9},{5,13},{9,1},{13,5},{2,10},{6,14},... | collective-permute-start | bytes 393224 | tf_op jit(solution)/shard_map/ppermute | solution.py:551
  86.1 3.5 %second_inverse.1 = (f32[64,64]{1,0:T(8,128)S(1)}, f32[64,64]{1,0:T(8,128)S(1)}) custom-call(f32[64,64]{1,0:T(8,128)S(1)} %copy-done.2, f32[64,64]{1,0:T(8,128)S(1)} %get-tuple-element.38.w_gram_ref), custom_call_target="tpu_custom_call" | custom-call | flops 1000 | bytes 1000 | tf_op jit(solution)/shard_map/second_inverse/pallas_call | solution.py:426
  91.6 6.9 %next_v.1 = (f32[64,1024]{1,0:T(8,128)}, f32[64,128]{1,0:T(8,128)S(1)}) custom-call(s32[1]{0:T(128)} %bitcast.place, s32[1]{0:T(128)} %bitcast.3.core, f32[64,512]{1,0:T(8,128)S(1)} %add_terms.1.own_ref, f32[64,512]{1,0:T(8,128)S(1)} %collective-permute-done.14.other_ref, f32[64,64]{1,0:T(8,128)S(1)} %get-tuple-element.53.after_ref.refs_0_, ...), custom_call_target="tpu_custom_call" | custom-call | flops 1000 | bytes 1000 | tf_op jit(solution)/shard_map/next_v/pallas_call | solution.py:509
  98.5 2.7 %collective-permute-start.16 = (f32[64,128]{1,0:T(8,128)S(1)}, f32[64,128]{1,0:T(8,128)S(1)}, u32[]{:S(2)}, u32[]{:S(2)}) collective-permute-start(f32[64,128]{1,0:T(8,128)S(1)} %get-tuple-element.55.refs_0_), channel_id=1, source_target_pairs={{0,2},{1,3},{2,0},{3,1},{4,6},{5,7},{6,4},{7,5},{8,10},{9,11},{10,... | collective-permute-start | bytes 98312 | tf_op jit(solution)/shard_map/ppermute | solution.py:551
  101.3 1.5 %collective-permute-start.17 = (f32[64,128]{1,0:T(8,128)S(1)}, f32[64,128]{1,0:T(8,128)S(1)}, u32[]{:S(2)}, u32[]{:S(2)}) collective-permute-start(f32[64,128]{1,0:T(8,128)S(1)} %get-tuple-element.55.refs_0_), channel_id=1, source_target_pairs={{0,3},{1,2},{2,1},{3,0},{4,7},{5,6},{6,5},{7,4},{8,11},{9,10},{10,... | collective-permute-start | bytes 98312 | tf_op jit(solution)/shard_map/ppermute | solution.py:551
  103.9 3.1 %collective-permute-done.17.refs_3_ = f32[64,128]{1,0:T(8,128)S(1)} collective-permute-done((f32[64,128]{1,0:T(8,128)S(1)}, f32[64,128]{1,0:T(8,128)S(1)}, u32[]{:S(2)}, u32[]{:S(2)}) %collective-permute-start.17) | collective-permute-done | bytes 32800 | tf_op jit(solution)/shard_map/ppermute | solution.py:551
  107.0 4.0 %next_w.1 = f32[32,64]{1,0:T(8,128)} custom-call(f32[64,128]{1,0:T(8,128)S(1)} %get-tuple-element.55.refs_0_, f32[64,128]{1,0:T(8,128)S(1)} %collective-permute-done.15.refs_1_, f32[64,128]{1,0:T(8,128)S(1)} %collective-permute-done.16.refs_2_, f32[64,128]{1,0:T(8,128)S(1)} %collective-permute-done.17.refs_3_, f32[64,64]{1,0:T(8,128)S(1)} %get-tuple-element.56.refs_4_), custom_call_target="tpu_custom_call" | custom-call | flops 1000 | bytes 1000 | tf_op jit(solution)/shard_map/next_w/pallas_call | solution.py:540
  (40 shorter events, 11.9 us)
Async XLA Ops:
  0.6 0.9 copy-start
  5.3 16.8 %collective-permute-start = (s16[560,256]{1,0:T(8,128)(2,1)S(1)}, s16[560,256]{1,0:T(8,128)(2,1)S(1)}, u32[]{:S(2)}, u32[]{:S(2)}) collective-permute-start(s16[560,256]{1,0:T(8,128)(2,1)S(1)} %project_send.3), channel_id=1, source_target_pairs={{0,3},{1,2},{2,1},{3,0},{4,7},{5,6},{6,5},{7,4},{8,11},{9,10},{10,... | collective-permute-start | bytes 860168 | tf_op jit(solution)/shard_map/ppermute | solution.py:551
  14.2 4.5 %copy-start.1 = (f32[32,64]{1,0:T(8,128)S(1)}, f32[32,64]{1,0:T(8,128)}, u32[]{:S(2)}) copy-start(f32[32,64]{1,0:T(8,128)} %refs_5_.1) | copy-start | bytes 24580
  14.2 20.6 %collective-permute-start.1 = (s16[560,256]{1,0:T(8,128)(2,1)S(1)}, s16[560,256]{1,0:T(8,128)(2,1)S(1)}, u32[]{:S(2)}, u32[]{:S(2)}) collective-permute-start(s16[560,256]{1,0:T(8,128)(2,1)S(1)} %project_send.4), channel_id=1, source_target_pairs={{0,2},{1,3},{2,0},{3,1},{4,6},{5,7},{6,4},{7,5},{8,10},{9,11},{10,... | collective-permute-start | bytes 860168 | tf_op jit(solution)/shard_map/ppermute | solution.py:551
  18.0 16.8 %copy-start.3 = (f32[64,64]{1,0:T(8,128)S(1)}, f32[64,64]{1,0:T(8,128)}, u32[]{:S(2)}) copy-start(f32[64,64]{1,0:T(8,128)} %h_ref.1) | copy-start | bytes 49156
  18.1 16.8 %copy-start.4 = (s32[32]{0:T(128)S(1)}, s32[32]{0:T(128)}, u32[]{:S(2)}) copy-start(s32[32]{0:T(128)} %counts_ref.1) | copy-start | bytes 388
  18.1 16.8 %collective-permute-start.2 = (s16[560,256]{1,0:T(8,128)(2,1)S(1)}, s16[560,256]{1,0:T(8,128)(2,1)S(1)}, u32[]{:S(2)}, u32[]{:S(2)}) collective-permute-start(s16[560,256]{1,0:T(8,128)(2,1)S(1)} %project_send.5), channel_id=1, source_target_pairs={{0,1},{1,0},{2,3},{3,2},{4,5},{5,4},{6,7},{7,6},{8,9},{9,8},{10,11... | collective-permute-start | bytes 860168 | tf_op jit(solution)/shard_map/ppermute | solution.py:551
  45.8 12.8 %collective-permute-start.9 = (bf16[8,64,256]{2,1,0:T(8,128)(2,1)S(1)}, bf16[8,64,256]{2,1,0:T(8,128)(2,1)S(1)}, u32[]{:S(2)}, u32[]{:S(2)}) collective-permute-start(bf16[8,64,256]{2,1,0:T(8,128)(2,1)S(1)} %get-tuple-element.34.frames_ref), channel_id=1, source_target_pairs={{0,1},{1,0},{2,3},{3,2},{4,5},{5,4},{6,7},{7,6},{8,9},{9,8},{10,11... | collective-permute-start | bytes 786440 | tf_op jit(solution)/shard_map/ppermute | solution.py:551
  45.9 21.7 %collective-permute-start.11 = (bf16[8,64,256]{2,1,0:T(8,128)(2,1)S(1)}, bf16[8,64,256]{2,1,0:T(8,128)(2,1)S(1)}, u32[]{:S(2)}, u32[]{:S(2)}) collective-permute-start(bf16[8,64,256]{2,1,0:T(8,128)(2,1)S(1)} %get-tuple-element.34.frames_ref), channel_id=1, source_target_pairs={{0,3},{1,2},{2,1},{3,0},{4,7},{5,6},{6,5},{7,4},{8,11},{9,10},{10,... | collective-permute-start | bytes 786440 | tf_op jit(solution)/shard_map/ppermute | solution.py:551
  48.4 24.9 %collective-permute-start.10 = (bf16[8,64,256]{2,1,0:T(8,128)(2,1)S(1)}, bf16[8,64,256]{2,1,0:T(8,128)(2,1)S(1)}, u32[]{:S(2)}, u32[]{:S(2)}) collective-permute-start(bf16[8,64,256]{2,1,0:T(8,128)(2,1)S(1)} %get-tuple-element.34.frames_ref), channel_id=1, source_target_pairs={{0,2},{1,3},{2,0},{3,1},{4,6},{5,7},{6,4},{7,5},{8,10},{9,11},{10,... | collective-permute-start | bytes 786440 | tf_op jit(solution)/shard_map/ppermute | solution.py:551
  49.4 1.5 %collective-permute-start.3 = (f32[64,128]{1,0:T(8,128)S(1)}, f32[64,128]{1,0:T(8,128)S(1)}, u32[]{:S(2)}, u32[]{:S(2)}) collective-permute-start(f32[64,128]{1,0:T(8,128)S(1)} %get-tuple-element.33.refs_0_), channel_id=1, source_target_pairs={{0,4},{4,0},{8,12},{12,8},{1,5},{5,1},{9,13},{13,9},{2,6},{6,2},{1... | collective-permute-start | bytes 98312 | tf_op jit(solution)/shard_map/ppermute | solution.py:551
  49.4 6.1 %collective-permute-start.4 = (f32[64,128]{1,0:T(8,128)S(1)}, f32[64,128]{1,0:T(8,128)S(1)}, u32[]{:S(2)}, u32[]{:S(2)}) collective-permute-start(f32[64,128]{1,0:T(8,128)S(1)} %get-tuple-element.33.refs_0_), channel_id=1, source_target_pairs={{0,8},{4,12},{8,0},{12,4},{1,9},{5,13},{9,1},{13,5},{2,10},{6,14},... | collective-permute-start | bytes 98312 | tf_op jit(solution)/shard_map/ppermute | solution.py:551
  50.9 4.6 %collective-permute-start.5 = (f32[64,128]{1,0:T(8,128)S(1)}, f32[64,128]{1,0:T(8,128)S(1)}, u32[]{:S(2)}, u32[]{:S(2)}) collective-permute-start(f32[64,128]{1,0:T(8,128)S(1)} %get-tuple-element.33.refs_0_), channel_id=1, source_target_pairs={{0,12},{4,8},{8,4},{12,0},{1,13},{5,9},{9,5},{13,1},{2,14},{6,10},... | collective-permute-start | bytes 98312 | tf_op jit(solution)/shard_map/ppermute | solution.py:551
  55.5 21.4 %collective-permute-start.6 = (f32[64,64]{1,0:T(8,128)S(1)}, f32[64,64]{1,0:T(8,128)S(1)}, u32[]{:S(2)}, u32[]{:S(2)}) collective-permute-start(f32[64,64]{1,0:T(8,128)S(1)} %get-tuple-element.36.refs_0_), channel_id=1, source_target_pairs={{0,1},{1,0},{2,3},{3,2},{4,5},{5,4},{6,7},{7,6},{8,9},{9,8},{10,11... | collective-permute-start | bytes 49160 | tf_op jit(solution)/shard_map/ppermute | solution.py:551
  56.5 20.5 %collective-permute-start.7 = (f32[64,64]{1,0:T(8,128)S(1)}, f32[64,64]{1,0:T(8,128)S(1)}, u32[]{:S(2)}, u32[]{:S(2)}) collective-permute-start(f32[64,64]{1,0:T(8,128)S(1)} %get-tuple-element.36.refs_0_), channel_id=1, source_target_pairs={{0,2},{1,3},{2,0},{3,1},{4,6},{5,7},{6,4},{7,5},{8,10},{9,11},{10,... | collective-permute-start | bytes 49160 | tf_op jit(solution)/shard_map/ppermute | solution.py:551
  58.6 18.4 %collective-permute-start.8 = (f32[64,64]{1,0:T(8,128)S(1)}, f32[64,64]{1,0:T(8,128)S(1)}, u32[]{:S(2)}, u32[]{:S(2)}) collective-permute-start(f32[64,64]{1,0:T(8,128)S(1)} %get-tuple-element.36.refs_0_), channel_id=1, source_target_pairs={{0,3},{1,2},{2,1},{3,0},{4,7},{5,6},{6,5},{7,4},{8,11},{9,10},{10,... | collective-permute-start | bytes 49160 | tf_op jit(solution)/shard_map/ppermute | solution.py:551
  78.0 8.0 %copy-start.2 = (f32[64,64]{1,0:T(8,128)S(1)}, f32[64,64]{1,0:T(8,128)}, u32[]{:S(2)}) copy-start(f32[64,64]{1,0:T(8,128)} %get-tuple-element.27.h_ref.refs_1_) | copy-start | bytes 49156
  83.1 1.4 %collective-permute-start.12 = (f32[64,512]{1,0:T(8,128)S(1)}, f32[64,512]{1,0:T(8,128)S(1)}, u32[]{:S(2)}, u32[]{:S(2)}) collective-permute-start(f32[64,512]{1,0:T(8,128)S(1)} %get-tuple-element.52), channel_id=1, source_target_pairs={{0,4},{4,0},{8,12},{12,8},{1,5},{5,1},{9,13},{13,9},{2,6},{6,2},{1... | collective-permute-start | bytes 393224 | tf_op jit(solution)/shard_map/ppermute | solution.py:551
  84.5 5.6 %collective-permute-start.13 = (f32[64,512]{1,0:T(8,128)S(1)}, f32[64,512]{1,0:T(8,128)S(1)}, u32[]{:S(2)}, u32[]{:S(2)}) collective-permute-start(f32[64,512]{1,0:T(8,128)S(1)} %add.3.a_ref), channel_id=1, source_target_pairs={{0,8},{4,12},{8,0},{12,4},{1,9},{5,13},{9,1},{13,5},{2,10},{6,14},... | collective-permute-start | bytes 393224 | tf_op jit(solution)/shard_map/ppermute | solution.py:551
  90.1 1.4 %collective-permute-start.14 = (f32[64,512]{1,0:T(8,128)S(1)}, f32[64,512]{1,0:T(8,128)S(1)}, u32[]{:S(2)}, u32[]{:S(2)}) collective-permute-start(f32[64,512]{1,0:T(8,128)S(1)} %add_terms.1.own_ref), channel_id=1, source_target_pairs={{0,4},{4,0},{8,12},{12,8},{1,5},{5,1},{9,13},{13,9},{2,6},{6,2},{1... | collective-permute-start | bytes 393224 | tf_op jit(solution)/shard_map/ppermute | solution.py:551
  98.4 4.4 %collective-permute-start.15 = (f32[64,128]{1,0:T(8,128)S(1)}, f32[64,128]{1,0:T(8,128)S(1)}, u32[]{:S(2)}, u32[]{:S(2)}) collective-permute-start(f32[64,128]{1,0:T(8,128)S(1)} %get-tuple-element.55.refs_0_), channel_id=1, source_target_pairs={{0,1},{1,0},{2,3},{3,2},{4,5},{5,4},{6,7},{7,6},{8,9},{9,8},{10,11... | collective-permute-start | bytes 98312 | tf_op jit(solution)/shard_map/ppermute | solution.py:551
  98.5 5.3 %collective-permute-start.16 = (f32[64,128]{1,0:T(8,128)S(1)}, f32[64,128]{1,0:T(8,128)S(1)}, u32[]{:S(2)}, u32[]{:S(2)}) collective-permute-start(f32[64,128]{1,0:T(8,128)S(1)} %get-tuple-element.55.refs_0_), channel_id=1, source_target_pairs={{0,2},{1,3},{2,0},{3,1},{4,6},{5,7},{6,4},{7,5},{8,10},{9,11},{10,... | collective-permute-start | bytes 98312 | tf_op jit(solution)/shard_map/ppermute | solution.py:551
  101.3 5.7 %collective-permute-start.17 = (f32[64,128]{1,0:T(8,128)S(1)}, f32[64,128]{1,0:T(8,128)S(1)}, u32[]{:S(2)}, u32[]{:S(2)}) collective-permute-start(f32[64,128]{1,0:T(8,128)S(1)} %get-tuple-element.55.refs_0_), channel_id=1, source_target_pairs={{0,3},{1,2},{2,1},{3,0},{4,7},{5,6},{6,5},{7,4},{8,11},{9,10},{10,... | collective-permute-start | bytes 98312 | tf_op jit(solution)/shard_map/ppermute | solution.py:551

commit v4 on v3

--- a/solution.py
+++ b/solution.py
@@ -48,15 +48,7 @@
     return lax.broadcasted_iota(jnp.int32, shape, len(shape) - 1)
 
 
-def batch_of(share):
-    return 4 if share % 4 == 0 else share
-
-
 ANY_SPEC = pl.BlockSpec(memory_space=pl.ANY)
-
-
-def whole(shape):
-    return pl.BlockSpec(shape, lambda *place: (0,) * len(shape))
 
 
 def parameters(mib):
@@ -82,21 +74,20 @@
     return jnp.ceil(jnp.log2(jnp.maximum(top, 1e-30)))
 
 
-def encode_batch(step, batch, v_ref, visits_refs, coded_ref, exponents_ref):
-    rank = v_ref.shape[0]
-    exponents = exponents_ref[...]
-    lanes = lane_numbers(exponents.shape)
-    for p in range(batch):
-        proj = low_dot(v_ref[...], visits_refs[p][0, 0], ROWS_BY_ROWS)
-        exponent = row_exponent(proj)
-        coded = jnp.floor(proj * (LEVELS / jnp.exp2(exponent)) + 0.5)
-        row = pl.multiple_of((step * batch + p) * rank, rank)
-        coded_ref[pl.ds(row, rank), :] = coded.astype(jnp.int32).astype(jnp.int16)
-        exponents = jnp.where(lanes == step * batch + p, exponent, exponents)
-    exponents_ref[...] = exponents
-
-
-def encode_rest(share, v_ref, coded_ref, exponents_ref):
+def fetch(source, buffers, sems):
+    copies = [
+        pltpu.make_async_copy(source.at[p], buffers.at[p], sems.at[p]) for p in range(buffers.shape[0])
+    ]
+    for copy in copies:
+        copy.start()
+    return copies
+
+
+def project_patient(v_ref, visits):
+    return low_dot(visits, v_ref[...], ROWS_BY_ROWS).T
+
+
+def encode_rest(share, v_ref, coded_ref, exponents):
     rank = v_ref.shape[0]
     gram = low_dot(v_ref[...], v_ref[...], ROWS_BY_ROWS)
     exponent = row_exponent(gram)
@@ -106,7 +97,6 @@
     digits = jnp.concatenate([first, second], axis=1)
     digits = jnp.concatenate([digits[: rank // 2], digits[rank // 2 :]], axis=1)
     coded_ref[pl.ds(share * rank, rank // 2), :] = digits.astype(jnp.int32).astype(jnp.int16)
-    exponents = exponents_ref[...]
     exponents = jnp.where(lane_numbers(exponents.shape) == share, exponent, exponents)
     rows = exponent_rows(share)
     last = exponents.T[:rows]
@@ -126,105 +116,103 @@
     return [rows(p * rank, rank) * steps[:, p : p + 1] for p in range(share)], gram
 
 
-def send_projection_kernel(batch, share, place, v_ref, *refs):
-    visits_refs = refs[:batch]
-    coded_ref, exponents_ref = refs[batch:]
-    step = pl.program_id(0)
-
-    @pl.when(step == 0)
-    def _():
-        exponents_ref[...] = jnp.zeros_like(exponents_ref)
-
-    encode_batch(step, batch, v_ref, visits_refs, coded_ref, exponents_ref)
-
-    @pl.when(step == share // batch - 1)
-    def _():
-        encode_rest(share, v_ref, coded_ref, exponents_ref)
-
-
-def own_projection_kernel(batch, place, v_ref, w_ref, *refs):
-    visits_refs = refs[:batch]
-    proj_ref, v_gram_ref, w_gram_ref = refs[batch:]
-
-    @pl.when(pl.program_id(0) == 0)
-    def _():
-        v_gram_ref[...] = low_dot(v_ref[...], v_ref[...], ROWS_BY_ROWS)
-        w_gram_ref[...] = high_dot(w_ref[...], w_ref[...], COLS_BY_COLS)
-
-    for p in range(batch):
-        proj_ref[p] = low_dot(v_ref[...], visits_refs[p][0, 0], ROWS_BY_ROWS)
-
-
-def visits_specs(slot, batch, slots, width):
-    return [
-        pl.BlockSpec((1, 1, slots, width), lambda i, place, p=p: (place[0] ^ slot, i * batch + p, 0, 0))
-        for p in range(batch)
-    ]
+def send_projection_kernel(slot, place, v_ref, visits_ref, coded_ref, buffers, sems):
+    copies = fetch(visits_ref.at[place[0] ^ slot], buffers, sems)
+    share, rank = len(copies), v_ref.shape[0]
+    exponents = jnp.zeros((rank, LANES), F32)
+    for p, copy in enumerate(copies):
+        copy.wait()
+        proj = project_patient(v_ref, buffers[p])
+        exponent = row_exponent(proj)
+        coded = jnp.floor(proj * (LEVELS / jnp.exp2(exponent)) + 0.5)
+        coded_ref[pl.ds(p * rank, rank), :] = coded.astype(jnp.int32).astype(jnp.int16)
+        exponents = jnp.where(lane_numbers(exponents.shape) == p, exponent, exponents)
+    encode_rest(share, v_ref, coded_ref, exponents)
+
+
+def own_projection_kernel(place, v_ref, w_ref, visits_ref, proj_ref, v_gram_ref, w_gram_ref, buffers, sems):
+    copies = fetch(visits_ref.at[place[0]], buffers, sems)
+    v_gram_ref[...] = low_dot(v_ref[...], v_ref[...], ROWS_BY_ROWS)
+    w_gram_ref[...] = high_dot(w_ref[...], w_ref[...], COLS_BY_COLS)
+    for p, copy in enumerate(copies):
+        copy.wait()
+        proj_ref[p] = project_patient(v_ref, buffers[p])
+
+
+def visits_buffers(visits):
+    share = visits.shape[1]
+    return [pltpu.VMEM(visits.shape[1:], BF16), pltpu.SemaphoreType.DMA((share,))]
 
 
 def project_for(slot, place, visits, v_rows):
     _, share, slots, width = visits.shape
     rank = v_rows.shape[0]
-    batch = batch_of(share)
-    coded = payload_shape(share, rank, slots)
-    return pl.pallas_call(
-        functools.partial(send_projection_kernel, batch, share),
-        grid_spec=pltpu.PrefetchScalarGridSpec(
-            num_scalar_prefetch=1,
-            grid=(share // batch,),
-            in_specs=[whole(v_rows.shape)] + visits_specs(slot, batch, slots, width),
-            out_specs=whole(coded),
-            scratch_shapes=[pltpu.VMEM((rank, LANES), F32)],
-        ),
-        out_shape=jax.ShapeDtypeStruct(coded, jnp.int16),
+    return pl.pallas_call(
+        functools.partial(send_projection_kernel, slot),
+        in_specs=[SMEM_SPEC, VMEM_SPEC, ANY_SPEC],
+        out_specs=VMEM_SPEC,
+        out_shape=jax.ShapeDtypeStruct(payload_shape(share, rank, slots), jnp.int16),
+        scratch_shapes=visits_buffers(visits),
         compiler_params=parameters(STREAM),
         cost_estimate=SHORT,
         name="project_send",
-    )(place, v_rows, *[visits] * batch)
+    )(place, v_rows, visits)
 
 
 def project_own(place, visits, v_rows, w_start):
     _, share, slots, width = visits.shape
     rank = v_rows.shape[0]
-    batch = batch_of(share)
     gram = (rank, rank)
     return pl.pallas_call(
-        functools.partial(own_projection_kernel, batch),
-        grid_spec=pltpu.PrefetchScalarGridSpec(
-            num_scalar_prefetch=1,
-            grid=(share // batch,),
-            in_specs=[whole(v_rows.shape), whole(w_start.shape)] + visits_specs(0, batch, slots, width),
-            out_specs=[
-                pl.BlockSpec((batch, rank, slots), lambda i, place: (i, 0, 0)),
-                whole(gram),
-                whole(gram),
-            ],
-        ),
+        own_projection_kernel,
+        in_specs=[SMEM_SPEC, VMEM_SPEC, VMEM_SPEC, ANY_SPEC],
+        out_specs=[VMEM_SPEC] * 3,
         out_shape=[
             jax.ShapeDtypeStruct((share, rank, slots), F32),
             jax.ShapeDtypeStruct(gram, F32),
             jax.ShapeDtypeStruct(gram, F32),
         ],
+        scratch_shapes=visits_buffers(visits),
         compiler_params=parameters(STREAM),
         cost_estimate=SHORT,
         name="project_own",
-    )(place, v_rows, w_start, *[visits] * batch)
+    )(place, v_rows, w_start, visits)
+
+
+def pair_inverse(a, b, c, d):
+    scale = 1.0 / (a * d - b * c)
+    return d * scale, b * scale, c * scale, a * scale
 
 
 def eliminate(table, rank):
-    rows = lax.broadcasted_iota(jnp.int32, table.shape, 0)
-    for i in range(0, rank, 2):
-        first = jnp.broadcast_to(table[:, i : i + 1], table.shape)
-        second = jnp.broadcast_to(table[:, i + 1 : i + 2], table.shape)
-        row_first, row_second = table[i : i + 1], table[i + 1 : i + 2]
-        a, b = first[i : i + 1], second[i : i + 1]
-        c, d = first[i + 1 : i + 2], second[i + 1 : i + 2]
-        scale = 1.0 / (a * d - b * c)
-        new_first = (d * row_first - b * row_second) * scale
-        new_second = (a * row_second - c * row_first) * scale
-        table = table - first * new_first - second * new_second
-        table = jnp.where(rows == i, new_first, jnp.where(rows == i + 1, new_second, table))
-    return table
+    tiles = [table[8 * t : 8 * t + 8] for t in range(rank // 8)]
+    rows = lax.broadcasted_iota(jnp.int32, tiles[0].shape, 0)
+    for i in range(0, rank, 4):
+        columns = [[jnp.broadcast_to(t[:, i + q : i + q + 1], t.shape) for q in range(4)] for t in tiles]
+        home, first = i // 8, i % 8
+        r0, r1, r2, r3 = (tiles[home][first + q : first + q + 1] for q in range(4))
+        m = [[columns[home][q][first + p : first + p + 1] for q in range(4)] for p in range(4)]
+        d, b, c, a = pair_inverse(m[0][0], m[0][1], m[1][0], m[1][1])
+        q02, q03 = d * m[0][2] - b * m[1][2], d * m[0][3] - b * m[1][3]
+        q12, q13 = a * m[1][2] - c * m[0][2], a * m[1][3] - c * m[0][3]
+        y0, y1 = d * r0 - b * r1, a * r1 - c * r0
+        z2 = r2 - (m[2][0] * y0 + m[2][1] * y1)
+        z3 = r3 - (m[3][0] * y0 + m[3][1] * y1)
+        d, b, c, a = pair_inverse(
+            m[2][2] - (m[2][0] * q02 + m[2][1] * q12),
+            m[2][3] - (m[2][0] * q03 + m[2][1] * q13),
+            m[3][2] - (m[3][0] * q02 + m[3][1] * q12),
+            m[3][3] - (m[3][0] * q03 + m[3][1] * q13),
+        )
+        n2, n3 = d * z2 - b * z3, a * z3 - c * z2
+        new = [y0 - (q02 * n2 + q03 * n3), y1 - (q12 * n2 + q13 * n3), n2, n3]
+        for t, (c0, c1, c2, c3) in enumerate(columns):
+            tile = tiles[t] - ((c0 * new[0] + c1 * new[1]) + (c2 * new[2] + c3 * new[3]))
+            if t == home:
+                for q in range(4):
+                    tile = jnp.where(rows == first + q, new[q], tile)
+            tiles[t] = tile
+    return jnp.concatenate(tiles, axis=0)
 
 
 def inverse_of(gram):
@@ -282,10 +270,12 @@
     first, second = two_parts(frame)
     if fine:
         both = low_dot(jnp.concatenate([first, second], axis=0), first, ROWS_BY_ROWS)
-        gram = both[:rank] + both[rank:] + low_dot(first, second, ROWS_BY_ROWS)
+        gram = both[:rank] + (both[rank:] + both[rank:].T)
         gram_first, gram_second = two_parts(gram)
-        moved = low_dot(jnp.concatenate([gram_first, gram_second], axis=0), first)
-        moved = moved[:rank] + moved[rank:] + low_dot(gram_first, second)
+        moved = low_dot(
+            jnp.concatenate([gram_first, gram_second, gram_first], axis=1),
+            jnp.concatenate([first, first, second], axis=0),
+        )
     else:
         moved = low_dot(low_dot(first, first, ROWS_BY_ROWS).astype(BF16), first)
     frames[p] = 1.5 * frame - 0.5 * moved
@@ -347,37 +337,44 @@
     )(place, counts, h_start, w_start, v_gram, w_gram, own, *coded)
 
 
-def projected_kernel(batch, place, frames_ref, *refs):
-    first_ref, second_ref, token_ref = refs[-3:]
+def projected_kernel(slot, place, frames_ref, visits_ref, *refs):
+    first_ref, second_ref, token_ref, buffers, first, second, sems, out_sems = refs[-8:]
+    copies = fetch(visits_ref.at[place[0] ^ slot], buffers, sems)
     rank = frames_ref.shape[1]
     token_ref[...] = jnp.zeros_like(token_ref)
-    for p in range(batch):
-        rows = slice(p * rank, (p + 1) * rank)
-        first_ref[0, rows], second_ref[0, rows] = two_parts(low_dot(frames_ref[p], refs[p][0, 0]))
+    sent = []
+    for p, copy in enumerate(copies):
+        copy.wait()
+        rows = pl.ds(p * rank, rank)
+        first[rows, :], second[rows, :] = two_parts(low_dot(frames_ref[p], buffers[p]))
+        for i, (source, target) in enumerate([(first, first_ref), (second, second_ref)]):
+            sent.append(pltpu.make_async_copy(source.at[rows], target.at[slot, rows], out_sems.at[i, p]))
+            sent[-1].start()
+    for copy in sent:
+        copy.wait()
 
 
 def project_frames(slot, place, frames, visits, before):
     n_slots, share, slots, width = visits.shape
     rank = frames.shape[1]
-    batch = batch_of(share)
     out = jax.ShapeDtypeStruct((n_slots, share * rank, width), BF16)
-    aliases = {batch + 2: 0, batch + 3: 1} if before else {}
     *before, token = pl.pallas_call(
-        functools.partial(projected_kernel, batch),
-        grid_spec=pltpu.PrefetchScalarGridSpec(
-            num_scalar_prefetch=1,
-            grid=(share // batch,),
-            in_specs=[pl.BlockSpec((batch, rank, slots), lambda i, place: (i, 0, 0))]
-            + visits_specs(slot, batch, slots, width)
-            + [ANY_SPEC] * len(before),
-            out_specs=[pl.BlockSpec((1, batch * rank, width), lambda i, place: (slot, i, 0))] * 2 + [whole((8, LANES))],
-        ),
+        functools.partial(projected_kernel, slot),
+        in_specs=[SMEM_SPEC, VMEM_SPEC, ANY_SPEC] + [ANY_SPEC] * len(before),
+        out_specs=[ANY_SPEC, ANY_SPEC, VMEM_SPEC],
         out_shape=[out, out, jax.ShapeDtypeStruct((8, LANES), F32)],
-        input_output_aliases=aliases,
+        scratch_shapes=[
+            pltpu.VMEM(visits.shape[1:], BF16),
+            pltpu.VMEM((share * rank, width), BF16),
+            pltpu.VMEM((share * rank, width), BF16),
+            pltpu.SemaphoreType.DMA((share,)),
+            pltpu.SemaphoreType.DMA((2, share)),
+        ],
+        input_output_aliases={3: 0, 4: 1} if before else {},
         compiler_params=parameters(STREAM),
         cost_estimate=SHORT,
         name="project_frames",
-    )(place, frames, *[visits] * batch, *before)
+    )(place, frames, visits, *before)
     return before, token
 
 
@@ -432,26 +429,24 @@
     )(h_next, w_gram)
 
 
-def v_terms_kernel(core, factor_ref, first_ref, second_ref, keep_ref, send_ref, terms_ref):
-    step = pl.program_id(0)
+def v_terms_kernel(core, factor_ref, first_ref, second_ref, keep_ref, send_ref, terms_ref, first, second, sems):
+    firsts = fetch(first_ref, first, sems.at[0])
+    seconds = fetch(second_ref, second, sems.at[1])
     rank, width = terms_ref.shape
     half = width // 2
-    large = low_dot(factor_ref[0], first_ref[0])
-    small = low_dot(factor_ref[0, : 2 * rank], second_ref[0])
-    terms = large[:rank] + (large[rank : 2 * rank] + small[:rank]) + (large[2 * rank :] + small[rank:])
-
-    @pl.when(step == 0)
-    def _():
-        terms_ref[...] = terms
-
-    @pl.when(step > 0)
-    def _():
-        terms_ref[...] += terms
-
-    @pl.when(step == pl.num_programs(0) - 1)
-    def _():
-        keep_ref[...] = terms_ref[:, pl.ds(pl.multiple_of(core[0] * half, half), half)]
-        send_ref[...] = terms_ref[:, pl.ds(pl.multiple_of((1 - core[0]) * half, half), half)]
+    for slot, copies in enumerate(zip(firsts, seconds)):
+        for copy in copies:
+            copy.wait()
+        large = low_dot(factor_ref[slot], first[slot])
+        small = low_dot(factor_ref[slot, : 2 * rank], second[slot])
+        terms = large[:rank] + (large[rank : 2 * rank] + small[:rank]) + (large[2 * rank :] + small[rank:])
+        terms_ref[...] = terms + terms_ref[...] if slot else terms
+    keep_ref[...] = terms_ref[:, pl.ds(pl.multiple_of(core[0] * half, half), half)]
+    send_ref[...] = terms_ref[:, pl.ds(pl.multiple_of((1 - core[0]) * half, half), half)]
+
+
+def projected_buffers(projected):
+    return [pltpu.VMEM(projected.shape, BF16)] * 2 + [pltpu.SemaphoreType.DMA((2, projected.shape[0]))]
 
 
 def all_v_terms(core, factor, first, second):
@@ -460,47 +455,39 @@
     half = (rank, width // 2)
     return pl.pallas_call(
         v_terms_kernel,
-        grid_spec=pltpu.PrefetchScalarGridSpec(
-            num_scalar_prefetch=1,
-            grid=(n_slots,),
-            in_specs=[
-                pl.BlockSpec((1, 3 * rank, rows), lambda i, core: (i, 0, 0)),
-                pl.BlockSpec((1, rows, width), lambda i, core: (i, 0, 0)),
-                pl.BlockSpec((1, rows, width), lambda i, core: (i, 0, 0)),
-            ],
-            out_specs=[whole(half)] * 2,
-            scratch_shapes=[pltpu.VMEM((rank, width), F32)],
-        ),
+        in_specs=[SMEM_SPEC, VMEM_SPEC, ANY_SPEC, ANY_SPEC],
+        out_specs=[VMEM_SPEC] * 2,
         out_shape=[jax.ShapeDtypeStruct(half, F32)] * 2,
+        scratch_shapes=[pltpu.VMEM((rank, width), F32)] + projected_buffers(first),
         compiler_params=parameters(STREAM),
         cost_estimate=SHORT,
         name="v_terms",
     )(core, factor, first, second)
 
 
-def next_v_kernel(share, place, core, own_ref, other_ref, *refs):
-    inverse_ref, h_ref, first_ref, second_ref, v_ref, sums_ref, v_parts, weights = refs
-    slot = pl.program_id(0)
+def next_v_kernel(share, place, core, own_ref, other_ref, inverse_ref, h_ref, first_ref, second_ref, v_ref, sums_ref, *refs):
+    v_parts, first, second, sems = refs
+    firsts = fetch(first_ref, first, sems.at[0])
+    seconds = fetch(second_ref, second, sems.at[1])
     rank = inverse_ref.shape[0]
-
-    @pl.when(slot == 0)
-    def _():
-        upper = core[0] == 1
-        left = jnp.where(upper, other_ref[...], own_ref[...])
-        right = jnp.where(upper, own_ref[...], other_ref[...])
-        v_rows = high_dot(inverse_ref[...], jnp.concatenate([left, right], axis=1))
-        v_ref[...] = v_rows
-        v_parts[...] = jnp.concatenate(two_parts(v_rows), axis=0)
-        weights[...] = jnp.concatenate([h_ref[...]] * 2, axis=1)
-        gram = low_dot(v_parts[...], v_parts[...], ROWS_BY_ROWS)
-        gram = gram[:rank, :rank] + (gram[:rank, rank:] + gram[rank:, :rank])
-        sums_ref[...] = jnp.concatenate([jnp.zeros((rank, rank), F32), gram], axis=1)
-
-    seen = low_dot(first_ref[0], v_parts[...], ROWS_BY_ROWS) + low_dot(second_ref[0], v_parts[...], ROWS_BY_ROWS)
-    first = (place[0] ^ slot) * share
-    for p in range(share):
-        row = jnp.sum(seen[p * rank : (p + 1) * rank] * weights[...], axis=0, keepdims=True)
-        sums_ref[pl.ds(first + p, 1), :rank] = row[:, :rank] + row[:, rank:]
+    upper = core[0] == 1
+    left = jnp.where(upper, other_ref[...], own_ref[...])
+    right = jnp.where(upper, own_ref[...], other_ref[...])
+    v_rows = high_dot(inverse_ref[...], jnp.concatenate([left, right], axis=1))
+    v_ref[...] = v_rows
+    v_parts[...] = jnp.concatenate(two_parts(v_rows), axis=0)
+    weights = jnp.concatenate([h_ref[...]] * 2, axis=1)
+    gram = low_dot(v_parts[...], v_parts[...], ROWS_BY_ROWS)
+    gram = gram[:rank, :rank] + (gram[:rank, rank:] + gram[rank:, :rank])
+    sums_ref[...] = jnp.concatenate([jnp.zeros((rank, rank), F32), gram], axis=1)
+    for slot, copies in enumerate(zip(firsts, seconds)):
+        for copy in copies:
+            copy.wait()
+        seen = low_dot(first[slot], v_parts[...], ROWS_BY_ROWS) + low_dot(second[slot], v_parts[...], ROWS_BY_ROWS)
+        start = (place[0] ^ slot) * share
+        for p in range(share):
+            row = jnp.sum(seen[p * rank : (p + 1) * rank] * weights, axis=0, keepdims=True)
+            sums_ref[pl.ds(start + p, 1), :rank] = row[:, :rank] + row[:, rank:]
 
 
 def next_v(place, core, own, other, inverse, h_next, first, second):
@@ -508,19 +495,13 @@
     rank = inverse.shape[0]
     return pl.pallas_call(
         functools.partial(next_v_kernel, rows // rank),
-        grid_spec=pltpu.PrefetchScalarGridSpec(
-            num_scalar_prefetch=2,
-            grid=(n_slots,),
-            in_specs=[whole(own.shape)] * 2
-            + [whole((rank, rank))] * 2
-            + [pl.BlockSpec((1, rows, width), lambda i, place, core: (i, 0, 0))] * 2,
-            out_specs=[whole((rank, width)), whole((rank, 2 * rank))],
-            scratch_shapes=[pltpu.VMEM((2 * rank, width), BF16), pltpu.VMEM((rank, 2 * rank), F32)],
-        ),
+        in_specs=[SMEM_SPEC] * 2 + [VMEM_SPEC] * 4 + [ANY_SPEC] * 2,
+        out_specs=[VMEM_SPEC] * 2,
         out_shape=[
             jax.ShapeDtypeStruct((rank, width), F32),
             jax.ShapeDtypeStruct((rank, 2 * rank), F32),
         ],
+        scratch_shapes=[pltpu.VMEM((2 * rank, width), BF16)] + projected_buffers(first),
         compiler_params=parameters(STREAM),
         cost_estimate=SHORT,
         name="next_v",

time: 111 us -> 128 us (1.15)
  Pallas kernels: 63.9 us -> 84.8 us
  waiting for transfers between devices: 22.3 us -> 18.7 us
    pallas_call x1, Pallas kernels: 11 us -> 25.8 us  [own_frames(): pl.pallas_call(functools.partial(frames_kernel, share, len(coded)), in_sp...]
    pallas_call x10, Pallas kernels: 41 us -> 49.1 us  [the longest x3 16.9 us: project_for(): pl.pallas_call(functools.partial(send_projection_kernel, slot), in_specs=...]
    ppermute x18, waiting for transfers between devices: 22.3 us -> 18.7 us  [swap(): return lax.ppermute(x, axis, pairs)]
  transfers between devices with their start and end apart: 18 -> 18, of which waited for: 7 -> 8; matrix products, arithmetic and copies ran while one was open for 0% -> 0% of each run, Pallas kernels for 29% -> 29%
where the time goes in v4:
time: 128 us
  Pallas kernels  84.8 us (66%)
  starting transfers between devices  22.4 us (18%)
  waiting for transfers between devices  18.7 us (15%)
    pallas_call x1, Pallas kernels, own_frames(): pl.pallas_call(functools.partial(frames_kernel, share, len(coded)), in_sp...  25.8 us
    ppermute x18, starting transfers between devices, swap(): return lax.ppermute(x, axis, pairs)  22.4 us
    ppermute x18, waiting for transfers between devices, swap(): return lax.ppermute(x, axis, pairs)  18.7 us
    pallas_call x3, Pallas kernels, project_for(): pl.pallas_call(functools.partial(send_projection_kernel, slot), in_specs=...  16.9 us
    pallas_call x4, Pallas kernels, project_frames(): pl.pallas_call(functools.partial(projected_kernel, slot), in_specs=[SMEM_...  15.3 us
    pallas_call x1, Pallas kernels, next_v(): pl.pallas_call(functools.partial(next_v_kernel, rows // rank), in_specs=[...  7.9 us
    pallas_call x1, Pallas kernels, project_own(): pl.pallas_call(own_projection_kernel, in_specs=[SMEM_SPEC, VMEM_SPEC, VME...  4.74 us
    pallas_call x1, Pallas kernels, all_v_terms(): pl.pallas_call(v_terms_kernel, in_specs=[SMEM_SPEC, VMEM_SPEC, ANY_SPEC,...  4.32 us
  transfers between devices with their start and end apart: 18, of which 8 were waited for; matrix products, arithmetic and copies ran while one was open for 0% of the time, Pallas kernels for 29%

profile of v4, /device:TPU:0, one launch (start us, length us, event | category | flops | bytes accessed | tf_op | source)
XLA Modules:
  0.0 127.6 jit_solution(17584103642942138181)
XLA Ops:
  1.5 5.6 %project_send.3 = s16[560,256]{1,0:T(8,128)(2,1)S(1)} custom-call(s32[1]{0:T(128)} %bitcast.place, bf16[64,1024]{1,0:T(8,128)(2,1)S(1)} %bitcast.5, bf16[4,8,256,1024]{3,2,1,0:T(8,128)(2,1)} %bitcast.9), custom_call_target="tpu_custom_call" | custom-call | flops 1000 | bytes 1000 | tf_op jit(solution)/shard_map/project_send/pallas_call | solution.py:150
  7.2 5.1 %collective-permute-start = (s16[560,256]{1,0:T(8,128)(2,1)S(1)}, s16[560,256]{1,0:T(8,128)(2,1)S(1)}, u32[]{:S(2)}, u32[]{:S(2)}) collective-permute-start(s16[560,256]{1,0:T(8,128)(2,1)S(1)} %project_send.3), channel_id=1, source_target_pairs={{0,3},{1,2},{2,1},{3,0},{4,7},{5,6},{6,5},{7,4},{8,11},{9,10},{10,... | collective-permute-start | bytes 860168 | tf_op jit(solution)/shard_map/ppermute | solution.py:532
  12.3 5.6 %project_send.4 = s16[560,256]{1,0:T(8,128)(2,1)S(1)} custom-call(s32[1]{0:T(128)} %bitcast.place, bf16[64,1024]{1,0:T(8,128)(2,1)S(1)} %bitcast.6, bf16[4,8,256,1024]{3,2,1,0:T(8,128)(2,1)} %bitcast.10), custom_call_target="tpu_custom_call" | custom-call | flops 1000 | bytes 1000 | tf_op jit(solution)/shard_map/project_send/pallas_call | solution.py:150
  18.0 5.6 %project_send.5 = s16[560,256]{1,0:T(8,128)(2,1)S(1)} custom-call(s32[1]{0:T(128)} %bitcast.place, bf16[64,1024]{1,0:T(8,128)(2,1)S(1)} %bitcast.7, bf16[4,8,256,1024]{3,2,1,0:T(8,128)(2,1)} %bitcast.11), custom_call_target="tpu_custom_call" | custom-call | flops 1000 | bytes 1000 | tf_op jit(solution)/shard_map/project_send/pallas_call | solution.py:150
  24.3 4.7 %project_own.1 = (f32[8,64,256]{2,1,0:T(8,128)S(1)}, f32[64,64]{1,0:T(8,128)S(1)}, f32[64,64]{1,0:T(8,128)S(1)}) custom-call(s32[1]{0:T(128)} %bitcast.place, bf16[64,1024]{1,0:T(8,128)(2,1)S(1)} %bitcast.8, f32[32,64]{1,0:T(8,128)S(1)} %copy-done.1, bf16[4,8,256,1024]{3,2,1,0:T(8,128)(2,1)} %bitcast.12), custom_call_target="tpu_custom_call" | custom-call | flops 1000 | bytes 1000 | tf_op jit(solution)/shard_map/project_own/pallas_call | solution.py:166
  29.1 7.7 %collective-permute-done.1.refs_1_ = s16[560,256]{1,0:T(8,128)(2,1)S(1)} collective-permute-done((s16[560,256]{1,0:T(8,128)(2,1)S(1)}, s16[560,256]{1,0:T(8,128)(2,1)S(1)}, u32[]{:S(2)}, u32[]{:S(2)}) %collective-permute-start.1) | collective-permute-done | bytes 286752 | tf_op jit(solution)/shard_map/ppermute | solution.py:532
  38.2 25.8 %own_frames.1 = (bf16[8,64,256]{2,1,0:T(8,128)(2,1)S(1)}, f32[64,128]{1,0:T(8,128)S(1)}, f32[64,64]{1,0:T(8,128)S(1)}) custom-call(s32[1]{0:T(128)} %bitcast.place, s32[32]{0:T(128)S(1)} %copy-done.4, f32[64,64]{1,0:T(8,128)S(1)} %copy-done.3, f32[32,64]{1,0:T(8,128)S(1)} %copy-done.1, f32[64,64]{1,0:T(8,128)S(1)} %get-tuple-element.30.v_gram_ref, ...), custom_call_target="tpu_custom_call" | custom-call | flops 1000 | bytes 1000 | tf_op jit(solution)/shard_map/own_frames/pallas_call | solution.py:324
  64.1 2.4 %collective-permute-start.11 = (bf16[8,64,256]{2,1,0:T(8,128)(2,1)S(1)}, bf16[8,64,256]{2,1,0:T(8,128)(2,1)S(1)}, u32[]{:S(2)}, u32[]{:S(2)}) collective-permute-start(bf16[8,64,256]{2,1,0:T(8,128)(2,1)S(1)} %get-tuple-element.34.frames_ref), channel_id=1, source_target_pairs={{0,3},{1,2},{2,1},{3,0},{4,7},{5,6},{6,5},{7,4},{8,11},{9,10},{10,... | collective-permute-start | bytes 786440 | tf_op jit(solution)/shard_map/ppermute | solution.py:532
  67.6 1.5 %collective-permute-start.4 = (f32[64,128]{1,0:T(8,128)S(1)}, f32[64,128]{1,0:T(8,128)S(1)}, u32[]{:S(2)}, u32[]{:S(2)}) collective-permute-start(f32[64,128]{1,0:T(8,128)S(1)} %get-tuple-element.33.refs_0_), channel_id=1, source_target_pairs={{0,8},{4,12},{8,0},{12,4},{1,9},{5,13},{9,1},{13,5},{2,10},{6,14},... | collective-permute-start | bytes 98312 | tf_op jit(solution)/shard_map/ppermute | solution.py:532
  70.0 3.7 %project_frames.4 = (bf16[4,512,1024]{2,1,0:T(8,128)(2,1)}, bf16[4,512,1024]{2,1,0:T(8,128)(2,1)}, f32[8,128]{1,0:T(8,128)S(1)}) custom-call(s32[1]{0:T(128)} %bitcast.place, bf16[8,64,256]{2,1,0:T(8,128)(2,1)S(1)} %get-tuple-element.34.frames_ref, bf16[4,8,256,1024]{3,2,1,0:T(8,128)(2,1)} %bitcast.13), custom_call_target="tpu_custom_call" | custom-call | flops 1000 | bytes 1000 | tf_op jit(solution)/shard_map/project_frames/pallas_call | solution.py:361
  74.8 1.9 %collective-permute-start.7 = (f32[64,64]{1,0:T(8,128)S(1)}, f32[64,64]{1,0:T(8,128)S(1)}, u32[]{:S(2)}, u32[]{:S(2)}) collective-permute-start(f32[64,64]{1,0:T(8,128)S(1)} %get-tuple-element.36.refs_0_), channel_id=1, source_target_pairs={{0,2},{1,3},{2,0},{3,1},{4,6},{5,7},{6,4},{7,5},{8,10},{9,11},{10,... | collective-permute-start | bytes 49160 | tf_op jit(solution)/shard_map/ppermute | solution.py:532
  78.2 3.7 %project_frames.5 = (bf16[4,512,1024]{2,1,0:T(8,128)(2,1)}, bf16[4,512,1024]{2,1,0:T(8,128)(2,1)}, f32[8,128]{1,0:T(8,128)S(1)}) custom-call(s32[1]{0:T(128)} %bitcast.place, bf16[8,64,256]{2,1,0:T(8,128)(2,1)S(1)} %collective-permute-done.9.frames_ref, bf16[4,8,256,1024]{3,2,1,0:T(8,128)(2,1)} %bitcast.14, ...), custom_call_target="tpu_custom_call", output_to_operand_aliasing={{0}: (3, {}), {1}: (4, {})} | custom-call | flops 1000 | bytes 1000 | tf_op jit(solution)/shard_map/project_frames/pallas_call | solution.py:361
  81.9 2.6 %first_inverse.1.refs_4_ = f32[64,64]{1,0:T(8,128)S(1)} custom-call(f32[64,64]{1,0:T(8,128)S(1)} %get-tuple-element.37.v_gram_ref, f32[64,64]{1,0:T(8,128)S(1)} %get-tuple-element.38.w_gram_ref, f32[8,128]{1,0:T(8,128)S(1)} %get-tuple-element.41.after_ref), custom_call_target="tpu_custom_call" | custom-call | flops 1000 | bytes 1000 | tf_op jit(solution)/shard_map/first_inverse/pallas_call | solution.py:236
  84.5 4.3 %project_frames.6 = (bf16[4,512,1024]{2,1,0:T(8,128)(2,1)}, bf16[4,512,1024]{2,1,0:T(8,128)(2,1)}, f32[8,128]{1,0:T(8,128)}) custom-call(s32[1]{0:T(128)} %bitcast.place, bf16[8,64,256]{2,1,0:T(8,128)(2,1)S(1)} %collective-permute-done.11.frames_ref, bf16[4,8,256,1024]{3,2,1,0:T(8,128)(2,1)} %bitcast.15, ...), custom_call_target="tpu_custom_call", output_to_operand_aliasing={{0}: (3, {}), {1}: (4, {})} | custom-call | flops 1000 | bytes 1000 | tf_op jit(solution)/shard_map/project_frames/pallas_call | solution.py:361
  90.1 3.7 %project_frames.7 = (bf16[4,512,1024]{2,1,0:T(8,128)(2,1)}, bf16[4,512,1024]{2,1,0:T(8,128)(2,1)}, f32[8,128]{1,0:T(8,128)S(1)}) custom-call(s32[1]{0:T(128)} %bitcast.place, bf16[8,64,256]{2,1,0:T(8,128)(2,1)S(1)} %collective-permute-done.10.frames_ref, bf16[4,8,256,1024]{3,2,1,0:T(8,128)(2,1)} %bitcast.16, ...), custom_call_target="tpu_custom_call", output_to_operand_aliasing={{0}: (3, {}), {1}: (4, {})} | custom-call | flops 1000 | bytes 1000 | tf_op jit(solution)/shard_map/project_frames/pallas_call | solution.py:361
  94.9 4.3 %v_terms.1 = (f32[64,512]{1,0:T(8,128)S(1)}, f32[64,512]{1,0:T(8,128)S(1)}) custom-call(s32[1]{0:T(128)} %bitcast.3.core, bf16[4,192,512]{2,1,0:T(8,128)(2,1)S(1)} %get-tuple-element.48.factor_ref, bf16[4,512,1024]{2,1,0:T(8,128)(2,1)} %get-tuple-element.49.first_ref, bf16[4,512,1024]{2,1,0:T(8,128)(2,1)} %get-tuple-element.50.second_ref), custom_call_target="tpu_custom_call" | custom-call | flops 1000 | bytes 1000 | tf_op jit(solution)/shard_map/v_terms/pallas_call | solution.py:456
  100.7 1.6 %collective-permute-start.13 = (f32[64,512]{1,0:T(8,128)S(1)}, f32[64,512]{1,0:T(8,128)S(1)}, u32[]{:S(2)}, u32[]{:S(2)}) collective-permute-start(f32[64,512]{1,0:T(8,128)S(1)} %add.3.a_ref), channel_id=1, source_target_pairs={{0,8},{4,12},{8,0},{12,4},{1,9},{5,13},{9,1},{13,5},{2,10},{6,14},... | collective-permute-start | bytes 393224 | tf_op jit(solution)/shard_map/ppermute | solution.py:532
  102.3 2.7 %second_inverse.1 = (f32[64,64]{1,0:T(8,128)S(1)}, f32[64,64]{1,0:T(8,128)S(1)}) custom-call(f32[64,64]{1,0:T(8,128)S(1)} %copy-done.2, f32[64,64]{1,0:T(8,128)S(1)} %get-tuple-element.38.w_gram_ref), custom_call_target="tpu_custom_call" | custom-call | flops 1000 | bytes 1000 | tf_op jit(solution)/shard_map/second_inverse/pallas_call | solution.py:423
  107.7 7.9 %next_v.1 = (f32[64,1024]{1,0:T(8,128)}, f32[64,128]{1,0:T(8,128)S(1)}) custom-call(s32[1]{0:T(128)} %bitcast.place, s32[1]{0:T(128)} %bitcast.3.core, f32[64,512]{1,0:T(8,128)S(1)} %add_terms.1.own_ref, f32[64,512]{1,0:T(8,128)S(1)} %collective-permute-done.14.other_ref, f32[64,64]{1,0:T(8,128)S(1)} %get-tuple-element.53.after_ref.inverse_ref, ...), custom_call_target="tpu_custom_call" | custom-call | flops 1000 | bytes 1000 | tf_op jit(solution)/shard_map/next_v/pallas_call | solution.py:496
  117.0 1.5 %collective-permute-start.16 = (f32[64,128]{1,0:T(8,128)S(1)}, f32[64,128]{1,0:T(8,128)S(1)}, u32[]{:S(2)}, u32[]{:S(2)}) collective-permute-start(f32[64,128]{1,0:T(8,128)S(1)} %get-tuple-element.55.refs_0_), channel_id=1, source_target_pairs={{0,2},{1,3},{2,0},{3,1},{4,6},{5,7},{6,4},{7,5},{8,10},{9,11},{10,... | collective-permute-start | bytes 98312 | tf_op jit(solution)/shard_map/ppermute | solution.py:532
  118.6 1.5 %collective-permute-start.17 = (f32[64,128]{1,0:T(8,128)S(1)}, f32[64,128]{1,0:T(8,128)S(1)}, u32[]{:S(2)}, u32[]{:S(2)}) collective-permute-start(f32[64,128]{1,0:T(8,128)S(1)} %get-tuple-element.55.refs_0_), channel_id=1, source_target_pairs={{0,3},{1,2},{2,1},{3,0},{4,7},{5,6},{6,5},{7,4},{8,11},{9,10},{10,... | collective-permute-start | bytes 98312 | tf_op jit(solution)/shard_map/ppermute | solution.py:532
  120.1 2.2 %collective-permute-done.16.refs_2_ = f32[64,128]{1,0:T(8,128)S(1)} collective-permute-done((f32[64,128]{1,0:T(8,128)S(1)}, f32[64,128]{1,0:T(8,128)S(1)}, u32[]{:S(2)}, u32[]{:S(2)}) %collective-permute-start.16) | collective-permute-done | bytes 32800 | tf_op jit(solution)/shard_map/ppermute | solution.py:532
  122.2 2.0 %collective-permute-done.17.refs_3_ = f32[64,128]{1,0:T(8,128)S(1)} collective-permute-done((f32[64,128]{1,0:T(8,128)S(1)}, f32[64,128]{1,0:T(8,128)S(1)}, u32[]{:S(2)}, u32[]{:S(2)}) %collective-permute-start.17) | collective-permute-done | bytes 32800 | tf_op jit(solution)/shard_map/ppermute | solution.py:532
  124.3 3.4 %next_w.1 = f32[32,64]{1,0:T(8,128)} custom-call(f32[64,128]{1,0:T(8,128)S(1)} %get-tuple-element.55.refs_0_, f32[64,128]{1,0:T(8,128)S(1)} %collective-permute-done.15.refs_1_, f32[64,128]{1,0:T(8,128)S(1)} %collective-permute-done.16.refs_2_, f32[64,128]{1,0:T(8,128)S(1)} %collective-permute-done.17.refs_3_, f32[64,64]{1,0:T(8,128)S(1)} %get-tuple-element.56.refs_4_), custom_call_target="tpu_custom_call" | custom-call | flops 1000 | bytes 1000 | tf_op jit(solution)/shard_map/next_w/pallas_call | solution.py:521
  (40 shorter events, 15.7 us)
Async XLA Ops:
  0.6 0.9 copy-start
  7.2 21.9 %collective-permute-start = (s16[560,256]{1,0:T(8,128)(2,1)S(1)}, s16[560,256]{1,0:T(8,128)(2,1)S(1)}, u32[]{:S(2)}, u32[]{:S(2)}) collective-permute-start(s16[560,256]{1,0:T(8,128)(2,1)S(1)} %project_send.3), channel_id=1, source_target_pairs={{0,3},{1,2},{2,1},{3,0},{4,7},{5,6},{6,5},{7,4},{8,11},{9,10},{10,... | collective-permute-start | bytes 860168 | tf_op jit(solution)/shard_map/ppermute | solution.py:532
  17.9 6.4 %copy-start.1 = (f32[32,64]{1,0:T(8,128)S(1)}, f32[32,64]{1,0:T(8,128)}, u32[]{:S(2)}) copy-start(f32[32,64]{1,0:T(8,128)} %refs_5_.1) | copy-start | bytes 24580
  17.9 18.9 %collective-permute-start.1 = (s16[560,256]{1,0:T(8,128)(2,1)S(1)}, s16[560,256]{1,0:T(8,128)(2,1)S(1)}, u32[]{:S(2)}, u32[]{:S(2)}) collective-permute-start(s16[560,256]{1,0:T(8,128)(2,1)S(1)} %project_send.4), channel_id=1, source_target_pairs={{0,2},{1,3},{2,0},{3,1},{4,6},{5,7},{6,4},{7,5},{8,10},{9,11},{10,... | collective-permute-start | bytes 860168 | tf_op jit(solution)/shard_map/ppermute | solution.py:532
  23.6 14.5 %copy-start.3 = (f32[64,64]{1,0:T(8,128)S(1)}, f32[64,64]{1,0:T(8,128)}, u32[]{:S(2)}) copy-start(f32[64,64]{1,0:T(8,128)} %h_ref.1) | copy-start | bytes 49156
  23.7 14.5 %copy-start.4 = (s32[32]{0:T(128)S(1)}, s32[32]{0:T(128)}, u32[]{:S(2)}) copy-start(s32[32]{0:T(128)} %counts_ref.1) | copy-start | bytes 388
  23.7 14.5 %collective-permute-start.2 = (s16[560,256]{1,0:T(8,128)(2,1)S(1)}, s16[560,256]{1,0:T(8,128)(2,1)S(1)}, u32[]{:S(2)}, u32[]{:S(2)}) collective-permute-start(s16[560,256]{1,0:T(8,128)(2,1)S(1)} %project_send.5), channel_id=1, source_target_pairs={{0,1},{1,0},{2,3},{3,2},{4,5},{5,4},{6,7},{7,6},{8,9},{9,8},{10,11... | collective-permute-start | bytes 860168 | tf_op jit(solution)/shard_map/ppermute | solution.py:532
  64.0 12.7 %collective-permute-start.9 = (bf16[8,64,256]{2,1,0:T(8,128)(2,1)S(1)}, bf16[8,64,256]{2,1,0:T(8,128)(2,1)S(1)}, u32[]{:S(2)}, u32[]{:S(2)}) collective-permute-start(bf16[8,64,256]{2,1,0:T(8,128)(2,1)S(1)} %get-tuple-element.34.frames_ref), channel_id=1, source_target_pairs={{0,1},{1,0},{2,3},{3,2},{4,5},{5,4},{6,7},{7,6},{8,9},{9,8},{10,11... | collective-permute-start | bytes 786440 | tf_op jit(solution)/shard_map/ppermute | solution.py:532
  64.1 20.4 %collective-permute-start.11 = (bf16[8,64,256]{2,1,0:T(8,128)(2,1)S(1)}, bf16[8,64,256]{2,1,0:T(8,128)(2,1)S(1)}, u32[]{:S(2)}, u32[]{:S(2)}) collective-permute-start(bf16[8,64,256]{2,1,0:T(8,128)(2,1)S(1)} %get-tuple-element.34.frames_ref), channel_id=1, source_target_pairs={{0,3},{1,2},{2,1},{3,0},{4,7},{5,6},{6,5},{7,4},{8,11},{9,10},{10,... | collective-permute-start | bytes 786440 | tf_op jit(solution)/shard_map/ppermute | solution.py:532
  66.5 23.7 %collective-permute-start.10 = (bf16[8,64,256]{2,1,0:T(8,128)(2,1)S(1)}, bf16[8,64,256]{2,1,0:T(8,128)(2,1)S(1)}, u32[]{:S(2)}, u32[]{:S(2)}) collective-permute-start(bf16[8,64,256]{2,1,0:T(8,128)(2,1)S(1)} %get-tuple-element.34.frames_ref), channel_id=1, source_target_pairs={{0,2},{1,3},{2,0},{3,1},{4,6},{5,7},{6,4},{7,5},{8,10},{9,11},{10,... | collective-permute-start | bytes 786440 | tf_op jit(solution)/shard_map/ppermute | solution.py:532
  67.6 1.5 %collective-permute-start.3 = (f32[64,128]{1,0:T(8,128)S(1)}, f32[64,128]{1,0:T(8,128)S(1)}, u32[]{:S(2)}, u32[]{:S(2)}) collective-permute-start(f32[64,128]{1,0:T(8,128)S(1)} %get-tuple-element.33.refs_0_), channel_id=1, source_target_pairs={{0,4},{4,0},{8,12},{12,8},{1,5},{5,1},{9,13},{13,9},{2,6},{6,2},{1... | collective-permute-start | bytes 98312 | tf_op jit(solution)/shard_map/ppermute | solution.py:532
  67.6 6.1 %collective-permute-start.4 = (f32[64,128]{1,0:T(8,128)S(1)}, f32[64,128]{1,0:T(8,128)S(1)}, u32[]{:S(2)}, u32[]{:S(2)}) collective-permute-start(f32[64,128]{1,0:T(8,128)S(1)} %get-tuple-element.33.refs_0_), channel_id=1, source_target_pairs={{0,8},{4,12},{8,0},{12,4},{1,9},{5,13},{9,1},{13,5},{2,10},{6,14},... | collective-permute-start | bytes 98312 | tf_op jit(solution)/shard_map/ppermute | solution.py:532
  69.1 4.7 %collective-permute-start.5 = (f32[64,128]{1,0:T(8,128)S(1)}, f32[64,128]{1,0:T(8,128)S(1)}, u32[]{:S(2)}, u32[]{:S(2)}) collective-permute-start(f32[64,128]{1,0:T(8,128)S(1)} %get-tuple-element.33.refs_0_), channel_id=1, source_target_pairs={{0,12},{4,8},{8,4},{12,0},{1,13},{5,9},{9,5},{13,1},{2,14},{6,10},... | collective-permute-start | bytes 98312 | tf_op jit(solution)/shard_map/ppermute | solution.py:532
  73.8 20.0 %collective-permute-start.6 = (f32[64,64]{1,0:T(8,128)S(1)}, f32[64,64]{1,0:T(8,128)S(1)}, u32[]{:S(2)}, u32[]{:S(2)}) collective-permute-start(f32[64,64]{1,0:T(8,128)S(1)} %get-tuple-element.36.refs_0_), channel_id=1, source_target_pairs={{0,1},{1,0},{2,3},{3,2},{4,5},{5,4},{6,7},{7,6},{8,9},{9,8},{10,11... | collective-permute-start | bytes 49160 | tf_op jit(solution)/shard_map/ppermute | solution.py:532
  74.8 19.0 %collective-permute-start.7 = (f32[64,64]{1,0:T(8,128)S(1)}, f32[64,64]{1,0:T(8,128)S(1)}, u32[]{:S(2)}, u32[]{:S(2)}) collective-permute-start(f32[64,64]{1,0:T(8,128)S(1)} %get-tuple-element.36.refs_0_), channel_id=1, source_target_pairs={{0,2},{1,3},{2,0},{3,1},{4,6},{5,7},{6,4},{7,5},{8,10},{9,11},{10,... | collective-permute-start | bytes 49160 | tf_op jit(solution)/shard_map/ppermute | solution.py:532
  76.7 17.1 %collective-permute-start.8 = (f32[64,64]{1,0:T(8,128)S(1)}, f32[64,64]{1,0:T(8,128)S(1)}, u32[]{:S(2)}, u32[]{:S(2)}) collective-permute-start(f32[64,64]{1,0:T(8,128)S(1)} %get-tuple-element.36.refs_0_), channel_id=1, source_target_pairs={{0,3},{1,2},{2,1},{3,0},{4,7},{5,6},{6,5},{7,4},{8,11},{9,10},{10,... | collective-permute-start | bytes 49160 | tf_op jit(solution)/shard_map/ppermute | solution.py:532
  94.9 7.3 %copy-start.2 = (f32[64,64]{1,0:T(8,128)S(1)}, f32[64,64]{1,0:T(8,128)}, u32[]{:S(2)}) copy-start(f32[64,64]{1,0:T(8,128)} %get-tuple-element.27.h_ref) | copy-start | bytes 49156
  99.2 1.4 %collective-permute-start.12 = (f32[64,512]{1,0:T(8,128)S(1)}, f32[64,512]{1,0:T(8,128)S(1)}, u32[]{:S(2)}, u32[]{:S(2)}) collective-permute-start(f32[64,512]{1,0:T(8,128)S(1)} %get-tuple-element.52), channel_id=1, source_target_pairs={{0,4},{4,0},{8,12},{12,8},{1,5},{5,1},{9,13},{13,9},{2,6},{6,2},{1... | collective-permute-start | bytes 393224 | tf_op jit(solution)/shard_map/ppermute | solution.py:532
  100.7 5.6 %collective-permute-start.13 = (f32[64,512]{1,0:T(8,128)S(1)}, f32[64,512]{1,0:T(8,128)S(1)}, u32[]{:S(2)}, u32[]{:S(2)}) collective-permute-start(f32[64,512]{1,0:T(8,128)S(1)} %add.3.a_ref), channel_id=1, source_target_pairs={{0,8},{4,12},{8,0},{12,4},{1,9},{5,13},{9,1},{13,5},{2,10},{6,14},... | collective-permute-start | bytes 393224 | tf_op jit(solution)/shard_map/ppermute | solution.py:532
  106.3 1.4 %collective-permute-start.14 = (f32[64,512]{1,0:T(8,128)S(1)}, f32[64,512]{1,0:T(8,128)S(1)}, u32[]{:S(2)}, u32[]{:S(2)}) collective-permute-start(f32[64,512]{1,0:T(8,128)S(1)} %add_terms.1.own_ref), channel_id=1, source_target_pairs={{0,4},{4,0},{8,12},{12,8},{1,5},{5,1},{9,13},{13,9},{2,6},{6,2},{1... | collective-permute-start | bytes 393224 | tf_op jit(solution)/shard_map/ppermute | solution.py:532
  115.6 4.5 %collective-permute-start.15 = (f32[64,128]{1,0:T(8,128)S(1)}, f32[64,128]{1,0:T(8,128)S(1)}, u32[]{:S(2)}, u32[]{:S(2)}) collective-permute-start(f32[64,128]{1,0:T(8,128)S(1)} %get-tuple-element.55.refs_0_), channel_id=1, source_target_pairs={{0,1},{1,0},{2,3},{3,2},{4,5},{5,4},{6,7},{7,6},{8,9},{9,8},{10,11... | collective-permute-start | bytes 98312 | tf_op jit(solution)/shard_map/ppermute | solution.py:532
  117.0 5.2 %collective-permute-start.16 = (f32[64,128]{1,0:T(8,128)S(1)}, f32[64,128]{1,0:T(8,128)S(1)}, u32[]{:S(2)}, u32[]{:S(2)}) collective-permute-start(f32[64,128]{1,0:T(8,128)S(1)} %get-tuple-element.55.refs_0_), channel_id=1, source_target_pairs={{0,2},{1,3},{2,0},{3,1},{4,6},{5,7},{6,4},{7,5},{8,10},{9,11},{10,... | collective-permute-start | bytes 98312 | tf_op jit(solution)/shard_map/ppermute | solution.py:532
  118.6 5.7 %collective-permute-start.17 = (f32[64,128]{1,0:T(8,128)S(1)}, f32[64,128]{1,0:T(8,128)S(1)}, u32[]{:S(2)}, u32[]{:S(2)}) collective-permute-start(f32[64,128]{1,0:T(8,128)S(1)} %get-tuple-element.55.refs_0_), channel_id=1, source_target_pairs={{0,3},{1,2},{2,1},{3,0},{4,7},{5,6},{6,5},{7,4},{8,11},{9,10},{10,... | collective-permute-start | bytes 98312 | tf_op jit(solution)/shard_map/ppermute | solution.py:532

commit v5 on v4

--- a/solution.py
+++ b/solution.py
@@ -51,6 +51,10 @@
 ANY_SPEC = pl.BlockSpec(memory_space=pl.ANY)
 
 
+def whole(shape):
+    return pl.BlockSpec(shape, lambda *place: (0,) * len(shape))
+
+
 def parameters(mib):
     return pltpu.CompilerParams(vmem_limit_bytes=mib * MIB)
 
@@ -61,12 +65,12 @@
 SMEM_SPEC = pl.BlockSpec(memory_space=pltpu.SMEM)
 
 
-def exponent_rows(share):
-    return -(-(share + 1) // 16) * 16
-
-
-def payload_shape(share, rank, slots):
-    return (share * rank + rank // 2 + exponent_rows(share), slots)
+def exponent_rows(count):
+    return -(-(count + 1) // 16) * 16
+
+
+def payload_shape(count, rank, slots, with_gram):
+    return (count * rank + (rank // 2 if with_gram else 0) + exponent_rows(count), slots)
 
 
 def row_exponent(x):
@@ -75,108 +79,99 @@
 
 
 def fetch(source, buffers, sems):
-    copies = [
-        pltpu.make_async_copy(source.at[p], buffers.at[p], sems.at[p]) for p in range(buffers.shape[0])
-    ]
+    copies = [pltpu.make_async_copy(source.at[p], buffers.at[p], sems.at[p]) for p in range(buffers.shape[0])]
     for copy in copies:
         copy.start()
     return copies
 
 
-def project_patient(v_ref, visits):
-    return low_dot(visits, v_ref[...], ROWS_BY_ROWS).T
-
-
-def encode_rest(share, v_ref, coded_ref, exponents):
-    rank = v_ref.shape[0]
-    gram = low_dot(v_ref[...], v_ref[...], ROWS_BY_ROWS)
-    exponent = row_exponent(gram)
-    scaled = gram * (LEVELS / jnp.exp2(exponent))
-    first = jnp.floor(scaled + 0.5)
-    second = jnp.floor((scaled - first) * (2 * LEVELS) + 0.5)
-    digits = jnp.concatenate([first, second], axis=1)
-    digits = jnp.concatenate([digits[: rank // 2], digits[rank // 2 :]], axis=1)
-    coded_ref[pl.ds(share * rank, rank // 2), :] = digits.astype(jnp.int32).astype(jnp.int16)
-    exponents = jnp.where(lane_numbers(exponents.shape) == share, exponent, exponents)
-    rows = exponent_rows(share)
-    last = exponents.T[:rows]
-    last = jnp.concatenate([last, jnp.zeros((rows, coded_ref.shape[1] - rank), F32)], axis=1)
-    coded_ref[pl.ds(share * rank + rank // 2, rows), :] = last.astype(jnp.int32).astype(jnp.int16)
-
-
-def decode(coded_ref, share, rank):
-    def rows(first, count):
-        return coded_ref[pl.ds(first, count), :].astype(jnp.int32).astype(F32)
-
-    exponents = rows(share * rank + rank // 2, exponent_rows(share))[:, :LANES].T
+def decode(coded_ref, count, rank, with_gram):
+    def rows(first, number):
+        return coded_ref[pl.ds(first, number), :].astype(jnp.int32).astype(F32)
+
+    gram_rows = rank // 2 if with_gram else 0
+    exponents = rows(count * rank + gram_rows, exponent_rows(count))[:, :LANES].T
     steps = jnp.exp2(exponents[:rank]) * (1.0 / LEVELS)
-    digits = rows(share * rank, rank // 2)
-    digits = jnp.concatenate([digits[:, : 2 * rank], digits[:, 2 * rank :]], axis=0)
-    gram = (digits[:, :rank] + digits[:, rank:] * (0.5 / LEVELS)) * steps[:, share : share + 1]
-    return [rows(p * rank, rank) * steps[:, p : p + 1] for p in range(share)], gram
-
-
-def send_projection_kernel(slot, place, v_ref, visits_ref, coded_ref, buffers, sems):
-    copies = fetch(visits_ref.at[place[0] ^ slot], buffers, sems)
-    share, rank = len(copies), v_ref.shape[0]
+    gram = None
+    if with_gram:
+        digits = rows(count * rank, gram_rows)
+        digits = jnp.concatenate([digits[:, : 2 * rank], digits[:, 2 * rank :]], axis=0)
+        gram = (digits[:, :rank] + digits[:, rank:] * (0.5 / LEVELS)) * steps[:, count : count + 1]
+    return [rows(p * rank, rank) * steps[:, p : p + 1] for p in range(count)], gram
+
+
+def send_projection_kernel(slot, first, with_gram, place, v_ref, visits_ref, coded_ref, buffers, sems):
+    count, rank = buffers.shape[0], v_ref.shape[0]
+    copies = fetch(visits_ref.at[place[0] ^ slot, pl.ds(first, count)], buffers, sems)
     exponents = jnp.zeros((rank, LANES), F32)
+    lanes = lane_numbers(exponents.shape)
+    end = count * rank
+    if with_gram:
+        gram = low_dot(v_ref[...], v_ref[...], ROWS_BY_ROWS)
+        exponent = row_exponent(gram)
+        scaled = gram * (LEVELS / jnp.exp2(exponent))
+        whole = jnp.floor(scaled + 0.5)
+        rest = jnp.floor((scaled - whole) * (2 * LEVELS) + 0.5)
+        digits = jnp.concatenate([whole, rest], axis=1)
+        digits = jnp.concatenate([digits[: rank // 2], digits[rank // 2 :]], axis=1)
+        coded_ref[pl.ds(end, rank // 2), :] = digits.astype(jnp.int32).astype(jnp.int16)
+        exponents = jnp.where(lanes == count, exponent, exponents)
+        end += rank // 2
     for p, copy in enumerate(copies):
         copy.wait()
-        proj = project_patient(v_ref, buffers[p])
+        proj = low_dot(v_ref[...], buffers[p], ROWS_BY_ROWS)
         exponent = row_exponent(proj)
         coded = jnp.floor(proj * (LEVELS / jnp.exp2(exponent)) + 0.5)
         coded_ref[pl.ds(p * rank, rank), :] = coded.astype(jnp.int32).astype(jnp.int16)
-        exponents = jnp.where(lane_numbers(exponents.shape) == p, exponent, exponents)
-    encode_rest(share, v_ref, coded_ref, exponents)
-
-
-def own_projection_kernel(place, v_ref, w_ref, visits_ref, proj_ref, v_gram_ref, w_gram_ref, buffers, sems):
+        exponents = jnp.where(lanes == p, exponent, exponents)
+    rows = exponent_rows(count)
+    last = jnp.concatenate([exponents.T[:rows], jnp.zeros((rows, coded_ref.shape[1] - rank), F32)], axis=1)
+    coded_ref[pl.ds(end, rows), :] = last.astype(jnp.int32).astype(jnp.int16)
+
+
+def own_projection_kernel(place, v_ref, w_ref, visits_ref, *refs):
+    *proj_refs, v_gram_ref, w_gram_ref, buffers, sems = refs
     copies = fetch(visits_ref.at[place[0]], buffers, sems)
     v_gram_ref[...] = low_dot(v_ref[...], v_ref[...], ROWS_BY_ROWS)
     w_gram_ref[...] = high_dot(w_ref[...], w_ref[...], COLS_BY_COLS)
+    count = len(copies) // len(proj_refs)
     for p, copy in enumerate(copies):
         copy.wait()
-        proj_ref[p] = project_patient(v_ref, buffers[p])
-
-
-def visits_buffers(visits):
-    share = visits.shape[1]
-    return [pltpu.VMEM(visits.shape[1:], BF16), pltpu.SemaphoreType.DMA((share,))]
-
-
-def project_for(slot, place, visits, v_rows):
+        proj_refs[p // count][p % count] = low_dot(v_ref[...], buffers[p], ROWS_BY_ROWS)
+
+
+def project_for(slot, part, n_parts, place, visits, v_rows):
     _, share, slots, width = visits.shape
     rank = v_rows.shape[0]
-    return pl.pallas_call(
-        functools.partial(send_projection_kernel, slot),
+    count = share // n_parts
+    return pl.pallas_call(
+        functools.partial(send_projection_kernel, slot, part * count, part == 0),
         in_specs=[SMEM_SPEC, VMEM_SPEC, ANY_SPEC],
         out_specs=VMEM_SPEC,
-        out_shape=jax.ShapeDtypeStruct(payload_shape(share, rank, slots), jnp.int16),
-        scratch_shapes=visits_buffers(visits),
+        out_shape=jax.ShapeDtypeStruct(payload_shape(count, rank, slots, part == 0), jnp.int16),
+        scratch_shapes=[pltpu.VMEM((count, slots, width), BF16), pltpu.SemaphoreType.DMA((count,))],
         compiler_params=parameters(STREAM),
         cost_estimate=SHORT,
         name="project_send",
     )(place, v_rows, visits)
 
 
-def project_own(place, visits, v_rows, w_start):
+def project_own(n_parts, place, visits, v_rows, w_start):
     _, share, slots, width = visits.shape
     rank = v_rows.shape[0]
-    gram = (rank, rank)
-    return pl.pallas_call(
+    gram = jax.ShapeDtypeStruct((rank, rank), F32)
+    proj = jax.ShapeDtypeStruct((share // n_parts, rank, slots), F32)
+    *own, v_gram, w_gram = pl.pallas_call(
         own_projection_kernel,
         in_specs=[SMEM_SPEC, VMEM_SPEC, VMEM_SPEC, ANY_SPEC],
-        out_specs=[VMEM_SPEC] * 3,
-        out_shape=[
-            jax.ShapeDtypeStruct((share, rank, slots), F32),
-            jax.ShapeDtypeStruct(gram, F32),
-            jax.ShapeDtypeStruct(gram, F32),
-        ],
-        scratch_shapes=visits_buffers(visits),
+        out_specs=[VMEM_SPEC] * (n_parts + 2),
+        out_shape=[proj] * n_parts + [gram] * 2,
+        scratch_shapes=[pltpu.VMEM((share, slots, width), BF16), pltpu.SemaphoreType.DMA((share,))],
         compiler_params=parameters(STREAM),
         cost_estimate=SHORT,
         name="project_own",
     )(place, v_rows, w_start, visits)
+    return own, v_gram, w_gram
 
 
 def pair_inverse(a, b, c, d):
@@ -270,28 +265,28 @@
     first, second = two_parts(frame)
     if fine:
         both = low_dot(jnp.concatenate([first, second], axis=0), first, ROWS_BY_ROWS)
-        gram = both[:rank] + (both[rank:] + both[rank:].T)
+        gram = both[:rank] + both[rank:] + low_dot(first, second, ROWS_BY_ROWS)
         gram_first, gram_second = two_parts(gram)
-        moved = low_dot(
-            jnp.concatenate([gram_first, gram_second, gram_first], axis=1),
-            jnp.concatenate([first, first, second], axis=0),
-        )
+        moved = low_dot(jnp.concatenate([gram_first, gram_second], axis=0), first)
+        moved = moved[:rank] + moved[rank:] + low_dot(gram_first, second)
     else:
         moved = low_dot(low_dot(first, first, ROWS_BY_ROWS).astype(BF16), first)
     frames[p] = 1.5 * frame - 0.5 * moved
 
 
-def frames_kernel(share, n_coded, place, counts_ref, h_ref, w_ref, v_gram_ref, w_gram_ref, own_ref, *refs):
-    coded = refs[:n_coded]
-    frames_ref, terms_ref, v_total_ref, proj, frames = refs[n_coded:]
-    first = place[0] * share
-    rank, slots = frames.shape[1:]
-    pieces = [own_ref[p] for p in range(share)]
+def frames_kernel(part, share, n_coded, place, counts_ref, h_ref, w_ref, v_gram_ref, w_gram_ref, own_ref, *refs):
+    coded, earlier = refs[:n_coded], refs[n_coded:-5]
+    frames_ref, terms_ref, v_total_ref, proj, frames = refs[-5:]
+    count, rank, slots = frames.shape
+    done = part * count
+    first = place[0] * share + done
+    pieces = [own_ref[p] for p in range(count)]
     v_gram = v_gram_ref[...]
     for code in coded:
-        arrived, gram = decode(code, share, rank)
+        arrived, gram = decode(code, count, rank, part == 0)
         pieces = [a + b for a, b in zip(pieces, arrived)]
-        v_gram = v_gram + gram
+        if gram is not None:
+            v_gram = v_gram + gram
     v_total_ref[...] = v_gram
     for p, piece in enumerate(pieces):
         proj[p] = piece
@@ -301,32 +296,36 @@
         frames[p] = mixed * lax.rsqrt(energy + epsilon)
 
     def sweep(fine, step, carry):
-        for p in range(share):
+        for p in range(count):
             sweep_once(frames, p, rank, fine)
         return carry
 
     lax.fori_loop(0, COARSE_STEPS, functools.partial(sweep, False), 0)
     lax.fori_loop(COARSE_STEPS, NS_STEPS, functools.partial(sweep, True), 0)
-    terms = jnp.zeros((rank, rank), F32)
-    for p in range(share):
+    terms = w_gram_ref[...]
+    if earlier:
+        frames_ref[:done] = earlier[0][...]
+        terms = earlier[1][...]
+    terms, w_gram = (terms[:, :rank], terms[:, rank:]) if earlier else (jnp.zeros_like(terms), terms)
+    for p in range(count):
         low = frames[p].astype(BF16)
-        frames_ref[p] = low
+        frames_ref[done + p] = low
         parts = three_parts(proj[p])
         product = low_dot(low, parts[0], ROWS_BY_ROWS)
-        for part in parts[1:]:
-            product = product + low_dot(low, part, ROWS_BY_ROWS)
+        for piece in parts[1:]:
+            product = product + low_dot(low, piece, ROWS_BY_ROWS)
         terms = terms + product * w_ref[pl.ds(first + p, 1), :]
-    terms_ref[...] = jnp.concatenate([terms, w_gram_ref[...]], axis=1)
-
-
-def own_frames(place, counts, h_start, w_start, v_gram, w_gram, own, coded):
-    share, rank, slots = own.shape
-    return pl.pallas_call(
-        functools.partial(frames_kernel, share, len(coded)),
-        in_specs=[SMEM_SPEC] * 2 + [VMEM_SPEC] * (5 + len(coded)),
+    terms_ref[...] = jnp.concatenate([terms, w_gram], axis=1)
+
+
+def own_frames(part, n_parts, place, counts, h_start, w_start, v_gram, w_gram, own, coded, earlier):
+    count, rank, slots = own.shape
+    return pl.pallas_call(
+        functools.partial(frames_kernel, part, count * n_parts, len(coded)),
+        in_specs=[SMEM_SPEC] * 2 + [VMEM_SPEC] * (5 + len(coded) + len(earlier)),
         out_specs=[VMEM_SPEC] * 3,
         out_shape=[
-            jax.ShapeDtypeStruct(own.shape, BF16),
+            jax.ShapeDtypeStruct(((part + 1) * count, rank, slots), BF16),
             jax.ShapeDtypeStruct((rank, 2 * rank), F32),
             jax.ShapeDtypeStruct((rank, rank), F32),
         ],
@@ -334,7 +333,7 @@
         compiler_params=parameters(SMALL),
         cost_estimate=SHORT,
         name="own_frames",
-    )(place, counts, h_start, w_start, v_gram, w_gram, own, *coded)
+    )(place, counts, h_start, w_start, v_gram, w_gram, own, *coded, *earlier)
 
 
 def projected_kernel(slot, place, frames_ref, visits_ref, *refs):
@@ -465,29 +464,34 @@
     )(core, factor, first, second)
 
 
-def next_v_kernel(share, place, core, own_ref, other_ref, inverse_ref, h_ref, first_ref, second_ref, v_ref, sums_ref, *refs):
-    v_parts, first, second, sems = refs
-    firsts = fetch(first_ref, first, sems.at[0])
-    seconds = fetch(second_ref, second, sems.at[1])
+def next_v_kernel(share, place, core, own_ref, other_ref, *refs):
+    inverse_ref, h_ref, first_ref, second_ref, v_ref, copies_ref, v_parts, weights, sums_ref = refs
+    slot = pl.program_id(0)
     rank = inverse_ref.shape[0]
-    upper = core[0] == 1
-    left = jnp.where(upper, other_ref[...], own_ref[...])
-    right = jnp.where(upper, own_ref[...], other_ref[...])
-    v_rows = high_dot(inverse_ref[...], jnp.concatenate([left, right], axis=1))
-    v_ref[...] = v_rows
-    v_parts[...] = jnp.concatenate(two_parts(v_rows), axis=0)
-    weights = jnp.concatenate([h_ref[...]] * 2, axis=1)
-    gram = low_dot(v_parts[...], v_parts[...], ROWS_BY_ROWS)
-    gram = gram[:rank, :rank] + (gram[:rank, rank:] + gram[rank:, :rank])
-    sums_ref[...] = jnp.concatenate([jnp.zeros((rank, rank), F32), gram], axis=1)
-    for slot, copies in enumerate(zip(firsts, seconds)):
-        for copy in copies:
-            copy.wait()
-        seen = low_dot(first[slot], v_parts[...], ROWS_BY_ROWS) + low_dot(second[slot], v_parts[...], ROWS_BY_ROWS)
-        start = (place[0] ^ slot) * share
-        for p in range(share):
-            row = jnp.sum(seen[p * rank : (p + 1) * rank] * weights, axis=0, keepdims=True)
-            sums_ref[pl.ds(start + p, 1), :rank] = row[:, :rank] + row[:, rank:]
+
+    @pl.when(slot == 0)
+    def _():
+        upper = core[0] == 1
+        left = jnp.where(upper, other_ref[...], own_ref[...])
+        right = jnp.where(upper, own_ref[...], other_ref[...])
+        v_rows = high_dot(inverse_ref[...], jnp.concatenate([left, right], axis=1))
+        v_ref[...] = v_rows
+        v_parts[...] = jnp.concatenate(two_parts(v_rows), axis=0)
+        weights[...] = jnp.concatenate([h_ref[...]] * 2, axis=1)
+        gram = low_dot(v_parts[...], v_parts[...], ROWS_BY_ROWS)
+        gram = gram[:rank, :rank] + (gram[:rank, rank:] + gram[rank:, :rank])
+        sums_ref[...] = jnp.concatenate([jnp.zeros((rank, rank), F32), gram], axis=1)
+
+    seen = low_dot(first_ref[0], v_parts[...], ROWS_BY_ROWS) + low_dot(second_ref[0], v_parts[...], ROWS_BY_ROWS)
+    first = (place[0] ^ slot) * share
+    for p in range(share):
+        row = jnp.sum(seen[p * rank : (p + 1) * rank] * weights[...], axis=0, keepdims=True)
+        sums_ref[pl.ds(first + p, 1), :rank] = row[:, :rank] + row[:, rank:]
+
+    @pl.when(slot == pl.num_programs(0) - 1)
+    def _():
+        for device in range(copies_ref.shape[0]):
+            copies_ref[device] = sums_ref[...]
 
 
 def next_v(place, core, own, other, inverse, h_next, first, second):
@@ -495,23 +499,30 @@
     rank = inverse.shape[0]
     return pl.pallas_call(
         functools.partial(next_v_kernel, rows // rank),
-        in_specs=[SMEM_SPEC] * 2 + [VMEM_SPEC] * 4 + [ANY_SPEC] * 2,
-        out_specs=[VMEM_SPEC] * 2,
+        grid_spec=pltpu.PrefetchScalarGridSpec(
+            num_scalar_prefetch=2,
+            grid=(n_slots,),
+            in_specs=[whole(own.shape)] * 2
+            + [whole((rank, rank))] * 2
+            + [pl.BlockSpec((1, rows, width), lambda i, place, core: (i, 0, 0))] * 2,
+            out_specs=[whole((rank, width)), whole((n_slots, rank, 2 * rank))],
+            scratch_shapes=[pltpu.VMEM((2 * rank, width), BF16)] + [pltpu.VMEM((rank, 2 * rank), F32)] * 2,
+        ),
         out_shape=[
             jax.ShapeDtypeStruct((rank, width), F32),
-            jax.ShapeDtypeStruct((rank, 2 * rank), F32),
+            jax.ShapeDtypeStruct((n_slots, rank, 2 * rank), F32),
         ],
-        scratch_shapes=[pltpu.VMEM((2 * rank, width), BF16)] + projected_buffers(first),
         compiler_params=parameters(STREAM),
         cost_estimate=SHORT,
         name="next_v",
     )(place, core, own, other, inverse, h_next, first, second)
 
 
-def next_w_kernel(n_sums, *refs):
-    gram_ref, w_ref = refs[n_sums:]
+def next_w_kernel(sums_ref, gram_ref, w_ref):
     patients, rank = w_ref.shape
-    sums = total(refs[:n_sums])
+    sums = sums_ref[0]
+    for device in range(1, sums_ref.shape[0]):
+        sums = sums + sums_ref[device]
     table = jnp.concatenate([sums[:, rank:] * gram_ref[...], sums.T[:rank]], axis=1)
     w_ref[...] = eliminate(table, rank).T[rank : rank + patients]
 
@@ -519,12 +530,14 @@
 def next_w(sums, h_gram, patients):
     rank = h_gram.shape[0]
     return pl.pallas_call(
-        functools.partial(next_w_kernel, len(sums)),
+        next_w_kernel,
+        in_specs=[VMEM_SPEC] * 2,
+        out_specs=VMEM_SPEC,
         out_shape=jax.ShapeDtypeStruct((patients, rank), F32),
         compiler_params=parameters(SMALL),
         cost_estimate=SHORT,
         name="next_w",
-    )(*sums, h_gram)
+    )(sums, h_gram)
 
 
 def swap(x, axis, slot):
@@ -573,10 +586,18 @@
     by_owner = visits.reshape(n, share, slots, width)
     v_rows = v_start.T
 
-    coded = [swap(project_for(slot, place, by_owner, v_rows), "feature", slot) for slot in range(n - 1, 0, -1)]
-    own, v_local, w_local = project_own(place, by_owner, v_rows, w_start)
-
-    frames, h_local, v_gram = own_frames(place, visit_counts, h_start, w_start, v_local, w_local, own, coded)
+    n_parts = 2 if share % 2 == 0 else 1
+    coded = [
+        [swap(project_for(slot, part, n_parts, place, by_owner, v_rows), "feature", slot) for slot in range(n - 1, 0, -1)]
+        for part in range(n_parts)
+    ]
+    own, v_gram, w_local = project_own(n_parts, place, by_owner, v_rows, w_start)
+    earlier = []
+    for part in range(n_parts):
+        frames, h_local, v_gram = own_frames(
+            part, n_parts, place, visit_counts, h_start, w_start, v_gram, w_local, own[part], coded[part], earlier
+        )
+        earlier = [frames, h_local]
     far = list(range(n - 1, 1, -1))
     all_frames = {0: frames} | {slot: swap(frames, "feature", slot) for slot in far + [1]}
     h_sums = all_terms(h_local, "patient")
@@ -594,7 +615,7 @@
     h_gram, second = second_inverse(h_next, w_gram)
     own_terms, other_terms = patient_halves(keep, send, second)
     v_next, sums = next_v(place, core, own_terms, other_terms, second, h_next, *projected)
-    w_next = next_w(all_terms(sums, "feature"), h_gram, patients)
+    w_next = next_w(lax.all_to_all(sums, "feature", 0, 0), h_gram, patients)
     return (h_next, v_next.T, w_next)
 
 

time: 128 us -> 119 us (0.930)
  waiting for transfers between devices: 18.7 us -> 6.65 us
  blocking collectives: 0 us -> 9.92 us
  Pallas kernels: 84.8 us -> 77.1 us
    ppermute x18, waiting for transfers between devices: 18.7 us -> 6.65 us  [swap(): return lax.ppermute(x, axis, pairs)]
    all_to_all x0 -> x1, blocking collectives: none -> 9.92 us  [on_device(): w_next = next_w(lax.all_to_all(sums, 'feature', 0, 0), h_gram, patients)]
    pallas_call x6 -> x10, Pallas kernels: 54 us -> 46.7 us  [the longest x6 19 us: project_for(): pl.pallas_call(functools.partial(send_projection_kernel, slot, part * cou...]
  transfers between devices with their start and end apart: 18 -> 18, of which waited for: 8 -> 4; matrix products, arithmetic and copies ran while one was open for 0% -> 0% of each run, Pallas kernels for 29% -> 42%
where the time goes in v5:
time: 119 us; the launch traced here: 118 us
  Pallas kernels  77.1 us (65%)
  starting transfers between devices  22.8 us (19%)
  blocking collectives  9.92 us (8%)
  waiting for transfers between devices  6.65 us (6%)
    ppermute x18, starting transfers between devices, swap(): return lax.ppermute(x, axis, pairs)  22.8 us
    pallas_call x6, Pallas kernels, project_for(): pl.pallas_call(functools.partial(send_projection_kernel, slot, part * cou...  19 us
    pallas_call x2, Pallas kernels, own_frames(): pl.pallas_call(functools.partial(frames_kernel, part, count * n_parts, le...  17.2 us
    pallas_call x4, Pallas kernels, project_frames(): pl.pallas_call(functools.partial(projected_kernel, slot), in_specs=[SMEM_...  15.3 us
    all_to_all x1, blocking collectives, on_device(): w_next = next_w(lax.all_to_all(sums, 'feature', 0, 0), h_gram, patients)  9.92 us
    pallas_call x1, Pallas kernels, next_v(): pl.pallas_call(functools.partial(next_v_kernel, rows // rank), grid_spec=...  7.09 us
    ppermute x18, waiting for transfers between devices, swap(): return lax.ppermute(x, axis, pairs)  6.65 us
    pallas_call x1, Pallas kernels, project_own(): pl.pallas_call(own_projection_kernel, in_specs=[SMEM_SPEC, VMEM_SPEC, VME...  4.35 us
  transfers between devices with their start and end apart: 18, of which 4 were waited for; matrix products, arithmetic and copies ran while one was open for 0% of the time, Pallas kernels for 42%

profile of v5, /device:TPU:0, one launch (start us, length us, event | category | flops | bytes accessed | tf_op | source)
XLA Modules:
  0.0 118.4 jit_solution(12027342513038510187)
XLA Ops:
  1.5 3.2 %project_send.6 = s16[304,256]{1,0:T(8,128)(2,1)S(1)} custom-call(s32[1]{0:T(128)} %bitcast.place, bf16[64,1024]{1,0:T(8,128)(2,1)S(1)} %bitcast.5, bf16[4,8,256,1024]{3,2,1,0:T(8,128)(2,1)} %bitcast.12), custom_call_target="tpu_custom_call" | custom-call | flops 1000 | bytes 1000 | tf_op jit(solution)/shard_map/project_send/pallas_call | solution.py:147
  4.7 5.1 %collective-permute-start = (s16[304,256]{1,0:T(8,128)(2,1)S(1)}, s16[304,256]{1,0:T(8,128)(2,1)S(1)}, u32[]{:S(2)}, u32[]{:S(2)}) collective-permute-start(s16[304,256]{1,0:T(8,128)(2,1)S(1)} %project_send.6), channel_id=1, source_target_pairs={{0,3},{1,2},{2,1},{3,0},{4,7},{5,6},{6,5},{7,4},{8,11},{9,10},{10,... | collective-permute-start | bytes 466952 | tf_op jit(solution)/shard_map/ppermute | solution.py:545
  9.8 3.2 %project_send.7 = s16[304,256]{1,0:T(8,128)(2,1)S(1)} custom-call(s32[1]{0:T(128)} %bitcast.place, bf16[64,1024]{1,0:T(8,128)(2,1)S(1)} %bitcast.6, bf16[4,8,256,1024]{3,2,1,0:T(8,128)(2,1)} %bitcast.13), custom_call_target="tpu_custom_call" | custom-call | flops 1000 | bytes 1000 | tf_op jit(solution)/shard_map/project_send/pallas_call | solution.py:147
  13.1 3.2 %project_send.8 = s16[304,256]{1,0:T(8,128)(2,1)S(1)} custom-call(s32[1]{0:T(128)} %bitcast.place, bf16[64,1024]{1,0:T(8,128)(2,1)S(1)} %bitcast.7, bf16[4,8,256,1024]{3,2,1,0:T(8,128)(2,1)} %bitcast.14), custom_call_target="tpu_custom_call" | custom-call | flops 1000 | bytes 1000 | tf_op jit(solution)/shard_map/project_send/pallas_call | solution.py:147
  16.9 3.2 %project_send.9 = s16[272,256]{1,0:T(8,128)(2,1)S(1)} custom-call(s32[1]{0:T(128)} %bitcast.place, bf16[64,1024]{1,0:T(8,128)(2,1)S(1)} %bitcast.8, bf16[4,8,256,1024]{3,2,1,0:T(8,128)(2,1)} %bitcast.15), custom_call_target="tpu_custom_call" | custom-call | flops 1000 | bytes 1000 | tf_op jit(solution)/shard_map/project_send/pallas_call | solution.py:147
  20.1 3.9 %collective-permute-start.3 = (s16[272,256]{1,0:T(8,128)(2,1)S(1)}, s16[272,256]{1,0:T(8,128)(2,1)S(1)}, u32[]{:S(2)}, u32[]{:S(2)}) collective-permute-start(s16[272,256]{1,0:T(8,128)(2,1)S(1)} %project_send.9), channel_id=1, source_target_pairs={{0,3},{1,2},{2,1},{3,0},{4,7},{5,6},{6,5},{7,4},{8,11},{9,10},{10,... | collective-permute-start | bytes 417800 | tf_op jit(solution)/shard_map/ppermute | solution.py:545
  23.9 3.2 %project_send.10 = s16[272,256]{1,0:T(8,128)(2,1)S(1)} custom-call(s32[1]{0:T(128)} %bitcast.place, bf16[64,1024]{1,0:T(8,128)(2,1)S(1)} %bitcast.9, bf16[4,8,256,1024]{3,2,1,0:T(8,128)(2,1)} %bitcast.16), custom_call_target="tpu_custom_call" | custom-call | flops 1000 | bytes 1000 | tf_op jit(solution)/shard_map/project_send/pallas_call | solution.py:147
  27.2 3.2 %project_send.11 = s16[272,256]{1,0:T(8,128)(2,1)S(1)} custom-call(s32[1]{0:T(128)} %bitcast.place, bf16[64,1024]{1,0:T(8,128)(2,1)S(1)} %bitcast.10, bf16[4,8,256,1024]{3,2,1,0:T(8,128)(2,1)} %bitcast.17), custom_call_target="tpu_custom_call" | custom-call | flops 1000 | bytes 1000 | tf_op jit(solution)/shard_map/project_send/pallas_call | solution.py:147
  31.1 4.3 %project_own.1 = (f32[4,64,256]{2,1,0:T(8,128)S(1)}, f32[4,64,256]{2,1,0:T(8,128)S(1)}, f32[64,64]{1,0:T(8,128)S(1)}, f32[64,64]{1,0:T(8,128)S(1)}) custom-call(s32[1]{0:T(128)} %bitcast.place, bf16[64,1024]{1,0:T(8,128)(2,1)S(1)} %bitcast.11, f32[32,64]{1,0:T(8,128)S(1)} %copy-done.1, bf16[4,8,256,1024]{3,2,1,0:T(8,128)(2,1)} %bitcast.18), custom_call_target="tpu_custom_call" | custom-call | flops 1000 | bytes 1000 | tf_op jit(solution)/shard_map/project_own/pallas_call | solution.py:164
  35.5 8.7 %own_frames.2 = (bf16[4,64,256]{2,1,0:T(8,128)(2,1)S(1)}, f32[64,128]{1,0:T(8,128)S(1)}, f32[64,64]{1,0:T(8,128)S(1)}) custom-call(s32[1]{0:T(128)} %bitcast.place, s32[32]{0:T(128)S(1)} %copy-done.4, f32[64,64]{1,0:T(8,128)S(1)} %copy-done.3, f32[32,64]{1,0:T(8,128)S(1)} %copy-done.1, f32[64,64]{1,0:T(8,128)S(1)} %get-tuple-element.34.v_gram_ref, ...), custom_call_target="tpu_custom_call" | custom-call | flops 1000 | bytes 1000 | tf_op jit(solution)/shard_map/own_frames/pallas_call | solution.py:323
  44.2 8.5 %own_frames.3 = (bf16[8,64,256]{2,1,0:T(8,128)(2,1)S(1)}, f32[64,128]{1,0:T(8,128)S(1)}, f32[64,64]{1,0:T(8,128)S(1)}) custom-call(s32[1]{0:T(128)} %bitcast.place, s32[32]{0:T(128)S(1)} %copy-done.4, f32[64,64]{1,0:T(8,128)S(1)} %copy-done.3, f32[32,64]{1,0:T(8,128)S(1)} %copy-done.1, f32[64,64]{1,0:T(8,128)S(1)} %get-tuple-element.37.v_gram_ref, ...), custom_call_target="tpu_custom_call" | custom-call | flops 1000 | bytes 1000 | tf_op jit(solution)/shard_map/own_frames/pallas_call | solution.py:323
  54.2 2.4 %collective-permute-start.14 = (bf16[8,64,256]{2,1,0:T(8,128)(2,1)S(1)}, bf16[8,64,256]{2,1,0:T(8,128)(2,1)S(1)}, u32[]{:S(2)}, u32[]{:S(2)}) collective-permute-start(bf16[8,64,256]{2,1,0:T(8,128)(2,1)S(1)} %get-tuple-element.42.frames_ref), channel_id=1, source_target_pairs={{0,3},{1,2},{2,1},{3,0},{4,7},{5,6},{6,5},{7,4},{8,11},{9,10},{10,... | collective-permute-start | bytes 786440 | tf_op jit(solution)/shard_map/ppermute | solution.py:545
  59.6 3.7 %project_frames.4 = (bf16[4,512,1024]{2,1,0:T(8,128)(2,1)}, bf16[4,512,1024]{2,1,0:T(8,128)(2,1)}, f32[8,128]{1,0:T(8,128)S(1)}) custom-call(s32[1]{0:T(128)} %bitcast.place, bf16[8,64,256]{2,1,0:T(8,128)(2,1)S(1)} %get-tuple-element.42.frames_ref, bf16[4,8,256,1024]{3,2,1,0:T(8,128)(2,1)} %bitcast.19), custom_call_target="tpu_custom_call" | custom-call | flops 1000 | bytes 1000 | tf_op jit(solution)/shard_map/project_frames/pallas_call | solution.py:360
  63.4 2.4 %collective-permute-start.10 = (f32[64,64]{1,0:T(8,128)S(1)}, f32[64,64]{1,0:T(8,128)S(1)}, u32[]{:S(2)}, u32[]{:S(2)}) collective-permute-start(f32[64,64]{1,0:T(8,128)S(1)} %get-tuple-element.44.refs_0_), channel_id=1, source_target_pairs={{0,2},{1,3},{2,0},{3,1},{4,6},{5,7},{6,4},{7,5},{8,10},{9,11},{10,... | collective-permute-start | bytes 49160 | tf_op jit(solution)/shard_map/ppermute | solution.py:545
  67.2 3.7 %project_frames.5 = (bf16[4,512,1024]{2,1,0:T(8,128)(2,1)}, bf16[4,512,1024]{2,1,0:T(8,128)(2,1)}, f32[8,128]{1,0:T(8,128)S(1)}) custom-call(s32[1]{0:T(128)} %bitcast.place, bf16[8,64,256]{2,1,0:T(8,128)(2,1)S(1)} %collective-permute-done.12.frames_ref, bf16[4,8,256,1024]{3,2,1,0:T(8,128)(2,1)} %bitcast.20, ...), custom_call_target="tpu_custom_call", output_to_operand_aliasing={{0}: (3, {}), {1}: (4, {})} | custom-call | flops 1000 | bytes 1000 | tf_op jit(solution)/shard_map/project_frames/pallas_call | solution.py:360
  70.9 2.6 %first_inverse.1.refs_4_ = f32[64,64]{1,0:T(8,128)S(1)} custom-call(f32[64,64]{1,0:T(8,128)S(1)} %get-tuple-element.45.v_gram_ref, f32[64,64]{1,0:T(8,128)S(1)} %get-tuple-element.46.w_gram_ref, f32[8,128]{1,0:T(8,128)S(1)} %get-tuple-element.49.after_ref), custom_call_target="tpu_custom_call" | custom-call | flops 1000 | bytes 1000 | tf_op jit(solution)/shard_map/first_inverse/pallas_call | solution.py:231
  73.5 4.3 %project_frames.6 = (bf16[4,512,1024]{2,1,0:T(8,128)(2,1)}, bf16[4,512,1024]{2,1,0:T(8,128)(2,1)}, f32[8,128]{1,0:T(8,128)}) custom-call(s32[1]{0:T(128)} %bitcast.place, bf16[8,64,256]{2,1,0:T(8,128)(2,1)S(1)} %collective-permute-done.14.frames_ref, bf16[4,8,256,1024]{3,2,1,0:T(8,128)(2,1)} %bitcast.21, ...), custom_call_target="tpu_custom_call", output_to_operand_aliasing={{0}: (3, {}), {1}: (4, {})} | custom-call | flops 1000 | bytes 1000 | tf_op jit(solution)/shard_map/project_frames/pallas_call | solution.py:360
  77.8 2.6 %collective-permute-done.13.frames_ref = bf16[8,64,256]{2,1,0:T(8,128)(2,1)S(1)} collective-permute-done((bf16[8,64,256]{2,1,0:T(8,128)(2,1)S(1)}, bf16[8,64,256]{2,1,0:T(8,128)(2,1)S(1)}, u32[]{:S(2)}, u32[]{:S(2)}) %collective-permute-start.13) | collective-permute-done | bytes 262176 | tf_op jit(solution)/shard_map/ppermute | solution.py:545
  80.4 3.7 %project_frames.7 = (bf16[4,512,1024]{2,1,0:T(8,128)(2,1)}, bf16[4,512,1024]{2,1,0:T(8,128)(2,1)}, f32[8,128]{1,0:T(8,128)S(1)}) custom-call(s32[1]{0:T(128)} %bitcast.place, bf16[8,64,256]{2,1,0:T(8,128)(2,1)S(1)} %collective-permute-done.13.frames_ref, bf16[4,8,256,1024]{3,2,1,0:T(8,128)(2,1)} %bitcast.22, ...), custom_call_target="tpu_custom_call", output_to_operand_aliasing={{0}: (3, {}), {1}: (4, {})} | custom-call | flops 1000 | bytes 1000 | tf_op jit(solution)/shard_map/project_frames/pallas_call | solution.py:360
  85.2 4.3 %v_terms.1 = (f32[64,512]{1,0:T(8,128)S(1)}, f32[64,512]{1,0:T(8,128)S(1)}) custom-call(s32[1]{0:T(128)} %bitcast.3.core, bf16[4,192,512]{2,1,0:T(8,128)(2,1)S(1)} %get-tuple-element.56.factor_ref, bf16[4,512,1024]{2,1,0:T(8,128)(2,1)} %get-tuple-element.57.first_ref.refs_2_, bf16[4,512,1024]{2,1,0:T(8,128)(2,1)} %get-tuple-element.58.second_ref.refs_3_), custom_call_target="tpu_custom_call" | custom-call | flops 1000 | bytes 1000 | tf_op jit(solution)/shard_map/v_terms/pallas_call | solution.py:455
  92.5 2.7 %second_inverse.1 = (f32[64,64]{1,0:T(8,128)S(1)}, f32[64,64]{1,0:T(8,128)S(1)}) custom-call(f32[64,64]{1,0:T(8,128)S(1)} %copy-done.2, f32[64,64]{1,0:T(8,128)S(1)} %get-tuple-element.46.w_gram_ref), custom_call_target="tpu_custom_call" | custom-call | flops 1000 | bytes 1000 | tf_op jit(solution)/shard_map/second_inverse/pallas_call | solution.py:422
  98.0 7.1 %next_v.1 = (f32[64,1024]{1,0:T(8,128)}, f32[4,64,128]{2,1,0:T(8,128)S(1)}) custom-call(s32[1]{0:T(128)} %bitcast.place, s32[1]{0:T(128)} %bitcast.3.core, f32[64,512]{1,0:T(8,128)S(1)} %add_terms.1.own_ref, f32[64,512]{1,0:T(8,128)S(1)} %collective-permute-done.17.other_ref, f32[64,64]{1,0:T(8,128)S(1)} %get-tuple-element.61.after_ref.refs_0_, ...), custom_call_target="tpu_custom_call" | custom-call | flops 1000 | bytes 1000 | tf_op jit(solution)/shard_map/next_v/pallas_call | solution.py:500
  105.1 9.9 %all_to_all.5.sums_ref = f32[4,64,128]{2,1,0:T(8,128)S(1)} all-to-all(f32[4,64,128]{2,1,0:T(8,128)S(1)} %get-tuple-element.63), channel_id=1, replica_groups=mesh['groups'=2,'patient'=4,'feature'=4] {'feature'}, dimensions={0} | all-to-all | bytes 262144 | tf_op jit(solution)/shard_map/all_to_all | solution.py:618
  115.0 3.4 %next_w.1 = f32[32,64]{1,0:T(8,128)} custom-call(f32[4,64,128]{2,1,0:T(8,128)S(1)} %all_to_all.5.sums_ref, f32[64,64]{1,0:T(8,128)S(1)} %get-tuple-element.64.gram_ref), custom_call_target="tpu_custom_call" | custom-call | flops 1000 | bytes 1000 | tf_op jit(solution)/shard_map/next_w/pallas_call | solution.py:532
  (45 shorter events, 15.1 us)
Async XLA Ops:
  0.6 0.9 copy-start
  4.7 25.7 %collective-permute-start = (s16[304,256]{1,0:T(8,128)(2,1)S(1)}, s16[304,256]{1,0:T(8,128)(2,1)S(1)}, u32[]{:S(2)}, u32[]{:S(2)}) collective-permute-start(s16[304,256]{1,0:T(8,128)(2,1)S(1)} %project_send.6), channel_id=1, source_target_pairs={{0,3},{1,2},{2,1},{3,0},{4,7},{5,6},{6,5},{7,4},{8,11},{9,10},{10,... | collective-permute-start | bytes 466952 | tf_op jit(solution)/shard_map/ppermute | solution.py:545
  13.0 22.4 %collective-permute-start.1 = (s16[304,256]{1,0:T(8,128)(2,1)S(1)}, s16[304,256]{1,0:T(8,128)(2,1)S(1)}, u32[]{:S(2)}, u32[]{:S(2)}) collective-permute-start(s16[304,256]{1,0:T(8,128)(2,1)S(1)} %project_send.7), channel_id=1, source_target_pairs={{0,2},{1,3},{2,0},{3,1},{4,6},{5,7},{6,4},{7,5},{8,10},{9,11},{10,... | collective-permute-start | bytes 466952 | tf_op jit(solution)/shard_map/ppermute | solution.py:545
  16.3 19.2 %collective-permute-start.2 = (s16[304,256]{1,0:T(8,128)(2,1)S(1)}, s16[304,256]{1,0:T(8,128)(2,1)S(1)}, u32[]{:S(2)}, u32[]{:S(2)}) collective-permute-start(s16[304,256]{1,0:T(8,128)(2,1)S(1)} %project_send.8), channel_id=1, source_target_pairs={{0,1},{1,0},{2,3},{3,2},{4,5},{5,4},{6,7},{7,6},{8,9},{9,8},{10,11... | collective-permute-start | bytes 466952 | tf_op jit(solution)/shard_map/ppermute | solution.py:545
  20.1 24.1 %collective-permute-start.3 = (s16[272,256]{1,0:T(8,128)(2,1)S(1)}, s16[272,256]{1,0:T(8,128)(2,1)S(1)}, u32[]{:S(2)}, u32[]{:S(2)}) collective-permute-start(s16[272,256]{1,0:T(8,128)(2,1)S(1)} %project_send.9), channel_id=1, source_target_pairs={{0,3},{1,2},{2,1},{3,0},{4,7},{5,6},{6,5},{7,4},{8,11},{9,10},{10,... | collective-permute-start | bytes 417800 | tf_op jit(solution)/shard_map/ppermute | solution.py:545
  27.1 3.9 %copy-start.1 = (f32[32,64]{1,0:T(8,128)S(1)}, f32[32,64]{1,0:T(8,128)}, u32[]{:S(2)}) copy-start(f32[32,64]{1,0:T(8,128)} %refs_5_.1) | copy-start | bytes 24580
  27.1 17.0 %collective-permute-start.4 = (s16[272,256]{1,0:T(8,128)(2,1)S(1)}, s16[272,256]{1,0:T(8,128)(2,1)S(1)}, u32[]{:S(2)}, u32[]{:S(2)}) collective-permute-start(s16[272,256]{1,0:T(8,128)(2,1)S(1)} %project_send.10), channel_id=1, source_target_pairs={{0,2},{1,3},{2,0},{3,1},{4,6},{5,7},{6,4},{7,5},{8,10},{9,11},{10,... | collective-permute-start | bytes 417800 | tf_op jit(solution)/shard_map/ppermute | solution.py:545
  30.4 5.1 %copy-start.3 = (f32[64,64]{1,0:T(8,128)S(1)}, f32[64,64]{1,0:T(8,128)}, u32[]{:S(2)}) copy-start(f32[64,64]{1,0:T(8,128)} %h_ref.3) | copy-start | bytes 49156
  30.4 5.1 %copy-start.4 = (s32[32]{0:T(128)S(1)}, s32[32]{0:T(128)}, u32[]{:S(2)}) copy-start(s32[32]{0:T(128)} %counts_ref.3) | copy-start | bytes 388
  30.4 13.8 %collective-permute-start.5 = (s16[272,256]{1,0:T(8,128)(2,1)S(1)}, s16[272,256]{1,0:T(8,128)(2,1)S(1)}, u32[]{:S(2)}, u32[]{:S(2)}) collective-permute-start(s16[272,256]{1,0:T(8,128)(2,1)S(1)} %project_send.11), channel_id=1, source_target_pairs={{0,1},{1,0},{2,3},{3,2},{4,5},{5,4},{6,7},{7,6},{8,9},{9,8},{10,11... | collective-permute-start | bytes 417800 | tf_op jit(solution)/shard_map/ppermute | solution.py:545
  52.7 14.5 %collective-permute-start.12 = (bf16[8,64,256]{2,1,0:T(8,128)(2,1)S(1)}, bf16[8,64,256]{2,1,0:T(8,128)(2,1)S(1)}, u32[]{:S(2)}, u32[]{:S(2)}) collective-permute-start(bf16[8,64,256]{2,1,0:T(8,128)(2,1)S(1)} %get-tuple-element.42.frames_ref), channel_id=1, source_target_pairs={{0,1},{1,0},{2,3},{3,2},{4,5},{5,4},{6,7},{7,6},{8,9},{9,8},{10,11... | collective-permute-start | bytes 786440 | tf_op jit(solution)/shard_map/ppermute | solution.py:545
  54.2 19.3 %collective-permute-start.14 = (bf16[8,64,256]{2,1,0:T(8,128)(2,1)S(1)}, bf16[8,64,256]{2,1,0:T(8,128)(2,1)S(1)}, u32[]{:S(2)}, u32[]{:S(2)}) collective-permute-start(bf16[8,64,256]{2,1,0:T(8,128)(2,1)S(1)} %get-tuple-element.42.frames_ref), channel_id=1, source_target_pairs={{0,3},{1,2},{2,1},{3,0},{4,7},{5,6},{6,5},{7,4},{8,11},{9,10},{10,... | collective-permute-start | bytes 786440 | tf_op jit(solution)/shard_map/ppermute | solution.py:545
  56.6 23.8 %collective-permute-start.13 = (bf16[8,64,256]{2,1,0:T(8,128)(2,1)S(1)}, bf16[8,64,256]{2,1,0:T(8,128)(2,1)S(1)}, u32[]{:S(2)}, u32[]{:S(2)}) collective-permute-start(bf16[8,64,256]{2,1,0:T(8,128)(2,1)S(1)} %get-tuple-element.42.frames_ref), channel_id=1, source_target_pairs={{0,2},{1,3},{2,0},{3,1},{4,6},{5,7},{6,4},{7,5},{8,10},{9,11},{10,... | collective-permute-start | bytes 786440 | tf_op jit(solution)/shard_map/ppermute | solution.py:545
  57.1 1.5 %collective-permute-start.6 = (f32[64,128]{1,0:T(8,128)S(1)}, f32[64,128]{1,0:T(8,128)S(1)}, u32[]{:S(2)}, u32[]{:S(2)}) collective-permute-start(f32[64,128]{1,0:T(8,128)S(1)} %get-tuple-element.41.refs_0_), channel_id=1, source_target_pairs={{0,4},{4,0},{8,12},{12,8},{1,5},{5,1},{9,13},{13,9},{2,6},{6,2},{1... | collective-permute-start | bytes 98312 | tf_op jit(solution)/shard_map/ppermute | solution.py:545
  57.1 6.2 %collective-permute-start.7 = (f32[64,128]{1,0:T(8,128)S(1)}, f32[64,128]{1,0:T(8,128)S(1)}, u32[]{:S(2)}, u32[]{:S(2)}) collective-permute-start(f32[64,128]{1,0:T(8,128)S(1)} %get-tuple-element.41.refs_0_), channel_id=1, source_target_pairs={{0,8},{4,12},{8,0},{12,4},{1,9},{5,13},{9,1},{13,5},{2,10},{6,14},... | collective-permute-start | bytes 98312 | tf_op jit(solution)/shard_map/ppermute | solution.py:545
  58.6 4.7 %collective-permute-start.8 = (f32[64,128]{1,0:T(8,128)S(1)}, f32[64,128]{1,0:T(8,128)S(1)}, u32[]{:S(2)}, u32[]{:S(2)}) collective-permute-start(f32[64,128]{1,0:T(8,128)S(1)} %get-tuple-element.41.refs_0_), channel_id=1, source_target_pairs={{0,12},{4,8},{8,4},{12,0},{1,13},{5,9},{9,5},{13,1},{2,14},{6,10},... | collective-permute-start | bytes 98312 | tf_op jit(solution)/shard_map/ppermute | solution.py:545
  63.4 20.7 %collective-permute-start.10 = (f32[64,64]{1,0:T(8,128)S(1)}, f32[64,64]{1,0:T(8,128)S(1)}, u32[]{:S(2)}, u32[]{:S(2)}) collective-permute-start(f32[64,64]{1,0:T(8,128)S(1)} %get-tuple-element.44.refs_0_), channel_id=1, source_target_pairs={{0,2},{1,3},{2,0},{3,1},{4,6},{5,7},{6,4},{7,5},{8,10},{9,11},{10,... | collective-permute-start | bytes 49160 | tf_op jit(solution)/shard_map/ppermute | solution.py:545
  65.8 18.3 %collective-permute-start.11 = (f32[64,64]{1,0:T(8,128)S(1)}, f32[64,64]{1,0:T(8,128)S(1)}, u32[]{:S(2)}, u32[]{:S(2)}) collective-permute-start(f32[64,64]{1,0:T(8,128)S(1)} %get-tuple-element.44.refs_0_), channel_id=1, source_target_pairs={{0,3},{1,2},{2,1},{3,0},{4,7},{5,6},{6,5},{7,4},{8,11},{9,10},{10,... | collective-permute-start | bytes 49160 | tf_op jit(solution)/shard_map/ppermute | solution.py:545
  67.2 16.9 %collective-permute-start.9 = (f32[64,64]{1,0:T(8,128)S(1)}, f32[64,64]{1,0:T(8,128)S(1)}, u32[]{:S(2)}, u32[]{:S(2)}) collective-permute-start(f32[64,64]{1,0:T(8,128)S(1)} %get-tuple-element.44.refs_0_), channel_id=1, source_target_pairs={{0,1},{1,0},{2,3},{3,2},{4,5},{5,4},{6,7},{7,6},{8,9},{9,8},{10,11... | collective-permute-start | bytes 49160 | tf_op jit(solution)/shard_map/ppermute | solution.py:545
  85.2 7.3 %copy-start.2 = (f32[64,64]{1,0:T(8,128)S(1)}, f32[64,64]{1,0:T(8,128)}, u32[]{:S(2)}) copy-start(f32[64,64]{1,0:T(8,128)} %get-tuple-element.31.h_ref.refs_1_) | copy-start | bytes 49156
  89.5 1.4 %collective-permute-start.15 = (f32[64,512]{1,0:T(8,128)S(1)}, f32[64,512]{1,0:T(8,128)S(1)}, u32[]{:S(2)}, u32[]{:S(2)}) collective-permute-start(f32[64,512]{1,0:T(8,128)S(1)} %get-tuple-element.60), channel_id=1, source_target_pairs={{0,4},{4,0},{8,12},{12,8},{1,5},{5,1},{9,13},{13,9},{2,6},{6,2},{1... | collective-permute-start | bytes 393224 | tf_op jit(solution)/shard_map/ppermute | solution.py:545
  91.0 5.6 %collective-permute-start.16 = (f32[64,512]{1,0:T(8,128)S(1)}, f32[64,512]{1,0:T(8,128)S(1)}, u32[]{:S(2)}, u32[]{:S(2)}) collective-permute-start(f32[64,512]{1,0:T(8,128)S(1)} %add.3.a_ref), channel_id=1, source_target_pairs={{0,8},{4,12},{8,0},{12,4},{1,9},{5,13},{9,1},{13,5},{2,10},{6,14},... | collective-permute-start | bytes 393224 | tf_op jit(solution)/shard_map/ppermute | solution.py:545
  96.6 1.4 %collective-permute-start.17 = (f32[64,512]{1,0:T(8,128)S(1)}, f32[64,512]{1,0:T(8,128)S(1)}, u32[]{:S(2)}, u32[]{:S(2)}) collective-permute-start(f32[64,512]{1,0:T(8,128)S(1)} %add_terms.1.own_ref), channel_id=1, source_target_pairs={{0,4},{4,0},{8,12},{12,8},{1,5},{5,1},{9,13},{13,9},{2,6},{6,2},{1... | collective-permute-start | bytes 393224 | tf_op jit(solution)/shard_map/ppermute | solution.py:545

commit v6 on v4

--- a/solution.py
+++ b/solution.py
@@ -49,14 +49,15 @@
 
 
 ANY_SPEC = pl.BlockSpec(memory_space=pl.ANY)
+HBM_SPEC = pl.BlockSpec(memory_space=pltpu.HBM)
 
 
 def parameters(mib):
     return pltpu.CompilerParams(vmem_limit_bytes=mib * MIB)
 
 
-STREAM = 50
-SMALL = 16
+LIMIT = 16
+AHEAD = 2
 VMEM_SPEC = pl.BlockSpec(memory_space=pltpu.VMEM)
 SMEM_SPEC = pl.BlockSpec(memory_space=pltpu.SMEM)
 
@@ -74,17 +75,16 @@
     return jnp.ceil(jnp.log2(jnp.maximum(top, 1e-30)))
 
 
-def fetch(source, buffers, sems):
-    copies = [
-        pltpu.make_async_copy(source.at[p], buffers.at[p], sems.at[p]) for p in range(buffers.shape[0])
-    ]
-    for copy in copies:
+def patients_of(source, buffers, sems):
+    count = buffers.shape[0]
+    copies = [pltpu.make_async_copy(source.at[p], buffers.at[p], sems.at[p]) for p in range(count)]
+    for copy in copies[:AHEAD]:
         copy.start()
-    return copies
-
-
-def project_patient(v_ref, visits):
-    return low_dot(visits, v_ref[...], ROWS_BY_ROWS).T
+    for p, copy in enumerate(copies):
+        copy.wait()
+        if p + AHEAD < count:
+            copies[p + AHEAD].start()
+        yield buffers[p]
 
 
 def encode_rest(share, v_ref, coded_ref, exponents):
@@ -116,13 +116,15 @@
     return [rows(p * rank, rank) * steps[:, p : p + 1] for p in range(share)], gram
 
 
-def send_projection_kernel(slot, place, v_ref, visits_ref, coded_ref, buffers, sems):
-    copies = fetch(visits_ref.at[place[0] ^ slot], buffers, sems)
-    share, rank = len(copies), v_ref.shape[0]
+def send_projection_kernel(slot, place, v_hbm, visits_ref, coded_ref, v_ref, buffers, sems, v_sem):
+    v_copy = pltpu.make_async_copy(v_hbm, v_ref, v_sem)
+    v_copy.start()
+    share, rank = buffers.shape[0], v_ref.shape[0]
     exponents = jnp.zeros((rank, LANES), F32)
-    for p, copy in enumerate(copies):
-        copy.wait()
-        proj = project_patient(v_ref, buffers[p])
+    for p, visits in enumerate(patients_of(visits_ref.at[place[0] ^ slot], buffers, sems)):
+        if p == 0:
+            v_copy.wait()
+        proj = low_dot(v_ref[...], visits, ROWS_BY_ROWS)
         exponent = row_exponent(proj)
         coded = jnp.floor(proj * (LEVELS / jnp.exp2(exponent)) + 0.5)
         coded_ref[pl.ds(p * rank, rank), :] = coded.astype(jnp.int32).astype(jnp.int16)
@@ -130,18 +132,24 @@
     encode_rest(share, v_ref, coded_ref, exponents)
 
 
-def own_projection_kernel(place, v_ref, w_ref, visits_ref, proj_ref, v_gram_ref, w_gram_ref, buffers, sems):
-    copies = fetch(visits_ref.at[place[0]], buffers, sems)
+def own_projection_kernel(place, v_hbm, w_ref, visits_ref, proj_ref, v_gram_ref, w_gram_ref, v_ref, buffers, sems, v_sem):
+    v_copy = pltpu.make_async_copy(v_hbm, v_ref, v_sem)
+    v_copy.start()
+    for p, visits in enumerate(patients_of(visits_ref.at[place[0]], buffers, sems)):
+        if p == 0:
+            v_copy.wait()
+        proj_ref[p] = low_dot(v_ref[...], visits, ROWS_BY_ROWS)
     v_gram_ref[...] = low_dot(v_ref[...], v_ref[...], ROWS_BY_ROWS)
     w_gram_ref[...] = high_dot(w_ref[...], w_ref[...], COLS_BY_COLS)
-    for p, copy in enumerate(copies):
-        copy.wait()
-        proj_ref[p] = project_patient(v_ref, buffers[p])
-
-
-def visits_buffers(visits):
-    share = visits.shape[1]
-    return [pltpu.VMEM(visits.shape[1:], BF16), pltpu.SemaphoreType.DMA((share,))]
+
+
+def projection_buffers(visits, v_rows):
+    return [
+        pltpu.VMEM(v_rows.shape, BF16),
+        pltpu.VMEM(visits.shape[1:], BF16),
+        pltpu.SemaphoreType.DMA((visits.shape[1],)),
+        pltpu.SemaphoreType.DMA,
+    ]
 
 
 def project_for(slot, place, visits, v_rows):
@@ -149,11 +157,11 @@
     rank = v_rows.shape[0]
     return pl.pallas_call(
         functools.partial(send_projection_kernel, slot),
-        in_specs=[SMEM_SPEC, VMEM_SPEC, ANY_SPEC],
+        in_specs=[SMEM_SPEC, HBM_SPEC, HBM_SPEC],
         out_specs=VMEM_SPEC,
         out_shape=jax.ShapeDtypeStruct(payload_shape(share, rank, slots), jnp.int16),
-        scratch_shapes=visits_buffers(visits),
-        compiler_params=parameters(STREAM),
+        scratch_shapes=projection_buffers(visits, v_rows),
+        compiler_params=parameters(LIMIT),
         cost_estimate=SHORT,
         name="project_send",
     )(place, v_rows, visits)
@@ -165,15 +173,15 @@
     gram = (rank, rank)
     return pl.pallas_call(
         own_projection_kernel,
-        in_specs=[SMEM_SPEC, VMEM_SPEC, VMEM_SPEC, ANY_SPEC],
+        in_specs=[SMEM_SPEC, HBM_SPEC, VMEM_SPEC, HBM_SPEC],
         out_specs=[VMEM_SPEC] * 3,
         out_shape=[
             jax.ShapeDtypeStruct((share, rank, slots), F32),
             jax.ShapeDtypeStruct(gram, F32),
             jax.ShapeDtypeStruct(gram, F32),
         ],
-        scratch_shapes=visits_buffers(visits),
-        compiler_params=parameters(STREAM),
+        scratch_shapes=projection_buffers(visits, v_rows),
+        compiler_params=parameters(LIMIT),
         cost_estimate=SHORT,
         name="project_own",
     )(place, v_rows, w_start, visits)
@@ -238,7 +246,7 @@
         in_specs=[VMEM_SPEC] * 2 + [ANY_SPEC],
         out_specs=VMEM_SPEC,
         out_shape=jax.ShapeDtypeStruct(w_gram.shape, F32),
-        compiler_params=parameters(SMALL),
+        compiler_params=parameters(LIMIT),
         cost_estimate=SHORT,
         name="first_inverse",
     )(v_gram, w_gram, after)
@@ -259,7 +267,7 @@
         in_specs=[VMEM_SPEC] * len(terms) + [ANY_SPEC],
         out_specs=[VMEM_SPEC] * 2,
         out_shape=[jax.ShapeDtypeStruct((rank, rank), F32)] * 2,
-        compiler_params=parameters(SMALL),
+        compiler_params=parameters(LIMIT),
         cost_estimate=SHORT,
         name="sum_h",
     )(*terms, after)
@@ -267,16 +275,15 @@
 
 def sweep_once(frames, p, rank, fine):
     frame = frames[p]
-    first, second = two_parts(frame)
     if fine:
-        both = low_dot(jnp.concatenate([first, second], axis=0), first, ROWS_BY_ROWS)
-        gram = both[:rank] + (both[rank:] + both[rank:].T)
-        gram_first, gram_second = two_parts(gram)
-        moved = low_dot(
-            jnp.concatenate([gram_first, gram_second, gram_first], axis=1),
-            jnp.concatenate([first, first, second], axis=0),
-        )
+        both = jnp.concatenate(two_parts(frame), axis=0)
+        blocks = low_dot(both, both, ROWS_BY_ROWS)
+        blocks = blocks[:rank] + blocks[rank:]
+        gram = blocks + pltpu.roll(blocks, rank, 1)
+        moved = low_dot(jnp.concatenate(two_parts(gram), axis=0), both)
+        moved = moved[:rank] + moved[rank:]
     else:
+        first = frame.astype(BF16)
         moved = low_dot(low_dot(first, first, ROWS_BY_ROWS).astype(BF16), first)
     frames[p] = 1.5 * frame - 0.5 * moved
 
@@ -331,51 +338,35 @@
             jax.ShapeDtypeStruct((rank, rank), F32),
         ],
         scratch_shapes=[pltpu.VMEM(own.shape, F32)] * 2,
-        compiler_params=parameters(SMALL),
+        compiler_params=parameters(LIMIT),
         cost_estimate=SHORT,
         name="own_frames",
     )(place, counts, h_start, w_start, v_gram, w_gram, own, *coded)
 
 
-def projected_kernel(slot, place, frames_ref, visits_ref, *refs):
-    first_ref, second_ref, token_ref, buffers, first, second, sems, out_sems = refs[-8:]
-    copies = fetch(visits_ref.at[place[0] ^ slot], buffers, sems)
-    rank = frames_ref.shape[1]
+def projected_kernel(slot, place, frames_ref, visits_ref, first_ref, second_ref, token_ref):
+    owner = place[0] ^ slot
+    share, rank, _ = frames_ref.shape
     token_ref[...] = jnp.zeros_like(token_ref)
-    sent = []
-    for p, copy in enumerate(copies):
-        copy.wait()
+    for p in range(share):
         rows = pl.ds(p * rank, rank)
-        first[rows, :], second[rows, :] = two_parts(low_dot(frames_ref[p], buffers[p]))
-        for i, (source, target) in enumerate([(first, first_ref), (second, second_ref)]):
-            sent.append(pltpu.make_async_copy(source.at[rows], target.at[slot, rows], out_sems.at[i, p]))
-            sent[-1].start()
-    for copy in sent:
-        copy.wait()
-
-
-def project_frames(slot, place, frames, visits, before):
-    n_slots, share, slots, width = visits.shape
+        first_ref[rows, :], second_ref[rows, :] = two_parts(low_dot(frames_ref[p], visits_ref[owner, p]))
+
+
+def project_frames(slot, place, frames, visits):
+    _, share, slots, width = visits.shape
     rank = frames.shape[1]
-    out = jax.ShapeDtypeStruct((n_slots, share * rank, width), BF16)
-    *before, token = pl.pallas_call(
+    out = jax.ShapeDtypeStruct((share * rank, width), BF16)
+    *parts, token = pl.pallas_call(
         functools.partial(projected_kernel, slot),
-        in_specs=[SMEM_SPEC, VMEM_SPEC, ANY_SPEC] + [ANY_SPEC] * len(before),
-        out_specs=[ANY_SPEC, ANY_SPEC, VMEM_SPEC],
+        in_specs=[SMEM_SPEC, VMEM_SPEC, VMEM_SPEC],
+        out_specs=[VMEM_SPEC] * 3,
         out_shape=[out, out, jax.ShapeDtypeStruct((8, LANES), F32)],
-        scratch_shapes=[
-            pltpu.VMEM(visits.shape[1:], BF16),
-            pltpu.VMEM((share * rank, width), BF16),
-            pltpu.VMEM((share * rank, width), BF16),
-            pltpu.SemaphoreType.DMA((share,)),
-            pltpu.SemaphoreType.DMA((2, share)),
-        ],
-        input_output_aliases={3: 0, 4: 1} if before else {},
-        compiler_params=parameters(STREAM),
+        compiler_params=parameters(LIMIT),
         cost_estimate=SHORT,
         name="project_frames",
-    )(place, frames, visits, *before)
-    return before, token
+    )(place, frames, visits)
+    return parts, token
 
 
 def next_h_kernel(n_terms, n_slots, place, *refs):
@@ -406,7 +397,7 @@
             jax.ShapeDtypeStruct(inverse.shape, F32),
             jax.ShapeDtypeStruct((n_slots, 3 * rank, share * rank), BF16),
         ],
-        compiler_params=parameters(SMALL),
+        compiler_params=parameters(LIMIT),
         cost_estimate=SHORT,
         name="next_h",
     )(place, *terms, inverse, w_start, after)
@@ -423,53 +414,45 @@
     return pl.pallas_call(
         second_inverse_kernel,
         out_shape=[out, out],
-        compiler_params=parameters(SMALL),
+        compiler_params=parameters(LIMIT),
         cost_estimate=SHORT,
         name="second_inverse",
     )(h_next, w_gram)
 
 
-def v_terms_kernel(core, factor_ref, first_ref, second_ref, keep_ref, send_ref, terms_ref, first, second, sems):
-    firsts = fetch(first_ref, first, sems.at[0])
-    seconds = fetch(second_ref, second, sems.at[1])
+def v_terms_kernel(core, factor_ref, *refs):
+    *parts, keep_ref, send_ref, terms_ref = refs
     rank, width = terms_ref.shape
     half = width // 2
-    for slot, copies in enumerate(zip(firsts, seconds)):
-        for copy in copies:
-            copy.wait()
-        large = low_dot(factor_ref[slot], first[slot])
-        small = low_dot(factor_ref[slot, : 2 * rank], second[slot])
+    for slot in range(len(parts) // 2):
+        large = low_dot(factor_ref[slot], parts[2 * slot][...])
+        small = low_dot(factor_ref[slot, : 2 * rank], parts[2 * slot + 1][...])
         terms = large[:rank] + (large[rank : 2 * rank] + small[:rank]) + (large[2 * rank :] + small[rank:])
         terms_ref[...] = terms + terms_ref[...] if slot else terms
     keep_ref[...] = terms_ref[:, pl.ds(pl.multiple_of(core[0] * half, half), half)]
     send_ref[...] = terms_ref[:, pl.ds(pl.multiple_of((1 - core[0]) * half, half), half)]
 
 
-def projected_buffers(projected):
-    return [pltpu.VMEM(projected.shape, BF16)] * 2 + [pltpu.SemaphoreType.DMA((2, projected.shape[0]))]
-
-
-def all_v_terms(core, factor, first, second):
-    n_slots, rows, width = first.shape
+def all_v_terms(core, factor, projected):
+    width = projected[0].shape[1]
     rank = factor.shape[1] // 3
     half = (rank, width // 2)
     return pl.pallas_call(
         v_terms_kernel,
-        in_specs=[SMEM_SPEC, VMEM_SPEC, ANY_SPEC, ANY_SPEC],
+        in_specs=[SMEM_SPEC] + [VMEM_SPEC] * (1 + len(projected)),
         out_specs=[VMEM_SPEC] * 2,
         out_shape=[jax.ShapeDtypeStruct(half, F32)] * 2,
-        scratch_shapes=[pltpu.VMEM((rank, width), F32)] + projected_buffers(first),
-        compiler_params=parameters(STREAM),
+        scratch_shapes=[pltpu.VMEM((rank, width), F32)],
+        compiler_params=parameters(LIMIT),
         cost_estimate=SHORT,
         name="v_terms",
-    )(core, factor, first, second)
-
-
-def next_v_kernel(share, place, core, own_ref, other_ref, inverse_ref, h_ref, first_ref, second_ref, v_ref, sums_ref, *refs):
-    v_parts, first, second, sems = refs
-    firsts = fetch(first_ref, first, sems.at[0])
-    seconds = fetch(second_ref, second, sems.at[1])
+    )(core, factor, *projected)
+
+
+def next_v_kernel(n_parts, place, core, own_ref, other_ref, inverse_ref, h_ref, *refs):
+    parts, (v_ref, sums_ref, v_parts) = refs[:n_parts], refs[n_parts:]
     rank = inverse_ref.shape[0]
+    share = parts[0].shape[0] // rank
     upper = core[0] == 1
     left = jnp.where(upper, other_ref[...], own_ref[...])
     right = jnp.where(upper, own_ref[...], other_ref[...])
@@ -480,32 +463,31 @@
     gram = low_dot(v_parts[...], v_parts[...], ROWS_BY_ROWS)
     gram = gram[:rank, :rank] + (gram[:rank, rank:] + gram[rank:, :rank])
     sums_ref[...] = jnp.concatenate([jnp.zeros((rank, rank), F32), gram], axis=1)
-    for slot, copies in enumerate(zip(firsts, seconds)):
-        for copy in copies:
-            copy.wait()
-        seen = low_dot(first[slot], v_parts[...], ROWS_BY_ROWS) + low_dot(second[slot], v_parts[...], ROWS_BY_ROWS)
-        start = (place[0] ^ slot) * share
+    for slot in range(n_parts // 2):
+        seen = low_dot(parts[2 * slot][...], v_parts[...], ROWS_BY_ROWS)
+        seen = seen + low_dot(parts[2 * slot + 1][...], v_parts[...], ROWS_BY_ROWS)
+        first = (place[0] ^ slot) * share
         for p in range(share):
             row = jnp.sum(seen[p * rank : (p + 1) * rank] * weights, axis=0, keepdims=True)
-            sums_ref[pl.ds(start + p, 1), :rank] = row[:, :rank] + row[:, rank:]
-
-
-def next_v(place, core, own, other, inverse, h_next, first, second):
-    n_slots, rows, width = first.shape
+            sums_ref[pl.ds(first + p, 1), :rank] = row[:, :rank] + row[:, rank:]
+
+
+def next_v(place, core, own, other, inverse, h_next, projected):
+    width = projected[0].shape[1]
     rank = inverse.shape[0]
     return pl.pallas_call(
-        functools.partial(next_v_kernel, rows // rank),
-        in_specs=[SMEM_SPEC] * 2 + [VMEM_SPEC] * 4 + [ANY_SPEC] * 2,
+        functools.partial(next_v_kernel, len(projected)),
+        in_specs=[SMEM_SPEC] * 2 + [VMEM_SPEC] * (4 + len(projected)),
         out_specs=[VMEM_SPEC] * 2,
         out_shape=[
             jax.ShapeDtypeStruct((rank, width), F32),
             jax.ShapeDtypeStruct((rank, 2 * rank), F32),
         ],
-        scratch_shapes=[pltpu.VMEM((2 * rank, width), BF16)] + projected_buffers(first),
-        compiler_params=parameters(STREAM),
+        scratch_shapes=[pltpu.VMEM((2 * rank, width), BF16)],
+        compiler_params=parameters(LIMIT),
         cost_estimate=SHORT,
         name="next_v",
-    )(place, core, own, other, inverse, h_next, first, second)
+    )(place, core, own, other, inverse, h_next, *projected)
 
 
 def next_w_kernel(n_sums, *refs):
@@ -521,7 +503,7 @@
     return pl.pallas_call(
         functools.partial(next_w_kernel, len(sums)),
         out_shape=jax.ShapeDtypeStruct((patients, rank), F32),
-        compiler_params=parameters(SMALL),
+        compiler_params=parameters(LIMIT),
         cost_estimate=SHORT,
         name="next_w",
     )(*sums, h_gram)
@@ -539,6 +521,15 @@
     return [x] + [swap(x, axis, s) for s in range(1, n)]
 
 
+def staged_terms(x, axis):
+    n = lax.axis_size(axis)
+    step = 1
+    while 2 * step < n:
+        x = x + swap(x, axis, step)
+        step *= 2
+    return [x, swap(x, axis, step)]
+
+
 def add_kernel(a_ref, b_ref, after_ref, sum_ref):
     sum_ref[...] = a_ref[...] + b_ref[...]
 
@@ -549,7 +540,7 @@
         in_specs=[VMEM_SPEC] * 2 + [ANY_SPEC],
         out_specs=VMEM_SPEC,
         out_shape=jax.ShapeDtypeStruct(a.shape, a.dtype),
-        compiler_params=parameters(SMALL),
+        compiler_params=parameters(LIMIT),
         cost_estimate=SHORT,
         name="add_terms",
     )(a, b, after)
@@ -571,30 +562,33 @@
     place = lax.axis_index("feature").astype(jnp.int32).reshape(1)
     core = lax.rem(lax.axis_index("patient").astype(jnp.int32), 2).reshape(1)
     by_owner = visits.reshape(n, share, slots, width)
-    v_rows = v_start.T
-
-    coded = [swap(project_for(slot, place, by_owner, v_rows), "feature", slot) for slot in range(n - 1, 0, -1)]
-    own, v_local, w_local = project_own(place, by_owner, v_rows, w_start)
+    in_hbm = pltpu.with_memory_space_constraint(by_owner, pltpu.HBM)
+    v_rows = pltpu.with_memory_space_constraint(v_start.T, pltpu.HBM)
+
+    coded = [swap(project_for(slot, place, in_hbm, v_rows), "feature", slot) for slot in range(n - 1, 0, -1)]
+    own, v_local, w_local = project_own(place, in_hbm, v_rows, w_start)
 
     frames, h_local, v_gram = own_frames(place, visit_counts, h_start, w_start, v_local, w_local, own, coded)
     far = list(range(n - 1, 1, -1))
     all_frames = {0: frames} | {slot: swap(frames, "feature", slot) for slot in far + [1]}
     h_sums = all_terms(h_local, "patient")
 
-    projected, token = project_frames(0, place, frames, by_owner, [])
+    parts, token = project_frames(0, place, frames, by_owner)
+    projected = {0: parts}
     h_sum, w_gram = sum_h(h_sums, token)
     h_terms = all_terms(h_sum, "feature")
-    projected, token = project_frames(1, place, all_frames[1], by_owner, projected)
+    projected[1], token = project_frames(1, place, all_frames[1], by_owner)
     first = first_inverse(v_gram, w_gram, token)
     for slot in far:
-        projected, token = project_frames(slot, place, all_frames[slot], by_owner, projected)
+        projected[slot], token = project_frames(slot, place, all_frames[slot], by_owner)
     h_next, factor = next_h(place, h_terms, first, w_start, n, token)
 
-    keep, send = all_v_terms(core, factor, *projected)
+    flat = [part for slot in range(n) for part in projected[slot]]
+    keep, send = all_v_terms(core, factor, flat)
     h_gram, second = second_inverse(h_next, w_gram)
     own_terms, other_terms = patient_halves(keep, send, second)
-    v_next, sums = next_v(place, core, own_terms, other_terms, second, h_next, *projected)
-    w_next = next_w(all_terms(sums, "feature"), h_gram, patients)
+    v_next, sums = next_v(place, core, own_terms, other_terms, second, h_next, flat)
+    w_next = next_w(staged_terms(sums, "feature"), h_gram, patients)
     return (h_next, v_next.T, w_next)
 
 

time: 128 us -> 107 us (0.84)
  Pallas kernels: 84.8 us -> 53.8 us
  local copies, waits for them, and re-layouts: 0.92 us -> 12.3 us
  starting transfers between devices: 22.4 us -> 16.6 us
  waiting for transfers between devices: 18.7 us -> 22.9 us
    pallas_call x1, Pallas kernels: 25.8 us -> 10.9 us  [own_frames(): pl.pallas_call(functools.partial(frames_kernel, share, len(coded)), in_sp...]
    unnamed x10 -> x20, local copies, waits for them, and re-layouts: 0.92 us -> 12.3 us
    pallas_call x4, Pallas kernels: 15.3 us -> 4.02 us  [project_frames(): pl.pallas_call(functools.partial(projected_kernel, slot), in_specs=[SMEM_...]
    pallas_call x3, Pallas kernels: 17 us -> 11 us  [the longest x1 6.58 us: project_own(): pl.pallas_call(own_projection_kernel, in_specs=[SMEM_SPEC, HBM_SPEC, VMEM...]
    ppermute x18 -> x17, starting transfers between devices: 22.4 us -> 16.6 us  [swap(): return lax.ppermute(x, axis, pairs)]
    ppermute x18 -> x17, waiting for transfers between devices: 18.7 us -> 22.9 us  [swap(): return lax.ppermute(x, axis, pairs)]
  transfers between devices with their start and end apart: 18 -> 17, of which waited for: 8 -> 10; matrix products, arithmetic and copies ran while one was open for 0% -> 0% of each run, Pallas kernels for 29% -> 27%
where the time goes in v6:
time: 107 us
  Pallas kernels  53.8 us (50%)
  waiting for transfers between devices  22.9 us (21%)
  starting transfers between devices  16.6 us (16%)
  local copies, waits for them, and re-layouts  12.3 us (11%)
    ppermute x17, waiting for transfers between devices, swap(): return lax.ppermute(x, axis, pairs)  22.9 us
    pallas_call x3, Pallas kernels, project_for(): pl.pallas_call(functools.partial(send_projection_kernel, slot), in_specs=...  18.1 us
    ppermute x17, starting transfers between devices, swap(): return lax.ppermute(x, axis, pairs)  16.6 us
    unnamed x20, local copies, waits for them, and re-layouts  12.3 us
    pallas_call x1, Pallas kernels, own_frames(): pl.pallas_call(functools.partial(frames_kernel, share, len(coded)), in_sp...  10.9 us
    pallas_call x1, Pallas kernels, project_own(): pl.pallas_call(own_projection_kernel, in_specs=[SMEM_SPEC, HBM_SPEC, VMEM...  6.58 us
    pallas_call x4, Pallas kernels, project_frames(): pl.pallas_call(functools.partial(projected_kernel, slot), in_specs=[SMEM_...  4.02 us
    pallas_call x1, Pallas kernels, next_w(): pl.pallas_call(functools.partial(next_w_kernel, len(sums)), out_shape=jax...  3.36 us
  transfers between devices with their start and end apart: 17, of which 10 were waited for; matrix products, arithmetic and copies ran while one was open for 0% of the time, Pallas kernels for 27%

profile of v6, /device:TPU:0, one launch (start us, length us, event | category | flops | bytes accessed | tf_op | source)
XLA Modules:
  0.0 106.6 jit_solution(3137383757985578109)
XLA Ops:
  0.6 5.5 %project_send.3 = s16[560,256]{1,0:T(8,128)(2,1)S(1)} custom-call(s32[1]{0:T(128)} %bitcast.place, bf16[64,1024]{1,0:T(8,128)(2,1)} %bitcast.15, bf16[4,8,256,1024]{3,2,1,0:T(8,128)(2,1)} %bitcast.5), custom_call_target="tpu_custom_call" | custom-call | flops 1000 | bytes 1000 | tf_op jit(solution)/shard_map/project_send/pallas_call | solution.py:158
  6.2 5.1 %collective-permute-start = (s16[560,256]{1,0:T(8,128)(2,1)S(1)}, s16[560,256]{1,0:T(8,128)(2,1)S(1)}, u32[]{:S(2)}, u32[]{:S(2)}) collective-permute-start(s16[560,256]{1,0:T(8,128)(2,1)S(1)} %project_send.3), channel_id=1, source_target_pairs={{0,3},{1,2},{2,1},{3,0},{4,7},{5,6},{6,5},{7,4},{8,11},{9,10},{10,... | collective-permute-start | bytes 860168 | tf_op jit(solution)/shard_map/ppermute | solution.py:514
  11.3 5.5 %project_send.4 = s16[560,256]{1,0:T(8,128)(2,1)S(1)} custom-call(s32[1]{0:T(128)} %bitcast.place, bf16[64,1024]{1,0:T(8,128)(2,1)} %bitcast.16, bf16[4,8,256,1024]{3,2,1,0:T(8,128)(2,1)} %bitcast.6), custom_call_target="tpu_custom_call" | custom-call | flops 1000 | bytes 1000 | tf_op jit(solution)/shard_map/project_send/pallas_call | solution.py:158
  17.0 7.0 %project_send.5 = s16[560,256]{1,0:T(8,128)(2,1)S(1)} custom-call(s32[1]{0:T(128)} %bitcast.place, bf16[64,1024]{1,0:T(8,128)(2,1)} %bitcast.17, bf16[4,8,256,1024]{3,2,1,0:T(8,128)(2,1)} %bitcast.7), custom_call_target="tpu_custom_call" | custom-call | flops 1000 | bytes 1000 | tf_op jit(solution)/shard_map/project_send/pallas_call | solution.py:158
  24.1 6.6 %project_own.1 = (f32[8,64,256]{2,1,0:T(8,128)S(1)}, f32[64,64]{1,0:T(8,128)S(1)}, f32[64,64]{1,0:T(8,128)S(1)}) custom-call(s32[1]{0:T(128)} %bitcast.place, bf16[64,1024]{1,0:T(8,128)(2,1)} %bitcast.18, f32[32,64]{1,0:T(8,128)S(1)} %copy-done.2, bf16[4,8,256,1024]{3,2,1,0:T(8,128)(2,1)} %bitcast.8), custom_call_target="tpu_custom_call" | custom-call | flops 1000 | bytes 1000 | tf_op jit(solution)/shard_map/project_own/pallas_call | solution.py:174
  30.7 5.2 %collective-permute-done.1.refs_1_ = s16[560,256]{1,0:T(8,128)(2,1)S(1)} collective-permute-done((s16[560,256]{1,0:T(8,128)(2,1)S(1)}, s16[560,256]{1,0:T(8,128)(2,1)S(1)}, u32[]{:S(2)}, u32[]{:S(2)}) %collective-permute-start.1) | collective-permute-done | bytes 286752 | tf_op jit(solution)/shard_map/ppermute | solution.py:514
  35.8 2.7 %collective-permute-done.2.refs_2_ = s16[560,256]{1,0:T(8,128)(2,1)S(1)} collective-permute-done((s16[560,256]{1,0:T(8,128)(2,1)S(1)}, s16[560,256]{1,0:T(8,128)(2,1)S(1)}, u32[]{:S(2)}, u32[]{:S(2)}) %collective-permute-start.2) | collective-permute-done | bytes 286752 | tf_op jit(solution)/shard_map/ppermute | solution.py:514
  38.5 10.9 %own_frames.1 = (bf16[8,64,256]{2,1,0:T(8,128)(2,1)S(1)}, f32[64,128]{1,0:T(8,128)S(1)}, f32[64,64]{1,0:T(8,128)S(1)}) custom-call(s32[1]{0:T(128)} %bitcast.place, s32[32]{0:T(128)S(1)} %copy-done.5, f32[64,64]{1,0:T(8,128)S(1)} %copy-done.4, f32[32,64]{1,0:T(8,128)S(1)} %copy-done.2, f32[64,64]{1,0:T(8,128)S(1)} %get-tuple-element.30.v_gram_ref, ...), custom_call_target="tpu_custom_call" | custom-call | flops 1000 | bytes 1000 | tf_op jit(solution)/shard_map/own_frames/pallas_call | solution.py:331
  49.5 1.5 %collective-permute-start.10 = (bf16[8,64,256]{2,1,0:T(8,128)(2,1)S(1)}, bf16[8,64,256]{2,1,0:T(8,128)(2,1)S(1)}, u32[]{:S(2)}, u32[]{:S(2)}) collective-permute-start(bf16[8,64,256]{2,1,0:T(8,128)(2,1)S(1)} %get-tuple-element.34.frames_ref), channel_id=1, source_target_pairs={{0,2},{1,3},{2,0},{3,1},{4,6},{5,7},{6,4},{7,5},{8,10},{9,11},{10,... | collective-permute-start | bytes 786440 | tf_op jit(solution)/shard_map/ppermute | solution.py:514
  51.0 2.9 %collective-permute-start.11 = (bf16[8,64,256]{2,1,0:T(8,128)(2,1)S(1)}, bf16[8,64,256]{2,1,0:T(8,128)(2,1)S(1)}, u32[]{:S(2)}, u32[]{:S(2)}) collective-permute-start(bf16[8,64,256]{2,1,0:T(8,128)(2,1)S(1)} %get-tuple-element.34.frames_ref), channel_id=1, source_target_pairs={{0,3},{1,2},{2,1},{3,0},{4,7},{5,6},{6,5},{7,4},{8,11},{9,10},{10,... | collective-permute-start | bytes 786440 | tf_op jit(solution)/shard_map/ppermute | solution.py:514
  53.9 1.5 %collective-permute-start.4 = (f32[64,128]{1,0:T(8,128)S(1)}, f32[64,128]{1,0:T(8,128)S(1)}, u32[]{:S(2)}, u32[]{:S(2)}) collective-permute-start(f32[64,128]{1,0:T(8,128)S(1)} %get-tuple-element.33.refs_0_), channel_id=1, source_target_pairs={{0,8},{4,12},{8,0},{12,4},{1,9},{5,13},{9,1},{13,5},{2,10},{6,14},... | collective-permute-start | bytes 98312 | tf_op jit(solution)/shard_map/ppermute | solution.py:514
  55.4 2.1 %collective-permute-done.5.refs_3_ = f32[64,128]{1,0:T(8,128)S(1)} collective-permute-done((f32[64,128]{1,0:T(8,128)S(1)}, f32[64,128]{1,0:T(8,128)S(1)}, u32[]{:S(2)}, u32[]{:S(2)}) %collective-permute-start.5) | collective-permute-done | bytes 32800 | tf_op jit(solution)/shard_map/ppermute | solution.py:514
  60.3 2.9 %collective-permute-start.6 = (f32[64,64]{1,0:T(8,128)S(1)}, f32[64,64]{1,0:T(8,128)S(1)}, u32[]{:S(2)}, u32[]{:S(2)}) collective-permute-start(f32[64,64]{1,0:T(8,128)S(1)} %get-tuple-element.36.refs_0_), channel_id=1, source_target_pairs={{0,1},{1,0},{2,3},{3,2},{4,5},{5,4},{6,7},{7,6},{8,9},{9,8},{10,11... | collective-permute-start | bytes 49160 | tf_op jit(solution)/shard_map/ppermute | solution.py:514
  63.2 5.8 %copy-done = bf16[32,256,1024]{2,1,0:T(8,128)(2,1)S(1)} copy-done((bf16[32,256,1024]{2,1,0:T(8,128)(2,1)S(1)}, bf16[32,256,1024]{2,1,0:T(8,128)(2,1)}, u32[]{:S(2)}) %copy-start) | copy-done | bytes 16777240
  69.9 2.6 %first_inverse.1.refs_4_ = f32[64,64]{1,0:T(8,128)S(1)} custom-call(f32[64,64]{1,0:T(8,128)S(1)} %get-tuple-element.37.v_gram_ref, f32[64,64]{1,0:T(8,128)S(1)} %get-tuple-element.38.w_gram_ref, f32[8,128]{1,0:T(8,128)S(1)} %get-tuple-element.39.after_ref), custom_call_target="tpu_custom_call" | custom-call | flops 1000 | bytes 1000 | tf_op jit(solution)/shard_map/first_inverse/pallas_call | solution.py:244
  72.5 5.8 %copy-done.1 = bf16[32,256,1024]{2,1,0:T(8,128)(2,1)S(1)} copy-done((bf16[32,256,1024]{2,1,0:T(8,128)(2,1)S(1)}, bf16[32,256,1024]{2,1,0:T(8,128)(2,1)}, u32[]{:S(2)}) %copy-start.1) | copy-done | bytes 16777240
  79.1 1.4 %project_frames.7 = (bf16[512,1024]{1,0:T(8,128)(2,1)S(1)}, bf16[512,1024]{1,0:T(8,128)(2,1)S(1)}, f32[8,128]{1,0:T(8,128)}) custom-call(s32[1]{0:T(128)} %bitcast.place, bf16[8,64,256]{2,1,0:T(8,128)(2,1)S(1)} %collective-permute-done.11.frames_ref, bf16[4,8,256,1024]{3,2,1,0:T(8,128)(2,1)S(1)} %bitcast.14), custom_call_target="tpu_custom_call" | custom-call | flops 1000 | bytes 1000 | tf_op jit(solution)/shard_map/project_frames/pallas_call | solution.py:360
  81.6 1.6 %v_terms.1 = (f32[64,512]{1,0:T(8,128)S(1)}, f32[64,512]{1,0:T(8,128)S(1)}) custom-call(s32[1]{0:T(128)} %bitcast.3.core, bf16[4,192,512]{2,1,0:T(8,128)(2,1)S(1)} %get-tuple-element.42.factor_ref, bf16[512,1024]{1,0:T(8,128)(2,1)S(1)} %get-tuple-element.43.refs_0_, bf16[512,1024]{1,0:T(8,128)(2,1)S(1)} %get-tuple-element.44.refs_1_, ...), custom_call_target="tpu_custom_call" | custom-call | flops 1000 | bytes 1000 | tf_op jit(solution)/shard_map/v_terms/pallas_call | solution.py:440
  83.3 1.3 %collective-permute-done.12 = f32[64,512]{1,0:T(8,128)S(1)} collective-permute-done((f32[64,512]{1,0:T(8,128)S(1)}, f32[64,512]{1,0:T(8,128)S(1)}, u32[]{:S(2)}, u32[]{:S(2)}) %collective-permute-start.12) | collective-permute-done | bytes 131104 | tf_op jit(solution)/shard_map/ppermute | solution.py:514
  86.7 2.7 %second_inverse.1 = (f32[64,64]{1,0:T(8,128)S(1)}, f32[64,64]{1,0:T(8,128)S(1)}) custom-call(f32[64,64]{1,0:T(8,128)S(1)} %copy-done.3, f32[64,64]{1,0:T(8,128)S(1)} %get-tuple-element.38.w_gram_ref), custom_call_target="tpu_custom_call" | custom-call | flops 1000 | bytes 1000 | tf_op jit(solution)/shard_map/second_inverse/pallas_call | solution.py:414
  91.7 2.8 %next_v.1 = (f32[64,1024]{1,0:T(8,128)}, f32[64,128]{1,0:T(8,128)S(1)}) custom-call(s32[1]{0:T(128)} %bitcast.place, s32[1]{0:T(128)} %bitcast.3.core, f32[64,512]{1,0:T(8,128)S(1)} %add_terms.1.own_ref, f32[64,512]{1,0:T(8,128)S(1)} %collective-permute-done.14.other_ref, f32[64,64]{1,0:T(8,128)S(1)} %get-tuple-element.53.after_ref.inverse_ref, ...), custom_call_target="tpu_custom_call" | custom-call | flops 1000 | bytes 1000 | tf_op jit(solution)/shard_map/next_v/pallas_call | solution.py:478
  94.5 3.9 %collective-permute-done.15 = f32[64,128]{1,0:T(8,128)S(1)} collective-permute-done((f32[64,128]{1,0:T(8,128)S(1)}, f32[64,128]{1,0:T(8,128)S(1)}, u32[]{:S(2)}, u32[]{:S(2)}) %collective-permute-start.15) | collective-permute-done | bytes 32800 | tf_op jit(solution)/shard_map/ppermute | solution.py:514
  98.4 4.8 %collective-permute-done.16.refs_1_ = f32[64,128]{1,0:T(8,128)S(1)} collective-permute-done((f32[64,128]{1,0:T(8,128)S(1)}, f32[64,128]{1,0:T(8,128)S(1)}, u32[]{:S(2)}, u32[]{:S(2)}) %collective-permute-start.16) | collective-permute-done | bytes 32800 | tf_op jit(solution)/shard_map/ppermute | solution.py:514
  103.3 3.4 %next_w.1 = f32[32,64]{1,0:T(8,128)} custom-call(f32[64,128]{1,0:T(8,128)S(1)} %add.7.refs_0_, f32[64,128]{1,0:T(8,128)S(1)} %collective-permute-done.16.refs_1_, f32[64,64]{1,0:T(8,128)S(1)} %get-tuple-element.56.refs_2_), custom_call_target="tpu_custom_call" | custom-call | flops 1000 | bytes 1000 | tf_op jit(solution)/shard_map/next_w/pallas_call | solution.py:503
  (50 shorter events, 10.3 us)
Async XLA Ops:
  6.2 17.9 %copy-start.2 = (f32[32,64]{1,0:T(8,128)S(1)}, f32[32,64]{1,0:T(8,128)}, u32[]{:S(2)}) copy-start(f32[32,64]{1,0:T(8,128)} %refs_5_.1) | copy-start | bytes 24580
  6.2 24.5 %collective-permute-start = (s16[560,256]{1,0:T(8,128)(2,1)S(1)}, s16[560,256]{1,0:T(8,128)(2,1)S(1)}, u32[]{:S(2)}, u32[]{:S(2)}) collective-permute-start(s16[560,256]{1,0:T(8,128)(2,1)S(1)} %project_send.3), channel_id=1, source_target_pairs={{0,3},{1,2},{2,1},{3,0},{4,7},{5,6},{6,5},{7,4},{8,11},{9,10},{10,... | collective-permute-start | bytes 860168 | tf_op jit(solution)/shard_map/ppermute | solution.py:514
  16.9 21.6 %copy-start.4 = (f32[64,64]{1,0:T(8,128)S(1)}, f32[64,64]{1,0:T(8,128)}, u32[]{:S(2)}) copy-start(f32[64,64]{1,0:T(8,128)} %h_ref.1) | copy-start | bytes 49156
  16.9 21.6 %copy-start.5 = (s32[32]{0:T(128)S(1)}, s32[32]{0:T(128)}, u32[]{:S(2)}) copy-start(s32[32]{0:T(128)} %counts_ref.1) | copy-start | bytes 388
  16.9 40.8 %slice-start = ((s8[16777216]{0:T(1024)(128)(4,1)}), s8[4194304]{0:T(1024)(128)(4,1)S(1)}, s32[]{:S(2)}) async-start(s8[16777216]{0:T(1024)(128)(4,1)} %bitcast.9), calls=%async_computation | async-start | bytes 8388608
  16.9 40.8 %slice-start.1 = ((s8[16777216]{0:T(1024)(128)(4,1)}), s8[4194304]{0:T(1024)(128)(4,1)S(1)}, s32[]{:S(2)}) async-start(s8[16777216]{0:T(1024)(128)(4,1)} %bitcast.9), calls=%async_computation.1 | async-start | bytes 8388608
  16.9 18.9 %collective-permute-start.1 = (s16[560,256]{1,0:T(8,128)(2,1)S(1)}, s16[560,256]{1,0:T(8,128)(2,1)S(1)}, u32[]{:S(2)}, u32[]{:S(2)}) collective-permute-start(s16[560,256]{1,0:T(8,128)(2,1)S(1)} %project_send.4), channel_id=1, source_target_pairs={{0,2},{1,3},{2,0},{3,1},{4,6},{5,7},{6,4},{7,5},{8,10},{9,11},{10,... | collective-permute-start | bytes 860168 | tf_op jit(solution)/shard_map/ppermute | solution.py:514
  24.0 33.8 %slice-start.2 = ((s8[16777216]{0:T(1024)(128)(4,1)}), s8[4194304]{0:T(1024)(128)(4,1)S(1)}, s32[]{:S(2)}) async-start(s8[16777216]{0:T(1024)(128)(4,1)} %bitcast.9), calls=%async_computation.2 | async-start | bytes 8388608
  24.0 33.7 %slice-start.3 = ((s8[16777216]{0:T(1024)(128)(4,1)}), s8[4194304]{0:T(1024)(128)(4,1)S(1)}, s32[]{:S(2)}) async-start(s8[16777216]{0:T(1024)(128)(4,1)} %bitcast.9), calls=%async_computation.3 | async-start | bytes 8388608
  24.0 14.5 %collective-permute-start.2 = (s16[560,256]{1,0:T(8,128)(2,1)S(1)}, s16[560,256]{1,0:T(8,128)(2,1)S(1)}, u32[]{:S(2)}, u32[]{:S(2)}) collective-permute-start(s16[560,256]{1,0:T(8,128)(2,1)S(1)} %project_send.5), channel_id=1, source_target_pairs={{0,1},{1,0},{2,3},{3,2},{4,5},{5,4},{6,7},{7,6},{8,9},{9,8},{10,11... | collective-permute-start | bytes 860168 | tf_op jit(solution)/shard_map/ppermute | solution.py:514
  49.5 10.9 %collective-permute-start.9 = (bf16[8,64,256]{2,1,0:T(8,128)(2,1)S(1)}, bf16[8,64,256]{2,1,0:T(8,128)(2,1)S(1)}, u32[]{:S(2)}, u32[]{:S(2)}) collective-permute-start(bf16[8,64,256]{2,1,0:T(8,128)(2,1)S(1)} %get-tuple-element.34.frames_ref), channel_id=1, source_target_pairs={{0,1},{1,0},{2,3},{3,2},{4,5},{5,4},{6,7},{7,6},{8,9},{9,8},{10,11... | collective-permute-start | bytes 786440 | tf_op jit(solution)/shard_map/ppermute | solution.py:514
  49.5 22.9 %collective-permute-start.10 = (bf16[8,64,256]{2,1,0:T(8,128)(2,1)S(1)}, bf16[8,64,256]{2,1,0:T(8,128)(2,1)S(1)}, u32[]{:S(2)}, u32[]{:S(2)}) collective-permute-start(bf16[8,64,256]{2,1,0:T(8,128)(2,1)S(1)} %get-tuple-element.34.frames_ref), channel_id=1, source_target_pairs={{0,2},{1,3},{2,0},{3,1},{4,6},{5,7},{6,4},{7,5},{8,10},{9,11},{10,... | collective-permute-start | bytes 786440 | tf_op jit(solution)/shard_map/ppermute | solution.py:514
  51.0 28.1 %collective-permute-start.11 = (bf16[8,64,256]{2,1,0:T(8,128)(2,1)S(1)}, bf16[8,64,256]{2,1,0:T(8,128)(2,1)S(1)}, u32[]{:S(2)}, u32[]{:S(2)}) collective-permute-start(bf16[8,64,256]{2,1,0:T(8,128)(2,1)S(1)} %get-tuple-element.34.frames_ref), channel_id=1, source_target_pairs={{0,3},{1,2},{2,1},{3,0},{4,7},{5,6},{6,5},{7,4},{8,11},{9,10},{10,... | collective-permute-start | bytes 786440 | tf_op jit(solution)/shard_map/ppermute | solution.py:514
  53.9 3.6 %collective-permute-start.5 = (f32[64,128]{1,0:T(8,128)S(1)}, f32[64,128]{1,0:T(8,128)S(1)}, u32[]{:S(2)}, u32[]{:S(2)}) collective-permute-start(f32[64,128]{1,0:T(8,128)S(1)} %get-tuple-element.33.refs_0_), channel_id=1, source_target_pairs={{0,12},{4,8},{8,4},{12,0},{1,13},{5,9},{9,5},{13,1},{2,14},{6,10},... | collective-permute-start | bytes 98312 | tf_op jit(solution)/shard_map/ppermute | solution.py:514
  53.9 4.7 %collective-permute-start.4 = (f32[64,128]{1,0:T(8,128)S(1)}, f32[64,128]{1,0:T(8,128)S(1)}, u32[]{:S(2)}, u32[]{:S(2)}) collective-permute-start(f32[64,128]{1,0:T(8,128)S(1)} %get-tuple-element.33.refs_0_), channel_id=1, source_target_pairs={{0,8},{4,12},{8,0},{12,4},{1,9},{5,13},{9,1},{13,5},{2,10},{6,14},... | collective-permute-start | bytes 98312 | tf_op jit(solution)/shard_map/ppermute | solution.py:514
  57.6 1.2 %collective-permute-start.3 = (f32[64,128]{1,0:T(8,128)S(1)}, f32[64,128]{1,0:T(8,128)S(1)}, u32[]{:S(2)}, u32[]{:S(2)}) collective-permute-start(f32[64,128]{1,0:T(8,128)S(1)} %get-tuple-element.33.refs_0_), channel_id=1, source_target_pairs={{0,4},{4,0},{8,12},{12,8},{1,5},{5,1},{9,13},{13,9},{2,6},{6,2},{1... | collective-permute-start | bytes 98312 | tf_op jit(solution)/shard_map/ppermute | solution.py:514
  58.8 21.7 %collective-permute-start.8 = (f32[64,64]{1,0:T(8,128)S(1)}, f32[64,64]{1,0:T(8,128)S(1)}, u32[]{:S(2)}, u32[]{:S(2)}) collective-permute-start(f32[64,64]{1,0:T(8,128)S(1)} %get-tuple-element.36.refs_0_), channel_id=1, source_target_pairs={{0,3},{1,2},{2,1},{3,0},{4,7},{5,6},{6,5},{7,4},{8,11},{9,10},{10,... | collective-permute-start | bytes 49160 | tf_op jit(solution)/shard_map/ppermute | solution.py:514
  59.8 20.8 %collective-permute-start.7 = (f32[64,64]{1,0:T(8,128)S(1)}, f32[64,64]{1,0:T(8,128)S(1)}, u32[]{:S(2)}, u32[]{:S(2)}) collective-permute-start(f32[64,64]{1,0:T(8,128)S(1)} %get-tuple-element.36.refs_0_), channel_id=1, source_target_pairs={{0,2},{1,3},{2,0},{3,1},{4,6},{5,7},{6,4},{7,5},{8,10},{9,11},{10,... | collective-permute-start | bytes 49160 | tf_op jit(solution)/shard_map/ppermute | solution.py:514
  60.3 20.2 %collective-permute-start.6 = (f32[64,64]{1,0:T(8,128)S(1)}, f32[64,64]{1,0:T(8,128)S(1)}, u32[]{:S(2)}, u32[]{:S(2)}) collective-permute-start(f32[64,64]{1,0:T(8,128)S(1)} %get-tuple-element.36.refs_0_), channel_id=1, source_target_pairs={{0,1},{1,0},{2,3},{3,2},{4,5},{5,4},{6,7},{7,6},{8,9},{9,8},{10,11... | collective-permute-start | bytes 49160 | tf_op jit(solution)/shard_map/ppermute | solution.py:514
  83.2 1.4 %collective-permute-start.12 = (f32[64,512]{1,0:T(8,128)S(1)}, f32[64,512]{1,0:T(8,128)S(1)}, u32[]{:S(2)}, u32[]{:S(2)}) collective-permute-start(f32[64,512]{1,0:T(8,128)S(1)} %get-tuple-element.52), channel_id=1, source_target_pairs={{0,4},{4,0},{8,12},{12,8},{1,5},{5,1},{9,13},{13,9},{2,6},{6,2},{1... | collective-permute-start | bytes 393224 | tf_op jit(solution)/shard_map/ppermute | solution.py:514
  84.7 5.6 %collective-permute-start.13 = (f32[64,512]{1,0:T(8,128)S(1)}, f32[64,512]{1,0:T(8,128)S(1)}, u32[]{:S(2)}, u32[]{:S(2)}) collective-permute-start(f32[64,512]{1,0:T(8,128)S(1)} %add.6.a_ref), channel_id=1, source_target_pairs={{0,8},{4,12},{8,0},{12,4},{1,9},{5,13},{9,1},{13,5},{2,10},{6,14},... | collective-permute-start | bytes 393224 | tf_op jit(solution)/shard_map/ppermute | solution.py:514
  90.3 1.4 %collective-permute-start.14 = (f32[64,512]{1,0:T(8,128)S(1)}, f32[64,512]{1,0:T(8,128)S(1)}, u32[]{:S(2)}, u32[]{:S(2)}) collective-permute-start(f32[64,512]{1,0:T(8,128)S(1)} %add_terms.1.own_ref), channel_id=1, source_target_pairs={{0,4},{4,0},{8,12},{12,8},{1,5},{5,1},{9,13},{13,9},{2,6},{6,2},{1... | collective-permute-start | bytes 393224 | tf_op jit(solution)/shard_map/ppermute | solution.py:514
  94.5 3.9 %collective-permute-start.15 = (f32[64,128]{1,0:T(8,128)S(1)}, f32[64,128]{1,0:T(8,128)S(1)}, u32[]{:S(2)}, u32[]{:S(2)}) collective-permute-start(f32[64,128]{1,0:T(8,128)S(1)} %get-tuple-element.55), channel_id=1, source_target_pairs={{0,1},{1,0},{2,3},{3,2},{4,5},{5,4},{6,7},{7,6},{8,9},{9,8},{10,11... | collective-permute-start | bytes 98312 | tf_op jit(solution)/shard_map/ppermute | solution.py:514
  98.4 4.8 %collective-permute-start.16 = (f32[64,128]{1,0:T(8,128)S(1)}, f32[64,128]{1,0:T(8,128)S(1)}, u32[]{:S(2)}, u32[]{:S(2)}) collective-permute-start(f32[64,128]{1,0:T(8,128)S(1)} %add.7.refs_0_), channel_id=1, source_target_pairs={{0,2},{1,3},{2,0},{3,1},{4,6},{5,7},{6,4},{7,5},{8,10},{9,11},{10,... | collective-permute-start | bytes 98312 | tf_op jit(solution)/shard_map/ppermute | solution.py:514
  (3 other events, 12.3 us)

commit v7 on v6

--- a/solution.py
+++ b/solution.py
@@ -44,6 +44,14 @@
     return first, second, (rest - second.astype(F32)).astype(BF16)
 
 
+def feature_of(place):
+    return place[0] >> 1
+
+
+def core_of(place):
+    return place[0] & 1
+
+
 def lane_numbers(shape):
     return lax.broadcasted_iota(jnp.int32, shape, len(shape) - 1)
 
@@ -56,8 +64,7 @@
     return pltpu.CompilerParams(vmem_limit_bytes=mib * MIB)
 
 
-LIMIT = 16
-AHEAD = 2
+LIMIT = 8
 VMEM_SPEC = pl.BlockSpec(memory_space=pltpu.VMEM)
 SMEM_SPEC = pl.BlockSpec(memory_space=pltpu.SMEM)
 
@@ -77,13 +84,14 @@
 
 def patients_of(source, buffers, sems):
     count = buffers.shape[0]
-    copies = [pltpu.make_async_copy(source.at[p], buffers.at[p], sems.at[p]) for p in range(count)]
-    for copy in copies[:AHEAD]:
+    group = count // sems.shape[0]
+    rows = [pl.ds(first, group) for first in range(0, count, group)]
+    copies = [pltpu.make_async_copy(source.at[r], buffers.at[r], sems.at[i]) for i, r in enumerate(rows)]
+    for copy in copies:
         copy.start()
-    for p, copy in enumerate(copies):
-        copy.wait()
-        if p + AHEAD < count:
-            copies[p + AHEAD].start()
+    for p in range(count):
+        if p % group == 0:
+            copies[p // group].wait()
         yield buffers[p]
 
 
@@ -121,7 +129,7 @@
     v_copy.start()
     share, rank = buffers.shape[0], v_ref.shape[0]
     exponents = jnp.zeros((rank, LANES), F32)
-    for p, visits in enumerate(patients_of(visits_ref.at[place[0] ^ slot], buffers, sems)):
+    for p, visits in enumerate(patients_of(visits_ref.at[feature_of(place) ^ slot], buffers, sems)):
         if p == 0:
             v_copy.wait()
         proj = low_dot(v_ref[...], visits, ROWS_BY_ROWS)
@@ -135,7 +143,7 @@
 def own_projection_kernel(place, v_hbm, w_ref, visits_ref, proj_ref, v_gram_ref, w_gram_ref, v_ref, buffers, sems, v_sem):
     v_copy = pltpu.make_async_copy(v_hbm, v_ref, v_sem)
     v_copy.start()
-    for p, visits in enumerate(patients_of(visits_ref.at[place[0]], buffers, sems)):
+    for p, visits in enumerate(patients_of(visits_ref.at[feature_of(place)], buffers, sems)):
         if p == 0:
             v_copy.wait()
         proj_ref[p] = low_dot(v_ref[...], visits, ROWS_BY_ROWS)
@@ -147,7 +155,7 @@
     return [
         pltpu.VMEM(v_rows.shape, BF16),
         pltpu.VMEM(visits.shape[1:], BF16),
-        pltpu.SemaphoreType.DMA((visits.shape[1],)),
+        pltpu.SemaphoreType.DMA((2 if visits.shape[1] % 2 == 0 else 1,)),
         pltpu.SemaphoreType.DMA,
     ]
 
@@ -273,25 +281,27 @@
     )(*terms, after)
 
 
-def sweep_once(frames, p, rank, fine):
-    frame = frames[p]
+def sweep_all(frames, rank, fine):
+    patients = range(frames.shape[0])
     if fine:
-        both = jnp.concatenate(two_parts(frame), axis=0)
-        blocks = low_dot(both, both, ROWS_BY_ROWS)
-        blocks = blocks[:rank] + blocks[rank:]
-        gram = blocks + pltpu.roll(blocks, rank, 1)
-        moved = low_dot(jnp.concatenate(two_parts(gram), axis=0), both)
-        moved = moved[:rank] + moved[rank:]
+        both = [jnp.concatenate(two_parts(frames[p]), axis=0) for p in patients]
+        blocks = [low_dot(x, x, ROWS_BY_ROWS) for x in both]
+        blocks = [x[:rank] + x[rank:] for x in blocks]
+        grams = [x + pltpu.roll(x, rank, 1) for x in blocks]
+        moved = [low_dot(jnp.concatenate(two_parts(g), axis=0), x) for g, x in zip(grams, both)]
+        moved = [x[:rank] + x[rank:] for x in moved]
     else:
-        first = frame.astype(BF16)
-        moved = low_dot(low_dot(first, first, ROWS_BY_ROWS).astype(BF16), first)
-    frames[p] = 1.5 * frame - 0.5 * moved
+        first = [frames[p].astype(BF16) for p in patients]
+        grams = [low_dot(x, x, ROWS_BY_ROWS).astype(BF16) for x in first]
+        moved = [low_dot(g, x) for g, x in zip(grams, first)]
+    for p in patients:
+        frames[p] = 1.5 * frames[p] - 0.5 * moved[p]
 
 
 def frames_kernel(share, n_coded, place, counts_ref, h_ref, w_ref, v_gram_ref, w_gram_ref, own_ref, *refs):
     coded = refs[:n_coded]
     frames_ref, terms_ref, v_total_ref, proj, frames = refs[n_coded:]
-    first = place[0] * share
+    first = feature_of(place) * share
     rank, slots = frames.shape[1:]
     pieces = [own_ref[p] for p in range(share)]
     v_gram = v_gram_ref[...]
@@ -308,8 +318,7 @@
         frames[p] = mixed * lax.rsqrt(energy + epsilon)
 
     def sweep(fine, step, carry):
-        for p in range(share):
-            sweep_once(frames, p, rank, fine)
+        sweep_all(frames, rank, fine)
         return carry
 
     lax.fori_loop(0, COARSE_STEPS, functools.partial(sweep, False), 0)
@@ -345,7 +354,7 @@
 
 
 def projected_kernel(slot, place, frames_ref, visits_ref, first_ref, second_ref, token_ref):
-    owner = place[0] ^ slot
+    owner = feature_of(place) ^ slot
     share, rank, _ = frames_ref.shape
     token_ref[...] = jnp.zeros_like(token_ref)
     for p in range(share):
@@ -370,8 +379,9 @@
 
 
 def next_h_kernel(n_terms, n_slots, place, *refs):
-    inverse_ref, w_ref, _, h_ref, factor_ref = refs[n_terms:]
+    inverse_ref, w_ref, _, result_ref, h_ref, factor_ref = refs[n_terms:]
     h_next = high_dot(total(refs[:n_terms]), inverse_ref[...])
+    result_ref[...] = h_next
     h_ref[...] = h_next
     rank = h_next.shape[0]
     patients = w_ref.shape[0]
@@ -380,7 +390,7 @@
     w_rows = jnp.concatenate([w_ref[...], jnp.zeros((LANES - patients, rank), F32)], axis=0)
     w_columns = w_rows.T
     for slot in range(n_slots):
-        first = (place[0] ^ slot) * share
+        first = (feature_of(place) ^ slot) * share
         columns = pltpu.roll(w_columns, jnp.where(first == 0, 0, LANES - first), 1)
         factor = jnp.concatenate([h_rows * columns[:, p : p + 1] for p in range(share)], axis=1)
         factor_ref[slot] = jnp.concatenate(three_parts(factor), axis=0)
@@ -392,8 +402,9 @@
     return pl.pallas_call(
         functools.partial(next_h_kernel, len(terms), n_slots),
         in_specs=[SMEM_SPEC] + [VMEM_SPEC] * (len(terms) + 2) + [ANY_SPEC],
-        out_specs=[VMEM_SPEC] * 2,
+        out_specs=[VMEM_SPEC] * 3,
         out_shape=[
+            jax.ShapeDtypeStruct(inverse.shape, F32),
             jax.ShapeDtypeStruct(inverse.shape, F32),
             jax.ShapeDtypeStruct((n_slots, 3 * rank, share * rank), BF16),
         ],
@@ -420,7 +431,7 @@
     )(h_next, w_gram)
 
 
-def v_terms_kernel(core, factor_ref, *refs):
+def v_terms_kernel(place, factor_ref, *refs):
     *parts, keep_ref, send_ref, terms_ref = refs
     rank, width = terms_ref.shape
     half = width // 2
@@ -429,11 +440,11 @@
         small = low_dot(factor_ref[slot, : 2 * rank], parts[2 * slot + 1][...])
         terms = large[:rank] + (large[rank : 2 * rank] + small[:rank]) + (large[2 * rank :] + small[rank:])
         terms_ref[...] = terms + terms_ref[...] if slot else terms
-    keep_ref[...] = terms_ref[:, pl.ds(pl.multiple_of(core[0] * half, half), half)]
-    send_ref[...] = terms_ref[:, pl.ds(pl.multiple_of((1 - core[0]) * half, half), half)]
-
-
-def all_v_terms(core, factor, projected):
+    keep_ref[...] = terms_ref[:, pl.ds(pl.multiple_of(core_of(place) * half, half), half)]
+    send_ref[...] = terms_ref[:, pl.ds(pl.multiple_of((1 - core_of(place)) * half, half), half)]
+
+
+def all_v_terms(place, factor, projected):
     width = projected[0].shape[1]
     rank = factor.shape[1] // 3
     half = (rank, width // 2)
@@ -446,14 +457,14 @@
         compiler_params=parameters(LIMIT),
         cost_estimate=SHORT,
         name="v_terms",
-    )(core, factor, *projected)
-
-
-def next_v_kernel(n_parts, place, core, own_ref, other_ref, inverse_ref, h_ref, *refs):
+    )(place, factor, *projected)
+
+
+def next_v_kernel(n_parts, place, own_ref, other_ref, inverse_ref, h_ref, *refs):
     parts, (v_ref, sums_ref, v_parts) = refs[:n_parts], refs[n_parts:]
     rank = inverse_ref.shape[0]
     share = parts[0].shape[0] // rank
-    upper = core[0] == 1
+    upper = core_of(place) == 1
     left = jnp.where(upper, other_ref[...], own_ref[...])
     right = jnp.where(upper, own_ref[...], other_ref[...])
     v_rows = high_dot(inverse_ref[...], jnp.concatenate([left, right], axis=1))
@@ -466,18 +477,18 @@
     for slot in range(n_parts // 2):
         seen = low_dot(parts[2 * slot][...], v_parts[...], ROWS_BY_ROWS)
         seen = seen + low_dot(parts[2 * slot + 1][...], v_parts[...], ROWS_BY_ROWS)
-        first = (place[0] ^ slot) * share
+        first = (feature_of(place) ^ slot) * share
         for p in range(share):
             row = jnp.sum(seen[p * rank : (p + 1) * rank] * weights, axis=0, keepdims=True)
             sums_ref[pl.ds(first + p, 1), :rank] = row[:, :rank] + row[:, rank:]
 
 
-def next_v(place, core, own, other, inverse, h_next, projected):
+def next_v(place, own, other, inverse, h_next, projected):
     width = projected[0].shape[1]
     rank = inverse.shape[0]
     return pl.pallas_call(
         functools.partial(next_v_kernel, len(projected)),
-        in_specs=[SMEM_SPEC] * 2 + [VMEM_SPEC] * (4 + len(projected)),
+        in_specs=[SMEM_SPEC] + [VMEM_SPEC] * (4 + len(projected)),
         out_specs=[VMEM_SPEC] * 2,
         out_shape=[
             jax.ShapeDtypeStruct((rank, width), F32),
@@ -487,7 +498,7 @@
         compiler_params=parameters(LIMIT),
         cost_estimate=SHORT,
         name="next_v",
-    )(place, core, own, other, inverse, h_next, *projected)
+    )(place, own, other, inverse, h_next, *projected)
 
 
 def next_w_kernel(n_sums, *refs):
@@ -525,32 +536,32 @@
     n = lax.axis_size(axis)
     step = 1
     while 2 * step < n:
-        x = x + swap(x, axis, step)
+        x = add(x, swap(x, axis, step), [])
         step *= 2
     return [x, swap(x, axis, step)]
 
 
-def add_kernel(a_ref, b_ref, after_ref, sum_ref):
-    sum_ref[...] = a_ref[...] + b_ref[...]
+def add_kernel(a_ref, b_ref, *refs):
+    refs[-1][...] = a_ref[...] + b_ref[...]
 
 
 def add(a, b, after):
     return pl.pallas_call(
         add_kernel,
-        in_specs=[VMEM_SPEC] * 2 + [ANY_SPEC],
+        in_specs=[VMEM_SPEC] * 2 + [ANY_SPEC] * len(after),
         out_specs=VMEM_SPEC,
         out_shape=jax.ShapeDtypeStruct(a.shape, a.dtype),
         compiler_params=parameters(LIMIT),
         cost_estimate=SHORT,
         name="add_terms",
-    )(a, b, after)
+    )(a, b, *after)
 
 
 def patient_halves(keep, send, after):
-    own = keep + swap(send, "patient", 1)
+    own = add(keep, swap(send, "patient", 1), [])
     step = 2
     while step < lax.axis_size("patient"):
-        own = add(own, swap(own, "patient", step), after)
+        own = add(own, swap(own, "patient", step), [after])
         step *= 2
     return own, swap(own, "patient", 1)
 
@@ -559,8 +570,7 @@
     n = lax.axis_size("feature")
     patients, slots, width = visits.shape
     share = patients // n
-    place = lax.axis_index("feature").astype(jnp.int32).reshape(1)
-    core = lax.rem(lax.axis_index("patient").astype(jnp.int32), 2).reshape(1)
+    place = (2 * lax.axis_index("feature") + (lax.axis_index("patient") & 1)).astype(jnp.int32).reshape(1)
     by_owner = visits.reshape(n, share, slots, width)
     in_hbm = pltpu.with_memory_space_constraint(by_owner, pltpu.HBM)
     v_rows = pltpu.with_memory_space_constraint(v_start.T, pltpu.HBM)
@@ -581,15 +591,15 @@
     first = first_inverse(v_gram, w_gram, token)
     for slot in far:
         projected[slot], token = project_frames(slot, place, all_frames[slot], by_owner)
-    h_next, factor = next_h(place, h_terms, first, w_start, n, token)
+    h_result, h_next, factor = next_h(place, h_terms, first, w_start, n, token)
 
     flat = [part for slot in range(n) for part in projected[slot]]
-    keep, send = all_v_terms(core, factor, flat)
+    keep, send = all_v_terms(place, factor, flat)
     h_gram, second = second_inverse(h_next, w_gram)
     own_terms, other_terms = patient_halves(keep, send, second)
-    v_next, sums = next_v(place, core, own_terms, other_terms, second, h_next, flat)
+    v_next, sums = next_v(place, own_terms, other_terms, second, h_next, flat)
     w_next = next_w(staged_terms(sums, "feature"), h_gram, patients)
-    return (h_next, v_next.T, w_next)
+    return (h_result, v_next.T, w_next)
 
 
 def solution(mesh):

time: 107 us -> 95.6 us (0.89)
  Pallas kernels: 53.8 us -> 40.6 us
  local copies, waits for them, and re-layouts: 12.3 us -> 0.04 us
  waiting for transfers between devices: 22.9 us -> 30.6 us
  starting transfers between devices: 16.6 us -> 23.4 us
    unnamed x20 -> x14, local copies, waits for them, and re-layouts: 12.3 us -> 0.04 us
    ppermute x17, waiting for transfers between devices: 22.9 us -> 30.6 us  [swap(): return lax.ppermute(x, axis, pairs)]
    pallas_call x3, Pallas kernels: 18.1 us -> 10.8 us  [project_for(): pl.pallas_call(functools.partial(send_projection_kernel, slot), in_specs=...]
    ppermute x17, starting transfers between devices: 16.6 us -> 23.4 us  [swap(): return lax.ppermute(x, axis, pairs)]
    pallas_call x1, Pallas kernels: 10.9 us -> 7.92 us  [own_frames(): pl.pallas_call(functools.partial(frames_kernel, share, len(coded)), in_sp...]
    pallas_call x1, Pallas kernels: 6.58 us -> 3.65 us  [project_own(): pl.pallas_call(own_projection_kernel, in_specs=[SMEM_SPEC, HBM_SPEC, VMEM...]
  transfers between devices with their start and end apart: 17 -> 17, of which waited for: 10 -> 10; matrix products, arithmetic and copies ran while one was open for 0% -> 0% of each run, Pallas kernels for 27% -> 21%
where the time goes in v7:
time: 95.6 us; the launch traced here: 95.4 us
  Pallas kernels  40.6 us (42%)
  waiting for transfers between devices  30.6 us (32%)
  starting transfers between devices  23.4 us (24%)
    ppermute x17, waiting for transfers between devices, swap(): return lax.ppermute(x, axis, pairs)  30.6 us
    ppermute x17, starting transfers between devices, swap(): return lax.ppermute(x, axis, pairs)  23.4 us
    pallas_call x3, Pallas kernels, project_for(): pl.pallas_call(functools.partial(send_projection_kernel, slot), in_specs=...  10.8 us
    pallas_call x1, Pallas kernels, own_frames(): pl.pallas_call(functools.partial(frames_kernel, share, len(coded)), in_sp...  7.92 us
    pallas_call x4, Pallas kernels, project_frames(): pl.pallas_call(functools.partial(projected_kernel, slot), in_specs=[SMEM_...  4.02 us
    pallas_call x1, Pallas kernels, project_own(): pl.pallas_call(own_projection_kernel, in_specs=[SMEM_SPEC, HBM_SPEC, VMEM...  3.65 us
    pallas_call x1, Pallas kernels, next_w(): pl.pallas_call(functools.partial(next_w_kernel, len(sums)), out_shape=jax...  3.36 us
    pallas_call x1, Pallas kernels, next_v(): pl.pallas_call(functools.partial(next_v_kernel, len(projected)), in_specs...  2.77 us
  transfers between devices with their start and end apart: 17, of which 10 were waited for; matrix products, arithmetic and copies ran while one was open for 0% of the time, Pallas kernels for 21%

profile of v7, /device:TPU:0, one launch (start us, length us, event | category | flops | bytes accessed | tf_op | source)
XLA Modules:
  0.0 95.4 jit_solution(15878335030801997903)
XLA Ops:
  0.6 3.6 %project_send.3 = s16[560,256]{1,0:T(8,128)(2,1)S(1)} custom-call(s32[1]{0:T(128)} %bitcast.place, bf16[64,1024]{1,0:T(8,128)(2,1)} %bitcast.14, bf16[4,8,256,1024]{3,2,1,0:T(8,128)(2,1)} %bitcast.4), custom_call_target="tpu_custom_call" | custom-call | flops 1000 | bytes 1000 | tf_op jit(solution)/shard_map/project_send/pallas_call | solution.py:166
  4.2 5.1 %collective-permute-start = (s16[560,256]{1,0:T(8,128)(2,1)S(1)}, s16[560,256]{1,0:T(8,128)(2,1)S(1)}, u32[]{:S(2)}, u32[]{:S(2)}) collective-permute-start(s16[560,256]{1,0:T(8,128)(2,1)S(1)} %project_send.3), channel_id=1, source_target_pairs={{0,3},{1,2},{2,1},{3,0},{4,7},{5,6},{6,5},{7,4},{8,11},{9,10},{10,... | collective-permute-start | bytes 860168 | tf_op jit(solution)/shard_map/ppermute | solution.py:525
  9.3 3.6 %project_send.4 = s16[560,256]{1,0:T(8,128)(2,1)S(1)} custom-call(s32[1]{0:T(128)} %bitcast.place, bf16[64,1024]{1,0:T(8,128)(2,1)} %bitcast.15, bf16[4,8,256,1024]{3,2,1,0:T(8,128)(2,1)} %bitcast.5), custom_call_target="tpu_custom_call" | custom-call | flops 1000 | bytes 1000 | tf_op jit(solution)/shard_map/project_send/pallas_call | solution.py:166
  13.0 3.7 %project_send.5 = s16[560,256]{1,0:T(8,128)(2,1)S(1)} custom-call(s32[1]{0:T(128)} %bitcast.place, bf16[64,1024]{1,0:T(8,128)(2,1)} %bitcast.16, bf16[4,8,256,1024]{3,2,1,0:T(8,128)(2,1)} %bitcast.6), custom_call_target="tpu_custom_call" | custom-call | flops 1000 | bytes 1000 | tf_op jit(solution)/shard_map/project_send/pallas_call | solution.py:166
  17.8 3.6 %project_own.1 = (f32[8,64,256]{2,1,0:T(8,128)S(1)}, f32[64,64]{1,0:T(8,128)S(1)}, f32[64,64]{1,0:T(8,128)S(1)}) custom-call(s32[1]{0:T(128)} %bitcast.place, bf16[64,1024]{1,0:T(8,128)(2,1)} %bitcast.17, f32[32,64]{1,0:T(8,128)S(1)} %copy-done, bf16[4,8,256,1024]{3,2,1,0:T(8,128)(2,1)} %bitcast.7), custom_call_target="tpu_custom_call" | custom-call | flops 1000 | bytes 1000 | tf_op jit(solution)/shard_map/project_own/pallas_call | solution.py:182
  21.4 12.3 %collective-permute-done.1.refs_1_ = s16[560,256]{1,0:T(8,128)(2,1)S(1)} collective-permute-done((s16[560,256]{1,0:T(8,128)(2,1)S(1)}, s16[560,256]{1,0:T(8,128)(2,1)S(1)}, u32[]{:S(2)}, u32[]{:S(2)}) %collective-permute-start.1) | collective-permute-done | bytes 286752 | tf_op jit(solution)/shard_map/ppermute | solution.py:525
  33.8 7.9 %own_frames.1 = (bf16[8,64,256]{2,1,0:T(8,128)(2,1)S(1)}, f32[64,128]{1,0:T(8,128)S(1)}, f32[64,64]{1,0:T(8,128)S(1)}) custom-call(s32[1]{0:T(128)} %bitcast.place, s32[32]{0:T(128)S(1)} %copy-done.2, f32[64,64]{1,0:T(8,128)S(1)} %copy-done.1, f32[32,64]{1,0:T(8,128)S(1)} %copy-done, f32[64,64]{1,0:T(8,128)S(1)} %get-tuple-element.31.v_gram_ref, ...), custom_call_target="tpu_custom_call" | custom-call | flops 1000 | bytes 1000 | tf_op jit(solution)/shard_map/own_frames/pallas_call | solution.py:340
  41.8 3.0 %collective-permute-start.10 = (bf16[8,64,256]{2,1,0:T(8,128)(2,1)S(1)}, bf16[8,64,256]{2,1,0:T(8,128)(2,1)S(1)}, u32[]{:S(2)}, u32[]{:S(2)}) collective-permute-start(bf16[8,64,256]{2,1,0:T(8,128)(2,1)S(1)} %get-tuple-element.35.frames_ref), channel_id=1, source_target_pairs={{0,2},{1,3},{2,0},{3,1},{4,6},{5,7},{6,4},{7,5},{8,10},{9,11},{10,... | collective-permute-start | bytes 786440 | tf_op jit(solution)/shard_map/ppermute | solution.py:525
  46.1 1.5 %collective-permute-start.4 = (f32[64,128]{1,0:T(8,128)S(1)}, f32[64,128]{1,0:T(8,128)S(1)}, u32[]{:S(2)}, u32[]{:S(2)}) collective-permute-start(f32[64,128]{1,0:T(8,128)S(1)} %get-tuple-element.34.refs_0_), channel_id=1, source_target_pairs={{0,8},{4,12},{8,0},{12,4},{1,9},{5,13},{9,1},{13,5},{2,10},{6,14},... | collective-permute-start | bytes 98312 | tf_op jit(solution)/shard_map/ppermute | solution.py:525
  51.1 3.0 %collective-permute-start.7 = (f32[64,64]{1,0:T(8,128)S(1)}, f32[64,64]{1,0:T(8,128)S(1)}, u32[]{:S(2)}, u32[]{:S(2)}) collective-permute-start(f32[64,64]{1,0:T(8,128)S(1)} %get-tuple-element.37.refs_0_), channel_id=1, source_target_pairs={{0,2},{1,3},{2,0},{3,1},{4,6},{5,7},{6,4},{7,5},{8,10},{9,11},{10,... | collective-permute-start | bytes 49160 | tf_op jit(solution)/shard_map/ppermute | solution.py:525
  54.1 1.5 %collective-permute-start.8 = (f32[64,64]{1,0:T(8,128)S(1)}, f32[64,64]{1,0:T(8,128)S(1)}, u32[]{:S(2)}, u32[]{:S(2)}) collective-permute-start(f32[64,64]{1,0:T(8,128)S(1)} %get-tuple-element.37.refs_0_), channel_id=1, source_target_pairs={{0,3},{1,2},{2,1},{3,0},{4,7},{5,6},{6,5},{7,4},{8,11},{9,10},{10,... | collective-permute-start | bytes 49160 | tf_op jit(solution)/shard_map/ppermute | solution.py:525
  56.5 2.6 %first_inverse.1.refs_4_ = f32[64,64]{1,0:T(8,128)S(1)} custom-call(f32[64,64]{1,0:T(8,128)S(1)} %get-tuple-element.38.v_gram_ref, f32[64,64]{1,0:T(8,128)S(1)} %get-tuple-element.39.w_gram_ref, f32[8,128]{1,0:T(8,128)S(1)} %get-tuple-element.40.after_ref), custom_call_target="tpu_custom_call" | custom-call | flops 1000 | bytes 1000 | tf_op jit(solution)/shard_map/first_inverse/pallas_call | solution.py:252
  59.0 5.6 %collective-permute-done.10.frames_ref = bf16[8,64,256]{2,1,0:T(8,128)(2,1)S(1)} collective-permute-done((bf16[8,64,256]{2,1,0:T(8,128)(2,1)S(1)}, bf16[8,64,256]{2,1,0:T(8,128)(2,1)S(1)}, u32[]{:S(2)}, u32[]{:S(2)}) %collective-permute-start.10) | collective-permute-done | bytes 262176 | tf_op jit(solution)/shard_map/ppermute | solution.py:525
  65.5 1.4 %project_frames.7 = (bf16[512,1024]{1,0:T(8,128)(2,1)S(1)}, bf16[512,1024]{1,0:T(8,128)(2,1)S(1)}, f32[8,128]{1,0:T(8,128)}) custom-call(s32[1]{0:T(128)} %bitcast.place, bf16[8,64,256]{2,1,0:T(8,128)(2,1)S(1)} %collective-permute-done.11.frames_ref, bf16[4,8,256,1024]{3,2,1,0:T(8,128)(2,1)S(1)} %bitcast.13), custom_call_target="tpu_custom_call" | custom-call | flops 1000 | bytes 1000 | tf_op jit(solution)/shard_map/project_frames/pallas_call | solution.py:369
  66.9 2.5 %collective-permute-done.7.refs_2_ = f32[64,64]{1,0:T(8,128)S(1)} collective-permute-done((f32[64,64]{1,0:T(8,128)S(1)}, f32[64,64]{1,0:T(8,128)S(1)}, u32[]{:S(2)}, u32[]{:S(2)}) %collective-permute-start.7) | collective-permute-done | bytes 16416 | tf_op jit(solution)/shard_map/ppermute | solution.py:525
  70.4 1.6 %v_terms.1 = (f32[64,512]{1,0:T(8,128)S(1)}, f32[64,512]{1,0:T(8,128)S(1)}) custom-call(s32[1]{0:T(128)} %bitcast.place, bf16[4,192,512]{2,1,0:T(8,128)(2,1)S(1)} %get-tuple-element.43.factor_ref, bf16[512,1024]{1,0:T(8,128)(2,1)S(1)} %get-tuple-element.44.refs_0_, bf16[512,1024]{1,0:T(8,128)(2,1)S(1)} %get-tuple-element.45.refs_1_, ...), custom_call_target="tpu_custom_call" | custom-call | flops 1000 | bytes 1000 | tf_op jit(solution)/shard_map/v_terms/pallas_call | solution.py:451
  73.5 1.6 %collective-permute-start.13 = (f32[64,512]{1,0:T(8,128)S(1)}, f32[64,512]{1,0:T(8,128)S(1)}, u32[]{:S(2)}, u32[]{:S(2)}) collective-permute-start(f32[64,512]{1,0:T(8,128)S(1)} %add_terms.3.a_ref), channel_id=1, source_target_pairs={{0,8},{4,12},{8,0},{12,4},{1,9},{5,13},{9,1},{13,5},{2,10},{6,14},... | collective-permute-start | bytes 393224 | tf_op jit(solution)/shard_map/ppermute | solution.py:525
  75.0 2.7 %second_inverse.1 = (f32[64,64]{1,0:T(8,128)S(1)}, f32[64,64]{1,0:T(8,128)S(1)}) custom-call(f32[64,64]{1,0:T(8,128)S(1)} %get-tuple-element.54.h_ref, f32[64,64]{1,0:T(8,128)S(1)} %get-tuple-element.39.w_gram_ref), custom_call_target="tpu_custom_call" | custom-call | flops 1000 | bytes 1000 | tf_op jit(solution)/shard_map/second_inverse/pallas_call | solution.py:425
  80.5 2.8 %next_v.1 = (f32[64,1024]{1,0:T(8,128)}, f32[64,128]{1,0:T(8,128)S(1)}) custom-call(s32[1]{0:T(128)} %bitcast.place, f32[64,512]{1,0:T(8,128)S(1)} %add_terms.4.own_ref, f32[64,512]{1,0:T(8,128)S(1)} %collective-permute-done.14.other_ref, f32[64,64]{1,0:T(8,128)S(1)} %get-tuple-element.55.refs_0_.inverse_ref, f32[64,64]{1,0:T(8,128)S(1)} %get-tuple-element.54.h_ref, ...), custom_call_target="tpu_custom_call" | custom-call | flops 1000 | bytes 1000 | tf_op jit(solution)/shard_map/next_v/pallas_call | solution.py:489
  83.3 1.6 %collective-permute-start.15 = (f32[64,128]{1,0:T(8,128)S(1)}, f32[64,128]{1,0:T(8,128)S(1)}, u32[]{:S(2)}, u32[]{:S(2)}) collective-permute-start(f32[64,128]{1,0:T(8,128)S(1)} %get-tuple-element.57.a_ref), channel_id=1, source_target_pairs={{0,1},{1,0},{2,3},{3,2},{4,5},{5,4},{6,7},{7,6},{8,9},{9,8},{10,11... | collective-permute-start | bytes 98312 | tf_op jit(solution)/shard_map/ppermute | solution.py:525
  84.9 2.3 %collective-permute-done.15.b_ref = f32[64,128]{1,0:T(8,128)S(1)} collective-permute-done((f32[64,128]{1,0:T(8,128)S(1)}, f32[64,128]{1,0:T(8,128)S(1)}, u32[]{:S(2)}, u32[]{:S(2)}) %collective-permute-start.15) | collective-permute-done | bytes 32800 | tf_op jit(solution)/shard_map/ppermute | solution.py:525
  87.2 2.4 %collective-permute-start.16 = (f32[64,128]{1,0:T(8,128)S(1)}, f32[64,128]{1,0:T(8,128)S(1)}, u32[]{:S(2)}, u32[]{:S(2)}) collective-permute-start(f32[64,128]{1,0:T(8,128)S(1)} %add_terms.5.refs_0_), channel_id=1, source_target_pairs={{0,2},{1,3},{2,0},{3,1},{4,6},{5,7},{6,4},{7,5},{8,10},{9,11},{10,... | collective-permute-start | bytes 98312 | tf_op jit(solution)/shard_map/ppermute | solution.py:525
  89.7 2.4 %collective-permute-done.16.refs_1_ = f32[64,128]{1,0:T(8,128)S(1)} collective-permute-done((f32[64,128]{1,0:T(8,128)S(1)}, f32[64,128]{1,0:T(8,128)S(1)}, u32[]{:S(2)}, u32[]{:S(2)}) %collective-permute-start.16) | collective-permute-done | bytes 32800 | tf_op jit(solution)/shard_map/ppermute | solution.py:525
  92.1 3.4 %next_w.1 = f32[32,64]{1,0:T(8,128)} custom-call(f32[64,128]{1,0:T(8,128)S(1)} %add_terms.5.refs_0_, f32[64,128]{1,0:T(8,128)S(1)} %collective-permute-done.16.refs_1_, f32[64,64]{1,0:T(8,128)S(1)} %get-tuple-element.58.refs_2_), custom_call_target="tpu_custom_call" | custom-call | flops 1000 | bytes 1000 | tf_op jit(solution)/shard_map/next_w/pallas_call | solution.py:514
  (44 shorter events, 12.8 us)
Async XLA Ops:
  4.2 13.6 %copy-start = (f32[32,64]{1,0:T(8,128)S(1)}, f32[32,64]{1,0:T(8,128)}, u32[]{:S(2)}) copy-start(f32[32,64]{1,0:T(8,128)} %refs_5_.1) | copy-start | bytes 24580
  4.2 17.2 %collective-permute-start = (s16[560,256]{1,0:T(8,128)(2,1)S(1)}, s16[560,256]{1,0:T(8,128)(2,1)S(1)}, u32[]{:S(2)}, u32[]{:S(2)}) collective-permute-start(s16[560,256]{1,0:T(8,128)(2,1)S(1)} %project_send.3), channel_id=1, source_target_pairs={{0,3},{1,2},{2,1},{3,0},{4,7},{5,6},{6,5},{7,4},{8,11},{9,10},{10,... | collective-permute-start | bytes 860168 | tf_op jit(solution)/shard_map/ppermute | solution.py:525
  12.9 20.9 %copy-start.1 = (f32[64,64]{1,0:T(8,128)S(1)}, f32[64,64]{1,0:T(8,128)}, u32[]{:S(2)}) copy-start(f32[64,64]{1,0:T(8,128)} %h_ref.1) | copy-start | bytes 49156
  12.9 20.8 %copy-start.2 = (s32[32]{0:T(128)S(1)}, s32[32]{0:T(128)}, u32[]{:S(2)}) copy-start(s32[32]{0:T(128)} %counts_ref.1) | copy-start | bytes 388
  12.9 35.7 %slice-start = ((s8[16777216]{0:T(1024)(128)(4,1)}), s8[4194304]{0:T(1024)(128)(4,1)S(1)}, s32[]{:S(2)}) async-start(s8[16777216]{0:T(1024)(128)(4,1)} %bitcast.8), calls=%async_computation | async-start | bytes 8388608
  12.9 35.7 %slice-start.1 = ((s8[16777216]{0:T(1024)(128)(4,1)}), s8[4194304]{0:T(1024)(128)(4,1)S(1)}, s32[]{:S(2)}) async-start(s8[16777216]{0:T(1024)(128)(4,1)} %bitcast.8), calls=%async_computation.1 | async-start | bytes 8388608
  12.9 20.8 %collective-permute-start.1 = (s16[560,256]{1,0:T(8,128)(2,1)S(1)}, s16[560,256]{1,0:T(8,128)(2,1)S(1)}, u32[]{:S(2)}, u32[]{:S(2)}) collective-permute-start(s16[560,256]{1,0:T(8,128)(2,1)S(1)} %project_send.4), channel_id=1, source_target_pairs={{0,2},{1,3},{2,0},{3,1},{4,6},{5,7},{6,4},{7,5},{8,10},{9,11},{10,... | collective-permute-start | bytes 860168 | tf_op jit(solution)/shard_map/ppermute | solution.py:525
  16.7 31.9 %slice-start.2 = ((s8[16777216]{0:T(1024)(128)(4,1)}), s8[4194304]{0:T(1024)(128)(4,1)S(1)}, s32[]{:S(2)}) async-start(s8[16777216]{0:T(1024)(128)(4,1)} %bitcast.8), calls=%async_computation.2 | async-start | bytes 8388608
  16.8 31.9 %slice-start.3 = ((s8[16777216]{0:T(1024)(128)(4,1)}), s8[4194304]{0:T(1024)(128)(4,1)S(1)}, s32[]{:S(2)}) async-start(s8[16777216]{0:T(1024)(128)(4,1)} %bitcast.8), calls=%async_computation.3 | async-start | bytes 8388608
  16.8 17.0 %collective-permute-start.2 = (s16[560,256]{1,0:T(8,128)(2,1)S(1)}, s16[560,256]{1,0:T(8,128)(2,1)S(1)}, u32[]{:S(2)}, u32[]{:S(2)}) collective-permute-start(s16[560,256]{1,0:T(8,128)(2,1)S(1)} %project_send.5), channel_id=1, source_target_pairs={{0,1},{1,0},{2,3},{3,2},{4,5},{5,4},{6,7},{7,6},{8,9},{9,8},{10,11... | collective-permute-start | bytes 860168 | tf_op jit(solution)/shard_map/ppermute | solution.py:525
  41.7 12.4 %collective-permute-start.9 = (bf16[8,64,256]{2,1,0:T(8,128)(2,1)S(1)}, bf16[8,64,256]{2,1,0:T(8,128)(2,1)S(1)}, u32[]{:S(2)}, u32[]{:S(2)}) collective-permute-start(bf16[8,64,256]{2,1,0:T(8,128)(2,1)S(1)} %get-tuple-element.35.frames_ref), channel_id=1, source_target_pairs={{0,1},{1,0},{2,3},{3,2},{4,5},{5,4},{6,7},{7,6},{8,9},{9,8},{10,11... | collective-permute-start | bytes 786440 | tf_op jit(solution)/shard_map/ppermute | solution.py:525
  41.8 22.9 %collective-permute-start.10 = (bf16[8,64,256]{2,1,0:T(8,128)(2,1)S(1)}, bf16[8,64,256]{2,1,0:T(8,128)(2,1)S(1)}, u32[]{:S(2)}, u32[]{:S(2)}) collective-permute-start(bf16[8,64,256]{2,1,0:T(8,128)(2,1)S(1)} %get-tuple-element.35.frames_ref), channel_id=1, source_target_pairs={{0,2},{1,3},{2,0},{3,1},{4,6},{5,7},{6,4},{7,5},{8,10},{9,11},{10,... | collective-permute-start | bytes 786440 | tf_op jit(solution)/shard_map/ppermute | solution.py:525
  44.8 20.7 %collective-permute-start.11 = (bf16[8,64,256]{2,1,0:T(8,128)(2,1)S(1)}, bf16[8,64,256]{2,1,0:T(8,128)(2,1)S(1)}, u32[]{:S(2)}, u32[]{:S(2)}) collective-permute-start(bf16[8,64,256]{2,1,0:T(8,128)(2,1)S(1)} %get-tuple-element.35.frames_ref), channel_id=1, source_target_pairs={{0,3},{1,2},{2,1},{3,0},{4,7},{5,6},{6,5},{7,4},{8,11},{9,10},{10,... | collective-permute-start | bytes 786440 | tf_op jit(solution)/shard_map/ppermute | solution.py:525
  46.1 1.5 %collective-permute-start.3 = (f32[64,128]{1,0:T(8,128)S(1)}, f32[64,128]{1,0:T(8,128)S(1)}, u32[]{:S(2)}, u32[]{:S(2)}) collective-permute-start(f32[64,128]{1,0:T(8,128)S(1)} %get-tuple-element.34.refs_0_), channel_id=1, source_target_pairs={{0,4},{4,0},{8,12},{12,8},{1,5},{5,1},{9,13},{13,9},{2,6},{6,2},{1... | collective-permute-start | bytes 98312 | tf_op jit(solution)/shard_map/ppermute | solution.py:525
  46.1 3.9 %collective-permute-start.4 = (f32[64,128]{1,0:T(8,128)S(1)}, f32[64,128]{1,0:T(8,128)S(1)}, u32[]{:S(2)}, u32[]{:S(2)}) collective-permute-start(f32[64,128]{1,0:T(8,128)S(1)} %get-tuple-element.34.refs_0_), channel_id=1, source_target_pairs={{0,8},{4,12},{8,0},{12,4},{1,9},{5,13},{9,1},{13,5},{2,10},{6,14},... | collective-permute-start | bytes 98312 | tf_op jit(solution)/shard_map/ppermute | solution.py:525
  47.6 3.3 %collective-permute-start.5 = (f32[64,128]{1,0:T(8,128)S(1)}, f32[64,128]{1,0:T(8,128)S(1)}, u32[]{:S(2)}, u32[]{:S(2)}) collective-permute-start(f32[64,128]{1,0:T(8,128)S(1)} %get-tuple-element.34.refs_0_), channel_id=1, source_target_pairs={{0,12},{4,8},{8,4},{12,0},{1,13},{5,9},{9,5},{13,1},{2,14},{6,10},... | collective-permute-start | bytes 98312 | tf_op jit(solution)/shard_map/ppermute | solution.py:525
  51.1 15.9 %collective-permute-start.6 = (f32[64,64]{1,0:T(8,128)S(1)}, f32[64,64]{1,0:T(8,128)S(1)}, u32[]{:S(2)}, u32[]{:S(2)}) collective-permute-start(f32[64,64]{1,0:T(8,128)S(1)} %get-tuple-element.37.refs_0_), channel_id=1, source_target_pairs={{0,1},{1,0},{2,3},{3,2},{4,5},{5,4},{6,7},{7,6},{8,9},{9,8},{10,11... | collective-permute-start | bytes 49160 | tf_op jit(solution)/shard_map/ppermute | solution.py:525
  51.1 18.4 %collective-permute-start.7 = (f32[64,64]{1,0:T(8,128)S(1)}, f32[64,64]{1,0:T(8,128)S(1)}, u32[]{:S(2)}, u32[]{:S(2)}) collective-permute-start(f32[64,64]{1,0:T(8,128)S(1)} %get-tuple-element.37.refs_0_), channel_id=1, source_target_pairs={{0,2},{1,3},{2,0},{3,1},{4,6},{5,7},{6,4},{7,5},{8,10},{9,11},{10,... | collective-permute-start | bytes 49160 | tf_op jit(solution)/shard_map/ppermute | solution.py:525
  54.1 15.3 %collective-permute-start.8 = (f32[64,64]{1,0:T(8,128)S(1)}, f32[64,64]{1,0:T(8,128)S(1)}, u32[]{:S(2)}, u32[]{:S(2)}) collective-permute-start(f32[64,64]{1,0:T(8,128)S(1)} %get-tuple-element.37.refs_0_), channel_id=1, source_target_pairs={{0,3},{1,2},{2,1},{3,0},{4,7},{5,6},{6,5},{7,4},{8,11},{9,10},{10,... | collective-permute-start | bytes 49160 | tf_op jit(solution)/shard_map/ppermute | solution.py:525
  72.0 1.4 %collective-permute-start.12 = (f32[64,512]{1,0:T(8,128)S(1)}, f32[64,512]{1,0:T(8,128)S(1)}, u32[]{:S(2)}, u32[]{:S(2)}) collective-permute-start(f32[64,512]{1,0:T(8,128)S(1)} %get-tuple-element.53), channel_id=1, source_target_pairs={{0,4},{4,0},{8,12},{12,8},{1,5},{5,1},{9,13},{13,9},{2,6},{6,2},{1... | collective-permute-start | bytes 393224 | tf_op jit(solution)/shard_map/ppermute | solution.py:525
  73.5 5.6 %collective-permute-start.13 = (f32[64,512]{1,0:T(8,128)S(1)}, f32[64,512]{1,0:T(8,128)S(1)}, u32[]{:S(2)}, u32[]{:S(2)}) collective-permute-start(f32[64,512]{1,0:T(8,128)S(1)} %add_terms.3.a_ref), channel_id=1, source_target_pairs={{0,8},{4,12},{8,0},{12,4},{1,9},{5,13},{9,1},{13,5},{2,10},{6,14},... | collective-permute-start | bytes 393224 | tf_op jit(solution)/shard_map/ppermute | solution.py:525
  79.1 1.4 %collective-permute-start.14 = (f32[64,512]{1,0:T(8,128)S(1)}, f32[64,512]{1,0:T(8,128)S(1)}, u32[]{:S(2)}, u32[]{:S(2)}) collective-permute-start(f32[64,512]{1,0:T(8,128)S(1)} %add_terms.4.own_ref), channel_id=1, source_target_pairs={{0,4},{4,0},{8,12},{12,8},{1,5},{5,1},{9,13},{13,9},{2,6},{6,2},{1... | collective-permute-start | bytes 393224 | tf_op jit(solution)/shard_map/ppermute | solution.py:525
  83.3 3.9 %collective-permute-start.15 = (f32[64,128]{1,0:T(8,128)S(1)}, f32[64,128]{1,0:T(8,128)S(1)}, u32[]{:S(2)}, u32[]{:S(2)}) collective-permute-start(f32[64,128]{1,0:T(8,128)S(1)} %get-tuple-element.57.a_ref), channel_id=1, source_target_pairs={{0,1},{1,0},{2,3},{3,2},{4,5},{5,4},{6,7},{7,6},{8,9},{9,8},{10,11... | collective-permute-start | bytes 98312 | tf_op jit(solution)/shard_map/ppermute | solution.py:525
  87.2 4.8 %collective-permute-start.16 = (f32[64,128]{1,0:T(8,128)S(1)}, f32[64,128]{1,0:T(8,128)S(1)}, u32[]{:S(2)}, u32[]{:S(2)}) collective-permute-start(f32[64,128]{1,0:T(8,128)S(1)} %add_terms.5.refs_0_), channel_id=1, source_target_pairs={{0,2},{1,3},{2,0},{3,1},{4,6},{5,7},{6,4},{7,5},{8,10},{9,11},{10,... | collective-permute-start | bytes 98312 | tf_op jit(solution)/shard_map/ppermute | solution.py:525

commit v8 on v7

--- a/solution.py
+++ b/solution.py
@@ -69,12 +69,12 @@
 SMEM_SPEC = pl.BlockSpec(memory_space=pltpu.SMEM)
 
 
-def exponent_rows(share):
-    return -(-(share + 1) // 16) * 16
-
-
-def payload_shape(share, rank, slots):
-    return (share * rank + rank // 2 + exponent_rows(share), slots)
+def exponent_rows(count):
+    return -(-(count + 1) // 16) * 16
+
+
+def payload_shape(count, rank, slots, with_gram):
+    return (count * rank + (rank // 2 if with_gram else 0) + exponent_rows(count), slots)
 
 
 def row_exponent(x):
@@ -95,60 +95,74 @@
         yield buffers[p]
 
 
-def encode_rest(share, v_ref, coded_ref, exponents):
+def decode(coded_ref, count, rank, with_gram):
+    def rows(first, number):
+        return coded_ref[pl.ds(first, number), :].astype(jnp.int32).astype(F32)
+
+    gram_rows = rank // 2 if with_gram else 0
+    exponents = rows(count * rank + gram_rows, exponent_rows(count))[:, :LANES].T
+    steps = jnp.exp2(exponents[:rank]) * (1.0 / LEVELS)
+    gram = None
+    if with_gram:
+        digits = rows(count * rank, gram_rows)
+        digits = jnp.concatenate([digits[:, : 2 * rank], digits[:, 2 * rank :]], axis=0)
+        gram = (digits[:, :rank] + digits[:, rank:] * (0.5 / LEVELS)) * steps[:, count : count + 1]
+    return [rows(p * rank, rank) * steps[:, p : p + 1] for p in range(count)], gram
+
+
+def encode_gram(v_ref, coded_ref, first_row):
     rank = v_ref.shape[0]
     gram = low_dot(v_ref[...], v_ref[...], ROWS_BY_ROWS)
     exponent = row_exponent(gram)
     scaled = gram * (LEVELS / jnp.exp2(exponent))
-    first = jnp.floor(scaled + 0.5)
-    second = jnp.floor((scaled - first) * (2 * LEVELS) + 0.5)
-    digits = jnp.concatenate([first, second], axis=1)
+    whole = jnp.floor(scaled + 0.5)
+    rest = jnp.floor((scaled - whole) * (2 * LEVELS) + 0.5)
+    digits = jnp.concatenate([whole, rest], axis=1)
     digits = jnp.concatenate([digits[: rank // 2], digits[rank // 2 :]], axis=1)
-    coded_ref[pl.ds(share * rank, rank // 2), :] = digits.astype(jnp.int32).astype(jnp.int16)
-    exponents = jnp.where(lane_numbers(exponents.shape) == share, exponent, exponents)
-    rows = exponent_rows(share)
-    last = exponents.T[:rows]
-    last = jnp.concatenate([last, jnp.zeros((rows, coded_ref.shape[1] - rank), F32)], axis=1)
-    coded_ref[pl.ds(share * rank + rank // 2, rows), :] = last.astype(jnp.int32).astype(jnp.int16)
-
-
-def decode(coded_ref, share, rank):
-    def rows(first, count):
-        return coded_ref[pl.ds(first, count), :].astype(jnp.int32).astype(F32)
-
-    exponents = rows(share * rank + rank // 2, exponent_rows(share))[:, :LANES].T
-    steps = jnp.exp2(exponents[:rank]) * (1.0 / LEVELS)
-    digits = rows(share * rank, rank // 2)
-    digits = jnp.concatenate([digits[:, : 2 * rank], digits[:, 2 * rank :]], axis=0)
-    gram = (digits[:, :rank] + digits[:, rank:] * (0.5 / LEVELS)) * steps[:, share : share + 1]
-    return [rows(p * rank, rank) * steps[:, p : p + 1] for p in range(share)], gram
-
-
-def send_projection_kernel(slot, place, v_hbm, visits_ref, coded_ref, v_ref, buffers, sems, v_sem):
+    coded_ref[pl.ds(first_row, rank // 2), :] = digits.astype(jnp.int32).astype(jnp.int16)
+    return exponent
+
+
+def send_projection_kernel(slot, place, v_hbm, visits_ref, *refs):
+    *coded_refs, v_ref, buffers, sems, v_sem = refs
     v_copy = pltpu.make_async_copy(v_hbm, v_ref, v_sem)
     v_copy.start()
-    share, rank = buffers.shape[0], v_ref.shape[0]
-    exponents = jnp.zeros((rank, LANES), F32)
+    rank = v_ref.shape[0]
+    count = buffers.shape[0] // len(coded_refs)
+    lanes = lane_numbers((rank, LANES))
+    exponents = [jnp.zeros((rank, LANES), F32) for _ in coded_refs]
     for p, visits in enumerate(patients_of(visits_ref.at[feature_of(place) ^ slot], buffers, sems)):
+        part, i = divmod(p, count)
         if p == 0:
             v_copy.wait()
         proj = low_dot(v_ref[...], visits, ROWS_BY_ROWS)
         exponent = row_exponent(proj)
         coded = jnp.floor(proj * (LEVELS / jnp.exp2(exponent)) + 0.5)
-        coded_ref[pl.ds(p * rank, rank), :] = coded.astype(jnp.int32).astype(jnp.int16)
-        exponents = jnp.where(lane_numbers(exponents.shape) == p, exponent, exponents)
-    encode_rest(share, v_ref, coded_ref, exponents)
-
-
-def own_projection_kernel(place, v_hbm, w_ref, visits_ref, proj_ref, v_gram_ref, w_gram_ref, v_ref, buffers, sems, v_sem):
+        coded_refs[part][pl.ds(i * rank, rank), :] = coded.astype(jnp.int32).astype(jnp.int16)
+        exponents[part] = jnp.where(lanes == i, exponent, exponents[part])
+    for part, coded_ref in enumerate(coded_refs):
+        end = count * rank
+        if part == 0:
+            exponents[0] = jnp.where(lanes == count, encode_gram(v_ref, coded_ref, end), exponents[0])
+            end += rank // 2
+        rows = exponent_rows(count)
+        last = exponents[part].T[:rows]
+        last = jnp.concatenate([last, jnp.zeros((rows, coded_ref.shape[1] - rank), F32)], axis=1)
+        coded_ref[pl.ds(end, rows), :] = last.astype(jnp.int32).astype(jnp.int16)
+
+
+def own_projection_kernel(place, v_hbm, w_ref, visits_ref, *refs):
+    *proj_refs, v_gram_ref, w_gram_ref, v_ref, buffers, sems, v_sem = refs
     v_copy = pltpu.make_async_copy(v_hbm, v_ref, v_sem)
     v_copy.start()
+    count = buffers.shape[0] // len(proj_refs)
     for p, visits in enumerate(patients_of(visits_ref.at[feature_of(place)], buffers, sems)):
         if p == 0:
             v_copy.wait()
-        proj_ref[p] = low_dot(v_ref[...], visits, ROWS_BY_ROWS)
+        proj_refs[p // count][p % count] = low_dot(v_ref[...], visits, ROWS_BY_ROWS)
     v_gram_ref[...] = low_dot(v_ref[...], v_ref[...], ROWS_BY_ROWS)
-    w_gram_ref[...] = high_dot(w_ref[...], w_ref[...], COLS_BY_COLS)
+    w_gram = high_dot(w_ref[...], w_ref[...], COLS_BY_COLS)
+    w_gram_ref[...] = jnp.concatenate([jnp.zeros_like(w_gram), w_gram], axis=1)
 
 
 def projection_buffers(visits, v_rows):
@@ -160,14 +174,15 @@
     ]
 
 
-def project_for(slot, place, visits, v_rows):
+def project_for(slot, n_parts, place, visits, v_rows):
     _, share, slots, width = visits.shape
     rank = v_rows.shape[0]
+    shapes = [payload_shape(share // n_parts, rank, slots, part == 0) for part in range(n_parts)]
     return pl.pallas_call(
         functools.partial(send_projection_kernel, slot),
         in_specs=[SMEM_SPEC, HBM_SPEC, HBM_SPEC],
-        out_specs=VMEM_SPEC,
-        out_shape=jax.ShapeDtypeStruct(payload_shape(share, rank, slots), jnp.int16),
+        out_specs=[VMEM_SPEC] * n_parts,
+        out_shape=[jax.ShapeDtypeStruct(shape, jnp.int16) for shape in shapes],
         scratch_shapes=projection_buffers(visits, v_rows),
         compiler_params=parameters(LIMIT),
         cost_estimate=SHORT,
@@ -175,24 +190,22 @@
     )(place, v_rows, visits)
 
 
-def project_own(place, visits, v_rows, w_start):
+def project_own(n_parts, place, visits, v_rows, w_start):
     _, share, slots, width = visits.shape
     rank = v_rows.shape[0]
-    gram = (rank, rank)
-    return pl.pallas_call(
+    gram = jax.ShapeDtypeStruct((rank, rank), F32)
+    proj = jax.ShapeDtypeStruct((share // n_parts, rank, slots), F32)
+    *own, v_gram, w_gram = pl.pallas_call(
         own_projection_kernel,
         in_specs=[SMEM_SPEC, HBM_SPEC, VMEM_SPEC, HBM_SPEC],
-        out_specs=[VMEM_SPEC] * 3,
-        out_shape=[
-            jax.ShapeDtypeStruct((share, rank, slots), F32),
-            jax.ShapeDtypeStruct(gram, F32),
-            jax.ShapeDtypeStruct(gram, F32),
-        ],
+        out_specs=[VMEM_SPEC] * (n_parts + 2),
+        out_shape=[proj] * n_parts + [gram, jax.ShapeDtypeStruct((rank, 2 * rank), F32)],
         scratch_shapes=projection_buffers(visits, v_rows),
         compiler_params=parameters(LIMIT),
         cost_estimate=SHORT,
         name="project_own",
     )(place, v_rows, w_start, visits)
+    return own, v_gram, w_gram
 
 
 def pair_inverse(a, b, c, d):
@@ -298,17 +311,18 @@
         frames[p] = 1.5 * frames[p] - 0.5 * moved[p]
 
 
-def frames_kernel(share, n_coded, place, counts_ref, h_ref, w_ref, v_gram_ref, w_gram_ref, own_ref, *refs):
+def frames_kernel(part, share, n_coded, place, counts_ref, h_ref, w_ref, v_gram_ref, before_ref, own_ref, *refs):
     coded = refs[:n_coded]
     frames_ref, terms_ref, v_total_ref, proj, frames = refs[n_coded:]
-    first = feature_of(place) * share
-    rank, slots = frames.shape[1:]
-    pieces = [own_ref[p] for p in range(share)]
+    count, rank, slots = frames.shape
+    first = feature_of(place) * share + part * count
+    pieces = [own_ref[p] for p in range(count)]
     v_gram = v_gram_ref[...]
     for code in coded:
-        arrived, gram = decode(code, share, rank)
+        arrived, gram = decode(code, count, rank, part == 0)
         pieces = [a + b for a, b in zip(pieces, arrived)]
-        v_gram = v_gram + gram
+        if gram is not None:
+            v_gram = v_gram + gram
     v_total_ref[...] = v_gram
     for p, piece in enumerate(pieces):
         proj[p] = piece
@@ -323,22 +337,23 @@
 
     lax.fori_loop(0, COARSE_STEPS, functools.partial(sweep, False), 0)
     lax.fori_loop(COARSE_STEPS, NS_STEPS, functools.partial(sweep, True), 0)
-    terms = jnp.zeros((rank, rank), F32)
-    for p in range(share):
+    before = before_ref[...]
+    terms = before[:, :rank]
+    for p in range(count):
         low = frames[p].astype(BF16)
         frames_ref[p] = low
         parts = three_parts(proj[p])
         product = low_dot(low, parts[0], ROWS_BY_ROWS)
-        for part in parts[1:]:
-            product = product + low_dot(low, part, ROWS_BY_ROWS)
+        for piece in parts[1:]:
+            product = product + low_dot(low, piece, ROWS_BY_ROWS)
         terms = terms + product * w_ref[pl.ds(first + p, 1), :]
-    terms_ref[...] = jnp.concatenate([terms, w_gram_ref[...]], axis=1)
-
-
-def own_frames(place, counts, h_start, w_start, v_gram, w_gram, own, coded):
-    share, rank, slots = own.shape
-    return pl.pallas_call(
-        functools.partial(frames_kernel, share, len(coded)),
+    terms_ref[...] = jnp.concatenate([terms, before[:, rank:]], axis=1)
+
+
+def own_frames(part, n_parts, place, counts, h_start, w_start, v_gram, before, own, coded):
+    count, rank, slots = own.shape
+    return pl.pallas_call(
+        functools.partial(frames_kernel, part, count * n_parts, len(coded)),
         in_specs=[SMEM_SPEC] * 2 + [VMEM_SPEC] * (5 + len(coded)),
         out_specs=[VMEM_SPEC] * 3,
         out_shape=[
@@ -350,32 +365,35 @@
         compiler_params=parameters(LIMIT),
         cost_estimate=SHORT,
         name="own_frames",
-    )(place, counts, h_start, w_start, v_gram, w_gram, own, *coded)
-
-
-def projected_kernel(slot, place, frames_ref, visits_ref, first_ref, second_ref, token_ref):
-    owner = feature_of(place) ^ slot
-    share, rank, _ = frames_ref.shape
+    )(place, counts, h_start, w_start, v_gram, before, own, *coded)
+
+
+def projected_kernel(items, place, visits_ref, *refs):
+    frames_refs, outs, token_ref = refs[: len(items)], refs[-2 * len(items) - 1 : -1], refs[-1]
     token_ref[...] = jnp.zeros_like(token_ref)
-    for p in range(share):
-        rows = pl.ds(p * rank, rank)
-        first_ref[rows, :], second_ref[rows, :] = two_parts(low_dot(frames_ref[p], visits_ref[owner, p]))
-
-
-def project_frames(slot, place, frames, visits):
-    _, share, slots, width = visits.shape
-    rank = frames.shape[1]
-    out = jax.ShapeDtypeStruct((share * rank, width), BF16)
+    for i, (slot, part) in enumerate(items):
+        owner = feature_of(place) ^ slot
+        count, rank, _ = frames_refs[i].shape
+        for p in range(count):
+            rows = pl.ds(p * rank, rank)
+            product = low_dot(frames_refs[i][p], visits_ref[owner, part * count + p])
+            outs[2 * i][rows, :], outs[2 * i + 1][rows, :] = two_parts(product)
+
+
+def project_frames(items, place, frames, visits, after):
+    width = visits.shape[-1]
+    count, rank, _ = frames[0, 0].shape
+    out = jax.ShapeDtypeStruct((count * rank, width), BF16)
     *parts, token = pl.pallas_call(
-        functools.partial(projected_kernel, slot),
-        in_specs=[SMEM_SPEC, VMEM_SPEC, VMEM_SPEC],
-        out_specs=[VMEM_SPEC] * 3,
-        out_shape=[out, out, jax.ShapeDtypeStruct((8, LANES), F32)],
+        functools.partial(projected_kernel, items),
+        in_specs=[SMEM_SPEC] + [VMEM_SPEC] * (1 + len(items)) + [ANY_SPEC] * len(after),
+        out_specs=[VMEM_SPEC] * (2 * len(items) + 1),
+        out_shape=[out] * (2 * len(items)) + [jax.ShapeDtypeStruct((8, LANES), F32)],
         compiler_params=parameters(LIMIT),
         cost_estimate=SHORT,
         name="project_frames",
-    )(place, frames, visits)
-    return parts, token
+    )(place, visits, *[frames[item] for item in items], *after)
+    return {item: parts[2 * i : 2 * i + 2] for i, item in enumerate(items)}, token
 
 
 def next_h_kernel(n_terms, n_slots, place, *refs):
@@ -435,11 +453,15 @@
     *parts, keep_ref, send_ref, terms_ref = refs
     rank, width = terms_ref.shape
     half = width // 2
-    for slot in range(len(parts) // 2):
-        large = low_dot(factor_ref[slot], parts[2 * slot][...])
-        small = low_dot(factor_ref[slot, : 2 * rank], parts[2 * slot + 1][...])
+    n_slots, _, rows = factor_ref.shape
+    count = parts[0].shape[0]
+    for i in range(len(parts) // 2):
+        slot, first = divmod(i * count, rows)
+        columns = pl.ds(first, count)
+        large = low_dot(factor_ref[slot, :, columns], parts[2 * i][...])
+        small = low_dot(factor_ref[slot, : 2 * rank, columns], parts[2 * i + 1][...])
         terms = large[:rank] + (large[rank : 2 * rank] + small[:rank]) + (large[2 * rank :] + small[rank:])
-        terms_ref[...] = terms + terms_ref[...] if slot else terms
+        terms_ref[...] = terms + terms_ref[...] if i else terms
     keep_ref[...] = terms_ref[:, pl.ds(pl.multiple_of(core_of(place) * half, half), half)]
     send_ref[...] = terms_ref[:, pl.ds(pl.multiple_of((1 - core_of(place)) * half, half), half)]
 
@@ -460,10 +482,10 @@
     )(place, factor, *projected)
 
 
-def next_v_kernel(n_parts, place, own_ref, other_ref, inverse_ref, h_ref, *refs):
+def next_v_kernel(n_parts, share, place, own_ref, other_ref, inverse_ref, h_ref, *refs):
     parts, (v_ref, sums_ref, v_parts) = refs[:n_parts], refs[n_parts:]
     rank = inverse_ref.shape[0]
-    share = parts[0].shape[0] // rank
+    count = parts[0].shape[0] // rank
     upper = core_of(place) == 1
     left = jnp.where(upper, other_ref[...], own_ref[...])
     right = jnp.where(upper, own_ref[...], other_ref[...])
@@ -474,20 +496,21 @@
     gram = low_dot(v_parts[...], v_parts[...], ROWS_BY_ROWS)
     gram = gram[:rank, :rank] + (gram[:rank, rank:] + gram[rank:, :rank])
     sums_ref[...] = jnp.concatenate([jnp.zeros((rank, rank), F32), gram], axis=1)
-    for slot in range(n_parts // 2):
-        seen = low_dot(parts[2 * slot][...], v_parts[...], ROWS_BY_ROWS)
-        seen = seen + low_dot(parts[2 * slot + 1][...], v_parts[...], ROWS_BY_ROWS)
-        first = (feature_of(place) ^ slot) * share
-        for p in range(share):
+    for i in range(n_parts // 2):
+        seen = low_dot(parts[2 * i][...], v_parts[...], ROWS_BY_ROWS)
+        seen = seen + low_dot(parts[2 * i + 1][...], v_parts[...], ROWS_BY_ROWS)
+        slot, done = divmod(i * count, share)
+        first = (feature_of(place) ^ slot) * share + done
+        for p in range(count):
             row = jnp.sum(seen[p * rank : (p + 1) * rank] * weights, axis=0, keepdims=True)
             sums_ref[pl.ds(first + p, 1), :rank] = row[:, :rank] + row[:, rank:]
 
 
-def next_v(place, own, other, inverse, h_next, projected):
+def next_v(share, place, own, other, inverse, h_next, projected):
     width = projected[0].shape[1]
     rank = inverse.shape[0]
     return pl.pallas_call(
-        functools.partial(next_v_kernel, len(projected)),
+        functools.partial(next_v_kernel, len(projected), share),
         in_specs=[SMEM_SPEC] + [VMEM_SPEC] * (4 + len(projected)),
         out_specs=[VMEM_SPEC] * 2,
         out_shape=[
@@ -532,11 +555,11 @@
     return [x] + [swap(x, axis, s) for s in range(1, n)]
 
 
-def staged_terms(x, axis):
+def staged_terms(x, axis, after):
     n = lax.axis_size(axis)
     step = 1
     while 2 * step < n:
-        x = add(x, swap(x, axis, step), [])
+        x = add(x, swap(x, axis, step), after)
         step *= 2
     return [x, swap(x, axis, step)]
 
@@ -575,30 +598,42 @@
     in_hbm = pltpu.with_memory_space_constraint(by_owner, pltpu.HBM)
     v_rows = pltpu.with_memory_space_constraint(v_start.T, pltpu.HBM)
 
-    coded = [swap(project_for(slot, place, in_hbm, v_rows), "feature", slot) for slot in range(n - 1, 0, -1)]
-    own, v_local, w_local = project_own(place, in_hbm, v_rows, w_start)
-
-    frames, h_local, v_gram = own_frames(place, visit_counts, h_start, w_start, v_local, w_local, own, coded)
+    n_parts = 2 if share % 2 == 0 else 1
+    halves = range(n_parts)
     far = list(range(n - 1, 1, -1))
-    all_frames = {0: frames} | {slot: swap(frames, "feature", slot) for slot in far + [1]}
-    h_sums = all_terms(h_local, "patient")
-
-    parts, token = project_frames(0, place, frames, by_owner)
-    projected = {0: parts}
-    h_sum, w_gram = sum_h(h_sums, token)
+    sent = {slot: project_for(slot, n_parts, place, in_hbm, v_rows) for slot in far + [1]}
+    coded = [[swap(sent[slot][part], "feature", slot) for slot in far + [1]] for part in halves]
+    own, v_gram, h_local = project_own(n_parts, place, in_hbm, v_rows, w_start)
+    frames = {}
+    for part in halves:
+        frames[0, part], h_local, v_gram = own_frames(
+            part, n_parts, place, visit_counts, h_start, w_start, v_gram, h_local, own[part], coded[part]
+        )
+        for slot in far + [1]:
+            frames[slot, part] = swap(frames[0, part], "feature", slot)
+
+    projected, token = project_frames([(0, part) for part in halves], place, frames, by_owner, [])
+    for part in halves[:-1]:
+        more, token = project_frames([(slot, part) for slot in [1] + far], place, frames, by_owner, [token])
+        projected |= more
+    h_sum, w_gram = sum_h(staged_terms(h_local, "patient", [token]), token)
     h_terms = all_terms(h_sum, "feature")
-    projected[1], token = project_frames(1, place, all_frames[1], by_owner)
-    first = first_inverse(v_gram, w_gram, token)
-    for slot in far:
-        projected[slot], token = project_frames(slot, place, all_frames[slot], by_owner)
+    last = halves[-1]
+    after = h_sum
+    for slot in [1] + far:
+        more, token = project_frames([(slot, last)], place, frames, by_owner, [after])
+        projected |= more
+        if slot == 1:
+            first = first_inverse(v_gram, w_gram, token)
+        after = token
     h_result, h_next, factor = next_h(place, h_terms, first, w_start, n, token)
 
-    flat = [part for slot in range(n) for part in projected[slot]]
+    flat = [x for slot in range(n) for part in halves for x in projected[slot, part]]
     keep, send = all_v_terms(place, factor, flat)
     h_gram, second = second_inverse(h_next, w_gram)
     own_terms, other_terms = patient_halves(keep, send, second)
-    v_next, sums = next_v(place, own_terms, other_terms, second, h_next, flat)
-    w_next = next_w(staged_terms(sums, "feature"), h_gram, patients)
+    v_next, sums = next_v(share, place, own_terms, other_terms, second, h_next, flat)
+    w_next = next_w(all_terms(sums, "feature"), h_gram, patients)
     return (h_result, v_next.T, w_next)
 
 

time: 95.6 us -> 95.9 us (level)
  waiting for transfers between devices: 30.6 us -> 18.3 us
  starting transfers between devices: 23.4 us -> 30.5 us
  Pallas kernels: 40.6 us -> 45.9 us
    ppermute x17 -> x23, waiting for transfers between devices: 30.6 us -> 18.3 us  [swap(): return lax.ppermute(x, axis, pairs)]
    ppermute x17 -> x23, starting transfers between devices: 23.4 us -> 30.5 us  [swap(): return lax.ppermute(x, axis, pairs)]
    pallas_call x6 -> x8, Pallas kernels: 14.7 us -> 20 us  [the longest x2 13.1 us: own_frames(): pl.pallas_call(functools.partial(frames_kernel, part, count * n_parts, le...]
  transfers between devices with their start and end apart: 17 -> 23, of which waited for: 10 -> 9; matrix products, arithmetic and copies ran while one was open for 0% -> 0% of each run, Pallas kernels for 21% -> 35%
where the time goes in v8:
time: 95.9 us; the launch traced here: 95.7 us
  Pallas kernels  45.9 us (48%)
  starting transfers between devices  30.5 us (32%)
  waiting for transfers between devices  18.3 us (19%)
    ppermute x23, starting transfers between devices, swap(): return lax.ppermute(x, axis, pairs)  30.5 us
    ppermute x23, waiting for transfers between devices, swap(): return lax.ppermute(x, axis, pairs)  18.3 us
    pallas_call x2, Pallas kernels, own_frames(): pl.pallas_call(functools.partial(frames_kernel, part, count * n_parts, le...  13.1 us
    pallas_call x3, Pallas kernels, project_for(): pl.pallas_call(functools.partial(send_projection_kernel, slot), in_specs=...  10.8 us
    pallas_call x1, Pallas kernels, project_own(): pl.pallas_call(own_projection_kernel, in_specs=[SMEM_SPEC, HBM_SPEC, VMEM...  3.83 us
    pallas_call x5, Pallas kernels, project_frames(): pl.pallas_call(functools.partial(projected_kernel, items), in_specs=[SMEM...  3.63 us
    pallas_call x1, Pallas kernels, next_w(): pl.pallas_call(functools.partial(next_w_kernel, len(sums)), out_shape=jax...  3.36 us
    pallas_call x1, Pallas kernels, next_v(): pl.pallas_call(functools.partial(next_v_kernel, len(projected), share), i...  3.23 us
  transfers between devices with their start and end apart: 23, of which 9 were waited for; matrix products, arithmetic and copies ran while one was open for 0% of the time, Pallas kernels for 35%

profile of v8, /device:TPU:0, one launch (start us, length us, event | category | flops | bytes accessed | tf_op | source)
XLA Modules:
  0.0 95.7 jit_solution(15102087601785699581)
XLA Ops:
  0.6 3.6 %project_send.3 = (s16[304,256]{1,0:T(8,128)(2,1)S(1)}, s16[272,256]{1,0:T(8,128)(2,1)S(1)}) custom-call(s32[1]{0:T(128)} %bitcast.place, bf16[64,1024]{1,0:T(8,128)(2,1)} %bitcast.15, bf16[4,8,256,1024]{3,2,1,0:T(8,128)(2,1)} %bitcast.4), custom_call_target="tpu_custom_call" | custom-call | flops 1000 | bytes 1000 | tf_op jit(solution)/shard_map/project_send/pallas_call | solution.py:181
  4.2 5.1 %collective-permute-start = (s16[304,256]{1,0:T(8,128)(2,1)S(1)}, s16[304,256]{1,0:T(8,128)(2,1)S(1)}, u32[]{:S(2)}, u32[]{:S(2)}) collective-permute-start(s16[304,256]{1,0:T(8,128)(2,1)S(1)} %get-tuple-element.54), channel_id=1, source_target_pairs={{0,3},{1,2},{2,1},{3,0},{4,7},{5,6},{6,5},{7,4},{8,11},{9,10},{10,... | collective-permute-start | bytes 466952 | tf_op jit(solution)/shard_map/ppermute | solution.py:548
  9.3 3.6 %project_send.4 = (s16[304,256]{1,0:T(8,128)(2,1)S(1)}, s16[272,256]{1,0:T(8,128)(2,1)S(1)}) custom-call(s32[1]{0:T(128)} %bitcast.place, bf16[64,1024]{1,0:T(8,128)(2,1)} %bitcast.16, bf16[4,8,256,1024]{3,2,1,0:T(8,128)(2,1)} %bitcast.5), custom_call_target="tpu_custom_call" | custom-call | flops 1000 | bytes 1000 | tf_op jit(solution)/shard_map/project_send/pallas_call | solution.py:181
  13.0 3.7 %project_send.5 = (s16[304,256]{1,0:T(8,128)(2,1)S(1)}, s16[272,256]{1,0:T(8,128)(2,1)S(1)}) custom-call(s32[1]{0:T(128)} %bitcast.place, bf16[64,1024]{1,0:T(8,128)(2,1)} %bitcast.17, bf16[4,8,256,1024]{3,2,1,0:T(8,128)(2,1)} %bitcast.6), custom_call_target="tpu_custom_call" | custom-call | flops 1000 | bytes 1000 | tf_op jit(solution)/shard_map/project_send/pallas_call | solution.py:181
  17.8 3.3 %collective-permute-start.3 = (s16[272,256]{1,0:T(8,128)(2,1)S(1)}, s16[272,256]{1,0:T(8,128)(2,1)S(1)}, u32[]{:S(2)}, u32[]{:S(2)}) collective-permute-start(s16[272,256]{1,0:T(8,128)(2,1)S(1)} %get-tuple-element.60), channel_id=1, source_target_pairs={{0,3},{1,2},{2,1},{3,0},{4,7},{5,6},{6,5},{7,4},{8,11},{9,10},{10,... | collective-permute-start | bytes 417800 | tf_op jit(solution)/shard_map/ppermute | solution.py:548
  22.2 3.8 %project_own.1 = (f32[4,64,256]{2,1,0:T(8,128)S(1)}, f32[4,64,256]{2,1,0:T(8,128)S(1)}, f32[64,64]{1,0:T(8,128)S(1)}, f32[64,128]{1,0:T(8,128)S(1)}) custom-call(s32[1]{0:T(128)} %bitcast.place, bf16[64,1024]{1,0:T(8,128)(2,1)} %bitcast.18, f32[32,64]{1,0:T(8,128)S(1)} %copy-done, bf16[4,8,256,1024]{3,2,1,0:T(8,128)(2,1)} %bitcast.7), custom_call_target="tpu_custom_call" | custom-call | flops 1000 | bytes 1000 | tf_op jit(solution)/shard_map/project_own/pallas_call | solution.py:198
  26.0 3.0 %collective-permute-done.2.refs_2_ = s16[304,256]{1,0:T(8,128)(2,1)S(1)} collective-permute-done((s16[304,256]{1,0:T(8,128)(2,1)S(1)}, s16[304,256]{1,0:T(8,128)(2,1)S(1)}, u32[]{:S(2)}, u32[]{:S(2)}) %collective-permute-start.2) | collective-permute-done | bytes 155680 | tf_op jit(solution)/shard_map/ppermute | solution.py:548
  29.0 6.5 %own_frames.2 = (bf16[4,64,256]{2,1,0:T(8,128)(2,1)S(1)}, f32[64,128]{1,0:T(8,128)S(1)}, f32[64,64]{1,0:T(8,128)S(1)}) custom-call(s32[1]{0:T(128)} %bitcast.place, s32[32]{0:T(128)S(1)} %copy-done.2, f32[64,64]{1,0:T(8,128)S(1)} %copy-done.1, f32[32,64]{1,0:T(8,128)S(1)} %copy-done, f32[64,64]{1,0:T(8,128)S(1)} %get-tuple-element.51.v_gram_ref, ...), custom_call_target="tpu_custom_call" | custom-call | flops 1000 | bytes 1000 | tf_op jit(solution)/shard_map/own_frames/pallas_call | solution.py:355
  35.5 2.9 %collective-permute-start.8 = (bf16[4,64,256]{2,1,0:T(8,128)(2,1)S(1)}, bf16[4,64,256]{2,1,0:T(8,128)(2,1)S(1)}, u32[]{:S(2)}, u32[]{:S(2)}) collective-permute-start(bf16[4,64,256]{2,1,0:T(8,128)(2,1)S(1)} %get-tuple-element.64.refs_0_), channel_id=1, source_target_pairs={{0,3},{1,2},{2,1},{3,0},{4,7},{5,6},{6,5},{7,4},{8,11},{9,10},{10,... | collective-permute-start | bytes 393224 | tf_op jit(solution)/shard_map/ppermute | solution.py:548
  39.0 6.6 %own_frames.3 = (bf16[4,64,256]{2,1,0:T(8,128)(2,1)S(1)}, f32[64,128]{1,0:T(8,128)S(1)}, f32[64,64]{1,0:T(8,128)S(1)}) custom-call(s32[1]{0:T(128)} %bitcast.place, s32[32]{0:T(128)S(1)} %copy-done.2, f32[64,64]{1,0:T(8,128)S(1)} %copy-done.1, f32[32,64]{1,0:T(8,128)S(1)} %copy-done, f32[64,64]{1,0:T(8,128)S(1)} %get-tuple-element.57.v_gram_ref, ...), custom_call_target="tpu_custom_call" | custom-call | flops 1000 | bytes 1000 | tf_op jit(solution)/shard_map/own_frames/pallas_call | solution.py:355
  46.7 2.9 %collective-permute-start.16 = (bf16[4,64,256]{2,1,0:T(8,128)(2,1)S(1)}, bf16[4,64,256]{2,1,0:T(8,128)(2,1)S(1)}, u32[]{:S(2)}, u32[]{:S(2)}) collective-permute-start(bf16[4,64,256]{2,1,0:T(8,128)(2,1)S(1)} %get-tuple-element.65.refs_1_), channel_id=1, source_target_pairs={{0,3},{1,2},{2,1},{3,0},{4,7},{5,6},{6,5},{7,4},{8,11},{9,10},{10,... | collective-permute-start | bytes 393224 | tf_op jit(solution)/shard_map/ppermute | solution.py:548
  50.6 1.6 %collective-permute-done.9.refs_2_ = bf16[4,64,256]{2,1,0:T(8,128)(2,1)S(1)} collective-permute-done((bf16[4,64,256]{2,1,0:T(8,128)(2,1)S(1)}, bf16[4,64,256]{2,1,0:T(8,128)(2,1)S(1)}, u32[]{:S(2)}, u32[]{:S(2)}) %collective-permute-start.9) | collective-permute-done | bytes 131104 | tf_op jit(solution)/shard_map/ppermute | solution.py:548
  53.5 1.6 %collective-permute-start.10 = (f32[64,128]{1,0:T(8,128)S(1)}, f32[64,128]{1,0:T(8,128)S(1)}, u32[]{:S(2)}, u32[]{:S(2)}) collective-permute-start(f32[64,128]{1,0:T(8,128)S(1)} %add_terms.3.refs_0_), channel_id=1, source_target_pairs={{0,8},{4,12},{8,0},{12,4},{1,9},{5,13},{9,1},{13,5},{2,10},{6,14},... | collective-permute-start | bytes 98312 | tf_op jit(solution)/shard_map/ppermute | solution.py:548
  55.0 2.4 %collective-permute-done.10.refs_1_ = f32[64,128]{1,0:T(8,128)S(1)} collective-permute-done((f32[64,128]{1,0:T(8,128)S(1)}, f32[64,128]{1,0:T(8,128)S(1)}, u32[]{:S(2)}, u32[]{:S(2)}) %collective-permute-start.10) | collective-permute-done | bytes 32800 | tf_op jit(solution)/shard_map/ppermute | solution.py:548
  57.7 6.2 %collective-permute-start.12 = (f32[64,64]{1,0:T(8,128)S(1)}, f32[64,64]{1,0:T(8,128)S(1)}, u32[]{:S(2)}, u32[]{:S(2)}) collective-permute-start(f32[64,64]{1,0:T(8,128)S(1)} %get-tuple-element.68.refs_1_.refs_0_), channel_id=1, source_target_pairs={{0,2},{1,3},{2,0},{3,1},{4,6},{5,7},{6,4},{7,5},{8,10},{9,11},{10,... | collective-permute-start | bytes 49160 | tf_op jit(solution)/shard_map/ppermute | solution.py:548
  64.3 2.6 %first_inverse.1.refs_4_ = f32[64,64]{1,0:T(8,128)S(1)} custom-call(f32[64,64]{1,0:T(8,128)S(1)} %get-tuple-element.69.v_gram_ref, f32[64,64]{1,0:T(8,128)S(1)} %get-tuple-element.70.w_gram_ref, f32[8,128]{1,0:T(8,128)S(1)} %get-tuple-element.71.after_ref.refs_1_), custom_call_target="tpu_custom_call" | custom-call | flops 1000 | bytes 1000 | tf_op jit(solution)/shard_map/first_inverse/pallas_call | solution.py:265
  68.0 1.6 %collective-permute-done.13.refs_3_ = f32[64,64]{1,0:T(8,128)S(1)} collective-permute-done((f32[64,64]{1,0:T(8,128)S(1)}, f32[64,64]{1,0:T(8,128)S(1)}, u32[]{:S(2)}, u32[]{:S(2)}) %collective-permute-start.13) | collective-permute-done | bytes 16416 | tf_op jit(solution)/shard_map/ppermute | solution.py:548
  70.5 1.6 %v_terms.1 = (f32[64,512]{1,0:T(8,128)S(1)}, f32[64,512]{1,0:T(8,128)S(1)}) custom-call(s32[1]{0:T(128)} %bitcast.place, bf16[4,192,512]{2,1,0:T(8,128)(2,1)S(1)} %get-tuple-element.75.factor_ref, bf16[256,1024]{1,0:T(8,128)(2,1)S(1)} %get-tuple-element.76.refs_0_, bf16[256,1024]{1,0:T(8,128)(2,1)S(1)} %get-tuple-element.77.refs_1_, ...), custom_call_target="tpu_custom_call" | custom-call | flops 1000 | bytes 1000 | tf_op jit(solution)/shard_map/v_terms/pallas_call | solution.py:473
  73.6 2.7 %second_inverse.1 = (f32[64,64]{1,0:T(8,128)S(1)}, f32[64,64]{1,0:T(8,128)S(1)}) custom-call(f32[64,64]{1,0:T(8,128)S(1)} %get-tuple-element.94.h_ref, f32[64,64]{1,0:T(8,128)S(1)} %get-tuple-element.70.w_gram_ref), custom_call_target="tpu_custom_call" | custom-call | flops 1000 | bytes 1000 | tf_op jit(solution)/shard_map/second_inverse/pallas_call | solution.py:443
  76.3 2.8 %collective-permute-done.18.b_ref = f32[64,512]{1,0:T(8,128)S(1)} collective-permute-done((f32[64,512]{1,0:T(8,128)S(1)}, f32[64,512]{1,0:T(8,128)S(1)}, u32[]{:S(2)}, u32[]{:S(2)}) %collective-permute-start.18) | collective-permute-done | bytes 131104 | tf_op jit(solution)/shard_map/ppermute | solution.py:548
  80.6 3.2 %next_v.1 = (f32[64,1024]{1,0:T(8,128)}, f32[64,128]{1,0:T(8,128)S(1)}) custom-call(s32[1]{0:T(128)} %bitcast.place, f32[64,512]{1,0:T(8,128)S(1)} %add_terms.5.own_ref, f32[64,512]{1,0:T(8,128)S(1)} %collective-permute-done.19.other_ref, f32[64,64]{1,0:T(8,128)S(1)} %get-tuple-element.95.refs_0_.inverse_ref, f32[64,64]{1,0:T(8,128)S(1)} %get-tuple-element.94.h_ref, ...), custom_call_target="tpu_custom_call" | custom-call | flops 1000 | bytes 1000 | tf_op jit(solution)/shard_map/next_v/pallas_call | solution.py:512
  83.8 2.8 %collective-permute-start.21 = (f32[64,128]{1,0:T(8,128)S(1)}, f32[64,128]{1,0:T(8,128)S(1)}, u32[]{:S(2)}, u32[]{:S(2)}) collective-permute-start(f32[64,128]{1,0:T(8,128)S(1)} %get-tuple-element.97.refs_0_), channel_id=1, source_target_pairs={{0,2},{1,3},{2,0},{3,1},{4,6},{5,7},{6,4},{7,5},{8,10},{9,11},{10,... | collective-permute-start | bytes 98312 | tf_op jit(solution)/shard_map/ppermute | solution.py:548
  88.7 3.6 %collective-permute-done.22.refs_3_ = f32[64,128]{1,0:T(8,128)S(1)} collective-permute-done((f32[64,128]{1,0:T(8,128)S(1)}, f32[64,128]{1,0:T(8,128)S(1)}, u32[]{:S(2)}, u32[]{:S(2)}) %collective-permute-start.22) | collective-permute-done | bytes 32800 | tf_op jit(solution)/shard_map/ppermute | solution.py:548
  92.4 3.4 %next_w.1 = f32[32,64]{1,0:T(8,128)} custom-call(f32[64,128]{1,0:T(8,128)S(1)} %get-tuple-element.97.refs_0_, f32[64,128]{1,0:T(8,128)S(1)} %collective-permute-done.20.refs_1_, f32[64,128]{1,0:T(8,128)S(1)} %collective-permute-done.21.refs_2_, f32[64,128]{1,0:T(8,128)S(1)} %collective-permute-done.22.refs_3_, f32[64,64]{1,0:T(8,128)S(1)} %get-tuple-element.98.refs_4_), custom_call_target="tpu_custom_call" | custom-call | flops 1000 | bytes 1000 | tf_op jit(solution)/shard_map/next_w/pallas_call | solution.py:537
  (58 shorter events, 13.8 us)
Async XLA Ops:
  4.2 16.8 %collective-permute-start = (s16[304,256]{1,0:T(8,128)(2,1)S(1)}, s16[304,256]{1,0:T(8,128)(2,1)S(1)}, u32[]{:S(2)}, u32[]{:S(2)}) collective-permute-start(s16[304,256]{1,0:T(8,128)(2,1)S(1)} %get-tuple-element.54), channel_id=1, source_target_pairs={{0,3},{1,2},{2,1},{3,0},{4,7},{5,6},{6,5},{7,4},{8,11},{9,10},{10,... | collective-permute-start | bytes 466952 | tf_op jit(solution)/shard_map/ppermute | solution.py:548
  12.9 36.7 %slice-start = ((s8[16777216]{0:T(1024)(128)(4,1)}), s8[4194304]{0:T(1024)(128)(4,1)S(1)}, s32[]{:S(2)}) async-start(s8[16777216]{0:T(1024)(128)(4,1)} %bitcast.8), calls=%async_computation | async-start | bytes 8388608
  12.9 13.0 %collective-permute-start.1 = (s16[304,256]{1,0:T(8,128)(2,1)S(1)}, s16[304,256]{1,0:T(8,128)(2,1)S(1)}, u32[]{:S(2)}, u32[]{:S(2)}) collective-permute-start(s16[304,256]{1,0:T(8,128)(2,1)S(1)} %get-tuple-element.55), channel_id=1, source_target_pairs={{0,2},{1,3},{2,0},{3,1},{4,6},{5,7},{6,4},{7,5},{8,10},{9,11},{10,... | collective-permute-start | bytes 466952 | tf_op jit(solution)/shard_map/ppermute | solution.py:548
  16.7 12.2 %collective-permute-start.2 = (s16[304,256]{1,0:T(8,128)(2,1)S(1)}, s16[304,256]{1,0:T(8,128)(2,1)S(1)}, u32[]{:S(2)}, u32[]{:S(2)}) collective-permute-start(s16[304,256]{1,0:T(8,128)(2,1)S(1)} %get-tuple-element.56), channel_id=1, source_target_pairs={{0,1},{1,0},{2,3},{3,2},{4,5},{5,4},{6,7},{7,6},{8,9},{9,8},{10,11... | collective-permute-start | bytes 466952 | tf_op jit(solution)/shard_map/ppermute | solution.py:548
  17.8 20.7 %collective-permute-start.3 = (s16[272,256]{1,0:T(8,128)(2,1)S(1)}, s16[272,256]{1,0:T(8,128)(2,1)S(1)}, u32[]{:S(2)}, u32[]{:S(2)}) collective-permute-start(s16[272,256]{1,0:T(8,128)(2,1)S(1)} %get-tuple-element.60), channel_id=1, source_target_pairs={{0,3},{1,2},{2,1},{3,0},{4,7},{5,6},{6,5},{7,4},{8,11},{9,10},{10,... | collective-permute-start | bytes 417800 | tf_op jit(solution)/shard_map/ppermute | solution.py:548
  21.0 18.0 %collective-permute-start.4 = (s16[272,256]{1,0:T(8,128)(2,1)S(1)}, s16[272,256]{1,0:T(8,128)(2,1)S(1)}, u32[]{:S(2)}, u32[]{:S(2)}) collective-permute-start(s16[272,256]{1,0:T(8,128)(2,1)S(1)} %get-tuple-element.61), channel_id=1, source_target_pairs={{0,2},{1,3},{2,0},{3,1},{4,6},{5,7},{6,4},{7,5},{8,10},{9,11},{10,... | collective-permute-start | bytes 417800 | tf_op jit(solution)/shard_map/ppermute | solution.py:548
  21.1 18.0 %collective-permute-start.5 = (s16[272,256]{1,0:T(8,128)(2,1)S(1)}, s16[272,256]{1,0:T(8,128)(2,1)S(1)}, u32[]{:S(2)}, u32[]{:S(2)}) collective-permute-start(s16[272,256]{1,0:T(8,128)(2,1)S(1)} %get-tuple-element.62), channel_id=1, source_target_pairs={{0,1},{1,0},{2,3},{3,2},{4,5},{5,4},{6,7},{7,6},{8,9},{9,8},{10,11... | collective-permute-start | bytes 417800 | tf_op jit(solution)/shard_map/ppermute | solution.py:548
  35.5 14.1 %collective-permute-start.7 = (bf16[4,64,256]{2,1,0:T(8,128)(2,1)S(1)}, bf16[4,64,256]{2,1,0:T(8,128)(2,1)S(1)}, u32[]{:S(2)}, u32[]{:S(2)}) collective-permute-start(bf16[4,64,256]{2,1,0:T(8,128)(2,1)S(1)} %get-tuple-element.64.refs_0_), channel_id=1, source_target_pairs={{0,1},{1,0},{2,3},{3,2},{4,5},{5,4},{6,7},{7,6},{8,9},{9,8},{10,11... | collective-permute-start | bytes 393224 | tf_op jit(solution)/shard_map/ppermute | solution.py:548
  35.5 14.0 %collective-permute-start.8 = (bf16[4,64,256]{2,1,0:T(8,128)(2,1)S(1)}, bf16[4,64,256]{2,1,0:T(8,128)(2,1)S(1)}, u32[]{:S(2)}, u32[]{:S(2)}) collective-permute-start(bf16[4,64,256]{2,1,0:T(8,128)(2,1)S(1)} %get-tuple-element.64.refs_0_), channel_id=1, source_target_pairs={{0,3},{1,2},{2,1},{3,0},{4,7},{5,6},{6,5},{7,4},{8,11},{9,10},{10,... | collective-permute-start | bytes 393224 | tf_op jit(solution)/shard_map/ppermute | solution.py:548
  38.5 13.7 %collective-permute-start.9 = (bf16[4,64,256]{2,1,0:T(8,128)(2,1)S(1)}, bf16[4,64,256]{2,1,0:T(8,128)(2,1)S(1)}, u32[]{:S(2)}, u32[]{:S(2)}) collective-permute-start(bf16[4,64,256]{2,1,0:T(8,128)(2,1)S(1)} %get-tuple-element.64.refs_0_), channel_id=1, source_target_pairs={{0,2},{1,3},{2,0},{3,1},{4,6},{5,7},{6,4},{7,5},{8,10},{9,11},{10,... | collective-permute-start | bytes 393224 | tf_op jit(solution)/shard_map/ppermute | solution.py:548
  45.7 18.2 %collective-permute-start.14 = (bf16[4,64,256]{2,1,0:T(8,128)(2,1)S(1)}, bf16[4,64,256]{2,1,0:T(8,128)(2,1)S(1)}, u32[]{:S(2)}, u32[]{:S(2)}) collective-permute-start(bf16[4,64,256]{2,1,0:T(8,128)(2,1)S(1)} %get-tuple-element.65.refs_1_), channel_id=1, source_target_pairs={{0,1},{1,0},{2,3},{3,2},{4,5},{5,4},{6,7},{7,6},{8,9},{9,8},{10,11... | collective-permute-start | bytes 393224 | tf_op jit(solution)/shard_map/ppermute | solution.py:548
  46.7 20.2 %collective-permute-start.16 = (bf16[4,64,256]{2,1,0:T(8,128)(2,1)S(1)}, bf16[4,64,256]{2,1,0:T(8,128)(2,1)S(1)}, u32[]{:S(2)}, u32[]{:S(2)}) collective-permute-start(bf16[4,64,256]{2,1,0:T(8,128)(2,1)S(1)} %get-tuple-element.65.refs_1_), channel_id=1, source_target_pairs={{0,3},{1,2},{2,1},{3,0},{4,7},{5,6},{6,5},{7,4},{8,11},{9,10},{10,... | collective-permute-start | bytes 393224 | tf_op jit(solution)/shard_map/ppermute | solution.py:548
  49.6 17.9 %collective-permute-start.15 = (bf16[4,64,256]{2,1,0:T(8,128)(2,1)S(1)}, bf16[4,64,256]{2,1,0:T(8,128)(2,1)S(1)}, u32[]{:S(2)}, u32[]{:S(2)}) collective-permute-start(bf16[4,64,256]{2,1,0:T(8,128)(2,1)S(1)} %get-tuple-element.65.refs_1_), channel_id=1, source_target_pairs={{0,2},{1,3},{2,0},{3,1},{4,6},{5,7},{6,4},{7,5},{8,10},{9,11},{10,... | collective-permute-start | bytes 393224 | tf_op jit(solution)/shard_map/ppermute | solution.py:548
  49.6 3.9 %collective-permute-start.6 = (f32[64,128]{1,0:T(8,128)S(1)}, f32[64,128]{1,0:T(8,128)S(1)}, u32[]{:S(2)}, u32[]{:S(2)}) collective-permute-start(f32[64,128]{1,0:T(8,128)S(1)} %get-tuple-element.63.a_ref), channel_id=1, source_target_pairs={{0,4},{4,0},{8,12},{12,8},{1,5},{5,1},{9,13},{13,9},{2,6},{6,2},{1... | collective-permute-start | bytes 98312 | tf_op jit(solution)/shard_map/ppermute | solution.py:548
  53.5 4.0 %collective-permute-start.10 = (f32[64,128]{1,0:T(8,128)S(1)}, f32[64,128]{1,0:T(8,128)S(1)}, u32[]{:S(2)}, u32[]{:S(2)}) collective-permute-start(f32[64,128]{1,0:T(8,128)S(1)} %add_terms.3.refs_0_), channel_id=1, source_target_pairs={{0,8},{4,12},{8,0},{12,4},{1,9},{5,13},{9,1},{13,5},{2,10},{6,14},... | collective-permute-start | bytes 98312 | tf_op jit(solution)/shard_map/ppermute | solution.py:548
  57.5 10.4 %collective-permute-start.11 = (f32[64,64]{1,0:T(8,128)S(1)}, f32[64,64]{1,0:T(8,128)S(1)}, u32[]{:S(2)}, u32[]{:S(2)}) collective-permute-start(f32[64,64]{1,0:T(8,128)S(1)} %get-tuple-element.68.refs_1_.refs_0_), channel_id=1, source_target_pairs={{0,1},{1,0},{2,3},{3,2},{4,5},{5,4},{6,7},{7,6},{8,9},{9,8},{10,11... | collective-permute-start | bytes 49160 | tf_op jit(solution)/shard_map/ppermute | solution.py:548
  57.7 10.3 %collective-permute-start.12 = (f32[64,64]{1,0:T(8,128)S(1)}, f32[64,64]{1,0:T(8,128)S(1)}, u32[]{:S(2)}, u32[]{:S(2)}) collective-permute-start(f32[64,64]{1,0:T(8,128)S(1)} %get-tuple-element.68.refs_1_.refs_0_), channel_id=1, source_target_pairs={{0,2},{1,3},{2,0},{3,1},{4,6},{5,7},{6,4},{7,5},{8,10},{9,11},{10,... | collective-permute-start | bytes 49160 | tf_op jit(solution)/shard_map/ppermute | solution.py:548
  63.8 5.7 %collective-permute-start.13 = (f32[64,64]{1,0:T(8,128)S(1)}, f32[64,64]{1,0:T(8,128)S(1)}, u32[]{:S(2)}, u32[]{:S(2)}) collective-permute-start(f32[64,64]{1,0:T(8,128)S(1)} %get-tuple-element.68.refs_1_.refs_0_), channel_id=1, source_target_pairs={{0,3},{1,2},{2,1},{3,0},{4,7},{5,6},{6,5},{7,4},{8,11},{9,10},{10,... | collective-permute-start | bytes 49160 | tf_op jit(solution)/shard_map/ppermute | solution.py:548
  72.1 1.4 %collective-permute-start.17 = (f32[64,512]{1,0:T(8,128)S(1)}, f32[64,512]{1,0:T(8,128)S(1)}, u32[]{:S(2)}, u32[]{:S(2)}) collective-permute-start(f32[64,512]{1,0:T(8,128)S(1)} %get-tuple-element.93), channel_id=1, source_target_pairs={{0,4},{4,0},{8,12},{12,8},{1,5},{5,1},{9,13},{13,9},{2,6},{6,2},{1... | collective-permute-start | bytes 393224 | tf_op jit(solution)/shard_map/ppermute | solution.py:548
  73.5 5.6 %collective-permute-start.18 = (f32[64,512]{1,0:T(8,128)S(1)}, f32[64,512]{1,0:T(8,128)S(1)}, u32[]{:S(2)}, u32[]{:S(2)}) collective-permute-start(f32[64,512]{1,0:T(8,128)S(1)} %add_terms.4.a_ref), channel_id=1, source_target_pairs={{0,8},{4,12},{8,0},{12,4},{1,9},{5,13},{9,1},{13,5},{2,10},{6,14},... | collective-permute-start | bytes 393224 | tf_op jit(solution)/shard_map/ppermute | solution.py:548
  79.2 1.4 %collective-permute-start.19 = (f32[64,512]{1,0:T(8,128)S(1)}, f32[64,512]{1,0:T(8,128)S(1)}, u32[]{:S(2)}, u32[]{:S(2)}) collective-permute-start(f32[64,512]{1,0:T(8,128)S(1)} %add_terms.5.own_ref), channel_id=1, source_target_pairs={{0,4},{4,0},{8,12},{12,8},{1,5},{5,1},{9,13},{13,9},{2,6},{6,2},{1... | collective-permute-start | bytes 393224 | tf_op jit(solution)/shard_map/ppermute | solution.py:548
  83.8 4.4 %collective-permute-start.20 = (f32[64,128]{1,0:T(8,128)S(1)}, f32[64,128]{1,0:T(8,128)S(1)}, u32[]{:S(2)}, u32[]{:S(2)}) collective-permute-start(f32[64,128]{1,0:T(8,128)S(1)} %get-tuple-element.97.refs_0_), channel_id=1, source_target_pairs={{0,1},{1,0},{2,3},{3,2},{4,5},{5,4},{6,7},{7,6},{8,9},{9,8},{10,11... | collective-permute-start | bytes 98312 | tf_op jit(solution)/shard_map/ppermute | solution.py:548
  83.8 4.9 %collective-permute-start.21 = (f32[64,128]{1,0:T(8,128)S(1)}, f32[64,128]{1,0:T(8,128)S(1)}, u32[]{:S(2)}, u32[]{:S(2)}) collective-permute-start(f32[64,128]{1,0:T(8,128)S(1)} %get-tuple-element.97.refs_0_), channel_id=1, source_target_pairs={{0,2},{1,3},{2,0},{3,1},{4,6},{5,7},{6,4},{7,5},{8,10},{9,11},{10,... | collective-permute-start | bytes 98312 | tf_op jit(solution)/shard_map/ppermute | solution.py:548
  86.6 5.7 %collective-permute-start.22 = (f32[64,128]{1,0:T(8,128)S(1)}, f32[64,128]{1,0:T(8,128)S(1)}, u32[]{:S(2)}, u32[]{:S(2)}) collective-permute-start(f32[64,128]{1,0:T(8,128)S(1)} %get-tuple-element.97.refs_0_), channel_id=1, source_target_pairs={{0,3},{1,2},{2,1},{3,0},{4,7},{5,6},{6,5},{7,4},{8,11},{9,10},{10,... | collective-permute-start | bytes 98312 | tf_op jit(solution)/shard_map/ppermute | solution.py:548
  (6 other events, 144.1 us)

commit v9 on v8

--- a/solution.py
+++ b/solution.py
@@ -82,32 +82,19 @@
     return jnp.ceil(jnp.log2(jnp.maximum(top, 1e-30)))
 
 
-def patients_of(source, buffers, sems):
-    count = buffers.shape[0]
-    group = count // sems.shape[0]
-    rows = [pl.ds(first, group) for first in range(0, count, group)]
-    copies = [pltpu.make_async_copy(source.at[r], buffers.at[r], sems.at[i]) for i, r in enumerate(rows)]
-    for copy in copies:
-        copy.start()
-    for p in range(count):
-        if p % group == 0:
-            copies[p // group].wait()
-        yield buffers[p]
-
-
-def decode(coded_ref, count, rank, with_gram):
-    def rows(first, number):
-        return coded_ref[pl.ds(first, number), :].astype(jnp.int32).astype(F32)
+def decode(coded_ref, total_count, first, count, rank, with_gram):
+    def rows(start, number):
+        return coded_ref[pl.ds(start, number), :].astype(jnp.int32).astype(F32)
 
     gram_rows = rank // 2 if with_gram else 0
-    exponents = rows(count * rank + gram_rows, exponent_rows(count))[:, :LANES].T
+    exponents = rows(total_count * rank + gram_rows, exponent_rows(total_count))[:, :LANES].T
     steps = jnp.exp2(exponents[:rank]) * (1.0 / LEVELS)
     gram = None
-    if with_gram:
-        digits = rows(count * rank, gram_rows)
+    if with_gram and first == 0:
+        digits = rows(total_count * rank, gram_rows)
         digits = jnp.concatenate([digits[:, : 2 * rank], digits[:, 2 * rank :]], axis=0)
-        gram = (digits[:, :rank] + digits[:, rank:] * (0.5 / LEVELS)) * steps[:, count : count + 1]
-    return [rows(p * rank, rank) * steps[:, p : p + 1] for p in range(count)], gram
+        gram = (digits[:, :rank] + digits[:, rank:] * (0.5 / LEVELS)) * steps[:, total_count : total_count + 1]
+    return [rows(p * rank, rank) * steps[:, p : p + 1] for p in range(first, first + count)], gram
 
 
 def encode_gram(v_ref, coded_ref, first_row):
@@ -123,71 +110,85 @@
     return exponent
 
 
-def send_projection_kernel(slot, place, v_hbm, visits_ref, *refs):
-    *coded_refs, v_ref, buffers, sems, v_sem = refs
-    v_copy = pltpu.make_async_copy(v_hbm, v_ref, v_sem)
-    v_copy.start()
-    rank = v_ref.shape[0]
-    count = buffers.shape[0] // len(coded_refs)
+def encode(patients, with_gram, v_ref, coded_ref):
+    count, rank = len(patients), v_ref.shape[0]
     lanes = lane_numbers((rank, LANES))
-    exponents = [jnp.zeros((rank, LANES), F32) for _ in coded_refs]
-    for p, visits in enumerate(patients_of(visits_ref.at[feature_of(place) ^ slot], buffers, sems)):
-        part, i = divmod(p, count)
-        if p == 0:
-            v_copy.wait()
-        proj = low_dot(v_ref[...], visits, ROWS_BY_ROWS)
+    exponents = jnp.zeros((rank, LANES), F32)
+    for p, visits in enumerate(patients):
+        proj = low_dot(v_ref[...], visits(), ROWS_BY_ROWS)
         exponent = row_exponent(proj)
         coded = jnp.floor(proj * (LEVELS / jnp.exp2(exponent)) + 0.5)
-        coded_refs[part][pl.ds(i * rank, rank), :] = coded.astype(jnp.int32).astype(jnp.int16)
-        exponents[part] = jnp.where(lanes == i, exponent, exponents[part])
-    for part, coded_ref in enumerate(coded_refs):
-        end = count * rank
-        if part == 0:
-            exponents[0] = jnp.where(lanes == count, encode_gram(v_ref, coded_ref, end), exponents[0])
-            end += rank // 2
-        rows = exponent_rows(count)
-        last = exponents[part].T[:rows]
-        last = jnp.concatenate([last, jnp.zeros((rows, coded_ref.shape[1] - rank), F32)], axis=1)
-        coded_ref[pl.ds(end, rows), :] = last.astype(jnp.int32).astype(jnp.int16)
-
-
-def own_projection_kernel(place, v_hbm, w_ref, visits_ref, *refs):
-    *proj_refs, v_gram_ref, w_gram_ref, v_ref, buffers, sems, v_sem = refs
+        coded_ref[pl.ds(p * rank, rank), :] = coded.astype(jnp.int32).astype(jnp.int16)
+        exponents = jnp.where(lanes == p, exponent, exponents)
+    end = count * rank
+    if with_gram:
+        exponents = jnp.where(lanes == count, encode_gram(v_ref, coded_ref, end), exponents)
+        end += rank // 2
+    rows = exponent_rows(count)
+    last = jnp.concatenate([exponents.T[:rows], jnp.zeros((rows, coded_ref.shape[1] - rank), F32)], axis=1)
+    coded_ref[pl.ds(end, rows), :] = last.astype(jnp.int32).astype(jnp.int16)
+
+
+def first_projection_kernel(slot, place, v_hbm, visits_ref, coded_ref, v_ref, buffers, sem, v_sem):
+    count = buffers.shape[0]
     v_copy = pltpu.make_async_copy(v_hbm, v_ref, v_sem)
+    visits_copy = pltpu.make_async_copy(visits_ref.at[feature_of(place) ^ slot, pl.ds(0, count)], buffers, sem)
     v_copy.start()
-    count = buffers.shape[0] // len(proj_refs)
-    for p, visits in enumerate(patients_of(visits_ref.at[feature_of(place)], buffers, sems)):
-        if p == 0:
-            v_copy.wait()
-        proj_refs[p // count][p % count] = low_dot(v_ref[...], visits, ROWS_BY_ROWS)
+    visits_copy.start()
+    v_copy.wait()
+    visits_copy.wait()
+    encode([lambda p=p: buffers[p] for p in range(count)], True, v_ref, coded_ref)
+
+
+def first_projection(slot, count, place, visits, v_rows):
+    _, share, slots, width = visits.shape
+    rank = v_rows.shape[0]
+    return pl.pallas_call(
+        functools.partial(first_projection_kernel, slot),
+        in_specs=[SMEM_SPEC, HBM_SPEC, HBM_SPEC],
+        out_specs=VMEM_SPEC,
+        out_shape=jax.ShapeDtypeStruct(payload_shape(count, rank, slots, True), jnp.int16),
+        scratch_shapes=[
+            pltpu.VMEM(v_rows.shape, BF16),
+            pltpu.VMEM((count, slots, width), BF16),
+            pltpu.SemaphoreType.DMA,
+            pltpu.SemaphoreType.DMA,
+        ],
+        compiler_params=parameters(LIMIT),
+        cost_estimate=SHORT,
+        name="project_first",
+    )(place, v_rows, visits)
+
+
+def send_projection_kernel(slot, pieces, place, v_ref, visits_ref, *coded_refs):
+    owner = feature_of(place) ^ slot
+    for (first, count, with_gram), coded_ref in zip(pieces, coded_refs):
+        patients = [lambda p=p: visits_ref[owner, p] for p in range(first, first + count)]
+        encode(patients, with_gram, v_ref, coded_ref)
+
+
+def project_for(slot, pieces, place, visits, v_rows):
+    rank, slots = v_rows.shape[0], visits.shape[2]
+    shapes = [payload_shape(count, rank, slots, with_gram) for _, count, with_gram in pieces]
+    return pl.pallas_call(
+        functools.partial(send_projection_kernel, slot, pieces),
+        in_specs=[SMEM_SPEC, VMEM_SPEC, VMEM_SPEC],
+        out_specs=[VMEM_SPEC] * len(pieces),
+        out_shape=[jax.ShapeDtypeStruct(shape, jnp.int16) for shape in shapes],
+        compiler_params=parameters(LIMIT),
+        cost_estimate=SHORT,
+        name="project_send",
+    )(place, v_rows, visits)
+
+
+def own_projection_kernel(place, v_ref, w_ref, visits_ref, *refs):
+    *proj_refs, v_gram_ref, w_gram_ref = refs
+    count = visits_ref.shape[1] // len(proj_refs)
+    for p in range(visits_ref.shape[1]):
+        proj_refs[p // count][p % count] = low_dot(v_ref[...], visits_ref[feature_of(place), p], ROWS_BY_ROWS)
     v_gram_ref[...] = low_dot(v_ref[...], v_ref[...], ROWS_BY_ROWS)
     w_gram = high_dot(w_ref[...], w_ref[...], COLS_BY_COLS)
     w_gram_ref[...] = jnp.concatenate([jnp.zeros_like(w_gram), w_gram], axis=1)
-
-
-def projection_buffers(visits, v_rows):
-    return [
-        pltpu.VMEM(v_rows.shape, BF16),
-        pltpu.VMEM(visits.shape[1:], BF16),
-        pltpu.SemaphoreType.DMA((2 if visits.shape[1] % 2 == 0 else 1,)),
-        pltpu.SemaphoreType.DMA,
-    ]
-
-
-def project_for(slot, n_parts, place, visits, v_rows):
-    _, share, slots, width = visits.shape
-    rank = v_rows.shape[0]
-    shapes = [payload_shape(share // n_parts, rank, slots, part == 0) for part in range(n_parts)]
-    return pl.pallas_call(
-        functools.partial(send_projection_kernel, slot),
-        in_specs=[SMEM_SPEC, HBM_SPEC, HBM_SPEC],
-        out_specs=[VMEM_SPEC] * n_parts,
-        out_shape=[jax.ShapeDtypeStruct(shape, jnp.int16) for shape in shapes],
-        scratch_shapes=projection_buffers(visits, v_rows),
-        compiler_params=parameters(LIMIT),
-        cost_estimate=SHORT,
-        name="project_send",
-    )(place, v_rows, visits)
 
 
 def project_own(n_parts, place, visits, v_rows, w_start):
@@ -197,10 +198,9 @@
     proj = jax.ShapeDtypeStruct((share // n_parts, rank, slots), F32)
     *own, v_gram, w_gram = pl.pallas_call(
         own_projection_kernel,
-        in_specs=[SMEM_SPEC, HBM_SPEC, VMEM_SPEC, HBM_SPEC],
+        in_specs=[SMEM_SPEC] + [VMEM_SPEC] * 3,
         out_specs=[VMEM_SPEC] * (n_parts + 2),
         out_shape=[proj] * n_parts + [gram, jax.ShapeDtypeStruct((rank, 2 * rank), F32)],
-        scratch_shapes=projection_buffers(visits, v_rows),
         compiler_params=parameters(LIMIT),
         cost_estimate=SHORT,
         name="project_own",
@@ -311,49 +311,54 @@
         frames[p] = 1.5 * frames[p] - 0.5 * moved[p]
 
 
-def frames_kernel(part, share, n_coded, place, counts_ref, h_ref, w_ref, v_gram_ref, before_ref, own_ref, *refs):
-    coded = refs[:n_coded]
-    frames_ref, terms_ref, v_total_ref, proj, frames = refs[n_coded:]
+def frames_kernel(layouts, part, share, place, counts_ref, h_ref, w_ref, v_gram_ref, before_ref, own_ref, *refs):
+    coded, refs = refs[: len(layouts)], refs[len(layouts) :]
+    frames_ref, terms_ref, v_total_ref, proj, frames = refs
     count, rank, slots = frames.shape
+    patients = range(count)
     first = feature_of(place) * share + part * count
-    pieces = [own_ref[p] for p in range(count)]
+    pieces = [own_ref[p] for p in patients]
     v_gram = v_gram_ref[...]
-    for code in coded:
-        arrived, gram = decode(code, count, rank, part == 0)
+    for code, (total_count, start, with_gram) in zip(coded, layouts):
+        arrived, gram = decode(code, total_count, start, count, rank, with_gram)
         pieces = [a + b for a, b in zip(pieces, arrived)]
         if gram is not None:
             v_gram = v_gram + gram
     v_total_ref[...] = v_gram
-    for p, piece in enumerate(pieces):
-        proj[p] = piece
-        mixed = high_dot(h_ref[...] * w_ref[pl.ds(first + p, 1), :], piece)
-        mixed = jnp.where(lane_numbers((rank, slots)) < counts_ref[first + p], mixed, 0.0)
-        energy = jnp.sum(jnp.sum(mixed * mixed, axis=1, keepdims=True), axis=0, keepdims=True)
-        frames[p] = mixed * lax.rsqrt(energy + epsilon)
+    for p in patients:
+        proj[p] = pieces[p]
+    weights = [w_ref[pl.ds(first + p, 1), :] for p in patients]
+    mixed = [high_dot(h_ref[...] * weights[p], pieces[p]) for p in patients]
+    lanes = lane_numbers((rank, slots))
+    mixed = [jnp.where(lanes < counts_ref[first + p], mixed[p], 0.0) for p in patients]
+    energy = [jnp.sum(jnp.sum(x * x, axis=1, keepdims=True), axis=0, keepdims=True) for x in mixed]
+    for p in patients:
+        frames[p] = mixed[p] * lax.rsqrt(energy[p] + epsilon)
 
     def sweep(fine, step, carry):
         sweep_all(frames, rank, fine)
         return carry
 
-    lax.fori_loop(0, COARSE_STEPS, functools.partial(sweep, False), 0)
-    lax.fori_loop(COARSE_STEPS, NS_STEPS, functools.partial(sweep, True), 0)
+    lax.fori_loop(0, COARSE_STEPS, functools.partial(sweep, False), 0, unroll=True)
+    lax.fori_loop(COARSE_STEPS, NS_STEPS, functools.partial(sweep, True), 0, unroll=3)
+    low = [frames[p].astype(BF16) for p in patients]
+    for p in patients:
+        frames_ref[p] = low[p]
+    products = [jnp.concatenate(three_parts(proj[p]), axis=0) for p in patients]
+    products = [low_dot(low[p], products[p], ROWS_BY_ROWS) for p in patients]
     before = before_ref[...]
     terms = before[:, :rank]
-    for p in range(count):
-        low = frames[p].astype(BF16)
-        frames_ref[p] = low
-        parts = three_parts(proj[p])
-        product = low_dot(low, parts[0], ROWS_BY_ROWS)
-        for piece in parts[1:]:
-            product = product + low_dot(low, piece, ROWS_BY_ROWS)
-        terms = terms + product * w_ref[pl.ds(first + p, 1), :]
+    for p in patients:
+        product = products[p][:, :rank] + (products[p][:, rank : 2 * rank] + products[p][:, 2 * rank :])
+        terms = terms + product * weights[p]
     terms_ref[...] = jnp.concatenate([terms, before[:, rank:]], axis=1)
 
 
-def own_frames(part, n_parts, place, counts, h_start, w_start, v_gram, before, own, coded):
+def own_frames(layouts, part, n_parts, place, counts, h_start, w_start, v_gram, before, own, coded):
     count, rank, slots = own.shape
-    return pl.pallas_call(
-        functools.partial(frames_kernel, part, count * n_parts, len(coded)),
+    share = count * n_parts
+    return pl.pallas_call(
+        functools.partial(frames_kernel, layouts, part, share),
         in_specs=[SMEM_SPEC] * 2 + [VMEM_SPEC] * (5 + len(coded)),
         out_specs=[VMEM_SPEC] * 3,
         out_shape=[
@@ -371,24 +376,26 @@
 def projected_kernel(items, place, visits_ref, *refs):
     frames_refs, outs, token_ref = refs[: len(items)], refs[-2 * len(items) - 1 : -1], refs[-1]
     token_ref[...] = jnp.zeros_like(token_ref)
-    for i, (slot, part) in enumerate(items):
+    for i, (slot, first) in enumerate(items):
         owner = feature_of(place) ^ slot
         count, rank, _ = frames_refs[i].shape
         for p in range(count):
             rows = pl.ds(p * rank, rank)
-            product = low_dot(frames_refs[i][p], visits_ref[owner, part * count + p])
+            product = low_dot(frames_refs[i][p], visits_ref[owner, first + p])
             outs[2 * i][rows, :], outs[2 * i + 1][rows, :] = two_parts(product)
 
 
 def project_frames(items, place, frames, visits, after):
     width = visits.shape[-1]
-    count, rank, _ = frames[0, 0].shape
-    out = jax.ShapeDtypeStruct((count * rank, width), BF16)
+    outs = []
+    for item in items:
+        count, rank, _ = frames[item].shape
+        outs += [jax.ShapeDtypeStruct((count * rank, width), BF16)] * 2
     *parts, token = pl.pallas_call(
         functools.partial(projected_kernel, items),
         in_specs=[SMEM_SPEC] + [VMEM_SPEC] * (1 + len(items)) + [ANY_SPEC] * len(after),
-        out_specs=[VMEM_SPEC] * (2 * len(items) + 1),
-        out_shape=[out] * (2 * len(items)) + [jax.ShapeDtypeStruct((8, LANES), F32)],
+        out_specs=[VMEM_SPEC] * (len(outs) + 1),
+        out_shape=outs + [jax.ShapeDtypeStruct((8, LANES), F32)],
         compiler_params=parameters(LIMIT),
         cost_estimate=SHORT,
         name="project_frames",
@@ -449,15 +456,12 @@
     )(h_next, w_gram)
 
 
-def v_terms_kernel(place, factor_ref, *refs):
+def v_terms_kernel(items, place, factor_ref, *refs):
     *parts, keep_ref, send_ref, terms_ref = refs
     rank, width = terms_ref.shape
     half = width // 2
-    n_slots, _, rows = factor_ref.shape
-    count = parts[0].shape[0]
-    for i in range(len(parts) // 2):
-        slot, first = divmod(i * count, rows)
-        columns = pl.ds(first, count)
+    for i, (slot, first) in enumerate(items):
+        columns = pl.ds(first * rank, parts[2 * i].shape[0])
         large = low_dot(factor_ref[slot, :, columns], parts[2 * i][...])
         small = low_dot(factor_ref[slot, : 2 * rank, columns], parts[2 * i + 1][...])
         terms = large[:rank] + (large[rank : 2 * rank] + small[:rank]) + (large[2 * rank :] + small[rank:])
@@ -466,12 +470,12 @@
     send_ref[...] = terms_ref[:, pl.ds(pl.multiple_of((1 - core_of(place)) * half, half), half)]
 
 
-def all_v_terms(place, factor, projected):
+def all_v_terms(items, place, factor, projected):
     width = projected[0].shape[1]
     rank = factor.shape[1] // 3
     half = (rank, width // 2)
     return pl.pallas_call(
-        v_terms_kernel,
+        functools.partial(v_terms_kernel, items),
         in_specs=[SMEM_SPEC] + [VMEM_SPEC] * (1 + len(projected)),
         out_specs=[VMEM_SPEC] * 2,
         out_shape=[jax.ShapeDtypeStruct(half, F32)] * 2,
@@ -482,10 +486,9 @@
     )(place, factor, *projected)
 
 
-def next_v_kernel(n_parts, share, place, own_ref, other_ref, inverse_ref, h_ref, *refs):
-    parts, (v_ref, sums_ref, v_parts) = refs[:n_parts], refs[n_parts:]
+def next_v_kernel(items, share, place, own_ref, other_ref, inverse_ref, h_ref, *refs):
+    *parts, v_ref, sums_ref, v_parts = refs
     rank = inverse_ref.shape[0]
-    count = parts[0].shape[0] // rank
     upper = core_of(place) == 1
     left = jnp.where(upper, other_ref[...], own_ref[...])
     right = jnp.where(upper, own_ref[...], other_ref[...])
@@ -496,21 +499,20 @@
     gram = low_dot(v_parts[...], v_parts[...], ROWS_BY_ROWS)
     gram = gram[:rank, :rank] + (gram[:rank, rank:] + gram[rank:, :rank])
     sums_ref[...] = jnp.concatenate([jnp.zeros((rank, rank), F32), gram], axis=1)
-    for i in range(n_parts // 2):
+    for i, (slot, done) in enumerate(items):
         seen = low_dot(parts[2 * i][...], v_parts[...], ROWS_BY_ROWS)
         seen = seen + low_dot(parts[2 * i + 1][...], v_parts[...], ROWS_BY_ROWS)
-        slot, done = divmod(i * count, share)
         first = (feature_of(place) ^ slot) * share + done
-        for p in range(count):
+        for p in range(seen.shape[0] // rank):
             row = jnp.sum(seen[p * rank : (p + 1) * rank] * weights, axis=0, keepdims=True)
             sums_ref[pl.ds(first + p, 1), :rank] = row[:, :rank] + row[:, rank:]
 
 
-def next_v(share, place, own, other, inverse, h_next, projected):
+def next_v(items, share, place, own, other, inverse, h_next, projected):
     width = projected[0].shape[1]
     rank = inverse.shape[0]
     return pl.pallas_call(
-        functools.partial(next_v_kernel, len(projected), share),
+        functools.partial(next_v_kernel, items, share),
         in_specs=[SMEM_SPEC] + [VMEM_SPEC] * (4 + len(projected)),
         out_specs=[VMEM_SPEC] * 2,
         out_shape=[
@@ -599,40 +601,54 @@
     v_rows = pltpu.with_memory_space_constraint(v_start.T, pltpu.HBM)
 
     n_parts = 2 if share % 2 == 0 else 1
-    halves = range(n_parts)
+    count = share // n_parts
+    firsts = [part * count for part in range(n_parts)]
     far = list(range(n - 1, 1, -1))
-    sent = {slot: project_for(slot, n_parts, place, in_hbm, v_rows) for slot in far + [1]}
-    coded = [[swap(sent[slot][part], "feature", slot) for slot in far + [1]] for part in halves]
-    own, v_gram, h_local = project_own(n_parts, place, in_hbm, v_rows, w_start)
+    v_near = v_start.T
+
+    sent = {(far[0], 0): first_projection(far[0], count, place, in_hbm, v_rows)}
+    for slot in far[1:] + [1]:
+        pieces = [(first, count, first == 0) for first in firsts]
+        codes = project_for(slot, pieces, place, by_owner, v_near)
+        sent |= {(slot, first): code for first, code in zip(firsts, codes)}
+    for first in firsts[1:]:
+        sent[far[0], first] = project_for(far[0], [(first, count, False)], place, by_owner, v_near)[0]
+    sent = {(slot, first): sent[slot, first] for first in firsts for slot in far + [1]}
+    arrived = {item: swap(code, "feature", item[0]) for item, code in sent.items()}
+    own, v_gram, h_local = project_own(n_parts, place, by_owner, v_near, w_start)
+
     frames = {}
-    for part in halves:
-        frames[0, part], h_local, v_gram = own_frames(
-            part, n_parts, place, visit_counts, h_start, w_start, v_gram, h_local, own[part], coded[part]
+    for part, first in enumerate(firsts):
+        layouts = [(count, 0, first == 0)] * (n - 1)
+        coded = [arrived[slot, first] for slot in far + [1]]
+        frames[0, first], h_local, v_total = own_frames(
+            layouts, part, n_parts, place, visit_counts, h_start, w_start, v_gram, h_local, own[part], coded
         )
+        v_gram = v_total if first == 0 else v_gram
         for slot in far + [1]:
-            frames[slot, part] = swap(frames[0, part], "feature", slot)
-
-    projected, token = project_frames([(0, part) for part in halves], place, frames, by_owner, [])
-    for part in halves[:-1]:
-        more, token = project_frames([(slot, part) for slot in [1] + far], place, frames, by_owner, [token])
+            frames[slot, first] = swap(frames[0, first], "feature", slot)
+
+    projected, token = project_frames([(0, first) for first in firsts], place, frames, by_owner, [])
+    for first in firsts[:-1]:
+        more, token = project_frames([(slot, first) for slot in [1] + far], place, frames, by_owner, [token])
         projected |= more
     h_sum, w_gram = sum_h(staged_terms(h_local, "patient", [token]), token)
     h_terms = all_terms(h_sum, "feature")
-    last = halves[-1]
     after = h_sum
     for slot in [1] + far:
-        more, token = project_frames([(slot, last)], place, frames, by_owner, [after])
+        more, token = project_frames([(slot, firsts[-1])], place, frames, by_owner, [after])
         projected |= more
         if slot == 1:
-            first = first_inverse(v_gram, w_gram, token)
+            inverse = first_inverse(v_gram, w_gram, token)
         after = token
-    h_result, h_next, factor = next_h(place, h_terms, first, w_start, n, token)
-
-    flat = [x for slot in range(n) for part in halves for x in projected[slot, part]]
-    keep, send = all_v_terms(place, factor, flat)
+    h_result, h_next, factor = next_h(place, h_terms, inverse, w_start, n, token)
+
+    items = list(projected)
+    flat = [x for item in items for x in projected[item]]
+    keep, send = all_v_terms(items, place, factor, flat)
     h_gram, second = second_inverse(h_next, w_gram)
     own_terms, other_terms = patient_halves(keep, send, second)
-    v_next, sums = next_v(share, place, own_terms, other_terms, second, h_next, flat)
+    v_next, sums = next_v(items, share, place, own_terms, other_terms, second, h_next, flat)
     w_next = next_w(all_terms(sums, "feature"), h_gram, patients)
     return (h_result, v_next.T, w_next)
 

time: 95.9 us -> 95.4 us (level)
  Pallas kernels: 45.9 us -> 39.3 us
  waiting for transfers between devices: 18.3 us -> 22.1 us
  starting transfers between devices: 30.5 us -> 32.9 us
    pallas_call x8 -> x9, Pallas kernels: 32.6 us -> 26 us  [the longest x2 12.6 us: own_frames(): pl.pallas_call(functools.partial(frames_kernel, layouts, part, share), in...]
    ppermute x23, waiting for transfers between devices: 18.3 us -> 22.1 us  [swap(): return lax.ppermute(x, axis, pairs)]
    ppermute x23, starting transfers between devices: 30.5 us -> 32.9 us  [swap(): return lax.ppermute(x, axis, pairs)]
  transfers between devices with their start and end apart: 23 -> 23, of which waited for: 9 -> 8; matrix products, arithmetic and copies ran while one was open for 0% -> 0% of each run, Pallas kernels for 35% -> 29%
where the time goes in v9:
time: 95.4 us; the launch traced here: 95.2 us
  Pallas kernels  39.3 us (41%)
  starting transfers between devices  32.9 us (34%)
  waiting for transfers between devices  22.1 us (23%)
    ppermute x23, starting transfers between devices, swap(): return lax.ppermute(x, axis, pairs)  32.9 us
    ppermute x23, waiting for transfers between devices, swap(): return lax.ppermute(x, axis, pairs)  22.1 us
    pallas_call x2, Pallas kernels, own_frames(): pl.pallas_call(functools.partial(frames_kernel, layouts, part, share), in...  12.6 us
    pallas_call x3, Pallas kernels, project_for(): pl.pallas_call(functools.partial(send_projection_kernel, slot, pieces), i...  4.21 us
    pallas_call x5, Pallas kernels, project_frames(): pl.pallas_call(functools.partial(projected_kernel, items), in_specs=[SMEM...  3.6 us
    pallas_call x1, Pallas kernels, next_w(): pl.pallas_call(functools.partial(next_w_kernel, len(sums)), out_shape=jax...  3.36 us
    pallas_call x1, Pallas kernels, next_v(): pl.pallas_call(functools.partial(next_v_kernel, items, share), in_specs=[...  3.23 us
    pallas_call x1, Pallas kernels, first_projection(): pl.pallas_call(functools.partial(first_projection_kernel, slot), in_specs...  2.84 us
  transfers between devices with their start and end apart: 23, of which 8 were waited for; matrix products, arithmetic and copies ran while one was open for 0% of the time, Pallas kernels for 29%

profile of v9, /device:TPU:0, one launch (start us, length us, event | category | flops | bytes accessed | tf_op | source)
XLA Modules:
  0.0 95.2 jit_solution(14095143795579467070)
XLA Ops:
  0.7 2.8 %project_first.1 = s16[304,256]{1,0:T(8,128)(2,1)S(1)} custom-call(s32[1]{0:T(128)} %bitcast.place, bf16[64,1024]{1,0:T(8,128)(2,1)} %bitcast.14, bf16[4,8,256,1024]{3,2,1,0:T(8,128)(2,1)} %bitcast.4), custom_call_target="tpu_custom_call" | custom-call | flops 1000 | bytes 1000 | tf_op jit(solution)/shard_map/project_first/pallas_call | solution.py:146
  3.5 5.1 %collective-permute-start = (s16[304,256]{1,0:T(8,128)(2,1)S(1)}, s16[304,256]{1,0:T(8,128)(2,1)S(1)}, u32[]{:S(2)}, u32[]{:S(2)}) collective-permute-start(s16[304,256]{1,0:T(8,128)(2,1)S(1)} %project_first.1), channel_id=1, source_target_pairs={{0,3},{1,2},{2,1},{3,0},{4,7},{5,6},{6,5},{7,4},{8,11},{9,10},{10,... | collective-permute-start | bytes 466952 | tf_op jit(solution)/shard_map/ppermute | solution.py:550
  8.6 1.6 %project_send.3 = (s16[304,256]{1,0:T(8,128)(2,1)S(1)}, s16[272,256]{1,0:T(8,128)(2,1)S(1)}) custom-call(s32[1]{0:T(128)} %bitcast.place, bf16[64,1024]{1,0:T(8,128)(2,1)S(1)} %bitcast.15, bf16[4,8,256,1024]{3,2,1,0:T(8,128)(2,1)S(1)} %bitcast.5), custom_call_target="tpu_custom_call" | custom-call | flops 1000 | bytes 1000 | tf_op jit(solution)/shard_map/project_send/pallas_call | solution.py:173
  10.3 2.6 %collective-permute-start.1 = (s16[304,256]{1,0:T(8,128)(2,1)S(1)}, s16[304,256]{1,0:T(8,128)(2,1)S(1)}, u32[]{:S(2)}, u32[]{:S(2)}) collective-permute-start(s16[304,256]{1,0:T(8,128)(2,1)S(1)} %get-tuple-element.51), channel_id=1, source_target_pairs={{0,2},{1,3},{2,0},{3,1},{4,6},{5,7},{6,4},{7,5},{8,10},{9,11},{10,... | collective-permute-start | bytes 466952 | tf_op jit(solution)/shard_map/ppermute | solution.py:550
  12.9 1.6 %project_send.4 = (s16[304,256]{1,0:T(8,128)(2,1)S(1)}, s16[272,256]{1,0:T(8,128)(2,1)S(1)}) custom-call(s32[1]{0:T(128)} %bitcast.place, bf16[64,1024]{1,0:T(8,128)(2,1)S(1)} %bitcast.16, bf16[4,8,256,1024]{3,2,1,0:T(8,128)(2,1)S(1)} %bitcast.6), custom_call_target="tpu_custom_call" | custom-call | flops 1000 | bytes 1000 | tf_op jit(solution)/shard_map/project_send/pallas_call | solution.py:173
  14.5 1.6 %collective-permute-start.2 = (s16[304,256]{1,0:T(8,128)(2,1)S(1)}, s16[304,256]{1,0:T(8,128)(2,1)S(1)}, u32[]{:S(2)}, u32[]{:S(2)}) collective-permute-start(s16[304,256]{1,0:T(8,128)(2,1)S(1)} %get-tuple-element.52), channel_id=1, source_target_pairs={{0,1},{1,0},{2,3},{3,2},{4,5},{5,4},{6,7},{7,6},{8,9},{9,8},{10,11... | collective-permute-start | bytes 466952 | tf_op jit(solution)/shard_map/ppermute | solution.py:550
  17.4 1.7 %collective-permute-start.4 = (s16[272,256]{1,0:T(8,128)(2,1)S(1)}, s16[272,256]{1,0:T(8,128)(2,1)S(1)}, u32[]{:S(2)}, u32[]{:S(2)}) collective-permute-start(s16[272,256]{1,0:T(8,128)(2,1)S(1)} %get-tuple-element.56), channel_id=1, source_target_pairs={{0,2},{1,3},{2,0},{3,1},{4,6},{5,7},{6,4},{7,5},{8,10},{9,11},{10,... | collective-permute-start | bytes 417800 | tf_op jit(solution)/shard_map/ppermute | solution.py:550
  19.0 2.5 %collective-permute-start.5 = (s16[272,256]{1,0:T(8,128)(2,1)S(1)}, s16[272,256]{1,0:T(8,128)(2,1)S(1)}, u32[]{:S(2)}, u32[]{:S(2)}) collective-permute-start(s16[272,256]{1,0:T(8,128)(2,1)S(1)} %get-tuple-element.57), channel_id=1, source_target_pairs={{0,1},{1,0},{2,3},{3,2},{4,5},{5,4},{6,7},{7,6},{8,9},{9,8},{10,11... | collective-permute-start | bytes 417800 | tf_op jit(solution)/shard_map/ppermute | solution.py:550
  23.1 5.7 %collective-permute-done.1.refs_1_ = s16[304,256]{1,0:T(8,128)(2,1)S(1)} collective-permute-done((s16[304,256]{1,0:T(8,128)(2,1)S(1)}, s16[304,256]{1,0:T(8,128)(2,1)S(1)}, u32[]{:S(2)}, u32[]{:S(2)}) %collective-permute-start.1) | collective-permute-done | bytes 155680 | tf_op jit(solution)/shard_map/ppermute | solution.py:550
  28.8 6.2 %own_frames.2 = (bf16[4,64,256]{2,1,0:T(8,128)(2,1)S(1)}, f32[64,128]{1,0:T(8,128)S(1)}, f32[64,64]{1,0:T(8,128)S(1)}) custom-call(s32[1]{0:T(128)} %bitcast.place, s32[32]{0:T(128)S(1)} %copy-done.4, f32[64,64]{1,0:T(8,128)S(1)} %copy-done.3, f32[32,64]{1,0:T(8,128)S(1)} %copy-done.2, f32[64,64]{1,0:T(8,128)S(1)} %get-tuple-element.48.v_gram_ref, ...), custom_call_target="tpu_custom_call" | custom-call | flops 1000 | bytes 1000 | tf_op jit(solution)/shard_map/own_frames/pallas_call | solution.py:360
  35.1 1.6 %collective-permute-start.8 = (bf16[4,64,256]{2,1,0:T(8,128)(2,1)S(1)}, bf16[4,64,256]{2,1,0:T(8,128)(2,1)S(1)}, u32[]{:S(2)}, u32[]{:S(2)}) collective-permute-start(bf16[4,64,256]{2,1,0:T(8,128)(2,1)S(1)} %get-tuple-element.59.refs_0_), channel_id=1, source_target_pairs={{0,3},{1,2},{2,1},{3,0},{4,7},{5,6},{6,5},{7,4},{8,11},{9,10},{10,... | collective-permute-start | bytes 393224 | tf_op jit(solution)/shard_map/ppermute | solution.py:550
  36.7 1.9 %collective-permute-start.9 = (bf16[4,64,256]{2,1,0:T(8,128)(2,1)S(1)}, bf16[4,64,256]{2,1,0:T(8,128)(2,1)S(1)}, u32[]{:S(2)}, u32[]{:S(2)}) collective-permute-start(bf16[4,64,256]{2,1,0:T(8,128)(2,1)S(1)} %get-tuple-element.59.refs_0_), channel_id=1, source_target_pairs={{0,2},{1,3},{2,0},{3,1},{4,6},{5,7},{6,4},{7,5},{8,10},{9,11},{10,... | collective-permute-start | bytes 393224 | tf_op jit(solution)/shard_map/ppermute | solution.py:550
  38.6 6.4 %own_frames.3 = (bf16[4,64,256]{2,1,0:T(8,128)(2,1)S(1)}, f32[64,128]{1,0:T(8,128)S(1)}, f32[64,64]{1,0:T(8,128)}) custom-call(s32[1]{0:T(128)} %bitcast.place, s32[32]{0:T(128)S(1)} %copy-done.4, f32[64,64]{1,0:T(8,128)S(1)} %copy-done.3, f32[32,64]{1,0:T(8,128)S(1)} %copy-done.2, f32[64,64]{1,0:T(8,128)S(1)} %get-tuple-element.53.v_gram_ref, ...), custom_call_target="tpu_custom_call" | custom-call | flops 1000 | bytes 1000 | tf_op jit(solution)/shard_map/own_frames/pallas_call | solution.py:360
  49.4 6.1 %collective-permute-done.9.refs_2_ = bf16[4,64,256]{2,1,0:T(8,128)(2,1)S(1)} collective-permute-done((bf16[4,64,256]{2,1,0:T(8,128)(2,1)S(1)}, bf16[4,64,256]{2,1,0:T(8,128)(2,1)S(1)}, u32[]{:S(2)}, u32[]{:S(2)}) %collective-permute-start.9) | collective-permute-done | bytes 131104 | tf_op jit(solution)/shard_map/ppermute | solution.py:550
  58.3 2.4 %collective-permute-done.10.refs_1_ = f32[64,128]{1,0:T(8,128)S(1)} collective-permute-done((f32[64,128]{1,0:T(8,128)S(1)}, f32[64,128]{1,0:T(8,128)S(1)}, u32[]{:S(2)}, u32[]{:S(2)}) %collective-permute-start.10) | collective-permute-done | bytes 32800 | tf_op jit(solution)/shard_map/ppermute | solution.py:550
  60.9 2.5 %collective-permute-start.12 = (f32[64,64]{1,0:T(8,128)S(1)}, f32[64,64]{1,0:T(8,128)S(1)}, u32[]{:S(2)}, u32[]{:S(2)}) collective-permute-start(f32[64,64]{1,0:T(8,128)S(1)} %get-tuple-element.63.refs_1_.refs_0_), channel_id=1, source_target_pairs={{0,2},{1,3},{2,0},{3,1},{4,6},{5,7},{6,4},{7,5},{8,10},{9,11},{10,... | collective-permute-start | bytes 49160 | tf_op jit(solution)/shard_map/ppermute | solution.py:550
  63.3 1.9 %collective-permute-start.13 = (f32[64,64]{1,0:T(8,128)S(1)}, f32[64,64]{1,0:T(8,128)S(1)}, u32[]{:S(2)}, u32[]{:S(2)}) collective-permute-start(f32[64,64]{1,0:T(8,128)S(1)} %get-tuple-element.63.refs_1_.refs_0_), channel_id=1, source_target_pairs={{0,3},{1,2},{2,1},{3,0},{4,7},{5,6},{6,5},{7,4},{8,11},{9,10},{10,... | collective-permute-start | bytes 49160 | tf_op jit(solution)/shard_map/ppermute | solution.py:550
  65.7 2.6 %first_inverse.1.refs_4_ = f32[64,64]{1,0:T(8,128)S(1)} custom-call(f32[64,64]{1,0:T(8,128)S(1)} %get-tuple-element.53.v_gram_ref, f32[64,64]{1,0:T(8,128)S(1)} %get-tuple-element.64.w_gram_ref, f32[8,128]{1,0:T(8,128)S(1)} %get-tuple-element.65.after_ref.refs_1_), custom_call_target="tpu_custom_call" | custom-call | flops 1000 | bytes 1000 | tf_op jit(solution)/shard_map/first_inverse/pallas_call | solution.py:265
  74.9 2.7 %second_inverse.1 = (f32[64,64]{1,0:T(8,128)S(1)}, f32[64,64]{1,0:T(8,128)S(1)}) custom-call(f32[64,64]{1,0:T(8,128)S(1)} %get-tuple-element.88.h_ref, f32[64,64]{1,0:T(8,128)S(1)} %get-tuple-element.64.w_gram_ref), custom_call_target="tpu_custom_call" | custom-call | flops 1000 | bytes 1000 | tf_op jit(solution)/shard_map/second_inverse/pallas_call | solution.py:450
  80.4 3.2 %next_v.1 = (f32[64,1024]{1,0:T(8,128)}, f32[64,128]{1,0:T(8,128)S(1)}) custom-call(s32[1]{0:T(128)} %bitcast.place, f32[64,512]{1,0:T(8,128)S(1)} %add_terms.5.own_ref, f32[64,512]{1,0:T(8,128)S(1)} %collective-permute-done.19.other_ref, f32[64,64]{1,0:T(8,128)S(1)} %get-tuple-element.89.refs_0_.inverse_ref, f32[64,64]{1,0:T(8,128)S(1)} %get-tuple-element.88.h_ref, ...), custom_call_target="tpu_custom_call" | custom-call | flops 1000 | bytes 1000 | tf_op jit(solution)/shard_map/next_v/pallas_call | solution.py:514
  83.7 2.5 %collective-permute-start.21 = (f32[64,128]{1,0:T(8,128)S(1)}, f32[64,128]{1,0:T(8,128)S(1)}, u32[]{:S(2)}, u32[]{:S(2)}) collective-permute-start(f32[64,128]{1,0:T(8,128)S(1)} %get-tuple-element.91.refs_0_), channel_id=1, source_target_pairs={{0,2},{1,3},{2,0},{3,1},{4,6},{5,7},{6,4},{7,5},{8,10},{9,11},{10,... | collective-permute-start | bytes 98312 | tf_op jit(solution)/shard_map/ppermute | solution.py:550
  86.1 1.9 %collective-permute-start.22 = (f32[64,128]{1,0:T(8,128)S(1)}, f32[64,128]{1,0:T(8,128)S(1)}, u32[]{:S(2)}, u32[]{:S(2)}) collective-permute-start(f32[64,128]{1,0:T(8,128)S(1)} %get-tuple-element.91.refs_0_), channel_id=1, source_target_pairs={{0,3},{1,2},{2,1},{3,0},{4,7},{5,6},{6,5},{7,4},{8,11},{9,10},{10,... | collective-permute-start | bytes 98312 | tf_op jit(solution)/shard_map/ppermute | solution.py:550
  89.1 2.8 %collective-permute-done.22.refs_3_ = f32[64,128]{1,0:T(8,128)S(1)} collective-permute-done((f32[64,128]{1,0:T(8,128)S(1)}, f32[64,128]{1,0:T(8,128)S(1)}, u32[]{:S(2)}, u32[]{:S(2)}) %collective-permute-start.22) | collective-permute-done | bytes 32800 | tf_op jit(solution)/shard_map/ppermute | solution.py:550
  91.8 3.4 %next_w.1 = f32[32,64]{1,0:T(8,128)} custom-call(f32[64,128]{1,0:T(8,128)S(1)} %get-tuple-element.91.refs_0_, f32[64,128]{1,0:T(8,128)S(1)} %collective-permute-done.20.refs_1_, f32[64,128]{1,0:T(8,128)S(1)} %collective-permute-done.21.refs_2_, f32[64,128]{1,0:T(8,128)S(1)} %collective-permute-done.22.refs_3_, f32[64,64]{1,0:T(8,128)S(1)} %get-tuple-element.92.refs_4_), custom_call_target="tpu_custom_call" | custom-call | flops 1000 | bytes 1000 | tf_op jit(solution)/shard_map/next_w/pallas_call | solution.py:539
  (54 shorter events, 21.0 us)
Async XLA Ops:
  3.5 15.5 %collective-permute-start = (s16[304,256]{1,0:T(8,128)(2,1)S(1)}, s16[304,256]{1,0:T(8,128)(2,1)S(1)}, u32[]{:S(2)}, u32[]{:S(2)}) collective-permute-start(s16[304,256]{1,0:T(8,128)(2,1)S(1)} %project_first.1), channel_id=1, source_target_pairs={{0,3},{1,2},{2,1},{3,0},{4,7},{5,6},{6,5},{7,4},{8,11},{9,10},{10,... | collective-permute-start | bytes 466952 | tf_op jit(solution)/shard_map/ppermute | solution.py:550
  10.3 18.5 %collective-permute-start.1 = (s16[304,256]{1,0:T(8,128)(2,1)S(1)}, s16[304,256]{1,0:T(8,128)(2,1)S(1)}, u32[]{:S(2)}, u32[]{:S(2)}) collective-permute-start(s16[304,256]{1,0:T(8,128)(2,1)S(1)} %get-tuple-element.51), channel_id=1, source_target_pairs={{0,2},{1,3},{2,0},{3,1},{4,6},{5,7},{6,4},{7,5},{8,10},{9,11},{10,... | collective-permute-start | bytes 466952 | tf_op jit(solution)/shard_map/ppermute | solution.py:550
  14.5 14.3 %copy-start.4 = (s32[32]{0:T(128)S(1)}, s32[32]{0:T(128)}, u32[]{:S(2)}) copy-start(s32[32]{0:T(128)} %counts_ref.3) | copy-start | bytes 388
  14.5 14.3 %collective-permute-start.2 = (s16[304,256]{1,0:T(8,128)(2,1)S(1)}, s16[304,256]{1,0:T(8,128)(2,1)S(1)}, u32[]{:S(2)}, u32[]{:S(2)}) collective-permute-start(s16[304,256]{1,0:T(8,128)(2,1)S(1)} %get-tuple-element.52), channel_id=1, source_target_pairs={{0,1},{1,0},{2,3},{3,2},{4,5},{5,4},{6,7},{7,6},{8,9},{9,8},{10,11... | collective-permute-start | bytes 466952 | tf_op jit(solution)/shard_map/ppermute | solution.py:550
  17.1 19.6 %collective-permute-start.3 = (s16[272,256]{1,0:T(8,128)(2,1)S(1)}, s16[272,256]{1,0:T(8,128)(2,1)S(1)}, u32[]{:S(2)}, u32[]{:S(2)}) collective-permute-start(s16[272,256]{1,0:T(8,128)(2,1)S(1)} %project_send.5), channel_id=1, source_target_pairs={{0,3},{1,2},{2,1},{3,0},{4,7},{5,6},{6,5},{7,4},{8,11},{9,10},{10,... | collective-permute-start | bytes 417800 | tf_op jit(solution)/shard_map/ppermute | solution.py:550
  17.4 21.2 %collective-permute-start.4 = (s16[272,256]{1,0:T(8,128)(2,1)S(1)}, s16[272,256]{1,0:T(8,128)(2,1)S(1)}, u32[]{:S(2)}, u32[]{:S(2)}) collective-permute-start(s16[272,256]{1,0:T(8,128)(2,1)S(1)} %get-tuple-element.56), channel_id=1, source_target_pairs={{0,2},{1,3},{2,0},{3,1},{4,6},{5,7},{6,4},{7,5},{8,10},{9,11},{10,... | collective-permute-start | bytes 417800 | tf_op jit(solution)/shard_map/ppermute | solution.py:550
  19.0 19.5 %collective-permute-start.5 = (s16[272,256]{1,0:T(8,128)(2,1)S(1)}, s16[272,256]{1,0:T(8,128)(2,1)S(1)}, u32[]{:S(2)}, u32[]{:S(2)}) collective-permute-start(s16[272,256]{1,0:T(8,128)(2,1)S(1)} %get-tuple-element.57), channel_id=1, source_target_pairs={{0,1},{1,0},{2,3},{3,2},{4,5},{5,4},{6,7},{7,6},{8,9},{9,8},{10,11... | collective-permute-start | bytes 417800 | tf_op jit(solution)/shard_map/ppermute | solution.py:550
  35.0 12.6 %collective-permute-start.7 = (bf16[4,64,256]{2,1,0:T(8,128)(2,1)S(1)}, bf16[4,64,256]{2,1,0:T(8,128)(2,1)S(1)}, u32[]{:S(2)}, u32[]{:S(2)}) collective-permute-start(bf16[4,64,256]{2,1,0:T(8,128)(2,1)S(1)} %get-tuple-element.59.refs_0_), channel_id=1, source_target_pairs={{0,1},{1,0},{2,3},{3,2},{4,5},{5,4},{6,7},{7,6},{8,9},{9,8},{10,11... | collective-permute-start | bytes 393224 | tf_op jit(solution)/shard_map/ppermute | solution.py:550
  35.1 13.4 %collective-permute-start.8 = (bf16[4,64,256]{2,1,0:T(8,128)(2,1)S(1)}, bf16[4,64,256]{2,1,0:T(8,128)(2,1)S(1)}, u32[]{:S(2)}, u32[]{:S(2)}) collective-permute-start(bf16[4,64,256]{2,1,0:T(8,128)(2,1)S(1)} %get-tuple-element.59.refs_0_), channel_id=1, source_target_pairs={{0,3},{1,2},{2,1},{3,0},{4,7},{5,6},{6,5},{7,4},{8,11},{9,10},{10,... | collective-permute-start | bytes 393224 | tf_op jit(solution)/shard_map/ppermute | solution.py:550
  36.7 18.8 %collective-permute-start.9 = (bf16[4,64,256]{2,1,0:T(8,128)(2,1)S(1)}, bf16[4,64,256]{2,1,0:T(8,128)(2,1)S(1)}, u32[]{:S(2)}, u32[]{:S(2)}) collective-permute-start(bf16[4,64,256]{2,1,0:T(8,128)(2,1)S(1)} %get-tuple-element.59.refs_0_), channel_id=1, source_target_pairs={{0,2},{1,3},{2,0},{3,1},{4,6},{5,7},{6,4},{7,5},{8,10},{9,11},{10,... | collective-permute-start | bytes 393224 | tf_op jit(solution)/shard_map/ppermute | solution.py:550
  45.0 18.4 %collective-permute-start.14 = (bf16[4,64,256]{2,1,0:T(8,128)(2,1)S(1)}, bf16[4,64,256]{2,1,0:T(8,128)(2,1)S(1)}, u32[]{:S(2)}, u32[]{:S(2)}) collective-permute-start(bf16[4,64,256]{2,1,0:T(8,128)(2,1)S(1)} %get-tuple-element.60.refs_1_), channel_id=1, source_target_pairs={{0,1},{1,0},{2,3},{3,2},{4,5},{5,4},{6,7},{7,6},{8,9},{9,8},{10,11... | collective-permute-start | bytes 393224 | tf_op jit(solution)/shard_map/ppermute | solution.py:550
  46.0 22.3 %collective-permute-start.16 = (bf16[4,64,256]{2,1,0:T(8,128)(2,1)S(1)}, bf16[4,64,256]{2,1,0:T(8,128)(2,1)S(1)}, u32[]{:S(2)}, u32[]{:S(2)}) collective-permute-start(bf16[4,64,256]{2,1,0:T(8,128)(2,1)S(1)} %get-tuple-element.60.refs_1_), channel_id=1, source_target_pairs={{0,3},{1,2},{2,1},{3,0},{4,7},{5,6},{6,5},{7,4},{8,11},{9,10},{10,... | collective-permute-start | bytes 393224 | tf_op jit(solution)/shard_map/ppermute | solution.py:550
  47.6 21.3 %collective-permute-start.15 = (bf16[4,64,256]{2,1,0:T(8,128)(2,1)S(1)}, bf16[4,64,256]{2,1,0:T(8,128)(2,1)S(1)}, u32[]{:S(2)}, u32[]{:S(2)}) collective-permute-start(bf16[4,64,256]{2,1,0:T(8,128)(2,1)S(1)} %get-tuple-element.60.refs_1_), channel_id=1, source_target_pairs={{0,2},{1,3},{2,0},{3,1},{4,6},{5,7},{6,4},{7,5},{8,10},{9,11},{10,... | collective-permute-start | bytes 393224 | tf_op jit(solution)/shard_map/ppermute | solution.py:550
  48.5 8.2 %collective-permute-start.6 = (f32[64,128]{1,0:T(8,128)S(1)}, f32[64,128]{1,0:T(8,128)S(1)}, u32[]{:S(2)}, u32[]{:S(2)}) collective-permute-start(f32[64,128]{1,0:T(8,128)S(1)} %get-tuple-element.58.a_ref), channel_id=1, source_target_pairs={{0,4},{4,0},{8,12},{12,8},{1,5},{5,1},{9,13},{13,9},{2,6},{6,2},{1... | collective-permute-start | bytes 98312 | tf_op jit(solution)/shard_map/ppermute | solution.py:550
  56.8 4.0 %collective-permute-start.10 = (f32[64,128]{1,0:T(8,128)S(1)}, f32[64,128]{1,0:T(8,128)S(1)}, u32[]{:S(2)}, u32[]{:S(2)}) collective-permute-start(f32[64,128]{1,0:T(8,128)S(1)} %add_terms.3.refs_0_), channel_id=1, source_target_pairs={{0,8},{4,12},{8,0},{12,4},{1,9},{5,13},{9,1},{13,5},{2,10},{6,14},... | collective-permute-start | bytes 98312 | tf_op jit(solution)/shard_map/ppermute | solution.py:550
  60.8 8.5 %collective-permute-start.11 = (f32[64,64]{1,0:T(8,128)S(1)}, f32[64,64]{1,0:T(8,128)S(1)}, u32[]{:S(2)}, u32[]{:S(2)}) collective-permute-start(f32[64,64]{1,0:T(8,128)S(1)} %get-tuple-element.63.refs_1_.refs_0_), channel_id=1, source_target_pairs={{0,1},{1,0},{2,3},{3,2},{4,5},{5,4},{6,7},{7,6},{8,9},{9,8},{10,11... | collective-permute-start | bytes 49160 | tf_op jit(solution)/shard_map/ppermute | solution.py:550
  60.9 8.5 %collective-permute-start.12 = (f32[64,64]{1,0:T(8,128)S(1)}, f32[64,64]{1,0:T(8,128)S(1)}, u32[]{:S(2)}, u32[]{:S(2)}) collective-permute-start(f32[64,64]{1,0:T(8,128)S(1)} %get-tuple-element.63.refs_1_.refs_0_), channel_id=1, source_target_pairs={{0,2},{1,3},{2,0},{3,1},{4,6},{5,7},{6,4},{7,5},{8,10},{9,11},{10,... | collective-permute-start | bytes 49160 | tf_op jit(solution)/shard_map/ppermute | solution.py:550
  63.3 6.0 %collective-permute-start.13 = (f32[64,64]{1,0:T(8,128)S(1)}, f32[64,64]{1,0:T(8,128)S(1)}, u32[]{:S(2)}, u32[]{:S(2)}) collective-permute-start(f32[64,64]{1,0:T(8,128)S(1)} %get-tuple-element.63.refs_1_.refs_0_), channel_id=1, source_target_pairs={{0,3},{1,2},{2,1},{3,0},{4,7},{5,6},{6,5},{7,4},{8,11},{9,10},{10,... | collective-permute-start | bytes 49160 | tf_op jit(solution)/shard_map/ppermute | solution.py:550
  71.9 1.4 %collective-permute-start.17 = (f32[64,512]{1,0:T(8,128)S(1)}, f32[64,512]{1,0:T(8,128)S(1)}, u32[]{:S(2)}, u32[]{:S(2)}) collective-permute-start(f32[64,512]{1,0:T(8,128)S(1)} %get-tuple-element.87), channel_id=1, source_target_pairs={{0,4},{4,0},{8,12},{12,8},{1,5},{5,1},{9,13},{13,9},{2,6},{6,2},{1... | collective-permute-start | bytes 393224 | tf_op jit(solution)/shard_map/ppermute | solution.py:550
  73.4 5.6 %collective-permute-start.18 = (f32[64,512]{1,0:T(8,128)S(1)}, f32[64,512]{1,0:T(8,128)S(1)}, u32[]{:S(2)}, u32[]{:S(2)}) collective-permute-start(f32[64,512]{1,0:T(8,128)S(1)} %add_terms.4.a_ref), channel_id=1, source_target_pairs={{0,8},{4,12},{8,0},{12,4},{1,9},{5,13},{9,1},{13,5},{2,10},{6,14},... | collective-permute-start | bytes 393224 | tf_op jit(solution)/shard_map/ppermute | solution.py:550
  79.0 1.4 %collective-permute-start.19 = (f32[64,512]{1,0:T(8,128)S(1)}, f32[64,512]{1,0:T(8,128)S(1)}, u32[]{:S(2)}, u32[]{:S(2)}) collective-permute-start(f32[64,512]{1,0:T(8,128)S(1)} %add_terms.5.own_ref), channel_id=1, source_target_pairs={{0,4},{4,0},{8,12},{12,8},{1,5},{5,1},{9,13},{13,9},{2,6},{6,2},{1... | collective-permute-start | bytes 393224 | tf_op jit(solution)/shard_map/ppermute | solution.py:550
  83.6 4.4 %collective-permute-start.20 = (f32[64,128]{1,0:T(8,128)S(1)}, f32[64,128]{1,0:T(8,128)S(1)}, u32[]{:S(2)}, u32[]{:S(2)}) collective-permute-start(f32[64,128]{1,0:T(8,128)S(1)} %get-tuple-element.91.refs_0_), channel_id=1, source_target_pairs={{0,1},{1,0},{2,3},{3,2},{4,5},{5,4},{6,7},{7,6},{8,9},{9,8},{10,11... | collective-permute-start | bytes 98312 | tf_op jit(solution)/shard_map/ppermute | solution.py:550
  83.7 5.4 %collective-permute-start.21 = (f32[64,128]{1,0:T(8,128)S(1)}, f32[64,128]{1,0:T(8,128)S(1)}, u32[]{:S(2)}, u32[]{:S(2)}) collective-permute-start(f32[64,128]{1,0:T(8,128)S(1)} %get-tuple-element.91.refs_0_), channel_id=1, source_target_pairs={{0,2},{1,3},{2,0},{3,1},{4,6},{5,7},{6,4},{7,5},{8,10},{9,11},{10,... | collective-permute-start | bytes 98312 | tf_op jit(solution)/shard_map/ppermute | solution.py:550
  86.1 5.7 %collective-permute-start.22 = (f32[64,128]{1,0:T(8,128)S(1)}, f32[64,128]{1,0:T(8,128)S(1)}, u32[]{:S(2)}, u32[]{:S(2)}) collective-permute-start(f32[64,128]{1,0:T(8,128)S(1)} %get-tuple-element.91.refs_0_), channel_id=1, source_target_pairs={{0,3},{1,2},{2,1},{3,0},{4,7},{5,6},{6,5},{7,4},{8,11},{9,10},{10,... | collective-permute-start | bytes 98312 | tf_op jit(solution)/shard_map/ppermute | solution.py:550
  (4 other events, 41.5 us)

commit v10 on v9

--- a/solution.py
+++ b/solution.py
@@ -69,12 +69,12 @@
 SMEM_SPEC = pl.BlockSpec(memory_space=pltpu.SMEM)
 
 
-def exponent_rows(count):
-    return -(-(count + 1) // 16) * 16
-
-
-def payload_shape(count, rank, slots, with_gram):
-    return (count * rank + (rank // 2 if with_gram else 0) + exponent_rows(count), slots)
+def exponent_rows(total_count):
+    return -(-(total_count + 1) // 16) * 16
+
+
+def payload_shape(total_count, rank, slots, with_gram):
+    return (total_count * rank + (rank // 2 if with_gram else 0) + exponent_rows(total_count), slots)
 
 
 def row_exponent(x):
@@ -82,76 +82,88 @@
     return jnp.ceil(jnp.log2(jnp.maximum(top, 1e-30)))
 
 
-def decode(coded_ref, total_count, first, count, rank, with_gram):
-    def rows(start, number):
-        return coded_ref[pl.ds(start, number), :].astype(jnp.int32).astype(F32)
-
-    gram_rows = rank // 2 if with_gram else 0
-    exponents = rows(total_count * rank + gram_rows, exponent_rows(total_count))[:, :LANES].T
-    steps = jnp.exp2(exponents[:rank]) * (1.0 / LEVELS)
-    gram = None
-    if with_gram and first == 0:
-        digits = rows(total_count * rank, gram_rows)
+class Payload:
+    def __init__(self, ref, slots, count, rank, with_gram):
+        self.ref, self.slots, self.count, self.rank, self.with_gram = ref, slots, count, rank, with_gram
+        self.entries = len(slots) * count
+        gram_rows = rank // 2 if with_gram else 0
+        exponents = self.rows(self.entries * rank + gram_rows, exponent_rows(self.entries))
+        self.steps = jnp.exp2(exponents[:, :LANES].T[:rank]) * (1.0 / LEVELS)
+
+    def rows(self, first, number):
+        return self.ref[pl.ds(first, number), :].astype(jnp.int32).astype(F32)
+
+    def proj(self, slot, p):
+        entry = self.slots.index(slot) * self.count + p
+        return self.rows(entry * self.rank, self.rank) * self.steps[:, entry : entry + 1]
+
+    def gram(self):
+        rank = self.rank
+        digits = self.rows(self.entries * rank, rank // 2)
         digits = jnp.concatenate([digits[:, : 2 * rank], digits[:, 2 * rank :]], axis=0)
-        gram = (digits[:, :rank] + digits[:, rank:] * (0.5 / LEVELS)) * steps[:, total_count : total_count + 1]
-    return [rows(p * rank, rank) * steps[:, p : p + 1] for p in range(first, first + count)], gram
-
-
-def encode_gram(v_ref, coded_ref, first_row):
-    rank = v_ref.shape[0]
-    gram = low_dot(v_ref[...], v_ref[...], ROWS_BY_ROWS)
-    exponent = row_exponent(gram)
-    scaled = gram * (LEVELS / jnp.exp2(exponent))
-    whole = jnp.floor(scaled + 0.5)
-    rest = jnp.floor((scaled - whole) * (2 * LEVELS) + 0.5)
-    digits = jnp.concatenate([whole, rest], axis=1)
-    digits = jnp.concatenate([digits[: rank // 2], digits[rank // 2 :]], axis=1)
-    coded_ref[pl.ds(first_row, rank // 2), :] = digits.astype(jnp.int32).astype(jnp.int16)
-    return exponent
-
-
-def encode(patients, with_gram, v_ref, coded_ref):
-    count, rank = len(patients), v_ref.shape[0]
+        return (digits[:, :rank] + digits[:, rank:] * (0.5 / LEVELS)) * self.steps[:, self.entries : self.entries + 1]
+
+
+def encode(values, gram, coded_ref, rank):
+    count = len(values)
     lanes = lane_numbers((rank, LANES))
     exponents = jnp.zeros((rank, LANES), F32)
-    for p, visits in enumerate(patients):
-        proj = low_dot(v_ref[...], visits(), ROWS_BY_ROWS)
+    for p, value in enumerate(values):
+        proj = value()
         exponent = row_exponent(proj)
         coded = jnp.floor(proj * (LEVELS / jnp.exp2(exponent)) + 0.5)
         coded_ref[pl.ds(p * rank, rank), :] = coded.astype(jnp.int32).astype(jnp.int16)
         exponents = jnp.where(lanes == p, exponent, exponents)
     end = count * rank
-    if with_gram:
-        exponents = jnp.where(lanes == count, encode_gram(v_ref, coded_ref, end), exponents)
+    if gram is not None:
+        exponent = row_exponent(gram)
+        scaled = gram * (LEVELS / jnp.exp2(exponent))
+        whole = jnp.floor(scaled + 0.5)
+        rest = jnp.floor((scaled - whole) * (2 * LEVELS) + 0.5)
+        digits = jnp.concatenate([whole, rest], axis=1)
+        digits = jnp.concatenate([digits[: rank // 2], digits[rank // 2 :]], axis=1)
+        coded_ref[pl.ds(end, rank // 2), :] = digits.astype(jnp.int32).astype(jnp.int16)
+        exponents = jnp.where(lanes == count, exponent, exponents)
         end += rank // 2
     rows = exponent_rows(count)
     last = jnp.concatenate([exponents.T[:rows], jnp.zeros((rows, coded_ref.shape[1] - rank), F32)], axis=1)
     coded_ref[pl.ds(end, rows), :] = last.astype(jnp.int32).astype(jnp.int16)
 
 
-def first_projection_kernel(slot, place, v_hbm, visits_ref, coded_ref, v_ref, buffers, sem, v_sem):
-    count = buffers.shape[0]
+def first_projection_kernel(slots, place, v_hbm, visits_ref, coded_ref, v_ref, buffers, sems, v_sem):
+    count = buffers.shape[1]
     v_copy = pltpu.make_async_copy(v_hbm, v_ref, v_sem)
-    visits_copy = pltpu.make_async_copy(visits_ref.at[feature_of(place) ^ slot, pl.ds(0, count)], buffers, sem)
     v_copy.start()
-    visits_copy.start()
+    copies = [
+        pltpu.make_async_copy(visits_ref.at[feature_of(place) ^ slot, pl.ds(0, count)], buffers.at[i], sems.at[i])
+        for i, slot in enumerate(slots)
+    ]
+    for copy in copies:
+        copy.start()
     v_copy.wait()
-    visits_copy.wait()
-    encode([lambda p=p: buffers[p] for p in range(count)], True, v_ref, coded_ref)
-
-
-def first_projection(slot, count, place, visits, v_rows):
-    _, share, slots, width = visits.shape
+    gram = low_dot(v_ref[...], v_ref[...], ROWS_BY_ROWS)
+
+    def value(i, p):
+        if p == 0:
+            copies[i].wait()
+        return low_dot(v_ref[...], buffers[i, p], ROWS_BY_ROWS)
+
+    values = [functools.partial(value, i, p) for i in range(len(slots)) for p in range(count)]
+    encode(values, gram, coded_ref, v_ref.shape[0])
+
+
+def first_projection(slots, count, place, visits, v_rows):
+    width = visits.shape[3]
     rank = v_rows.shape[0]
     return pl.pallas_call(
-        functools.partial(first_projection_kernel, slot),
+        functools.partial(first_projection_kernel, slots),
         in_specs=[SMEM_SPEC, HBM_SPEC, HBM_SPEC],
         out_specs=VMEM_SPEC,
-        out_shape=jax.ShapeDtypeStruct(payload_shape(count, rank, slots, True), jnp.int16),
+        out_shape=jax.ShapeDtypeStruct(payload_shape(len(slots) * count, rank, visits.shape[2], True), jnp.int16),
         scratch_shapes=[
             pltpu.VMEM(v_rows.shape, BF16),
-            pltpu.VMEM((count, slots, width), BF16),
-            pltpu.SemaphoreType.DMA,
+            pltpu.VMEM((len(slots), count) + visits.shape[2:], BF16),
+            pltpu.SemaphoreType.DMA((len(slots),)),
             pltpu.SemaphoreType.DMA,
         ],
         compiler_params=parameters(LIMIT),
@@ -160,25 +172,36 @@
     )(place, v_rows, visits)
 
 
-def send_projection_kernel(slot, pieces, place, v_ref, visits_ref, *coded_refs):
-    owner = feature_of(place) ^ slot
-    for (first, count, with_gram), coded_ref in zip(pieces, coded_refs):
-        patients = [lambda p=p: visits_ref[owner, p] for p in range(first, first + count)]
-        encode(patients, with_gram, v_ref, coded_ref)
-
-
-def project_for(slot, pieces, place, visits, v_rows):
-    rank, slots = v_rows.shape[0], visits.shape[2]
-    shapes = [payload_shape(count, rank, slots, with_gram) for _, count, with_gram in pieces]
-    return pl.pallas_call(
-        functools.partial(send_projection_kernel, slot, pieces),
-        in_specs=[SMEM_SPEC, VMEM_SPEC, VMEM_SPEC],
-        out_specs=[VMEM_SPEC] * len(pieces),
-        out_shape=[jax.ShapeDtypeStruct(shape, jnp.int16) for shape in shapes],
-        compiler_params=parameters(LIMIT),
-        cost_estimate=SHORT,
-        name="project_send",
-    )(place, v_rows, visits)
+def next_projection_kernel(slots, first, count, layouts, place, v_ref, visits_ref, *refs):
+    *arrived, coded_ref = refs
+    rank = v_ref.shape[0]
+    arrived = [Payload(ref, layout, count, rank, first == 0) for ref, layout in zip(arrived, layouts)]
+
+    def value(slot, p):
+        proj = low_dot(v_ref[...], visits_ref[feature_of(place) ^ slot, first + p], ROWS_BY_ROWS)
+        for payload in arrived:
+            proj = proj + payload.proj(slot, p)
+        return proj
+
+    gram = None
+    if first == 0:
+        gram = low_dot(v_ref[...], v_ref[...], ROWS_BY_ROWS)
+        for payload in arrived:
+            gram = gram + payload.gram()
+    encode([functools.partial(value, slot, p) for slot in slots for p in range(count)], gram, coded_ref, rank)
+
+
+def next_projection(slots, first, count, layouts, place, visits, v_rows, arrived):
+    rank = v_rows.shape[0]
+    return pl.pallas_call(
+        functools.partial(next_projection_kernel, slots, first, count, layouts),
+        in_specs=[SMEM_SPEC] + [VMEM_SPEC] * (2 + len(arrived)),
+        out_specs=VMEM_SPEC,
+        out_shape=jax.ShapeDtypeStruct(payload_shape(len(slots) * count, rank, visits.shape[2], first == 0), jnp.int16),
+        compiler_params=parameters(LIMIT),
+        cost_estimate=SHORT,
+        name="project_next",
+    )(place, v_rows, visits, *arrived)
 
 
 def own_projection_kernel(place, v_ref, w_ref, visits_ref, *refs):
@@ -319,11 +342,11 @@
     first = feature_of(place) * share + part * count
     pieces = [own_ref[p] for p in patients]
     v_gram = v_gram_ref[...]
-    for code, (total_count, start, with_gram) in zip(coded, layouts):
-        arrived, gram = decode(code, total_count, start, count, rank, with_gram)
-        pieces = [a + b for a, b in zip(pieces, arrived)]
-        if gram is not None:
-            v_gram = v_gram + gram
+    for code, layout in zip(coded, layouts):
+        payload = Payload(code, layout, count, rank, part == 0)
+        pieces = [pieces[p] + payload.proj(0, p) for p in patients]
+        if part == 0:
+            v_gram = v_gram + payload.gram()
     v_total_ref[...] = v_gram
     for p in patients:
         proj[p] = pieces[p]
@@ -376,13 +399,36 @@
 def projected_kernel(items, place, visits_ref, *refs):
     frames_refs, outs, token_ref = refs[: len(items)], refs[-2 * len(items) - 1 : -1], refs[-1]
     token_ref[...] = jnp.zeros_like(token_ref)
-    for i, (slot, first) in enumerate(items):
-        owner = feature_of(place) ^ slot
-        count, rank, _ = frames_refs[i].shape
-        for p in range(count):
+    for i, (slots, first) in enumerate(items):
+        total_count, rank, _ = frames_refs[i].shape
+        count = total_count // len(slots)
+        for p in range(total_count):
             rows = pl.ds(p * rank, rank)
-            product = low_dot(frames_refs[i][p], visits_ref[owner, first + p])
+            owner = feature_of(place) ^ slots[p // count]
+            product = low_dot(frames_refs[i][p], visits_ref[owner, first + p % count])
             outs[2 * i][rows, :], outs[2 * i + 1][rows, :] = two_parts(product)
+
+
+def join_kernel(count, *refs):
+    out_ref = refs[-1]
+    first = 0
+    for part in refs[:count]:
+        out_ref[first : first + part.shape[0]] = part[...]
+        first += part.shape[0]
+
+
+def join(parts, after):
+    if len(parts) == 1:
+        return parts[0]
+    return pl.pallas_call(
+        functools.partial(join_kernel, len(parts)),
+        in_specs=[VMEM_SPEC] * len(parts) + [ANY_SPEC] * len(after),
+        out_specs=VMEM_SPEC,
+        out_shape=jax.ShapeDtypeStruct((sum(x.shape[0] for x in parts),) + parts[0].shape[1:], parts[0].dtype),
+        compiler_params=parameters(LIMIT),
+        cost_estimate=SHORT,
+        name="join_frames",
+    )(*parts, *after)
 
 
 def project_frames(items, place, frames, visits, after):
@@ -460,12 +506,17 @@
     *parts, keep_ref, send_ref, terms_ref = refs
     rank, width = terms_ref.shape
     half = width // 2
-    for i, (slot, first) in enumerate(items):
-        columns = pl.ds(first * rank, parts[2 * i].shape[0])
-        large = low_dot(factor_ref[slot, :, columns], parts[2 * i][...])
-        small = low_dot(factor_ref[slot, : 2 * rank, columns], parts[2 * i + 1][...])
-        terms = large[:rank] + (large[rank : 2 * rank] + small[:rank]) + (large[2 * rank :] + small[rank:])
-        terms_ref[...] = terms + terms_ref[...] if i else terms
+    total = None
+    for i, (slots, first) in enumerate(items):
+        count = parts[2 * i].shape[0] // len(slots)
+        columns = pl.ds(first * rank, count)
+        for k, slot in enumerate(slots):
+            rows = pl.ds(k * count, count)
+            large = low_dot(factor_ref[slot, :, columns], parts[2 * i][rows, :])
+            small = low_dot(factor_ref[slot, : 2 * rank, columns], parts[2 * i + 1][rows, :])
+            terms = large[:rank] + (large[rank : 2 * rank] + small[:rank]) + (large[2 * rank :] + small[rank:])
+            total = terms if total is None else total + terms
+    terms_ref[...] = total
     keep_ref[...] = terms_ref[:, pl.ds(pl.multiple_of(core_of(place) * half, half), half)]
     send_ref[...] = terms_ref[:, pl.ds(pl.multiple_of((1 - core_of(place)) * half, half), half)]
 
@@ -499,13 +550,14 @@
     gram = low_dot(v_parts[...], v_parts[...], ROWS_BY_ROWS)
     gram = gram[:rank, :rank] + (gram[:rank, rank:] + gram[rank:, :rank])
     sums_ref[...] = jnp.concatenate([jnp.zeros((rank, rank), F32), gram], axis=1)
-    for i, (slot, done) in enumerate(items):
+    for i, (slots, done) in enumerate(items):
         seen = low_dot(parts[2 * i][...], v_parts[...], ROWS_BY_ROWS)
         seen = seen + low_dot(parts[2 * i + 1][...], v_parts[...], ROWS_BY_ROWS)
-        first = (feature_of(place) ^ slot) * share + done
+        count = seen.shape[0] // rank // len(slots)
         for p in range(seen.shape[0] // rank):
+            patient = (feature_of(place) ^ slots[p // count]) * share + done + p % count
             row = jnp.sum(seen[p * rank : (p + 1) * rank] * weights, axis=0, keepdims=True)
-            sums_ref[pl.ds(first + p, 1), :rank] = row[:, :rank] + row[:, rank:]
+            sums_ref[pl.ds(patient, 1), :rank] = row[:, :rank] + row[:, rank:]
 
 
 def next_v(items, share, place, own, other, inverse, h_next, projected):
@@ -603,44 +655,59 @@
     n_parts = 2 if share % 2 == 0 else 1
     count = share // n_parts
     firsts = [part * count for part in range(n_parts)]
-    far = list(range(n - 1, 1, -1))
+    bits = [1 << i for i in range(n.bit_length() - 1)]
     v_near = v_start.T
 
-    sent = {(far[0], 0): first_projection(far[0], count, place, in_hbm, v_rows)}
-    for slot in far[1:] + [1]:
-        pieces = [(first, count, first == 0) for first in firsts]
-        codes = project_for(slot, pieces, place, by_owner, v_near)
-        sent |= {(slot, first): code for first, code in zip(firsts, codes)}
-    for first in firsts[1:]:
-        sent[far[0], first] = project_for(far[0], [(first, count, False)], place, by_owner, v_near)[0]
-    sent = {(slot, first): sent[slot, first] for first in firsts for slot in far + [1]}
-    arrived = {item: swap(code, "feature", item[0]) for item, code in sent.items()}
+    def send(bit):
+        return [slot for slot in range(n) if slot & bit and not slot & (bit - 1)]
+
+    def receive(bit):
+        return [slot ^ bit for slot in send(bit)]
+
+    arrived = [[] for _ in firsts]
+    for i, bit in enumerate(bits):
+        layouts = [receive(before) for before in bits[:i]]
+        for part, first in enumerate(firsts):
+            if i == 0 and part == 0:
+                code = first_projection(send(bit), count, place, in_hbm, v_rows)
+            else:
+                code = next_projection(send(bit), first, count, layouts, place, by_owner, v_near, arrived[part])
+            arrived[part] = arrived[part] + [swap(code, "feature", bit)]
     own, v_gram, h_local = project_own(n_parts, place, by_owner, v_near, w_start)
 
-    frames = {}
+    layouts = [receive(bit) for bit in bits]
+    frames = [[] for _ in firsts]
+
+    def double(part, after):
+        for bit in bits[::-1]:
+            slots = tuple(slot ^ bit for group, _ in frames[part] for slot in group)
+            frames[part].append((slots, swap(join([x for _, x in frames[part]], after), "feature", bit)))
+
+    def project_groups(groups, after):
+        arrays = {(frames[part][k][0], firsts[part]): frames[part][k][1] for part, k in groups}
+        return project_frames(list(arrays), place, arrays, by_owner, after)
+
     for part, first in enumerate(firsts):
-        layouts = [(count, 0, first == 0)] * (n - 1)
-        coded = [arrived[slot, first] for slot in far + [1]]
-        frames[0, first], h_local, v_total = own_frames(
-            layouts, part, n_parts, place, visit_counts, h_start, w_start, v_gram, h_local, own[part], coded
+        low, h_local, v_total = own_frames(
+            layouts, part, n_parts, place, visit_counts, h_start, w_start, v_gram, h_local, own[part], arrived[part]
         )
         v_gram = v_total if first == 0 else v_gram
-        for slot in far + [1]:
-            frames[slot, first] = swap(frames[0, first], "feature", slot)
-
-    projected, token = project_frames([(0, first) for first in firsts], place, frames, by_owner, [])
-    for first in firsts[:-1]:
-        more, token = project_frames([(slot, first) for slot in [1] + far], place, frames, by_owner, [token])
+        frames[part].append(((0,), low))
+        if part < n_parts - 1:
+            double(part, [])
+
+    last = len(bits)
+    projected, token = project_groups([(part, 0) for part in range(n_parts)], [])
+    h_sums = staged_terms(h_local, "patient", [token])
+    double(n_parts - 1, h_sums[:1])
+    h_sum, w_gram = sum_h(h_sums, token)
+    h_terms = all_terms(h_sum, "feature")
+    order = [(part, k) for part in range(n_parts) for k in range(1, last + 1)]
+    for group in order:
+        more, token = project_groups([group], [token])
         projected |= more
-    h_sum, w_gram = sum_h(staged_terms(h_local, "patient", [token]), token)
-    h_terms = all_terms(h_sum, "feature")
-    after = h_sum
-    for slot in [1] + far:
-        more, token = project_frames([(slot, firsts[-1])], place, frames, by_owner, [after])
-        projected |= more
-        if slot == 1:
+        if group == order[-2]:
             inverse = first_inverse(v_gram, w_gram, token)
-        after = token
     h_result, h_next, factor = next_h(place, h_terms, inverse, w_start, n, token)
 
     items = list(projected)

time: 95.4 us -> 91.3 us (0.957)
  waiting for transfers between devices: 22.1 us -> 15.1 us
  starting transfers between devices: 32.9 us -> 35.1 us
    ppermute x23 -> x19, waiting for transfers between devices: 22.1 us -> 15.1 us  [swap(): return lax.ppermute(x, axis, pairs)]
    ppermute x23 -> x19, starting transfers between devices: 32.9 us -> 35.1 us  [swap(): return lax.ppermute(x, axis, pairs)]
    pallas_call x4 -> x6, Pallas kernels: 7.05 us -> 7.48 us  [the longest x1 3.91 us: first_projection(): pl.pallas_call(functools.partial(first_projection_kernel, slots), in_spec...]
  transfers between devices with their start and end apart: 23 -> 19, of which waited for: 8 -> 9; matrix products, arithmetic and copies ran while one was open for 0% -> 0% of each run, Pallas kernels for 29% -> 29%
where the time goes in v10:
time: 91.3 us; the launch traced here: 91.1 us
  Pallas kernels  39.8 us (44%)
  starting transfers between devices  35.1 us (38%)
  waiting for transfers between devices  15.1 us (17%)
    ppermute x19, starting transfers between devices, swap(): return lax.ppermute(x, axis, pairs)  35.1 us
    ppermute x19, waiting for transfers between devices, swap(): return lax.ppermute(x, axis, pairs)  15.1 us
    pallas_call x2, Pallas kernels, own_frames(): pl.pallas_call(functools.partial(frames_kernel, layouts, part, share), in...  12.5 us
    pallas_call x1, Pallas kernels, first_projection(): pl.pallas_call(functools.partial(first_projection_kernel, slots), in_spec...  3.91 us
    pallas_call x5, Pallas kernels, project_frames(): pl.pallas_call(functools.partial(projected_kernel, items), in_specs=[SMEM...  3.61 us
    pallas_call x3, Pallas kernels, next_projection(): pl.pallas_call(functools.partial(next_projection_kernel, slots, first, co...  3.54 us
    pallas_call x1, Pallas kernels, next_w(): pl.pallas_call(functools.partial(next_w_kernel, len(sums)), out_shape=jax...  3.36 us
    pallas_call x1, Pallas kernels, next_v(): pl.pallas_call(functools.partial(next_v_kernel, items, share), in_specs=[...  3.28 us
  transfers between devices with their start and end apart: 19, of which 9 were waited for; matrix products, arithmetic and copies ran while one was open for 0% of the time, Pallas kernels for 29%

profile of v10, /device:TPU:0, one launch (start us, length us, event | category | flops | bytes accessed | tf_op | source)
XLA Modules:
  0.0 91.1 jit_solution(10624989627108531849)
XLA Ops:
  0.7 3.9 %project_first.1 = s16[560,256]{1,0:T(8,128)(2,1)S(1)} custom-call(s32[1]{0:T(128)} %bitcast.place, bf16[64,1024]{1,0:T(8,128)(2,1)} %bitcast.14, bf16[4,8,256,1024]{3,2,1,0:T(8,128)(2,1)} %bitcast.4), custom_call_target="tpu_custom_call" | custom-call | flops 1000 | bytes 1000 | tf_op jit(solution)/shard_map/project_first/pallas_call | solution.py:158
  4.6 3.0 %collective-permute-start = (s16[560,256]{1,0:T(8,128)(2,1)S(1)}, s16[560,256]{1,0:T(8,128)(2,1)S(1)}, u32[]{:S(2)}, u32[]{:S(2)}) collective-permute-start(s16[560,256]{1,0:T(8,128)(2,1)S(1)} %project_first.1), channel_id=1, source_target_pairs={{0,1},{1,0},{2,3},{3,2},{4,5},{5,4},{6,7},{7,6},{8,9},{9,8},{10,11... | collective-permute-start | bytes 860168 | tf_op jit(solution)/shard_map/ppermute | solution.py:602
  7.8 1.6 %project_next.4 = s16[528,256]{1,0:T(8,128)(2,1)S(1)} custom-call(s32[1]{0:T(128)} %bitcast.place, bf16[64,1024]{1,0:T(8,128)(2,1)S(1)} %bitcast.15, bf16[4,8,256,1024]{3,2,1,0:T(8,128)(2,1)S(1)} %bitcast.5), custom_call_target="tpu_custom_call" | custom-call | flops 1000 | bytes 1000 | tf_op jit(solution)/shard_map/project_next/pallas_call | solution.py:196
  9.4 3.1 %collective-permute-start.2 = (s16[528,256]{1,0:T(8,128)(2,1)S(1)}, s16[528,256]{1,0:T(8,128)(2,1)S(1)}, u32[]{:S(2)}, u32[]{:S(2)}) collective-permute-start(s16[528,256]{1,0:T(8,128)(2,1)S(1)} %project_next.4), channel_id=1, source_target_pairs={{0,1},{1,0},{2,3},{3,2},{4,5},{5,4},{6,7},{7,6},{8,9},{9,8},{10,11... | collective-permute-start | bytes 811016 | tf_op jit(solution)/shard_map/ppermute | solution.py:602
  12.4 2.8 %collective-permute-done.refs_0_ = s16[560,256]{1,0:T(8,128)(2,1)S(1)} collective-permute-done((s16[560,256]{1,0:T(8,128)(2,1)S(1)}, s16[560,256]{1,0:T(8,128)(2,1)S(1)}, u32[]{:S(2)}, u32[]{:S(2)}) %collective-permute-start) | collective-permute-done | bytes 286752 | tf_op jit(solution)/shard_map/ppermute | solution.py:602
  16.3 3.3 %collective-permute-start.1 = (s16[304,256]{1,0:T(8,128)(2,1)S(1)}, s16[304,256]{1,0:T(8,128)(2,1)S(1)}, u32[]{:S(2)}, u32[]{:S(2)}) collective-permute-start(s16[304,256]{1,0:T(8,128)(2,1)S(1)} %project_next.3), channel_id=1, source_target_pairs={{0,2},{1,3},{2,0},{3,1},{4,6},{5,7},{6,4},{7,5},{8,10},{9,11},{10,... | collective-permute-start | bytes 466952 | tf_op jit(solution)/shard_map/ppermute | solution.py:602
  19.6 3.4 %collective-permute-done.2.refs_0_ = s16[528,256]{1,0:T(8,128)(2,1)S(1)} collective-permute-done((s16[528,256]{1,0:T(8,128)(2,1)S(1)}, s16[528,256]{1,0:T(8,128)(2,1)S(1)}, u32[]{:S(2)}, u32[]{:S(2)}) %collective-permute-start.2) | collective-permute-done | bytes 270368 | tf_op jit(solution)/shard_map/ppermute | solution.py:602
  25.3 1.5 %project_own.1 = (f32[4,64,256]{2,1,0:T(8,128)S(1)}, f32[4,64,256]{2,1,0:T(8,128)S(1)}, f32[64,64]{1,0:T(8,128)S(1)}, f32[64,128]{1,0:T(8,128)S(1)}) custom-call(s32[1]{0:T(128)} %bitcast.place, bf16[64,1024]{1,0:T(8,128)(2,1)S(1)} %bitcast.18, f32[32,64]{1,0:T(8,128)S(1)} %copy-done.2, bf16[4,8,256,1024]{3,2,1,0:T(8,128)(2,1)S(1)} %bitcast.8), custom_call_target="tpu_custom_call" | custom-call | flops 1000 | bytes 1000 | tf_op jit(solution)/shard_map/project_own/pallas_call | solution.py:222
  26.9 6.2 %own_frames.2 = (bf16[4,64,256]{2,1,0:T(8,128)(2,1)S(1)}, f32[64,128]{1,0:T(8,128)S(1)}, f32[64,64]{1,0:T(8,128)S(1)}) custom-call(s32[1]{0:T(128)} %bitcast.place, s32[32]{0:T(128)S(1)} %copy-done.4, f32[64,64]{1,0:T(8,128)S(1)} %copy-done.3, f32[32,64]{1,0:T(8,128)S(1)} %copy-done.2, f32[64,64]{1,0:T(8,128)S(1)} %get-tuple-element.40.v_gram_ref, ...), custom_call_target="tpu_custom_call" | custom-call | flops 1000 | bytes 1000 | tf_op jit(solution)/shard_map/own_frames/pallas_call | solution.py:383
  33.1 1.7 %collective-permute-start.10 = (bf16[4,64,256]{2,1,0:T(8,128)(2,1)S(1)}, bf16[4,64,256]{2,1,0:T(8,128)(2,1)S(1)}, u32[]{:S(2)}, u32[]{:S(2)}) collective-permute-start(bf16[4,64,256]{2,1,0:T(8,128)(2,1)S(1)} %get-tuple-element.47.refs_0_), channel_id=1, source_target_pairs={{0,2},{1,3},{2,0},{3,1},{4,6},{5,7},{6,4},{7,5},{8,10},{9,11},{10,... | collective-permute-start | bytes 393224 | tf_op jit(solution)/shard_map/ppermute | solution.py:602
  34.7 6.3 %own_frames.3 = (bf16[4,64,256]{2,1,0:T(8,128)(2,1)S(1)}, f32[64,128]{1,0:T(8,128)S(1)}, f32[64,64]{1,0:T(8,128)}) custom-call(s32[1]{0:T(128)} %bitcast.place, s32[32]{0:T(128)S(1)} %copy-done.4, f32[64,64]{1,0:T(8,128)S(1)} %copy-done.3, f32[32,64]{1,0:T(8,128)S(1)} %copy-done.2, f32[64,64]{1,0:T(8,128)S(1)} %get-tuple-element.43.v_gram_ref, ...), custom_call_target="tpu_custom_call" | custom-call | flops 1000 | bytes 1000 | tf_op jit(solution)/shard_map/own_frames/pallas_call | solution.py:383
  42.5 3.3 %collective-permute-start.11 = (bf16[8,64,256]{2,1,0:T(8,128)(2,1)S(1)}, bf16[8,64,256]{2,1,0:T(8,128)(2,1)S(1)}, u32[]{:S(2)}, u32[]{:S(2)}) collective-permute-start(bf16[8,64,256]{2,1,0:T(8,128)(2,1)S(1)} %join_frames.2), channel_id=1, source_target_pairs={{0,1},{1,0},{2,3},{3,2},{4,5},{5,4},{6,7},{7,6},{8,9},{9,8},{10,11... | collective-permute-start | bytes 786440 | tf_op jit(solution)/shard_map/ppermute | solution.py:602
  47.0 6.0 %collective-permute-start.12 = (bf16[8,64,256]{2,1,0:T(8,128)(2,1)S(1)}, bf16[8,64,256]{2,1,0:T(8,128)(2,1)S(1)}, u32[]{:S(2)}, u32[]{:S(2)}) collective-permute-start(bf16[8,64,256]{2,1,0:T(8,128)(2,1)S(1)} %join_frames.3), channel_id=1, source_target_pairs={{0,1},{1,0},{2,3},{3,2},{4,5},{5,4},{6,7},{7,6},{8,9},{9,8},{10,11... | collective-permute-start | bytes 786440 | tf_op jit(solution)/shard_map/ppermute | solution.py:602
  53.0 1.5 %collective-permute-start.5 = (f32[64,128]{1,0:T(8,128)S(1)}, f32[64,128]{1,0:T(8,128)S(1)}, u32[]{:S(2)}, u32[]{:S(2)}) collective-permute-start(f32[64,128]{1,0:T(8,128)S(1)} %add_terms.3.refs_0_.refs_2_), channel_id=1, source_target_pairs={{0,8},{4,12},{8,0},{12,4},{1,9},{5,13},{9,1},{13,5},{2,10},{6,14},... | collective-permute-start | bytes 98312 | tf_op jit(solution)/shard_map/ppermute | solution.py:602
  54.5 2.4 %collective-permute-done.5.refs_1_ = f32[64,128]{1,0:T(8,128)S(1)} collective-permute-done((f32[64,128]{1,0:T(8,128)S(1)}, f32[64,128]{1,0:T(8,128)S(1)}, u32[]{:S(2)}, u32[]{:S(2)}) %collective-permute-start.5) | collective-permute-done | bytes 32800 | tf_op jit(solution)/shard_map/ppermute | solution.py:602
  57.1 4.3 %collective-permute-start.8 = (f32[64,64]{1,0:T(8,128)S(1)}, f32[64,64]{1,0:T(8,128)S(1)}, u32[]{:S(2)}, u32[]{:S(2)}) collective-permute-start(f32[64,64]{1,0:T(8,128)S(1)} %get-tuple-element.50.refs_0_), channel_id=1, source_target_pairs={{0,3},{1,2},{2,1},{3,0},{4,7},{5,6},{6,5},{7,4},{8,11},{9,10},{10,... | collective-permute-start | bytes 49160 | tf_op jit(solution)/shard_map/ppermute | solution.py:602
  63.3 2.6 %first_inverse.1.refs_4_ = f32[64,64]{1,0:T(8,128)S(1)} custom-call(f32[64,64]{1,0:T(8,128)S(1)} %get-tuple-element.43.v_gram_ref, f32[64,64]{1,0:T(8,128)S(1)} %get-tuple-element.51.w_gram_ref, f32[8,128]{1,0:T(8,128)S(1)} %get-tuple-element.54.after_ref.refs_1_), custom_call_target="tpu_custom_call" | custom-call | flops 1000 | bytes 1000 | tf_op jit(solution)/shard_map/first_inverse/pallas_call | solution.py:288
  67.8 1.6 %v_terms.1 = (f32[64,512]{1,0:T(8,128)S(1)}, f32[64,512]{1,0:T(8,128)S(1)}) custom-call(s32[1]{0:T(128)} %bitcast.place, bf16[4,192,512]{2,1,0:T(8,128)(2,1)S(1)} %get-tuple-element.57.factor_ref, bf16[256,1024]{1,0:T(8,128)(2,1)S(1)} %get-tuple-element.58.refs_0_, bf16[256,1024]{1,0:T(8,128)(2,1)S(1)} %get-tuple-element.59.refs_1_, ...), custom_call_target="tpu_custom_call" | custom-call | flops 1000 | bytes 1000 | tf_op jit(solution)/shard_map/v_terms/pallas_call | solution.py:528
  70.8 1.6 %collective-permute-start.14 = (f32[64,512]{1,0:T(8,128)S(1)}, f32[64,512]{1,0:T(8,128)S(1)}, u32[]{:S(2)}, u32[]{:S(2)}) collective-permute-start(f32[64,512]{1,0:T(8,128)S(1)} %add_terms.4.a_ref), channel_id=1, source_target_pairs={{0,8},{4,12},{8,0},{12,4},{1,9},{5,13},{9,1},{13,5},{2,10},{6,14},... | collective-permute-start | bytes 393224 | tf_op jit(solution)/shard_map/ppermute | solution.py:602
  72.4 2.7 %second_inverse.1 = (f32[64,64]{1,0:T(8,128)S(1)}, f32[64,64]{1,0:T(8,128)S(1)}) custom-call(f32[64,64]{1,0:T(8,128)S(1)} %get-tuple-element.72.h_ref, f32[64,64]{1,0:T(8,128)S(1)} %get-tuple-element.51.w_gram_ref), custom_call_target="tpu_custom_call" | custom-call | flops 1000 | bytes 1000 | tf_op jit(solution)/shard_map/second_inverse/pallas_call | solution.py:496
  77.9 3.3 %next_v.1 = (f32[64,1024]{1,0:T(8,128)}, f32[64,128]{1,0:T(8,128)S(1)}) custom-call(s32[1]{0:T(128)} %bitcast.place, f32[64,512]{1,0:T(8,128)S(1)} %add_terms.5.own_ref, f32[64,512]{1,0:T(8,128)S(1)} %collective-permute-done.15.other_ref, f32[64,64]{1,0:T(8,128)S(1)} %get-tuple-element.73.refs_0_.inverse_ref, f32[64,64]{1,0:T(8,128)S(1)} %get-tuple-element.72.h_ref, ...), custom_call_target="tpu_custom_call" | custom-call | flops 1000 | bytes 1000 | tf_op jit(solution)/shard_map/next_v/pallas_call | solution.py:566
  82.0 3.5 %collective-permute-start.18 = (f32[64,128]{1,0:T(8,128)S(1)}, f32[64,128]{1,0:T(8,128)S(1)}, u32[]{:S(2)}, u32[]{:S(2)}) collective-permute-start(f32[64,128]{1,0:T(8,128)S(1)} %get-tuple-element.75.refs_0_), channel_id=1, source_target_pairs={{0,3},{1,2},{2,1},{3,0},{4,7},{5,6},{6,5},{7,4},{8,11},{9,10},{10,... | collective-permute-start | bytes 98312 | tf_op jit(solution)/shard_map/ppermute | solution.py:602
  86.0 1.8 %collective-permute-done.18.refs_3_ = f32[64,128]{1,0:T(8,128)S(1)} collective-permute-done((f32[64,128]{1,0:T(8,128)S(1)}, f32[64,128]{1,0:T(8,128)S(1)}, u32[]{:S(2)}, u32[]{:S(2)}) %collective-permute-start.18) | collective-permute-done | bytes 32800 | tf_op jit(solution)/shard_map/ppermute | solution.py:602
  87.8 3.4 %next_w.1 = f32[32,64]{1,0:T(8,128)} custom-call(f32[64,128]{1,0:T(8,128)S(1)} %get-tuple-element.75.refs_0_, f32[64,128]{1,0:T(8,128)S(1)} %collective-permute-done.16.refs_1_, f32[64,128]{1,0:T(8,128)S(1)} %collective-permute-done.17.refs_2_, f32[64,128]{1,0:T(8,128)S(1)} %collective-permute-done.18.refs_3_, f32[64,64]{1,0:T(8,128)S(1)} %get-tuple-element.76.refs_4_), custom_call_target="tpu_custom_call" | custom-call | flops 1000 | bytes 1000 | tf_op jit(solution)/shard_map/next_w/pallas_call | solution.py:591
  (48 shorter events, 15.5 us)
Async XLA Ops:
  0.6 7.0 %copy-start.1 = (bf16[1024,64]{0,1:T(8,128)(2,1)S(1)}, bf16[1024,64]{0,1:T(8,128)(2,1)}, u32[]{:S(2)}) copy-start(bf16[1024,64]{0,1:T(8,128)(2,1)} %param.8) | copy-start | bytes 393220
  0.6 7.1 %copy-start = (bf16[32,256,1024]{2,1,0:T(8,128)(2,1)S(1)}, bf16[32,256,1024]{2,1,0:T(8,128)(2,1)}, u32[]{:S(2)}) copy-start(bf16[32,256,1024]{2,1,0:T(8,128)(2,1)} %param.5) | copy-start | bytes 50331652
  4.6 10.7 %collective-permute-start = (s16[560,256]{1,0:T(8,128)(2,1)S(1)}, s16[560,256]{1,0:T(8,128)(2,1)S(1)}, u32[]{:S(2)}, u32[]{:S(2)}) collective-permute-start(s16[560,256]{1,0:T(8,128)(2,1)S(1)} %project_first.1), channel_id=1, source_target_pairs={{0,1},{1,0},{2,3},{3,2},{4,5},{5,4},{6,7},{7,6},{8,9},{9,8},{10,11... | collective-permute-start | bytes 860168 | tf_op jit(solution)/shard_map/ppermute | solution.py:602
  9.4 15.9 %copy-start.2 = (f32[32,64]{1,0:T(8,128)S(1)}, f32[32,64]{1,0:T(8,128)}, u32[]{:S(2)}) copy-start(f32[32,64]{1,0:T(8,128)} %refs_5_.1) | copy-start | bytes 24580
  9.4 13.6 %collective-permute-start.2 = (s16[528,256]{1,0:T(8,128)(2,1)S(1)}, s16[528,256]{1,0:T(8,128)(2,1)S(1)}, u32[]{:S(2)}, u32[]{:S(2)}) collective-permute-start(s16[528,256]{1,0:T(8,128)(2,1)S(1)} %project_next.4), channel_id=1, source_target_pairs={{0,1},{1,0},{2,3},{3,2},{4,5},{5,4},{6,7},{7,6},{8,9},{9,8},{10,11... | collective-permute-start | bytes 811016 | tf_op jit(solution)/shard_map/ppermute | solution.py:602
  16.3 10.6 %copy-start.3 = (f32[64,64]{1,0:T(8,128)S(1)}, f32[64,64]{1,0:T(8,128)}, u32[]{:S(2)}) copy-start(f32[64,64]{1,0:T(8,128)} %h_ref.3) | copy-start | bytes 49156
  16.3 10.6 %copy-start.4 = (s32[32]{0:T(128)S(1)}, s32[32]{0:T(128)}, u32[]{:S(2)}) copy-start(s32[32]{0:T(128)} %counts_ref.3) | copy-start | bytes 388
  16.3 10.6 %collective-permute-start.1 = (s16[304,256]{1,0:T(8,128)(2,1)S(1)}, s16[304,256]{1,0:T(8,128)(2,1)S(1)}, u32[]{:S(2)}, u32[]{:S(2)}) collective-permute-start(s16[304,256]{1,0:T(8,128)(2,1)S(1)} %project_next.3), channel_id=1, source_target_pairs={{0,2},{1,3},{2,0},{3,1},{4,6},{5,7},{6,4},{7,5},{8,10},{9,11},{10,... | collective-permute-start | bytes 466952 | tf_op jit(solution)/shard_map/ppermute | solution.py:602
  23.9 10.8 %collective-permute-start.3 = (s16[272,256]{1,0:T(8,128)(2,1)S(1)}, s16[272,256]{1,0:T(8,128)(2,1)S(1)}, u32[]{:S(2)}, u32[]{:S(2)}) collective-permute-start(s16[272,256]{1,0:T(8,128)(2,1)S(1)} %project_next.5), channel_id=1, source_target_pairs={{0,2},{1,3},{2,0},{3,1},{4,6},{5,7},{6,4},{7,5},{8,10},{9,11},{10,... | collective-permute-start | bytes 417800 | tf_op jit(solution)/shard_map/ppermute | solution.py:602
  33.1 9.4 %collective-permute-start.10 = (bf16[4,64,256]{2,1,0:T(8,128)(2,1)S(1)}, bf16[4,64,256]{2,1,0:T(8,128)(2,1)S(1)}, u32[]{:S(2)}, u32[]{:S(2)}) collective-permute-start(bf16[4,64,256]{2,1,0:T(8,128)(2,1)S(1)} %get-tuple-element.47.refs_0_), channel_id=1, source_target_pairs={{0,2},{1,3},{2,0},{3,1},{4,6},{5,7},{6,4},{7,5},{8,10},{9,11},{10,... | collective-permute-start | bytes 393224 | tf_op jit(solution)/shard_map/ppermute | solution.py:602
  41.1 5.9 %collective-permute-start.9 = (bf16[4,64,256]{2,1,0:T(8,128)(2,1)S(1)}, bf16[4,64,256]{2,1,0:T(8,128)(2,1)S(1)}, u32[]{:S(2)}, u32[]{:S(2)}) collective-permute-start(bf16[4,64,256]{2,1,0:T(8,128)(2,1)S(1)} %get-tuple-element.48.refs_1_.refs_0_), channel_id=1, source_target_pairs={{0,2},{1,3},{2,0},{3,1},{4,6},{5,7},{6,4},{7,5},{8,10},{9,11},{10,... | collective-permute-start | bytes 393224 | tf_op jit(solution)/shard_map/ppermute | solution.py:602
  42.5 4.2 %collective-permute-start.4 = (f32[64,128]{1,0:T(8,128)S(1)}, f32[64,128]{1,0:T(8,128)S(1)}, u32[]{:S(2)}, u32[]{:S(2)}) collective-permute-start(f32[64,128]{1,0:T(8,128)S(1)} %get-tuple-element.46.a_ref), channel_id=1, source_target_pairs={{0,4},{4,0},{8,12},{12,8},{1,5},{5,1},{9,13},{13,9},{2,6},{6,2},{1... | collective-permute-start | bytes 98312 | tf_op jit(solution)/shard_map/ppermute | solution.py:602
  42.5 19.4 %collective-permute-start.11 = (bf16[8,64,256]{2,1,0:T(8,128)(2,1)S(1)}, bf16[8,64,256]{2,1,0:T(8,128)(2,1)S(1)}, u32[]{:S(2)}, u32[]{:S(2)}) collective-permute-start(bf16[8,64,256]{2,1,0:T(8,128)(2,1)S(1)} %join_frames.2), channel_id=1, source_target_pairs={{0,1},{1,0},{2,3},{3,2},{4,5},{5,4},{6,7},{7,6},{8,9},{9,8},{10,11... | collective-permute-start | bytes 786440 | tf_op jit(solution)/shard_map/ppermute | solution.py:602
  47.0 18.8 %collective-permute-start.12 = (bf16[8,64,256]{2,1,0:T(8,128)(2,1)S(1)}, bf16[8,64,256]{2,1,0:T(8,128)(2,1)S(1)}, u32[]{:S(2)}, u32[]{:S(2)}) collective-permute-start(bf16[8,64,256]{2,1,0:T(8,128)(2,1)S(1)} %join_frames.3), channel_id=1, source_target_pairs={{0,1},{1,0},{2,3},{3,2},{4,5},{5,4},{6,7},{7,6},{8,9},{9,8},{10,11... | collective-permute-start | bytes 786440 | tf_op jit(solution)/shard_map/ppermute | solution.py:602
  53.0 3.9 %collective-permute-start.5 = (f32[64,128]{1,0:T(8,128)S(1)}, f32[64,128]{1,0:T(8,128)S(1)}, u32[]{:S(2)}, u32[]{:S(2)}) collective-permute-start(f32[64,128]{1,0:T(8,128)S(1)} %add_terms.3.refs_0_.refs_2_), channel_id=1, source_target_pairs={{0,8},{4,12},{8,0},{12,4},{1,9},{5,13},{9,1},{13,5},{2,10},{6,14},... | collective-permute-start | bytes 98312 | tf_op jit(solution)/shard_map/ppermute | solution.py:602
  57.0 9.8 %collective-permute-start.6 = (f32[64,64]{1,0:T(8,128)S(1)}, f32[64,64]{1,0:T(8,128)S(1)}, u32[]{:S(2)}, u32[]{:S(2)}) collective-permute-start(f32[64,64]{1,0:T(8,128)S(1)} %get-tuple-element.50.refs_0_), channel_id=1, source_target_pairs={{0,1},{1,0},{2,3},{3,2},{4,5},{5,4},{6,7},{7,6},{8,9},{9,8},{10,11... | collective-permute-start | bytes 49160 | tf_op jit(solution)/shard_map/ppermute | solution.py:602
  57.1 9.7 %collective-permute-start.7 = (f32[64,64]{1,0:T(8,128)S(1)}, f32[64,64]{1,0:T(8,128)S(1)}, u32[]{:S(2)}, u32[]{:S(2)}) collective-permute-start(f32[64,64]{1,0:T(8,128)S(1)} %get-tuple-element.50.refs_0_), channel_id=1, source_target_pairs={{0,2},{1,3},{2,0},{3,1},{4,6},{5,7},{6,4},{7,5},{8,10},{9,11},{10,... | collective-permute-start | bytes 49160 | tf_op jit(solution)/shard_map/ppermute | solution.py:602
  57.1 9.7 %collective-permute-start.8 = (f32[64,64]{1,0:T(8,128)S(1)}, f32[64,64]{1,0:T(8,128)S(1)}, u32[]{:S(2)}, u32[]{:S(2)}) collective-permute-start(f32[64,64]{1,0:T(8,128)S(1)} %get-tuple-element.50.refs_0_), channel_id=1, source_target_pairs={{0,3},{1,2},{2,1},{3,0},{4,7},{5,6},{6,5},{7,4},{8,11},{9,10},{10,... | collective-permute-start | bytes 49160 | tf_op jit(solution)/shard_map/ppermute | solution.py:602
  69.4 1.4 %collective-permute-start.13 = (f32[64,512]{1,0:T(8,128)S(1)}, f32[64,512]{1,0:T(8,128)S(1)}, u32[]{:S(2)}, u32[]{:S(2)}) collective-permute-start(f32[64,512]{1,0:T(8,128)S(1)} %get-tuple-element.71), channel_id=1, source_target_pairs={{0,4},{4,0},{8,12},{12,8},{1,5},{5,1},{9,13},{13,9},{2,6},{6,2},{1... | collective-permute-start | bytes 393224 | tf_op jit(solution)/shard_map/ppermute | solution.py:602
  70.8 5.6 %collective-permute-start.14 = (f32[64,512]{1,0:T(8,128)S(1)}, f32[64,512]{1,0:T(8,128)S(1)}, u32[]{:S(2)}, u32[]{:S(2)}) collective-permute-start(f32[64,512]{1,0:T(8,128)S(1)} %add_terms.4.a_ref), channel_id=1, source_target_pairs={{0,8},{4,12},{8,0},{12,4},{1,9},{5,13},{9,1},{13,5},{2,10},{6,14},... | collective-permute-start | bytes 393224 | tf_op jit(solution)/shard_map/ppermute | solution.py:602
  76.5 1.4 %collective-permute-start.15 = (f32[64,512]{1,0:T(8,128)S(1)}, f32[64,512]{1,0:T(8,128)S(1)}, u32[]{:S(2)}, u32[]{:S(2)}) collective-permute-start(f32[64,512]{1,0:T(8,128)S(1)} %add_terms.5.own_ref), channel_id=1, source_target_pairs={{0,4},{4,0},{8,12},{12,8},{1,5},{5,1},{9,13},{13,9},{2,6},{6,2},{1... | collective-permute-start | bytes 393224 | tf_op jit(solution)/shard_map/ppermute | solution.py:602
  81.1 4.4 %collective-permute-start.16 = (f32[64,128]{1,0:T(8,128)S(1)}, f32[64,128]{1,0:T(8,128)S(1)}, u32[]{:S(2)}, u32[]{:S(2)}) collective-permute-start(f32[64,128]{1,0:T(8,128)S(1)} %get-tuple-element.75.refs_0_), channel_id=1, source_target_pairs={{0,1},{1,0},{2,3},{3,2},{4,5},{5,4},{6,7},{7,6},{8,9},{9,8},{10,11... | collective-permute-start | bytes 98312 | tf_op jit(solution)/shard_map/ppermute | solution.py:602
  81.2 4.8 %collective-permute-start.17 = (f32[64,128]{1,0:T(8,128)S(1)}, f32[64,128]{1,0:T(8,128)S(1)}, u32[]{:S(2)}, u32[]{:S(2)}) collective-permute-start(f32[64,128]{1,0:T(8,128)S(1)} %get-tuple-element.75.refs_0_), channel_id=1, source_target_pairs={{0,2},{1,3},{2,0},{3,1},{4,6},{5,7},{6,4},{7,5},{8,10},{9,11},{10,... | collective-permute-start | bytes 98312 | tf_op jit(solution)/shard_map/ppermute | solution.py:602
  82.0 5.7 %collective-permute-start.18 = (f32[64,128]{1,0:T(8,128)S(1)}, f32[64,128]{1,0:T(8,128)S(1)}, u32[]{:S(2)}, u32[]{:S(2)}) collective-permute-start(f32[64,128]{1,0:T(8,128)S(1)} %get-tuple-element.75.refs_0_), channel_id=1, source_target_pairs={{0,3},{1,2},{2,1},{3,0},{4,7},{5,6},{6,5},{7,4},{8,11},{9,10},{10,... | collective-permute-start | bytes 98312 | tf_op jit(solution)/shard_map/ppermute | solution.py:602

commit v11 on v10

--- a/solution.py
+++ b/solution.py
@@ -173,9 +173,9 @@
 
 
 def next_projection_kernel(slots, first, count, layouts, place, v_ref, visits_ref, *refs):
-    *arrived, coded_ref = refs
+    coded_ref = refs[-1]
     rank = v_ref.shape[0]
-    arrived = [Payload(ref, layout, count, rank, first == 0) for ref, layout in zip(arrived, layouts)]
+    arrived = [Payload(ref, layout, count, rank, first == 0) for ref, layout in zip(refs, layouts)]
 
     def value(slot, p):
         proj = low_dot(v_ref[...], visits_ref[feature_of(place) ^ slot, first + p], ROWS_BY_ROWS)
@@ -191,44 +191,58 @@
     encode([functools.partial(value, slot, p) for slot in slots for p in range(count)], gram, coded_ref, rank)
 
 
-def next_projection(slots, first, count, layouts, place, visits, v_rows, arrived):
+def next_projection(slots, first, count, layouts, place, visits, v_rows, arrived, after):
     rank = v_rows.shape[0]
     return pl.pallas_call(
         functools.partial(next_projection_kernel, slots, first, count, layouts),
-        in_specs=[SMEM_SPEC] + [VMEM_SPEC] * (2 + len(arrived)),
+        in_specs=[SMEM_SPEC] + [VMEM_SPEC] * (2 + len(arrived)) + [ANY_SPEC] * len(after),
         out_specs=VMEM_SPEC,
         out_shape=jax.ShapeDtypeStruct(payload_shape(len(slots) * count, rank, visits.shape[2], first == 0), jnp.int16),
         compiler_params=parameters(LIMIT),
         cost_estimate=SHORT,
         name="project_next",
-    )(place, v_rows, visits, *arrived)
-
-
-def own_projection_kernel(place, v_ref, w_ref, visits_ref, *refs):
-    *proj_refs, v_gram_ref, w_gram_ref = refs
+    )(place, v_rows, visits, *arrived, *after)
+
+
+def w_gram_kernel(w_ref, gram_ref):
+    gram_ref[...] = high_dot(w_ref[...], w_ref[...], COLS_BY_COLS)
+
+
+def own_w_gram(w_start):
+    rank = w_start.shape[1]
+    return pl.pallas_call(
+        w_gram_kernel,
+        in_specs=[VMEM_SPEC],
+        out_specs=VMEM_SPEC,
+        out_shape=jax.ShapeDtypeStruct((rank, rank), F32),
+        compiler_params=parameters(LIMIT),
+        cost_estimate=SHORT,
+        name="own_w_gram",
+    )(w_start)
+
+
+def own_projection_kernel(place, v_ref, visits_ref, *refs):
+    *proj_refs, v_gram_ref = refs
     count = visits_ref.shape[1] // len(proj_refs)
     for p in range(visits_ref.shape[1]):
         proj_refs[p // count][p % count] = low_dot(v_ref[...], visits_ref[feature_of(place), p], ROWS_BY_ROWS)
     v_gram_ref[...] = low_dot(v_ref[...], v_ref[...], ROWS_BY_ROWS)
-    w_gram = high_dot(w_ref[...], w_ref[...], COLS_BY_COLS)
-    w_gram_ref[...] = jnp.concatenate([jnp.zeros_like(w_gram), w_gram], axis=1)
-
-
-def project_own(n_parts, place, visits, v_rows, w_start):
+
+
+def project_own(n_parts, place, visits, v_rows):
     _, share, slots, width = visits.shape
     rank = v_rows.shape[0]
-    gram = jax.ShapeDtypeStruct((rank, rank), F32)
     proj = jax.ShapeDtypeStruct((share // n_parts, rank, slots), F32)
-    *own, v_gram, w_gram = pl.pallas_call(
+    *own, v_gram = pl.pallas_call(
         own_projection_kernel,
-        in_specs=[SMEM_SPEC] + [VMEM_SPEC] * 3,
-        out_specs=[VMEM_SPEC] * (n_parts + 2),
-        out_shape=[proj] * n_parts + [gram, jax.ShapeDtypeStruct((rank, 2 * rank), F32)],
+        in_specs=[SMEM_SPEC] + [VMEM_SPEC] * 2,
+        out_specs=[VMEM_SPEC] * (n_parts + 1),
+        out_shape=[proj] * n_parts + [jax.ShapeDtypeStruct((rank, rank), F32)],
         compiler_params=parameters(LIMIT),
         cost_estimate=SHORT,
         name="project_own",
-    )(place, v_rows, w_start, visits)
-    return own, v_gram, w_gram
+    )(place, v_rows, visits)
+    return own, v_gram
 
 
 def pair_inverse(a, b, c, d):
@@ -280,41 +294,24 @@
     return out
 
 
-def first_inverse_kernel(v_gram_ref, w_gram_ref, after_ref, inverse_ref):
-    inverse_ref[...] = inverse_of(w_gram_ref[...] * v_gram_ref[...])
-
-
-def first_inverse(v_gram, w_gram, after):
+def first_inverse_kernel(v_gram_ref, *refs):
+    *terms, w_gram_ref, inverse_ref = refs
+    w_gram = total(terms)
+    w_gram_ref[...] = w_gram
+    inverse_ref[...] = inverse_of(w_gram * v_gram_ref[...])
+
+
+def first_inverse(v_gram, w_grams):
+    out = jax.ShapeDtypeStruct(v_gram.shape, F32)
     return pl.pallas_call(
         first_inverse_kernel,
-        in_specs=[VMEM_SPEC] * 2 + [ANY_SPEC],
-        out_specs=VMEM_SPEC,
-        out_shape=jax.ShapeDtypeStruct(w_gram.shape, F32),
+        in_specs=[VMEM_SPEC] * (1 + len(w_grams)),
+        out_specs=[VMEM_SPEC] * 2,
+        out_shape=[out, out],
         compiler_params=parameters(LIMIT),
         cost_estimate=SHORT,
         name="first_inverse",
-    )(v_gram, w_gram, after)
-
-
-def sum_h_kernel(n_terms, *refs):
-    h_ref, w_gram_ref = refs[n_terms + 1 :]
-    rank = h_ref.shape[0]
-    both = total(refs[:n_terms])
-    h_ref[...] = both[:, :rank]
-    w_gram_ref[...] = both[:, rank:]
-
-
-def sum_h(terms, after):
-    rank = terms[0].shape[0]
-    return pl.pallas_call(
-        functools.partial(sum_h_kernel, len(terms)),
-        in_specs=[VMEM_SPEC] * len(terms) + [ANY_SPEC],
-        out_specs=[VMEM_SPEC] * 2,
-        out_shape=[jax.ShapeDtypeStruct((rank, rank), F32)] * 2,
-        compiler_params=parameters(LIMIT),
-        cost_estimate=SHORT,
-        name="sum_h",
-    )(*terms, after)
+    )(v_gram, *w_grams)
 
 
 def sweep_all(frames, rank, fine):
@@ -369,12 +366,11 @@
         frames_ref[p] = low[p]
     products = [jnp.concatenate(three_parts(proj[p]), axis=0) for p in patients]
     products = [low_dot(low[p], products[p], ROWS_BY_ROWS) for p in patients]
-    before = before_ref[...]
-    terms = before[:, :rank]
+    terms = before_ref[...] if part else jnp.zeros((rank, rank), F32)
     for p in patients:
         product = products[p][:, :rank] + (products[p][:, rank : 2 * rank] + products[p][:, 2 * rank :])
         terms = terms + product * weights[p]
-    terms_ref[...] = jnp.concatenate([terms, before[:, rank:]], axis=1)
+    terms_ref[...] = terms
 
 
 def own_frames(layouts, part, n_parts, place, counts, h_start, w_start, v_gram, before, own, coded):
@@ -386,7 +382,7 @@
         out_specs=[VMEM_SPEC] * 3,
         out_shape=[
             jax.ShapeDtypeStruct(own.shape, BF16),
-            jax.ShapeDtypeStruct((rank, 2 * rank), F32),
+            jax.ShapeDtypeStruct((rank, rank), F32),
             jax.ShapeDtypeStruct((rank, rank), F32),
         ],
         scratch_shapes=[pltpu.VMEM(own.shape, F32)] * 2,
@@ -664,6 +660,7 @@
     def receive(bit):
         return [slot ^ bit for slot in send(bit)]
 
+    w_grams = staged_terms(own_w_gram(w_start), "patient", [])
     arrived = [[] for _ in firsts]
     for i, bit in enumerate(bits):
         layouts = [receive(before) for before in bits[:i]]
@@ -671,9 +668,13 @@
             if i == 0 and part == 0:
                 code = first_projection(send(bit), count, place, in_hbm, v_rows)
             else:
-                code = next_projection(send(bit), first, count, layouts, place, by_owner, v_near, arrived[part])
+                after = [w_grams[part]] if i else []
+                code = next_projection(
+                    send(bit), first, count, layouts, place, by_owner, v_near, arrived[part], after
+                )
             arrived[part] = arrived[part] + [swap(code, "feature", bit)]
-    own, v_gram, h_local = project_own(n_parts, place, by_owner, v_near, w_start)
+    own, v_gram = project_own(n_parts, place, by_owner, v_near)
+    h_local = v_gram
 
     layouts = [receive(bit) for bit in bits]
     frames = [[] for _ in firsts]
@@ -698,16 +699,19 @@
 
     last = len(bits)
     projected, token = project_groups([(part, 0) for part in range(n_parts)], [])
+    w_gram, inverse = first_inverse(v_gram, w_grams)
     h_sums = staged_terms(h_local, "patient", [token])
-    double(n_parts - 1, h_sums[:1])
-    h_sum, w_gram = sum_h(h_sums, token)
-    h_terms = all_terms(h_sum, "feature")
+    h_sum = add(*h_sums, [inverse])
+    double(n_parts - 1, [h_sum])
     order = [(part, k) for part in range(n_parts) for k in range(1, last + 1)]
-    for group in order:
-        more, token = project_groups([group], [token])
+    more, token = project_groups(order[:1], [h_sum])
+    projected |= more
+    h_terms = staged_terms(h_sum, "feature", [token])
+    after = h_terms[:1]
+    for group in order[1:]:
+        more, token = project_groups([group], after)
         projected |= more
-        if group == order[-2]:
-            inverse = first_inverse(v_gram, w_gram, token)
+        after = [token]
     h_result, h_next, factor = next_h(place, h_terms, inverse, w_start, n, token)
 
     items = list(projected)

time: 91.3 us -> 96.9 us (1.061)
  waiting for transfers between devices: 15.1 us -> 26 us
  starting transfers between devices: 35.1 us -> 29.8 us
    ppermute x19 -> x20, waiting for transfers between devices: 15.1 us -> 26 us  [swap(): return lax.ppermute(x, axis, pairs)]
    ppermute x19 -> x20, starting transfers between devices: 35.1 us -> 29.8 us  [swap(): return lax.ppermute(x, axis, pairs)]
  transfers between devices with their start and end apart: 19 -> 20, of which waited for: 9 -> 10; matrix products, arithmetic and copies ran while one was open for 0% -> 0% of each run, Pallas kernels for 29% -> 28%
where the time goes in v11:
time: 96.9 us; the launch traced here: 96.8 us
  Pallas kernels  39.8 us (41%)
  starting transfers between devices  29.8 us (31%)
  waiting for transfers between devices  26 us (27%)
    ppermute x20, starting transfers between devices, swap(): return lax.ppermute(x, axis, pairs)  29.8 us
    ppermute x20, waiting for transfers between devices, swap(): return lax.ppermute(x, axis, pairs)  26 us
    pallas_call x2, Pallas kernels, own_frames(): pl.pallas_call(functools.partial(frames_kernel, layouts, part, share), in...  12.5 us
    pallas_call x1, Pallas kernels, first_projection(): pl.pallas_call(functools.partial(first_projection_kernel, slots), in_spec...  3.91 us
    pallas_call x5, Pallas kernels, project_frames(): pl.pallas_call(functools.partial(projected_kernel, items), in_specs=[SMEM...  3.62 us
    pallas_call x3, Pallas kernels, next_projection(): pl.pallas_call(functools.partial(next_projection_kernel, slots, first, co...  3.51 us
    pallas_call x1, Pallas kernels, next_w(): pl.pallas_call(functools.partial(next_w_kernel, len(sums)), out_shape=jax...  3.36 us
    pallas_call x1, Pallas kernels, next_v(): pl.pallas_call(functools.partial(next_v_kernel, items, share), in_specs=[...  3.27 us
  transfers between devices with their start and end apart: 20, of which 10 were waited for; matrix products, arithmetic and copies ran while one was open for 0% of the time, Pallas kernels for 28%

profile of v11, /device:TPU:0, one launch (start us, length us, event | category | flops | bytes accessed | tf_op | source)
XLA Modules:
  0.0 96.8 jit_solution(4383377413501062936)
XLA Ops:
  0.7 3.9 %project_first.1 = s16[560,256]{1,0:T(8,128)(2,1)S(1)} custom-call(s32[1]{0:T(128)} %bitcast.place, bf16[64,1024]{1,0:T(8,128)(2,1)} %bitcast.14, bf16[4,8,256,1024]{3,2,1,0:T(8,128)(2,1)} %bitcast.4), custom_call_target="tpu_custom_call" | custom-call | flops 1000 | bytes 1000 | tf_op jit(solution)/shard_map/project_first/pallas_call | solution.py:158
  4.6 3.0 %collective-permute-start = (s16[560,256]{1,0:T(8,128)(2,1)S(1)}, s16[560,256]{1,0:T(8,128)(2,1)S(1)}, u32[]{:S(2)}, u32[]{:S(2)}) collective-permute-start(s16[560,256]{1,0:T(8,128)(2,1)S(1)} %project_first.1), channel_id=1, source_target_pairs={{0,1},{1,0},{2,3},{3,2},{4,5},{5,4},{6,7},{7,6},{8,9},{9,8},{10,11... | collective-permute-start | bytes 860168 | tf_op jit(solution)/shard_map/ppermute | solution.py:598
  7.8 1.6 %project_next.4 = s16[528,256]{1,0:T(8,128)(2,1)S(1)} custom-call(s32[1]{0:T(128)} %bitcast.place, bf16[64,1024]{1,0:T(8,128)(2,1)S(1)} %bitcast.15, bf16[4,8,256,1024]{3,2,1,0:T(8,128)(2,1)S(1)} %bitcast.5), custom_call_target="tpu_custom_call" | custom-call | flops 1000 | bytes 1000 | tf_op jit(solution)/shard_map/project_next/pallas_call | solution.py:196
  9.4 3.1 %collective-permute-start.3 = (s16[528,256]{1,0:T(8,128)(2,1)S(1)}, s16[528,256]{1,0:T(8,128)(2,1)S(1)}, u32[]{:S(2)}, u32[]{:S(2)}) collective-permute-start(s16[528,256]{1,0:T(8,128)(2,1)S(1)} %project_next.4), channel_id=1, source_target_pairs={{0,1},{1,0},{2,3},{3,2},{4,5},{5,4},{6,7},{7,6},{8,9},{9,8},{10,11... | collective-permute-start | bytes 811016 | tf_op jit(solution)/shard_map/ppermute | solution.py:598
  16.3 3.3 %collective-permute-start.2 = (s16[304,256]{1,0:T(8,128)(2,1)S(1)}, s16[304,256]{1,0:T(8,128)(2,1)S(1)}, u32[]{:S(2)}, u32[]{:S(2)}) collective-permute-start(s16[304,256]{1,0:T(8,128)(2,1)S(1)} %project_next.3), channel_id=1, source_target_pairs={{0,2},{1,3},{2,0},{3,1},{4,6},{5,7},{6,4},{7,5},{8,10},{9,11},{10,... | collective-permute-start | bytes 466952 | tf_op jit(solution)/shard_map/ppermute | solution.py:598
  19.6 1.5 %collective-permute-start.4 = (f32[64,64]{1,0:T(8,128)S(1)}, f32[64,64]{1,0:T(8,128)S(1)}, u32[]{:S(2)}, u32[]{:S(2)}) collective-permute-start(f32[64,64]{1,0:T(8,128)S(1)} %add_terms.6.refs_1_.refs_0_), channel_id=1, source_target_pairs={{0,8},{4,12},{8,0},{12,4},{1,9},{5,13},{9,1},{13,5},{2,10},{6,14},... | collective-permute-start | bytes 49160 | tf_op jit(solution)/shard_map/ppermute | solution.py:598
  21.1 2.4 %collective-permute-done.4.refs_1_ = f32[64,64]{1,0:T(8,128)S(1)} collective-permute-done((f32[64,64]{1,0:T(8,128)S(1)}, f32[64,64]{1,0:T(8,128)S(1)}, u32[]{:S(2)}, u32[]{:S(2)}) %collective-permute-start.4) | collective-permute-done | bytes 16416 | tf_op jit(solution)/shard_map/ppermute | solution.py:598
  26.8 6.2 %own_frames.2 = (bf16[4,64,256]{2,1,0:T(8,128)(2,1)S(1)}, f32[64,64]{1,0:T(8,128)S(1)}, f32[64,64]{1,0:T(8,128)S(1)}) custom-call(s32[1]{0:T(128)} %bitcast.place, s32[32]{0:T(128)S(1)} %copy-done.4, f32[64,64]{1,0:T(8,128)S(1)} %copy-done.3, f32[32,64]{1,0:T(8,128)S(1)} %copy-done.2, f32[64,64]{1,0:T(8,128)S(1)} %get-tuple-element.39.v_gram_ref.before_ref, ...), custom_call_target="tpu_custom_call" | custom-call | flops 1000 | bytes 1000 | tf_op jit(solution)/shard_map/own_frames/pallas_call | solution.py:379
  33.0 2.2 %collective-permute-start.9 = (bf16[4,64,256]{2,1,0:T(8,128)(2,1)S(1)}, bf16[4,64,256]{2,1,0:T(8,128)(2,1)S(1)}, u32[]{:S(2)}, u32[]{:S(2)}) collective-permute-start(bf16[4,64,256]{2,1,0:T(8,128)(2,1)S(1)} %get-tuple-element.45.refs_0_), channel_id=1, source_target_pairs={{0,2},{1,3},{2,0},{3,1},{4,6},{5,7},{6,4},{7,5},{8,10},{9,11},{10,... | collective-permute-start | bytes 393224 | tf_op jit(solution)/shard_map/ppermute | solution.py:598
  35.1 6.3 %own_frames.3 = (bf16[4,64,256]{2,1,0:T(8,128)(2,1)S(1)}, f32[64,64]{1,0:T(8,128)S(1)}, f32[64,64]{1,0:T(8,128)}) custom-call(s32[1]{0:T(128)} %bitcast.place, s32[32]{0:T(128)S(1)} %copy-done.4, f32[64,64]{1,0:T(8,128)S(1)} %copy-done.3, f32[32,64]{1,0:T(8,128)S(1)} %copy-done.2, f32[64,64]{1,0:T(8,128)S(1)} %get-tuple-element.41.v_gram_ref, ...), custom_call_target="tpu_custom_call" | custom-call | flops 1000 | bytes 1000 | tf_op jit(solution)/shard_map/own_frames/pallas_call | solution.py:379
  45.1 2.6 %first_inverse.1 = (f32[64,64]{1,0:T(8,128)S(1)}, f32[64,64]{1,0:T(8,128)S(1)}) custom-call(f32[64,64]{1,0:T(8,128)S(1)} %get-tuple-element.41.v_gram_ref, f32[64,64]{1,0:T(8,128)S(1)} %add_terms.6.refs_1_.refs_0_, f32[64,64]{1,0:T(8,128)S(1)} %collective-permute-done.4.refs_1_), custom_call_target="tpu_custom_call" | custom-call | flops 1000 | bytes 1000 | tf_op jit(solution)/shard_map/first_inverse/pallas_call | solution.py:306
  47.7 3.4 %collective-permute-start.13 = (bf16[8,64,256]{2,1,0:T(8,128)(2,1)S(1)}, bf16[8,64,256]{2,1,0:T(8,128)(2,1)S(1)}, u32[]{:S(2)}, u32[]{:S(2)}) collective-permute-start(bf16[8,64,256]{2,1,0:T(8,128)(2,1)S(1)} %join_frames.3), channel_id=1, source_target_pairs={{0,1},{1,0},{2,3},{3,2},{4,5},{5,4},{6,7},{7,6},{8,9},{9,8},{10,11... | collective-permute-start | bytes 786440 | tf_op jit(solution)/shard_map/ppermute | solution.py:598
  51.6 1.6 %collective-permute-start.8 = (f32[64,64]{1,0:T(8,128)S(1)}, f32[64,64]{1,0:T(8,128)S(1)}, u32[]{:S(2)}, u32[]{:S(2)}) collective-permute-start(f32[64,64]{1,0:T(8,128)S(1)} %add_terms.8.refs_1_.a_ref.refs_2_), channel_id=1, source_target_pairs={{0,1},{1,0},{2,3},{3,2},{4,5},{5,4},{6,7},{7,6},{8,9},{9,8},{10,11... | collective-permute-start | bytes 49160 | tf_op jit(solution)/shard_map/ppermute | solution.py:598
  53.8 10.1 %collective-permute-done.8.b_ref = f32[64,64]{1,0:T(8,128)S(1)} collective-permute-done((f32[64,64]{1,0:T(8,128)S(1)}, f32[64,64]{1,0:T(8,128)S(1)}, u32[]{:S(2)}, u32[]{:S(2)}) %collective-permute-start.8) | collective-permute-done | bytes 16416 | tf_op jit(solution)/shard_map/ppermute | solution.py:598
  63.9 2.8 %collective-permute-start.10 = (f32[64,64]{1,0:T(8,128)S(1)}, f32[64,64]{1,0:T(8,128)S(1)}, u32[]{:S(2)}, u32[]{:S(2)}) collective-permute-start(f32[64,64]{1,0:T(8,128)S(1)} %add_terms.9.refs_1_.refs_0_), channel_id=1, source_target_pairs={{0,2},{1,3},{2,0},{3,1},{4,6},{5,7},{6,4},{7,5},{8,10},{9,11},{10,... | collective-permute-start | bytes 49160 | tf_op jit(solution)/shard_map/ppermute | solution.py:598
  70.0 1.6 %v_terms.1 = (f32[64,512]{1,0:T(8,128)S(1)}, f32[64,512]{1,0:T(8,128)S(1)}) custom-call(s32[1]{0:T(128)} %bitcast.place, bf16[4,192,512]{2,1,0:T(8,128)(2,1)S(1)} %get-tuple-element.54.factor_ref, bf16[256,1024]{1,0:T(8,128)(2,1)S(1)} %get-tuple-element.55.refs_0_, bf16[256,1024]{1,0:T(8,128)(2,1)S(1)} %get-tuple-element.56.refs_1_, ...), custom_call_target="tpu_custom_call" | custom-call | flops 1000 | bytes 1000 | tf_op jit(solution)/shard_map/v_terms/pallas_call | solution.py:524
  73.7 2.7 %second_inverse.1 = (f32[64,64]{1,0:T(8,128)S(1)}, f32[64,64]{1,0:T(8,128)S(1)}) custom-call(f32[64,64]{1,0:T(8,128)S(1)} %get-tuple-element.69.h_ref, f32[64,64]{1,0:T(8,128)S(1)} %get-tuple-element.70.w_gram_ref), custom_call_target="tpu_custom_call" | custom-call | flops 1000 | bytes 1000 | tf_op jit(solution)/shard_map/second_inverse/pallas_call | solution.py:492
  76.4 2.3 %collective-permute-done.15.b_ref = f32[64,512]{1,0:T(8,128)S(1)} collective-permute-done((f32[64,512]{1,0:T(8,128)S(1)}, f32[64,512]{1,0:T(8,128)S(1)}, u32[]{:S(2)}, u32[]{:S(2)}) %collective-permute-start.15) | collective-permute-done | bytes 131104 | tf_op jit(solution)/shard_map/ppermute | solution.py:598
  80.1 3.3 %next_v.1 = (f32[64,1024]{1,0:T(8,128)}, f32[64,128]{1,0:T(8,128)S(1)}) custom-call(s32[1]{0:T(128)} %bitcast.place, f32[64,512]{1,0:T(8,128)S(1)} %add_terms.11.own_ref, f32[64,512]{1,0:T(8,128)S(1)} %collective-permute-done.16.other_ref, f32[64,64]{1,0:T(8,128)S(1)} %get-tuple-element.71.refs_0_.inverse_ref, f32[64,64]{1,0:T(8,128)S(1)} %get-tuple-element.69.h_ref, ...), custom_call_target="tpu_custom_call" | custom-call | flops 1000 | bytes 1000 | tf_op jit(solution)/shard_map/next_v/pallas_call | solution.py:562
  83.4 1.7 %collective-permute-start.17 = (f32[64,128]{1,0:T(8,128)S(1)}, f32[64,128]{1,0:T(8,128)S(1)}, u32[]{:S(2)}, u32[]{:S(2)}) collective-permute-start(f32[64,128]{1,0:T(8,128)S(1)} %get-tuple-element.73.refs_0_), channel_id=1, source_target_pairs={{0,1},{1,0},{2,3},{3,2},{4,5},{5,4},{6,7},{7,6},{8,9},{9,8},{10,11... | collective-permute-start | bytes 98312 | tf_op jit(solution)/shard_map/ppermute | solution.py:598
  85.1 2.6 %collective-permute-start.18 = (f32[64,128]{1,0:T(8,128)S(1)}, f32[64,128]{1,0:T(8,128)S(1)}, u32[]{:S(2)}, u32[]{:S(2)}) collective-permute-start(f32[64,128]{1,0:T(8,128)S(1)} %get-tuple-element.73.refs_0_), channel_id=1, source_target_pairs={{0,2},{1,3},{2,0},{3,1},{4,6},{5,7},{6,4},{7,5},{8,10},{9,11},{10,... | collective-permute-start | bytes 98312 | tf_op jit(solution)/shard_map/ppermute | solution.py:598
  87.8 2.6 %collective-permute-done.18.refs_2_ = f32[64,128]{1,0:T(8,128)S(1)} collective-permute-done((f32[64,128]{1,0:T(8,128)S(1)}, f32[64,128]{1,0:T(8,128)S(1)}, u32[]{:S(2)}, u32[]{:S(2)}) %collective-permute-start.18) | collective-permute-done | bytes 32800 | tf_op jit(solution)/shard_map/ppermute | solution.py:598
  90.4 3.1 %collective-permute-done.19.refs_3_ = f32[64,128]{1,0:T(8,128)S(1)} collective-permute-done((f32[64,128]{1,0:T(8,128)S(1)}, f32[64,128]{1,0:T(8,128)S(1)}, u32[]{:S(2)}, u32[]{:S(2)}) %collective-permute-start.19) | collective-permute-done | bytes 32800 | tf_op jit(solution)/shard_map/ppermute | solution.py:598
  93.4 3.4 %next_w.1 = f32[32,64]{1,0:T(8,128)} custom-call(f32[64,128]{1,0:T(8,128)S(1)} %get-tuple-element.73.refs_0_, f32[64,128]{1,0:T(8,128)S(1)} %collective-permute-done.17.refs_1_, f32[64,128]{1,0:T(8,128)S(1)} %collective-permute-done.18.refs_2_, f32[64,128]{1,0:T(8,128)S(1)} %collective-permute-done.19.refs_3_, f32[64,64]{1,0:T(8,128)S(1)} %get-tuple-element.74.refs_4_), custom_call_target="tpu_custom_call" | custom-call | flops 1000 | bytes 1000 | tf_op jit(solution)/shard_map/next_w/pallas_call | solution.py:587
  (53 shorter events, 18.5 us)
Async XLA Ops:
  0.6 7.1 %copy-start = (bf16[32,256,1024]{2,1,0:T(8,128)(2,1)S(1)}, bf16[32,256,1024]{2,1,0:T(8,128)(2,1)}, u32[]{:S(2)}) copy-start(bf16[32,256,1024]{2,1,0:T(8,128)(2,1)} %param.5) | copy-start | bytes 50331652
  0.7 11.8 %copy-start.2 = (f32[32,64]{1,0:T(8,128)S(1)}, f32[32,64]{1,0:T(8,128)}, u32[]{:S(2)}) copy-start(f32[32,64]{1,0:T(8,128)} %refs_3_.1) | copy-start | bytes 24580
  4.6 10.7 %collective-permute-start = (s16[560,256]{1,0:T(8,128)(2,1)S(1)}, s16[560,256]{1,0:T(8,128)(2,1)S(1)}, u32[]{:S(2)}, u32[]{:S(2)}) collective-permute-start(s16[560,256]{1,0:T(8,128)(2,1)S(1)} %project_first.1), channel_id=1, source_target_pairs={{0,1},{1,0},{2,3},{3,2},{4,5},{5,4},{6,7},{7,6},{8,9},{9,8},{10,11... | collective-permute-start | bytes 860168 | tf_op jit(solution)/shard_map/ppermute | solution.py:598
  9.4 14.2 %collective-permute-start.3 = (s16[528,256]{1,0:T(8,128)(2,1)S(1)}, s16[528,256]{1,0:T(8,128)(2,1)S(1)}, u32[]{:S(2)}, u32[]{:S(2)}) collective-permute-start(s16[528,256]{1,0:T(8,128)(2,1)S(1)} %project_next.4), channel_id=1, source_target_pairs={{0,1},{1,0},{2,3},{3,2},{4,5},{5,4},{6,7},{7,6},{8,9},{9,8},{10,11... | collective-permute-start | bytes 811016 | tf_op jit(solution)/shard_map/ppermute | solution.py:598
  12.6 1.3 %collective-permute-start.1 = (f32[64,64]{1,0:T(8,128)S(1)}, f32[64,64]{1,0:T(8,128)S(1)}, u32[]{:S(2)}, u32[]{:S(2)}) collective-permute-start(f32[64,64]{1,0:T(8,128)S(1)} %own_w_gram.1.a_ref), channel_id=1, source_target_pairs={{0,4},{4,0},{8,12},{12,8},{1,5},{5,1},{9,13},{13,9},{2,6},{6,2},{1... | collective-permute-start | bytes 49160 | tf_op jit(solution)/shard_map/ppermute | solution.py:598
  16.3 10.5 %copy-start.3 = (f32[64,64]{1,0:T(8,128)S(1)}, f32[64,64]{1,0:T(8,128)}, u32[]{:S(2)}) copy-start(f32[64,64]{1,0:T(8,128)} %h_ref.3) | copy-start | bytes 49156
  16.3 10.5 %copy-start.4 = (s32[32]{0:T(128)S(1)}, s32[32]{0:T(128)}, u32[]{:S(2)}) copy-start(s32[32]{0:T(128)} %counts_ref.3) | copy-start | bytes 388
  16.3 10.5 %collective-permute-start.2 = (s16[304,256]{1,0:T(8,128)(2,1)S(1)}, s16[304,256]{1,0:T(8,128)(2,1)S(1)}, u32[]{:S(2)}, u32[]{:S(2)}) collective-permute-start(s16[304,256]{1,0:T(8,128)(2,1)S(1)} %project_next.3), channel_id=1, source_target_pairs={{0,2},{1,3},{2,0},{3,1},{4,6},{5,7},{6,4},{7,5},{8,10},{9,11},{10,... | collective-permute-start | bytes 466952 | tf_op jit(solution)/shard_map/ppermute | solution.py:598
  19.6 3.9 %collective-permute-start.4 = (f32[64,64]{1,0:T(8,128)S(1)}, f32[64,64]{1,0:T(8,128)S(1)}, u32[]{:S(2)}, u32[]{:S(2)}) collective-permute-start(f32[64,64]{1,0:T(8,128)S(1)} %add_terms.6.refs_1_.refs_0_), channel_id=1, source_target_pairs={{0,8},{4,12},{8,0},{12,4},{1,9},{5,13},{9,1},{13,5},{2,10},{6,14},... | collective-permute-start | bytes 49160 | tf_op jit(solution)/shard_map/ppermute | solution.py:598
  24.5 10.7 %collective-permute-start.5 = (s16[272,256]{1,0:T(8,128)(2,1)S(1)}, s16[272,256]{1,0:T(8,128)(2,1)S(1)}, u32[]{:S(2)}, u32[]{:S(2)}) collective-permute-start(s16[272,256]{1,0:T(8,128)(2,1)S(1)} %project_next.5), channel_id=1, source_target_pairs={{0,2},{1,3},{2,0},{3,1},{4,6},{5,7},{6,4},{7,5},{8,10},{9,11},{10,... | collective-permute-start | bytes 417800 | tf_op jit(solution)/shard_map/ppermute | solution.py:598
  33.0 14.7 %collective-permute-start.9 = (bf16[4,64,256]{2,1,0:T(8,128)(2,1)S(1)}, bf16[4,64,256]{2,1,0:T(8,128)(2,1)S(1)}, u32[]{:S(2)}, u32[]{:S(2)}) collective-permute-start(bf16[4,64,256]{2,1,0:T(8,128)(2,1)S(1)} %get-tuple-element.45.refs_0_), channel_id=1, source_target_pairs={{0,2},{1,3},{2,0},{3,1},{4,6},{5,7},{6,4},{7,5},{8,10},{9,11},{10,... | collective-permute-start | bytes 393224 | tf_op jit(solution)/shard_map/ppermute | solution.py:598
  41.5 9.6 %collective-permute-start.11 = (bf16[4,64,256]{2,1,0:T(8,128)(2,1)S(1)}, bf16[4,64,256]{2,1,0:T(8,128)(2,1)S(1)}, u32[]{:S(2)}, u32[]{:S(2)}) collective-permute-start(bf16[4,64,256]{2,1,0:T(8,128)(2,1)S(1)} %get-tuple-element.46.refs_1_.refs_0_), channel_id=1, source_target_pairs={{0,2},{1,3},{2,0},{3,1},{4,6},{5,7},{6,4},{7,5},{8,10},{9,11},{10,... | collective-permute-start | bytes 393224 | tf_op jit(solution)/shard_map/ppermute | solution.py:598
  42.4 1.2 %collective-permute-start.6 = (f32[64,64]{1,0:T(8,128)S(1)}, f32[64,64]{1,0:T(8,128)S(1)}, u32[]{:S(2)}, u32[]{:S(2)}) collective-permute-start(f32[64,64]{1,0:T(8,128)S(1)} %get-tuple-element.44.a_ref), channel_id=1, source_target_pairs={{0,4},{4,0},{8,12},{12,8},{1,5},{5,1},{9,13},{13,9},{2,6},{6,2},{1... | collective-permute-start | bytes 49160 | tf_op jit(solution)/shard_map/ppermute | solution.py:598
  43.6 7.5 %collective-permute-start.7 = (f32[64,64]{1,0:T(8,128)S(1)}, f32[64,64]{1,0:T(8,128)S(1)}, u32[]{:S(2)}, u32[]{:S(2)}) collective-permute-start(f32[64,64]{1,0:T(8,128)S(1)} %add_terms.7.a_ref), channel_id=1, source_target_pairs={{0,8},{4,12},{8,0},{12,4},{1,9},{5,13},{9,1},{13,5},{2,10},{6,14},... | collective-permute-start | bytes 49160 | tf_op jit(solution)/shard_map/ppermute | solution.py:598
  47.7 19.1 %collective-permute-start.13 = (bf16[8,64,256]{2,1,0:T(8,128)(2,1)S(1)}, bf16[8,64,256]{2,1,0:T(8,128)(2,1)S(1)}, u32[]{:S(2)}, u32[]{:S(2)}) collective-permute-start(bf16[8,64,256]{2,1,0:T(8,128)(2,1)S(1)} %join_frames.3), channel_id=1, source_target_pairs={{0,1},{1,0},{2,3},{3,2},{4,5},{5,4},{6,7},{7,6},{8,9},{9,8},{10,11... | collective-permute-start | bytes 786440 | tf_op jit(solution)/shard_map/ppermute | solution.py:598
  51.2 17.0 %collective-permute-start.12 = (bf16[8,64,256]{2,1,0:T(8,128)(2,1)S(1)}, bf16[8,64,256]{2,1,0:T(8,128)(2,1)S(1)}, u32[]{:S(2)}, u32[]{:S(2)}) collective-permute-start(bf16[8,64,256]{2,1,0:T(8,128)(2,1)S(1)} %join_frames.2), channel_id=1, source_target_pairs={{0,1},{1,0},{2,3},{3,2},{4,5},{5,4},{6,7},{7,6},{8,9},{9,8},{10,11... | collective-permute-start | bytes 786440 | tf_op jit(solution)/shard_map/ppermute | solution.py:598
  51.6 12.3 %collective-permute-start.8 = (f32[64,64]{1,0:T(8,128)S(1)}, f32[64,64]{1,0:T(8,128)S(1)}, u32[]{:S(2)}, u32[]{:S(2)}) collective-permute-start(f32[64,64]{1,0:T(8,128)S(1)} %add_terms.8.refs_1_.a_ref.refs_2_), channel_id=1, source_target_pairs={{0,1},{1,0},{2,3},{3,2},{4,5},{5,4},{6,7},{7,6},{8,9},{9,8},{10,11... | collective-permute-start | bytes 49160 | tf_op jit(solution)/shard_map/ppermute | solution.py:598
  63.9 5.1 %collective-permute-start.10 = (f32[64,64]{1,0:T(8,128)S(1)}, f32[64,64]{1,0:T(8,128)S(1)}, u32[]{:S(2)}, u32[]{:S(2)}) collective-permute-start(f32[64,64]{1,0:T(8,128)S(1)} %add_terms.9.refs_1_.refs_0_), channel_id=1, source_target_pairs={{0,2},{1,3},{2,0},{3,1},{4,6},{5,7},{6,4},{7,5},{8,10},{9,11},{10,... | collective-permute-start | bytes 49160 | tf_op jit(solution)/shard_map/ppermute | solution.py:598
  71.6 1.4 %collective-permute-start.14 = (f32[64,512]{1,0:T(8,128)S(1)}, f32[64,512]{1,0:T(8,128)S(1)}, u32[]{:S(2)}, u32[]{:S(2)}) collective-permute-start(f32[64,512]{1,0:T(8,128)S(1)} %get-tuple-element.68), channel_id=1, source_target_pairs={{0,4},{4,0},{8,12},{12,8},{1,5},{5,1},{9,13},{13,9},{2,6},{6,2},{1... | collective-permute-start | bytes 393224 | tf_op jit(solution)/shard_map/ppermute | solution.py:598
  73.1 5.6 %collective-permute-start.15 = (f32[64,512]{1,0:T(8,128)S(1)}, f32[64,512]{1,0:T(8,128)S(1)}, u32[]{:S(2)}, u32[]{:S(2)}) collective-permute-start(f32[64,512]{1,0:T(8,128)S(1)} %add_terms.10.a_ref), channel_id=1, source_target_pairs={{0,8},{4,12},{8,0},{12,4},{1,9},{5,13},{9,1},{13,5},{2,10},{6,14},... | collective-permute-start | bytes 393224 | tf_op jit(solution)/shard_map/ppermute | solution.py:598
  78.7 1.4 %collective-permute-start.16 = (f32[64,512]{1,0:T(8,128)S(1)}, f32[64,512]{1,0:T(8,128)S(1)}, u32[]{:S(2)}, u32[]{:S(2)}) collective-permute-start(f32[64,512]{1,0:T(8,128)S(1)} %add_terms.11.own_ref), channel_id=1, source_target_pairs={{0,4},{4,0},{8,12},{12,8},{1,5},{5,1},{9,13},{13,9},{2,6},{6,2},{1... | collective-permute-start | bytes 393224 | tf_op jit(solution)/shard_map/ppermute | solution.py:598
  83.4 4.4 %collective-permute-start.17 = (f32[64,128]{1,0:T(8,128)S(1)}, f32[64,128]{1,0:T(8,128)S(1)}, u32[]{:S(2)}, u32[]{:S(2)}) collective-permute-start(f32[64,128]{1,0:T(8,128)S(1)} %get-tuple-element.73.refs_0_), channel_id=1, source_target_pairs={{0,1},{1,0},{2,3},{3,2},{4,5},{5,4},{6,7},{7,6},{8,9},{9,8},{10,11... | collective-permute-start | bytes 98312 | tf_op jit(solution)/shard_map/ppermute | solution.py:598
  85.1 5.2 %collective-permute-start.18 = (f32[64,128]{1,0:T(8,128)S(1)}, f32[64,128]{1,0:T(8,128)S(1)}, u32[]{:S(2)}, u32[]{:S(2)}) collective-permute-start(f32[64,128]{1,0:T(8,128)S(1)} %get-tuple-element.73.refs_0_), channel_id=1, source_target_pairs={{0,2},{1,3},{2,0},{3,1},{4,6},{5,7},{6,4},{7,5},{8,10},{9,11},{10,... | collective-permute-start | bytes 98312 | tf_op jit(solution)/shard_map/ppermute | solution.py:598
  87.7 5.7 %collective-permute-start.19 = (f32[64,128]{1,0:T(8,128)S(1)}, f32[64,128]{1,0:T(8,128)S(1)}, u32[]{:S(2)}, u32[]{:S(2)}) collective-permute-start(f32[64,128]{1,0:T(8,128)S(1)} %get-tuple-element.73.refs_0_), channel_id=1, source_target_pairs={{0,3},{1,2},{2,1},{3,0},{4,7},{5,6},{6,5},{7,4},{8,11},{9,10},{10,... | collective-permute-start | bytes 98312 | tf_op jit(solution)/shard_map/ppermute | solution.py:598
  (1 other events, 7.0 us)

commit v12 on v11

--- a/solution.py
+++ b/solution.py
@@ -295,23 +295,23 @@
 
 
 def first_inverse_kernel(v_gram_ref, *refs):
-    *terms, w_gram_ref, inverse_ref = refs
+    *terms, _, w_gram_ref, inverse_ref = refs
     w_gram = total(terms)
     w_gram_ref[...] = w_gram
     inverse_ref[...] = inverse_of(w_gram * v_gram_ref[...])
 
 
-def first_inverse(v_gram, w_grams):
+def first_inverse(v_gram, w_grams, after):
     out = jax.ShapeDtypeStruct(v_gram.shape, F32)
     return pl.pallas_call(
         first_inverse_kernel,
-        in_specs=[VMEM_SPEC] * (1 + len(w_grams)),
+        in_specs=[VMEM_SPEC] * (1 + len(w_grams)) + [ANY_SPEC],
         out_specs=[VMEM_SPEC] * 2,
         out_shape=[out, out],
         compiler_params=parameters(LIMIT),
         cost_estimate=SHORT,
         name="first_inverse",
-    )(v_gram, *w_grams)
+    )(v_gram, *w_grams, after)
 
 
 def sweep_all(frames, rank, fine):
@@ -605,13 +605,13 @@
     return [x] + [swap(x, axis, s) for s in range(1, n)]
 
 
-def staged_terms(x, axis, after):
+def staged_terms(x, axis, after, far_first=False):
     n = lax.axis_size(axis)
-    step = 1
-    while 2 * step < n:
+    steps = [1 << i for i in range(n.bit_length() - 1)]
+    steps = steps[::-1] if far_first else steps
+    for step in steps[:-1]:
         x = add(x, swap(x, axis, step), after)
-        step *= 2
-    return [x, swap(x, axis, step)]
+    return [x, swap(x, axis, steps[-1])]
 
 
 def add_kernel(a_ref, b_ref, *refs):
@@ -678,11 +678,14 @@
 
     layouts = [receive(bit) for bit in bits]
     frames = [[] for _ in firsts]
+    joined = []
 
     def double(part, after):
         for bit in bits[::-1]:
             slots = tuple(slot ^ bit for group, _ in frames[part] for slot in group)
-            frames[part].append((slots, swap(join([x for _, x in frames[part]], after), "feature", bit)))
+            joined = join([x for _, x in frames[part]], after)
+            frames[part].append((slots, swap(joined, "feature", bit)))
+        return [joined]
 
     def project_groups(groups, after):
         arrays = {(frames[part][k][0], firsts[part]): frames[part][k][1] for part, k in groups}
@@ -695,20 +698,20 @@
         v_gram = v_total if first == 0 else v_gram
         frames[part].append(((0,), low))
         if part < n_parts - 1:
-            double(part, [])
+            joined = double(part, [])
 
     last = len(bits)
-    projected, token = project_groups([(part, 0) for part in range(n_parts)], [])
-    w_gram, inverse = first_inverse(v_gram, w_grams)
+    projected, token = project_groups([(part, 0) for part in range(n_parts)], joined)
     h_sums = staged_terms(h_local, "patient", [token])
-    h_sum = add(*h_sums, [inverse])
+    h_sum = add(*h_sums, [])
     double(n_parts - 1, [h_sum])
     order = [(part, k) for part in range(n_parts) for k in range(1, last + 1)]
-    more, token = project_groups(order[:1], [h_sum])
+    more, token = project_groups(order[:-2], [h_sum])
     projected |= more
-    h_terms = staged_terms(h_sum, "feature", [token])
+    w_gram, inverse = first_inverse(v_gram, w_grams, token)
+    h_terms = staged_terms(h_sum, "feature", [inverse], far_first=True)
     after = h_terms[:1]
-    for group in order[1:]:
+    for group in order[-2:]:
         more, token = project_groups([group], after)
         projected |= more
         after = [token]

time: 96.9 us -> 91 us (0.939)
  waiting for transfers between devices: 26 us -> 17 us
  starting transfers between devices: 29.8 us -> 33.2 us
    ppermute x20, waiting for transfers between devices: 26 us -> 17 us  [swap(): return lax.ppermute(x, axis, pairs)]
    ppermute x20, starting transfers between devices: 29.8 us -> 33.2 us  [swap(): return lax.ppermute(x, axis, pairs)]
    pallas_call x5 -> x4, Pallas kernels: 3.62 us -> 3.48 us  [project_frames(): pl.pallas_call(functools.partial(projected_kernel, items), in_specs=[SMEM...]
  transfers between devices with their start and end apart: 20 -> 20, of which waited for: 10 -> 12; matrix products, arithmetic and copies ran while one was open for 0% -> 0% of each run, Pallas kernels for 28% -> 29%
where the time goes in v12:
time: 91 us; the launch traced here: 90.9 us
  Pallas kernels  39.7 us (44%)
  starting transfers between devices  33.2 us (36%)
  waiting for transfers between devices  17 us (19%)
    ppermute x20, starting transfers between devices, swap(): return lax.ppermute(x, axis, pairs)  33.2 us
    ppermute x20, waiting for transfers between devices, swap(): return lax.ppermute(x, axis, pairs)  17 us
    pallas_call x2, Pallas kernels, own_frames(): pl.pallas_call(functools.partial(frames_kernel, layouts, part, share), in...  12.5 us
    pallas_call x1, Pallas kernels, first_projection(): pl.pallas_call(functools.partial(first_projection_kernel, slots), in_spec...  3.91 us
    pallas_call x3, Pallas kernels, next_projection(): pl.pallas_call(functools.partial(next_projection_kernel, slots, first, co...  3.51 us
    pallas_call x4, Pallas kernels, project_frames(): pl.pallas_call(functools.partial(projected_kernel, items), in_specs=[SMEM...  3.48 us
    pallas_call x1, Pallas kernels, next_w(): pl.pallas_call(functools.partial(next_w_kernel, len(sums)), out_shape=jax...  3.36 us
    pallas_call x1, Pallas kernels, next_v(): pl.pallas_call(functools.partial(next_v_kernel, items, share), in_specs=[...  3.28 us
  transfers between devices with their start and end apart: 20, of which 12 were waited for; matrix products, arithmetic and copies ran while one was open for 0% of the time, Pallas kernels for 29%

profile of v12, /device:TPU:0, one launch (start us, length us, event | category | flops | bytes accessed | tf_op | source)
XLA Modules:
  0.0 90.9 jit_solution(9642429889855582711)
XLA Ops:
  0.7 3.9 %project_first.1 = s16[560,256]{1,0:T(8,128)(2,1)S(1)} custom-call(s32[1]{0:T(128)} %bitcast.place, bf16[64,1024]{1,0:T(8,128)(2,1)} %bitcast.13, bf16[4,8,256,1024]{3,2,1,0:T(8,128)(2,1)} %bitcast.4), custom_call_target="tpu_custom_call" | custom-call | flops 1000 | bytes 1000 | tf_op jit(solution)/shard_map/project_first/pallas_call | solution.py:158
  4.6 3.0 %collective-permute-start = (s16[560,256]{1,0:T(8,128)(2,1)S(1)}, s16[560,256]{1,0:T(8,128)(2,1)S(1)}, u32[]{:S(2)}, u32[]{:S(2)}) collective-permute-start(s16[560,256]{1,0:T(8,128)(2,1)S(1)} %project_first.1), channel_id=1, source_target_pairs={{0,1},{1,0},{2,3},{3,2},{4,5},{5,4},{6,7},{7,6},{8,9},{9,8},{10,11... | collective-permute-start | bytes 860168 | tf_op jit(solution)/shard_map/ppermute | solution.py:598
  7.8 1.6 %project_next.4 = s16[528,256]{1,0:T(8,128)(2,1)S(1)} custom-call(s32[1]{0:T(128)} %bitcast.place, bf16[64,1024]{1,0:T(8,128)(2,1)S(1)} %bitcast.14, bf16[4,8,256,1024]{3,2,1,0:T(8,128)(2,1)S(1)} %bitcast.5), custom_call_target="tpu_custom_call" | custom-call | flops 1000 | bytes 1000 | tf_op jit(solution)/shard_map/project_next/pallas_call | solution.py:196
  9.4 3.1 %collective-permute-start.3 = (s16[528,256]{1,0:T(8,128)(2,1)S(1)}, s16[528,256]{1,0:T(8,128)(2,1)S(1)}, u32[]{:S(2)}, u32[]{:S(2)}) collective-permute-start(s16[528,256]{1,0:T(8,128)(2,1)S(1)} %project_next.4), channel_id=1, source_target_pairs={{0,1},{1,0},{2,3},{3,2},{4,5},{5,4},{6,7},{7,6},{8,9},{9,8},{10,11... | collective-permute-start | bytes 811016 | tf_op jit(solution)/shard_map/ppermute | solution.py:598
  16.3 3.3 %collective-permute-start.2 = (s16[304,256]{1,0:T(8,128)(2,1)S(1)}, s16[304,256]{1,0:T(8,128)(2,1)S(1)}, u32[]{:S(2)}, u32[]{:S(2)}) collective-permute-start(s16[304,256]{1,0:T(8,128)(2,1)S(1)} %project_next.3), channel_id=1, source_target_pairs={{0,2},{1,3},{2,0},{3,1},{4,6},{5,7},{6,4},{7,5},{8,10},{9,11},{10,... | collective-permute-start | bytes 466952 | tf_op jit(solution)/shard_map/ppermute | solution.py:598
  21.1 2.4 %collective-permute-done.4.refs_1_ = f32[64,64]{1,0:T(8,128)S(1)} collective-permute-done((f32[64,64]{1,0:T(8,128)S(1)}, f32[64,64]{1,0:T(8,128)S(1)}, u32[]{:S(2)}, u32[]{:S(2)}) %collective-permute-start.4) | collective-permute-done | bytes 16416 | tf_op jit(solution)/shard_map/ppermute | solution.py:598
  26.8 6.2 %own_frames.2 = (bf16[4,64,256]{2,1,0:T(8,128)(2,1)S(1)}, f32[64,64]{1,0:T(8,128)S(1)}, f32[64,64]{1,0:T(8,128)S(1)}) custom-call(s32[1]{0:T(128)} %bitcast.place, s32[32]{0:T(128)S(1)} %copy-done.4, f32[64,64]{1,0:T(8,128)S(1)} %copy-done.3, f32[32,64]{1,0:T(8,128)S(1)} %copy-done.2, f32[64,64]{1,0:T(8,128)S(1)} %get-tuple-element.38.v_gram_ref.before_ref, ...), custom_call_target="tpu_custom_call" | custom-call | flops 1000 | bytes 1000 | tf_op jit(solution)/shard_map/own_frames/pallas_call | solution.py:379
  33.0 2.2 %collective-permute-start.7 = (bf16[4,64,256]{2,1,0:T(8,128)(2,1)S(1)}, bf16[4,64,256]{2,1,0:T(8,128)(2,1)S(1)}, u32[]{:S(2)}, u32[]{:S(2)}) collective-permute-start(bf16[4,64,256]{2,1,0:T(8,128)(2,1)S(1)} %get-tuple-element.44.refs_0_), channel_id=1, source_target_pairs={{0,2},{1,3},{2,0},{3,1},{4,6},{5,7},{6,4},{7,5},{8,10},{9,11},{10,... | collective-permute-start | bytes 393224 | tf_op jit(solution)/shard_map/ppermute | solution.py:598
  35.1 6.3 %own_frames.3 = (bf16[4,64,256]{2,1,0:T(8,128)(2,1)S(1)}, f32[64,64]{1,0:T(8,128)S(1)}, f32[64,64]{1,0:T(8,128)}) custom-call(s32[1]{0:T(128)} %bitcast.place, s32[32]{0:T(128)S(1)} %copy-done.4, f32[64,64]{1,0:T(8,128)S(1)} %copy-done.3, f32[32,64]{1,0:T(8,128)S(1)} %copy-done.2, f32[64,64]{1,0:T(8,128)S(1)} %get-tuple-element.40.v_gram_ref, ...), custom_call_target="tpu_custom_call" | custom-call | flops 1000 | bytes 1000 | tf_op jit(solution)/shard_map/own_frames/pallas_call | solution.py:379
  43.3 3.5 %collective-permute-start.10 = (bf16[8,64,256]{2,1,0:T(8,128)(2,1)S(1)}, bf16[8,64,256]{2,1,0:T(8,128)(2,1)S(1)}, u32[]{:S(2)}, u32[]{:S(2)}) collective-permute-start(bf16[8,64,256]{2,1,0:T(8,128)(2,1)S(1)} %join_frames.2.refs_2_), channel_id=1, source_target_pairs={{0,1},{1,0},{2,3},{3,2},{4,5},{5,4},{6,7},{7,6},{8,9},{9,8},{10,11... | collective-permute-start | bytes 786440 | tf_op jit(solution)/shard_map/ppermute | solution.py:598
  46.7 1.6 %collective-permute-start.8 = (f32[64,64]{1,0:T(8,128)S(1)}, f32[64,64]{1,0:T(8,128)S(1)}, u32[]{:S(2)}, u32[]{:S(2)}) collective-permute-start(f32[64,64]{1,0:T(8,128)S(1)} %add_terms.7.a_ref), channel_id=1, source_target_pairs={{0,8},{4,12},{8,0},{12,4},{1,9},{5,13},{9,1},{13,5},{2,10},{6,14},... | collective-permute-start | bytes 49160 | tf_op jit(solution)/shard_map/ppermute | solution.py:598
  48.3 2.4 %collective-permute-done.8.b_ref = f32[64,64]{1,0:T(8,128)S(1)} collective-permute-done((f32[64,64]{1,0:T(8,128)S(1)}, f32[64,64]{1,0:T(8,128)S(1)}, u32[]{:S(2)}, u32[]{:S(2)}) %collective-permute-start.8) | collective-permute-done | bytes 16416 | tf_op jit(solution)/shard_map/ppermute | solution.py:598
  52.2 1.6 %collective-permute-start.9 = (f32[64,64]{1,0:T(8,128)S(1)}, f32[64,64]{1,0:T(8,128)S(1)}, u32[]{:S(2)}, u32[]{:S(2)}) collective-permute-start(f32[64,64]{1,0:T(8,128)S(1)} %add_terms.8.refs_2_.a_ref), channel_id=1, source_target_pairs={{0,2},{1,3},{2,0},{3,1},{4,6},{5,7},{6,4},{7,5},{8,10},{9,11},{10,... | collective-permute-start | bytes 49160 | tf_op jit(solution)/shard_map/ppermute | solution.py:598
  55.1 2.6 %first_inverse.1 = (f32[64,64]{1,0:T(8,128)S(1)}, f32[64,64]{1,0:T(8,128)S(1)}) custom-call(f32[64,64]{1,0:T(8,128)S(1)} %get-tuple-element.40.v_gram_ref, f32[64,64]{1,0:T(8,128)S(1)} %add_terms.6.refs_1_.refs_0_, f32[64,64]{1,0:T(8,128)S(1)} %collective-permute-done.4.refs_1_, f32[8,128]{1,0:T(8,128)S(1)} %get-tuple-element.47.refs_2_), custom_call_target="tpu_custom_call" | custom-call | flops 1000 | bytes 1000 | tf_op jit(solution)/shard_map/first_inverse/pallas_call | solution.py:306
  57.7 1.5 %collective-permute-done.9.b_ref = f32[64,64]{1,0:T(8,128)S(1)} collective-permute-done((f32[64,64]{1,0:T(8,128)S(1)}, f32[64,64]{1,0:T(8,128)S(1)}, u32[]{:S(2)}, u32[]{:S(2)}) %collective-permute-start.9) | collective-permute-done | bytes 16416 | tf_op jit(solution)/shard_map/ppermute | solution.py:598
  59.3 4.2 %collective-permute-start.11 = (f32[64,64]{1,0:T(8,128)S(1)}, f32[64,64]{1,0:T(8,128)S(1)}, u32[]{:S(2)}, u32[]{:S(2)}) collective-permute-start(f32[64,64]{1,0:T(8,128)S(1)} %add_terms.9.refs_1_.refs_0_), channel_id=1, source_target_pairs={{0,1},{1,0},{2,3},{3,2},{4,5},{5,4},{6,7},{7,6},{8,9},{9,8},{10,11... | collective-permute-start | bytes 49160 | tf_op jit(solution)/shard_map/ppermute | solution.py:598
  66.3 1.6 %v_terms.1 = (f32[64,512]{1,0:T(8,128)S(1)}, f32[64,512]{1,0:T(8,128)S(1)}) custom-call(s32[1]{0:T(128)} %bitcast.place, bf16[4,192,512]{2,1,0:T(8,128)(2,1)S(1)} %get-tuple-element.52.factor_ref, bf16[256,1024]{1,0:T(8,128)(2,1)S(1)} %get-tuple-element.53.refs_0_, bf16[256,1024]{1,0:T(8,128)(2,1)S(1)} %get-tuple-element.54.refs_1_, ...), custom_call_target="tpu_custom_call" | custom-call | flops 1000 | bytes 1000 | tf_op jit(solution)/shard_map/v_terms/pallas_call | solution.py:524
  69.4 1.6 %collective-permute-start.15 = (f32[64,512]{1,0:T(8,128)S(1)}, f32[64,512]{1,0:T(8,128)S(1)}, u32[]{:S(2)}, u32[]{:S(2)}) collective-permute-start(f32[64,512]{1,0:T(8,128)S(1)} %add_terms.10.a_ref), channel_id=1, source_target_pairs={{0,8},{4,12},{8,0},{12,4},{1,9},{5,13},{9,1},{13,5},{2,10},{6,14},... | collective-permute-start | bytes 393224 | tf_op jit(solution)/shard_map/ppermute | solution.py:598
  70.9 2.7 %second_inverse.1 = (f32[64,64]{1,0:T(8,128)S(1)}, f32[64,64]{1,0:T(8,128)S(1)}) custom-call(f32[64,64]{1,0:T(8,128)S(1)} %get-tuple-element.67.h_ref, f32[64,64]{1,0:T(8,128)S(1)} %get-tuple-element.68.w_gram_ref), custom_call_target="tpu_custom_call" | custom-call | flops 1000 | bytes 1000 | tf_op jit(solution)/shard_map/second_inverse/pallas_call | solution.py:492
  76.4 3.3 %next_v.1 = (f32[64,1024]{1,0:T(8,128)}, f32[64,128]{1,0:T(8,128)S(1)}) custom-call(s32[1]{0:T(128)} %bitcast.place, f32[64,512]{1,0:T(8,128)S(1)} %add_terms.11.own_ref, f32[64,512]{1,0:T(8,128)S(1)} %collective-permute-done.16.other_ref, f32[64,64]{1,0:T(8,128)S(1)} %get-tuple-element.69.refs_0_.inverse_ref, f32[64,64]{1,0:T(8,128)S(1)} %get-tuple-element.67.h_ref, ...), custom_call_target="tpu_custom_call" | custom-call | flops 1000 | bytes 1000 | tf_op jit(solution)/shard_map/next_v/pallas_call | solution.py:562
  79.7 2.0 %collective-permute-start.17 = (f32[64,128]{1,0:T(8,128)S(1)}, f32[64,128]{1,0:T(8,128)S(1)}, u32[]{:S(2)}, u32[]{:S(2)}) collective-permute-start(f32[64,128]{1,0:T(8,128)S(1)} %get-tuple-element.71.refs_0_), channel_id=1, source_target_pairs={{0,1},{1,0},{2,3},{3,2},{4,5},{5,4},{6,7},{7,6},{8,9},{9,8},{10,11... | collective-permute-start | bytes 98312 | tf_op jit(solution)/shard_map/ppermute | solution.py:598
  81.7 2.4 %collective-permute-start.19 = (f32[64,128]{1,0:T(8,128)S(1)}, f32[64,128]{1,0:T(8,128)S(1)}, u32[]{:S(2)}, u32[]{:S(2)}) collective-permute-start(f32[64,128]{1,0:T(8,128)S(1)} %get-tuple-element.71.refs_0_), channel_id=1, source_target_pairs={{0,3},{1,2},{2,1},{3,0},{4,7},{5,6},{6,5},{7,4},{8,11},{9,10},{10,... | collective-permute-start | bytes 98312 | tf_op jit(solution)/shard_map/ppermute | solution.py:598
  84.1 2.8 %collective-permute-done.18.refs_2_ = f32[64,128]{1,0:T(8,128)S(1)} collective-permute-done((f32[64,128]{1,0:T(8,128)S(1)}, f32[64,128]{1,0:T(8,128)S(1)}, u32[]{:S(2)}, u32[]{:S(2)}) %collective-permute-start.18) | collective-permute-done | bytes 32800 | tf_op jit(solution)/shard_map/ppermute | solution.py:598
  87.5 3.4 %next_w.1 = f32[32,64]{1,0:T(8,128)} custom-call(f32[64,128]{1,0:T(8,128)S(1)} %get-tuple-element.71.refs_0_, f32[64,128]{1,0:T(8,128)S(1)} %collective-permute-done.17.refs_1_, f32[64,128]{1,0:T(8,128)S(1)} %collective-permute-done.18.refs_2_, f32[64,128]{1,0:T(8,128)S(1)} %collective-permute-done.19.refs_3_, f32[64,64]{1,0:T(8,128)S(1)} %get-tuple-element.72.refs_4_), custom_call_target="tpu_custom_call" | custom-call | flops 1000 | bytes 1000 | tf_op jit(solution)/shard_map/next_w/pallas_call | solution.py:587
  (52 shorter events, 21.0 us)
Async XLA Ops:
  0.6 7.1 %copy-start = (bf16[32,256,1024]{2,1,0:T(8,128)(2,1)S(1)}, bf16[32,256,1024]{2,1,0:T(8,128)(2,1)}, u32[]{:S(2)}) copy-start(bf16[32,256,1024]{2,1,0:T(8,128)(2,1)} %param.5) | copy-start | bytes 50331652
  0.7 11.8 %copy-start.2 = (f32[32,64]{1,0:T(8,128)S(1)}, f32[32,64]{1,0:T(8,128)}, u32[]{:S(2)}) copy-start(f32[32,64]{1,0:T(8,128)} %refs_3_.1) | copy-start | bytes 24580
  4.6 10.7 %collective-permute-start = (s16[560,256]{1,0:T(8,128)(2,1)S(1)}, s16[560,256]{1,0:T(8,128)(2,1)S(1)}, u32[]{:S(2)}, u32[]{:S(2)}) collective-permute-start(s16[560,256]{1,0:T(8,128)(2,1)S(1)} %project_first.1), channel_id=1, source_target_pairs={{0,1},{1,0},{2,3},{3,2},{4,5},{5,4},{6,7},{7,6},{8,9},{9,8},{10,11... | collective-permute-start | bytes 860168 | tf_op jit(solution)/shard_map/ppermute | solution.py:598
  9.4 14.2 %collective-permute-start.3 = (s16[528,256]{1,0:T(8,128)(2,1)S(1)}, s16[528,256]{1,0:T(8,128)(2,1)S(1)}, u32[]{:S(2)}, u32[]{:S(2)}) collective-permute-start(s16[528,256]{1,0:T(8,128)(2,1)S(1)} %project_next.4), channel_id=1, source_target_pairs={{0,1},{1,0},{2,3},{3,2},{4,5},{5,4},{6,7},{7,6},{8,9},{9,8},{10,11... | collective-permute-start | bytes 811016 | tf_op jit(solution)/shard_map/ppermute | solution.py:598
  12.6 1.3 %collective-permute-start.1 = (f32[64,64]{1,0:T(8,128)S(1)}, f32[64,64]{1,0:T(8,128)S(1)}, u32[]{:S(2)}, u32[]{:S(2)}) collective-permute-start(f32[64,64]{1,0:T(8,128)S(1)} %own_w_gram.1.a_ref), channel_id=1, source_target_pairs={{0,4},{4,0},{8,12},{12,8},{1,5},{5,1},{9,13},{13,9},{2,6},{6,2},{1... | collective-permute-start | bytes 49160 | tf_op jit(solution)/shard_map/ppermute | solution.py:598
  16.3 10.5 %copy-start.3 = (f32[64,64]{1,0:T(8,128)S(1)}, f32[64,64]{1,0:T(8,128)}, u32[]{:S(2)}) copy-start(f32[64,64]{1,0:T(8,128)} %h_ref.3) | copy-start | bytes 49156
  16.3 10.5 %copy-start.4 = (s32[32]{0:T(128)S(1)}, s32[32]{0:T(128)}, u32[]{:S(2)}) copy-start(s32[32]{0:T(128)} %counts_ref.3) | copy-start | bytes 388
  16.3 10.5 %collective-permute-start.2 = (s16[304,256]{1,0:T(8,128)(2,1)S(1)}, s16[304,256]{1,0:T(8,128)(2,1)S(1)}, u32[]{:S(2)}, u32[]{:S(2)}) collective-permute-start(s16[304,256]{1,0:T(8,128)(2,1)S(1)} %project_next.3), channel_id=1, source_target_pairs={{0,2},{1,3},{2,0},{3,1},{4,6},{5,7},{6,4},{7,5},{8,10},{9,11},{10,... | collective-permute-start | bytes 466952 | tf_op jit(solution)/shard_map/ppermute | solution.py:598
  19.6 3.9 %collective-permute-start.4 = (f32[64,64]{1,0:T(8,128)S(1)}, f32[64,64]{1,0:T(8,128)S(1)}, u32[]{:S(2)}, u32[]{:S(2)}) collective-permute-start(f32[64,64]{1,0:T(8,128)S(1)} %add_terms.6.refs_1_.refs_0_), channel_id=1, source_target_pairs={{0,8},{4,12},{8,0},{12,4},{1,9},{5,13},{9,1},{13,5},{2,10},{6,14},... | collective-permute-start | bytes 49160 | tf_op jit(solution)/shard_map/ppermute | solution.py:598
  24.5 10.7 %collective-permute-start.5 = (s16[272,256]{1,0:T(8,128)(2,1)S(1)}, s16[272,256]{1,0:T(8,128)(2,1)S(1)}, u32[]{:S(2)}, u32[]{:S(2)}) collective-permute-start(s16[272,256]{1,0:T(8,128)(2,1)S(1)} %project_next.5), channel_id=1, source_target_pairs={{0,2},{1,3},{2,0},{3,1},{4,6},{5,7},{6,4},{7,5},{8,10},{9,11},{10,... | collective-permute-start | bytes 417800 | tf_op jit(solution)/shard_map/ppermute | solution.py:598
  33.0 9.4 %collective-permute-start.7 = (bf16[4,64,256]{2,1,0:T(8,128)(2,1)S(1)}, bf16[4,64,256]{2,1,0:T(8,128)(2,1)S(1)}, u32[]{:S(2)}, u32[]{:S(2)}) collective-permute-start(bf16[4,64,256]{2,1,0:T(8,128)(2,1)S(1)} %get-tuple-element.44.refs_0_), channel_id=1, source_target_pairs={{0,2},{1,3},{2,0},{3,1},{4,6},{5,7},{6,4},{7,5},{8,10},{9,11},{10,... | collective-permute-start | bytes 393224 | tf_op jit(solution)/shard_map/ppermute | solution.py:598
  41.5 9.2 %collective-permute-start.12 = (bf16[4,64,256]{2,1,0:T(8,128)(2,1)S(1)}, bf16[4,64,256]{2,1,0:T(8,128)(2,1)S(1)}, u32[]{:S(2)}, u32[]{:S(2)}) collective-permute-start(bf16[4,64,256]{2,1,0:T(8,128)(2,1)S(1)} %get-tuple-element.45.refs_1_.refs_0_), channel_id=1, source_target_pairs={{0,2},{1,3},{2,0},{3,1},{4,6},{5,7},{6,4},{7,5},{8,10},{9,11},{10,... | collective-permute-start | bytes 393224 | tf_op jit(solution)/shard_map/ppermute | solution.py:598
  42.4 4.4 %collective-permute-start.6 = (f32[64,64]{1,0:T(8,128)S(1)}, f32[64,64]{1,0:T(8,128)S(1)}, u32[]{:S(2)}, u32[]{:S(2)}) collective-permute-start(f32[64,64]{1,0:T(8,128)S(1)} %get-tuple-element.43.a_ref), channel_id=1, source_target_pairs={{0,4},{4,0},{8,12},{12,8},{1,5},{5,1},{9,13},{13,9},{2,6},{6,2},{1... | collective-permute-start | bytes 49160 | tf_op jit(solution)/shard_map/ppermute | solution.py:598
  43.3 10.6 %collective-permute-start.10 = (bf16[8,64,256]{2,1,0:T(8,128)(2,1)S(1)}, bf16[8,64,256]{2,1,0:T(8,128)(2,1)S(1)}, u32[]{:S(2)}, u32[]{:S(2)}) collective-permute-start(bf16[8,64,256]{2,1,0:T(8,128)(2,1)S(1)} %join_frames.2.refs_2_), channel_id=1, source_target_pairs={{0,1},{1,0},{2,3},{3,2},{4,5},{5,4},{6,7},{7,6},{8,9},{9,8},{10,11... | collective-permute-start | bytes 786440 | tf_op jit(solution)/shard_map/ppermute | solution.py:598
  46.7 4.0 %collective-permute-start.8 = (f32[64,64]{1,0:T(8,128)S(1)}, f32[64,64]{1,0:T(8,128)S(1)}, u32[]{:S(2)}, u32[]{:S(2)}) collective-permute-start(f32[64,64]{1,0:T(8,128)S(1)} %add_terms.7.a_ref), channel_id=1, source_target_pairs={{0,8},{4,12},{8,0},{12,4},{1,9},{5,13},{9,1},{13,5},{2,10},{6,14},... | collective-permute-start | bytes 49160 | tf_op jit(solution)/shard_map/ppermute | solution.py:598
  50.8 13.2 %collective-permute-start.13 = (bf16[8,64,256]{2,1,0:T(8,128)(2,1)S(1)}, bf16[8,64,256]{2,1,0:T(8,128)(2,1)S(1)}, u32[]{:S(2)}, u32[]{:S(2)}) collective-permute-start(bf16[8,64,256]{2,1,0:T(8,128)(2,1)S(1)} %join_frames.3), channel_id=1, source_target_pairs={{0,1},{1,0},{2,3},{3,2},{4,5},{5,4},{6,7},{7,6},{8,9},{9,8},{10,11... | collective-permute-start | bytes 786440 | tf_op jit(solution)/shard_map/ppermute | solution.py:598
  52.2 7.0 %collective-permute-start.9 = (f32[64,64]{1,0:T(8,128)S(1)}, f32[64,64]{1,0:T(8,128)S(1)}, u32[]{:S(2)}, u32[]{:S(2)}) collective-permute-start(f32[64,64]{1,0:T(8,128)S(1)} %add_terms.8.refs_2_.a_ref), channel_id=1, source_target_pairs={{0,2},{1,3},{2,0},{3,1},{4,6},{5,7},{6,4},{7,5},{8,10},{9,11},{10,... | collective-permute-start | bytes 49160 | tf_op jit(solution)/shard_map/ppermute | solution.py:598
  59.3 6.1 %collective-permute-start.11 = (f32[64,64]{1,0:T(8,128)S(1)}, f32[64,64]{1,0:T(8,128)S(1)}, u32[]{:S(2)}, u32[]{:S(2)}) collective-permute-start(f32[64,64]{1,0:T(8,128)S(1)} %add_terms.9.refs_1_.refs_0_), channel_id=1, source_target_pairs={{0,1},{1,0},{2,3},{3,2},{4,5},{5,4},{6,7},{7,6},{8,9},{9,8},{10,11... | collective-permute-start | bytes 49160 | tf_op jit(solution)/shard_map/ppermute | solution.py:598
  67.9 1.4 %collective-permute-start.14 = (f32[64,512]{1,0:T(8,128)S(1)}, f32[64,512]{1,0:T(8,128)S(1)}, u32[]{:S(2)}, u32[]{:S(2)}) collective-permute-start(f32[64,512]{1,0:T(8,128)S(1)} %get-tuple-element.66), channel_id=1, source_target_pairs={{0,4},{4,0},{8,12},{12,8},{1,5},{5,1},{9,13},{13,9},{2,6},{6,2},{1... | collective-permute-start | bytes 393224 | tf_op jit(solution)/shard_map/ppermute | solution.py:598
  69.4 5.6 %collective-permute-start.15 = (f32[64,512]{1,0:T(8,128)S(1)}, f32[64,512]{1,0:T(8,128)S(1)}, u32[]{:S(2)}, u32[]{:S(2)}) collective-permute-start(f32[64,512]{1,0:T(8,128)S(1)} %add_terms.10.a_ref), channel_id=1, source_target_pairs={{0,8},{4,12},{8,0},{12,4},{1,9},{5,13},{9,1},{13,5},{2,10},{6,14},... | collective-permute-start | bytes 393224 | tf_op jit(solution)/shard_map/ppermute | solution.py:598
  75.0 1.4 %collective-permute-start.16 = (f32[64,512]{1,0:T(8,128)S(1)}, f32[64,512]{1,0:T(8,128)S(1)}, u32[]{:S(2)}, u32[]{:S(2)}) collective-permute-start(f32[64,512]{1,0:T(8,128)S(1)} %add_terms.11.own_ref), channel_id=1, source_target_pairs={{0,4},{4,0},{8,12},{12,8},{1,5},{5,1},{9,13},{13,9},{2,6},{6,2},{1... | collective-permute-start | bytes 393224 | tf_op jit(solution)/shard_map/ppermute | solution.py:598
  79.7 4.4 %collective-permute-start.17 = (f32[64,128]{1,0:T(8,128)S(1)}, f32[64,128]{1,0:T(8,128)S(1)}, u32[]{:S(2)}, u32[]{:S(2)}) collective-permute-start(f32[64,128]{1,0:T(8,128)S(1)} %get-tuple-element.71.refs_0_), channel_id=1, source_target_pairs={{0,1},{1,0},{2,3},{3,2},{4,5},{5,4},{6,7},{7,6},{8,9},{9,8},{10,11... | collective-permute-start | bytes 98312 | tf_op jit(solution)/shard_map/ppermute | solution.py:598
  81.7 5.2 %collective-permute-start.18 = (f32[64,128]{1,0:T(8,128)S(1)}, f32[64,128]{1,0:T(8,128)S(1)}, u32[]{:S(2)}, u32[]{:S(2)}) collective-permute-start(f32[64,128]{1,0:T(8,128)S(1)} %get-tuple-element.71.refs_0_), channel_id=1, source_target_pairs={{0,2},{1,3},{2,0},{3,1},{4,6},{5,7},{6,4},{7,5},{8,10},{9,11},{10,... | collective-permute-start | bytes 98312 | tf_op jit(solution)/shard_map/ppermute | solution.py:598
  81.7 5.8 %collective-permute-start.19 = (f32[64,128]{1,0:T(8,128)S(1)}, f32[64,128]{1,0:T(8,128)S(1)}, u32[]{:S(2)}, u32[]{:S(2)}) collective-permute-start(f32[64,128]{1,0:T(8,128)S(1)} %get-tuple-element.71.refs_0_), channel_id=1, source_target_pairs={{0,3},{1,2},{2,1},{3,0},{4,7},{5,6},{6,5},{7,4},{8,11},{9,10},{10,... | collective-permute-start | bytes 98312 | tf_op jit(solution)/shard_map/ppermute | solution.py:598
  (1 other events, 7.0 us)

commit v13 on v12

--- a/solution.py
+++ b/solution.py
@@ -245,39 +245,37 @@
     return own, v_gram
 
 
-def pair_inverse(a, b, c, d):
-    scale = 1.0 / (a * d - b * c)
-    return d * scale, b * scale, c * scale, a * scale
+def solve_tile(columns, tile):
+    rows = lax.broadcasted_iota(jnp.int32, tile.shape, 0)
+    for a in range(0, 8, 2):
+        b = a + 1
+        first, second = columns[a], columns[b]
+        m_aa, m_ab, m_ba, m_bb = first[a:b], second[a:b], first[b : b + 1], second[b : b + 1]
+        scale = 1.0 / (m_aa * m_bb - m_ab * m_ba)
+        m_aa, m_ab, m_ba, m_bb = m_aa * scale, m_ab * scale, m_ba * scale, m_bb * scale
+
+        def step(x):
+            x_a, x_b = x[a:b], x[b : b + 1]
+            new_a, new_b = m_bb * x_a - m_ab * x_b, m_aa * x_b - m_ba * x_a
+            x = x - (first * new_a + second * new_b)
+            return jnp.where(rows == a, new_a, jnp.where(rows == b, new_b, x))
+
+        tile = step(tile)
+        columns = [step(x) if q > b else x for q, x in enumerate(columns)]
+    return tile
 
 
 def eliminate(table, rank):
     tiles = [table[8 * t : 8 * t + 8] for t in range(rank // 8)]
-    rows = lax.broadcasted_iota(jnp.int32, tiles[0].shape, 0)
-    for i in range(0, rank, 4):
-        columns = [[jnp.broadcast_to(t[:, i + q : i + q + 1], t.shape) for q in range(4)] for t in tiles]
-        home, first = i // 8, i % 8
-        r0, r1, r2, r3 = (tiles[home][first + q : first + q + 1] for q in range(4))
-        m = [[columns[home][q][first + p : first + p + 1] for q in range(4)] for p in range(4)]
-        d, b, c, a = pair_inverse(m[0][0], m[0][1], m[1][0], m[1][1])
-        q02, q03 = d * m[0][2] - b * m[1][2], d * m[0][3] - b * m[1][3]
-        q12, q13 = a * m[1][2] - c * m[0][2], a * m[1][3] - c * m[0][3]
-        y0, y1 = d * r0 - b * r1, a * r1 - c * r0
-        z2 = r2 - (m[2][0] * y0 + m[2][1] * y1)
-        z3 = r3 - (m[3][0] * y0 + m[3][1] * y1)
-        d, b, c, a = pair_inverse(
-            m[2][2] - (m[2][0] * q02 + m[2][1] * q12),
-            m[2][3] - (m[2][0] * q03 + m[2][1] * q13),
-            m[3][2] - (m[3][0] * q02 + m[3][1] * q12),
-            m[3][3] - (m[3][0] * q03 + m[3][1] * q13),
-        )
-        n2, n3 = d * z2 - b * z3, a * z3 - c * z2
-        new = [y0 - (q02 * n2 + q03 * n3), y1 - (q12 * n2 + q13 * n3), n2, n3]
-        for t, (c0, c1, c2, c3) in enumerate(columns):
-            tile = tiles[t] - ((c0 * new[0] + c1 * new[1]) + (c2 * new[2] + c3 * new[3]))
-            if t == home:
-                for q in range(4):
-                    tile = jnp.where(rows == first + q, new[q], tile)
-            tiles[t] = tile
+    for home in range(rank // 8):
+        first = 8 * home
+        columns = [[jnp.broadcast_to(t[:, q : q + 1], t.shape) for q in range(first, first + 8)] for t in tiles]
+        solved = solve_tile(columns[home], tiles[home])
+        for t, tile in enumerate(tiles):
+            terms = [column * solved[q : q + 1] for q, column in enumerate(columns[t])]
+            while len(terms) > 1:
+                terms = [x + y for x, y in zip(terms[::2], terms[1::2])]
+            tiles[t] = solved if t == home else tile - terms[0]
     return jnp.concatenate(tiles, axis=0)
 
 
@@ -605,10 +603,9 @@
     return [x] + [swap(x, axis, s) for s in range(1, n)]
 
 
-def staged_terms(x, axis, after, far_first=False):
+def staged_terms(x, axis, after):
     n = lax.axis_size(axis)
     steps = [1 << i for i in range(n.bit_length() - 1)]
-    steps = steps[::-1] if far_first else steps
     for step in steps[:-1]:
         x = add(x, swap(x, axis, step), after)
     return [x, swap(x, axis, steps[-1])]
@@ -661,6 +658,8 @@
         return [slot ^ bit for slot in send(bit)]
 
     w_grams = staged_terms(own_w_gram(w_start), "patient", [])
+    own, v_gram = project_own(n_parts, place, by_owner, v_near)
+    h_local = v_gram
     arrived = [[] for _ in firsts]
     for i, bit in enumerate(bits):
         layouts = [receive(before) for before in bits[:i]]
@@ -668,13 +667,11 @@
             if i == 0 and part == 0:
                 code = first_projection(send(bit), count, place, in_hbm, v_rows)
             else:
-                after = [w_grams[part]] if i else []
+                after = [w_grams[part]] + [v_gram] * part if i else []
                 code = next_projection(
                     send(bit), first, count, layouts, place, by_owner, v_near, arrived[part], after
                 )
             arrived[part] = arrived[part] + [swap(code, "feature", bit)]
-    own, v_gram = project_own(n_parts, place, by_owner, v_near)
-    h_local = v_gram
 
     layouts = [receive(bit) for bit in bits]
     frames = [[] for _ in firsts]
@@ -706,11 +703,11 @@
     h_sum = add(*h_sums, [])
     double(n_parts - 1, [h_sum])
     order = [(part, k) for part in range(n_parts) for k in range(1, last + 1)]
+    h_terms = all_terms(h_sum, "feature")
     more, token = project_groups(order[:-2], [h_sum])
     projected |= more
     w_gram, inverse = first_inverse(v_gram, w_grams, token)
-    h_terms = staged_terms(h_sum, "feature", [inverse], far_first=True)
-    after = h_terms[:1]
+    after = [inverse]
     for group in order[-2:]:
         more, token = project_groups([group], after)
         projected |= more

time: 91 us -> 90.3 us (level)
  Pallas kernels: 39.7 us -> 36.6 us
  waiting for transfers between devices: 17 us -> 19.2 us
    ppermute x20 -> x21, waiting for transfers between devices: 17 us -> 19.2 us  [swap(): return lax.ppermute(x, axis, pairs)]
    pallas_call x1, Pallas kernels: 3.36 us -> 2.27 us  [next_w(): pl.pallas_call(functools.partial(next_w_kernel, len(sums)), out_shape=jax...]
    pallas_call x1, Pallas kernels: 2.58 us -> 1.55 us  [first_inverse(): pl.pallas_call(first_inverse_kernel, in_specs=[VMEM_SPEC] * (1 + len(w_gr...]
    pallas_call x1, Pallas kernels: 2.73 us -> 1.7 us  [second_inverse(): pl.pallas_call(second_inverse_kernel, out_shape=[out, out], compiler_para...]
    ppermute x20 -> x21, starting transfers between devices: 33.2 us -> 33.3 us  [swap(): return lax.ppermute(x, axis, pairs)]
  transfers between devices with their start and end apart: 20 -> 21, of which waited for: 12 -> 12; matrix products, arithmetic and copies ran while one was open for 0% -> 0% of each run, Pallas kernels for 29% -> 27%
where the time goes in v13:
time: 90.3 us; the launch traced here: 90.1 us
  Pallas kernels  36.6 us (41%)
  starting transfers between devices  33.3 us (37%)
  waiting for transfers between devices  19.2 us (21%)
    ppermute x21, starting transfers between devices, swap(): return lax.ppermute(x, axis, pairs)  33.3 us
    ppermute x21, waiting for transfers between devices, swap(): return lax.ppermute(x, axis, pairs)  19.2 us
    pallas_call x2, Pallas kernels, own_frames(): pl.pallas_call(functools.partial(frames_kernel, layouts, part, share), in...  12.5 us
    pallas_call x1, Pallas kernels, first_projection(): pl.pallas_call(functools.partial(first_projection_kernel, slots), in_spec...  3.91 us
    pallas_call x3, Pallas kernels, next_projection(): pl.pallas_call(functools.partial(next_projection_kernel, slots, first, co...  3.51 us
    pallas_call x4, Pallas kernels, project_frames(): pl.pallas_call(functools.partial(projected_kernel, items), in_specs=[SMEM...  3.49 us
    pallas_call x1, Pallas kernels, next_v(): pl.pallas_call(functools.partial(next_v_kernel, items, share), in_specs=[...  3.28 us
    pallas_call x1, Pallas kernels, next_w(): pl.pallas_call(functools.partial(next_w_kernel, len(sums)), out_shape=jax...  2.27 us
  transfers between devices with their start and end apart: 21, of which 12 were waited for; matrix products, arithmetic and copies ran while one was open for 0% of the time, Pallas kernels for 27%

profile of v13, /device:TPU:0, one launch (start us, length us, event | category | flops | bytes accessed | tf_op | source)
XLA Modules:
  0.0 90.1 jit_solution(10009766434209875733)
XLA Ops:
  0.7 3.9 %project_first.1 = s16[560,256]{1,0:T(8,128)(2,1)S(1)} custom-call(s32[1]{0:T(128)} %bitcast.place, bf16[64,1024]{1,0:T(8,128)(2,1)} %bitcast.13, bf16[4,8,256,1024]{3,2,1,0:T(8,128)(2,1)} %bitcast.4), custom_call_target="tpu_custom_call" | custom-call | flops 1000 | bytes 1000 | tf_op jit(solution)/shard_map/project_first/pallas_call | solution.py:158
  4.6 3.0 %collective-permute-start = (s16[560,256]{1,0:T(8,128)(2,1)S(1)}, s16[560,256]{1,0:T(8,128)(2,1)S(1)}, u32[]{:S(2)}, u32[]{:S(2)}) collective-permute-start(s16[560,256]{1,0:T(8,128)(2,1)S(1)} %project_first.1), channel_id=1, source_target_pairs={{0,1},{1,0},{2,3},{3,2},{4,5},{5,4},{6,7},{7,6},{8,9},{9,8},{10,11... | collective-permute-start | bytes 860168 | tf_op jit(solution)/shard_map/ppermute | solution.py:596
  7.8 1.6 %project_next.4 = s16[528,256]{1,0:T(8,128)(2,1)S(1)} custom-call(s32[1]{0:T(128)} %bitcast.place, bf16[64,1024]{1,0:T(8,128)(2,1)S(1)} %bitcast.14, bf16[4,8,256,1024]{3,2,1,0:T(8,128)(2,1)S(1)} %bitcast.5), custom_call_target="tpu_custom_call" | custom-call | flops 1000 | bytes 1000 | tf_op jit(solution)/shard_map/project_next/pallas_call | solution.py:196
  9.4 3.1 %collective-permute-start.3 = (s16[528,256]{1,0:T(8,128)(2,1)S(1)}, s16[528,256]{1,0:T(8,128)(2,1)S(1)}, u32[]{:S(2)}, u32[]{:S(2)}) collective-permute-start(s16[528,256]{1,0:T(8,128)(2,1)S(1)} %project_next.4), channel_id=1, source_target_pairs={{0,1},{1,0},{2,3},{3,2},{4,5},{5,4},{6,7},{7,6},{8,9},{9,8},{10,11... | collective-permute-start | bytes 811016 | tf_op jit(solution)/shard_map/ppermute | solution.py:596
  16.3 3.3 %collective-permute-start.2 = (s16[304,256]{1,0:T(8,128)(2,1)S(1)}, s16[304,256]{1,0:T(8,128)(2,1)S(1)}, u32[]{:S(2)}, u32[]{:S(2)}) collective-permute-start(s16[304,256]{1,0:T(8,128)(2,1)S(1)} %project_next.3), channel_id=1, source_target_pairs={{0,2},{1,3},{2,0},{3,1},{4,6},{5,7},{6,4},{7,5},{8,10},{9,11},{10,... | collective-permute-start | bytes 466952 | tf_op jit(solution)/shard_map/ppermute | solution.py:596
  26.2 6.2 %own_frames.2 = (bf16[4,64,256]{2,1,0:T(8,128)(2,1)S(1)}, f32[64,64]{1,0:T(8,128)S(1)}, f32[64,64]{1,0:T(8,128)S(1)}) custom-call(s32[1]{0:T(128)} %bitcast.place, s32[32]{0:T(128)S(1)} %copy-done.4, f32[64,64]{1,0:T(8,128)S(1)} %copy-done.3, f32[32,64]{1,0:T(8,128)S(1)} %copy-done.2, f32[64,64]{1,0:T(8,128)S(1)} %get-tuple-element.38.v_gram_ref.before_ref.refs_2_, ...), custom_call_target="tpu_custom_call" | custom-call | flops 1000 | bytes 1000 | tf_op jit(solution)/shard_map/own_frames/pallas_call | solution.py:377
  33.7 6.3 %own_frames.3 = (bf16[4,64,256]{2,1,0:T(8,128)(2,1)S(1)}, f32[64,64]{1,0:T(8,128)S(1)}, f32[64,64]{1,0:T(8,128)}) custom-call(s32[1]{0:T(128)} %bitcast.place, s32[32]{0:T(128)S(1)} %copy-done.4, f32[64,64]{1,0:T(8,128)S(1)} %copy-done.3, f32[32,64]{1,0:T(8,128)S(1)} %copy-done.2, f32[64,64]{1,0:T(8,128)S(1)} %get-tuple-element.40.v_gram_ref, ...), custom_call_target="tpu_custom_call" | custom-call | flops 1000 | bytes 1000 | tf_op jit(solution)/shard_map/own_frames/pallas_call | solution.py:377
  40.0 1.7 %collective-permute-start.13 = (bf16[4,64,256]{2,1,0:T(8,128)(2,1)S(1)}, bf16[4,64,256]{2,1,0:T(8,128)(2,1)S(1)}, u32[]{:S(2)}, u32[]{:S(2)}) collective-permute-start(bf16[4,64,256]{2,1,0:T(8,128)(2,1)S(1)} %get-tuple-element.45.refs_1_.refs_0_), channel_id=1, source_target_pairs={{0,2},{1,3},{2,0},{3,1},{4,6},{5,7},{6,4},{7,5},{8,10},{9,11},{10,... | collective-permute-start | bytes 393224 | tf_op jit(solution)/shard_map/ppermute | solution.py:596
  43.0 1.9 %collective-permute-start.8 = (f32[64,64]{1,0:T(8,128)S(1)}, f32[64,64]{1,0:T(8,128)S(1)}, u32[]{:S(2)}, u32[]{:S(2)}) collective-permute-start(f32[64,64]{1,0:T(8,128)S(1)} %add_terms.6.a_ref), channel_id=1, source_target_pairs={{0,8},{4,12},{8,0},{12,4},{1,9},{5,13},{9,1},{13,5},{2,10},{6,14},... | collective-permute-start | bytes 49160 | tf_op jit(solution)/shard_map/ppermute | solution.py:596
  44.9 3.6 %collective-permute-start.12 = (bf16[8,64,256]{2,1,0:T(8,128)(2,1)S(1)}, bf16[8,64,256]{2,1,0:T(8,128)(2,1)S(1)}, u32[]{:S(2)}, u32[]{:S(2)}) collective-permute-start(bf16[8,64,256]{2,1,0:T(8,128)(2,1)S(1)} %join_frames.2.refs_2_), channel_id=1, source_target_pairs={{0,1},{1,0},{2,3},{3,2},{4,5},{5,4},{6,7},{7,6},{8,9},{9,8},{10,11... | collective-permute-start | bytes 786440 | tf_op jit(solution)/shard_map/ppermute | solution.py:596
  48.5 3.1 %collective-permute-start.14 = (bf16[8,64,256]{2,1,0:T(8,128)(2,1)S(1)}, bf16[8,64,256]{2,1,0:T(8,128)(2,1)S(1)}, u32[]{:S(2)}, u32[]{:S(2)}) collective-permute-start(bf16[8,64,256]{2,1,0:T(8,128)(2,1)S(1)} %join_frames.3), channel_id=1, source_target_pairs={{0,1},{1,0},{2,3},{3,2},{4,5},{5,4},{6,7},{7,6},{8,9},{9,8},{10,11... | collective-permute-start | bytes 786440 | tf_op jit(solution)/shard_map/ppermute | solution.py:596
  51.7 2.2 %collective-permute-start.10 = (f32[64,64]{1,0:T(8,128)S(1)}, f32[64,64]{1,0:T(8,128)S(1)}, u32[]{:S(2)}, u32[]{:S(2)}) collective-permute-start(f32[64,64]{1,0:T(8,128)S(1)} %add_terms.7.refs_2_.refs_0_), channel_id=1, source_target_pairs={{0,2},{1,3},{2,0},{3,1},{4,6},{5,7},{6,4},{7,5},{8,10},{9,11},{10,... | collective-permute-start | bytes 49160 | tf_op jit(solution)/shard_map/ppermute | solution.py:596
  53.9 2.1 %collective-permute-start.11 = (f32[64,64]{1,0:T(8,128)S(1)}, f32[64,64]{1,0:T(8,128)S(1)}, u32[]{:S(2)}, u32[]{:S(2)}) collective-permute-start(f32[64,64]{1,0:T(8,128)S(1)} %add_terms.7.refs_2_.refs_0_), channel_id=1, source_target_pairs={{0,3},{1,2},{2,1},{3,0},{4,7},{5,6},{6,5},{7,4},{8,11},{9,10},{10,... | collective-permute-start | bytes 49160 | tf_op jit(solution)/shard_map/ppermute | solution.py:596
  57.2 1.6 %first_inverse.1 = (f32[64,64]{1,0:T(8,128)S(1)}, f32[64,64]{1,0:T(8,128)S(1)}) custom-call(f32[64,64]{1,0:T(8,128)S(1)} %get-tuple-element.40.v_gram_ref, f32[64,64]{1,0:T(8,128)S(1)} %add_terms.5.refs_1_.refs_0_, f32[64,64]{1,0:T(8,128)S(1)} %collective-permute-done.4.refs_1_, f32[8,128]{1,0:T(8,128)S(1)} %get-tuple-element.47.refs_2_), custom_call_target="tpu_custom_call" | custom-call | flops 1000 | bytes 1000 | tf_op jit(solution)/shard_map/first_inverse/pallas_call | solution.py:304
  59.3 2.3 %collective-permute-done.14.refs_0_ = bf16[8,64,256]{2,1,0:T(8,128)(2,1)S(1)} collective-permute-done((bf16[8,64,256]{2,1,0:T(8,128)(2,1)S(1)}, bf16[8,64,256]{2,1,0:T(8,128)(2,1)S(1)}, u32[]{:S(2)}, u32[]{:S(2)}) %collective-permute-start.14) | collective-permute-done | bytes 262176 | tf_op jit(solution)/shard_map/ppermute | solution.py:596
  62.5 2.4 %collective-permute-done.11.refs_3_ = f32[64,64]{1,0:T(8,128)S(1)} collective-permute-done((f32[64,64]{1,0:T(8,128)S(1)}, f32[64,64]{1,0:T(8,128)S(1)}, u32[]{:S(2)}, u32[]{:S(2)}) %collective-permute-start.11) | collective-permute-done | bytes 16416 | tf_op jit(solution)/shard_map/ppermute | solution.py:596
  65.9 1.6 %v_terms.1 = (f32[64,512]{1,0:T(8,128)S(1)}, f32[64,512]{1,0:T(8,128)S(1)}) custom-call(s32[1]{0:T(128)} %bitcast.place, bf16[4,192,512]{2,1,0:T(8,128)(2,1)S(1)} %get-tuple-element.52.factor_ref, bf16[256,1024]{1,0:T(8,128)(2,1)S(1)} %get-tuple-element.53.refs_0_, bf16[256,1024]{1,0:T(8,128)(2,1)S(1)} %get-tuple-element.54.refs_1_, ...), custom_call_target="tpu_custom_call" | custom-call | flops 1000 | bytes 1000 | tf_op jit(solution)/shard_map/v_terms/pallas_call | solution.py:522
  69.9 1.7 %second_inverse.1 = (f32[64,64]{1,0:T(8,128)S(1)}, f32[64,64]{1,0:T(8,128)S(1)}) custom-call(f32[64,64]{1,0:T(8,128)S(1)} %get-tuple-element.67.h_ref, f32[64,64]{1,0:T(8,128)S(1)} %get-tuple-element.68.w_gram_ref), custom_call_target="tpu_custom_call" | custom-call | flops 1000 | bytes 1000 | tf_op jit(solution)/shard_map/second_inverse/pallas_call | solution.py:490
  71.6 3.0 %collective-permute-done.16.b_ref = f32[64,512]{1,0:T(8,128)S(1)} collective-permute-done((f32[64,512]{1,0:T(8,128)S(1)}, f32[64,512]{1,0:T(8,128)S(1)}, u32[]{:S(2)}, u32[]{:S(2)}) %collective-permute-start.16) | collective-permute-done | bytes 131104 | tf_op jit(solution)/shard_map/ppermute | solution.py:596
  76.0 3.3 %next_v.1 = (f32[64,1024]{1,0:T(8,128)}, f32[64,128]{1,0:T(8,128)S(1)}) custom-call(s32[1]{0:T(128)} %bitcast.place, f32[64,512]{1,0:T(8,128)S(1)} %add_terms.9.own_ref, f32[64,512]{1,0:T(8,128)S(1)} %collective-permute-done.17.other_ref, f32[64,64]{1,0:T(8,128)S(1)} %get-tuple-element.69.refs_0_.inverse_ref, f32[64,64]{1,0:T(8,128)S(1)} %get-tuple-element.67.h_ref, ...), custom_call_target="tpu_custom_call" | custom-call | flops 1000 | bytes 1000 | tf_op jit(solution)/shard_map/next_v/pallas_call | solution.py:560
  79.5 2.6 %collective-permute-start.19 = (f32[64,128]{1,0:T(8,128)S(1)}, f32[64,128]{1,0:T(8,128)S(1)}, u32[]{:S(2)}, u32[]{:S(2)}) collective-permute-start(f32[64,128]{1,0:T(8,128)S(1)} %get-tuple-element.71.refs_0_), channel_id=1, source_target_pairs={{0,2},{1,3},{2,0},{3,1},{4,6},{5,7},{6,4},{7,5},{8,10},{9,11},{10,... | collective-permute-start | bytes 98312 | tf_op jit(solution)/shard_map/ppermute | solution.py:596
  82.1 1.5 %collective-permute-start.20 = (f32[64,128]{1,0:T(8,128)S(1)}, f32[64,128]{1,0:T(8,128)S(1)}, u32[]{:S(2)}, u32[]{:S(2)}) collective-permute-start(f32[64,128]{1,0:T(8,128)S(1)} %get-tuple-element.71.refs_0_), channel_id=1, source_target_pairs={{0,3},{1,2},{2,1},{3,0},{4,7},{5,6},{6,5},{7,4},{8,11},{9,10},{10,... | collective-permute-start | bytes 98312 | tf_op jit(solution)/shard_map/ppermute | solution.py:596
  84.9 2.9 %collective-permute-done.20.refs_3_ = f32[64,128]{1,0:T(8,128)S(1)} collective-permute-done((f32[64,128]{1,0:T(8,128)S(1)}, f32[64,128]{1,0:T(8,128)S(1)}, u32[]{:S(2)}, u32[]{:S(2)}) %collective-permute-start.20) | collective-permute-done | bytes 32800 | tf_op jit(solution)/shard_map/ppermute | solution.py:596
  87.8 2.3 %next_w.1 = f32[32,64]{1,0:T(8,128)} custom-call(f32[64,128]{1,0:T(8,128)S(1)} %get-tuple-element.71.refs_0_, f32[64,128]{1,0:T(8,128)S(1)} %collective-permute-done.18.refs_1_, f32[64,128]{1,0:T(8,128)S(1)} %collective-permute-done.19.refs_2_, f32[64,128]{1,0:T(8,128)S(1)} %collective-permute-done.20.refs_3_, f32[64,64]{1,0:T(8,128)S(1)} %get-tuple-element.72.refs_4_), custom_call_target="tpu_custom_call" | custom-call | flops 1000 | bytes 1000 | tf_op jit(solution)/shard_map/next_w/pallas_call | solution.py:585
  (53 shorter events, 22.1 us)
Async XLA Ops:
  0.7 11.8 %copy-start.2 = (f32[32,64]{1,0:T(8,128)S(1)}, f32[32,64]{1,0:T(8,128)}, u32[]{:S(2)}) copy-start(f32[32,64]{1,0:T(8,128)} %refs_5_.1) | copy-start | bytes 24580
  4.6 10.7 %collective-permute-start = (s16[560,256]{1,0:T(8,128)(2,1)S(1)}, s16[560,256]{1,0:T(8,128)(2,1)S(1)}, u32[]{:S(2)}, u32[]{:S(2)}) collective-permute-start(s16[560,256]{1,0:T(8,128)(2,1)S(1)} %project_first.1), channel_id=1, source_target_pairs={{0,1},{1,0},{2,3},{3,2},{4,5},{5,4},{6,7},{7,6},{8,9},{9,8},{10,11... | collective-permute-start | bytes 860168 | tf_op jit(solution)/shard_map/ppermute | solution.py:596
  9.4 14.2 %collective-permute-start.3 = (s16[528,256]{1,0:T(8,128)(2,1)S(1)}, s16[528,256]{1,0:T(8,128)(2,1)S(1)}, u32[]{:S(2)}, u32[]{:S(2)}) collective-permute-start(s16[528,256]{1,0:T(8,128)(2,1)S(1)} %project_next.4), channel_id=1, source_target_pairs={{0,1},{1,0},{2,3},{3,2},{4,5},{5,4},{6,7},{7,6},{8,9},{9,8},{10,11... | collective-permute-start | bytes 811016 | tf_op jit(solution)/shard_map/ppermute | solution.py:596
  12.6 1.3 %collective-permute-start.1 = (f32[64,64]{1,0:T(8,128)S(1)}, f32[64,64]{1,0:T(8,128)S(1)}, u32[]{:S(2)}, u32[]{:S(2)}) collective-permute-start(f32[64,64]{1,0:T(8,128)S(1)} %own_w_gram.1.a_ref), channel_id=1, source_target_pairs={{0,4},{4,0},{8,12},{12,8},{1,5},{5,1},{9,13},{13,9},{2,6},{6,2},{1... | collective-permute-start | bytes 49160 | tf_op jit(solution)/shard_map/ppermute | solution.py:596
  16.3 9.9 %copy-start.3 = (f32[64,64]{1,0:T(8,128)S(1)}, f32[64,64]{1,0:T(8,128)}, u32[]{:S(2)}) copy-start(f32[64,64]{1,0:T(8,128)} %h_ref.3) | copy-start | bytes 49156
  16.3 9.9 %copy-start.4 = (s32[32]{0:T(128)S(1)}, s32[32]{0:T(128)}, u32[]{:S(2)}) copy-start(s32[32]{0:T(128)} %counts_ref.3) | copy-start | bytes 388
  16.3 9.9 %collective-permute-start.2 = (s16[304,256]{1,0:T(8,128)(2,1)S(1)}, s16[304,256]{1,0:T(8,128)(2,1)S(1)}, u32[]{:S(2)}, u32[]{:S(2)}) collective-permute-start(s16[304,256]{1,0:T(8,128)(2,1)S(1)} %project_next.3), channel_id=1, source_target_pairs={{0,2},{1,3},{2,0},{3,1},{4,6},{5,7},{6,4},{7,5},{8,10},{9,11},{10,... | collective-permute-start | bytes 466952 | tf_op jit(solution)/shard_map/ppermute | solution.py:596
  19.6 3.9 %collective-permute-start.4 = (f32[64,64]{1,0:T(8,128)S(1)}, f32[64,64]{1,0:T(8,128)S(1)}, u32[]{:S(2)}, u32[]{:S(2)}) collective-permute-start(f32[64,64]{1,0:T(8,128)S(1)} %add_terms.5.refs_1_.refs_0_), channel_id=1, source_target_pairs={{0,8},{4,12},{8,0},{12,4},{1,9},{5,13},{9,1},{13,5},{2,10},{6,14},... | collective-permute-start | bytes 49160 | tf_op jit(solution)/shard_map/ppermute | solution.py:596
  24.5 9.2 %collective-permute-start.5 = (s16[272,256]{1,0:T(8,128)(2,1)S(1)}, s16[272,256]{1,0:T(8,128)(2,1)S(1)}, u32[]{:S(2)}, u32[]{:S(2)}) collective-permute-start(s16[272,256]{1,0:T(8,128)(2,1)S(1)} %project_next.5), channel_id=1, source_target_pairs={{0,2},{1,3},{2,0},{3,1},{4,6},{5,7},{6,4},{7,5},{8,10},{9,11},{10,... | collective-permute-start | bytes 417800 | tf_op jit(solution)/shard_map/ppermute | solution.py:596
  32.4 9.4 %collective-permute-start.7 = (bf16[4,64,256]{2,1,0:T(8,128)(2,1)S(1)}, bf16[4,64,256]{2,1,0:T(8,128)(2,1)S(1)}, u32[]{:S(2)}, u32[]{:S(2)}) collective-permute-start(bf16[4,64,256]{2,1,0:T(8,128)(2,1)S(1)} %get-tuple-element.44.refs_0_), channel_id=1, source_target_pairs={{0,2},{1,3},{2,0},{3,1},{4,6},{5,7},{6,4},{7,5},{8,10},{9,11},{10,... | collective-permute-start | bytes 393224 | tf_op jit(solution)/shard_map/ppermute | solution.py:596
  40.0 8.4 %collective-permute-start.13 = (bf16[4,64,256]{2,1,0:T(8,128)(2,1)S(1)}, bf16[4,64,256]{2,1,0:T(8,128)(2,1)S(1)}, u32[]{:S(2)}, u32[]{:S(2)}) collective-permute-start(bf16[4,64,256]{2,1,0:T(8,128)(2,1)S(1)} %get-tuple-element.45.refs_1_.refs_0_), channel_id=1, source_target_pairs={{0,2},{1,3},{2,0},{3,1},{4,6},{5,7},{6,4},{7,5},{8,10},{9,11},{10,... | collective-permute-start | bytes 393224 | tf_op jit(solution)/shard_map/ppermute | solution.py:596
  41.8 1.2 %collective-permute-start.6 = (f32[64,64]{1,0:T(8,128)S(1)}, f32[64,64]{1,0:T(8,128)S(1)}, u32[]{:S(2)}, u32[]{:S(2)}) collective-permute-start(f32[64,64]{1,0:T(8,128)S(1)} %get-tuple-element.43.a_ref), channel_id=1, source_target_pairs={{0,4},{4,0},{8,12},{12,8},{1,5},{5,1},{9,13},{13,9},{2,6},{6,2},{1... | collective-permute-start | bytes 49160 | tf_op jit(solution)/shard_map/ppermute | solution.py:596
  43.0 5.5 %collective-permute-start.8 = (f32[64,64]{1,0:T(8,128)S(1)}, f32[64,64]{1,0:T(8,128)S(1)}, u32[]{:S(2)}, u32[]{:S(2)}) collective-permute-start(f32[64,64]{1,0:T(8,128)S(1)} %add_terms.6.a_ref), channel_id=1, source_target_pairs={{0,8},{4,12},{8,0},{12,4},{1,9},{5,13},{9,1},{13,5},{2,10},{6,14},... | collective-permute-start | bytes 49160 | tf_op jit(solution)/shard_map/ppermute | solution.py:596
  44.9 11.1 %collective-permute-start.12 = (bf16[8,64,256]{2,1,0:T(8,128)(2,1)S(1)}, bf16[8,64,256]{2,1,0:T(8,128)(2,1)S(1)}, u32[]{:S(2)}, u32[]{:S(2)}) collective-permute-start(bf16[8,64,256]{2,1,0:T(8,128)(2,1)S(1)} %join_frames.2.refs_2_), channel_id=1, source_target_pairs={{0,1},{1,0},{2,3},{3,2},{4,5},{5,4},{6,7},{7,6},{8,9},{9,8},{10,11... | collective-permute-start | bytes 786440 | tf_op jit(solution)/shard_map/ppermute | solution.py:596
  48.5 13.1 %collective-permute-start.14 = (bf16[8,64,256]{2,1,0:T(8,128)(2,1)S(1)}, bf16[8,64,256]{2,1,0:T(8,128)(2,1)S(1)}, u32[]{:S(2)}, u32[]{:S(2)}) collective-permute-start(bf16[8,64,256]{2,1,0:T(8,128)(2,1)S(1)} %join_frames.3), channel_id=1, source_target_pairs={{0,1},{1,0},{2,3},{3,2},{4,5},{5,4},{6,7},{7,6},{8,9},{9,8},{10,11... | collective-permute-start | bytes 786440 | tf_op jit(solution)/shard_map/ppermute | solution.py:596
  51.6 10.9 %collective-permute-start.9 = (f32[64,64]{1,0:T(8,128)S(1)}, f32[64,64]{1,0:T(8,128)S(1)}, u32[]{:S(2)}, u32[]{:S(2)}) collective-permute-start(f32[64,64]{1,0:T(8,128)S(1)} %add_terms.7.refs_2_.refs_0_), channel_id=1, source_target_pairs={{0,1},{1,0},{2,3},{3,2},{4,5},{5,4},{6,7},{7,6},{8,9},{9,8},{10,11... | collective-permute-start | bytes 49160 | tf_op jit(solution)/shard_map/ppermute | solution.py:596
  51.7 10.8 %collective-permute-start.10 = (f32[64,64]{1,0:T(8,128)S(1)}, f32[64,64]{1,0:T(8,128)S(1)}, u32[]{:S(2)}, u32[]{:S(2)}) collective-permute-start(f32[64,64]{1,0:T(8,128)S(1)} %add_terms.7.refs_2_.refs_0_), channel_id=1, source_target_pairs={{0,2},{1,3},{2,0},{3,1},{4,6},{5,7},{6,4},{7,5},{8,10},{9,11},{10,... | collective-permute-start | bytes 49160 | tf_op jit(solution)/shard_map/ppermute | solution.py:596
  53.9 11.0 %collective-permute-start.11 = (f32[64,64]{1,0:T(8,128)S(1)}, f32[64,64]{1,0:T(8,128)S(1)}, u32[]{:S(2)}, u32[]{:S(2)}) collective-permute-start(f32[64,64]{1,0:T(8,128)S(1)} %add_terms.7.refs_2_.refs_0_), channel_id=1, source_target_pairs={{0,3},{1,2},{2,1},{3,0},{4,7},{5,6},{6,5},{7,4},{8,11},{9,10},{10,... | collective-permute-start | bytes 49160 | tf_op jit(solution)/shard_map/ppermute | solution.py:596
  67.5 1.4 %collective-permute-start.15 = (f32[64,512]{1,0:T(8,128)S(1)}, f32[64,512]{1,0:T(8,128)S(1)}, u32[]{:S(2)}, u32[]{:S(2)}) collective-permute-start(f32[64,512]{1,0:T(8,128)S(1)} %get-tuple-element.66), channel_id=1, source_target_pairs={{0,4},{4,0},{8,12},{12,8},{1,5},{5,1},{9,13},{13,9},{2,6},{6,2},{1... | collective-permute-start | bytes 393224 | tf_op jit(solution)/shard_map/ppermute | solution.py:596
  68.9 5.6 %collective-permute-start.16 = (f32[64,512]{1,0:T(8,128)S(1)}, f32[64,512]{1,0:T(8,128)S(1)}, u32[]{:S(2)}, u32[]{:S(2)}) collective-permute-start(f32[64,512]{1,0:T(8,128)S(1)} %add_terms.8.a_ref), channel_id=1, source_target_pairs={{0,8},{4,12},{8,0},{12,4},{1,9},{5,13},{9,1},{13,5},{2,10},{6,14},... | collective-permute-start | bytes 393224 | tf_op jit(solution)/shard_map/ppermute | solution.py:596
  74.6 1.4 %collective-permute-start.17 = (f32[64,512]{1,0:T(8,128)S(1)}, f32[64,512]{1,0:T(8,128)S(1)}, u32[]{:S(2)}, u32[]{:S(2)}) collective-permute-start(f32[64,512]{1,0:T(8,128)S(1)} %add_terms.9.own_ref), channel_id=1, source_target_pairs={{0,4},{4,0},{8,12},{12,8},{1,5},{5,1},{9,13},{13,9},{2,6},{6,2},{1... | collective-permute-start | bytes 393224 | tf_op jit(solution)/shard_map/ppermute | solution.py:596
  79.3 4.4 %collective-permute-start.18 = (f32[64,128]{1,0:T(8,128)S(1)}, f32[64,128]{1,0:T(8,128)S(1)}, u32[]{:S(2)}, u32[]{:S(2)}) collective-permute-start(f32[64,128]{1,0:T(8,128)S(1)} %get-tuple-element.71.refs_0_), channel_id=1, source_target_pairs={{0,1},{1,0},{2,3},{3,2},{4,5},{5,4},{6,7},{7,6},{8,9},{9,8},{10,11... | collective-permute-start | bytes 98312 | tf_op jit(solution)/shard_map/ppermute | solution.py:596
  79.5 5.4 %collective-permute-start.19 = (f32[64,128]{1,0:T(8,128)S(1)}, f32[64,128]{1,0:T(8,128)S(1)}, u32[]{:S(2)}, u32[]{:S(2)}) collective-permute-start(f32[64,128]{1,0:T(8,128)S(1)} %get-tuple-element.71.refs_0_), channel_id=1, source_target_pairs={{0,2},{1,3},{2,0},{3,1},{4,6},{5,7},{6,4},{7,5},{8,10},{9,11},{10,... | collective-permute-start | bytes 98312 | tf_op jit(solution)/shard_map/ppermute | solution.py:596
  82.1 5.7 %collective-permute-start.20 = (f32[64,128]{1,0:T(8,128)S(1)}, f32[64,128]{1,0:T(8,128)S(1)}, u32[]{:S(2)}, u32[]{:S(2)}) collective-permute-start(f32[64,128]{1,0:T(8,128)S(1)} %get-tuple-element.71.refs_0_), channel_id=1, source_target_pairs={{0,3},{1,2},{2,1},{3,0},{4,7},{5,6},{6,5},{7,4},{8,11},{9,10},{10,... | collective-permute-start | bytes 98312 | tf_op jit(solution)/shard_map/ppermute | solution.py:596
  (2 other events, 14.1 us)

commit v14 on v13

--- a/solution.py
+++ b/solution.py
@@ -130,7 +130,7 @@
     coded_ref[pl.ds(end, rows), :] = last.astype(jnp.int32).astype(jnp.int16)
 
 
-def first_projection_kernel(slots, place, v_hbm, visits_ref, coded_ref, v_ref, buffers, sems, v_sem):
+def first_projection_kernel(slots, with_gram, place, v_hbm, visits_ref, coded_ref, v_ref, buffers, sems, v_sem):
     count = buffers.shape[1]
     v_copy = pltpu.make_async_copy(v_hbm, v_ref, v_sem)
     v_copy.start()
@@ -141,7 +141,6 @@
     for copy in copies:
         copy.start()
     v_copy.wait()
-    gram = low_dot(v_ref[...], v_ref[...], ROWS_BY_ROWS)
 
     def value(i, p):
         if p == 0:
@@ -149,17 +148,18 @@
         return low_dot(v_ref[...], buffers[i, p], ROWS_BY_ROWS)
 
     values = [functools.partial(value, i, p) for i in range(len(slots)) for p in range(count)]
+    gram = low_dot(v_ref[...], v_ref[...], ROWS_BY_ROWS) if with_gram else None
     encode(values, gram, coded_ref, v_ref.shape[0])
 
 
-def first_projection(slots, count, place, visits, v_rows):
+def first_projection(slots, count, with_gram, place, visits, v_rows):
     width = visits.shape[3]
     rank = v_rows.shape[0]
     return pl.pallas_call(
-        functools.partial(first_projection_kernel, slots),
+        functools.partial(first_projection_kernel, slots, with_gram),
         in_specs=[SMEM_SPEC, HBM_SPEC, HBM_SPEC],
         out_specs=VMEM_SPEC,
-        out_shape=jax.ShapeDtypeStruct(payload_shape(len(slots) * count, rank, visits.shape[2], True), jnp.int16),
+        out_shape=jax.ShapeDtypeStruct(payload_shape(len(slots) * count, rank, visits.shape[2], with_gram), jnp.int16),
         scratch_shapes=[
             pltpu.VMEM(v_rows.shape, BF16),
             pltpu.VMEM((len(slots), count) + visits.shape[2:], BF16),
@@ -172,10 +172,10 @@
     )(place, v_rows, visits)
 
 
-def next_projection_kernel(slots, first, count, layouts, place, v_ref, visits_ref, *refs):
+def next_projection_kernel(slots, first, count, with_gram, layouts, place, v_ref, visits_ref, *refs):
     coded_ref = refs[-1]
     rank = v_ref.shape[0]
-    arrived = [Payload(ref, layout, count, rank, first == 0) for ref, layout in zip(refs, layouts)]
+    arrived = [Payload(ref, layout, count, rank, with_gram) for ref, layout in zip(refs, layouts)]
 
     def value(slot, p):
         proj = low_dot(v_ref[...], visits_ref[feature_of(place) ^ slot, first + p], ROWS_BY_ROWS)
@@ -184,20 +184,20 @@
         return proj
 
     gram = None
-    if first == 0:
+    if with_gram:
         gram = low_dot(v_ref[...], v_ref[...], ROWS_BY_ROWS)
         for payload in arrived:
             gram = gram + payload.gram()
     encode([functools.partial(value, slot, p) for slot in slots for p in range(count)], gram, coded_ref, rank)
 
 
-def next_projection(slots, first, count, layouts, place, visits, v_rows, arrived, after):
+def next_projection(slots, first, count, with_gram, layouts, place, visits, v_rows, arrived, after):
     rank = v_rows.shape[0]
     return pl.pallas_call(
-        functools.partial(next_projection_kernel, slots, first, count, layouts),
+        functools.partial(next_projection_kernel, slots, first, count, with_gram, layouts),
         in_specs=[SMEM_SPEC] + [VMEM_SPEC] * (2 + len(arrived)) + [ANY_SPEC] * len(after),
         out_specs=VMEM_SPEC,
-        out_shape=jax.ShapeDtypeStruct(payload_shape(len(slots) * count, rank, visits.shape[2], first == 0), jnp.int16),
+        out_shape=jax.ShapeDtypeStruct(payload_shape(len(slots) * count, rank, visits.shape[2], with_gram), jnp.int16),
         compiler_params=parameters(LIMIT),
         cost_estimate=SHORT,
         name="project_next",
@@ -338,9 +338,9 @@
     pieces = [own_ref[p] for p in patients]
     v_gram = v_gram_ref[...]
     for code, layout in zip(coded, layouts):
-        payload = Payload(code, layout, count, rank, part == 0)
+        payload = Payload(code, layout, count, rank, (part + 1) * count == share)
         pieces = [pieces[p] + payload.proj(0, p) for p in patients]
-        if part == 0:
+        if payload.with_gram:
             v_gram = v_gram + payload.gram()
     v_total_ref[...] = v_gram
     for p in patients:
@@ -665,11 +665,11 @@
         layouts = [receive(before) for before in bits[:i]]
         for part, first in enumerate(firsts):
             if i == 0 and part == 0:
-                code = first_projection(send(bit), count, place, in_hbm, v_rows)
+                code = first_projection(send(bit), count, n_parts == 1, place, in_hbm, v_rows)
             else:
                 after = [w_grams[part]] + [v_gram] * part if i else []
                 code = next_projection(
-                    send(bit), first, count, layouts, place, by_owner, v_near, arrived[part], after
+                    send(bit), first, count, part == n_parts - 1, layouts, place, by_owner, v_near, arrived[part], after
                 )
             arrived[part] = arrived[part] + [swap(code, "feature", bit)]
 
@@ -692,24 +692,24 @@
         low, h_local, v_total = own_frames(
             layouts, part, n_parts, place, visit_counts, h_start, w_start, v_gram, h_local, own[part], arrived[part]
         )
-        v_gram = v_total if first == 0 else v_gram
+        v_gram = v_total
         frames[part].append(((0,), low))
-        if part < n_parts - 1:
-            joined = double(part, [])
 
     last = len(bits)
+    for part in range(n_parts - 1):
+        joined = double(part, [frames[-1][0][1]])
     projected, token = project_groups([(part, 0) for part in range(n_parts)], joined)
+    early = [(part, k) for part in range(n_parts - 1) for k in range(1, last + 1)]
     h_sums = staged_terms(h_local, "patient", [token])
-    h_sum = add(*h_sums, [])
-    double(n_parts - 1, [h_sum])
-    order = [(part, k) for part in range(n_parts) for k in range(1, last + 1)]
+    more, token = project_groups(early, h_sums[:1])
+    projected |= more
+    h_sum = add(*h_sums, [token])
+    joined = double(n_parts - 1, [h_sum])
     h_terms = all_terms(h_sum, "feature")
-    more, token = project_groups(order[:-2], [h_sum])
-    projected |= more
-    w_gram, inverse = first_inverse(v_gram, w_grams, token)
+    w_gram, inverse = first_inverse(v_gram, w_grams, joined[0])
     after = [inverse]
-    for group in order[-2:]:
-        more, token = project_groups([group], after)
+    for k in range(1, last + 1):
+        more, token = project_groups([(n_parts - 1, k)], after)
         projected |= more
         after = [token]
     h_result, h_next, factor = next_h(place, h_terms, inverse, w_start, n, token)

time: 90.3 us -> 86.9 us (0.962)
  starting transfers between devices: 33.3 us -> 28.3 us
  waiting for transfers between devices: 19.2 us -> 20.8 us
    ppermute x21, starting transfers between devices: 33.3 us -> 28.3 us  [swap(): return lax.ppermute(x, axis, pairs)]
    ppermute x21, waiting for transfers between devices: 19.2 us -> 20.8 us  [swap(): return lax.ppermute(x, axis, pairs)]
  transfers between devices with their start and end apart: 21 -> 21, of which waited for: 12 -> 13; matrix products, arithmetic and copies ran while one was open for 0% -> 0% of each run, Pallas kernels for 27% -> 28%
where the time goes in v14:
time: 86.9 us; the launch traced here: 86.8 us
  Pallas kernels  36.4 us (42%)
  starting transfers between devices  28.3 us (33%)
  waiting for transfers between devices  20.8 us (24%)
  between operations  0.87 us (1%)
    ppermute x21, starting transfers between devices, swap(): return lax.ppermute(x, axis, pairs)  28.3 us
    ppermute x21, waiting for transfers between devices, swap(): return lax.ppermute(x, axis, pairs)  20.8 us
    pallas_call x2, Pallas kernels, own_frames(): pl.pallas_call(functools.partial(frames_kernel, layouts, part, share), in...  12.5 us
    pallas_call x1, Pallas kernels, first_projection(): pl.pallas_call(functools.partial(first_projection_kernel, slots, with_gra...  3.73 us
    pallas_call x3, Pallas kernels, next_projection(): pl.pallas_call(functools.partial(next_projection_kernel, slots, first, co...  3.56 us
    pallas_call x4, Pallas kernels, project_frames(): pl.pallas_call(functools.partial(projected_kernel, items), in_specs=[SMEM...  3.49 us
    pallas_call x1, Pallas kernels, next_v(): pl.pallas_call(functools.partial(next_v_kernel, items, share), in_specs=[...  3.27 us
    pallas_call x1, Pallas kernels, next_w(): pl.pallas_call(functools.partial(next_w_kernel, len(sums)), out_shape=jax...  2.27 us
  transfers between devices with their start and end apart: 21, of which 13 were waited for; matrix products, arithmetic and copies ran while one was open for 0% of the time, Pallas kernels for 28%

profile of v14, /device:TPU:0, one launch (start us, length us, event | category | flops | bytes accessed | tf_op | source)
XLA Modules:
  0.0 86.8 jit_solution(2078856999944259674)
XLA Ops:
  0.7 3.7 %project_first.1 = s16[528,256]{1,0:T(8,128)(2,1)S(1)} custom-call(s32[1]{0:T(128)} %bitcast.place, bf16[64,1024]{1,0:T(8,128)(2,1)} %bitcast.13, bf16[4,8,256,1024]{3,2,1,0:T(8,128)(2,1)} %bitcast.4), custom_call_target="tpu_custom_call" | custom-call | flops 1000 | bytes 1000 | tf_op jit(solution)/shard_map/project_first/pallas_call | solution.py:158
  4.4 3.0 %collective-permute-start = (s16[528,256]{1,0:T(8,128)(2,1)S(1)}, s16[528,256]{1,0:T(8,128)(2,1)S(1)}, u32[]{:S(2)}, u32[]{:S(2)}) collective-permute-start(s16[528,256]{1,0:T(8,128)(2,1)S(1)} %project_first.1), channel_id=1, source_target_pairs={{0,1},{1,0},{2,3},{3,2},{4,5},{5,4},{6,7},{7,6},{8,9},{9,8},{10,11... | collective-permute-start | bytes 811016 | tf_op jit(solution)/shard_map/ppermute | solution.py:596
  7.8 1.6 %project_next.4 = s16[560,256]{1,0:T(8,128)(2,1)S(1)} custom-call(s32[1]{0:T(128)} %bitcast.place, bf16[64,1024]{1,0:T(8,128)(2,1)S(1)} %bitcast.14, bf16[4,8,256,1024]{3,2,1,0:T(8,128)(2,1)S(1)} %bitcast.5), custom_call_target="tpu_custom_call" | custom-call | flops 1000 | bytes 1000 | tf_op jit(solution)/shard_map/project_next/pallas_call | solution.py:196
  9.4 3.0 %collective-permute-start.3 = (s16[560,256]{1,0:T(8,128)(2,1)S(1)}, s16[560,256]{1,0:T(8,128)(2,1)S(1)}, u32[]{:S(2)}, u32[]{:S(2)}) collective-permute-start(s16[560,256]{1,0:T(8,128)(2,1)S(1)} %project_next.4), channel_id=1, source_target_pairs={{0,1},{1,0},{2,3},{3,2},{4,5},{5,4},{6,7},{7,6},{8,9},{9,8},{10,11... | collective-permute-start | bytes 860168 | tf_op jit(solution)/shard_map/ppermute | solution.py:596
  15.6 3.2 %collective-permute-start.2 = (s16[272,256]{1,0:T(8,128)(2,1)S(1)}, s16[272,256]{1,0:T(8,128)(2,1)S(1)}, u32[]{:S(2)}, u32[]{:S(2)}) collective-permute-start(s16[272,256]{1,0:T(8,128)(2,1)S(1)} %project_next.3), channel_id=1, source_target_pairs={{0,2},{1,3},{2,0},{3,1},{4,6},{5,7},{6,4},{7,5},{8,10},{9,11},{10,... | collective-permute-start | bytes 417800 | tf_op jit(solution)/shard_map/ppermute | solution.py:596
  18.8 1.5 %collective-permute-start.4 = (f32[64,64]{1,0:T(8,128)S(1)}, f32[64,64]{1,0:T(8,128)S(1)}, u32[]{:S(2)}, u32[]{:S(2)}) collective-permute-start(f32[64,64]{1,0:T(8,128)S(1)} %add_terms.5.refs_1_.refs_0_), channel_id=1, source_target_pairs={{0,8},{4,12},{8,0},{12,4},{1,9},{5,13},{9,1},{13,5},{2,10},{6,14},... | collective-permute-start | bytes 49160 | tf_op jit(solution)/shard_map/ppermute | solution.py:596
  24.9 6.2 %own_frames.2 = (bf16[4,64,256]{2,1,0:T(8,128)(2,1)S(1)}, f32[64,64]{1,0:T(8,128)S(1)}, f32[64,64]{1,0:T(8,128)S(1)}) custom-call(s32[1]{0:T(128)} %bitcast.place, s32[32]{0:T(128)S(1)} %copy-done.4, f32[64,64]{1,0:T(8,128)S(1)} %copy-done.3, f32[32,64]{1,0:T(8,128)S(1)} %copy-done.2, f32[64,64]{1,0:T(8,128)S(1)} %get-tuple-element.39.v_gram_ref.before_ref.refs_2_, ...), custom_call_target="tpu_custom_call" | custom-call | flops 1000 | bytes 1000 | tf_op jit(solution)/shard_map/own_frames/pallas_call | solution.py:377
  31.1 2.1 %collective-permute-start.7 = (bf16[4,64,256]{2,1,0:T(8,128)(2,1)S(1)}, bf16[4,64,256]{2,1,0:T(8,128)(2,1)S(1)}, u32[]{:S(2)}, u32[]{:S(2)}) collective-permute-start(bf16[4,64,256]{2,1,0:T(8,128)(2,1)S(1)} %get-tuple-element.45.refs_0_), channel_id=1, source_target_pairs={{0,2},{1,3},{2,0},{3,1},{4,6},{5,7},{6,4},{7,5},{8,10},{9,11},{10,... | collective-permute-start | bytes 393224 | tf_op jit(solution)/shard_map/ppermute | solution.py:596
  33.6 6.4 %own_frames.3 = (bf16[4,64,256]{2,1,0:T(8,128)(2,1)S(1)}, f32[64,64]{1,0:T(8,128)S(1)}, f32[64,64]{1,0:T(8,128)S(1)}) custom-call(s32[1]{0:T(128)} %bitcast.place, s32[32]{0:T(128)S(1)} %copy-done.4, f32[64,64]{1,0:T(8,128)S(1)} %copy-done.3, f32[32,64]{1,0:T(8,128)S(1)} %copy-done.2, f32[64,64]{1,0:T(8,128)S(1)} %get-tuple-element.41.v_gram_ref, ...), custom_call_target="tpu_custom_call" | custom-call | flops 1000 | bytes 1000 | tf_op jit(solution)/shard_map/own_frames/pallas_call | solution.py:377
  41.2 1.6 %collective-permute-start.13 = (bf16[4,64,256]{2,1,0:T(8,128)(2,1)S(1)}, bf16[4,64,256]{2,1,0:T(8,128)(2,1)S(1)}, u32[]{:S(2)}, u32[]{:S(2)}) collective-permute-start(bf16[4,64,256]{2,1,0:T(8,128)(2,1)S(1)} %get-tuple-element.46.refs_2_.refs_1_.refs_0_), channel_id=1, source_target_pairs={{0,2},{1,3},{2,0},{3,1},{4,6},{5,7},{6,4},{7,5},{8,10},{9,11},{10,... | collective-permute-start | bytes 393224 | tf_op jit(solution)/shard_map/ppermute | solution.py:596
  44.1 1.5 %collective-permute-start.8 = (f32[64,64]{1,0:T(8,128)S(1)}, f32[64,64]{1,0:T(8,128)S(1)}, u32[]{:S(2)}, u32[]{:S(2)}) collective-permute-start(f32[64,64]{1,0:T(8,128)S(1)} %add_terms.6.refs_2_.a_ref), channel_id=1, source_target_pairs={{0,8},{4,12},{8,0},{12,4},{1,9},{5,13},{9,1},{13,5},{2,10},{6,14},... | collective-permute-start | bytes 49160 | tf_op jit(solution)/shard_map/ppermute | solution.py:596
  45.6 5.4 %collective-permute-done.9.refs_1_ = bf16[8,64,256]{2,1,0:T(8,128)(2,1)S(1)} collective-permute-done((bf16[8,64,256]{2,1,0:T(8,128)(2,1)S(1)}, bf16[8,64,256]{2,1,0:T(8,128)(2,1)S(1)}, u32[]{:S(2)}, u32[]{:S(2)}) %collective-permute-start.9) | collective-permute-done | bytes 262176 | tf_op jit(solution)/shard_map/ppermute | solution.py:596
  52.4 2.0 %collective-permute-start.10 = (f32[64,64]{1,0:T(8,128)S(1)}, f32[64,64]{1,0:T(8,128)S(1)}, u32[]{:S(2)}, u32[]{:S(2)}) collective-permute-start(f32[64,64]{1,0:T(8,128)S(1)} %add_terms.7.refs_2_.refs_0_), channel_id=1, source_target_pairs={{0,1},{1,0},{2,3},{3,2},{4,5},{5,4},{6,7},{7,6},{8,9},{9,8},{10,11... | collective-permute-start | bytes 49160 | tf_op jit(solution)/shard_map/ppermute | solution.py:596
  54.4 2.4 %collective-permute-start.12 = (f32[64,64]{1,0:T(8,128)S(1)}, f32[64,64]{1,0:T(8,128)S(1)}, u32[]{:S(2)}, u32[]{:S(2)}) collective-permute-start(f32[64,64]{1,0:T(8,128)S(1)} %add_terms.7.refs_2_.refs_0_), channel_id=1, source_target_pairs={{0,3},{1,2},{2,1},{3,0},{4,7},{5,6},{6,5},{7,4},{8,11},{9,10},{10,... | collective-permute-start | bytes 49160 | tf_op jit(solution)/shard_map/ppermute | solution.py:596
  56.9 1.6 %first_inverse.1 = (f32[64,64]{1,0:T(8,128)S(1)}, f32[64,64]{1,0:T(8,128)S(1)}) custom-call(f32[64,64]{1,0:T(8,128)S(1)} %get-tuple-element.49.v_gram_ref, f32[64,64]{1,0:T(8,128)S(1)} %add_terms.5.refs_1_.refs_0_, f32[64,64]{1,0:T(8,128)S(1)} %collective-permute-done.4.refs_1_, bf16[8,64,256]{2,1,0:T(8,128)(2,1)S(1)} %join_frames.3.refs_2_), custom_call_target="tpu_custom_call" | custom-call | flops 1000 | bytes 1000 | tf_op jit(solution)/shard_map/first_inverse/pallas_call | solution.py:304
  58.9 2.5 %collective-permute-done.14.refs_0_ = bf16[8,64,256]{2,1,0:T(8,128)(2,1)S(1)} collective-permute-done((bf16[8,64,256]{2,1,0:T(8,128)(2,1)S(1)}, bf16[8,64,256]{2,1,0:T(8,128)(2,1)S(1)}, u32[]{:S(2)}, u32[]{:S(2)}) %collective-permute-start.14) | collective-permute-done | bytes 262176 | tf_op jit(solution)/shard_map/ppermute | solution.py:596
  63.3 1.6 %v_terms.1 = (f32[64,512]{1,0:T(8,128)S(1)}, f32[64,512]{1,0:T(8,128)S(1)}) custom-call(s32[1]{0:T(128)} %bitcast.place, bf16[4,192,512]{2,1,0:T(8,128)(2,1)S(1)} %get-tuple-element.54.factor_ref, bf16[256,1024]{1,0:T(8,128)(2,1)S(1)} %get-tuple-element.55.refs_0_, bf16[256,1024]{1,0:T(8,128)(2,1)S(1)} %get-tuple-element.56.refs_1_, ...), custom_call_target="tpu_custom_call" | custom-call | flops 1000 | bytes 1000 | tf_op jit(solution)/shard_map/v_terms/pallas_call | solution.py:522
  67.4 1.7 %second_inverse.1 = (f32[64,64]{1,0:T(8,128)S(1)}, f32[64,64]{1,0:T(8,128)S(1)}) custom-call(f32[64,64]{1,0:T(8,128)S(1)} %get-tuple-element.69.h_ref, f32[64,64]{1,0:T(8,128)S(1)} %get-tuple-element.70.w_gram_ref), custom_call_target="tpu_custom_call" | custom-call | flops 1000 | bytes 1000 | tf_op jit(solution)/shard_map/second_inverse/pallas_call | solution.py:490
  69.1 2.9 %collective-permute-done.16.b_ref = f32[64,512]{1,0:T(8,128)S(1)} collective-permute-done((f32[64,512]{1,0:T(8,128)S(1)}, f32[64,512]{1,0:T(8,128)S(1)}, u32[]{:S(2)}, u32[]{:S(2)}) %collective-permute-start.16) | collective-permute-done | bytes 131104 | tf_op jit(solution)/shard_map/ppermute | solution.py:596
  73.4 3.3 %next_v.1 = (f32[64,1024]{1,0:T(8,128)}, f32[64,128]{1,0:T(8,128)S(1)}) custom-call(s32[1]{0:T(128)} %bitcast.place, f32[64,512]{1,0:T(8,128)S(1)} %add_terms.9.own_ref, f32[64,512]{1,0:T(8,128)S(1)} %collective-permute-done.17.other_ref, f32[64,64]{1,0:T(8,128)S(1)} %get-tuple-element.71.refs_0_.inverse_ref, f32[64,64]{1,0:T(8,128)S(1)} %get-tuple-element.69.h_ref, ...), custom_call_target="tpu_custom_call" | custom-call | flops 1000 | bytes 1000 | tf_op jit(solution)/shard_map/next_v/pallas_call | solution.py:560
  76.7 2.1 %collective-permute-start.19 = (f32[64,128]{1,0:T(8,128)S(1)}, f32[64,128]{1,0:T(8,128)S(1)}, u32[]{:S(2)}, u32[]{:S(2)}) collective-permute-start(f32[64,128]{1,0:T(8,128)S(1)} %get-tuple-element.73.refs_0_), channel_id=1, source_target_pairs={{0,2},{1,3},{2,0},{3,1},{4,6},{5,7},{6,4},{7,5},{8,10},{9,11},{10,... | collective-permute-start | bytes 98312 | tf_op jit(solution)/shard_map/ppermute | solution.py:596
  78.8 2.3 %collective-permute-start.20 = (f32[64,128]{1,0:T(8,128)S(1)}, f32[64,128]{1,0:T(8,128)S(1)}, u32[]{:S(2)}, u32[]{:S(2)}) collective-permute-start(f32[64,128]{1,0:T(8,128)S(1)} %get-tuple-element.73.refs_0_), channel_id=1, source_target_pairs={{0,3},{1,2},{2,1},{3,0},{4,7},{5,6},{6,5},{7,4},{8,11},{9,10},{10,... | collective-permute-start | bytes 98312 | tf_op jit(solution)/shard_map/ppermute | solution.py:596
  81.5 3.0 %collective-permute-done.20.refs_3_ = f32[64,128]{1,0:T(8,128)S(1)} collective-permute-done((f32[64,128]{1,0:T(8,128)S(1)}, f32[64,128]{1,0:T(8,128)S(1)}, u32[]{:S(2)}, u32[]{:S(2)}) %collective-permute-start.20) | collective-permute-done | bytes 32800 | tf_op jit(solution)/shard_map/ppermute | solution.py:596
  84.5 2.3 %next_w.1 = f32[32,64]{1,0:T(8,128)} custom-call(f32[64,128]{1,0:T(8,128)S(1)} %get-tuple-element.73.refs_0_, f32[64,128]{1,0:T(8,128)S(1)} %collective-permute-done.18.refs_1_, f32[64,128]{1,0:T(8,128)S(1)} %collective-permute-done.19.refs_2_, f32[64,128]{1,0:T(8,128)S(1)} %collective-permute-done.20.refs_3_, f32[64,64]{1,0:T(8,128)S(1)} %get-tuple-element.74.refs_4_), custom_call_target="tpu_custom_call" | custom-call | flops 1000 | bytes 1000 | tf_op jit(solution)/shard_map/next_w/pallas_call | solution.py:585
  (53 shorter events, 18.9 us)
Async XLA Ops:
  0.7 11.8 %copy-start.2 = (f32[32,64]{1,0:T(8,128)S(1)}, f32[32,64]{1,0:T(8,128)}, u32[]{:S(2)}) copy-start(f32[32,64]{1,0:T(8,128)} %refs_5_.1) | copy-start | bytes 24580
  4.4 10.2 %collective-permute-start = (s16[528,256]{1,0:T(8,128)(2,1)S(1)}, s16[528,256]{1,0:T(8,128)(2,1)S(1)}, u32[]{:S(2)}, u32[]{:S(2)}) collective-permute-start(s16[528,256]{1,0:T(8,128)(2,1)S(1)} %project_first.1), channel_id=1, source_target_pairs={{0,1},{1,0},{2,3},{3,2},{4,5},{5,4},{6,7},{7,6},{8,9},{9,8},{10,11... | collective-permute-start | bytes 811016 | tf_op jit(solution)/shard_map/ppermute | solution.py:596
  9.4 13.6 %collective-permute-start.3 = (s16[560,256]{1,0:T(8,128)(2,1)S(1)}, s16[560,256]{1,0:T(8,128)(2,1)S(1)}, u32[]{:S(2)}, u32[]{:S(2)}) collective-permute-start(s16[560,256]{1,0:T(8,128)(2,1)S(1)} %project_next.4), channel_id=1, source_target_pairs={{0,1},{1,0},{2,3},{3,2},{4,5},{5,4},{6,7},{7,6},{8,9},{9,8},{10,11... | collective-permute-start | bytes 860168 | tf_op jit(solution)/shard_map/ppermute | solution.py:596
  12.7 1.3 %collective-permute-start.1 = (f32[64,64]{1,0:T(8,128)S(1)}, f32[64,64]{1,0:T(8,128)S(1)}, u32[]{:S(2)}, u32[]{:S(2)}) collective-permute-start(f32[64,64]{1,0:T(8,128)S(1)} %own_w_gram.1.a_ref), channel_id=1, source_target_pairs={{0,4},{4,0},{8,12},{12,8},{1,5},{5,1},{9,13},{13,9},{2,6},{6,2},{1... | collective-permute-start | bytes 49160 | tf_op jit(solution)/shard_map/ppermute | solution.py:596
  15.6 9.4 %copy-start.3 = (f32[64,64]{1,0:T(8,128)S(1)}, f32[64,64]{1,0:T(8,128)}, u32[]{:S(2)}) copy-start(f32[64,64]{1,0:T(8,128)} %h_ref.3) | copy-start | bytes 49156
  15.6 9.4 %copy-start.4 = (s32[32]{0:T(128)S(1)}, s32[32]{0:T(128)}, u32[]{:S(2)}) copy-start(s32[32]{0:T(128)} %counts_ref.3) | copy-start | bytes 388
  15.6 9.4 %collective-permute-start.2 = (s16[272,256]{1,0:T(8,128)(2,1)S(1)}, s16[272,256]{1,0:T(8,128)(2,1)S(1)}, u32[]{:S(2)}, u32[]{:S(2)}) collective-permute-start(s16[272,256]{1,0:T(8,128)(2,1)S(1)} %project_next.3), channel_id=1, source_target_pairs={{0,2},{1,3},{2,0},{3,1},{4,6},{5,7},{6,4},{7,5},{8,10},{9,11},{10,... | collective-permute-start | bytes 417800 | tf_op jit(solution)/shard_map/ppermute | solution.py:596
  18.8 3.9 %collective-permute-start.4 = (f32[64,64]{1,0:T(8,128)S(1)}, f32[64,64]{1,0:T(8,128)S(1)}, u32[]{:S(2)}, u32[]{:S(2)}) collective-permute-start(f32[64,64]{1,0:T(8,128)S(1)} %add_terms.5.refs_1_.refs_0_), channel_id=1, source_target_pairs={{0,8},{4,12},{8,0},{12,4},{1,9},{5,13},{9,1},{13,5},{2,10},{6,14},... | collective-permute-start | bytes 49160 | tf_op jit(solution)/shard_map/ppermute | solution.py:596
  24.0 9.6 %collective-permute-start.5 = (s16[304,256]{1,0:T(8,128)(2,1)S(1)}, s16[304,256]{1,0:T(8,128)(2,1)S(1)}, u32[]{:S(2)}, u32[]{:S(2)}) collective-permute-start(s16[304,256]{1,0:T(8,128)(2,1)S(1)} %project_next.5), channel_id=1, source_target_pairs={{0,2},{1,3},{2,0},{3,1},{4,6},{5,7},{6,4},{7,5},{8,10},{9,11},{10,... | collective-permute-start | bytes 466952 | tf_op jit(solution)/shard_map/ppermute | solution.py:596
  31.1 8.9 %collective-permute-start.7 = (bf16[4,64,256]{2,1,0:T(8,128)(2,1)S(1)}, bf16[4,64,256]{2,1,0:T(8,128)(2,1)S(1)}, u32[]{:S(2)}, u32[]{:S(2)}) collective-permute-start(bf16[4,64,256]{2,1,0:T(8,128)(2,1)S(1)} %get-tuple-element.45.refs_0_), channel_id=1, source_target_pairs={{0,2},{1,3},{2,0},{3,1},{4,6},{5,7},{6,4},{7,5},{8,10},{9,11},{10,... | collective-permute-start | bytes 393224 | tf_op jit(solution)/shard_map/ppermute | solution.py:596
  40.0 11.0 %collective-permute-start.9 = (bf16[8,64,256]{2,1,0:T(8,128)(2,1)S(1)}, bf16[8,64,256]{2,1,0:T(8,128)(2,1)S(1)}, u32[]{:S(2)}, u32[]{:S(2)}) collective-permute-start(bf16[8,64,256]{2,1,0:T(8,128)(2,1)S(1)} %join_frames.2.refs_2_), channel_id=1, source_target_pairs={{0,1},{1,0},{2,3},{3,2},{4,5},{5,4},{6,7},{7,6},{8,9},{9,8},{10,11... | collective-permute-start | bytes 786440 | tf_op jit(solution)/shard_map/ppermute | solution.py:596
  41.2 11.1 %collective-permute-start.13 = (bf16[4,64,256]{2,1,0:T(8,128)(2,1)S(1)}, bf16[4,64,256]{2,1,0:T(8,128)(2,1)S(1)}, u32[]{:S(2)}, u32[]{:S(2)}) collective-permute-start(bf16[4,64,256]{2,1,0:T(8,128)(2,1)S(1)} %get-tuple-element.46.refs_2_.refs_1_.refs_0_), channel_id=1, source_target_pairs={{0,2},{1,3},{2,0},{3,1},{4,6},{5,7},{6,4},{7,5},{8,10},{9,11},{10,... | collective-permute-start | bytes 393224 | tf_op jit(solution)/shard_map/ppermute | solution.py:596
  42.9 1.2 %collective-permute-start.6 = (f32[64,64]{1,0:T(8,128)S(1)}, f32[64,64]{1,0:T(8,128)S(1)}, u32[]{:S(2)}, u32[]{:S(2)}) collective-permute-start(f32[64,64]{1,0:T(8,128)S(1)} %get-tuple-element.44.a_ref), channel_id=1, source_target_pairs={{0,4},{4,0},{8,12},{12,8},{1,5},{5,1},{9,13},{13,9},{2,6},{6,2},{1... | collective-permute-start | bytes 49160 | tf_op jit(solution)/shard_map/ppermute | solution.py:596
  44.1 8.2 %collective-permute-start.8 = (f32[64,64]{1,0:T(8,128)S(1)}, f32[64,64]{1,0:T(8,128)S(1)}, u32[]{:S(2)}, u32[]{:S(2)}) collective-permute-start(f32[64,64]{1,0:T(8,128)S(1)} %add_terms.6.refs_2_.a_ref), channel_id=1, source_target_pairs={{0,8},{4,12},{8,0},{12,4},{1,9},{5,13},{9,1},{13,5},{2,10},{6,14},... | collective-permute-start | bytes 49160 | tf_op jit(solution)/shard_map/ppermute | solution.py:596
  52.3 9.1 %collective-permute-start.14 = (bf16[8,64,256]{2,1,0:T(8,128)(2,1)S(1)}, bf16[8,64,256]{2,1,0:T(8,128)(2,1)S(1)}, u32[]{:S(2)}, u32[]{:S(2)}) collective-permute-start(bf16[8,64,256]{2,1,0:T(8,128)(2,1)S(1)} %join_frames.3.refs_2_), channel_id=1, source_target_pairs={{0,1},{1,0},{2,3},{3,2},{4,5},{5,4},{6,7},{7,6},{8,9},{9,8},{10,11... | collective-permute-start | bytes 786440 | tf_op jit(solution)/shard_map/ppermute | solution.py:596
  52.4 9.9 %collective-permute-start.10 = (f32[64,64]{1,0:T(8,128)S(1)}, f32[64,64]{1,0:T(8,128)S(1)}, u32[]{:S(2)}, u32[]{:S(2)}) collective-permute-start(f32[64,64]{1,0:T(8,128)S(1)} %add_terms.7.refs_2_.refs_0_), channel_id=1, source_target_pairs={{0,1},{1,0},{2,3},{3,2},{4,5},{5,4},{6,7},{7,6},{8,9},{9,8},{10,11... | collective-permute-start | bytes 49160 | tf_op jit(solution)/shard_map/ppermute | solution.py:596
  54.4 7.9 %collective-permute-start.11 = (f32[64,64]{1,0:T(8,128)S(1)}, f32[64,64]{1,0:T(8,128)S(1)}, u32[]{:S(2)}, u32[]{:S(2)}) collective-permute-start(f32[64,64]{1,0:T(8,128)S(1)} %add_terms.7.refs_2_.refs_0_), channel_id=1, source_target_pairs={{0,2},{1,3},{2,0},{3,1},{4,6},{5,7},{6,4},{7,5},{8,10},{9,11},{10,... | collective-permute-start | bytes 49160 | tf_op jit(solution)/shard_map/ppermute | solution.py:596
  54.4 7.9 %collective-permute-start.12 = (f32[64,64]{1,0:T(8,128)S(1)}, f32[64,64]{1,0:T(8,128)S(1)}, u32[]{:S(2)}, u32[]{:S(2)}) collective-permute-start(f32[64,64]{1,0:T(8,128)S(1)} %add_terms.7.refs_2_.refs_0_), channel_id=1, source_target_pairs={{0,3},{1,2},{2,1},{3,0},{4,7},{5,6},{6,5},{7,4},{8,11},{9,10},{10,... | collective-permute-start | bytes 49160 | tf_op jit(solution)/shard_map/ppermute | solution.py:596
  65.0 1.4 %collective-permute-start.15 = (f32[64,512]{1,0:T(8,128)S(1)}, f32[64,512]{1,0:T(8,128)S(1)}, u32[]{:S(2)}, u32[]{:S(2)}) collective-permute-start(f32[64,512]{1,0:T(8,128)S(1)} %get-tuple-element.68), channel_id=1, source_target_pairs={{0,4},{4,0},{8,12},{12,8},{1,5},{5,1},{9,13},{13,9},{2,6},{6,2},{1... | collective-permute-start | bytes 393224 | tf_op jit(solution)/shard_map/ppermute | solution.py:596
  66.4 5.6 %collective-permute-start.16 = (f32[64,512]{1,0:T(8,128)S(1)}, f32[64,512]{1,0:T(8,128)S(1)}, u32[]{:S(2)}, u32[]{:S(2)}) collective-permute-start(f32[64,512]{1,0:T(8,128)S(1)} %add_terms.8.a_ref), channel_id=1, source_target_pairs={{0,8},{4,12},{8,0},{12,4},{1,9},{5,13},{9,1},{13,5},{2,10},{6,14},... | collective-permute-start | bytes 393224 | tf_op jit(solution)/shard_map/ppermute | solution.py:596
  72.0 1.4 %collective-permute-start.17 = (f32[64,512]{1,0:T(8,128)S(1)}, f32[64,512]{1,0:T(8,128)S(1)}, u32[]{:S(2)}, u32[]{:S(2)}) collective-permute-start(f32[64,512]{1,0:T(8,128)S(1)} %add_terms.9.own_ref), channel_id=1, source_target_pairs={{0,4},{4,0},{8,12},{12,8},{1,5},{5,1},{9,13},{13,9},{2,6},{6,2},{1... | collective-permute-start | bytes 393224 | tf_op jit(solution)/shard_map/ppermute | solution.py:596
  76.7 4.4 %collective-permute-start.18 = (f32[64,128]{1,0:T(8,128)S(1)}, f32[64,128]{1,0:T(8,128)S(1)}, u32[]{:S(2)}, u32[]{:S(2)}) collective-permute-start(f32[64,128]{1,0:T(8,128)S(1)} %get-tuple-element.73.refs_0_), channel_id=1, source_target_pairs={{0,1},{1,0},{2,3},{3,2},{4,5},{5,4},{6,7},{7,6},{8,9},{9,8},{10,11... | collective-permute-start | bytes 98312 | tf_op jit(solution)/shard_map/ppermute | solution.py:596
  76.7 4.8 %collective-permute-start.19 = (f32[64,128]{1,0:T(8,128)S(1)}, f32[64,128]{1,0:T(8,128)S(1)}, u32[]{:S(2)}, u32[]{:S(2)}) collective-permute-start(f32[64,128]{1,0:T(8,128)S(1)} %get-tuple-element.73.refs_0_), channel_id=1, source_target_pairs={{0,2},{1,3},{2,0},{3,1},{4,6},{5,7},{6,4},{7,5},{8,10},{9,11},{10,... | collective-permute-start | bytes 98312 | tf_op jit(solution)/shard_map/ppermute | solution.py:596
  78.8 5.7 %collective-permute-start.20 = (f32[64,128]{1,0:T(8,128)S(1)}, f32[64,128]{1,0:T(8,128)S(1)}, u32[]{:S(2)}, u32[]{:S(2)}) collective-permute-start(f32[64,128]{1,0:T(8,128)S(1)} %get-tuple-element.73.refs_0_), channel_id=1, source_target_pairs={{0,3},{1,2},{2,1},{3,0},{4,7},{5,6},{6,5},{7,4},{8,11},{9,10},{10,... | collective-permute-start | bytes 98312 | tf_op jit(solution)/shard_map/ppermute | solution.py:596
  (2 other events, 13.9 us)

commit v15 on v14

--- a/solution.py
+++ b/solution.py
@@ -496,39 +496,36 @@
     )(h_next, w_gram)
 
 
-def v_terms_kernel(items, place, factor_ref, *refs):
-    *parts, keep_ref, send_ref, terms_ref = refs
-    rank, width = terms_ref.shape
-    half = width // 2
+def v_terms_kernel(items, sent, place, factor_ref, *refs):
+    parts, terms_ref = refs[: 2 * len(items)], refs[-1]
+    rank, half = terms_ref.shape
+    upper = core_of(place) ^ 1 if sent else core_of(place)
+    features = pl.ds(pl.multiple_of(upper * half, half), half)
     total = None
     for i, (slots, first) in enumerate(items):
         count = parts[2 * i].shape[0] // len(slots)
         columns = pl.ds(first * rank, count)
         for k, slot in enumerate(slots):
             rows = pl.ds(k * count, count)
-            large = low_dot(factor_ref[slot, :, columns], parts[2 * i][rows, :])
-            small = low_dot(factor_ref[slot, : 2 * rank, columns], parts[2 * i + 1][rows, :])
+            large = low_dot(factor_ref[slot, :, columns], parts[2 * i][rows, features])
+            small = low_dot(factor_ref[slot, : 2 * rank, columns], parts[2 * i + 1][rows, features])
             terms = large[:rank] + (large[rank : 2 * rank] + small[:rank]) + (large[2 * rank :] + small[rank:])
             total = terms if total is None else total + terms
     terms_ref[...] = total
-    keep_ref[...] = terms_ref[:, pl.ds(pl.multiple_of(core_of(place) * half, half), half)]
-    send_ref[...] = terms_ref[:, pl.ds(pl.multiple_of((1 - core_of(place)) * half, half), half)]
-
-
-def all_v_terms(items, place, factor, projected):
+
+
+def half_v_terms(items, sent, place, factor, projected, after):
     width = projected[0].shape[1]
     rank = factor.shape[1] // 3
-    half = (rank, width // 2)
-    return pl.pallas_call(
-        functools.partial(v_terms_kernel, items),
-        in_specs=[SMEM_SPEC] + [VMEM_SPEC] * (1 + len(projected)),
-        out_specs=[VMEM_SPEC] * 2,
-        out_shape=[jax.ShapeDtypeStruct(half, F32)] * 2,
-        scratch_shapes=[pltpu.VMEM((rank, width), F32)],
+    return pl.pallas_call(
+        functools.partial(v_terms_kernel, items, sent),
+        in_specs=[SMEM_SPEC] + [VMEM_SPEC] * (1 + len(projected)) + [ANY_SPEC] * len(after),
+        out_specs=VMEM_SPEC,
+        out_shape=jax.ShapeDtypeStruct((rank, width // 2), F32),
         compiler_params=parameters(LIMIT),
         cost_estimate=SHORT,
         name="v_terms",
-    )(place, factor, *projected)
+    )(place, factor, *projected, *after)
 
 
 def next_v_kernel(items, share, place, own_ref, other_ref, inverse_ref, h_ref, *refs):
@@ -698,25 +695,26 @@
     last = len(bits)
     for part in range(n_parts - 1):
         joined = double(part, [frames[-1][0][1]])
-    projected, token = project_groups([(part, 0) for part in range(n_parts)], joined)
-    early = [(part, k) for part in range(n_parts - 1) for k in range(1, last + 1)]
+    first_groups = [(part, 0) for part in range(n_parts)] + [(part, 1) for part in range(n_parts - 1)]
+    early = [(part, k) for part in range(n_parts - 1) for k in range(2, last + 1)]
+    projected, token = project_groups(first_groups, joined)
     h_sums = staged_terms(h_local, "patient", [token])
-    more, token = project_groups(early, h_sums[:1])
-    projected |= more
-    h_sum = add(*h_sums, [token])
-    joined = double(n_parts - 1, [h_sum])
+    w_gram, inverse = first_inverse(v_gram, w_grams, h_sums[0])
+    h_sum = add(*h_sums, [inverse])
+    joined = double(n_parts - 1, [h_sum] + [frames[part][k][1] for part, k in early])
     h_terms = all_terms(h_sum, "feature")
-    w_gram, inverse = first_inverse(v_gram, w_grams, joined[0])
-    after = [inverse]
-    for k in range(1, last + 1):
-        more, token = project_groups([(n_parts - 1, k)], after)
-        projected |= more
-        after = [token]
+    after = joined
+    for groups in [early] + [[(n_parts - 1, k)] for k in range(1, last + 1)]:
+        if groups:
+            more, token = project_groups(groups, after)
+            projected |= more
+            after = [token]
     h_result, h_next, factor = next_h(place, h_terms, inverse, w_start, n, token)
 
     items = list(projected)
     flat = [x for item in items for x in projected[item]]
-    keep, send = all_v_terms(items, place, factor, flat)
+    send = half_v_terms(items, True, place, factor, flat, [])
+    keep = half_v_terms(items, False, place, factor, flat, [send])
     h_gram, second = second_inverse(h_next, w_gram)
     own_terms, other_terms = patient_halves(keep, send, second)
     v_next, sums = next_v(items, share, place, own_terms, other_terms, second, h_next, flat)

time: 86.9 us -> 84.9 us (0.977)
  waiting for transfers between devices: 20.8 us -> 18.6 us
    ppermute x21, waiting for transfers between devices: 20.8 us -> 18.6 us  [swap(): return lax.ppermute(x, axis, pairs)]
    pallas_call x1 -> x2, Pallas kernels: 1.62 us -> 1.77 us  [half_v_terms(): pl.pallas_call(functools.partial(v_terms_kernel, items, sent), in_specs=[...]
  transfers between devices with their start and end apart: 21 -> 21, of which waited for: 13 -> 14; matrix products, arithmetic and copies ran while one was open for 0% -> 0% of each run, Pallas kernels for 28% -> 30%
where the time goes in v15:
time: 84.9 us; the launch traced here: 84.7 us
  Pallas kernels  36.6 us (43%)
  starting transfers between devices  28.3 us (33%)
  waiting for transfers between devices  18.6 us (22%)
  between operations  0.86 us (1%)
    ppermute x21, starting transfers between devices, swap(): return lax.ppermute(x, axis, pairs)  28.3 us
    ppermute x21, waiting for transfers between devices, swap(): return lax.ppermute(x, axis, pairs)  18.6 us
    pallas_call x2, Pallas kernels, own_frames(): pl.pallas_call(functools.partial(frames_kernel, layouts, part, share), in...  12.5 us
    pallas_call x1, Pallas kernels, first_projection(): pl.pallas_call(functools.partial(first_projection_kernel, slots, with_gra...  3.73 us
    pallas_call x3, Pallas kernels, next_projection(): pl.pallas_call(functools.partial(next_projection_kernel, slots, first, co...  3.56 us
    pallas_call x4, Pallas kernels, project_frames(): pl.pallas_call(functools.partial(projected_kernel, items), in_specs=[SMEM...  3.5 us
    pallas_call x1, Pallas kernels, next_v(): pl.pallas_call(functools.partial(next_v_kernel, items, share), in_specs=[...  3.28 us
    pallas_call x1, Pallas kernels, next_w(): pl.pallas_call(functools.partial(next_w_kernel, len(sums)), out_shape=jax...  2.27 us
  transfers between devices with their start and end apart: 21, of which 14 were waited for; matrix products, arithmetic and copies ran while one was open for 0% of the time, Pallas kernels for 30%

profile of v15, /device:TPU:0, one launch (start us, length us, event | category | flops | bytes accessed | tf_op | source)
XLA Modules:
  0.0 84.7 jit_solution(13806063522044970630)
XLA Ops:
  0.7 3.7 %project_first.1 = s16[528,256]{1,0:T(8,128)(2,1)S(1)} custom-call(s32[1]{0:T(128)} %bitcast.place, bf16[64,1024]{1,0:T(8,128)(2,1)} %bitcast.13, bf16[4,8,256,1024]{3,2,1,0:T(8,128)(2,1)} %bitcast.4), custom_call_target="tpu_custom_call" | custom-call | flops 1000 | bytes 1000 | tf_op jit(solution)/shard_map/project_first/pallas_call | solution.py:158
  4.4 3.0 %collective-permute-start = (s16[528,256]{1,0:T(8,128)(2,1)S(1)}, s16[528,256]{1,0:T(8,128)(2,1)S(1)}, u32[]{:S(2)}, u32[]{:S(2)}) collective-permute-start(s16[528,256]{1,0:T(8,128)(2,1)S(1)} %project_first.1), channel_id=1, source_target_pairs={{0,1},{1,0},{2,3},{3,2},{4,5},{5,4},{6,7},{7,6},{8,9},{9,8},{10,11... | collective-permute-start | bytes 811016 | tf_op jit(solution)/shard_map/ppermute | solution.py:593
  7.8 1.6 %project_next.4 = s16[560,256]{1,0:T(8,128)(2,1)S(1)} custom-call(s32[1]{0:T(128)} %bitcast.place, bf16[64,1024]{1,0:T(8,128)(2,1)S(1)} %bitcast.14, bf16[4,8,256,1024]{3,2,1,0:T(8,128)(2,1)S(1)} %bitcast.5), custom_call_target="tpu_custom_call" | custom-call | flops 1000 | bytes 1000 | tf_op jit(solution)/shard_map/project_next/pallas_call | solution.py:196
  9.4 3.0 %collective-permute-start.3 = (s16[560,256]{1,0:T(8,128)(2,1)S(1)}, s16[560,256]{1,0:T(8,128)(2,1)S(1)}, u32[]{:S(2)}, u32[]{:S(2)}) collective-permute-start(s16[560,256]{1,0:T(8,128)(2,1)S(1)} %project_next.4), channel_id=1, source_target_pairs={{0,1},{1,0},{2,3},{3,2},{4,5},{5,4},{6,7},{7,6},{8,9},{9,8},{10,11... | collective-permute-start | bytes 860168 | tf_op jit(solution)/shard_map/ppermute | solution.py:593
  15.6 3.2 %collective-permute-start.2 = (s16[272,256]{1,0:T(8,128)(2,1)S(1)}, s16[272,256]{1,0:T(8,128)(2,1)S(1)}, u32[]{:S(2)}, u32[]{:S(2)}) collective-permute-start(s16[272,256]{1,0:T(8,128)(2,1)S(1)} %project_next.3), channel_id=1, source_target_pairs={{0,2},{1,3},{2,0},{3,1},{4,6},{5,7},{6,4},{7,5},{8,10},{9,11},{10,... | collective-permute-start | bytes 417800 | tf_op jit(solution)/shard_map/ppermute | solution.py:593
  18.8 1.5 %collective-permute-start.4 = (f32[64,64]{1,0:T(8,128)S(1)}, f32[64,64]{1,0:T(8,128)S(1)}, u32[]{:S(2)}, u32[]{:S(2)}) collective-permute-start(f32[64,64]{1,0:T(8,128)S(1)} %add_terms.5.refs_1_.refs_0_), channel_id=1, source_target_pairs={{0,8},{4,12},{8,0},{12,4},{1,9},{5,13},{9,1},{13,5},{2,10},{6,14},... | collective-permute-start | bytes 49160 | tf_op jit(solution)/shard_map/ppermute | solution.py:593
  20.2 1.4 %project_own.1 = (f32[4,64,256]{2,1,0:T(8,128)S(1)}, f32[4,64,256]{2,1,0:T(8,128)S(1)}, f32[64,64]{1,0:T(8,128)S(1)}) custom-call(s32[1]{0:T(128)} %bitcast.place, bf16[64,1024]{1,0:T(8,128)(2,1)S(1)} %bitcast.16, bf16[4,8,256,1024]{3,2,1,0:T(8,128)(2,1)S(1)} %bitcast.7), custom_call_target="tpu_custom_call" | custom-call | flops 1000 | bytes 1000 | tf_op jit(solution)/shard_map/project_own/pallas_call | solution.py:236
  24.9 6.2 %own_frames.2 = (bf16[4,64,256]{2,1,0:T(8,128)(2,1)S(1)}, f32[64,64]{1,0:T(8,128)S(1)}, f32[64,64]{1,0:T(8,128)S(1)}) custom-call(s32[1]{0:T(128)} %bitcast.place, s32[32]{0:T(128)S(1)} %copy-done.4, f32[64,64]{1,0:T(8,128)S(1)} %copy-done.3, f32[32,64]{1,0:T(8,128)S(1)} %copy-done.2, f32[64,64]{1,0:T(8,128)S(1)} %get-tuple-element.37.v_gram_ref.before_ref.refs_2_, ...), custom_call_target="tpu_custom_call" | custom-call | flops 1000 | bytes 1000 | tf_op jit(solution)/shard_map/own_frames/pallas_call | solution.py:377
  31.1 2.1 %collective-permute-start.7 = (bf16[4,64,256]{2,1,0:T(8,128)(2,1)S(1)}, bf16[4,64,256]{2,1,0:T(8,128)(2,1)S(1)}, u32[]{:S(2)}, u32[]{:S(2)}) collective-permute-start(bf16[4,64,256]{2,1,0:T(8,128)(2,1)S(1)} %get-tuple-element.43.refs_0_), channel_id=1, source_target_pairs={{0,2},{1,3},{2,0},{3,1},{4,6},{5,7},{6,4},{7,5},{8,10},{9,11},{10,... | collective-permute-start | bytes 393224 | tf_op jit(solution)/shard_map/ppermute | solution.py:593
  33.6 6.4 %own_frames.3 = (bf16[4,64,256]{2,1,0:T(8,128)(2,1)S(1)}, f32[64,64]{1,0:T(8,128)S(1)}, f32[64,64]{1,0:T(8,128)S(1)}) custom-call(s32[1]{0:T(128)} %bitcast.place, s32[32]{0:T(128)S(1)} %copy-done.4, f32[64,64]{1,0:T(8,128)S(1)} %copy-done.3, f32[32,64]{1,0:T(8,128)S(1)} %copy-done.2, f32[64,64]{1,0:T(8,128)S(1)} %get-tuple-element.39.v_gram_ref, ...), custom_call_target="tpu_custom_call" | custom-call | flops 1000 | bytes 1000 | tf_op jit(solution)/shard_map/own_frames/pallas_call | solution.py:377
  41.2 1.6 %collective-permute-start.12 = (bf16[4,64,256]{2,1,0:T(8,128)(2,1)S(1)}, bf16[4,64,256]{2,1,0:T(8,128)(2,1)S(1)}, u32[]{:S(2)}, u32[]{:S(2)}) collective-permute-start(bf16[4,64,256]{2,1,0:T(8,128)(2,1)S(1)} %get-tuple-element.44.refs_2_.refs_1_.refs_0_), channel_id=1, source_target_pairs={{0,2},{1,3},{2,0},{3,1},{4,6},{5,7},{6,4},{7,5},{8,10},{9,11},{10,... | collective-permute-start | bytes 393224 | tf_op jit(solution)/shard_map/ppermute | solution.py:593
  44.2 1.6 %collective-permute-start.8 = (f32[64,64]{1,0:T(8,128)S(1)}, f32[64,64]{1,0:T(8,128)S(1)}, u32[]{:S(2)}, u32[]{:S(2)}) collective-permute-start(f32[64,64]{1,0:T(8,128)S(1)} %add_terms.6.refs_2_.a_ref), channel_id=1, source_target_pairs={{0,8},{4,12},{8,0},{12,4},{1,9},{5,13},{9,1},{13,5},{2,10},{6,14},... | collective-permute-start | bytes 49160 | tf_op jit(solution)/shard_map/ppermute | solution.py:593
  45.7 1.6 %first_inverse.1 = (f32[64,64]{1,0:T(8,128)S(1)}, f32[64,64]{1,0:T(8,128)S(1)}) custom-call(f32[64,64]{1,0:T(8,128)S(1)} %get-tuple-element.46.v_gram_ref, f32[64,64]{1,0:T(8,128)S(1)} %add_terms.5.refs_1_.refs_0_, f32[64,64]{1,0:T(8,128)S(1)} %collective-permute-done.4.refs_1_, f32[64,64]{1,0:T(8,128)S(1)} %add_terms.6.refs_2_.a_ref), custom_call_target="tpu_custom_call" | custom-call | flops 1000 | bytes 1000 | tf_op jit(solution)/shard_map/first_inverse/pallas_call | solution.py:304
  48.8 2.2 %collective-permute-done.13.refs_3_.refs_0_ = bf16[8,64,256]{2,1,0:T(8,128)(2,1)S(1)} collective-permute-done((bf16[8,64,256]{2,1,0:T(8,128)(2,1)S(1)}, bf16[8,64,256]{2,1,0:T(8,128)(2,1)S(1)}, u32[]{:S(2)}, u32[]{:S(2)}) %collective-permute-start.13) | collective-permute-done | bytes 262176 | tf_op jit(solution)/shard_map/ppermute | solution.py:593
  51.1 2.0 %collective-permute-start.9 = (f32[64,64]{1,0:T(8,128)S(1)}, f32[64,64]{1,0:T(8,128)S(1)}, u32[]{:S(2)}, u32[]{:S(2)}) collective-permute-start(f32[64,64]{1,0:T(8,128)S(1)} %add_terms.7.refs_2_.refs_0_), channel_id=1, source_target_pairs={{0,1},{1,0},{2,3},{3,2},{4,5},{5,4},{6,7},{7,6},{8,9},{9,8},{10,11... | collective-permute-start | bytes 49160 | tf_op jit(solution)/shard_map/ppermute | solution.py:593
  57.0 3.2 %collective-permute-done.14.refs_0_ = bf16[8,64,256]{2,1,0:T(8,128)(2,1)S(1)} collective-permute-done((bf16[8,64,256]{2,1,0:T(8,128)(2,1)S(1)}, bf16[8,64,256]{2,1,0:T(8,128)(2,1)S(1)}, u32[]{:S(2)}, u32[]{:S(2)}) %collective-permute-start.14) | collective-permute-done | bytes 262176 | tf_op jit(solution)/shard_map/ppermute | solution.py:593
  65.3 1.7 %second_inverse.1 = (f32[64,64]{1,0:T(8,128)S(1)}, f32[64,64]{1,0:T(8,128)S(1)}) custom-call(f32[64,64]{1,0:T(8,128)S(1)} %get-tuple-element.65.h_ref, f32[64,64]{1,0:T(8,128)S(1)} %get-tuple-element.66.w_gram_ref), custom_call_target="tpu_custom_call" | custom-call | flops 1000 | bytes 1000 | tf_op jit(solution)/shard_map/second_inverse/pallas_call | solution.py:490
  67.0 2.9 %collective-permute-done.16.b_ref = f32[64,512]{1,0:T(8,128)S(1)} collective-permute-done((f32[64,512]{1,0:T(8,128)S(1)}, f32[64,512]{1,0:T(8,128)S(1)}, u32[]{:S(2)}, u32[]{:S(2)}) %collective-permute-start.16) | collective-permute-done | bytes 131104 | tf_op jit(solution)/shard_map/ppermute | solution.py:593
  70.0 1.3 %collective-permute-done.17.other_ref = f32[64,512]{1,0:T(8,128)S(1)} collective-permute-done((f32[64,512]{1,0:T(8,128)S(1)}, f32[64,512]{1,0:T(8,128)S(1)}, u32[]{:S(2)}, u32[]{:S(2)}) %collective-permute-start.17) | collective-permute-done | bytes 131104 | tf_op jit(solution)/shard_map/ppermute | solution.py:593
  71.4 3.3 %next_v.1 = (f32[64,1024]{1,0:T(8,128)}, f32[64,128]{1,0:T(8,128)S(1)}) custom-call(s32[1]{0:T(128)} %bitcast.place, f32[64,512]{1,0:T(8,128)S(1)} %add_terms.9.own_ref, f32[64,512]{1,0:T(8,128)S(1)} %collective-permute-done.17.other_ref, f32[64,64]{1,0:T(8,128)S(1)} %get-tuple-element.67.refs_0_.inverse_ref, f32[64,64]{1,0:T(8,128)S(1)} %get-tuple-element.65.h_ref, ...), custom_call_target="tpu_custom_call" | custom-call | flops 1000 | bytes 1000 | tf_op jit(solution)/shard_map/next_v/pallas_call | solution.py:557
  74.7 2.1 %collective-permute-start.19 = (f32[64,128]{1,0:T(8,128)S(1)}, f32[64,128]{1,0:T(8,128)S(1)}, u32[]{:S(2)}, u32[]{:S(2)}) collective-permute-start(f32[64,128]{1,0:T(8,128)S(1)} %get-tuple-element.69.refs_0_), channel_id=1, source_target_pairs={{0,2},{1,3},{2,0},{3,1},{4,6},{5,7},{6,4},{7,5},{8,10},{9,11},{10,... | collective-permute-start | bytes 98312 | tf_op jit(solution)/shard_map/ppermute | solution.py:593
  76.8 2.3 %collective-permute-start.20 = (f32[64,128]{1,0:T(8,128)S(1)}, f32[64,128]{1,0:T(8,128)S(1)}, u32[]{:S(2)}, u32[]{:S(2)}) collective-permute-start(f32[64,128]{1,0:T(8,128)S(1)} %get-tuple-element.69.refs_0_), channel_id=1, source_target_pairs={{0,3},{1,2},{2,1},{3,0},{4,7},{5,6},{6,5},{7,4},{8,11},{9,10},{10,... | collective-permute-start | bytes 98312 | tf_op jit(solution)/shard_map/ppermute | solution.py:593
  79.5 3.0 %collective-permute-done.20.refs_3_ = f32[64,128]{1,0:T(8,128)S(1)} collective-permute-done((f32[64,128]{1,0:T(8,128)S(1)}, f32[64,128]{1,0:T(8,128)S(1)}, u32[]{:S(2)}, u32[]{:S(2)}) %collective-permute-start.20) | collective-permute-done | bytes 32800 | tf_op jit(solution)/shard_map/ppermute | solution.py:593
  82.5 2.3 %next_w.1 = f32[32,64]{1,0:T(8,128)} custom-call(f32[64,128]{1,0:T(8,128)S(1)} %get-tuple-element.69.refs_0_, f32[64,128]{1,0:T(8,128)S(1)} %collective-permute-done.18.refs_1_, f32[64,128]{1,0:T(8,128)S(1)} %collective-permute-done.19.refs_2_, f32[64,128]{1,0:T(8,128)S(1)} %collective-permute-done.20.refs_3_, f32[64,64]{1,0:T(8,128)S(1)} %get-tuple-element.70.refs_4_), custom_call_target="tpu_custom_call" | custom-call | flops 1000 | bytes 1000 | tf_op jit(solution)/shard_map/next_w/pallas_call | solution.py:582
  (54 shorter events, 20.7 us)
Async XLA Ops:
  0.7 11.8 %copy-start.2 = (f32[32,64]{1,0:T(8,128)S(1)}, f32[32,64]{1,0:T(8,128)}, u32[]{:S(2)}) copy-start(f32[32,64]{1,0:T(8,128)} %refs_5_.1) | copy-start | bytes 24580
  4.4 10.2 %collective-permute-start = (s16[528,256]{1,0:T(8,128)(2,1)S(1)}, s16[528,256]{1,0:T(8,128)(2,1)S(1)}, u32[]{:S(2)}, u32[]{:S(2)}) collective-permute-start(s16[528,256]{1,0:T(8,128)(2,1)S(1)} %project_first.1), channel_id=1, source_target_pairs={{0,1},{1,0},{2,3},{3,2},{4,5},{5,4},{6,7},{7,6},{8,9},{9,8},{10,11... | collective-permute-start | bytes 811016 | tf_op jit(solution)/shard_map/ppermute | solution.py:593
  9.4 13.6 %collective-permute-start.3 = (s16[560,256]{1,0:T(8,128)(2,1)S(1)}, s16[560,256]{1,0:T(8,128)(2,1)S(1)}, u32[]{:S(2)}, u32[]{:S(2)}) collective-permute-start(s16[560,256]{1,0:T(8,128)(2,1)S(1)} %project_next.4), channel_id=1, source_target_pairs={{0,1},{1,0},{2,3},{3,2},{4,5},{5,4},{6,7},{7,6},{8,9},{9,8},{10,11... | collective-permute-start | bytes 860168 | tf_op jit(solution)/shard_map/ppermute | solution.py:593
  12.7 1.3 %collective-permute-start.1 = (f32[64,64]{1,0:T(8,128)S(1)}, f32[64,64]{1,0:T(8,128)S(1)}, u32[]{:S(2)}, u32[]{:S(2)}) collective-permute-start(f32[64,64]{1,0:T(8,128)S(1)} %own_w_gram.1.a_ref), channel_id=1, source_target_pairs={{0,4},{4,0},{8,12},{12,8},{1,5},{5,1},{9,13},{13,9},{2,6},{6,2},{1... | collective-permute-start | bytes 49160 | tf_op jit(solution)/shard_map/ppermute | solution.py:593
  15.6 9.4 %copy-start.3 = (f32[64,64]{1,0:T(8,128)S(1)}, f32[64,64]{1,0:T(8,128)}, u32[]{:S(2)}) copy-start(f32[64,64]{1,0:T(8,128)} %h_ref.3) | copy-start | bytes 49156
  15.6 9.4 %copy-start.4 = (s32[32]{0:T(128)S(1)}, s32[32]{0:T(128)}, u32[]{:S(2)}) copy-start(s32[32]{0:T(128)} %counts_ref.3) | copy-start | bytes 388
  15.6 9.4 %collective-permute-start.2 = (s16[272,256]{1,0:T(8,128)(2,1)S(1)}, s16[272,256]{1,0:T(8,128)(2,1)S(1)}, u32[]{:S(2)}, u32[]{:S(2)}) collective-permute-start(s16[272,256]{1,0:T(8,128)(2,1)S(1)} %project_next.3), channel_id=1, source_target_pairs={{0,2},{1,3},{2,0},{3,1},{4,6},{5,7},{6,4},{7,5},{8,10},{9,11},{10,... | collective-permute-start | bytes 417800 | tf_op jit(solution)/shard_map/ppermute | solution.py:593
  18.8 3.9 %collective-permute-start.4 = (f32[64,64]{1,0:T(8,128)S(1)}, f32[64,64]{1,0:T(8,128)S(1)}, u32[]{:S(2)}, u32[]{:S(2)}) collective-permute-start(f32[64,64]{1,0:T(8,128)S(1)} %add_terms.5.refs_1_.refs_0_), channel_id=1, source_target_pairs={{0,8},{4,12},{8,0},{12,4},{1,9},{5,13},{9,1},{13,5},{2,10},{6,14},... | collective-permute-start | bytes 49160 | tf_op jit(solution)/shard_map/ppermute | solution.py:593
  24.0 9.6 %collective-permute-start.5 = (s16[304,256]{1,0:T(8,128)(2,1)S(1)}, s16[304,256]{1,0:T(8,128)(2,1)S(1)}, u32[]{:S(2)}, u32[]{:S(2)}) collective-permute-start(s16[304,256]{1,0:T(8,128)(2,1)S(1)} %project_next.5), channel_id=1, source_target_pairs={{0,2},{1,3},{2,0},{3,1},{4,6},{5,7},{6,4},{7,5},{8,10},{9,11},{10,... | collective-permute-start | bytes 466952 | tf_op jit(solution)/shard_map/ppermute | solution.py:593
  31.1 8.9 %collective-permute-start.7 = (bf16[4,64,256]{2,1,0:T(8,128)(2,1)S(1)}, bf16[4,64,256]{2,1,0:T(8,128)(2,1)S(1)}, u32[]{:S(2)}, u32[]{:S(2)}) collective-permute-start(bf16[4,64,256]{2,1,0:T(8,128)(2,1)S(1)} %get-tuple-element.43.refs_0_), channel_id=1, source_target_pairs={{0,2},{1,3},{2,0},{3,1},{4,6},{5,7},{6,4},{7,5},{8,10},{9,11},{10,... | collective-permute-start | bytes 393224 | tf_op jit(solution)/shard_map/ppermute | solution.py:593
  40.0 11.0 %collective-permute-start.13 = (bf16[8,64,256]{2,1,0:T(8,128)(2,1)S(1)}, bf16[8,64,256]{2,1,0:T(8,128)(2,1)S(1)}, u32[]{:S(2)}, u32[]{:S(2)}) collective-permute-start(bf16[8,64,256]{2,1,0:T(8,128)(2,1)S(1)} %join_frames.2.refs_3_), channel_id=1, source_target_pairs={{0,1},{1,0},{2,3},{3,2},{4,5},{5,4},{6,7},{7,6},{8,9},{9,8},{10,11... | collective-permute-start | bytes 786440 | tf_op jit(solution)/shard_map/ppermute | solution.py:593
  41.2 7.6 %collective-permute-start.12 = (bf16[4,64,256]{2,1,0:T(8,128)(2,1)S(1)}, bf16[4,64,256]{2,1,0:T(8,128)(2,1)S(1)}, u32[]{:S(2)}, u32[]{:S(2)}) collective-permute-start(bf16[4,64,256]{2,1,0:T(8,128)(2,1)S(1)} %get-tuple-element.44.refs_2_.refs_1_.refs_0_), channel_id=1, source_target_pairs={{0,2},{1,3},{2,0},{3,1},{4,6},{5,7},{6,4},{7,5},{8,10},{9,11},{10,... | collective-permute-start | bytes 393224 | tf_op jit(solution)/shard_map/ppermute | solution.py:593
  42.9 1.3 %collective-permute-start.6 = (f32[64,64]{1,0:T(8,128)S(1)}, f32[64,64]{1,0:T(8,128)S(1)}, u32[]{:S(2)}, u32[]{:S(2)}) collective-permute-start(f32[64,64]{1,0:T(8,128)S(1)} %get-tuple-element.42.a_ref), channel_id=1, source_target_pairs={{0,4},{4,0},{8,12},{12,8},{1,5},{5,1},{9,13},{13,9},{2,6},{6,2},{1... | collective-permute-start | bytes 49160 | tf_op jit(solution)/shard_map/ppermute | solution.py:593
  44.2 4.0 %collective-permute-start.8 = (f32[64,64]{1,0:T(8,128)S(1)}, f32[64,64]{1,0:T(8,128)S(1)}, u32[]{:S(2)}, u32[]{:S(2)}) collective-permute-start(f32[64,64]{1,0:T(8,128)S(1)} %add_terms.6.refs_2_.a_ref), channel_id=1, source_target_pairs={{0,8},{4,12},{8,0},{12,4},{1,9},{5,13},{9,1},{13,5},{2,10},{6,14},... | collective-permute-start | bytes 49160 | tf_op jit(solution)/shard_map/ppermute | solution.py:593
  51.0 9.1 %collective-permute-start.14 = (bf16[8,64,256]{2,1,0:T(8,128)(2,1)S(1)}, bf16[8,64,256]{2,1,0:T(8,128)(2,1)S(1)}, u32[]{:S(2)}, u32[]{:S(2)}) collective-permute-start(bf16[8,64,256]{2,1,0:T(8,128)(2,1)S(1)} %join_frames.3.refs_1_), channel_id=1, source_target_pairs={{0,1},{1,0},{2,3},{3,2},{4,5},{5,4},{6,7},{7,6},{8,9},{9,8},{10,11... | collective-permute-start | bytes 786440 | tf_op jit(solution)/shard_map/ppermute | solution.py:593
  51.1 9.9 %collective-permute-start.9 = (f32[64,64]{1,0:T(8,128)S(1)}, f32[64,64]{1,0:T(8,128)S(1)}, u32[]{:S(2)}, u32[]{:S(2)}) collective-permute-start(f32[64,64]{1,0:T(8,128)S(1)} %add_terms.7.refs_2_.refs_0_), channel_id=1, source_target_pairs={{0,1},{1,0},{2,3},{3,2},{4,5},{5,4},{6,7},{7,6},{8,9},{9,8},{10,11... | collective-permute-start | bytes 49160 | tf_op jit(solution)/shard_map/ppermute | solution.py:593
  53.1 7.9 %collective-permute-start.10 = (f32[64,64]{1,0:T(8,128)S(1)}, f32[64,64]{1,0:T(8,128)S(1)}, u32[]{:S(2)}, u32[]{:S(2)}) collective-permute-start(f32[64,64]{1,0:T(8,128)S(1)} %add_terms.7.refs_2_.refs_0_), channel_id=1, source_target_pairs={{0,2},{1,3},{2,0},{3,1},{4,6},{5,7},{6,4},{7,5},{8,10},{9,11},{10,... | collective-permute-start | bytes 49160 | tf_op jit(solution)/shard_map/ppermute | solution.py:593
  54.3 6.7 %collective-permute-start.11 = (f32[64,64]{1,0:T(8,128)S(1)}, f32[64,64]{1,0:T(8,128)S(1)}, u32[]{:S(2)}, u32[]{:S(2)}) collective-permute-start(f32[64,64]{1,0:T(8,128)S(1)} %add_terms.7.refs_2_.refs_0_), channel_id=1, source_target_pairs={{0,3},{1,2},{2,1},{3,0},{4,7},{5,6},{6,5},{7,4},{8,11},{9,10},{10,... | collective-permute-start | bytes 49160 | tf_op jit(solution)/shard_map/ppermute | solution.py:593
  62.9 1.4 %collective-permute-start.15 = (f32[64,512]{1,0:T(8,128)S(1)}, f32[64,512]{1,0:T(8,128)S(1)}, u32[]{:S(2)}, u32[]{:S(2)}) collective-permute-start(f32[64,512]{1,0:T(8,128)S(1)} %v_terms.2.refs_12_), channel_id=1, source_target_pairs={{0,4},{4,0},{8,12},{12,8},{1,5},{5,1},{9,13},{13,9},{2,6},{6,2},{1... | collective-permute-start | bytes 393224 | tf_op jit(solution)/shard_map/ppermute | solution.py:593
  64.3 5.6 %collective-permute-start.16 = (f32[64,512]{1,0:T(8,128)S(1)}, f32[64,512]{1,0:T(8,128)S(1)}, u32[]{:S(2)}, u32[]{:S(2)}) collective-permute-start(f32[64,512]{1,0:T(8,128)S(1)} %add_terms.8.a_ref), channel_id=1, source_target_pairs={{0,8},{4,12},{8,0},{12,4},{1,9},{5,13},{9,1},{13,5},{2,10},{6,14},... | collective-permute-start | bytes 393224 | tf_op jit(solution)/shard_map/ppermute | solution.py:593
  70.0 1.4 %collective-permute-start.17 = (f32[64,512]{1,0:T(8,128)S(1)}, f32[64,512]{1,0:T(8,128)S(1)}, u32[]{:S(2)}, u32[]{:S(2)}) collective-permute-start(f32[64,512]{1,0:T(8,128)S(1)} %add_terms.9.own_ref), channel_id=1, source_target_pairs={{0,4},{4,0},{8,12},{12,8},{1,5},{5,1},{9,13},{13,9},{2,6},{6,2},{1... | collective-permute-start | bytes 393224 | tf_op jit(solution)/shard_map/ppermute | solution.py:593
  74.7 4.4 %collective-permute-start.18 = (f32[64,128]{1,0:T(8,128)S(1)}, f32[64,128]{1,0:T(8,128)S(1)}, u32[]{:S(2)}, u32[]{:S(2)}) collective-permute-start(f32[64,128]{1,0:T(8,128)S(1)} %get-tuple-element.69.refs_0_), channel_id=1, source_target_pairs={{0,1},{1,0},{2,3},{3,2},{4,5},{5,4},{6,7},{7,6},{8,9},{9,8},{10,11... | collective-permute-start | bytes 98312 | tf_op jit(solution)/shard_map/ppermute | solution.py:593
  74.7 4.8 %collective-permute-start.19 = (f32[64,128]{1,0:T(8,128)S(1)}, f32[64,128]{1,0:T(8,128)S(1)}, u32[]{:S(2)}, u32[]{:S(2)}) collective-permute-start(f32[64,128]{1,0:T(8,128)S(1)} %get-tuple-element.69.refs_0_), channel_id=1, source_target_pairs={{0,2},{1,3},{2,0},{3,1},{4,6},{5,7},{6,4},{7,5},{8,10},{9,11},{10,... | collective-permute-start | bytes 98312 | tf_op jit(solution)/shard_map/ppermute | solution.py:593
  76.8 5.7 %collective-permute-start.20 = (f32[64,128]{1,0:T(8,128)S(1)}, f32[64,128]{1,0:T(8,128)S(1)}, u32[]{:S(2)}, u32[]{:S(2)}) collective-permute-start(f32[64,128]{1,0:T(8,128)S(1)} %get-tuple-element.69.refs_0_), channel_id=1, source_target_pairs={{0,3},{1,2},{2,1},{3,0},{4,7},{5,6},{6,5},{7,4},{8,11},{9,10},{10,... | collective-permute-start | bytes 98312 | tf_op jit(solution)/shard_map/ppermute | solution.py:593
  (2 other events, 13.9 us)

commit v16 on v15

--- a/solution.py
+++ b/solution.py
@@ -204,21 +204,33 @@
     )(place, v_rows, visits, *arrived, *after)
 
 
-def w_gram_kernel(w_ref, gram_ref):
+def spread_w_kernel(n_slots, place, w_ref, gram_ref, spread_ref):
     gram_ref[...] = high_dot(w_ref[...], w_ref[...], COLS_BY_COLS)
-
-
-def own_w_gram(w_start):
-    rank = w_start.shape[1]
-    return pl.pallas_call(
-        w_gram_kernel,
-        in_specs=[VMEM_SPEC],
-        out_specs=VMEM_SPEC,
-        out_shape=jax.ShapeDtypeStruct((rank, rank), F32),
-        compiler_params=parameters(LIMIT),
-        cost_estimate=SHORT,
-        name="own_w_gram",
-    )(w_start)
+    patients, rank = w_ref.shape
+    share = patients // n_slots
+    w_rows = jnp.concatenate([w_ref[...], jnp.zeros((LANES - patients, rank), F32)], axis=0)
+    w_columns = w_rows.T
+    for slot in range(n_slots):
+        first = (feature_of(place) ^ slot) * share
+        columns = pltpu.roll(w_columns, jnp.where(first == 0, 0, LANES - first), 1)
+        spread = [jnp.broadcast_to(columns[:, p : p + 1], (rank, rank)) for p in range(share)]
+        spread_ref[slot] = jnp.concatenate(spread, axis=1)
+
+
+def spread_w(place, w_start, n_slots):
+    patients, rank = w_start.shape
+    return pl.pallas_call(
+        functools.partial(spread_w_kernel, n_slots),
+        in_specs=[SMEM_SPEC, VMEM_SPEC],
+        out_specs=[VMEM_SPEC] * 2,
+        out_shape=[
+            jax.ShapeDtypeStruct((rank, rank), F32),
+            jax.ShapeDtypeStruct((n_slots, rank, patients // n_slots * rank), F32),
+        ],
+        compiler_params=parameters(LIMIT),
+        cost_estimate=SHORT,
+        name="spread_w",
+    )(place, w_start)
 
 
 def own_projection_kernel(place, v_ref, visits_ref, *refs):
@@ -358,7 +370,7 @@
         return carry
 
     lax.fori_loop(0, COARSE_STEPS, functools.partial(sweep, False), 0, unroll=True)
-    lax.fori_loop(COARSE_STEPS, NS_STEPS, functools.partial(sweep, True), 0, unroll=3)
+    lax.fori_loop(COARSE_STEPS, NS_STEPS, functools.partial(sweep, True), 0, unroll=True)
     low = [frames[p].astype(BF16) for p in patients]
     for p in patients:
         frames_ref[p] = low[p]
@@ -443,40 +455,33 @@
     return {item: parts[2 * i : 2 * i + 2] for i, item in enumerate(items)}, token
 
 
-def next_h_kernel(n_terms, n_slots, place, *refs):
-    inverse_ref, w_ref, _, result_ref, h_ref, factor_ref = refs[n_terms:]
+def next_h_kernel(n_terms, *refs):
+    inverse_ref, spread_ref, _, result_ref, h_ref, factor_ref = refs[n_terms:]
     h_next = high_dot(total(refs[:n_terms]), inverse_ref[...])
     result_ref[...] = h_next
     h_ref[...] = h_next
     rank = h_next.shape[0]
-    patients = w_ref.shape[0]
-    share = patients // n_slots
     h_rows = h_next.T
-    w_rows = jnp.concatenate([w_ref[...], jnp.zeros((LANES - patients, rank), F32)], axis=0)
-    w_columns = w_rows.T
-    for slot in range(n_slots):
-        first = (feature_of(place) ^ slot) * share
-        columns = pltpu.roll(w_columns, jnp.where(first == 0, 0, LANES - first), 1)
-        factor = jnp.concatenate([h_rows * columns[:, p : p + 1] for p in range(share)], axis=1)
-        factor_ref[slot] = jnp.concatenate(three_parts(factor), axis=0)
-
-
-def next_h(place, terms, inverse, w_start, n_slots, after):
-    patients, rank = w_start.shape
-    share = patients // n_slots
-    return pl.pallas_call(
-        functools.partial(next_h_kernel, len(terms), n_slots),
-        in_specs=[SMEM_SPEC] + [VMEM_SPEC] * (len(terms) + 2) + [ANY_SPEC],
+    h_rows = jnp.concatenate([h_rows] * (spread_ref.shape[2] // rank), axis=1)
+    for slot in range(spread_ref.shape[0]):
+        factor_ref[slot] = jnp.concatenate(three_parts(h_rows * spread_ref[slot]), axis=0)
+
+
+def next_h(terms, inverse, spread, after):
+    n_slots, rank, columns = spread.shape
+    return pl.pallas_call(
+        functools.partial(next_h_kernel, len(terms)),
+        in_specs=[VMEM_SPEC] * (len(terms) + 2) + [ANY_SPEC],
         out_specs=[VMEM_SPEC] * 3,
         out_shape=[
             jax.ShapeDtypeStruct(inverse.shape, F32),
             jax.ShapeDtypeStruct(inverse.shape, F32),
-            jax.ShapeDtypeStruct((n_slots, 3 * rank, share * rank), BF16),
+            jax.ShapeDtypeStruct((n_slots, 3 * rank, columns), BF16),
         ],
         compiler_params=parameters(LIMIT),
         cost_estimate=SHORT,
         name="next_h",
-    )(place, *terms, inverse, w_start, after)
+    )(*terms, inverse, spread, after)
 
 
 def second_inverse_kernel(h_ref, w_gram_ref, gram_ref, inverse_ref):
@@ -528,45 +533,51 @@
     )(place, factor, *projected, *after)
 
 
-def next_v_kernel(items, share, place, own_ref, other_ref, inverse_ref, h_ref, *refs):
-    *parts, v_ref, sums_ref, v_parts = refs
-    rank = inverse_ref.shape[0]
-    upper = core_of(place) == 1
-    left = jnp.where(upper, other_ref[...], own_ref[...])
-    right = jnp.where(upper, own_ref[...], other_ref[...])
-    v_rows = high_dot(inverse_ref[...], jnp.concatenate([left, right], axis=1))
-    v_ref[...] = v_rows
+def next_v_kernel(items, share, later, place, terms_ref, inverse_ref, h_ref, *refs):
+    parts, refs = refs[: 2 * len(items)], refs[2 * len(items) :]
+    rank, half = terms_ref.shape
+    here = pl.multiple_of((core_of(place) ^ 1 if later else core_of(place)) * half, half)
+    features = pl.ds(here, half)
+    v_rows = high_dot(inverse_ref[...], terms_ref[...])
+    if later:
+        v_before_ref, before_ref, v_ref, sums_ref, v_parts = refs
+        v_ref[:, features] = v_rows
+        v_ref[:, pl.ds(pl.multiple_of(half - here, half), half)] = v_before_ref[...]
+        sums = before_ref[...]
+    else:
+        v_ref, sums_ref, v_parts = refs
+        v_ref[...] = v_rows
+        sums = jnp.zeros((rank, 2 * rank), F32)
     v_parts[...] = jnp.concatenate(two_parts(v_rows), axis=0)
     weights = jnp.concatenate([h_ref[...]] * 2, axis=1)
     gram = low_dot(v_parts[...], v_parts[...], ROWS_BY_ROWS)
     gram = gram[:rank, :rank] + (gram[:rank, rank:] + gram[rank:, :rank])
-    sums_ref[...] = jnp.concatenate([jnp.zeros((rank, rank), F32), gram], axis=1)
+    sums_ref[...] = sums + jnp.concatenate([jnp.zeros((rank, rank), F32), gram], axis=1)
     for i, (slots, done) in enumerate(items):
-        seen = low_dot(parts[2 * i][...], v_parts[...], ROWS_BY_ROWS)
-        seen = seen + low_dot(parts[2 * i + 1][...], v_parts[...], ROWS_BY_ROWS)
+        seen = low_dot(parts[2 * i][:, features], v_parts[...], ROWS_BY_ROWS)
+        seen = seen + low_dot(parts[2 * i + 1][:, features], v_parts[...], ROWS_BY_ROWS)
         count = seen.shape[0] // rank // len(slots)
         for p in range(seen.shape[0] // rank):
             patient = (feature_of(place) ^ slots[p // count]) * share + done + p % count
             row = jnp.sum(seen[p * rank : (p + 1) * rank] * weights, axis=0, keepdims=True)
-            sums_ref[pl.ds(patient, 1), :rank] = row[:, :rank] + row[:, rank:]
-
-
-def next_v(items, share, place, own, other, inverse, h_next, projected):
-    width = projected[0].shape[1]
-    rank = inverse.shape[0]
-    return pl.pallas_call(
-        functools.partial(next_v_kernel, items, share),
-        in_specs=[SMEM_SPEC] + [VMEM_SPEC] * (4 + len(projected)),
+            sums_ref[pl.ds(patient, 1), :rank] += row[:, :rank] + row[:, rank:]
+
+
+def half_v(items, share, place, terms, inverse, h_next, projected, before):
+    rank, half = terms.shape
+    return pl.pallas_call(
+        functools.partial(next_v_kernel, items, share, bool(before)),
+        in_specs=[SMEM_SPEC] + [VMEM_SPEC] * (3 + len(projected) + len(before)),
         out_specs=[VMEM_SPEC] * 2,
         out_shape=[
-            jax.ShapeDtypeStruct((rank, width), F32),
+            jax.ShapeDtypeStruct((rank, 2 * half if before else half), F32),
             jax.ShapeDtypeStruct((rank, 2 * rank), F32),
         ],
-        scratch_shapes=[pltpu.VMEM((2 * rank, width), BF16)],
+        scratch_shapes=[pltpu.VMEM((2 * rank, half), BF16)],
         compiler_params=parameters(LIMIT),
         cost_estimate=SHORT,
         name="next_v",
-    )(place, own, other, inverse, h_next, *projected)
+    )(place, terms, inverse, h_next, *projected, *before)
 
 
 def next_w_kernel(n_sums, *refs):
@@ -654,7 +665,8 @@
     def receive(bit):
         return [slot ^ bit for slot in send(bit)]
 
-    w_grams = staged_terms(own_w_gram(w_start), "patient", [])
+    w_gram, spread = spread_w(place, w_start, n)
+    w_grams = staged_terms(w_gram, "patient", [])
     own, v_gram = project_own(n_parts, place, by_owner, v_near)
     h_local = v_gram
     arrived = [[] for _ in firsts]
@@ -709,7 +721,7 @@
             more, token = project_groups(groups, after)
             projected |= more
             after = [token]
-    h_result, h_next, factor = next_h(place, h_terms, inverse, w_start, n, token)
+    h_result, h_next, factor = next_h(h_terms, inverse, spread, token)
 
     items = list(projected)
     flat = [x for item in items for x in projected[item]]
@@ -717,7 +729,8 @@
     keep = half_v_terms(items, False, place, factor, flat, [send])
     h_gram, second = second_inverse(h_next, w_gram)
     own_terms, other_terms = patient_halves(keep, send, second)
-    v_next, sums = next_v(items, share, place, own_terms, other_terms, second, h_next, flat)
+    before = half_v(items, share, place, own_terms, second, h_next, flat, [])
+    v_next, sums = half_v(items, share, place, other_terms, second, h_next, flat, before)
     w_next = next_w(all_terms(sums, "feature"), h_gram, patients)
     return (h_result, v_next.T, w_next)
 

time: 84.9 us -> 81.8 us (0.963)
  waiting for transfers between devices: 18.6 us -> 12.9 us
  starting transfers between devices: 28.3 us -> 30.5 us
    ppermute x21, waiting for transfers between devices: 18.6 us -> 12.9 us  [swap(): return lax.ppermute(x, axis, pairs)]
    ppermute x21, starting transfers between devices: 28.3 us -> 30.5 us  [swap(): return lax.ppermute(x, axis, pairs)]
    pallas_call x3 -> x4, Pallas kernels: 4.47 us -> 5.49 us  [the longest x2 3.89 us: half_v(): pl.pallas_call(functools.partial(next_v_kernel, items, share, bool(before...]
  transfers between devices with their start and end apart: 21 -> 21, of which waited for: 14 -> 12; matrix products, arithmetic and copies ran while one was open for 0% -> 0% of each run, Pallas kernels for 30% -> 33%
where the time goes in v16:
time: 81.8 us; the launch traced here: 81.7 us
  Pallas kernels  37.1 us (45%)
  starting transfers between devices  30.5 us (37%)
  waiting for transfers between devices  12.9 us (16%)
  between operations  0.84 us (1%)
    ppermute x21, starting transfers between devices, swap(): return lax.ppermute(x, axis, pairs)  30.5 us
    ppermute x21, waiting for transfers between devices, swap(): return lax.ppermute(x, axis, pairs)  12.9 us
    pallas_call x2, Pallas kernels, own_frames(): pl.pallas_call(functools.partial(frames_kernel, layouts, part, share), in...  11.9 us
    pallas_call x2, Pallas kernels, half_v(): pl.pallas_call(functools.partial(next_v_kernel, items, share, bool(before...  3.89 us
    pallas_call x1, Pallas kernels, first_projection(): pl.pallas_call(functools.partial(first_projection_kernel, slots, with_gra...  3.73 us
    pallas_call x3, Pallas kernels, next_projection(): pl.pallas_call(functools.partial(next_projection_kernel, slots, first, co...  3.56 us
    pallas_call x4, Pallas kernels, project_frames(): pl.pallas_call(functools.partial(projected_kernel, items), in_specs=[SMEM...  3.49 us
    pallas_call x1, Pallas kernels, next_w(): pl.pallas_call(functools.partial(next_w_kernel, len(sums)), out_shape=jax...  2.27 us
  transfers between devices with their start and end apart: 21, of which 12 were waited for; matrix products, arithmetic and copies ran while one was open for 0% of the time, Pallas kernels for 33%

profile of v16, /device:TPU:0, one launch (start us, length us, event | category | flops | bytes accessed | tf_op | source)
XLA Modules:
  0.0 81.7 jit_solution(8514468166896841457)
XLA Ops:
  0.7 3.7 %project_first.1 = s16[528,256]{1,0:T(8,128)(2,1)S(1)} custom-call(s32[1]{0:T(128)} %bitcast.place, bf16[64,1024]{1,0:T(8,128)(2,1)} %bitcast.13, bf16[4,8,256,1024]{3,2,1,0:T(8,128)(2,1)} %bitcast.4), custom_call_target="tpu_custom_call" | custom-call | flops 1000 | bytes 1000 | tf_op jit(solution)/shard_map/project_first/pallas_call | solution.py:158
  4.4 3.0 %collective-permute-start = (s16[528,256]{1,0:T(8,128)(2,1)S(1)}, s16[528,256]{1,0:T(8,128)(2,1)S(1)}, u32[]{:S(2)}, u32[]{:S(2)}) collective-permute-start(s16[528,256]{1,0:T(8,128)(2,1)S(1)} %project_first.1), channel_id=1, source_target_pairs={{0,1},{1,0},{2,3},{3,2},{4,5},{5,4},{6,7},{7,6},{8,9},{9,8},{10,11... | collective-permute-start | bytes 811016 | tf_op jit(solution)/shard_map/ppermute | solution.py:604
  7.8 1.6 %project_next.4 = s16[560,256]{1,0:T(8,128)(2,1)S(1)} custom-call(s32[1]{0:T(128)} %bitcast.place, bf16[64,1024]{1,0:T(8,128)(2,1)S(1)} %bitcast.14, bf16[4,8,256,1024]{3,2,1,0:T(8,128)(2,1)S(1)} %bitcast.5), custom_call_target="tpu_custom_call" | custom-call | flops 1000 | bytes 1000 | tf_op jit(solution)/shard_map/project_next/pallas_call | solution.py:196
  9.4 3.0 %collective-permute-start.3 = (s16[560,256]{1,0:T(8,128)(2,1)S(1)}, s16[560,256]{1,0:T(8,128)(2,1)S(1)}, u32[]{:S(2)}, u32[]{:S(2)}) collective-permute-start(s16[560,256]{1,0:T(8,128)(2,1)S(1)} %project_next.4), channel_id=1, source_target_pairs={{0,1},{1,0},{2,3},{3,2},{4,5},{5,4},{6,7},{7,6},{8,9},{9,8},{10,11... | collective-permute-start | bytes 860168 | tf_op jit(solution)/shard_map/ppermute | solution.py:604
  15.6 3.2 %collective-permute-start.2 = (s16[272,256]{1,0:T(8,128)(2,1)S(1)}, s16[272,256]{1,0:T(8,128)(2,1)S(1)}, u32[]{:S(2)}, u32[]{:S(2)}) collective-permute-start(s16[272,256]{1,0:T(8,128)(2,1)S(1)} %project_next.3), channel_id=1, source_target_pairs={{0,2},{1,3},{2,0},{3,1},{4,6},{5,7},{6,4},{7,5},{8,10},{9,11},{10,... | collective-permute-start | bytes 417800 | tf_op jit(solution)/shard_map/ppermute | solution.py:604
  24.9 6.0 %own_frames.2 = (bf16[4,64,256]{2,1,0:T(8,128)(2,1)S(1)}, f32[64,64]{1,0:T(8,128)S(1)}, f32[64,64]{1,0:T(8,128)S(1)}) custom-call(s32[1]{0:T(128)} %bitcast.place, s32[32]{0:T(128)S(1)} %copy-done.4, f32[64,64]{1,0:T(8,128)S(1)} %copy-done.3, f32[32,64]{1,0:T(8,128)S(1)} %copy-done.2, f32[64,64]{1,0:T(8,128)S(1)} %get-tuple-element.41.v_gram_ref.before_ref.refs_2_, ...), custom_call_target="tpu_custom_call" | custom-call | flops 1000 | bytes 1000 | tf_op jit(solution)/shard_map/own_frames/pallas_call | solution.py:389
  30.9 2.1 %collective-permute-start.7 = (bf16[4,64,256]{2,1,0:T(8,128)(2,1)S(1)}, bf16[4,64,256]{2,1,0:T(8,128)(2,1)S(1)}, u32[]{:S(2)}, u32[]{:S(2)}) collective-permute-start(bf16[4,64,256]{2,1,0:T(8,128)(2,1)S(1)} %get-tuple-element.48.refs_0_), channel_id=1, source_target_pairs={{0,2},{1,3},{2,0},{3,1},{4,6},{5,7},{6,4},{7,5},{8,10},{9,11},{10,... | collective-permute-start | bytes 393224 | tf_op jit(solution)/shard_map/ppermute | solution.py:604
  33.0 6.0 %own_frames.3 = (bf16[4,64,256]{2,1,0:T(8,128)(2,1)S(1)}, f32[64,64]{1,0:T(8,128)S(1)}, f32[64,64]{1,0:T(8,128)S(1)}) custom-call(s32[1]{0:T(128)} %bitcast.place, s32[32]{0:T(128)S(1)} %copy-done.4, f32[64,64]{1,0:T(8,128)S(1)} %copy-done.3, f32[32,64]{1,0:T(8,128)S(1)} %copy-done.2, f32[64,64]{1,0:T(8,128)S(1)} %get-tuple-element.44.v_gram_ref, ...), custom_call_target="tpu_custom_call" | custom-call | flops 1000 | bytes 1000 | tf_op jit(solution)/shard_map/own_frames/pallas_call | solution.py:389
  40.6 1.6 %collective-permute-start.12 = (bf16[4,64,256]{2,1,0:T(8,128)(2,1)S(1)}, bf16[4,64,256]{2,1,0:T(8,128)(2,1)S(1)}, u32[]{:S(2)}, u32[]{:S(2)}) collective-permute-start(bf16[4,64,256]{2,1,0:T(8,128)(2,1)S(1)} %get-tuple-element.49.refs_2_.refs_1_.refs_0_), channel_id=1, source_target_pairs={{0,2},{1,3},{2,0},{3,1},{4,6},{5,7},{6,4},{7,5},{8,10},{9,11},{10,... | collective-permute-start | bytes 393224 | tf_op jit(solution)/shard_map/ppermute | solution.py:604
  43.5 1.6 %collective-permute-start.8 = (f32[64,64]{1,0:T(8,128)S(1)}, f32[64,64]{1,0:T(8,128)S(1)}, u32[]{:S(2)}, u32[]{:S(2)}) collective-permute-start(f32[64,64]{1,0:T(8,128)S(1)} %add_terms.6.refs_2_.a_ref), channel_id=1, source_target_pairs={{0,8},{4,12},{8,0},{12,4},{1,9},{5,13},{9,1},{13,5},{2,10},{6,14},... | collective-permute-start | bytes 49160 | tf_op jit(solution)/shard_map/ppermute | solution.py:604
  45.1 1.7 %first_inverse.1 = (f32[64,64]{1,0:T(8,128)S(1)}, f32[64,64]{1,0:T(8,128)S(1)}) custom-call(f32[64,64]{1,0:T(8,128)S(1)} %get-tuple-element.51.v_gram_ref, f32[64,64]{1,0:T(8,128)S(1)} %add_terms.5.refs_1_.refs_0_, f32[64,64]{1,0:T(8,128)S(1)} %collective-permute-done.4.refs_1_, f32[64,64]{1,0:T(8,128)S(1)} %add_terms.6.refs_2_.a_ref), custom_call_target="tpu_custom_call" | custom-call | flops 1000 | bytes 1000 | tf_op jit(solution)/shard_map/first_inverse/pallas_call | solution.py:316
  47.7 1.8 %collective-permute-done.13.refs_3_.refs_0_ = bf16[8,64,256]{2,1,0:T(8,128)(2,1)S(1)} collective-permute-done((bf16[8,64,256]{2,1,0:T(8,128)(2,1)S(1)}, bf16[8,64,256]{2,1,0:T(8,128)(2,1)S(1)}, u32[]{:S(2)}, u32[]{:S(2)}) %collective-permute-start.13) | collective-permute-done | bytes 262176 | tf_op jit(solution)/shard_map/ppermute | solution.py:604
  50.5 1.8 %collective-permute-start.11 = (f32[64,64]{1,0:T(8,128)S(1)}, f32[64,64]{1,0:T(8,128)S(1)}, u32[]{:S(2)}, u32[]{:S(2)}) collective-permute-start(f32[64,64]{1,0:T(8,128)S(1)} %add_terms.7.refs_2_.refs_0_), channel_id=1, source_target_pairs={{0,3},{1,2},{2,1},{3,0},{4,7},{5,6},{6,5},{7,4},{8,11},{9,10},{10,... | collective-permute-start | bytes 49160 | tf_op jit(solution)/shard_map/ppermute | solution.py:604
  53.1 1.8 %collective-permute-start.9 = (f32[64,64]{1,0:T(8,128)S(1)}, f32[64,64]{1,0:T(8,128)S(1)}, u32[]{:S(2)}, u32[]{:S(2)}) collective-permute-start(f32[64,64]{1,0:T(8,128)S(1)} %add_terms.7.refs_2_.refs_0_), channel_id=1, source_target_pairs={{0,1},{1,0},{2,3},{3,2},{4,5},{5,4},{6,7},{7,6},{8,9},{9,8},{10,11... | collective-permute-start | bytes 49160 | tf_op jit(solution)/shard_map/ppermute | solution.py:604
  56.3 1.9 %collective-permute-done.14.refs_0_ = bf16[8,64,256]{2,1,0:T(8,128)(2,1)S(1)} collective-permute-done((bf16[8,64,256]{2,1,0:T(8,128)(2,1)S(1)}, bf16[8,64,256]{2,1,0:T(8,128)(2,1)S(1)}, u32[]{:S(2)}, u32[]{:S(2)}) %collective-permute-start.14) | collective-permute-done | bytes 262176 | tf_op jit(solution)/shard_map/ppermute | solution.py:604
  62.2 2.4 %collective-permute-start.16 = (f32[64,512]{1,0:T(8,128)S(1)}, f32[64,512]{1,0:T(8,128)S(1)}, u32[]{:S(2)}, u32[]{:S(2)}) collective-permute-start(f32[64,512]{1,0:T(8,128)S(1)} %add_terms.8.a_ref), channel_id=1, source_target_pairs={{0,8},{4,12},{8,0},{12,4},{1,9},{5,13},{9,1},{13,5},{2,10},{6,14},... | collective-permute-start | bytes 393224 | tf_op jit(solution)/shard_map/ppermute | solution.py:604
  64.6 1.7 %second_inverse.1 = (f32[64,64]{1,0:T(8,128)S(1)}, f32[64,64]{1,0:T(8,128)S(1)}) custom-call(f32[64,64]{1,0:T(8,128)S(1)} %get-tuple-element.71.h_ref, f32[64,64]{1,0:T(8,128)S(1)} %get-tuple-element.72.w_gram_ref), custom_call_target="tpu_custom_call" | custom-call | flops 1000 | bytes 1000 | tf_op jit(solution)/shard_map/second_inverse/pallas_call | solution.py:495
  66.3 2.1 %collective-permute-done.16.b_ref = f32[64,512]{1,0:T(8,128)S(1)} collective-permute-done((f32[64,512]{1,0:T(8,128)S(1)}, f32[64,512]{1,0:T(8,128)S(1)}, u32[]{:S(2)}, u32[]{:S(2)}) %collective-permute-start.16) | collective-permute-done | bytes 131104 | tf_op jit(solution)/shard_map/ppermute | solution.py:604
  68.5 1.6 %next_v.2 = (f32[64,512]{1,0:T(8,128)S(1)}, f32[64,128]{1,0:T(8,128)S(1)}) custom-call(s32[1]{0:T(128)} %bitcast.place, f32[64,512]{1,0:T(8,128)S(1)} %add_terms.9.terms_ref, f32[64,64]{1,0:T(8,128)S(1)} %get-tuple-element.73.refs_0_.inverse_ref, f32[64,64]{1,0:T(8,128)S(1)} %get-tuple-element.71.h_ref, bf16[256,1024]{1,0:T(8,128)(2,1)S(1)} %get-tuple-element.59.refs_0_, ...), custom_call_target="tpu_custom_call" | custom-call | flops 1000 | bytes 1000 | tf_op jit(solution)/shard_map/next_v/pallas_call | solution.py:568
  70.2 2.3 %next_v.3 = (f32[64,1024]{1,0:T(8,128)}, f32[64,128]{1,0:T(8,128)S(1)}) custom-call(s32[1]{0:T(128)} %bitcast.place, f32[64,512]{1,0:T(8,128)S(1)} %collective-permute-done.17.terms_ref, f32[64,64]{1,0:T(8,128)S(1)} %get-tuple-element.73.refs_0_.inverse_ref, f32[64,64]{1,0:T(8,128)S(1)} %get-tuple-element.71.h_ref, ...), custom_call_target="tpu_custom_call" | custom-call | flops 1000 | bytes 1000 | tf_op jit(solution)/shard_map/next_v/pallas_call | solution.py:568
  72.4 1.8 %collective-permute-start.20 = (f32[64,128]{1,0:T(8,128)S(1)}, f32[64,128]{1,0:T(8,128)S(1)}, u32[]{:S(2)}, u32[]{:S(2)}) collective-permute-start(f32[64,128]{1,0:T(8,128)S(1)} %get-tuple-element.77.refs_0_), channel_id=1, source_target_pairs={{0,3},{1,2},{2,1},{3,0},{4,7},{5,6},{6,5},{7,4},{8,11},{9,10},{10,... | collective-permute-start | bytes 98312 | tf_op jit(solution)/shard_map/ppermute | solution.py:604
  74.3 2.5 %collective-permute-start.18 = (f32[64,128]{1,0:T(8,128)S(1)}, f32[64,128]{1,0:T(8,128)S(1)}, u32[]{:S(2)}, u32[]{:S(2)}) collective-permute-start(f32[64,128]{1,0:T(8,128)S(1)} %get-tuple-element.77.refs_0_), channel_id=1, source_target_pairs={{0,1},{1,0},{2,3},{3,2},{4,5},{5,4},{6,7},{7,6},{8,9},{9,8},{10,11... | collective-permute-start | bytes 98312 | tf_op jit(solution)/shard_map/ppermute | solution.py:604
  76.8 1.6 %collective-permute-done.20.refs_3_ = f32[64,128]{1,0:T(8,128)S(1)} collective-permute-done((f32[64,128]{1,0:T(8,128)S(1)}, f32[64,128]{1,0:T(8,128)S(1)}, u32[]{:S(2)}, u32[]{:S(2)}) %collective-permute-start.20) | collective-permute-done | bytes 32800 | tf_op jit(solution)/shard_map/ppermute | solution.py:604
  79.4 2.3 %next_w.1 = f32[32,64]{1,0:T(8,128)} custom-call(f32[64,128]{1,0:T(8,128)S(1)} %get-tuple-element.77.refs_0_, f32[64,128]{1,0:T(8,128)S(1)} %collective-permute-done.18.refs_1_, f32[64,128]{1,0:T(8,128)S(1)} %collective-permute-done.19.refs_2_, f32[64,128]{1,0:T(8,128)S(1)} %collective-permute-done.20.refs_3_, f32[64,64]{1,0:T(8,128)S(1)} %get-tuple-element.78.refs_4_), custom_call_target="tpu_custom_call" | custom-call | flops 1000 | bytes 1000 | tf_op jit(solution)/shard_map/next_w/pallas_call | solution.py:593
  (55 shorter events, 21.6 us)
Async XLA Ops:
  0.7 11.8 %copy-start.2 = (f32[32,64]{1,0:T(8,128)S(1)}, f32[32,64]{1,0:T(8,128)}, u32[]{:S(2)}) copy-start(f32[32,64]{1,0:T(8,128)} %w_ref.5) | copy-start | bytes 24580
  4.4 10.2 %collective-permute-start = (s16[528,256]{1,0:T(8,128)(2,1)S(1)}, s16[528,256]{1,0:T(8,128)(2,1)S(1)}, u32[]{:S(2)}, u32[]{:S(2)}) collective-permute-start(s16[528,256]{1,0:T(8,128)(2,1)S(1)} %project_first.1), channel_id=1, source_target_pairs={{0,1},{1,0},{2,3},{3,2},{4,5},{5,4},{6,7},{7,6},{8,9},{9,8},{10,11... | collective-permute-start | bytes 811016 | tf_op jit(solution)/shard_map/ppermute | solution.py:604
  9.4 13.6 %collective-permute-start.3 = (s16[560,256]{1,0:T(8,128)(2,1)S(1)}, s16[560,256]{1,0:T(8,128)(2,1)S(1)}, u32[]{:S(2)}, u32[]{:S(2)}) collective-permute-start(s16[560,256]{1,0:T(8,128)(2,1)S(1)} %project_next.4), channel_id=1, source_target_pairs={{0,1},{1,0},{2,3},{3,2},{4,5},{5,4},{6,7},{7,6},{8,9},{9,8},{10,11... | collective-permute-start | bytes 860168 | tf_op jit(solution)/shard_map/ppermute | solution.py:604
  13.3 1.3 %collective-permute-start.1 = (f32[64,64]{1,0:T(8,128)S(1)}, f32[64,64]{1,0:T(8,128)S(1)}, u32[]{:S(2)}, u32[]{:S(2)}) collective-permute-start(f32[64,64]{1,0:T(8,128)S(1)} %get-tuple-element.43.a_ref), channel_id=1, source_target_pairs={{0,4},{4,0},{8,12},{12,8},{1,5},{5,1},{9,13},{13,9},{2,6},{6,2},{1... | collective-permute-start | bytes 49160 | tf_op jit(solution)/shard_map/ppermute | solution.py:604
  15.6 9.4 %copy-start.3 = (f32[64,64]{1,0:T(8,128)S(1)}, f32[64,64]{1,0:T(8,128)}, u32[]{:S(2)}) copy-start(f32[64,64]{1,0:T(8,128)} %h_ref.3) | copy-start | bytes 49156
  15.6 9.4 %copy-start.4 = (s32[32]{0:T(128)S(1)}, s32[32]{0:T(128)}, u32[]{:S(2)}) copy-start(s32[32]{0:T(128)} %counts_ref.3) | copy-start | bytes 388
  15.6 9.4 %collective-permute-start.2 = (s16[272,256]{1,0:T(8,128)(2,1)S(1)}, s16[272,256]{1,0:T(8,128)(2,1)S(1)}, u32[]{:S(2)}, u32[]{:S(2)}) collective-permute-start(s16[272,256]{1,0:T(8,128)(2,1)S(1)} %project_next.3), channel_id=1, source_target_pairs={{0,2},{1,3},{2,0},{3,1},{4,6},{5,7},{6,4},{7,5},{8,10},{9,11},{10,... | collective-permute-start | bytes 417800 | tf_op jit(solution)/shard_map/ppermute | solution.py:604
  18.8 3.9 %collective-permute-start.4 = (f32[64,64]{1,0:T(8,128)S(1)}, f32[64,64]{1,0:T(8,128)S(1)}, u32[]{:S(2)}, u32[]{:S(2)}) collective-permute-start(f32[64,64]{1,0:T(8,128)S(1)} %add_terms.5.refs_1_.refs_0_), channel_id=1, source_target_pairs={{0,8},{4,12},{8,0},{12,4},{1,9},{5,13},{9,1},{13,5},{2,10},{6,14},... | collective-permute-start | bytes 49160 | tf_op jit(solution)/shard_map/ppermute | solution.py:604
  24.0 9.0 %collective-permute-start.5 = (s16[304,256]{1,0:T(8,128)(2,1)S(1)}, s16[304,256]{1,0:T(8,128)(2,1)S(1)}, u32[]{:S(2)}, u32[]{:S(2)}) collective-permute-start(s16[304,256]{1,0:T(8,128)(2,1)S(1)} %project_next.5), channel_id=1, source_target_pairs={{0,2},{1,3},{2,0},{3,1},{4,6},{5,7},{6,4},{7,5},{8,10},{9,11},{10,... | collective-permute-start | bytes 466952 | tf_op jit(solution)/shard_map/ppermute | solution.py:604
  30.9 8.5 %collective-permute-start.7 = (bf16[4,64,256]{2,1,0:T(8,128)(2,1)S(1)}, bf16[4,64,256]{2,1,0:T(8,128)(2,1)S(1)}, u32[]{:S(2)}, u32[]{:S(2)}) collective-permute-start(bf16[4,64,256]{2,1,0:T(8,128)(2,1)S(1)} %get-tuple-element.48.refs_0_), channel_id=1, source_target_pairs={{0,2},{1,3},{2,0},{3,1},{4,6},{5,7},{6,4},{7,5},{8,10},{9,11},{10,... | collective-permute-start | bytes 393224 | tf_op jit(solution)/shard_map/ppermute | solution.py:604
  39.4 10.1 %collective-permute-start.13 = (bf16[8,64,256]{2,1,0:T(8,128)(2,1)S(1)}, bf16[8,64,256]{2,1,0:T(8,128)(2,1)S(1)}, u32[]{:S(2)}, u32[]{:S(2)}) collective-permute-start(bf16[8,64,256]{2,1,0:T(8,128)(2,1)S(1)} %join_frames.2.refs_3_), channel_id=1, source_target_pairs={{0,1},{1,0},{2,3},{3,2},{4,5},{5,4},{6,7},{7,6},{8,9},{9,8},{10,11... | collective-permute-start | bytes 786440 | tf_op jit(solution)/shard_map/ppermute | solution.py:604
  40.6 7.1 %collective-permute-start.12 = (bf16[4,64,256]{2,1,0:T(8,128)(2,1)S(1)}, bf16[4,64,256]{2,1,0:T(8,128)(2,1)S(1)}, u32[]{:S(2)}, u32[]{:S(2)}) collective-permute-start(bf16[4,64,256]{2,1,0:T(8,128)(2,1)S(1)} %get-tuple-element.49.refs_2_.refs_1_.refs_0_), channel_id=1, source_target_pairs={{0,2},{1,3},{2,0},{3,1},{4,6},{5,7},{6,4},{7,5},{8,10},{9,11},{10,... | collective-permute-start | bytes 393224 | tf_op jit(solution)/shard_map/ppermute | solution.py:604
  42.3 1.3 %collective-permute-start.6 = (f32[64,64]{1,0:T(8,128)S(1)}, f32[64,64]{1,0:T(8,128)S(1)}, u32[]{:S(2)}, u32[]{:S(2)}) collective-permute-start(f32[64,64]{1,0:T(8,128)S(1)} %get-tuple-element.47.a_ref), channel_id=1, source_target_pairs={{0,4},{4,0},{8,12},{12,8},{1,5},{5,1},{9,13},{13,9},{2,6},{6,2},{1... | collective-permute-start | bytes 49160 | tf_op jit(solution)/shard_map/ppermute | solution.py:604
  43.5 4.0 %collective-permute-start.8 = (f32[64,64]{1,0:T(8,128)S(1)}, f32[64,64]{1,0:T(8,128)S(1)}, u32[]{:S(2)}, u32[]{:S(2)}) collective-permute-start(f32[64,64]{1,0:T(8,128)S(1)} %add_terms.6.refs_2_.a_ref), channel_id=1, source_target_pairs={{0,8},{4,12},{8,0},{12,4},{1,9},{5,13},{9,1},{13,5},{2,10},{6,14},... | collective-permute-start | bytes 49160 | tf_op jit(solution)/shard_map/ppermute | solution.py:604
  49.6 8.7 %collective-permute-start.14 = (bf16[8,64,256]{2,1,0:T(8,128)(2,1)S(1)}, bf16[8,64,256]{2,1,0:T(8,128)(2,1)S(1)}, u32[]{:S(2)}, u32[]{:S(2)}) collective-permute-start(bf16[8,64,256]{2,1,0:T(8,128)(2,1)S(1)} %join_frames.3.refs_1_), channel_id=1, source_target_pairs={{0,1},{1,0},{2,3},{3,2},{4,5},{5,4},{6,7},{7,6},{8,9},{9,8},{10,11... | collective-permute-start | bytes 786440 | tf_op jit(solution)/shard_map/ppermute | solution.py:604
  50.5 8.6 %collective-permute-start.11 = (f32[64,64]{1,0:T(8,128)S(1)}, f32[64,64]{1,0:T(8,128)S(1)}, u32[]{:S(2)}, u32[]{:S(2)}) collective-permute-start(f32[64,64]{1,0:T(8,128)S(1)} %add_terms.7.refs_2_.refs_0_), channel_id=1, source_target_pairs={{0,3},{1,2},{2,1},{3,0},{4,7},{5,6},{6,5},{7,4},{8,11},{9,10},{10,... | collective-permute-start | bytes 49160 | tf_op jit(solution)/shard_map/ppermute | solution.py:604
  52.3 6.8 %collective-permute-start.10 = (f32[64,64]{1,0:T(8,128)S(1)}, f32[64,64]{1,0:T(8,128)S(1)}, u32[]{:S(2)}, u32[]{:S(2)}) collective-permute-start(f32[64,64]{1,0:T(8,128)S(1)} %add_terms.7.refs_2_.refs_0_), channel_id=1, source_target_pairs={{0,2},{1,3},{2,0},{3,1},{4,6},{5,7},{6,4},{7,5},{8,10},{9,11},{10,... | collective-permute-start | bytes 49160 | tf_op jit(solution)/shard_map/ppermute | solution.py:604
  53.1 6.0 %collective-permute-start.9 = (f32[64,64]{1,0:T(8,128)S(1)}, f32[64,64]{1,0:T(8,128)S(1)}, u32[]{:S(2)}, u32[]{:S(2)}) collective-permute-start(f32[64,64]{1,0:T(8,128)S(1)} %add_terms.7.refs_2_.refs_0_), channel_id=1, source_target_pairs={{0,1},{1,0},{2,3},{3,2},{4,5},{5,4},{6,7},{7,6},{8,9},{9,8},{10,11... | collective-permute-start | bytes 49160 | tf_op jit(solution)/shard_map/ppermute | solution.py:604
  60.8 1.4 %collective-permute-start.15 = (f32[64,512]{1,0:T(8,128)S(1)}, f32[64,512]{1,0:T(8,128)S(1)}, u32[]{:S(2)}, u32[]{:S(2)}) collective-permute-start(f32[64,512]{1,0:T(8,128)S(1)} %v_terms.2.refs_12_), channel_id=1, source_target_pairs={{0,4},{4,0},{8,12},{12,8},{1,5},{5,1},{9,13},{13,9},{2,6},{6,2},{1... | collective-permute-start | bytes 393224 | tf_op jit(solution)/shard_map/ppermute | solution.py:604
  62.2 6.2 %collective-permute-start.16 = (f32[64,512]{1,0:T(8,128)S(1)}, f32[64,512]{1,0:T(8,128)S(1)}, u32[]{:S(2)}, u32[]{:S(2)}) collective-permute-start(f32[64,512]{1,0:T(8,128)S(1)} %add_terms.8.a_ref), channel_id=1, source_target_pairs={{0,8},{4,12},{8,0},{12,4},{1,9},{5,13},{9,1},{13,5},{2,10},{6,14},... | collective-permute-start | bytes 393224 | tf_op jit(solution)/shard_map/ppermute | solution.py:604
  68.4 1.7 %collective-permute-start.17 = (f32[64,512]{1,0:T(8,128)S(1)}, f32[64,512]{1,0:T(8,128)S(1)}, u32[]{:S(2)}, u32[]{:S(2)}) collective-permute-start(f32[64,512]{1,0:T(8,128)S(1)} %add_terms.9.terms_ref), channel_id=1, source_target_pairs={{0,4},{4,0},{8,12},{12,8},{1,5},{5,1},{9,13},{13,9},{2,6},{6,2},{1... | collective-permute-start | bytes 393224 | tf_op jit(solution)/shard_map/ppermute | solution.py:604
  72.4 6.0 %collective-permute-start.20 = (f32[64,128]{1,0:T(8,128)S(1)}, f32[64,128]{1,0:T(8,128)S(1)}, u32[]{:S(2)}, u32[]{:S(2)}) collective-permute-start(f32[64,128]{1,0:T(8,128)S(1)} %get-tuple-element.77.refs_0_), channel_id=1, source_target_pairs={{0,3},{1,2},{2,1},{3,0},{4,7},{5,6},{6,5},{7,4},{8,11},{9,10},{10,... | collective-permute-start | bytes 98312 | tf_op jit(solution)/shard_map/ppermute | solution.py:604
  74.3 5.1 %collective-permute-start.19 = (f32[64,128]{1,0:T(8,128)S(1)}, f32[64,128]{1,0:T(8,128)S(1)}, u32[]{:S(2)}, u32[]{:S(2)}) collective-permute-start(f32[64,128]{1,0:T(8,128)S(1)} %get-tuple-element.77.refs_0_), channel_id=1, source_target_pairs={{0,2},{1,3},{2,0},{3,1},{4,6},{5,7},{6,4},{7,5},{8,10},{9,11},{10,... | collective-permute-start | bytes 98312 | tf_op jit(solution)/shard_map/ppermute | solution.py:604
  74.3 5.1 %collective-permute-start.18 = (f32[64,128]{1,0:T(8,128)S(1)}, f32[64,128]{1,0:T(8,128)S(1)}, u32[]{:S(2)}, u32[]{:S(2)}) collective-permute-start(f32[64,128]{1,0:T(8,128)S(1)} %get-tuple-element.77.refs_0_), channel_id=1, source_target_pairs={{0,1},{1,0},{2,3},{3,2},{4,5},{5,4},{6,7},{7,6},{8,9},{9,8},{10,11... | collective-permute-start | bytes 98312 | tf_op jit(solution)/shard_map/ppermute | solution.py:604
  (2 other events, 13.9 us)

commit v17 on v16

--- a/solution.py
+++ b/solution.py
@@ -539,15 +539,9 @@
     here = pl.multiple_of((core_of(place) ^ 1 if later else core_of(place)) * half, half)
     features = pl.ds(here, half)
     v_rows = high_dot(inverse_ref[...], terms_ref[...])
-    if later:
-        v_before_ref, before_ref, v_ref, sums_ref, v_parts = refs
-        v_ref[:, features] = v_rows
-        v_ref[:, pl.ds(pl.multiple_of(half - here, half), half)] = v_before_ref[...]
-        sums = before_ref[...]
-    else:
-        v_ref, sums_ref, v_parts = refs
-        v_ref[...] = v_rows
-        sums = jnp.zeros((rank, 2 * rank), F32)
+    *before, v_ref, sums_ref, v_parts = refs
+    v_ref[...] = v_rows
+    sums = before[0][...] if later else jnp.zeros((rank, 2 * rank), F32)
     v_parts[...] = jnp.concatenate(two_parts(v_rows), axis=0)
     weights = jnp.concatenate([h_ref[...]] * 2, axis=1)
     gram = low_dot(v_parts[...], v_parts[...], ROWS_BY_ROWS)
@@ -570,7 +564,7 @@
         in_specs=[SMEM_SPEC] + [VMEM_SPEC] * (3 + len(projected) + len(before)),
         out_specs=[VMEM_SPEC] * 2,
         out_shape=[
-            jax.ShapeDtypeStruct((rank, 2 * half if before else half), F32),
+            jax.ShapeDtypeStruct((rank, half), F32),
             jax.ShapeDtypeStruct((rank, 2 * rank), F32),
         ],
         scratch_shapes=[pltpu.VMEM((2 * rank, half), BF16)],
@@ -580,23 +574,46 @@
     )(place, terms, inverse, h_next, *projected, *before)
 
 
+def whole_v_kernel(place, own_ref, other_ref, v_ref, token_ref):
+    half = own_ref.shape[1]
+    upper = core_of(place) == 1
+    v_ref[:, :half] = jnp.where(upper, other_ref[...], own_ref[...])
+    v_ref[:, half:] = jnp.where(upper, own_ref[...], other_ref[...])
+    token_ref[...] = jnp.zeros_like(token_ref)
+
+
+def whole_v(place, own, other):
+    rank, half = own.shape
+    return pl.pallas_call(
+        whole_v_kernel,
+        in_specs=[SMEM_SPEC] + [VMEM_SPEC] * 2,
+        out_specs=[VMEM_SPEC] * 2,
+        out_shape=[jax.ShapeDtypeStruct((rank, 2 * half), F32), jax.ShapeDtypeStruct((8, LANES), F32)],
+        compiler_params=parameters(LIMIT),
+        cost_estimate=SHORT,
+        name="whole_v",
+    )(place, own, other)
+
+
 def next_w_kernel(n_sums, *refs):
-    gram_ref, w_ref = refs[n_sums:]
+    gram_ref, _, w_ref = refs[n_sums:]
     patients, rank = w_ref.shape
     sums = total(refs[:n_sums])
     table = jnp.concatenate([sums[:, rank:] * gram_ref[...], sums.T[:rank]], axis=1)
     w_ref[...] = eliminate(table, rank).T[rank : rank + patients]
 
 
-def next_w(sums, h_gram, patients):
+def next_w(sums, h_gram, patients, after):
     rank = h_gram.shape[0]
     return pl.pallas_call(
         functools.partial(next_w_kernel, len(sums)),
+        in_specs=[VMEM_SPEC] * (len(sums) + 1) + [ANY_SPEC],
+        out_specs=VMEM_SPEC,
         out_shape=jax.ShapeDtypeStruct((patients, rank), F32),
         compiler_params=parameters(LIMIT),
         cost_estimate=SHORT,
         name="next_w",
-    )(*sums, h_gram)
+    )(*sums, h_gram, after)
 
 
 def swap(x, axis, slot):
@@ -712,15 +729,16 @@
     projected, token = project_groups(first_groups, joined)
     h_sums = staged_terms(h_local, "patient", [token])
     w_gram, inverse = first_inverse(v_gram, w_grams, h_sums[0])
-    h_sum = add(*h_sums, [inverse])
-    joined = double(n_parts - 1, [h_sum] + [frames[part][k][1] for part, k in early])
+    after = double(n_parts - 1, [inverse])
+    if early:
+        more, token = project_groups(early, after)
+        projected |= more
+        after = [token]
+    h_sum = add(*h_sums, after)
     h_terms = all_terms(h_sum, "feature")
-    after = joined
-    for groups in [early] + [[(n_parts - 1, k)] for k in range(1, last + 1)]:
-        if groups:
-            more, token = project_groups(groups, after)
-            projected |= more
-            after = [token]
+    for k in range(1, last + 1):
+        more, token = project_groups([(n_parts - 1, k)], [h_sum] if k == 1 else [token])
+        projected |= more
     h_result, h_next, factor = next_h(h_terms, inverse, spread, token)
 
     items = list(projected)
@@ -729,9 +747,10 @@
     keep = half_v_terms(items, False, place, factor, flat, [send])
     h_gram, second = second_inverse(h_next, w_gram)
     own_terms, other_terms = patient_halves(keep, send, second)
-    before = half_v(items, share, place, own_terms, second, h_next, flat, [])
-    v_next, sums = half_v(items, share, place, other_terms, second, h_next, flat, before)
-    w_next = next_w(all_terms(sums, "feature"), h_gram, patients)
+    v_own, before = half_v(items, share, place, own_terms, second, h_next, flat, [])
+    v_other, sums = half_v(items, share, place, other_terms, second, h_next, flat, [before])
+    v_next, token = whole_v(place, v_own, v_other)
+    w_next = next_w(all_terms(sums, "feature"), h_gram, patients, token)
     return (h_result, v_next.T, w_next)
 
 

time: 81.8 us -> 94.7 us (1.16)
  waiting for transfers between devices: 12.9 us -> 23.1 us
  local copies, waits for them, and re-layouts: 0.36 us -> 6.7 us
  starting transfers between devices: 30.5 us -> 26.7 us
    ppermute x21, waiting for transfers between devices: 12.9 us -> 23.1 us  [swap(): return lax.ppermute(x, axis, pairs)]
    unnamed x10 -> x20, local copies, waits for them, and re-layouts: 0.36 us -> 6.7 us
    ppermute x21, starting transfers between devices: 30.5 us -> 26.7 us  [swap(): return lax.ppermute(x, axis, pairs)]
    pallas_call x1 -> x2, Pallas kernels: 2.27 us -> 2.99 us  [the longest x1 2.27 us: next_w(): pl.pallas_call(functools.partial(next_w_kernel, len(sums)), in_specs=[VME...]
  transfers between devices with their start and end apart: 21 -> 21, of which waited for: 12 -> 12; matrix products, arithmetic and copies ran while one was open for 0% -> 0% of each run, Pallas kernels for 33% -> 32%
where the time goes in v17:
time: 94.7 us; the launch traced here: 94.5 us
  Pallas kernels  37.1 us (39%)
  starting transfers between devices  26.7 us (28%)
  waiting for transfers between devices  23.1 us (24%)
  local copies, waits for them, and re-layouts  6.7 us (7%)
    ppermute x21, starting transfers between devices, swap(): return lax.ppermute(x, axis, pairs)  26.7 us
    ppermute x21, waiting for transfers between devices, swap(): return lax.ppermute(x, axis, pairs)  23.1 us
    pallas_call x2, Pallas kernels, own_frames(): pl.pallas_call(functools.partial(frames_kernel, layouts, part, share), in...  11.9 us
    unnamed x20, local copies, waits for them, and re-layouts  6.7 us
    pallas_call x1, Pallas kernels, first_projection(): pl.pallas_call(functools.partial(first_projection_kernel, slots, with_gra...  3.61 us
    pallas_call x3, Pallas kernels, next_projection(): pl.pallas_call(functools.partial(next_projection_kernel, slots, first, co...  3.57 us
    pallas_call x4, Pallas kernels, project_frames(): pl.pallas_call(functools.partial(projected_kernel, items), in_specs=[SMEM...  3.49 us
    pallas_call x2, Pallas kernels, half_v(): pl.pallas_call(functools.partial(next_v_kernel, items, share, bool(before...  3.24 us
  transfers between devices with their start and end apart: 21, of which 12 were waited for; matrix products, arithmetic and copies ran while one was open for 0% of the time, Pallas kernels for 32%

profile of v17, /device:TPU:0, one launch (start us, length us, event | category | flops | bytes accessed | tf_op | source)
XLA Modules:
  0.0 94.5 jit_solution(8863847666388843808)
XLA Ops:
  0.6 5.8 %copy-done = bf16[32,256,1024]{2,1,0:T(8,128)(2,1)S(1)} copy-done((bf16[32,256,1024]{2,1,0:T(8,128)(2,1)S(1)}, bf16[32,256,1024]{2,1,0:T(8,128)(2,1)}, u32[]{:S(2)}) %copy-start) | copy-done | bytes 16777240
  7.3 1.6 %project_next.4 = s16[560,256]{1,0:T(8,128)(2,1)S(1)} custom-call(s32[1]{0:T(128)} %bitcast.place, bf16[64,1024]{1,0:T(8,128)(2,1)S(1)} %bitcast.16, bf16[4,8,256,1024]{3,2,1,0:T(8,128)(2,1)S(1)} %bitcast.5), custom_call_target="tpu_custom_call" | custom-call | flops 1000 | bytes 1000 | tf_op jit(solution)/shard_map/project_next/pallas_call | solution.py:196
  9.0 3.1 %collective-permute-start.3 = (s16[560,256]{1,0:T(8,128)(2,1)S(1)}, s16[560,256]{1,0:T(8,128)(2,1)S(1)}, u32[]{:S(2)}, u32[]{:S(2)}) collective-permute-start(s16[560,256]{1,0:T(8,128)(2,1)S(1)} %project_next.4), channel_id=1, source_target_pairs={{0,1},{1,0},{2,3},{3,2},{4,5},{5,4},{6,7},{7,6},{8,9},{9,8},{10,11... | collective-permute-start | bytes 860168 | tf_op jit(solution)/shard_map/ppermute | solution.py:621
  12.0 3.6 %project_first.1 = s16[528,256]{1,0:T(8,128)(2,1)S(1)} custom-call(s32[1]{0:T(128)} %bitcast.place, bf16[64,1024]{1,0:T(8,128)(2,1)} %bitcast.15, bf16[4,8,256,1024]{3,2,1,0:T(8,128)(2,1)} %bitcast.4), custom_call_target="tpu_custom_call" | custom-call | flops 1000 | bytes 1000 | tf_op jit(solution)/shard_map/project_first/pallas_call | solution.py:158
  18.5 1.9 %collective-permute-start.4 = (f32[64,64]{1,0:T(8,128)S(1)}, f32[64,64]{1,0:T(8,128)S(1)}, u32[]{:S(2)}, u32[]{:S(2)}) collective-permute-start(f32[64,64]{1,0:T(8,128)S(1)} %add_terms.5.refs_1_.refs_0_), channel_id=1, source_target_pairs={{0,8},{4,12},{8,0},{12,4},{1,9},{5,13},{9,1},{13,5},{2,10},{6,14},... | collective-permute-start | bytes 49160 | tf_op jit(solution)/shard_map/ppermute | solution.py:621
  21.9 2.8 %collective-permute-done.refs_0_ = s16[528,256]{1,0:T(8,128)(2,1)S(1)} collective-permute-done((s16[528,256]{1,0:T(8,128)(2,1)S(1)}, s16[528,256]{1,0:T(8,128)(2,1)S(1)}, u32[]{:S(2)}, u32[]{:S(2)}) %collective-permute-start) | collective-permute-done | bytes 270368 | tf_op jit(solution)/shard_map/ppermute | solution.py:621
  25.6 2.8 %collective-permute-start.2 = (s16[272,256]{1,0:T(8,128)(2,1)S(1)}, s16[272,256]{1,0:T(8,128)(2,1)S(1)}, u32[]{:S(2)}, u32[]{:S(2)}) collective-permute-start(s16[272,256]{1,0:T(8,128)(2,1)S(1)} %project_next.3), channel_id=1, source_target_pairs={{0,2},{1,3},{2,0},{3,1},{4,6},{5,7},{6,4},{7,5},{8,10},{9,11},{10,... | collective-permute-start | bytes 417800 | tf_op jit(solution)/shard_map/ppermute | solution.py:621
  29.6 9.1 %collective-permute-done.2.refs_1_ = s16[272,256]{1,0:T(8,128)(2,1)S(1)} collective-permute-done((s16[272,256]{1,0:T(8,128)(2,1)S(1)}, s16[272,256]{1,0:T(8,128)(2,1)S(1)}, u32[]{:S(2)}, u32[]{:S(2)}) %collective-permute-start.2) | collective-permute-done | bytes 139296 | tf_op jit(solution)/shard_map/ppermute | solution.py:621
  38.7 6.0 %own_frames.2 = (bf16[4,64,256]{2,1,0:T(8,128)(2,1)S(1)}, f32[64,64]{1,0:T(8,128)S(1)}, f32[64,64]{1,0:T(8,128)S(1)}) custom-call(s32[1]{0:T(128)} %bitcast.place, s32[32]{0:T(128)S(1)} %copy-done.5, f32[64,64]{1,0:T(8,128)S(1)} %copy-done.4, f32[32,64]{1,0:T(8,128)S(1)} %copy-done.3, f32[64,64]{1,0:T(8,128)S(1)} %get-tuple-element.43.v_gram_ref.before_ref.refs_2_, ...), custom_call_target="tpu_custom_call" | custom-call | flops 1000 | bytes 1000 | tf_op jit(solution)/shard_map/own_frames/pallas_call | solution.py:389
  44.8 6.0 %own_frames.3 = (bf16[4,64,256]{2,1,0:T(8,128)(2,1)S(1)}, f32[64,64]{1,0:T(8,128)S(1)}, f32[64,64]{1,0:T(8,128)S(1)}) custom-call(s32[1]{0:T(128)} %bitcast.place, s32[32]{0:T(128)S(1)} %copy-done.5, f32[64,64]{1,0:T(8,128)S(1)} %copy-done.4, f32[32,64]{1,0:T(8,128)S(1)} %copy-done.3, f32[64,64]{1,0:T(8,128)S(1)} %get-tuple-element.46.v_gram_ref, ...), custom_call_target="tpu_custom_call" | custom-call | flops 1000 | bytes 1000 | tf_op jit(solution)/shard_map/own_frames/pallas_call | solution.py:389
  50.7 3.0 %collective-permute-start.10 = (bf16[4,64,256]{2,1,0:T(8,128)(2,1)S(1)}, bf16[4,64,256]{2,1,0:T(8,128)(2,1)S(1)}, u32[]{:S(2)}, u32[]{:S(2)}) collective-permute-start(bf16[4,64,256]{2,1,0:T(8,128)(2,1)S(1)} %get-tuple-element.51.refs_2_.refs_1_.refs_0_), channel_id=1, source_target_pairs={{0,2},{1,3},{2,0},{3,1},{4,6},{5,7},{6,4},{7,5},{8,10},{9,11},{10,... | collective-permute-start | bytes 393224 | tf_op jit(solution)/shard_map/ppermute | solution.py:621
  55.5 1.7 %first_inverse.1 = (f32[64,64]{1,0:T(8,128)S(1)}, f32[64,64]{1,0:T(8,128)S(1)}) custom-call(f32[64,64]{1,0:T(8,128)S(1)} %get-tuple-element.53.v_gram_ref, f32[64,64]{1,0:T(8,128)S(1)} %add_terms.5.refs_1_.refs_0_, f32[64,64]{1,0:T(8,128)S(1)} %collective-permute-done.4.refs_1_, f32[64,64]{1,0:T(8,128)S(1)} %add_terms.6.refs_2_.a_ref), custom_call_target="tpu_custom_call" | custom-call | flops 1000 | bytes 1000 | tf_op jit(solution)/shard_map/first_inverse/pallas_call | solution.py:316
  58.2 3.1 %collective-permute-start.14 = (bf16[8,64,256]{2,1,0:T(8,128)(2,1)S(1)}, bf16[8,64,256]{2,1,0:T(8,128)(2,1)S(1)}, u32[]{:S(2)}, u32[]{:S(2)}) collective-permute-start(bf16[8,64,256]{2,1,0:T(8,128)(2,1)S(1)} %join_frames.3.refs_1_), channel_id=1, source_target_pairs={{0,1},{1,0},{2,3},{3,2},{4,5},{5,4},{6,7},{7,6},{8,9},{9,8},{10,11... | collective-permute-start | bytes 786440 | tf_op jit(solution)/shard_map/ppermute | solution.py:621
  61.4 1.5 %collective-permute-start.8 = (f32[64,64]{1,0:T(8,128)S(1)}, f32[64,64]{1,0:T(8,128)S(1)}, u32[]{:S(2)}, u32[]{:S(2)}) collective-permute-start(f32[64,64]{1,0:T(8,128)S(1)} %add_terms.6.refs_2_.a_ref), channel_id=1, source_target_pairs={{0,8},{4,12},{8,0},{12,4},{1,9},{5,13},{9,1},{13,5},{2,10},{6,14},... | collective-permute-start | bytes 49160 | tf_op jit(solution)/shard_map/ppermute | solution.py:621
  65.3 2.6 %collective-permute-start.13 = (f32[64,64]{1,0:T(8,128)S(1)}, f32[64,64]{1,0:T(8,128)S(1)}, u32[]{:S(2)}, u32[]{:S(2)}) collective-permute-start(f32[64,64]{1,0:T(8,128)S(1)} %add_terms.7.refs_1_.refs_0_), channel_id=1, source_target_pairs={{0,3},{1,2},{2,1},{3,0},{4,7},{5,6},{6,5},{7,4},{8,11},{9,10},{10,... | collective-permute-start | bytes 49160 | tf_op jit(solution)/shard_map/ppermute | solution.py:621
  68.1 1.6 %collective-permute-start.11 = (f32[64,64]{1,0:T(8,128)S(1)}, f32[64,64]{1,0:T(8,128)S(1)}, u32[]{:S(2)}, u32[]{:S(2)}) collective-permute-start(f32[64,64]{1,0:T(8,128)S(1)} %add_terms.7.refs_1_.refs_0_), channel_id=1, source_target_pairs={{0,1},{1,0},{2,3},{3,2},{4,5},{5,4},{6,7},{7,6},{8,9},{9,8},{10,11... | collective-permute-start | bytes 49160 | tf_op jit(solution)/shard_map/ppermute | solution.py:621
  71.5 1.5 %collective-permute-done.12.refs_2_ = f32[64,64]{1,0:T(8,128)S(1)} collective-permute-done((f32[64,64]{1,0:T(8,128)S(1)}, f32[64,64]{1,0:T(8,128)S(1)}, u32[]{:S(2)}, u32[]{:S(2)}) %collective-permute-start.12) | collective-permute-done | bytes 16416 | tf_op jit(solution)/shard_map/ppermute | solution.py:621
  77.0 1.7 %second_inverse.1 = (f32[64,64]{1,0:T(8,128)S(1)}, f32[64,64]{1,0:T(8,128)S(1)}) custom-call(f32[64,64]{1,0:T(8,128)S(1)} %get-tuple-element.73.h_ref, f32[64,64]{1,0:T(8,128)S(1)} %get-tuple-element.74.w_gram_ref), custom_call_target="tpu_custom_call" | custom-call | flops 1000 | bytes 1000 | tf_op jit(solution)/shard_map/second_inverse/pallas_call | solution.py:495
  78.7 3.0 %collective-permute-done.16.b_ref = f32[64,512]{1,0:T(8,128)S(1)} collective-permute-done((f32[64,512]{1,0:T(8,128)S(1)}, f32[64,512]{1,0:T(8,128)S(1)}, u32[]{:S(2)}, u32[]{:S(2)}) %collective-permute-start.16) | collective-permute-done | bytes 131104 | tf_op jit(solution)/shard_map/ppermute | solution.py:621
  81.8 1.6 %next_v.2 = (f32[64,512]{1,0:T(8,128)S(1)}, f32[64,128]{1,0:T(8,128)S(1)}) custom-call(s32[1]{0:T(128)} %bitcast.place, f32[64,512]{1,0:T(8,128)S(1)} %add_terms.9.terms_ref, f32[64,64]{1,0:T(8,128)S(1)} %get-tuple-element.75.refs_0_.inverse_ref, f32[64,64]{1,0:T(8,128)S(1)} %get-tuple-element.73.h_ref, bf16[256,1024]{1,0:T(8,128)(2,1)S(1)} %get-tuple-element.61.refs_0_, ...), custom_call_target="tpu_custom_call" | custom-call | flops 1000 | bytes 1000 | tf_op jit(solution)/shard_map/next_v/pallas_call | solution.py:562
  83.5 1.6 %next_v.3 = (f32[64,512]{1,0:T(8,128)S(1)}, f32[64,128]{1,0:T(8,128)S(1)}) custom-call(s32[1]{0:T(128)} %bitcast.place, f32[64,512]{1,0:T(8,128)S(1)} %collective-permute-done.17.terms_ref, f32[64,64]{1,0:T(8,128)S(1)} %get-tuple-element.75.refs_0_.inverse_ref, f32[64,64]{1,0:T(8,128)S(1)} %get-tuple-element.73.h_ref, ...), custom_call_target="tpu_custom_call" | custom-call | flops 1000 | bytes 1000 | tf_op jit(solution)/shard_map/next_v/pallas_call | solution.py:562
  85.1 1.7 %collective-permute-start.20 = (f32[64,128]{1,0:T(8,128)S(1)}, f32[64,128]{1,0:T(8,128)S(1)}, u32[]{:S(2)}, u32[]{:S(2)}) collective-permute-start(f32[64,128]{1,0:T(8,128)S(1)} %get-tuple-element.80.refs_0_), channel_id=1, source_target_pairs={{0,3},{1,2},{2,1},{3,0},{4,7},{5,6},{6,5},{7,4},{8,11},{9,10},{10,... | collective-permute-start | bytes 98312 | tf_op jit(solution)/shard_map/ppermute | solution.py:621
  87.1 2.4 %collective-permute-start.18 = (f32[64,128]{1,0:T(8,128)S(1)}, f32[64,128]{1,0:T(8,128)S(1)}, u32[]{:S(2)}, u32[]{:S(2)}) collective-permute-start(f32[64,128]{1,0:T(8,128)S(1)} %get-tuple-element.80.refs_0_), channel_id=1, source_target_pairs={{0,1},{1,0},{2,3},{3,2},{4,5},{5,4},{6,7},{7,6},{8,9},{9,8},{10,11... | collective-permute-start | bytes 98312 | tf_op jit(solution)/shard_map/ppermute | solution.py:621
  92.2 2.3 %next_w.1 = f32[32,64]{1,0:T(8,128)} custom-call(f32[64,128]{1,0:T(8,128)S(1)} %get-tuple-element.80.refs_0_, f32[64,128]{1,0:T(8,128)S(1)} %collective-permute-done.18.refs_1_, f32[64,128]{1,0:T(8,128)S(1)} %collective-permute-done.19.refs_2_, f32[64,128]{1,0:T(8,128)S(1)} %collective-permute-done.20.refs_3_, f32[64,64]{1,0:T(8,128)S(1)} %get-tuple-element.81.refs_4_, ...), custom_call_target="tpu_custom_call" | custom-call | flops 1000 | bytes 1000 | tf_op jit(solution)/shard_map/next_w/pallas_call | solution.py:608
  (67 shorter events, 21.7 us)
Async XLA Ops:
  7.3 13.1 %copy-start.2 = (bf16[1024,64]{0,1:T(8,128)(2,1)S(1)}, bf16[1024,64]{0,1:T(8,128)(2,1)}, u32[]{:S(2)}) copy-start(bf16[1024,64]{0,1:T(8,128)(2,1)} %param.8) | copy-start | bytes 393220
  9.0 19.4 %collective-permute-start.3 = (s16[560,256]{1,0:T(8,128)(2,1)S(1)}, s16[560,256]{1,0:T(8,128)(2,1)S(1)}, u32[]{:S(2)}, u32[]{:S(2)}) collective-permute-start(s16[560,256]{1,0:T(8,128)(2,1)S(1)} %project_next.4), channel_id=1, source_target_pairs={{0,1},{1,0},{2,3},{3,2},{4,5},{5,4},{6,7},{7,6},{8,9},{9,8},{10,11... | collective-permute-start | bytes 860168 | tf_op jit(solution)/shard_map/ppermute | solution.py:621
  15.7 9.0 %collective-permute-start = (s16[528,256]{1,0:T(8,128)(2,1)S(1)}, s16[528,256]{1,0:T(8,128)(2,1)S(1)}, u32[]{:S(2)}, u32[]{:S(2)}) collective-permute-start(s16[528,256]{1,0:T(8,128)(2,1)S(1)} %project_first.1), channel_id=1, source_target_pairs={{0,1},{1,0},{2,3},{3,2},{4,5},{5,4},{6,7},{7,6},{8,9},{9,8},{10,11... | collective-permute-start | bytes 811016 | tf_op jit(solution)/shard_map/ppermute | solution.py:621
  17.2 1.3 %collective-permute-start.1 = (f32[64,64]{1,0:T(8,128)S(1)}, f32[64,64]{1,0:T(8,128)S(1)}, u32[]{:S(2)}, u32[]{:S(2)}) collective-permute-start(f32[64,64]{1,0:T(8,128)S(1)} %get-tuple-element.45.a_ref), channel_id=1, source_target_pairs={{0,4},{4,0},{8,12},{12,8},{1,5},{5,1},{9,13},{13,9},{2,6},{6,2},{1... | collective-permute-start | bytes 49160 | tf_op jit(solution)/shard_map/ppermute | solution.py:621
  18.5 9.9 %collective-permute-start.4 = (f32[64,64]{1,0:T(8,128)S(1)}, f32[64,64]{1,0:T(8,128)S(1)}, u32[]{:S(2)}, u32[]{:S(2)}) collective-permute-start(f32[64,64]{1,0:T(8,128)S(1)} %add_terms.5.refs_1_.refs_0_), channel_id=1, source_target_pairs={{0,8},{4,12},{8,0},{12,4},{1,9},{5,13},{9,1},{13,5},{2,10},{6,14},... | collective-permute-start | bytes 49160 | tf_op jit(solution)/shard_map/ppermute | solution.py:621
  21.9 16.9 %copy-start.4 = (f32[64,64]{1,0:T(8,128)S(1)}, f32[64,64]{1,0:T(8,128)}, u32[]{:S(2)}) copy-start(f32[64,64]{1,0:T(8,128)} %h_ref.3) | copy-start | bytes 49156
  21.9 16.8 %copy-start.5 = (s32[32]{0:T(128)S(1)}, s32[32]{0:T(128)}, u32[]{:S(2)}) copy-start(s32[32]{0:T(128)} %counts_ref.3) | copy-start | bytes 388
  25.6 13.1 %collective-permute-start.2 = (s16[272,256]{1,0:T(8,128)(2,1)S(1)}, s16[272,256]{1,0:T(8,128)(2,1)S(1)}, u32[]{:S(2)}, u32[]{:S(2)}) collective-permute-start(s16[272,256]{1,0:T(8,128)(2,1)S(1)} %project_next.3), channel_id=1, source_target_pairs={{0,2},{1,3},{2,0},{3,1},{4,6},{5,7},{6,4},{7,5},{8,10},{9,11},{10,... | collective-permute-start | bytes 417800 | tf_op jit(solution)/shard_map/ppermute | solution.py:621
  29.4 15.3 %collective-permute-start.5 = (s16[304,256]{1,0:T(8,128)(2,1)S(1)}, s16[304,256]{1,0:T(8,128)(2,1)S(1)}, u32[]{:S(2)}, u32[]{:S(2)}) collective-permute-start(s16[304,256]{1,0:T(8,128)(2,1)S(1)} %project_next.5), channel_id=1, source_target_pairs={{0,2},{1,3},{2,0},{3,1},{4,6},{5,7},{6,4},{7,5},{8,10},{9,11},{10,... | collective-permute-start | bytes 466952 | tf_op jit(solution)/shard_map/ppermute | solution.py:621
  44.7 9.0 %collective-permute-start.7 = (bf16[4,64,256]{2,1,0:T(8,128)(2,1)S(1)}, bf16[4,64,256]{2,1,0:T(8,128)(2,1)S(1)}, u32[]{:S(2)}, u32[]{:S(2)}) collective-permute-start(bf16[4,64,256]{2,1,0:T(8,128)(2,1)S(1)} %get-tuple-element.50.refs_0_), channel_id=1, source_target_pairs={{0,2},{1,3},{2,0},{3,1},{4,6},{5,7},{6,4},{7,5},{8,10},{9,11},{10,... | collective-permute-start | bytes 393224 | tf_op jit(solution)/shard_map/ppermute | solution.py:621
  50.7 7.5 %collective-permute-start.10 = (bf16[4,64,256]{2,1,0:T(8,128)(2,1)S(1)}, bf16[4,64,256]{2,1,0:T(8,128)(2,1)S(1)}, u32[]{:S(2)}, u32[]{:S(2)}) collective-permute-start(bf16[4,64,256]{2,1,0:T(8,128)(2,1)S(1)} %get-tuple-element.51.refs_2_.refs_1_.refs_0_), channel_id=1, source_target_pairs={{0,2},{1,3},{2,0},{3,1},{4,6},{5,7},{6,4},{7,5},{8,10},{9,11},{10,... | collective-permute-start | bytes 393224 | tf_op jit(solution)/shard_map/ppermute | solution.py:621
  53.7 1.8 %collective-permute-start.6 = (f32[64,64]{1,0:T(8,128)S(1)}, f32[64,64]{1,0:T(8,128)S(1)}, u32[]{:S(2)}, u32[]{:S(2)}) collective-permute-start(f32[64,64]{1,0:T(8,128)S(1)} %get-tuple-element.49.a_ref), channel_id=1, source_target_pairs={{0,4},{4,0},{8,12},{12,8},{1,5},{5,1},{9,13},{13,9},{2,6},{6,2},{1... | collective-permute-start | bytes 49160 | tf_op jit(solution)/shard_map/ppermute | solution.py:621
  53.7 9.5 %collective-permute-start.9 = (bf16[8,64,256]{2,1,0:T(8,128)(2,1)S(1)}, bf16[8,64,256]{2,1,0:T(8,128)(2,1)S(1)}, u32[]{:S(2)}, u32[]{:S(2)}) collective-permute-start(bf16[8,64,256]{2,1,0:T(8,128)(2,1)S(1)} %join_frames.2.refs_3_), channel_id=1, source_target_pairs={{0,1},{1,0},{2,3},{3,2},{4,5},{5,4},{6,7},{7,6},{8,9},{9,8},{10,11... | collective-permute-start | bytes 786440 | tf_op jit(solution)/shard_map/ppermute | solution.py:621
  58.2 11.9 %collective-permute-start.14 = (bf16[8,64,256]{2,1,0:T(8,128)(2,1)S(1)}, bf16[8,64,256]{2,1,0:T(8,128)(2,1)S(1)}, u32[]{:S(2)}, u32[]{:S(2)}) collective-permute-start(bf16[8,64,256]{2,1,0:T(8,128)(2,1)S(1)} %join_frames.3.refs_1_), channel_id=1, source_target_pairs={{0,1},{1,0},{2,3},{3,2},{4,5},{5,4},{6,7},{7,6},{8,9},{9,8},{10,11... | collective-permute-start | bytes 786440 | tf_op jit(solution)/shard_map/ppermute | solution.py:621
  61.4 3.9 %collective-permute-start.8 = (f32[64,64]{1,0:T(8,128)S(1)}, f32[64,64]{1,0:T(8,128)S(1)}, u32[]{:S(2)}, u32[]{:S(2)}) collective-permute-start(f32[64,64]{1,0:T(8,128)S(1)} %add_terms.6.refs_2_.a_ref), channel_id=1, source_target_pairs={{0,8},{4,12},{8,0},{12,4},{1,9},{5,13},{9,1},{13,5},{2,10},{6,14},... | collective-permute-start | bytes 49160 | tf_op jit(solution)/shard_map/ppermute | solution.py:621
  65.3 6.2 %collective-permute-start.13 = (f32[64,64]{1,0:T(8,128)S(1)}, f32[64,64]{1,0:T(8,128)S(1)}, u32[]{:S(2)}, u32[]{:S(2)}) collective-permute-start(f32[64,64]{1,0:T(8,128)S(1)} %add_terms.7.refs_1_.refs_0_), channel_id=1, source_target_pairs={{0,3},{1,2},{2,1},{3,0},{4,7},{5,6},{6,5},{7,4},{8,11},{9,10},{10,... | collective-permute-start | bytes 49160 | tf_op jit(solution)/shard_map/ppermute | solution.py:621
  67.9 5.1 %collective-permute-start.12 = (f32[64,64]{1,0:T(8,128)S(1)}, f32[64,64]{1,0:T(8,128)S(1)}, u32[]{:S(2)}, u32[]{:S(2)}) collective-permute-start(f32[64,64]{1,0:T(8,128)S(1)} %add_terms.7.refs_1_.refs_0_), channel_id=1, source_target_pairs={{0,2},{1,3},{2,0},{3,1},{4,6},{5,7},{6,4},{7,5},{8,10},{9,11},{10,... | collective-permute-start | bytes 49160 | tf_op jit(solution)/shard_map/ppermute | solution.py:621
  68.1 4.9 %collective-permute-start.11 = (f32[64,64]{1,0:T(8,128)S(1)}, f32[64,64]{1,0:T(8,128)S(1)}, u32[]{:S(2)}, u32[]{:S(2)}) collective-permute-start(f32[64,64]{1,0:T(8,128)S(1)} %add_terms.7.refs_1_.refs_0_), channel_id=1, source_target_pairs={{0,1},{1,0},{2,3},{3,2},{4,5},{5,4},{6,7},{7,6},{8,9},{9,8},{10,11... | collective-permute-start | bytes 49160 | tf_op jit(solution)/shard_map/ppermute | solution.py:621
  74.7 1.4 %collective-permute-start.15 = (f32[64,512]{1,0:T(8,128)S(1)}, f32[64,512]{1,0:T(8,128)S(1)}, u32[]{:S(2)}, u32[]{:S(2)}) collective-permute-start(f32[64,512]{1,0:T(8,128)S(1)} %v_terms.2.refs_12_), channel_id=1, source_target_pairs={{0,4},{4,0},{8,12},{12,8},{1,5},{5,1},{9,13},{13,9},{2,6},{6,2},{1... | collective-permute-start | bytes 393224 | tf_op jit(solution)/shard_map/ppermute | solution.py:621
  76.1 5.6 %collective-permute-start.16 = (f32[64,512]{1,0:T(8,128)S(1)}, f32[64,512]{1,0:T(8,128)S(1)}, u32[]{:S(2)}, u32[]{:S(2)}) collective-permute-start(f32[64,512]{1,0:T(8,128)S(1)} %add_terms.8.a_ref), channel_id=1, source_target_pairs={{0,8},{4,12},{8,0},{12,4},{1,9},{5,13},{9,1},{13,5},{2,10},{6,14},... | collective-permute-start | bytes 393224 | tf_op jit(solution)/shard_map/ppermute | solution.py:621
  81.8 1.7 %collective-permute-start.17 = (f32[64,512]{1,0:T(8,128)S(1)}, f32[64,512]{1,0:T(8,128)S(1)}, u32[]{:S(2)}, u32[]{:S(2)}) collective-permute-start(f32[64,512]{1,0:T(8,128)S(1)} %add_terms.9.terms_ref), channel_id=1, source_target_pairs={{0,4},{4,0},{8,12},{12,8},{1,5},{5,1},{9,13},{13,9},{2,6},{6,2},{1... | collective-permute-start | bytes 393224 | tf_op jit(solution)/shard_map/ppermute | solution.py:621
  85.1 6.1 %collective-permute-start.20 = (f32[64,128]{1,0:T(8,128)S(1)}, f32[64,128]{1,0:T(8,128)S(1)}, u32[]{:S(2)}, u32[]{:S(2)}) collective-permute-start(f32[64,128]{1,0:T(8,128)S(1)} %get-tuple-element.80.refs_0_), channel_id=1, source_target_pairs={{0,3},{1,2},{2,1},{3,0},{4,7},{5,6},{6,5},{7,4},{8,11},{9,10},{10,... | collective-permute-start | bytes 98312 | tf_op jit(solution)/shard_map/ppermute | solution.py:621
  86.8 5.5 %collective-permute-start.19 = (f32[64,128]{1,0:T(8,128)S(1)}, f32[64,128]{1,0:T(8,128)S(1)}, u32[]{:S(2)}, u32[]{:S(2)}) collective-permute-start(f32[64,128]{1,0:T(8,128)S(1)} %get-tuple-element.80.refs_0_), channel_id=1, source_target_pairs={{0,2},{1,3},{2,0},{3,1},{4,6},{5,7},{6,4},{7,5},{8,10},{9,11},{10,... | collective-permute-start | bytes 98312 | tf_op jit(solution)/shard_map/ppermute | solution.py:621
  87.1 5.1 %collective-permute-start.18 = (f32[64,128]{1,0:T(8,128)S(1)}, f32[64,128]{1,0:T(8,128)S(1)}, u32[]{:S(2)}, u32[]{:S(2)}) collective-permute-start(f32[64,128]{1,0:T(8,128)S(1)} %get-tuple-element.80.refs_0_), channel_id=1, source_target_pairs={{0,1},{1,0},{2,3},{3,2},{4,5},{5,4},{6,7},{7,6},{8,9},{9,8},{10,11... | collective-permute-start | bytes 98312 | tf_op jit(solution)/shard_map/ppermute | solution.py:621
  (7 other events, 64.7 us)

commit v18 on v17

--- a/solution.py
+++ b/solution.py
@@ -729,16 +729,15 @@
     projected, token = project_groups(first_groups, joined)
     h_sums = staged_terms(h_local, "patient", [token])
     w_gram, inverse = first_inverse(v_gram, w_grams, h_sums[0])
-    after = double(n_parts - 1, [inverse])
-    if early:
-        more, token = project_groups(early, after)
-        projected |= more
-        after = [token]
-    h_sum = add(*h_sums, after)
+    h_sum = add(*h_sums, [inverse])
+    joined = double(n_parts - 1, [h_sum] + [frames[part][k][1] for part, k in early])
     h_terms = all_terms(h_sum, "feature")
-    for k in range(1, last + 1):
-        more, token = project_groups([(n_parts - 1, k)], [h_sum] if k == 1 else [token])
-        projected |= more
+    after = joined
+    for groups in [early] + [[(n_parts - 1, k)] for k in range(1, last + 1)]:
+        if groups:
+            more, token = project_groups(groups, after)
+            projected |= more
+            after = [token]
     h_result, h_next, factor = next_h(h_terms, inverse, spread, token)
 
     items = list(projected)

time: 94.7 us -> 81.2 us (0.86)
  waiting for transfers between devices: 23.1 us -> 12.2 us
  local copies, waits for them, and re-layouts: 6.7 us -> 0.36 us
  starting transfers between devices: 26.7 us -> 30.5 us
    ppermute x21, waiting for transfers between devices: 23.1 us -> 12.2 us  [swap(): return lax.ppermute(x, axis, pairs)]
    unnamed x20 -> x10, local copies, waits for them, and re-layouts: 6.7 us -> 0.36 us
    ppermute x21, starting transfers between devices: 26.7 us -> 30.5 us  [swap(): return lax.ppermute(x, axis, pairs)]
  transfers between devices with their start and end apart: 21 -> 21, of which waited for: 12 -> 12; matrix products, arithmetic and copies ran while one was open for 0% -> 0% of each run, Pallas kernels for 32% -> 34%
where the time goes in v18:
time: 81.2 us; the launch traced here: 81.1 us
  Pallas kernels  37.2 us (46%)
  starting transfers between devices  30.5 us (38%)
  waiting for transfers between devices  12.2 us (15%)
  between operations  0.84 us (1%)
    ppermute x21, starting transfers between devices, swap(): return lax.ppermute(x, axis, pairs)  30.5 us
    ppermute x21, waiting for transfers between devices, swap(): return lax.ppermute(x, axis, pairs)  12.2 us
    pallas_call x2, Pallas kernels, own_frames(): pl.pallas_call(functools.partial(frames_kernel, layouts, part, share), in...  11.9 us
    pallas_call x1, Pallas kernels, first_projection(): pl.pallas_call(functools.partial(first_projection_kernel, slots, with_gra...  3.73 us
    pallas_call x3, Pallas kernels, next_projection(): pl.pallas_call(functools.partial(next_projection_kernel, slots, first, co...  3.56 us
    pallas_call x4, Pallas kernels, project_frames(): pl.pallas_call(functools.partial(projected_kernel, items), in_specs=[SMEM...  3.49 us
    pallas_call x2, Pallas kernels, half_v(): pl.pallas_call(functools.partial(next_v_kernel, items, share, bool(before...  3.25 us
    pallas_call x1, Pallas kernels, next_w(): pl.pallas_call(functools.partial(next_w_kernel, len(sums)), in_specs=[VME...  2.27 us
  transfers between devices with their start and end apart: 21, of which 12 were waited for; matrix products, arithmetic and copies ran while one was open for 0% of the time, Pallas kernels for 34%

profile of v18, /device:TPU:0, one launch (start us, length us, event | category | flops | bytes accessed | tf_op | source)
XLA Modules:
  0.0 81.1 jit_solution(3028121208039269561)
XLA Ops:
  0.7 3.7 %project_first.1 = s16[528,256]{1,0:T(8,128)(2,1)S(1)} custom-call(s32[1]{0:T(128)} %bitcast.place, bf16[64,1024]{1,0:T(8,128)(2,1)} %bitcast.13, bf16[4,8,256,1024]{3,2,1,0:T(8,128)(2,1)} %bitcast.4), custom_call_target="tpu_custom_call" | custom-call | flops 1000 | bytes 1000 | tf_op jit(solution)/shard_map/project_first/pallas_call | solution.py:158
  4.4 3.0 %collective-permute-start = (s16[528,256]{1,0:T(8,128)(2,1)S(1)}, s16[528,256]{1,0:T(8,128)(2,1)S(1)}, u32[]{:S(2)}, u32[]{:S(2)}) collective-permute-start(s16[528,256]{1,0:T(8,128)(2,1)S(1)} %project_first.1), channel_id=1, source_target_pairs={{0,1},{1,0},{2,3},{3,2},{4,5},{5,4},{6,7},{7,6},{8,9},{9,8},{10,11... | collective-permute-start | bytes 811016 | tf_op jit(solution)/shard_map/ppermute | solution.py:621
  7.8 1.6 %project_next.4 = s16[560,256]{1,0:T(8,128)(2,1)S(1)} custom-call(s32[1]{0:T(128)} %bitcast.place, bf16[64,1024]{1,0:T(8,128)(2,1)S(1)} %bitcast.14, bf16[4,8,256,1024]{3,2,1,0:T(8,128)(2,1)S(1)} %bitcast.5), custom_call_target="tpu_custom_call" | custom-call | flops 1000 | bytes 1000 | tf_op jit(solution)/shard_map/project_next/pallas_call | solution.py:196
  9.4 3.0 %collective-permute-start.3 = (s16[560,256]{1,0:T(8,128)(2,1)S(1)}, s16[560,256]{1,0:T(8,128)(2,1)S(1)}, u32[]{:S(2)}, u32[]{:S(2)}) collective-permute-start(s16[560,256]{1,0:T(8,128)(2,1)S(1)} %project_next.4), channel_id=1, source_target_pairs={{0,1},{1,0},{2,3},{3,2},{4,5},{5,4},{6,7},{7,6},{8,9},{9,8},{10,11... | collective-permute-start | bytes 860168 | tf_op jit(solution)/shard_map/ppermute | solution.py:621
  15.6 3.2 %collective-permute-start.2 = (s16[272,256]{1,0:T(8,128)(2,1)S(1)}, s16[272,256]{1,0:T(8,128)(2,1)S(1)}, u32[]{:S(2)}, u32[]{:S(2)}) collective-permute-start(s16[272,256]{1,0:T(8,128)(2,1)S(1)} %project_next.3), channel_id=1, source_target_pairs={{0,2},{1,3},{2,0},{3,1},{4,6},{5,7},{6,4},{7,5},{8,10},{9,11},{10,... | collective-permute-start | bytes 417800 | tf_op jit(solution)/shard_map/ppermute | solution.py:621
  18.8 1.5 %collective-permute-start.4 = (f32[64,64]{1,0:T(8,128)S(1)}, f32[64,64]{1,0:T(8,128)S(1)}, u32[]{:S(2)}, u32[]{:S(2)}) collective-permute-start(f32[64,64]{1,0:T(8,128)S(1)} %add_terms.5.refs_1_.refs_0_), channel_id=1, source_target_pairs={{0,8},{4,12},{8,0},{12,4},{1,9},{5,13},{9,1},{13,5},{2,10},{6,14},... | collective-permute-start | bytes 49160 | tf_op jit(solution)/shard_map/ppermute | solution.py:621
  24.9 6.0 %own_frames.2 = (bf16[4,64,256]{2,1,0:T(8,128)(2,1)S(1)}, f32[64,64]{1,0:T(8,128)S(1)}, f32[64,64]{1,0:T(8,128)S(1)}) custom-call(s32[1]{0:T(128)} %bitcast.place, s32[32]{0:T(128)S(1)} %copy-done.4, f32[64,64]{1,0:T(8,128)S(1)} %copy-done.3, f32[32,64]{1,0:T(8,128)S(1)} %copy-done.2, f32[64,64]{1,0:T(8,128)S(1)} %get-tuple-element.43.v_gram_ref.before_ref.refs_2_, ...), custom_call_target="tpu_custom_call" | custom-call | flops 1000 | bytes 1000 | tf_op jit(solution)/shard_map/own_frames/pallas_call | solution.py:389
  30.9 2.1 %collective-permute-start.7 = (bf16[4,64,256]{2,1,0:T(8,128)(2,1)S(1)}, bf16[4,64,256]{2,1,0:T(8,128)(2,1)S(1)}, u32[]{:S(2)}, u32[]{:S(2)}) collective-permute-start(bf16[4,64,256]{2,1,0:T(8,128)(2,1)S(1)} %get-tuple-element.50.refs_0_), channel_id=1, source_target_pairs={{0,2},{1,3},{2,0},{3,1},{4,6},{5,7},{6,4},{7,5},{8,10},{9,11},{10,... | collective-permute-start | bytes 393224 | tf_op jit(solution)/shard_map/ppermute | solution.py:621
  33.0 6.0 %own_frames.3 = (bf16[4,64,256]{2,1,0:T(8,128)(2,1)S(1)}, f32[64,64]{1,0:T(8,128)S(1)}, f32[64,64]{1,0:T(8,128)S(1)}) custom-call(s32[1]{0:T(128)} %bitcast.place, s32[32]{0:T(128)S(1)} %copy-done.4, f32[64,64]{1,0:T(8,128)S(1)} %copy-done.3, f32[32,64]{1,0:T(8,128)S(1)} %copy-done.2, f32[64,64]{1,0:T(8,128)S(1)} %get-tuple-element.46.v_gram_ref, ...), custom_call_target="tpu_custom_call" | custom-call | flops 1000 | bytes 1000 | tf_op jit(solution)/shard_map/own_frames/pallas_call | solution.py:389
  40.6 1.6 %collective-permute-start.12 = (bf16[4,64,256]{2,1,0:T(8,128)(2,1)S(1)}, bf16[4,64,256]{2,1,0:T(8,128)(2,1)S(1)}, u32[]{:S(2)}, u32[]{:S(2)}) collective-permute-start(bf16[4,64,256]{2,1,0:T(8,128)(2,1)S(1)} %get-tuple-element.51.refs_2_.refs_1_.refs_0_), channel_id=1, source_target_pairs={{0,2},{1,3},{2,0},{3,1},{4,6},{5,7},{6,4},{7,5},{8,10},{9,11},{10,... | collective-permute-start | bytes 393224 | tf_op jit(solution)/shard_map/ppermute | solution.py:621
  43.5 1.6 %collective-permute-start.8 = (f32[64,64]{1,0:T(8,128)S(1)}, f32[64,64]{1,0:T(8,128)S(1)}, u32[]{:S(2)}, u32[]{:S(2)}) collective-permute-start(f32[64,64]{1,0:T(8,128)S(1)} %add_terms.6.refs_2_.a_ref), channel_id=1, source_target_pairs={{0,8},{4,12},{8,0},{12,4},{1,9},{5,13},{9,1},{13,5},{2,10},{6,14},... | collective-permute-start | bytes 49160 | tf_op jit(solution)/shard_map/ppermute | solution.py:621
  45.1 1.7 %first_inverse.1 = (f32[64,64]{1,0:T(8,128)S(1)}, f32[64,64]{1,0:T(8,128)S(1)}) custom-call(f32[64,64]{1,0:T(8,128)S(1)} %get-tuple-element.53.v_gram_ref, f32[64,64]{1,0:T(8,128)S(1)} %add_terms.5.refs_1_.refs_0_, f32[64,64]{1,0:T(8,128)S(1)} %collective-permute-done.4.refs_1_, f32[64,64]{1,0:T(8,128)S(1)} %add_terms.6.refs_2_.a_ref), custom_call_target="tpu_custom_call" | custom-call | flops 1000 | bytes 1000 | tf_op jit(solution)/shard_map/first_inverse/pallas_call | solution.py:316
  47.7 1.8 %collective-permute-done.13.refs_3_.refs_0_ = bf16[8,64,256]{2,1,0:T(8,128)(2,1)S(1)} collective-permute-done((bf16[8,64,256]{2,1,0:T(8,128)(2,1)S(1)}, bf16[8,64,256]{2,1,0:T(8,128)(2,1)S(1)}, u32[]{:S(2)}, u32[]{:S(2)}) %collective-permute-start.13) | collective-permute-done | bytes 262176 | tf_op jit(solution)/shard_map/ppermute | solution.py:621
  50.5 1.8 %collective-permute-start.11 = (f32[64,64]{1,0:T(8,128)S(1)}, f32[64,64]{1,0:T(8,128)S(1)}, u32[]{:S(2)}, u32[]{:S(2)}) collective-permute-start(f32[64,64]{1,0:T(8,128)S(1)} %add_terms.7.refs_2_.refs_0_), channel_id=1, source_target_pairs={{0,3},{1,2},{2,1},{3,0},{4,7},{5,6},{6,5},{7,4},{8,11},{9,10},{10,... | collective-permute-start | bytes 49160 | tf_op jit(solution)/shard_map/ppermute | solution.py:621
  53.1 1.8 %collective-permute-start.9 = (f32[64,64]{1,0:T(8,128)S(1)}, f32[64,64]{1,0:T(8,128)S(1)}, u32[]{:S(2)}, u32[]{:S(2)}) collective-permute-start(f32[64,64]{1,0:T(8,128)S(1)} %add_terms.7.refs_2_.refs_0_), channel_id=1, source_target_pairs={{0,1},{1,0},{2,3},{3,2},{4,5},{5,4},{6,7},{7,6},{8,9},{9,8},{10,11... | collective-permute-start | bytes 49160 | tf_op jit(solution)/shard_map/ppermute | solution.py:621
  56.3 1.9 %collective-permute-done.14.refs_0_ = bf16[8,64,256]{2,1,0:T(8,128)(2,1)S(1)} collective-permute-done((bf16[8,64,256]{2,1,0:T(8,128)(2,1)S(1)}, bf16[8,64,256]{2,1,0:T(8,128)(2,1)S(1)}, u32[]{:S(2)}, u32[]{:S(2)}) %collective-permute-start.14) | collective-permute-done | bytes 262176 | tf_op jit(solution)/shard_map/ppermute | solution.py:621
  62.2 2.4 %collective-permute-start.16 = (f32[64,512]{1,0:T(8,128)S(1)}, f32[64,512]{1,0:T(8,128)S(1)}, u32[]{:S(2)}, u32[]{:S(2)}) collective-permute-start(f32[64,512]{1,0:T(8,128)S(1)} %add_terms.8.a_ref), channel_id=1, source_target_pairs={{0,8},{4,12},{8,0},{12,4},{1,9},{5,13},{9,1},{13,5},{2,10},{6,14},... | collective-permute-start | bytes 393224 | tf_op jit(solution)/shard_map/ppermute | solution.py:621
  64.6 1.7 %second_inverse.1 = (f32[64,64]{1,0:T(8,128)S(1)}, f32[64,64]{1,0:T(8,128)S(1)}) custom-call(f32[64,64]{1,0:T(8,128)S(1)} %get-tuple-element.73.h_ref, f32[64,64]{1,0:T(8,128)S(1)} %get-tuple-element.74.w_gram_ref), custom_call_target="tpu_custom_call" | custom-call | flops 1000 | bytes 1000 | tf_op jit(solution)/shard_map/second_inverse/pallas_call | solution.py:495
  66.3 2.1 %collective-permute-done.16.b_ref = f32[64,512]{1,0:T(8,128)S(1)} collective-permute-done((f32[64,512]{1,0:T(8,128)S(1)}, f32[64,512]{1,0:T(8,128)S(1)}, u32[]{:S(2)}, u32[]{:S(2)}) %collective-permute-start.16) | collective-permute-done | bytes 131104 | tf_op jit(solution)/shard_map/ppermute | solution.py:621
  68.5 1.6 %next_v.2 = (f32[64,512]{1,0:T(8,128)S(1)}, f32[64,128]{1,0:T(8,128)S(1)}) custom-call(s32[1]{0:T(128)} %bitcast.place, f32[64,512]{1,0:T(8,128)S(1)} %add_terms.9.terms_ref, f32[64,64]{1,0:T(8,128)S(1)} %get-tuple-element.75.refs_0_.inverse_ref, f32[64,64]{1,0:T(8,128)S(1)} %get-tuple-element.73.h_ref, bf16[256,1024]{1,0:T(8,128)(2,1)S(1)} %get-tuple-element.61.refs_0_, ...), custom_call_target="tpu_custom_call" | custom-call | flops 1000 | bytes 1000 | tf_op jit(solution)/shard_map/next_v/pallas_call | solution.py:562
  70.2 1.6 %next_v.3 = (f32[64,512]{1,0:T(8,128)S(1)}, f32[64,128]{1,0:T(8,128)S(1)}) custom-call(s32[1]{0:T(128)} %bitcast.place, f32[64,512]{1,0:T(8,128)S(1)} %collective-permute-done.17.terms_ref, f32[64,64]{1,0:T(8,128)S(1)} %get-tuple-element.75.refs_0_.inverse_ref, f32[64,64]{1,0:T(8,128)S(1)} %get-tuple-element.73.h_ref, ...), custom_call_target="tpu_custom_call" | custom-call | flops 1000 | bytes 1000 | tf_op jit(solution)/shard_map/next_v/pallas_call | solution.py:562
  71.8 1.9 %collective-permute-start.20 = (f32[64,128]{1,0:T(8,128)S(1)}, f32[64,128]{1,0:T(8,128)S(1)}, u32[]{:S(2)}, u32[]{:S(2)}) collective-permute-start(f32[64,128]{1,0:T(8,128)S(1)} %get-tuple-element.80.refs_0_), channel_id=1, source_target_pairs={{0,3},{1,2},{2,1},{3,0},{4,7},{5,6},{6,5},{7,4},{8,11},{9,10},{10,... | collective-permute-start | bytes 98312 | tf_op jit(solution)/shard_map/ppermute | solution.py:621
  73.7 2.5 %collective-permute-start.18 = (f32[64,128]{1,0:T(8,128)S(1)}, f32[64,128]{1,0:T(8,128)S(1)}, u32[]{:S(2)}, u32[]{:S(2)}) collective-permute-start(f32[64,128]{1,0:T(8,128)S(1)} %get-tuple-element.80.refs_0_), channel_id=1, source_target_pairs={{0,1},{1,0},{2,3},{3,2},{4,5},{5,4},{6,7},{7,6},{8,9},{9,8},{10,11... | collective-permute-start | bytes 98312 | tf_op jit(solution)/shard_map/ppermute | solution.py:621
  78.8 2.3 %next_w.1 = f32[32,64]{1,0:T(8,128)} custom-call(f32[64,128]{1,0:T(8,128)S(1)} %get-tuple-element.80.refs_0_, f32[64,128]{1,0:T(8,128)S(1)} %collective-permute-done.18.refs_1_, f32[64,128]{1,0:T(8,128)S(1)} %collective-permute-done.19.refs_2_, f32[64,128]{1,0:T(8,128)S(1)} %collective-permute-done.20.refs_3_, f32[64,64]{1,0:T(8,128)S(1)} %get-tuple-element.81.refs_4_, ...), custom_call_target="tpu_custom_call" | custom-call | flops 1000 | bytes 1000 | tf_op jit(solution)/shard_map/next_w/pallas_call | solution.py:608
  (56 shorter events, 21.7 us)
Async XLA Ops:
  0.7 11.8 %copy-start.2 = (f32[32,64]{1,0:T(8,128)S(1)}, f32[32,64]{1,0:T(8,128)}, u32[]{:S(2)}) copy-start(f32[32,64]{1,0:T(8,128)} %w_ref.5) | copy-start | bytes 24580
  4.4 10.2 %collective-permute-start = (s16[528,256]{1,0:T(8,128)(2,1)S(1)}, s16[528,256]{1,0:T(8,128)(2,1)S(1)}, u32[]{:S(2)}, u32[]{:S(2)}) collective-permute-start(s16[528,256]{1,0:T(8,128)(2,1)S(1)} %project_first.1), channel_id=1, source_target_pairs={{0,1},{1,0},{2,3},{3,2},{4,5},{5,4},{6,7},{7,6},{8,9},{9,8},{10,11... | collective-permute-start | bytes 811016 | tf_op jit(solution)/shard_map/ppermute | solution.py:621
  9.4 13.6 %collective-permute-start.3 = (s16[560,256]{1,0:T(8,128)(2,1)S(1)}, s16[560,256]{1,0:T(8,128)(2,1)S(1)}, u32[]{:S(2)}, u32[]{:S(2)}) collective-permute-start(s16[560,256]{1,0:T(8,128)(2,1)S(1)} %project_next.4), channel_id=1, source_target_pairs={{0,1},{1,0},{2,3},{3,2},{4,5},{5,4},{6,7},{7,6},{8,9},{9,8},{10,11... | collective-permute-start | bytes 860168 | tf_op jit(solution)/shard_map/ppermute | solution.py:621
  13.3 1.3 %collective-permute-start.1 = (f32[64,64]{1,0:T(8,128)S(1)}, f32[64,64]{1,0:T(8,128)S(1)}, u32[]{:S(2)}, u32[]{:S(2)}) collective-permute-start(f32[64,64]{1,0:T(8,128)S(1)} %get-tuple-element.45.a_ref), channel_id=1, source_target_pairs={{0,4},{4,0},{8,12},{12,8},{1,5},{5,1},{9,13},{13,9},{2,6},{6,2},{1... | collective-permute-start | bytes 49160 | tf_op jit(solution)/shard_map/ppermute | solution.py:621
  15.6 9.4 %copy-start.3 = (f32[64,64]{1,0:T(8,128)S(1)}, f32[64,64]{1,0:T(8,128)}, u32[]{:S(2)}) copy-start(f32[64,64]{1,0:T(8,128)} %h_ref.3) | copy-start | bytes 49156
  15.6 9.4 %copy-start.4 = (s32[32]{0:T(128)S(1)}, s32[32]{0:T(128)}, u32[]{:S(2)}) copy-start(s32[32]{0:T(128)} %counts_ref.3) | copy-start | bytes 388
  15.6 9.4 %collective-permute-start.2 = (s16[272,256]{1,0:T(8,128)(2,1)S(1)}, s16[272,256]{1,0:T(8,128)(2,1)S(1)}, u32[]{:S(2)}, u32[]{:S(2)}) collective-permute-start(s16[272,256]{1,0:T(8,128)(2,1)S(1)} %project_next.3), channel_id=1, source_target_pairs={{0,2},{1,3},{2,0},{3,1},{4,6},{5,7},{6,4},{7,5},{8,10},{9,11},{10,... | collective-permute-start | bytes 417800 | tf_op jit(solution)/shard_map/ppermute | solution.py:621
  18.8 3.9 %collective-permute-start.4 = (f32[64,64]{1,0:T(8,128)S(1)}, f32[64,64]{1,0:T(8,128)S(1)}, u32[]{:S(2)}, u32[]{:S(2)}) collective-permute-start(f32[64,64]{1,0:T(8,128)S(1)} %add_terms.5.refs_1_.refs_0_), channel_id=1, source_target_pairs={{0,8},{4,12},{8,0},{12,4},{1,9},{5,13},{9,1},{13,5},{2,10},{6,14},... | collective-permute-start | bytes 49160 | tf_op jit(solution)/shard_map/ppermute | solution.py:621
  24.0 9.0 %collective-permute-start.5 = (s16[304,256]{1,0:T(8,128)(2,1)S(1)}, s16[304,256]{1,0:T(8,128)(2,1)S(1)}, u32[]{:S(2)}, u32[]{:S(2)}) collective-permute-start(s16[304,256]{1,0:T(8,128)(2,1)S(1)} %project_next.5), channel_id=1, source_target_pairs={{0,2},{1,3},{2,0},{3,1},{4,6},{5,7},{6,4},{7,5},{8,10},{9,11},{10,... | collective-permute-start | bytes 466952 | tf_op jit(solution)/shard_map/ppermute | solution.py:621
  30.9 8.5 %collective-permute-start.7 = (bf16[4,64,256]{2,1,0:T(8,128)(2,1)S(1)}, bf16[4,64,256]{2,1,0:T(8,128)(2,1)S(1)}, u32[]{:S(2)}, u32[]{:S(2)}) collective-permute-start(bf16[4,64,256]{2,1,0:T(8,128)(2,1)S(1)} %get-tuple-element.50.refs_0_), channel_id=1, source_target_pairs={{0,2},{1,3},{2,0},{3,1},{4,6},{5,7},{6,4},{7,5},{8,10},{9,11},{10,... | collective-permute-start | bytes 393224 | tf_op jit(solution)/shard_map/ppermute | solution.py:621
  39.4 10.1 %collective-permute-start.13 = (bf16[8,64,256]{2,1,0:T(8,128)(2,1)S(1)}, bf16[8,64,256]{2,1,0:T(8,128)(2,1)S(1)}, u32[]{:S(2)}, u32[]{:S(2)}) collective-permute-start(bf16[8,64,256]{2,1,0:T(8,128)(2,1)S(1)} %join_frames.2.refs_3_), channel_id=1, source_target_pairs={{0,1},{1,0},{2,3},{3,2},{4,5},{5,4},{6,7},{7,6},{8,9},{9,8},{10,11... | collective-permute-start | bytes 786440 | tf_op jit(solution)/shard_map/ppermute | solution.py:621
  40.6 7.1 %collective-permute-start.12 = (bf16[4,64,256]{2,1,0:T(8,128)(2,1)S(1)}, bf16[4,64,256]{2,1,0:T(8,128)(2,1)S(1)}, u32[]{:S(2)}, u32[]{:S(2)}) collective-permute-start(bf16[4,64,256]{2,1,0:T(8,128)(2,1)S(1)} %get-tuple-element.51.refs_2_.refs_1_.refs_0_), channel_id=1, source_target_pairs={{0,2},{1,3},{2,0},{3,1},{4,6},{5,7},{6,4},{7,5},{8,10},{9,11},{10,... | collective-permute-start | bytes 393224 | tf_op jit(solution)/shard_map/ppermute | solution.py:621
  42.3 1.3 %collective-permute-start.6 = (f32[64,64]{1,0:T(8,128)S(1)}, f32[64,64]{1,0:T(8,128)S(1)}, u32[]{:S(2)}, u32[]{:S(2)}) collective-permute-start(f32[64,64]{1,0:T(8,128)S(1)} %get-tuple-element.49.a_ref), channel_id=1, source_target_pairs={{0,4},{4,0},{8,12},{12,8},{1,5},{5,1},{9,13},{13,9},{2,6},{6,2},{1... | collective-permute-start | bytes 49160 | tf_op jit(solution)/shard_map/ppermute | solution.py:621
  43.5 4.0 %collective-permute-start.8 = (f32[64,64]{1,0:T(8,128)S(1)}, f32[64,64]{1,0:T(8,128)S(1)}, u32[]{:S(2)}, u32[]{:S(2)}) collective-permute-start(f32[64,64]{1,0:T(8,128)S(1)} %add_terms.6.refs_2_.a_ref), channel_id=1, source_target_pairs={{0,8},{4,12},{8,0},{12,4},{1,9},{5,13},{9,1},{13,5},{2,10},{6,14},... | collective-permute-start | bytes 49160 | tf_op jit(solution)/shard_map/ppermute | solution.py:621
  49.6 8.7 %collective-permute-start.14 = (bf16[8,64,256]{2,1,0:T(8,128)(2,1)S(1)}, bf16[8,64,256]{2,1,0:T(8,128)(2,1)S(1)}, u32[]{:S(2)}, u32[]{:S(2)}) collective-permute-start(bf16[8,64,256]{2,1,0:T(8,128)(2,1)S(1)} %join_frames.3.refs_1_), channel_id=1, source_target_pairs={{0,1},{1,0},{2,3},{3,2},{4,5},{5,4},{6,7},{7,6},{8,9},{9,8},{10,11... | collective-permute-start | bytes 786440 | tf_op jit(solution)/shard_map/ppermute | solution.py:621
  50.5 8.6 %collective-permute-start.11 = (f32[64,64]{1,0:T(8,128)S(1)}, f32[64,64]{1,0:T(8,128)S(1)}, u32[]{:S(2)}, u32[]{:S(2)}) collective-permute-start(f32[64,64]{1,0:T(8,128)S(1)} %add_terms.7.refs_2_.refs_0_), channel_id=1, source_target_pairs={{0,3},{1,2},{2,1},{3,0},{4,7},{5,6},{6,5},{7,4},{8,11},{9,10},{10,... | collective-permute-start | bytes 49160 | tf_op jit(solution)/shard_map/ppermute | solution.py:621
  52.3 6.8 %collective-permute-start.10 = (f32[64,64]{1,0:T(8,128)S(1)}, f32[64,64]{1,0:T(8,128)S(1)}, u32[]{:S(2)}, u32[]{:S(2)}) collective-permute-start(f32[64,64]{1,0:T(8,128)S(1)} %add_terms.7.refs_2_.refs_0_), channel_id=1, source_target_pairs={{0,2},{1,3},{2,0},{3,1},{4,6},{5,7},{6,4},{7,5},{8,10},{9,11},{10,... | collective-permute-start | bytes 49160 | tf_op jit(solution)/shard_map/ppermute | solution.py:621
  53.1 6.0 %collective-permute-start.9 = (f32[64,64]{1,0:T(8,128)S(1)}, f32[64,64]{1,0:T(8,128)S(1)}, u32[]{:S(2)}, u32[]{:S(2)}) collective-permute-start(f32[64,64]{1,0:T(8,128)S(1)} %add_terms.7.refs_2_.refs_0_), channel_id=1, source_target_pairs={{0,1},{1,0},{2,3},{3,2},{4,5},{5,4},{6,7},{7,6},{8,9},{9,8},{10,11... | collective-permute-start | bytes 49160 | tf_op jit(solution)/shard_map/ppermute | solution.py:621
  60.8 1.4 %collective-permute-start.15 = (f32[64,512]{1,0:T(8,128)S(1)}, f32[64,512]{1,0:T(8,128)S(1)}, u32[]{:S(2)}, u32[]{:S(2)}) collective-permute-start(f32[64,512]{1,0:T(8,128)S(1)} %v_terms.2.refs_12_), channel_id=1, source_target_pairs={{0,4},{4,0},{8,12},{12,8},{1,5},{5,1},{9,13},{13,9},{2,6},{6,2},{1... | collective-permute-start | bytes 393224 | tf_op jit(solution)/shard_map/ppermute | solution.py:621
  62.2 6.2 %collective-permute-start.16 = (f32[64,512]{1,0:T(8,128)S(1)}, f32[64,512]{1,0:T(8,128)S(1)}, u32[]{:S(2)}, u32[]{:S(2)}) collective-permute-start(f32[64,512]{1,0:T(8,128)S(1)} %add_terms.8.a_ref), channel_id=1, source_target_pairs={{0,8},{4,12},{8,0},{12,4},{1,9},{5,13},{9,1},{13,5},{2,10},{6,14},... | collective-permute-start | bytes 393224 | tf_op jit(solution)/shard_map/ppermute | solution.py:621
  68.4 1.7 %collective-permute-start.17 = (f32[64,512]{1,0:T(8,128)S(1)}, f32[64,512]{1,0:T(8,128)S(1)}, u32[]{:S(2)}, u32[]{:S(2)}) collective-permute-start(f32[64,512]{1,0:T(8,128)S(1)} %add_terms.9.terms_ref), channel_id=1, source_target_pairs={{0,4},{4,0},{8,12},{12,8},{1,5},{5,1},{9,13},{13,9},{2,6},{6,2},{1... | collective-permute-start | bytes 393224 | tf_op jit(solution)/shard_map/ppermute | solution.py:621
  71.8 6.0 %collective-permute-start.20 = (f32[64,128]{1,0:T(8,128)S(1)}, f32[64,128]{1,0:T(8,128)S(1)}, u32[]{:S(2)}, u32[]{:S(2)}) collective-permute-start(f32[64,128]{1,0:T(8,128)S(1)} %get-tuple-element.80.refs_0_), channel_id=1, source_target_pairs={{0,3},{1,2},{2,1},{3,0},{4,7},{5,6},{6,5},{7,4},{8,11},{9,10},{10,... | collective-permute-start | bytes 98312 | tf_op jit(solution)/shard_map/ppermute | solution.py:621
  73.7 5.1 %collective-permute-start.19 = (f32[64,128]{1,0:T(8,128)S(1)}, f32[64,128]{1,0:T(8,128)S(1)}, u32[]{:S(2)}, u32[]{:S(2)}) collective-permute-start(f32[64,128]{1,0:T(8,128)S(1)} %get-tuple-element.80.refs_0_), channel_id=1, source_target_pairs={{0,2},{1,3},{2,0},{3,1},{4,6},{5,7},{6,4},{7,5},{8,10},{9,11},{10,... | collective-permute-start | bytes 98312 | tf_op jit(solution)/shard_map/ppermute | solution.py:621
  73.7 5.1 %collective-permute-start.18 = (f32[64,128]{1,0:T(8,128)S(1)}, f32[64,128]{1,0:T(8,128)S(1)}, u32[]{:S(2)}, u32[]{:S(2)}) collective-permute-start(f32[64,128]{1,0:T(8,128)S(1)} %get-tuple-element.80.refs_0_), channel_id=1, source_target_pairs={{0,1},{1,0},{2,3},{3,2},{4,5},{5,4},{6,7},{7,6},{8,9},{9,8},{10,11... | collective-permute-start | bytes 98312 | tf_op jit(solution)/shard_map/ppermute | solution.py:621
  (2 other events, 13.9 us)

commit v19 on v18

--- a/solution.py
+++ b/solution.py
@@ -134,17 +134,20 @@
     count = buffers.shape[1]
     v_copy = pltpu.make_async_copy(v_hbm, v_ref, v_sem)
     v_copy.start()
-    copies = [
-        pltpu.make_async_copy(visits_ref.at[feature_of(place) ^ slot, pl.ds(0, count)], buffers.at[i], sems.at[i])
-        for i, slot in enumerate(slots)
-    ]
-    for copy in copies:
-        copy.start()
+    pieces = sems.shape[1]
+    piece = count // pieces
+    copies = []
+    for i, slot in enumerate(slots):
+        for j in range(pieces):
+            rows = pl.ds(j * piece, piece)
+            source = visits_ref.at[feature_of(place) ^ slot, rows]
+            copies.append(pltpu.make_async_copy(source, buffers.at[i, rows], sems.at[i, j]))
+            copies[-1].start()
     v_copy.wait()
 
     def value(i, p):
-        if p == 0:
-            copies[i].wait()
+        if p % piece == 0:
+            copies[i * pieces + p // piece].wait()
         return low_dot(v_ref[...], buffers[i, p], ROWS_BY_ROWS)
 
     values = [functools.partial(value, i, p) for i in range(len(slots)) for p in range(count)]
@@ -163,7 +166,7 @@
         scratch_shapes=[
             pltpu.VMEM(v_rows.shape, BF16),
             pltpu.VMEM((len(slots), count) + visits.shape[2:], BF16),
-            pltpu.SemaphoreType.DMA((len(slots),)),
+            pltpu.SemaphoreType.DMA((len(slots), 2 if count % 2 == 0 else 1)),
             pltpu.SemaphoreType.DMA,
         ],
         compiler_params=parameters(LIMIT),
@@ -233,27 +236,30 @@
     )(place, w_start)
 
 
-def own_projection_kernel(place, v_ref, visits_ref, *refs):
+def own_projection_kernel(layout, place, v_ref, visits_ref, arrived_ref, *refs):
     *proj_refs, v_gram_ref = refs
-    count = visits_ref.shape[1] // len(proj_refs)
+    count, rank, _ = proj_refs[0].shape
+    payload = Payload(arrived_ref, layout, count, rank, len(proj_refs) == 1)
     for p in range(visits_ref.shape[1]):
-        proj_refs[p // count][p % count] = low_dot(v_ref[...], visits_ref[feature_of(place), p], ROWS_BY_ROWS)
-    v_gram_ref[...] = low_dot(v_ref[...], v_ref[...], ROWS_BY_ROWS)
-
-
-def project_own(n_parts, place, visits, v_rows):
+        proj = low_dot(v_ref[...], visits_ref[feature_of(place), p], ROWS_BY_ROWS)
+        proj_refs[p // count][p % count] = proj + payload.proj(0, p) if p < count else proj
+    gram = low_dot(v_ref[...], v_ref[...], ROWS_BY_ROWS)
+    v_gram_ref[...] = gram + payload.gram() if payload.with_gram else gram
+
+
+def project_own(n_parts, layout, place, visits, v_rows, arrived):
     _, share, slots, width = visits.shape
     rank = v_rows.shape[0]
     proj = jax.ShapeDtypeStruct((share // n_parts, rank, slots), F32)
     *own, v_gram = pl.pallas_call(
-        own_projection_kernel,
-        in_specs=[SMEM_SPEC] + [VMEM_SPEC] * 2,
+        functools.partial(own_projection_kernel, layout),
+        in_specs=[SMEM_SPEC] + [VMEM_SPEC] * 3,
         out_specs=[VMEM_SPEC] * (n_parts + 1),
         out_shape=[proj] * n_parts + [jax.ShapeDtypeStruct((rank, rank), F32)],
         compiler_params=parameters(LIMIT),
         cost_estimate=SHORT,
         name="project_own",
-    )(place, v_rows, visits)
+    )(place, v_rows, visits, arrived)
     return own, v_gram
 
 
@@ -684,8 +690,6 @@
 
     w_gram, spread = spread_w(place, w_start, n)
     w_grams = staged_terms(w_gram, "patient", [])
-    own, v_gram = project_own(n_parts, place, by_owner, v_near)
-    h_local = v_gram
     arrived = [[] for _ in firsts]
     for i, bit in enumerate(bits):
         layouts = [receive(before) for before in bits[:i]]
@@ -698,6 +702,8 @@
                     send(bit), first, count, part == n_parts - 1, layouts, place, by_owner, v_near, arrived[part], after
                 )
             arrived[part] = arrived[part] + [swap(code, "feature", bit)]
+        if i == 0:
+            own, v_gram = project_own(n_parts, receive(bit), place, by_owner, v_near, arrived[0][0])
 
     layouts = [receive(bit) for bit in bits]
     frames = [[] for _ in firsts]
@@ -714,9 +720,20 @@
         arrays = {(frames[part][k][0], firsts[part]): frames[part][k][1] for part, k in groups}
         return project_frames(list(arrays), place, arrays, by_owner, after)
 
+    h_local = v_gram
     for part, first in enumerate(firsts):
         low, h_local, v_total = own_frames(
-            layouts, part, n_parts, place, visit_counts, h_start, w_start, v_gram, h_local, own[part], arrived[part]
+            layouts[part == 0 :],
+            part,
+            n_parts,
+            place,
+            visit_counts,
+            h_start,
+            w_start,
+            v_gram,
+            h_local,
+            own[part],
+            arrived[part][part == 0 :],
         )
         v_gram = v_total
         frames[part].append(((0,), low))

time: 81.2 us -> 81.1 us (level)
  starting transfers between devices: 30.5 us -> 28.2 us
  waiting for transfers between devices: 12.2 us -> 14.2 us
    ppermute x21, starting transfers between devices: 30.5 us -> 28.2 us  [swap(): return lax.ppermute(x, axis, pairs)]
    ppermute x21, waiting for transfers between devices: 12.2 us -> 14.2 us  [swap(): return lax.ppermute(x, axis, pairs)]
  transfers between devices with their start and end apart: 21 -> 21, of which waited for: 12 -> 11; matrix products, arithmetic and copies ran while one was open for 0% -> 0% of each run, Pallas kernels for 34% -> 34%
where the time goes in v19:
time: 81.1 us; the launch traced here: 81 us
  Pallas kernels  37.7 us (46%)
  starting transfers between devices  28.2 us (35%)
  waiting for transfers between devices  14.2 us (18%)
  between operations  0.85 us (1%)
    ppermute x21, starting transfers between devices, swap(): return lax.ppermute(x, axis, pairs)  28.2 us
    ppermute x21, waiting for transfers between devices, swap(): return lax.ppermute(x, axis, pairs)  14.2 us
    pallas_call x2, Pallas kernels, own_frames(): pl.pallas_call(functools.partial(frames_kernel, layouts, part, share), in...  12 us
    pallas_call x1, Pallas kernels, first_projection(): pl.pallas_call(functools.partial(first_projection_kernel, slots, with_gra...  4.37 us
    pallas_call x3, Pallas kernels, next_projection(): pl.pallas_call(functools.partial(next_projection_kernel, slots, first, co...  3.56 us
    pallas_call x4, Pallas kernels, project_frames(): pl.pallas_call(functools.partial(projected_kernel, items), in_specs=[SMEM...  3.49 us
    pallas_call x2, Pallas kernels, half_v(): pl.pallas_call(functools.partial(next_v_kernel, items, share, bool(before...  3.25 us
    pallas_call x1, Pallas kernels, next_w(): pl.pallas_call(functools.partial(next_w_kernel, len(sums)), in_specs=[VME...  2.27 us
  transfers between devices with their start and end apart: 21, of which 11 were waited for; matrix products, arithmetic and copies ran while one was open for 0% of the time, Pallas kernels for 34%

profile of v19, /device:TPU:0, one launch (start us, length us, event | category | flops | bytes accessed | tf_op | source)
XLA Modules:
  0.0 81.0 jit_solution(15644989529725176704)
XLA Ops:
  0.7 4.4 %project_first.1 = s16[528,256]{1,0:T(8,128)(2,1)S(1)} custom-call(s32[1]{0:T(128)} %bitcast.place, bf16[64,1024]{1,0:T(8,128)(2,1)} %bitcast.13, bf16[4,8,256,1024]{3,2,1,0:T(8,128)(2,1)} %bitcast.4), custom_call_target="tpu_custom_call" | custom-call | flops 1000 | bytes 1000 | tf_op jit(solution)/shard_map/project_first/pallas_call | solution.py:161
  5.0 3.1 %collective-permute-start = (s16[528,256]{1,0:T(8,128)(2,1)S(1)}, s16[528,256]{1,0:T(8,128)(2,1)S(1)}, u32[]{:S(2)}, u32[]{:S(2)}) collective-permute-start(s16[528,256]{1,0:T(8,128)(2,1)S(1)} %project_first.1), channel_id=1, source_target_pairs={{0,1},{1,0},{2,3},{3,2},{4,5},{5,4},{6,7},{7,6},{8,9},{9,8},{10,11... | collective-permute-start | bytes 811016 | tf_op jit(solution)/shard_map/ppermute | solution.py:627
  8.1 1.6 %project_next.4 = s16[560,256]{1,0:T(8,128)(2,1)S(1)} custom-call(s32[1]{0:T(128)} %bitcast.place, bf16[64,1024]{1,0:T(8,128)(2,1)S(1)} %bitcast.14, bf16[4,8,256,1024]{3,2,1,0:T(8,128)(2,1)S(1)} %bitcast.5), custom_call_target="tpu_custom_call" | custom-call | flops 1000 | bytes 1000 | tf_op jit(solution)/shard_map/project_next/pallas_call | solution.py:199
  9.8 2.7 %collective-permute-start.3 = (s16[560,256]{1,0:T(8,128)(2,1)S(1)}, s16[560,256]{1,0:T(8,128)(2,1)S(1)}, u32[]{:S(2)}, u32[]{:S(2)}) collective-permute-start(s16[560,256]{1,0:T(8,128)(2,1)S(1)} %project_next.4), channel_id=1, source_target_pairs={{0,1},{1,0},{2,3},{3,2},{4,5},{5,4},{6,7},{7,6},{8,9},{9,8},{10,11... | collective-permute-start | bytes 860168 | tf_op jit(solution)/shard_map/ppermute | solution.py:627
  16.4 3.1 %collective-permute-start.2 = (s16[272,256]{1,0:T(8,128)(2,1)S(1)}, s16[272,256]{1,0:T(8,128)(2,1)S(1)}, u32[]{:S(2)}, u32[]{:S(2)}) collective-permute-start(s16[272,256]{1,0:T(8,128)(2,1)S(1)} %project_next.3), channel_id=1, source_target_pairs={{0,2},{1,3},{2,0},{3,1},{4,6},{5,7},{6,4},{7,5},{8,10},{9,11},{10,... | collective-permute-start | bytes 417800 | tf_op jit(solution)/shard_map/ppermute | solution.py:627
  19.5 1.5 %collective-permute-start.4 = (f32[64,64]{1,0:T(8,128)S(1)}, f32[64,64]{1,0:T(8,128)S(1)}, u32[]{:S(2)}, u32[]{:S(2)}) collective-permute-start(f32[64,64]{1,0:T(8,128)S(1)} %add_terms.5.refs_1_.refs_0_), channel_id=1, source_target_pairs={{0,8},{4,12},{8,0},{12,4},{1,9},{5,13},{9,1},{13,5},{2,10},{6,14},... | collective-permute-start | bytes 49160 | tf_op jit(solution)/shard_map/ppermute | solution.py:627
  21.0 1.4 %project_own.1 = (f32[4,64,256]{2,1,0:T(8,128)S(1)}, f32[4,64,256]{2,1,0:T(8,128)S(1)}, f32[64,64]{1,0:T(8,128)S(1)}) custom-call(s32[1]{0:T(128)} %bitcast.place, bf16[64,1024]{1,0:T(8,128)(2,1)S(1)} %bitcast.16, bf16[4,8,256,1024]{3,2,1,0:T(8,128)(2,1)S(1)} %bitcast.7, s16[528,256]{1,0:T(8,128)(2,1)S(1)} %collective-permute-done.arrived_ref.refs_0_), custom_call_target="tpu_custom_call" | custom-call | flops 1000 | bytes 1000 | tf_op jit(solution)/shard_map/project_own/pallas_call | solution.py:254
  25.7 6.0 %own_frames.2 = (bf16[4,64,256]{2,1,0:T(8,128)(2,1)S(1)}, f32[64,64]{1,0:T(8,128)S(1)}, f32[64,64]{1,0:T(8,128)S(1)}) custom-call(s32[1]{0:T(128)} %bitcast.place, s32[32]{0:T(128)S(1)} %copy-done.4, f32[64,64]{1,0:T(8,128)S(1)} %copy-done.3, f32[32,64]{1,0:T(8,128)S(1)} %copy-done.2, f32[64,64]{1,0:T(8,128)S(1)} %get-tuple-element.43.v_gram_ref.before_ref.refs_2_, ...), custom_call_target="tpu_custom_call" | custom-call | flops 1000 | bytes 1000 | tf_op jit(solution)/shard_map/own_frames/pallas_call | solution.py:395
  31.7 2.0 %collective-permute-start.7 = (bf16[4,64,256]{2,1,0:T(8,128)(2,1)S(1)}, bf16[4,64,256]{2,1,0:T(8,128)(2,1)S(1)}, u32[]{:S(2)}, u32[]{:S(2)}) collective-permute-start(bf16[4,64,256]{2,1,0:T(8,128)(2,1)S(1)} %get-tuple-element.50.refs_0_), channel_id=1, source_target_pairs={{0,2},{1,3},{2,0},{3,1},{4,6},{5,7},{6,4},{7,5},{8,10},{9,11},{10,... | collective-permute-start | bytes 393224 | tf_op jit(solution)/shard_map/ppermute | solution.py:627
  33.7 6.0 %own_frames.3 = (bf16[4,64,256]{2,1,0:T(8,128)(2,1)S(1)}, f32[64,64]{1,0:T(8,128)S(1)}, f32[64,64]{1,0:T(8,128)S(1)}) custom-call(s32[1]{0:T(128)} %bitcast.place, s32[32]{0:T(128)S(1)} %copy-done.4, f32[64,64]{1,0:T(8,128)S(1)} %copy-done.3, f32[32,64]{1,0:T(8,128)S(1)} %copy-done.2, f32[64,64]{1,0:T(8,128)S(1)} %get-tuple-element.46.v_gram_ref, ...), custom_call_target="tpu_custom_call" | custom-call | flops 1000 | bytes 1000 | tf_op jit(solution)/shard_map/own_frames/pallas_call | solution.py:395
  39.8 1.5 %collective-permute-start.13 = (bf16[8,64,256]{2,1,0:T(8,128)(2,1)S(1)}, bf16[8,64,256]{2,1,0:T(8,128)(2,1)S(1)}, u32[]{:S(2)}, u32[]{:S(2)}) collective-permute-start(bf16[8,64,256]{2,1,0:T(8,128)(2,1)S(1)} %join_frames.2.refs_3_), channel_id=1, source_target_pairs={{0,1},{1,0},{2,3},{3,2},{4,5},{5,4},{6,7},{7,6},{8,9},{9,8},{10,11... | collective-permute-start | bytes 786440 | tf_op jit(solution)/shard_map/ppermute | solution.py:627
  41.3 1.7 %collective-permute-start.12 = (bf16[4,64,256]{2,1,0:T(8,128)(2,1)S(1)}, bf16[4,64,256]{2,1,0:T(8,128)(2,1)S(1)}, u32[]{:S(2)}, u32[]{:S(2)}) collective-permute-start(bf16[4,64,256]{2,1,0:T(8,128)(2,1)S(1)} %get-tuple-element.51.refs_2_.refs_1_.refs_0_), channel_id=1, source_target_pairs={{0,2},{1,3},{2,0},{3,1},{4,6},{5,7},{6,4},{7,5},{8,10},{9,11},{10,... | collective-permute-start | bytes 393224 | tf_op jit(solution)/shard_map/ppermute | solution.py:627
  43.0 1.2 %project_frames.4 = (bf16[256,1024]{1,0:T(8,128)(2,1)S(1)}, bf16[256,1024]{1,0:T(8,128)(2,1)S(1)}, bf16[256,1024]{1,0:T(8,128)(2,1)S(1)}, bf16[256,1024]{1,0:T(8...) custom-call(s32[1]{0:T(128)} %bitcast.place, ...), custom_call_target="tpu_custom_call" | custom-call | flops 1000 | bytes 1000 | tf_op jit(solution)/shard_map/project_frames/pallas_call | solution.py:452
  44.3 1.8 %collective-permute-start.8 = (f32[64,64]{1,0:T(8,128)S(1)}, f32[64,64]{1,0:T(8,128)S(1)}, u32[]{:S(2)}, u32[]{:S(2)}) collective-permute-start(f32[64,64]{1,0:T(8,128)S(1)} %add_terms.6.refs_2_.a_ref), channel_id=1, source_target_pairs={{0,8},{4,12},{8,0},{12,4},{1,9},{5,13},{9,1},{13,5},{2,10},{6,14},... | collective-permute-start | bytes 49160 | tf_op jit(solution)/shard_map/ppermute | solution.py:627
  46.0 1.6 %first_inverse.1 = (f32[64,64]{1,0:T(8,128)S(1)}, f32[64,64]{1,0:T(8,128)S(1)}) custom-call(f32[64,64]{1,0:T(8,128)S(1)} %get-tuple-element.53.v_gram_ref, f32[64,64]{1,0:T(8,128)S(1)} %add_terms.5.refs_1_.refs_0_, f32[64,64]{1,0:T(8,128)S(1)} %collective-permute-done.4.refs_1_, f32[64,64]{1,0:T(8,128)S(1)} %add_terms.6.refs_2_.a_ref), custom_call_target="tpu_custom_call" | custom-call | flops 1000 | bytes 1000 | tf_op jit(solution)/shard_map/first_inverse/pallas_call | solution.py:322
  48.4 1.6 %collective-permute-done.13.refs_3_.refs_0_ = bf16[8,64,256]{2,1,0:T(8,128)(2,1)S(1)} collective-permute-done((bf16[8,64,256]{2,1,0:T(8,128)(2,1)S(1)}, bf16[8,64,256]{2,1,0:T(8,128)(2,1)S(1)}, u32[]{:S(2)}, u32[]{:S(2)}) %collective-permute-start.13) | collective-permute-done | bytes 262176 | tf_op jit(solution)/shard_map/ppermute | solution.py:627
  50.4 2.3 %collective-permute-start.11 = (f32[64,64]{1,0:T(8,128)S(1)}, f32[64,64]{1,0:T(8,128)S(1)}, u32[]{:S(2)}, u32[]{:S(2)}) collective-permute-start(f32[64,64]{1,0:T(8,128)S(1)} %add_terms.7.refs_2_.refs_0_), channel_id=1, source_target_pairs={{0,3},{1,2},{2,1},{3,0},{4,7},{5,6},{6,5},{7,4},{8,11},{9,10},{10,... | collective-permute-start | bytes 49160 | tf_op jit(solution)/shard_map/ppermute | solution.py:627
  56.2 2.8 %collective-permute-done.14.refs_0_ = bf16[8,64,256]{2,1,0:T(8,128)(2,1)S(1)} collective-permute-done((bf16[8,64,256]{2,1,0:T(8,128)(2,1)S(1)}, bf16[8,64,256]{2,1,0:T(8,128)(2,1)S(1)}, u32[]{:S(2)}, u32[]{:S(2)}) %collective-permute-start.14) | collective-permute-done | bytes 262176 | tf_op jit(solution)/shard_map/ppermute | solution.py:627
  63.4 1.7 %second_inverse.1 = (f32[64,64]{1,0:T(8,128)S(1)}, f32[64,64]{1,0:T(8,128)S(1)}) custom-call(f32[64,64]{1,0:T(8,128)S(1)} %get-tuple-element.73.h_ref, f32[64,64]{1,0:T(8,128)S(1)} %get-tuple-element.74.w_gram_ref), custom_call_target="tpu_custom_call" | custom-call | flops 1000 | bytes 1000 | tf_op jit(solution)/shard_map/second_inverse/pallas_call | solution.py:501
  65.1 3.5 %collective-permute-done.16.b_ref = f32[64,512]{1,0:T(8,128)S(1)} collective-permute-done((f32[64,512]{1,0:T(8,128)S(1)}, f32[64,512]{1,0:T(8,128)S(1)}, u32[]{:S(2)}, u32[]{:S(2)}) %collective-permute-start.16) | collective-permute-done | bytes 131104 | tf_op jit(solution)/shard_map/ppermute | solution.py:627
  68.7 1.6 %next_v.2 = (f32[64,512]{1,0:T(8,128)S(1)}, f32[64,128]{1,0:T(8,128)S(1)}) custom-call(s32[1]{0:T(128)} %bitcast.place, f32[64,512]{1,0:T(8,128)S(1)} %add_terms.9.terms_ref, f32[64,64]{1,0:T(8,128)S(1)} %get-tuple-element.75.refs_0_.inverse_ref, f32[64,64]{1,0:T(8,128)S(1)} %get-tuple-element.73.h_ref, bf16[256,1024]{1,0:T(8,128)(2,1)S(1)} %get-tuple-element.61.refs_0_, ...), custom_call_target="tpu_custom_call" | custom-call | flops 1000 | bytes 1000 | tf_op jit(solution)/shard_map/next_v/pallas_call | solution.py:568
  70.4 1.6 %next_v.3 = (f32[64,512]{1,0:T(8,128)S(1)}, f32[64,128]{1,0:T(8,128)S(1)}) custom-call(s32[1]{0:T(128)} %bitcast.place, f32[64,512]{1,0:T(8,128)S(1)} %collective-permute-done.17.terms_ref, f32[64,64]{1,0:T(8,128)S(1)} %get-tuple-element.75.refs_0_.inverse_ref, f32[64,64]{1,0:T(8,128)S(1)} %get-tuple-element.73.h_ref, ...), custom_call_target="tpu_custom_call" | custom-call | flops 1000 | bytes 1000 | tf_op jit(solution)/shard_map/next_v/pallas_call | solution.py:568
  73.2 3.2 %collective-permute-start.18 = (f32[64,128]{1,0:T(8,128)S(1)}, f32[64,128]{1,0:T(8,128)S(1)}, u32[]{:S(2)}, u32[]{:S(2)}) collective-permute-start(f32[64,128]{1,0:T(8,128)S(1)} %get-tuple-element.80.refs_0_), channel_id=1, source_target_pairs={{0,1},{1,0},{2,3},{3,2},{4,5},{5,4},{6,7},{7,6},{8,9},{9,8},{10,11... | collective-permute-start | bytes 98312 | tf_op jit(solution)/shard_map/ppermute | solution.py:627
  78.7 2.3 %next_w.1 = f32[32,64]{1,0:T(8,128)} custom-call(f32[64,128]{1,0:T(8,128)S(1)} %get-tuple-element.80.refs_0_, f32[64,128]{1,0:T(8,128)S(1)} %collective-permute-done.18.refs_1_, f32[64,128]{1,0:T(8,128)S(1)} %collective-permute-done.19.refs_2_, f32[64,128]{1,0:T(8,128)S(1)} %collective-permute-done.20.refs_3_, f32[64,64]{1,0:T(8,128)S(1)} %get-tuple-element.81.refs_4_, ...), custom_call_target="tpu_custom_call" | custom-call | flops 1000 | bytes 1000 | tf_op jit(solution)/shard_map/next_w/pallas_call | solution.py:614
  (56 shorter events, 19.8 us)
Async XLA Ops:
  0.7 11.8 %copy-start.2 = (f32[32,64]{1,0:T(8,128)S(1)}, f32[32,64]{1,0:T(8,128)}, u32[]{:S(2)}) copy-start(f32[32,64]{1,0:T(8,128)} %w_ref.5) | copy-start | bytes 24580
  5.0 10.4 %collective-permute-start = (s16[528,256]{1,0:T(8,128)(2,1)S(1)}, s16[528,256]{1,0:T(8,128)(2,1)S(1)}, u32[]{:S(2)}, u32[]{:S(2)}) collective-permute-start(s16[528,256]{1,0:T(8,128)(2,1)S(1)} %project_first.1), channel_id=1, source_target_pairs={{0,1},{1,0},{2,3},{3,2},{4,5},{5,4},{6,7},{7,6},{8,9},{9,8},{10,11... | collective-permute-start | bytes 811016 | tf_op jit(solution)/shard_map/ppermute | solution.py:627
  9.8 14.0 %collective-permute-start.3 = (s16[560,256]{1,0:T(8,128)(2,1)S(1)}, s16[560,256]{1,0:T(8,128)(2,1)S(1)}, u32[]{:S(2)}, u32[]{:S(2)}) collective-permute-start(s16[560,256]{1,0:T(8,128)(2,1)S(1)} %project_next.4), channel_id=1, source_target_pairs={{0,1},{1,0},{2,3},{3,2},{4,5},{5,4},{6,7},{7,6},{8,9},{9,8},{10,11... | collective-permute-start | bytes 860168 | tf_op jit(solution)/shard_map/ppermute | solution.py:627
  13.3 1.3 %collective-permute-start.1 = (f32[64,64]{1,0:T(8,128)S(1)}, f32[64,64]{1,0:T(8,128)S(1)}, u32[]{:S(2)}, u32[]{:S(2)}) collective-permute-start(f32[64,64]{1,0:T(8,128)S(1)} %get-tuple-element.45.a_ref), channel_id=1, source_target_pairs={{0,4},{4,0},{8,12},{12,8},{1,5},{5,1},{9,13},{13,9},{2,6},{6,2},{1... | collective-permute-start | bytes 49160 | tf_op jit(solution)/shard_map/ppermute | solution.py:627
  16.4 9.3 %copy-start.3 = (f32[64,64]{1,0:T(8,128)S(1)}, f32[64,64]{1,0:T(8,128)}, u32[]{:S(2)}) copy-start(f32[64,64]{1,0:T(8,128)} %h_ref.3) | copy-start | bytes 49156
  16.4 9.3 %copy-start.4 = (s32[32]{0:T(128)S(1)}, s32[32]{0:T(128)}, u32[]{:S(2)}) copy-start(s32[32]{0:T(128)} %counts_ref.3) | copy-start | bytes 388
  16.4 9.3 %collective-permute-start.2 = (s16[272,256]{1,0:T(8,128)(2,1)S(1)}, s16[272,256]{1,0:T(8,128)(2,1)S(1)}, u32[]{:S(2)}, u32[]{:S(2)}) collective-permute-start(s16[272,256]{1,0:T(8,128)(2,1)S(1)} %project_next.3), channel_id=1, source_target_pairs={{0,2},{1,3},{2,0},{3,1},{4,6},{5,7},{6,4},{7,5},{8,10},{9,11},{10,... | collective-permute-start | bytes 417800 | tf_op jit(solution)/shard_map/ppermute | solution.py:627
  19.5 3.9 %collective-permute-start.4 = (f32[64,64]{1,0:T(8,128)S(1)}, f32[64,64]{1,0:T(8,128)S(1)}, u32[]{:S(2)}, u32[]{:S(2)}) collective-permute-start(f32[64,64]{1,0:T(8,128)S(1)} %add_terms.5.refs_1_.refs_0_), channel_id=1, source_target_pairs={{0,8},{4,12},{8,0},{12,4},{1,9},{5,13},{9,1},{13,5},{2,10},{6,14},... | collective-permute-start | bytes 49160 | tf_op jit(solution)/shard_map/ppermute | solution.py:627
  24.7 9.0 %collective-permute-start.5 = (s16[304,256]{1,0:T(8,128)(2,1)S(1)}, s16[304,256]{1,0:T(8,128)(2,1)S(1)}, u32[]{:S(2)}, u32[]{:S(2)}) collective-permute-start(s16[304,256]{1,0:T(8,128)(2,1)S(1)} %project_next.5), channel_id=1, source_target_pairs={{0,2},{1,3},{2,0},{3,1},{4,6},{5,7},{6,4},{7,5},{8,10},{9,11},{10,... | collective-permute-start | bytes 466952 | tf_op jit(solution)/shard_map/ppermute | solution.py:627
  31.7 8.0 %collective-permute-start.7 = (bf16[4,64,256]{2,1,0:T(8,128)(2,1)S(1)}, bf16[4,64,256]{2,1,0:T(8,128)(2,1)S(1)}, u32[]{:S(2)}, u32[]{:S(2)}) collective-permute-start(bf16[4,64,256]{2,1,0:T(8,128)(2,1)S(1)} %get-tuple-element.50.refs_0_), channel_id=1, source_target_pairs={{0,2},{1,3},{2,0},{3,1},{4,6},{5,7},{6,4},{7,5},{8,10},{9,11},{10,... | collective-permute-start | bytes 393224 | tf_op jit(solution)/shard_map/ppermute | solution.py:627
  39.8 10.2 %collective-permute-start.13 = (bf16[8,64,256]{2,1,0:T(8,128)(2,1)S(1)}, bf16[8,64,256]{2,1,0:T(8,128)(2,1)S(1)}, u32[]{:S(2)}, u32[]{:S(2)}) collective-permute-start(bf16[8,64,256]{2,1,0:T(8,128)(2,1)S(1)} %join_frames.2.refs_3_), channel_id=1, source_target_pairs={{0,1},{1,0},{2,3},{3,2},{4,5},{5,4},{6,7},{7,6},{8,9},{9,8},{10,11... | collective-permute-start | bytes 786440 | tf_op jit(solution)/shard_map/ppermute | solution.py:627
  41.3 7.2 %collective-permute-start.12 = (bf16[4,64,256]{2,1,0:T(8,128)(2,1)S(1)}, bf16[4,64,256]{2,1,0:T(8,128)(2,1)S(1)}, u32[]{:S(2)}, u32[]{:S(2)}) collective-permute-start(bf16[4,64,256]{2,1,0:T(8,128)(2,1)S(1)} %get-tuple-element.51.refs_2_.refs_1_.refs_0_), channel_id=1, source_target_pairs={{0,2},{1,3},{2,0},{3,1},{4,6},{5,7},{6,4},{7,5},{8,10},{9,11},{10,... | collective-permute-start | bytes 393224 | tf_op jit(solution)/shard_map/ppermute | solution.py:627
  43.0 1.3 %collective-permute-start.6 = (f32[64,64]{1,0:T(8,128)S(1)}, f32[64,64]{1,0:T(8,128)S(1)}, u32[]{:S(2)}, u32[]{:S(2)}) collective-permute-start(f32[64,64]{1,0:T(8,128)S(1)} %get-tuple-element.49.a_ref), channel_id=1, source_target_pairs={{0,4},{4,0},{8,12},{12,8},{1,5},{5,1},{9,13},{13,9},{2,6},{6,2},{1... | collective-permute-start | bytes 49160 | tf_op jit(solution)/shard_map/ppermute | solution.py:627
  44.3 4.2 %collective-permute-start.8 = (f32[64,64]{1,0:T(8,128)S(1)}, f32[64,64]{1,0:T(8,128)S(1)}, u32[]{:S(2)}, u32[]{:S(2)}) collective-permute-start(f32[64,64]{1,0:T(8,128)S(1)} %add_terms.6.refs_2_.a_ref), channel_id=1, source_target_pairs={{0,8},{4,12},{8,0},{12,4},{1,9},{5,13},{9,1},{13,5},{2,10},{6,14},... | collective-permute-start | bytes 49160 | tf_op jit(solution)/shard_map/ppermute | solution.py:627
  50.0 9.0 %collective-permute-start.14 = (bf16[8,64,256]{2,1,0:T(8,128)(2,1)S(1)}, bf16[8,64,256]{2,1,0:T(8,128)(2,1)S(1)}, u32[]{:S(2)}, u32[]{:S(2)}) collective-permute-start(bf16[8,64,256]{2,1,0:T(8,128)(2,1)S(1)} %join_frames.3.refs_1_), channel_id=1, source_target_pairs={{0,1},{1,0},{2,3},{3,2},{4,5},{5,4},{6,7},{7,6},{8,9},{9,8},{10,11... | collective-permute-start | bytes 786440 | tf_op jit(solution)/shard_map/ppermute | solution.py:627
  50.4 9.5 %collective-permute-start.11 = (f32[64,64]{1,0:T(8,128)S(1)}, f32[64,64]{1,0:T(8,128)S(1)}, u32[]{:S(2)}, u32[]{:S(2)}) collective-permute-start(f32[64,64]{1,0:T(8,128)S(1)} %add_terms.7.refs_2_.refs_0_), channel_id=1, source_target_pairs={{0,3},{1,2},{2,1},{3,0},{4,7},{5,6},{6,5},{7,4},{8,11},{9,10},{10,... | collective-permute-start | bytes 49160 | tf_op jit(solution)/shard_map/ppermute | solution.py:627
  52.7 7.2 %collective-permute-start.10 = (f32[64,64]{1,0:T(8,128)S(1)}, f32[64,64]{1,0:T(8,128)S(1)}, u32[]{:S(2)}, u32[]{:S(2)}) collective-permute-start(f32[64,64]{1,0:T(8,128)S(1)} %add_terms.7.refs_2_.refs_0_), channel_id=1, source_target_pairs={{0,2},{1,3},{2,0},{3,1},{4,6},{5,7},{6,4},{7,5},{8,10},{9,11},{10,... | collective-permute-start | bytes 49160 | tf_op jit(solution)/shard_map/ppermute | solution.py:627
  53.6 6.4 %collective-permute-start.9 = (f32[64,64]{1,0:T(8,128)S(1)}, f32[64,64]{1,0:T(8,128)S(1)}, u32[]{:S(2)}, u32[]{:S(2)}) collective-permute-start(f32[64,64]{1,0:T(8,128)S(1)} %add_terms.7.refs_2_.refs_0_), channel_id=1, source_target_pairs={{0,1},{1,0},{2,3},{3,2},{4,5},{5,4},{6,7},{7,6},{8,9},{9,8},{10,11... | collective-permute-start | bytes 49160 | tf_op jit(solution)/shard_map/ppermute | solution.py:627
  61.6 1.4 %collective-permute-start.15 = (f32[64,512]{1,0:T(8,128)S(1)}, f32[64,512]{1,0:T(8,128)S(1)}, u32[]{:S(2)}, u32[]{:S(2)}) collective-permute-start(f32[64,512]{1,0:T(8,128)S(1)} %v_terms.2.refs_12_), channel_id=1, source_target_pairs={{0,4},{4,0},{8,12},{12,8},{1,5},{5,1},{9,13},{13,9},{2,6},{6,2},{1... | collective-permute-start | bytes 393224 | tf_op jit(solution)/shard_map/ppermute | solution.py:627
  63.0 5.6 %collective-permute-start.16 = (f32[64,512]{1,0:T(8,128)S(1)}, f32[64,512]{1,0:T(8,128)S(1)}, u32[]{:S(2)}, u32[]{:S(2)}) collective-permute-start(f32[64,512]{1,0:T(8,128)S(1)} %add_terms.8.a_ref), channel_id=1, source_target_pairs={{0,8},{4,12},{8,0},{12,4},{1,9},{5,13},{9,1},{13,5},{2,10},{6,14},... | collective-permute-start | bytes 393224 | tf_op jit(solution)/shard_map/ppermute | solution.py:627
  68.7 1.7 %collective-permute-start.17 = (f32[64,512]{1,0:T(8,128)S(1)}, f32[64,512]{1,0:T(8,128)S(1)}, u32[]{:S(2)}, u32[]{:S(2)}) collective-permute-start(f32[64,512]{1,0:T(8,128)S(1)} %add_terms.9.terms_ref), channel_id=1, source_target_pairs={{0,4},{4,0},{8,12},{12,8},{1,5},{5,1},{9,13},{13,9},{2,6},{6,2},{1... | collective-permute-start | bytes 393224 | tf_op jit(solution)/shard_map/ppermute | solution.py:627
  72.0 6.1 %collective-permute-start.20 = (f32[64,128]{1,0:T(8,128)S(1)}, f32[64,128]{1,0:T(8,128)S(1)}, u32[]{:S(2)}, u32[]{:S(2)}) collective-permute-start(f32[64,128]{1,0:T(8,128)S(1)} %get-tuple-element.80.refs_0_), channel_id=1, source_target_pairs={{0,3},{1,2},{2,1},{3,0},{4,7},{5,6},{6,5},{7,4},{8,11},{9,10},{10,... | collective-permute-start | bytes 98312 | tf_op jit(solution)/shard_map/ppermute | solution.py:627
  72.9 5.8 %collective-permute-start.19 = (f32[64,128]{1,0:T(8,128)S(1)}, f32[64,128]{1,0:T(8,128)S(1)}, u32[]{:S(2)}, u32[]{:S(2)}) collective-permute-start(f32[64,128]{1,0:T(8,128)S(1)} %get-tuple-element.80.refs_0_), channel_id=1, source_target_pairs={{0,2},{1,3},{2,0},{3,1},{4,6},{5,7},{6,4},{7,5},{8,10},{9,11},{10,... | collective-permute-start | bytes 98312 | tf_op jit(solution)/shard_map/ppermute | solution.py:627
  73.2 5.5 %collective-permute-start.18 = (f32[64,128]{1,0:T(8,128)S(1)}, f32[64,128]{1,0:T(8,128)S(1)}, u32[]{:S(2)}, u32[]{:S(2)}) collective-permute-start(f32[64,128]{1,0:T(8,128)S(1)} %get-tuple-element.80.refs_0_), channel_id=1, source_target_pairs={{0,1},{1,0},{2,3},{3,2},{4,5},{5,4},{6,7},{7,6},{8,9},{9,8},{10,11... | collective-permute-start | bytes 98312 | tf_op jit(solution)/shard_map/ppermute | solution.py:627
  (2 other events, 15.0 us)

commit v20 on v19

--- a/solution.py
+++ b/solution.py
@@ -130,7 +130,7 @@
     coded_ref[pl.ds(end, rows), :] = last.astype(jnp.int32).astype(jnp.int16)
 
 
-def first_projection_kernel(slots, with_gram, place, v_hbm, visits_ref, coded_ref, v_ref, buffers, sems, v_sem):
+def first_projection_kernel(slots, place, v_hbm, visits_ref, coded_ref, v_ref, buffers, sems, v_sem):
     count = buffers.shape[1]
     v_copy = pltpu.make_async_copy(v_hbm, v_ref, v_sem)
     v_copy.start()
@@ -151,22 +151,22 @@
         return low_dot(v_ref[...], buffers[i, p], ROWS_BY_ROWS)
 
     values = [functools.partial(value, i, p) for i in range(len(slots)) for p in range(count)]
-    gram = low_dot(v_ref[...], v_ref[...], ROWS_BY_ROWS) if with_gram else None
+    gram = low_dot(v_ref[...], v_ref[...], ROWS_BY_ROWS)
     encode(values, gram, coded_ref, v_ref.shape[0])
 
 
-def first_projection(slots, count, with_gram, place, visits, v_rows):
+def first_projection(slots, count, place, visits, v_rows):
     width = visits.shape[3]
     rank = v_rows.shape[0]
     return pl.pallas_call(
-        functools.partial(first_projection_kernel, slots, with_gram),
+        functools.partial(first_projection_kernel, slots),
         in_specs=[SMEM_SPEC, HBM_SPEC, HBM_SPEC],
         out_specs=VMEM_SPEC,
-        out_shape=jax.ShapeDtypeStruct(payload_shape(len(slots) * count, rank, visits.shape[2], with_gram), jnp.int16),
+        out_shape=jax.ShapeDtypeStruct(payload_shape(len(slots) * count, rank, visits.shape[2], True), jnp.int16),
         scratch_shapes=[
             pltpu.VMEM(v_rows.shape, BF16),
             pltpu.VMEM((len(slots), count) + visits.shape[2:], BF16),
-            pltpu.SemaphoreType.DMA((len(slots), 2 if count % 2 == 0 else 1)),
+            pltpu.SemaphoreType.DMA((len(slots), 1)),
             pltpu.SemaphoreType.DMA,
         ],
         compiler_params=parameters(LIMIT),
@@ -178,7 +178,7 @@
 def next_projection_kernel(slots, first, count, with_gram, layouts, place, v_ref, visits_ref, *refs):
     coded_ref = refs[-1]
     rank = v_ref.shape[0]
-    arrived = [Payload(ref, layout, count, rank, with_gram) for ref, layout in zip(refs, layouts)]
+    arrived = [Payload(ref, layout, count, rank, carried) for ref, (layout, carried) in zip(refs, layouts)]
 
     def value(slot, p):
         proj = low_dot(v_ref[...], visits_ref[feature_of(place) ^ slot, first + p], ROWS_BY_ROWS)
@@ -239,12 +239,11 @@
 def own_projection_kernel(layout, place, v_ref, visits_ref, arrived_ref, *refs):
     *proj_refs, v_gram_ref = refs
     count, rank, _ = proj_refs[0].shape
-    payload = Payload(arrived_ref, layout, count, rank, len(proj_refs) == 1)
+    payload = Payload(arrived_ref, layout, count, rank, True)
     for p in range(visits_ref.shape[1]):
         proj = low_dot(v_ref[...], visits_ref[feature_of(place), p], ROWS_BY_ROWS)
         proj_refs[p // count][p % count] = proj + payload.proj(0, p) if p < count else proj
-    gram = low_dot(v_ref[...], v_ref[...], ROWS_BY_ROWS)
-    v_gram_ref[...] = gram + payload.gram() if payload.with_gram else gram
+    v_gram_ref[...] = low_dot(v_ref[...], v_ref[...], ROWS_BY_ROWS) + payload.gram()
 
 
 def project_own(n_parts, layout, place, visits, v_rows, arrived):
@@ -355,8 +354,8 @@
     first = feature_of(place) * share + part * count
     pieces = [own_ref[p] for p in patients]
     v_gram = v_gram_ref[...]
-    for code, layout in zip(coded, layouts):
-        payload = Payload(code, layout, count, rank, (part + 1) * count == share)
+    for code, (layout, carried) in zip(coded, layouts):
+        payload = Payload(code, layout, count, rank, carried)
         pieces = [pieces[p] + payload.proj(0, p) for p in patients]
         if payload.with_gram:
             v_gram = v_gram + payload.gram()
@@ -690,22 +689,32 @@
 
     w_gram, spread = spread_w(place, w_start, n)
     w_grams = staged_terms(w_gram, "patient", [])
+    def layouts(stages, part):
+        return [(receive(bit), part == 0) for bit in bits[:stages]]
+
     arrived = [[] for _ in firsts]
     for i, bit in enumerate(bits):
-        layouts = [receive(before) for before in bits[:i]]
         for part, first in enumerate(firsts):
             if i == 0 and part == 0:
-                code = first_projection(send(bit), count, n_parts == 1, place, in_hbm, v_rows)
+                code = first_projection(send(bit), count, place, in_hbm, v_rows)
             else:
                 after = [w_grams[part]] + [v_gram] * part if i else []
                 code = next_projection(
-                    send(bit), first, count, part == n_parts - 1, layouts, place, by_owner, v_near, arrived[part], after
+                    send(bit),
+                    first,
+                    count,
+                    part == 0,
+                    layouts(i, part),
+                    place,
+                    by_owner,
+                    v_near,
+                    arrived[part],
+                    after,
                 )
             arrived[part] = arrived[part] + [swap(code, "feature", bit)]
         if i == 0:
             own, v_gram = project_own(n_parts, receive(bit), place, by_owner, v_near, arrived[0][0])
 
-    layouts = [receive(bit) for bit in bits]
     frames = [[] for _ in firsts]
     joined = []
 
@@ -723,7 +732,7 @@
     h_local = v_gram
     for part, first in enumerate(firsts):
         low, h_local, v_total = own_frames(
-            layouts[part == 0 :],
+            layouts(len(bits), part)[part == 0 :],
             part,
             n_parts,
             place,
@@ -746,10 +755,10 @@
     projected, token = project_groups(first_groups, joined)
     h_sums = staged_terms(h_local, "patient", [token])
     w_gram, inverse = first_inverse(v_gram, w_grams, h_sums[0])
-    h_sum = add(*h_sums, [inverse])
-    joined = double(n_parts - 1, [h_sum] + [frames[part][k][1] for part, k in early])
+    joined = double(n_parts - 1, [inverse])
+    h_sum = add(*h_sums, joined + [frames[part][k][1] for part, k in early])
     h_terms = all_terms(h_sum, "feature")
-    after = joined
+    after = [h_sum]
     for groups in [early] + [[(n_parts - 1, k)] for k in range(1, last + 1)]:
         if groups:
             more, token = project_groups(groups, after)

time: 81.1 us -> 84.9 us (1.047)
  starting transfers between devices: 28.2 us -> 35.1 us
  waiting for transfers between devices: 14.2 us -> 11.4 us
    ppermute x21, starting transfers between devices: 28.2 us -> 35.1 us  [swap(): return lax.ppermute(x, axis, pairs)]
    ppermute x21, waiting for transfers between devices: 14.2 us -> 11.4 us  [swap(): return lax.ppermute(x, axis, pairs)]
  transfers between devices with their start and end apart: 21 -> 21, of which waited for: 11 -> 10; matrix products, arithmetic and copies ran while one was open for 0% -> 0% of each run, Pallas kernels for 34% -> 33%
where the time goes in v20:
time: 84.9 us; the launch traced here: 84.8 us
  Pallas kernels  37.3 us (44%)
  starting transfers between devices  35.1 us (41%)
  waiting for transfers between devices  11.4 us (13%)
  between operations  0.86 us (1%)
    ppermute x21, starting transfers between devices, swap(): return lax.ppermute(x, axis, pairs)  35.1 us
    pallas_call x2, Pallas kernels, own_frames(): pl.pallas_call(functools.partial(frames_kernel, layouts, part, share), in...  11.9 us
    ppermute x21, waiting for transfers between devices, swap(): return lax.ppermute(x, axis, pairs)  11.4 us
    pallas_call x1, Pallas kernels, first_projection(): pl.pallas_call(functools.partial(first_projection_kernel, slots), in_spec...  3.91 us
    pallas_call x3, Pallas kernels, next_projection(): pl.pallas_call(functools.partial(next_projection_kernel, slots, first, co...  3.5 us
    pallas_call x4, Pallas kernels, project_frames(): pl.pallas_call(functools.partial(projected_kernel, items), in_specs=[SMEM...  3.49 us
    pallas_call x2, Pallas kernels, half_v(): pl.pallas_call(functools.partial(next_v_kernel, items, share, bool(before...  3.24 us
    pallas_call x1, Pallas kernels, next_w(): pl.pallas_call(functools.partial(next_w_kernel, len(sums)), in_specs=[VME...  2.27 us
  transfers between devices with their start and end apart: 21, of which 10 were waited for; matrix products, arithmetic and copies ran while one was open for 0% of the time, Pallas kernels for 33%

profile of v20, /device:TPU:0, one launch (start us, length us, event | category | flops | bytes accessed | tf_op | source)
XLA Modules:
  0.0 84.8 jit_solution(15988183083319019461)
XLA Ops:
  0.7 3.9 %project_first.1 = s16[560,256]{1,0:T(8,128)(2,1)S(1)} custom-call(s32[1]{0:T(128)} %bitcast.place, bf16[64,1024]{1,0:T(8,128)(2,1)} %bitcast.13, bf16[4,8,256,1024]{3,2,1,0:T(8,128)(2,1)} %bitcast.4), custom_call_target="tpu_custom_call" | custom-call | flops 1000 | bytes 1000 | tf_op jit(solution)/shard_map/project_first/pallas_call | solution.py:161
  4.6 3.0 %collective-permute-start = (s16[560,256]{1,0:T(8,128)(2,1)S(1)}, s16[560,256]{1,0:T(8,128)(2,1)S(1)}, u32[]{:S(2)}, u32[]{:S(2)}) collective-permute-start(s16[560,256]{1,0:T(8,128)(2,1)S(1)} %project_first.1), channel_id=1, source_target_pairs={{0,1},{1,0},{2,3},{3,2},{4,5},{5,4},{6,7},{7,6},{8,9},{9,8},{10,11... | collective-permute-start | bytes 860168 | tf_op jit(solution)/shard_map/ppermute | solution.py:626
  7.8 1.6 %project_next.4 = s16[528,256]{1,0:T(8,128)(2,1)S(1)} custom-call(s32[1]{0:T(128)} %bitcast.place, bf16[64,1024]{1,0:T(8,128)(2,1)S(1)} %bitcast.14, bf16[4,8,256,1024]{3,2,1,0:T(8,128)(2,1)S(1)} %bitcast.5), custom_call_target="tpu_custom_call" | custom-call | flops 1000 | bytes 1000 | tf_op jit(solution)/shard_map/project_next/pallas_call | solution.py:199
  9.4 3.1 %collective-permute-start.3 = (s16[528,256]{1,0:T(8,128)(2,1)S(1)}, s16[528,256]{1,0:T(8,128)(2,1)S(1)}, u32[]{:S(2)}, u32[]{:S(2)}) collective-permute-start(s16[528,256]{1,0:T(8,128)(2,1)S(1)} %project_next.4), channel_id=1, source_target_pairs={{0,1},{1,0},{2,3},{3,2},{4,5},{5,4},{6,7},{7,6},{8,9},{9,8},{10,11... | collective-permute-start | bytes 811016 | tf_op jit(solution)/shard_map/ppermute | solution.py:626
  16.3 3.3 %collective-permute-start.2 = (s16[304,256]{1,0:T(8,128)(2,1)S(1)}, s16[304,256]{1,0:T(8,128)(2,1)S(1)}, u32[]{:S(2)}, u32[]{:S(2)}) collective-permute-start(s16[304,256]{1,0:T(8,128)(2,1)S(1)} %project_next.3), channel_id=1, source_target_pairs={{0,2},{1,3},{2,0},{3,1},{4,6},{5,7},{6,4},{7,5},{8,10},{9,11},{10,... | collective-permute-start | bytes 466952 | tf_op jit(solution)/shard_map/ppermute | solution.py:626
  19.6 1.5 %collective-permute-start.4 = (f32[64,64]{1,0:T(8,128)S(1)}, f32[64,64]{1,0:T(8,128)S(1)}, u32[]{:S(2)}, u32[]{:S(2)}) collective-permute-start(f32[64,64]{1,0:T(8,128)S(1)} %add_terms.5.refs_1_.refs_0_), channel_id=1, source_target_pairs={{0,8},{4,12},{8,0},{12,4},{1,9},{5,13},{9,1},{13,5},{2,10},{6,14},... | collective-permute-start | bytes 49160 | tf_op jit(solution)/shard_map/ppermute | solution.py:626
  21.1 1.4 %project_own.1 = (f32[4,64,256]{2,1,0:T(8,128)S(1)}, f32[4,64,256]{2,1,0:T(8,128)S(1)}, f32[64,64]{1,0:T(8,128)S(1)}) custom-call(s32[1]{0:T(128)} %bitcast.place, bf16[64,1024]{1,0:T(8,128)(2,1)S(1)} %bitcast.16, bf16[4,8,256,1024]{3,2,1,0:T(8,128)(2,1)S(1)} %bitcast.7, s16[560,256]{1,0:T(8,128)(2,1)S(1)} %collective-permute-done.arrived_ref.refs_0_), custom_call_target="tpu_custom_call" | custom-call | flops 1000 | bytes 1000 | tf_op jit(solution)/shard_map/project_own/pallas_call | solution.py:253
  26.2 6.0 %own_frames.2 = (bf16[4,64,256]{2,1,0:T(8,128)(2,1)S(1)}, f32[64,64]{1,0:T(8,128)S(1)}, f32[64,64]{1,0:T(8,128)S(1)}) custom-call(s32[1]{0:T(128)} %bitcast.place, s32[32]{0:T(128)S(1)} %copy-done.4, f32[64,64]{1,0:T(8,128)S(1)} %copy-done.3, f32[32,64]{1,0:T(8,128)S(1)} %copy-done.2, f32[64,64]{1,0:T(8,128)S(1)} %get-tuple-element.43.v_gram_ref.before_ref.refs_2_, ...), custom_call_target="tpu_custom_call" | custom-call | flops 1000 | bytes 1000 | tf_op jit(solution)/shard_map/own_frames/pallas_call | solution.py:394
  32.1 1.3 %collective-permute-start.7 = (bf16[4,64,256]{2,1,0:T(8,128)(2,1)S(1)}, bf16[4,64,256]{2,1,0:T(8,128)(2,1)S(1)}, u32[]{:S(2)}, u32[]{:S(2)}) collective-permute-start(bf16[4,64,256]{2,1,0:T(8,128)(2,1)S(1)} %get-tuple-element.50.refs_0_), channel_id=1, source_target_pairs={{0,2},{1,3},{2,0},{3,1},{4,6},{5,7},{6,4},{7,5},{8,10},{9,11},{10,... | collective-permute-start | bytes 393224 | tf_op jit(solution)/shard_map/ppermute | solution.py:626
  33.5 6.0 %own_frames.3 = (bf16[4,64,256]{2,1,0:T(8,128)(2,1)S(1)}, f32[64,64]{1,0:T(8,128)S(1)}, f32[64,64]{1,0:T(8,128)S(1)}) custom-call(s32[1]{0:T(128)} %bitcast.place, s32[32]{0:T(128)S(1)} %copy-done.4, f32[64,64]{1,0:T(8,128)S(1)} %copy-done.3, f32[32,64]{1,0:T(8,128)S(1)} %copy-done.2, f32[64,64]{1,0:T(8,128)S(1)} %get-tuple-element.46.v_gram_ref, ...), custom_call_target="tpu_custom_call" | custom-call | flops 1000 | bytes 1000 | tf_op jit(solution)/shard_map/own_frames/pallas_call | solution.py:394
  39.4 1.7 %collective-permute-start.9 = (bf16[4,64,256]{2,1,0:T(8,128)(2,1)S(1)}, bf16[4,64,256]{2,1,0:T(8,128)(2,1)S(1)}, u32[]{:S(2)}, u32[]{:S(2)}) collective-permute-start(bf16[4,64,256]{2,1,0:T(8,128)(2,1)S(1)} %get-tuple-element.51.refs_2_.refs_1_.refs_0_), channel_id=1, source_target_pairs={{0,2},{1,3},{2,0},{3,1},{4,6},{5,7},{6,4},{7,5},{8,10},{9,11},{10,... | collective-permute-start | bytes 393224 | tf_op jit(solution)/shard_map/ppermute | solution.py:626
  41.2 4.0 %collective-permute-start.10 = (bf16[8,64,256]{2,1,0:T(8,128)(2,1)S(1)}, bf16[8,64,256]{2,1,0:T(8,128)(2,1)S(1)}, u32[]{:S(2)}, u32[]{:S(2)}) collective-permute-start(bf16[8,64,256]{2,1,0:T(8,128)(2,1)S(1)} %join_frames.2.refs_3_), channel_id=1, source_target_pairs={{0,1},{1,0},{2,3},{3,2},{4,5},{5,4},{6,7},{7,6},{8,9},{9,8},{10,11... | collective-permute-start | bytes 786440 | tf_op jit(solution)/shard_map/ppermute | solution.py:626
  46.4 1.7 %first_inverse.1 = (f32[64,64]{1,0:T(8,128)S(1)}, f32[64,64]{1,0:T(8,128)S(1)}) custom-call(f32[64,64]{1,0:T(8,128)S(1)} %get-tuple-element.53.v_gram_ref, f32[64,64]{1,0:T(8,128)S(1)} %add_terms.5.refs_1_.refs_0_, f32[64,64]{1,0:T(8,128)S(1)} %collective-permute-done.4.refs_1_, f32[64,64]{1,0:T(8,128)S(1)} %add_terms.6.refs_2_.a_ref), custom_call_target="tpu_custom_call" | custom-call | flops 1000 | bytes 1000 | tf_op jit(solution)/shard_map/first_inverse/pallas_call | solution.py:321
  48.2 4.1 %collective-permute-start.14 = (bf16[8,64,256]{2,1,0:T(8,128)(2,1)S(1)}, bf16[8,64,256]{2,1,0:T(8,128)(2,1)S(1)}, u32[]{:S(2)}, u32[]{:S(2)}) collective-permute-start(bf16[8,64,256]{2,1,0:T(8,128)(2,1)S(1)} %join_frames.3.refs_0_), channel_id=1, source_target_pairs={{0,1},{1,0},{2,3},{3,2},{4,5},{5,4},{6,7},{7,6},{8,9},{9,8},{10,11... | collective-permute-start | bytes 786440 | tf_op jit(solution)/shard_map/ppermute | solution.py:626
  52.3 1.5 %collective-permute-start.8 = (f32[64,64]{1,0:T(8,128)S(1)}, f32[64,64]{1,0:T(8,128)S(1)}, u32[]{:S(2)}, u32[]{:S(2)}) collective-permute-start(f32[64,64]{1,0:T(8,128)S(1)} %add_terms.6.refs_2_.a_ref), channel_id=1, source_target_pairs={{0,8},{4,12},{8,0},{12,4},{1,9},{5,13},{9,1},{13,5},{2,10},{6,14},... | collective-permute-start | bytes 49160 | tf_op jit(solution)/shard_map/ppermute | solution.py:626
  53.8 2.4 %collective-permute-done.8.b_ref = f32[64,64]{1,0:T(8,128)S(1)} collective-permute-done((f32[64,64]{1,0:T(8,128)S(1)}, f32[64,64]{1,0:T(8,128)S(1)}, u32[]{:S(2)}, u32[]{:S(2)}) %collective-permute-start.8) | collective-permute-done | bytes 16416 | tf_op jit(solution)/shard_map/ppermute | solution.py:626
  57.9 2.8 %collective-permute-start.11 = (f32[64,64]{1,0:T(8,128)S(1)}, f32[64,64]{1,0:T(8,128)S(1)}, u32[]{:S(2)}, u32[]{:S(2)}) collective-permute-start(f32[64,64]{1,0:T(8,128)S(1)} %add_terms.7.refs_1_.refs_0_), channel_id=1, source_target_pairs={{0,1},{1,0},{2,3},{3,2},{4,5},{5,4},{6,7},{7,6},{8,9},{9,8},{10,11... | collective-permute-start | bytes 49160 | tf_op jit(solution)/shard_map/ppermute | solution.py:626
  66.1 1.6 %collective-permute-start.16 = (f32[64,512]{1,0:T(8,128)S(1)}, f32[64,512]{1,0:T(8,128)S(1)}, u32[]{:S(2)}, u32[]{:S(2)}) collective-permute-start(f32[64,512]{1,0:T(8,128)S(1)} %add_terms.8.a_ref), channel_id=1, source_target_pairs={{0,8},{4,12},{8,0},{12,4},{1,9},{5,13},{9,1},{13,5},{2,10},{6,14},... | collective-permute-start | bytes 393224 | tf_op jit(solution)/shard_map/ppermute | solution.py:626
  67.6 1.7 %second_inverse.1 = (f32[64,64]{1,0:T(8,128)S(1)}, f32[64,64]{1,0:T(8,128)S(1)}) custom-call(f32[64,64]{1,0:T(8,128)S(1)} %get-tuple-element.73.h_ref, f32[64,64]{1,0:T(8,128)S(1)} %get-tuple-element.74.w_gram_ref), custom_call_target="tpu_custom_call" | custom-call | flops 1000 | bytes 1000 | tf_op jit(solution)/shard_map/second_inverse/pallas_call | solution.py:500
  69.3 2.4 %collective-permute-done.16.b_ref = f32[64,512]{1,0:T(8,128)S(1)} collective-permute-done((f32[64,512]{1,0:T(8,128)S(1)}, f32[64,512]{1,0:T(8,128)S(1)}, u32[]{:S(2)}, u32[]{:S(2)}) %collective-permute-start.16) | collective-permute-done | bytes 131104 | tf_op jit(solution)/shard_map/ppermute | solution.py:626
  71.8 1.6 %next_v.2 = (f32[64,512]{1,0:T(8,128)S(1)}, f32[64,128]{1,0:T(8,128)S(1)}) custom-call(s32[1]{0:T(128)} %bitcast.place, f32[64,512]{1,0:T(8,128)S(1)} %add_terms.9.terms_ref, f32[64,64]{1,0:T(8,128)S(1)} %get-tuple-element.75.refs_0_.inverse_ref, f32[64,64]{1,0:T(8,128)S(1)} %get-tuple-element.73.h_ref, bf16[256,1024]{1,0:T(8,128)(2,1)S(1)} %get-tuple-element.61.refs_0_, ...), custom_call_target="tpu_custom_call" | custom-call | flops 1000 | bytes 1000 | tf_op jit(solution)/shard_map/next_v/pallas_call | solution.py:567
  73.4 1.6 %next_v.3 = (f32[64,512]{1,0:T(8,128)S(1)}, f32[64,128]{1,0:T(8,128)S(1)}) custom-call(s32[1]{0:T(128)} %bitcast.place, f32[64,512]{1,0:T(8,128)S(1)} %collective-permute-done.17.terms_ref, f32[64,64]{1,0:T(8,128)S(1)} %get-tuple-element.75.refs_0_.inverse_ref, f32[64,64]{1,0:T(8,128)S(1)} %get-tuple-element.73.h_ref, ...), custom_call_target="tpu_custom_call" | custom-call | flops 1000 | bytes 1000 | tf_op jit(solution)/shard_map/next_v/pallas_call | solution.py:567
  75.1 2.1 %collective-permute-start.20 = (f32[64,128]{1,0:T(8,128)S(1)}, f32[64,128]{1,0:T(8,128)S(1)}, u32[]{:S(2)}, u32[]{:S(2)}) collective-permute-start(f32[64,128]{1,0:T(8,128)S(1)} %get-tuple-element.80.refs_0_), channel_id=1, source_target_pairs={{0,3},{1,2},{2,1},{3,0},{4,7},{5,6},{6,5},{7,4},{8,11},{9,10},{10,... | collective-permute-start | bytes 98312 | tf_op jit(solution)/shard_map/ppermute | solution.py:626
  82.5 2.3 %next_w.1 = f32[32,64]{1,0:T(8,128)} custom-call(f32[64,128]{1,0:T(8,128)S(1)} %get-tuple-element.80.refs_0_, f32[64,128]{1,0:T(8,128)S(1)} %collective-permute-done.18.refs_1_, f32[64,128]{1,0:T(8,128)S(1)} %collective-permute-done.19.refs_2_, f32[64,128]{1,0:T(8,128)S(1)} %collective-permute-done.20.refs_3_, f32[64,64]{1,0:T(8,128)S(1)} %get-tuple-element.81.refs_4_, ...), custom_call_target="tpu_custom_call" | custom-call | flops 1000 | bytes 1000 | tf_op jit(solution)/shard_map/next_w/pallas_call | solution.py:613
  (56 shorter events, 21.4 us)
Async XLA Ops:
  0.7 11.8 %copy-start.2 = (f32[32,64]{1,0:T(8,128)S(1)}, f32[32,64]{1,0:T(8,128)}, u32[]{:S(2)}) copy-start(f32[32,64]{1,0:T(8,128)} %w_ref.5) | copy-start | bytes 24580
  4.6 10.7 %collective-permute-start = (s16[560,256]{1,0:T(8,128)(2,1)S(1)}, s16[560,256]{1,0:T(8,128)(2,1)S(1)}, u32[]{:S(2)}, u32[]{:S(2)}) collective-permute-start(s16[560,256]{1,0:T(8,128)(2,1)S(1)} %project_first.1), channel_id=1, source_target_pairs={{0,1},{1,0},{2,3},{3,2},{4,5},{5,4},{6,7},{7,6},{8,9},{9,8},{10,11... | collective-permute-start | bytes 860168 | tf_op jit(solution)/shard_map/ppermute | solution.py:626
  9.4 14.2 %collective-permute-start.3 = (s16[528,256]{1,0:T(8,128)(2,1)S(1)}, s16[528,256]{1,0:T(8,128)(2,1)S(1)}, u32[]{:S(2)}, u32[]{:S(2)}) collective-permute-start(s16[528,256]{1,0:T(8,128)(2,1)S(1)} %project_next.4), channel_id=1, source_target_pairs={{0,1},{1,0},{2,3},{3,2},{4,5},{5,4},{6,7},{7,6},{8,9},{9,8},{10,11... | collective-permute-start | bytes 811016 | tf_op jit(solution)/shard_map/ppermute | solution.py:626
  13.2 1.3 %collective-permute-start.1 = (f32[64,64]{1,0:T(8,128)S(1)}, f32[64,64]{1,0:T(8,128)S(1)}, u32[]{:S(2)}, u32[]{:S(2)}) collective-permute-start(f32[64,64]{1,0:T(8,128)S(1)} %get-tuple-element.45.a_ref), channel_id=1, source_target_pairs={{0,4},{4,0},{8,12},{12,8},{1,5},{5,1},{9,13},{13,9},{2,6},{6,2},{1... | collective-permute-start | bytes 49160 | tf_op jit(solution)/shard_map/ppermute | solution.py:626
  16.3 9.9 %copy-start.3 = (f32[64,64]{1,0:T(8,128)S(1)}, f32[64,64]{1,0:T(8,128)}, u32[]{:S(2)}) copy-start(f32[64,64]{1,0:T(8,128)} %h_ref.3) | copy-start | bytes 49156
  16.3 9.9 %copy-start.4 = (s32[32]{0:T(128)S(1)}, s32[32]{0:T(128)}, u32[]{:S(2)}) copy-start(s32[32]{0:T(128)} %counts_ref.3) | copy-start | bytes 388
  16.3 9.9 %collective-permute-start.2 = (s16[304,256]{1,0:T(8,128)(2,1)S(1)}, s16[304,256]{1,0:T(8,128)(2,1)S(1)}, u32[]{:S(2)}, u32[]{:S(2)}) collective-permute-start(s16[304,256]{1,0:T(8,128)(2,1)S(1)} %project_next.3), channel_id=1, source_target_pairs={{0,2},{1,3},{2,0},{3,1},{4,6},{5,7},{6,4},{7,5},{8,10},{9,11},{10,... | collective-permute-start | bytes 466952 | tf_op jit(solution)/shard_map/ppermute | solution.py:626
  19.6 3.9 %collective-permute-start.4 = (f32[64,64]{1,0:T(8,128)S(1)}, f32[64,64]{1,0:T(8,128)S(1)}, u32[]{:S(2)}, u32[]{:S(2)}) collective-permute-start(f32[64,64]{1,0:T(8,128)S(1)} %add_terms.5.refs_1_.refs_0_), channel_id=1, source_target_pairs={{0,8},{4,12},{8,0},{12,4},{1,9},{5,13},{9,1},{13,5},{2,10},{6,14},... | collective-permute-start | bytes 49160 | tf_op jit(solution)/shard_map/ppermute | solution.py:626
  24.5 9.0 %collective-permute-start.5 = (s16[272,256]{1,0:T(8,128)(2,1)S(1)}, s16[272,256]{1,0:T(8,128)(2,1)S(1)}, u32[]{:S(2)}, u32[]{:S(2)}) collective-permute-start(s16[272,256]{1,0:T(8,128)(2,1)S(1)} %project_next.5), channel_id=1, source_target_pairs={{0,2},{1,3},{2,0},{3,1},{4,6},{5,7},{6,4},{7,5},{8,10},{9,11},{10,... | collective-permute-start | bytes 417800 | tf_op jit(solution)/shard_map/ppermute | solution.py:626
  32.1 9.0 %collective-permute-start.7 = (bf16[4,64,256]{2,1,0:T(8,128)(2,1)S(1)}, bf16[4,64,256]{2,1,0:T(8,128)(2,1)S(1)}, u32[]{:S(2)}, u32[]{:S(2)}) collective-permute-start(bf16[4,64,256]{2,1,0:T(8,128)(2,1)S(1)} %get-tuple-element.50.refs_0_), channel_id=1, source_target_pairs={{0,2},{1,3},{2,0},{3,1},{4,6},{5,7},{6,4},{7,5},{8,10},{9,11},{10,... | collective-permute-start | bytes 393224 | tf_op jit(solution)/shard_map/ppermute | solution.py:626
  39.4 8.7 %collective-permute-start.9 = (bf16[4,64,256]{2,1,0:T(8,128)(2,1)S(1)}, bf16[4,64,256]{2,1,0:T(8,128)(2,1)S(1)}, u32[]{:S(2)}, u32[]{:S(2)}) collective-permute-start(bf16[4,64,256]{2,1,0:T(8,128)(2,1)S(1)} %get-tuple-element.51.refs_2_.refs_1_.refs_0_), channel_id=1, source_target_pairs={{0,2},{1,3},{2,0},{3,1},{4,6},{5,7},{6,4},{7,5},{8,10},{9,11},{10,... | collective-permute-start | bytes 393224 | tf_op jit(solution)/shard_map/ppermute | solution.py:626
  41.1 5.3 %collective-permute-start.6 = (f32[64,64]{1,0:T(8,128)S(1)}, f32[64,64]{1,0:T(8,128)S(1)}, u32[]{:S(2)}, u32[]{:S(2)}) collective-permute-start(f32[64,64]{1,0:T(8,128)S(1)} %get-tuple-element.49.a_ref), channel_id=1, source_target_pairs={{0,4},{4,0},{8,12},{12,8},{1,5},{5,1},{9,13},{13,9},{2,6},{6,2},{1... | collective-permute-start | bytes 49160 | tf_op jit(solution)/shard_map/ppermute | solution.py:626
  41.2 15.1 %collective-permute-start.10 = (bf16[8,64,256]{2,1,0:T(8,128)(2,1)S(1)}, bf16[8,64,256]{2,1,0:T(8,128)(2,1)S(1)}, u32[]{:S(2)}, u32[]{:S(2)}) collective-permute-start(bf16[8,64,256]{2,1,0:T(8,128)(2,1)S(1)} %join_frames.2.refs_3_), channel_id=1, source_target_pairs={{0,1},{1,0},{2,3},{3,2},{4,5},{5,4},{6,7},{7,6},{8,9},{9,8},{10,11... | collective-permute-start | bytes 786440 | tf_op jit(solution)/shard_map/ppermute | solution.py:626
  48.2 13.9 %collective-permute-start.14 = (bf16[8,64,256]{2,1,0:T(8,128)(2,1)S(1)}, bf16[8,64,256]{2,1,0:T(8,128)(2,1)S(1)}, u32[]{:S(2)}, u32[]{:S(2)}) collective-permute-start(bf16[8,64,256]{2,1,0:T(8,128)(2,1)S(1)} %join_frames.3.refs_0_), channel_id=1, source_target_pairs={{0,1},{1,0},{2,3},{3,2},{4,5},{5,4},{6,7},{7,6},{8,9},{9,8},{10,11... | collective-permute-start | bytes 786440 | tf_op jit(solution)/shard_map/ppermute | solution.py:626
  52.3 3.9 %collective-permute-start.8 = (f32[64,64]{1,0:T(8,128)S(1)}, f32[64,64]{1,0:T(8,128)S(1)}, u32[]{:S(2)}, u32[]{:S(2)}) collective-permute-start(f32[64,64]{1,0:T(8,128)S(1)} %add_terms.6.refs_2_.a_ref), channel_id=1, source_target_pairs={{0,8},{4,12},{8,0},{12,4},{1,9},{5,13},{9,1},{13,5},{2,10},{6,14},... | collective-permute-start | bytes 49160 | tf_op jit(solution)/shard_map/ppermute | solution.py:626
  56.3 6.7 %collective-permute-start.13 = (f32[64,64]{1,0:T(8,128)S(1)}, f32[64,64]{1,0:T(8,128)S(1)}, u32[]{:S(2)}, u32[]{:S(2)}) collective-permute-start(f32[64,64]{1,0:T(8,128)S(1)} %add_terms.7.refs_1_.refs_0_), channel_id=1, source_target_pairs={{0,3},{1,2},{2,1},{3,0},{4,7},{5,6},{6,5},{7,4},{8,11},{9,10},{10,... | collective-permute-start | bytes 49160 | tf_op jit(solution)/shard_map/ppermute | solution.py:626
  56.8 6.2 %collective-permute-start.12 = (f32[64,64]{1,0:T(8,128)S(1)}, f32[64,64]{1,0:T(8,128)S(1)}, u32[]{:S(2)}, u32[]{:S(2)}) collective-permute-start(f32[64,64]{1,0:T(8,128)S(1)} %add_terms.7.refs_1_.refs_0_), channel_id=1, source_target_pairs={{0,2},{1,3},{2,0},{3,1},{4,6},{5,7},{6,4},{7,5},{8,10},{9,11},{10,... | collective-permute-start | bytes 49160 | tf_op jit(solution)/shard_map/ppermute | solution.py:626
  57.9 5.1 %collective-permute-start.11 = (f32[64,64]{1,0:T(8,128)S(1)}, f32[64,64]{1,0:T(8,128)S(1)}, u32[]{:S(2)}, u32[]{:S(2)}) collective-permute-start(f32[64,64]{1,0:T(8,128)S(1)} %add_terms.7.refs_1_.refs_0_), channel_id=1, source_target_pairs={{0,1},{1,0},{2,3},{3,2},{4,5},{5,4},{6,7},{7,6},{8,9},{9,8},{10,11... | collective-permute-start | bytes 49160 | tf_op jit(solution)/shard_map/ppermute | solution.py:626
  64.7 1.4 %collective-permute-start.15 = (f32[64,512]{1,0:T(8,128)S(1)}, f32[64,512]{1,0:T(8,128)S(1)}, u32[]{:S(2)}, u32[]{:S(2)}) collective-permute-start(f32[64,512]{1,0:T(8,128)S(1)} %v_terms.2.refs_12_), channel_id=1, source_target_pairs={{0,4},{4,0},{8,12},{12,8},{1,5},{5,1},{9,13},{13,9},{2,6},{6,2},{1... | collective-permute-start | bytes 393224 | tf_op jit(solution)/shard_map/ppermute | solution.py:626
  66.1 5.6 %collective-permute-start.16 = (f32[64,512]{1,0:T(8,128)S(1)}, f32[64,512]{1,0:T(8,128)S(1)}, u32[]{:S(2)}, u32[]{:S(2)}) collective-permute-start(f32[64,512]{1,0:T(8,128)S(1)} %add_terms.8.a_ref), channel_id=1, source_target_pairs={{0,8},{4,12},{8,0},{12,4},{1,9},{5,13},{9,1},{13,5},{2,10},{6,14},... | collective-permute-start | bytes 393224 | tf_op jit(solution)/shard_map/ppermute | solution.py:626
  71.7 1.7 %collective-permute-start.17 = (f32[64,512]{1,0:T(8,128)S(1)}, f32[64,512]{1,0:T(8,128)S(1)}, u32[]{:S(2)}, u32[]{:S(2)}) collective-permute-start(f32[64,512]{1,0:T(8,128)S(1)} %add_terms.9.terms_ref), channel_id=1, source_target_pairs={{0,4},{4,0},{8,12},{12,8},{1,5},{5,1},{9,13},{13,9},{2,6},{6,2},{1... | collective-permute-start | bytes 393224 | tf_op jit(solution)/shard_map/ppermute | solution.py:626
  75.1 6.1 %collective-permute-start.20 = (f32[64,128]{1,0:T(8,128)S(1)}, f32[64,128]{1,0:T(8,128)S(1)}, u32[]{:S(2)}, u32[]{:S(2)}) collective-permute-start(f32[64,128]{1,0:T(8,128)S(1)} %get-tuple-element.80.refs_0_), channel_id=1, source_target_pairs={{0,3},{1,2},{2,1},{3,0},{4,7},{5,6},{6,5},{7,4},{8,11},{9,10},{10,... | collective-permute-start | bytes 98312 | tf_op jit(solution)/shard_map/ppermute | solution.py:626
  77.1 5.1 %collective-permute-start.19 = (f32[64,128]{1,0:T(8,128)S(1)}, f32[64,128]{1,0:T(8,128)S(1)}, u32[]{:S(2)}, u32[]{:S(2)}) collective-permute-start(f32[64,128]{1,0:T(8,128)S(1)} %get-tuple-element.80.refs_0_), channel_id=1, source_target_pairs={{0,2},{1,3},{2,0},{3,1},{4,6},{5,7},{6,4},{7,5},{8,10},{9,11},{10,... | collective-permute-start | bytes 98312 | tf_op jit(solution)/shard_map/ppermute | solution.py:626
  78.2 4.3 %collective-permute-start.18 = (f32[64,128]{1,0:T(8,128)S(1)}, f32[64,128]{1,0:T(8,128)S(1)}, u32[]{:S(2)}, u32[]{:S(2)}) collective-permute-start(f32[64,128]{1,0:T(8,128)S(1)} %get-tuple-element.80.refs_0_), channel_id=1, source_target_pairs={{0,1},{1,0},{2,3},{3,2},{4,5},{5,4},{6,7},{7,6},{8,9},{9,8},{10,11... | collective-permute-start | bytes 98312 | tf_op jit(solution)/shard_map/ppermute | solution.py:626
  (2 other events, 14.1 us)

commit v21 on v19

--- a/solution.py
+++ b/solution.py
@@ -166,7 +166,7 @@
         scratch_shapes=[
             pltpu.VMEM(v_rows.shape, BF16),
             pltpu.VMEM((len(slots), count) + visits.shape[2:], BF16),
-            pltpu.SemaphoreType.DMA((len(slots), 2 if count % 2 == 0 else 1)),
+            pltpu.SemaphoreType.DMA((len(slots), 1)),
             pltpu.SemaphoreType.DMA,
         ],
         compiler_params=parameters(LIMIT),

time: 81.1 us -> 81.2 us (level)
  starting transfers between devices: 28.2 us -> 30.5 us
  waiting for transfers between devices: 14.2 us -> 12.1 us
    ppermute x21, starting transfers between devices: 28.2 us -> 30.5 us  [swap(): return lax.ppermute(x, axis, pairs)]
    ppermute x21, waiting for transfers between devices: 14.2 us -> 12.1 us  [swap(): return lax.ppermute(x, axis, pairs)]
  transfers between devices with their start and end apart: 21 -> 21, of which waited for: 11 -> 12; matrix products, arithmetic and copies ran while one was open for 0% -> 0% of each run, Pallas kernels for 34% -> 34%
where the time goes in v21:
time: 81.2 us; the launch traced here: 81.1 us
  Pallas kernels  37.2 us (46%)
  starting transfers between devices  30.5 us (38%)
  waiting for transfers between devices  12.1 us (15%)
  between operations  0.84 us (1%)
    ppermute x21, starting transfers between devices, swap(): return lax.ppermute(x, axis, pairs)  30.5 us
    ppermute x21, waiting for transfers between devices, swap(): return lax.ppermute(x, axis, pairs)  12.1 us
    pallas_call x2, Pallas kernels, own_frames(): pl.pallas_call(functools.partial(frames_kernel, layouts, part, share), in...  12 us
    pallas_call x1, Pallas kernels, first_projection(): pl.pallas_call(functools.partial(first_projection_kernel, slots, with_gra...  3.73 us
    pallas_call x3, Pallas kernels, next_projection(): pl.pallas_call(functools.partial(next_projection_kernel, slots, first, co...  3.56 us
    pallas_call x4, Pallas kernels, project_frames(): pl.pallas_call(functools.partial(projected_kernel, items), in_specs=[SMEM...  3.49 us
    pallas_call x2, Pallas kernels, half_v(): pl.pallas_call(functools.partial(next_v_kernel, items, share, bool(before...  3.25 us
    pallas_call x1, Pallas kernels, next_w(): pl.pallas_call(functools.partial(next_w_kernel, len(sums)), in_specs=[VME...  2.27 us
  transfers between devices with their start and end apart: 21, of which 12 were waited for; matrix products, arithmetic and copies ran while one was open for 0% of the time, Pallas kernels for 34%

profile of v21, /device:TPU:0, one launch (start us, length us, event | category | flops | bytes accessed | tf_op | source)
XLA Modules:
  0.0 81.1 jit_solution(9485455043035315153)
XLA Ops:
  0.7 3.7 %project_first.1 = s16[528,256]{1,0:T(8,128)(2,1)S(1)} custom-call(s32[1]{0:T(128)} %bitcast.place, bf16[64,1024]{1,0:T(8,128)(2,1)} %bitcast.13, bf16[4,8,256,1024]{3,2,1,0:T(8,128)(2,1)} %bitcast.4), custom_call_target="tpu_custom_call" | custom-call | flops 1000 | bytes 1000 | tf_op jit(solution)/shard_map/project_first/pallas_call | solution.py:161
  4.4 3.0 %collective-permute-start = (s16[528,256]{1,0:T(8,128)(2,1)S(1)}, s16[528,256]{1,0:T(8,128)(2,1)S(1)}, u32[]{:S(2)}, u32[]{:S(2)}) collective-permute-start(s16[528,256]{1,0:T(8,128)(2,1)S(1)} %project_first.1), channel_id=1, source_target_pairs={{0,1},{1,0},{2,3},{3,2},{4,5},{5,4},{6,7},{7,6},{8,9},{9,8},{10,11... | collective-permute-start | bytes 811016 | tf_op jit(solution)/shard_map/ppermute | solution.py:627
  7.8 1.6 %project_next.4 = s16[560,256]{1,0:T(8,128)(2,1)S(1)} custom-call(s32[1]{0:T(128)} %bitcast.place, bf16[64,1024]{1,0:T(8,128)(2,1)S(1)} %bitcast.14, bf16[4,8,256,1024]{3,2,1,0:T(8,128)(2,1)S(1)} %bitcast.5), custom_call_target="tpu_custom_call" | custom-call | flops 1000 | bytes 1000 | tf_op jit(solution)/shard_map/project_next/pallas_call | solution.py:199
  9.4 3.0 %collective-permute-start.3 = (s16[560,256]{1,0:T(8,128)(2,1)S(1)}, s16[560,256]{1,0:T(8,128)(2,1)S(1)}, u32[]{:S(2)}, u32[]{:S(2)}) collective-permute-start(s16[560,256]{1,0:T(8,128)(2,1)S(1)} %project_next.4), channel_id=1, source_target_pairs={{0,1},{1,0},{2,3},{3,2},{4,5},{5,4},{6,7},{7,6},{8,9},{9,8},{10,11... | collective-permute-start | bytes 860168 | tf_op jit(solution)/shard_map/ppermute | solution.py:627
  15.6 3.2 %collective-permute-start.2 = (s16[272,256]{1,0:T(8,128)(2,1)S(1)}, s16[272,256]{1,0:T(8,128)(2,1)S(1)}, u32[]{:S(2)}, u32[]{:S(2)}) collective-permute-start(s16[272,256]{1,0:T(8,128)(2,1)S(1)} %project_next.3), channel_id=1, source_target_pairs={{0,2},{1,3},{2,0},{3,1},{4,6},{5,7},{6,4},{7,5},{8,10},{9,11},{10,... | collective-permute-start | bytes 417800 | tf_op jit(solution)/shard_map/ppermute | solution.py:627
  18.8 1.5 %collective-permute-start.4 = (f32[64,64]{1,0:T(8,128)S(1)}, f32[64,64]{1,0:T(8,128)S(1)}, u32[]{:S(2)}, u32[]{:S(2)}) collective-permute-start(f32[64,64]{1,0:T(8,128)S(1)} %add_terms.5.refs_1_.refs_0_), channel_id=1, source_target_pairs={{0,8},{4,12},{8,0},{12,4},{1,9},{5,13},{9,1},{13,5},{2,10},{6,14},... | collective-permute-start | bytes 49160 | tf_op jit(solution)/shard_map/ppermute | solution.py:627
  24.9 6.0 %own_frames.2 = (bf16[4,64,256]{2,1,0:T(8,128)(2,1)S(1)}, f32[64,64]{1,0:T(8,128)S(1)}, f32[64,64]{1,0:T(8,128)S(1)}) custom-call(s32[1]{0:T(128)} %bitcast.place, s32[32]{0:T(128)S(1)} %copy-done.4, f32[64,64]{1,0:T(8,128)S(1)} %copy-done.3, f32[32,64]{1,0:T(8,128)S(1)} %copy-done.2, f32[64,64]{1,0:T(8,128)S(1)} %get-tuple-element.43.v_gram_ref.before_ref.refs_2_, ...), custom_call_target="tpu_custom_call" | custom-call | flops 1000 | bytes 1000 | tf_op jit(solution)/shard_map/own_frames/pallas_call | solution.py:395
  30.9 2.1 %collective-permute-start.7 = (bf16[4,64,256]{2,1,0:T(8,128)(2,1)S(1)}, bf16[4,64,256]{2,1,0:T(8,128)(2,1)S(1)}, u32[]{:S(2)}, u32[]{:S(2)}) collective-permute-start(bf16[4,64,256]{2,1,0:T(8,128)(2,1)S(1)} %get-tuple-element.50.refs_0_), channel_id=1, source_target_pairs={{0,2},{1,3},{2,0},{3,1},{4,6},{5,7},{6,4},{7,5},{8,10},{9,11},{10,... | collective-permute-start | bytes 393224 | tf_op jit(solution)/shard_map/ppermute | solution.py:627
  33.1 6.0 %own_frames.3 = (bf16[4,64,256]{2,1,0:T(8,128)(2,1)S(1)}, f32[64,64]{1,0:T(8,128)S(1)}, f32[64,64]{1,0:T(8,128)S(1)}) custom-call(s32[1]{0:T(128)} %bitcast.place, s32[32]{0:T(128)S(1)} %copy-done.4, f32[64,64]{1,0:T(8,128)S(1)} %copy-done.3, f32[32,64]{1,0:T(8,128)S(1)} %copy-done.2, f32[64,64]{1,0:T(8,128)S(1)} %get-tuple-element.46.v_gram_ref, ...), custom_call_target="tpu_custom_call" | custom-call | flops 1000 | bytes 1000 | tf_op jit(solution)/shard_map/own_frames/pallas_call | solution.py:395
  40.7 1.6 %collective-permute-start.12 = (bf16[4,64,256]{2,1,0:T(8,128)(2,1)S(1)}, bf16[4,64,256]{2,1,0:T(8,128)(2,1)S(1)}, u32[]{:S(2)}, u32[]{:S(2)}) collective-permute-start(bf16[4,64,256]{2,1,0:T(8,128)(2,1)S(1)} %get-tuple-element.51.refs_2_.refs_1_.refs_0_), channel_id=1, source_target_pairs={{0,2},{1,3},{2,0},{3,1},{4,6},{5,7},{6,4},{7,5},{8,10},{9,11},{10,... | collective-permute-start | bytes 393224 | tf_op jit(solution)/shard_map/ppermute | solution.py:627
  43.6 1.6 %collective-permute-start.8 = (f32[64,64]{1,0:T(8,128)S(1)}, f32[64,64]{1,0:T(8,128)S(1)}, u32[]{:S(2)}, u32[]{:S(2)}) collective-permute-start(f32[64,64]{1,0:T(8,128)S(1)} %add_terms.6.refs_2_.a_ref), channel_id=1, source_target_pairs={{0,8},{4,12},{8,0},{12,4},{1,9},{5,13},{9,1},{13,5},{2,10},{6,14},... | collective-permute-start | bytes 49160 | tf_op jit(solution)/shard_map/ppermute | solution.py:627
  45.1 1.7 %first_inverse.1 = (f32[64,64]{1,0:T(8,128)S(1)}, f32[64,64]{1,0:T(8,128)S(1)}) custom-call(f32[64,64]{1,0:T(8,128)S(1)} %get-tuple-element.53.v_gram_ref, f32[64,64]{1,0:T(8,128)S(1)} %add_terms.5.refs_1_.refs_0_, f32[64,64]{1,0:T(8,128)S(1)} %collective-permute-done.4.refs_1_, f32[64,64]{1,0:T(8,128)S(1)} %add_terms.6.refs_2_.a_ref), custom_call_target="tpu_custom_call" | custom-call | flops 1000 | bytes 1000 | tf_op jit(solution)/shard_map/first_inverse/pallas_call | solution.py:322
  47.8 1.7 %collective-permute-done.13.refs_3_.refs_0_ = bf16[8,64,256]{2,1,0:T(8,128)(2,1)S(1)} collective-permute-done((bf16[8,64,256]{2,1,0:T(8,128)(2,1)S(1)}, bf16[8,64,256]{2,1,0:T(8,128)(2,1)S(1)}, u32[]{:S(2)}, u32[]{:S(2)}) %collective-permute-start.13) | collective-permute-done | bytes 262176 | tf_op jit(solution)/shard_map/ppermute | solution.py:627
  50.5 1.8 %collective-permute-start.11 = (f32[64,64]{1,0:T(8,128)S(1)}, f32[64,64]{1,0:T(8,128)S(1)}, u32[]{:S(2)}, u32[]{:S(2)}) collective-permute-start(f32[64,64]{1,0:T(8,128)S(1)} %add_terms.7.refs_2_.refs_0_), channel_id=1, source_target_pairs={{0,3},{1,2},{2,1},{3,0},{4,7},{5,6},{6,5},{7,4},{8,11},{9,10},{10,... | collective-permute-start | bytes 49160 | tf_op jit(solution)/shard_map/ppermute | solution.py:627
  53.2 1.8 %collective-permute-start.9 = (f32[64,64]{1,0:T(8,128)S(1)}, f32[64,64]{1,0:T(8,128)S(1)}, u32[]{:S(2)}, u32[]{:S(2)}) collective-permute-start(f32[64,64]{1,0:T(8,128)S(1)} %add_terms.7.refs_2_.refs_0_), channel_id=1, source_target_pairs={{0,1},{1,0},{2,3},{3,2},{4,5},{5,4},{6,7},{7,6},{8,9},{9,8},{10,11... | collective-permute-start | bytes 49160 | tf_op jit(solution)/shard_map/ppermute | solution.py:627
  56.3 1.9 %collective-permute-done.14.refs_0_ = bf16[8,64,256]{2,1,0:T(8,128)(2,1)S(1)} collective-permute-done((bf16[8,64,256]{2,1,0:T(8,128)(2,1)S(1)}, bf16[8,64,256]{2,1,0:T(8,128)(2,1)S(1)}, u32[]{:S(2)}, u32[]{:S(2)}) %collective-permute-start.14) | collective-permute-done | bytes 262176 | tf_op jit(solution)/shard_map/ppermute | solution.py:627
  62.2 2.4 %collective-permute-start.16 = (f32[64,512]{1,0:T(8,128)S(1)}, f32[64,512]{1,0:T(8,128)S(1)}, u32[]{:S(2)}, u32[]{:S(2)}) collective-permute-start(f32[64,512]{1,0:T(8,128)S(1)} %add_terms.8.a_ref), channel_id=1, source_target_pairs={{0,8},{4,12},{8,0},{12,4},{1,9},{5,13},{9,1},{13,5},{2,10},{6,14},... | collective-permute-start | bytes 393224 | tf_op jit(solution)/shard_map/ppermute | solution.py:627
  64.6 1.7 %second_inverse.1 = (f32[64,64]{1,0:T(8,128)S(1)}, f32[64,64]{1,0:T(8,128)S(1)}) custom-call(f32[64,64]{1,0:T(8,128)S(1)} %get-tuple-element.73.h_ref, f32[64,64]{1,0:T(8,128)S(1)} %get-tuple-element.74.w_gram_ref), custom_call_target="tpu_custom_call" | custom-call | flops 1000 | bytes 1000 | tf_op jit(solution)/shard_map/second_inverse/pallas_call | solution.py:501
  66.3 2.1 %collective-permute-done.16.b_ref = f32[64,512]{1,0:T(8,128)S(1)} collective-permute-done((f32[64,512]{1,0:T(8,128)S(1)}, f32[64,512]{1,0:T(8,128)S(1)}, u32[]{:S(2)}, u32[]{:S(2)}) %collective-permute-start.16) | collective-permute-done | bytes 131104 | tf_op jit(solution)/shard_map/ppermute | solution.py:627
  68.5 1.6 %next_v.2 = (f32[64,512]{1,0:T(8,128)S(1)}, f32[64,128]{1,0:T(8,128)S(1)}) custom-call(s32[1]{0:T(128)} %bitcast.place, f32[64,512]{1,0:T(8,128)S(1)} %add_terms.9.terms_ref, f32[64,64]{1,0:T(8,128)S(1)} %get-tuple-element.75.refs_0_.inverse_ref, f32[64,64]{1,0:T(8,128)S(1)} %get-tuple-element.73.h_ref, bf16[256,1024]{1,0:T(8,128)(2,1)S(1)} %get-tuple-element.61.refs_0_, ...), custom_call_target="tpu_custom_call" | custom-call | flops 1000 | bytes 1000 | tf_op jit(solution)/shard_map/next_v/pallas_call | solution.py:568
  70.1 1.6 %next_v.3 = (f32[64,512]{1,0:T(8,128)S(1)}, f32[64,128]{1,0:T(8,128)S(1)}) custom-call(s32[1]{0:T(128)} %bitcast.place, f32[64,512]{1,0:T(8,128)S(1)} %collective-permute-done.17.terms_ref, f32[64,64]{1,0:T(8,128)S(1)} %get-tuple-element.75.refs_0_.inverse_ref, f32[64,64]{1,0:T(8,128)S(1)} %get-tuple-element.73.h_ref, ...), custom_call_target="tpu_custom_call" | custom-call | flops 1000 | bytes 1000 | tf_op jit(solution)/shard_map/next_v/pallas_call | solution.py:568
  71.8 1.9 %collective-permute-start.20 = (f32[64,128]{1,0:T(8,128)S(1)}, f32[64,128]{1,0:T(8,128)S(1)}, u32[]{:S(2)}, u32[]{:S(2)}) collective-permute-start(f32[64,128]{1,0:T(8,128)S(1)} %get-tuple-element.80.refs_0_), channel_id=1, source_target_pairs={{0,3},{1,2},{2,1},{3,0},{4,7},{5,6},{6,5},{7,4},{8,11},{9,10},{10,... | collective-permute-start | bytes 98312 | tf_op jit(solution)/shard_map/ppermute | solution.py:627
  73.7 2.5 %collective-permute-start.18 = (f32[64,128]{1,0:T(8,128)S(1)}, f32[64,128]{1,0:T(8,128)S(1)}, u32[]{:S(2)}, u32[]{:S(2)}) collective-permute-start(f32[64,128]{1,0:T(8,128)S(1)} %get-tuple-element.80.refs_0_), channel_id=1, source_target_pairs={{0,1},{1,0},{2,3},{3,2},{4,5},{5,4},{6,7},{7,6},{8,9},{9,8},{10,11... | collective-permute-start | bytes 98312 | tf_op jit(solution)/shard_map/ppermute | solution.py:627
  78.8 2.3 %next_w.1 = f32[32,64]{1,0:T(8,128)} custom-call(f32[64,128]{1,0:T(8,128)S(1)} %get-tuple-element.80.refs_0_, f32[64,128]{1,0:T(8,128)S(1)} %collective-permute-done.18.refs_1_, f32[64,128]{1,0:T(8,128)S(1)} %collective-permute-done.19.refs_2_, f32[64,128]{1,0:T(8,128)S(1)} %collective-permute-done.20.refs_3_, f32[64,64]{1,0:T(8,128)S(1)} %get-tuple-element.81.refs_4_, ...), custom_call_target="tpu_custom_call" | custom-call | flops 1000 | bytes 1000 | tf_op jit(solution)/shard_map/next_w/pallas_call | solution.py:614
  (56 shorter events, 21.8 us)
Async XLA Ops:
  0.7 11.8 %copy-start.2 = (f32[32,64]{1,0:T(8,128)S(1)}, f32[32,64]{1,0:T(8,128)}, u32[]{:S(2)}) copy-start(f32[32,64]{1,0:T(8,128)} %w_ref.5) | copy-start | bytes 24580
  4.4 10.2 %collective-permute-start = (s16[528,256]{1,0:T(8,128)(2,1)S(1)}, s16[528,256]{1,0:T(8,128)(2,1)S(1)}, u32[]{:S(2)}, u32[]{:S(2)}) collective-permute-start(s16[528,256]{1,0:T(8,128)(2,1)S(1)} %project_first.1), channel_id=1, source_target_pairs={{0,1},{1,0},{2,3},{3,2},{4,5},{5,4},{6,7},{7,6},{8,9},{9,8},{10,11... | collective-permute-start | bytes 811016 | tf_op jit(solution)/shard_map/ppermute | solution.py:627
  9.4 13.6 %collective-permute-start.3 = (s16[560,256]{1,0:T(8,128)(2,1)S(1)}, s16[560,256]{1,0:T(8,128)(2,1)S(1)}, u32[]{:S(2)}, u32[]{:S(2)}) collective-permute-start(s16[560,256]{1,0:T(8,128)(2,1)S(1)} %project_next.4), channel_id=1, source_target_pairs={{0,1},{1,0},{2,3},{3,2},{4,5},{5,4},{6,7},{7,6},{8,9},{9,8},{10,11... | collective-permute-start | bytes 860168 | tf_op jit(solution)/shard_map/ppermute | solution.py:627
  13.3 1.3 %collective-permute-start.1 = (f32[64,64]{1,0:T(8,128)S(1)}, f32[64,64]{1,0:T(8,128)S(1)}, u32[]{:S(2)}, u32[]{:S(2)}) collective-permute-start(f32[64,64]{1,0:T(8,128)S(1)} %get-tuple-element.45.a_ref), channel_id=1, source_target_pairs={{0,4},{4,0},{8,12},{12,8},{1,5},{5,1},{9,13},{13,9},{2,6},{6,2},{1... | collective-permute-start | bytes 49160 | tf_op jit(solution)/shard_map/ppermute | solution.py:627
  15.5 9.4 %copy-start.3 = (f32[64,64]{1,0:T(8,128)S(1)}, f32[64,64]{1,0:T(8,128)}, u32[]{:S(2)}) copy-start(f32[64,64]{1,0:T(8,128)} %h_ref.3) | copy-start | bytes 49156
  15.6 9.4 %copy-start.4 = (s32[32]{0:T(128)S(1)}, s32[32]{0:T(128)}, u32[]{:S(2)}) copy-start(s32[32]{0:T(128)} %counts_ref.3) | copy-start | bytes 388
  15.6 9.4 %collective-permute-start.2 = (s16[272,256]{1,0:T(8,128)(2,1)S(1)}, s16[272,256]{1,0:T(8,128)(2,1)S(1)}, u32[]{:S(2)}, u32[]{:S(2)}) collective-permute-start(s16[272,256]{1,0:T(8,128)(2,1)S(1)} %project_next.3), channel_id=1, source_target_pairs={{0,2},{1,3},{2,0},{3,1},{4,6},{5,7},{6,4},{7,5},{8,10},{9,11},{10,... | collective-permute-start | bytes 417800 | tf_op jit(solution)/shard_map/ppermute | solution.py:627
  18.8 3.9 %collective-permute-start.4 = (f32[64,64]{1,0:T(8,128)S(1)}, f32[64,64]{1,0:T(8,128)S(1)}, u32[]{:S(2)}, u32[]{:S(2)}) collective-permute-start(f32[64,64]{1,0:T(8,128)S(1)} %add_terms.5.refs_1_.refs_0_), channel_id=1, source_target_pairs={{0,8},{4,12},{8,0},{12,4},{1,9},{5,13},{9,1},{13,5},{2,10},{6,14},... | collective-permute-start | bytes 49160 | tf_op jit(solution)/shard_map/ppermute | solution.py:627
  24.0 9.0 %collective-permute-start.5 = (s16[304,256]{1,0:T(8,128)(2,1)S(1)}, s16[304,256]{1,0:T(8,128)(2,1)S(1)}, u32[]{:S(2)}, u32[]{:S(2)}) collective-permute-start(s16[304,256]{1,0:T(8,128)(2,1)S(1)} %project_next.5), channel_id=1, source_target_pairs={{0,2},{1,3},{2,0},{3,1},{4,6},{5,7},{6,4},{7,5},{8,10},{9,11},{10,... | collective-permute-start | bytes 466952 | tf_op jit(solution)/shard_map/ppermute | solution.py:627
  30.9 8.5 %collective-permute-start.7 = (bf16[4,64,256]{2,1,0:T(8,128)(2,1)S(1)}, bf16[4,64,256]{2,1,0:T(8,128)(2,1)S(1)}, u32[]{:S(2)}, u32[]{:S(2)}) collective-permute-start(bf16[4,64,256]{2,1,0:T(8,128)(2,1)S(1)} %get-tuple-element.50.refs_0_), channel_id=1, source_target_pairs={{0,2},{1,3},{2,0},{3,1},{4,6},{5,7},{6,4},{7,5},{8,10},{9,11},{10,... | collective-permute-start | bytes 393224 | tf_op jit(solution)/shard_map/ppermute | solution.py:627
  39.5 10.1 %collective-permute-start.13 = (bf16[8,64,256]{2,1,0:T(8,128)(2,1)S(1)}, bf16[8,64,256]{2,1,0:T(8,128)(2,1)S(1)}, u32[]{:S(2)}, u32[]{:S(2)}) collective-permute-start(bf16[8,64,256]{2,1,0:T(8,128)(2,1)S(1)} %join_frames.2.refs_3_), channel_id=1, source_target_pairs={{0,1},{1,0},{2,3},{3,2},{4,5},{5,4},{6,7},{7,6},{8,9},{9,8},{10,11... | collective-permute-start | bytes 786440 | tf_op jit(solution)/shard_map/ppermute | solution.py:627
  40.7 7.2 %collective-permute-start.12 = (bf16[4,64,256]{2,1,0:T(8,128)(2,1)S(1)}, bf16[4,64,256]{2,1,0:T(8,128)(2,1)S(1)}, u32[]{:S(2)}, u32[]{:S(2)}) collective-permute-start(bf16[4,64,256]{2,1,0:T(8,128)(2,1)S(1)} %get-tuple-element.51.refs_2_.refs_1_.refs_0_), channel_id=1, source_target_pairs={{0,2},{1,3},{2,0},{3,1},{4,6},{5,7},{6,4},{7,5},{8,10},{9,11},{10,... | collective-permute-start | bytes 393224 | tf_op jit(solution)/shard_map/ppermute | solution.py:627
  42.3 1.3 %collective-permute-start.6 = (f32[64,64]{1,0:T(8,128)S(1)}, f32[64,64]{1,0:T(8,128)S(1)}, u32[]{:S(2)}, u32[]{:S(2)}) collective-permute-start(f32[64,64]{1,0:T(8,128)S(1)} %get-tuple-element.49.a_ref), channel_id=1, source_target_pairs={{0,4},{4,0},{8,12},{12,8},{1,5},{5,1},{9,13},{13,9},{2,6},{6,2},{1... | collective-permute-start | bytes 49160 | tf_op jit(solution)/shard_map/ppermute | solution.py:627
  43.6 4.0 %collective-permute-start.8 = (f32[64,64]{1,0:T(8,128)S(1)}, f32[64,64]{1,0:T(8,128)S(1)}, u32[]{:S(2)}, u32[]{:S(2)}) collective-permute-start(f32[64,64]{1,0:T(8,128)S(1)} %add_terms.6.refs_2_.a_ref), channel_id=1, source_target_pairs={{0,8},{4,12},{8,0},{12,4},{1,9},{5,13},{9,1},{13,5},{2,10},{6,14},... | collective-permute-start | bytes 49160 | tf_op jit(solution)/shard_map/ppermute | solution.py:627
  49.6 8.7 %collective-permute-start.14 = (bf16[8,64,256]{2,1,0:T(8,128)(2,1)S(1)}, bf16[8,64,256]{2,1,0:T(8,128)(2,1)S(1)}, u32[]{:S(2)}, u32[]{:S(2)}) collective-permute-start(bf16[8,64,256]{2,1,0:T(8,128)(2,1)S(1)} %join_frames.3.refs_1_), channel_id=1, source_target_pairs={{0,1},{1,0},{2,3},{3,2},{4,5},{5,4},{6,7},{7,6},{8,9},{9,8},{10,11... | collective-permute-start | bytes 786440 | tf_op jit(solution)/shard_map/ppermute | solution.py:627
  50.5 8.6 %collective-permute-start.11 = (f32[64,64]{1,0:T(8,128)S(1)}, f32[64,64]{1,0:T(8,128)S(1)}, u32[]{:S(2)}, u32[]{:S(2)}) collective-permute-start(f32[64,64]{1,0:T(8,128)S(1)} %add_terms.7.refs_2_.refs_0_), channel_id=1, source_target_pairs={{0,3},{1,2},{2,1},{3,0},{4,7},{5,6},{6,5},{7,4},{8,11},{9,10},{10,... | collective-permute-start | bytes 49160 | tf_op jit(solution)/shard_map/ppermute | solution.py:627
  52.3 6.8 %collective-permute-start.10 = (f32[64,64]{1,0:T(8,128)S(1)}, f32[64,64]{1,0:T(8,128)S(1)}, u32[]{:S(2)}, u32[]{:S(2)}) collective-permute-start(f32[64,64]{1,0:T(8,128)S(1)} %add_terms.7.refs_2_.refs_0_), channel_id=1, source_target_pairs={{0,2},{1,3},{2,0},{3,1},{4,6},{5,7},{6,4},{7,5},{8,10},{9,11},{10,... | collective-permute-start | bytes 49160 | tf_op jit(solution)/shard_map/ppermute | solution.py:627
  53.2 6.0 %collective-permute-start.9 = (f32[64,64]{1,0:T(8,128)S(1)}, f32[64,64]{1,0:T(8,128)S(1)}, u32[]{:S(2)}, u32[]{:S(2)}) collective-permute-start(f32[64,64]{1,0:T(8,128)S(1)} %add_terms.7.refs_2_.refs_0_), channel_id=1, source_target_pairs={{0,1},{1,0},{2,3},{3,2},{4,5},{5,4},{6,7},{7,6},{8,9},{9,8},{10,11... | collective-permute-start | bytes 49160 | tf_op jit(solution)/shard_map/ppermute | solution.py:627
  60.8 1.4 %collective-permute-start.15 = (f32[64,512]{1,0:T(8,128)S(1)}, f32[64,512]{1,0:T(8,128)S(1)}, u32[]{:S(2)}, u32[]{:S(2)}) collective-permute-start(f32[64,512]{1,0:T(8,128)S(1)} %v_terms.2.refs_12_), channel_id=1, source_target_pairs={{0,4},{4,0},{8,12},{12,8},{1,5},{5,1},{9,13},{13,9},{2,6},{6,2},{1... | collective-permute-start | bytes 393224 | tf_op jit(solution)/shard_map/ppermute | solution.py:627
  62.2 6.2 %collective-permute-start.16 = (f32[64,512]{1,0:T(8,128)S(1)}, f32[64,512]{1,0:T(8,128)S(1)}, u32[]{:S(2)}, u32[]{:S(2)}) collective-permute-start(f32[64,512]{1,0:T(8,128)S(1)} %add_terms.8.a_ref), channel_id=1, source_target_pairs={{0,8},{4,12},{8,0},{12,4},{1,9},{5,13},{9,1},{13,5},{2,10},{6,14},... | collective-permute-start | bytes 393224 | tf_op jit(solution)/shard_map/ppermute | solution.py:627
  68.4 1.7 %collective-permute-start.17 = (f32[64,512]{1,0:T(8,128)S(1)}, f32[64,512]{1,0:T(8,128)S(1)}, u32[]{:S(2)}, u32[]{:S(2)}) collective-permute-start(f32[64,512]{1,0:T(8,128)S(1)} %add_terms.9.terms_ref), channel_id=1, source_target_pairs={{0,4},{4,0},{8,12},{12,8},{1,5},{5,1},{9,13},{13,9},{2,6},{6,2},{1... | collective-permute-start | bytes 393224 | tf_op jit(solution)/shard_map/ppermute | solution.py:627
  71.8 6.0 %collective-permute-start.20 = (f32[64,128]{1,0:T(8,128)S(1)}, f32[64,128]{1,0:T(8,128)S(1)}, u32[]{:S(2)}, u32[]{:S(2)}) collective-permute-start(f32[64,128]{1,0:T(8,128)S(1)} %get-tuple-element.80.refs_0_), channel_id=1, source_target_pairs={{0,3},{1,2},{2,1},{3,0},{4,7},{5,6},{6,5},{7,4},{8,11},{9,10},{10,... | collective-permute-start | bytes 98312 | tf_op jit(solution)/shard_map/ppermute | solution.py:627
  73.7 5.1 %collective-permute-start.19 = (f32[64,128]{1,0:T(8,128)S(1)}, f32[64,128]{1,0:T(8,128)S(1)}, u32[]{:S(2)}, u32[]{:S(2)}) collective-permute-start(f32[64,128]{1,0:T(8,128)S(1)} %get-tuple-element.80.refs_0_), channel_id=1, source_target_pairs={{0,2},{1,3},{2,0},{3,1},{4,6},{5,7},{6,4},{7,5},{8,10},{9,11},{10,... | collective-permute-start | bytes 98312 | tf_op jit(solution)/shard_map/ppermute | solution.py:627
  73.7 5.1 %collective-permute-start.18 = (f32[64,128]{1,0:T(8,128)S(1)}, f32[64,128]{1,0:T(8,128)S(1)}, u32[]{:S(2)}, u32[]{:S(2)}) collective-permute-start(f32[64,128]{1,0:T(8,128)S(1)} %get-tuple-element.80.refs_0_), channel_id=1, source_target_pairs={{0,1},{1,0},{2,3},{3,2},{4,5},{5,4},{6,7},{7,6},{8,9},{9,8},{10,11... | collective-permute-start | bytes 98312 | tf_op jit(solution)/shard_map/ppermute | solution.py:627
  (2 other events, 13.9 us)

commit v22 on v21

--- a/solution.py
+++ b/solution.py
@@ -42,6 +42,16 @@
     rest = x - first.astype(F32)
     second = rest.astype(BF16)
     return first, second, (rest - second.astype(F32)).astype(BF16)
+
+
+def stacked_dot(a, b):
+    n = a.shape[0]
+    a_first, a_second, a_third = three_parts(a)
+    b_first, b_second, b_third = three_parts(b)
+    x = low_dot(jnp.concatenate([a_first, a_second, a_third], axis=0), b_first)
+    y = low_dot(jnp.concatenate([a_first, a_second], axis=0), b_second)
+    z = low_dot(a_first, b_third)
+    return x[:n] + ((x[n : 2 * n] + y[:n]) + ((x[2 * n :] + y[n:]) + z))
 
 
 def feature_of(place):
@@ -364,7 +374,7 @@
     for p in patients:
         proj[p] = pieces[p]
     weights = [w_ref[pl.ds(first + p, 1), :] for p in patients]
-    mixed = [high_dot(h_ref[...] * weights[p], pieces[p]) for p in patients]
+    mixed = [stacked_dot(h_ref[...] * weights[p], pieces[p]) for p in patients]
     lanes = lane_numbers((rank, slots))
     mixed = [jnp.where(lanes < counts_ref[first + p], mixed[p], 0.0) for p in patients]
     energy = [jnp.sum(jnp.sum(x * x, axis=1, keepdims=True), axis=0, keepdims=True) for x in mixed]
@@ -463,7 +473,7 @@
 
 def next_h_kernel(n_terms, *refs):
     inverse_ref, spread_ref, _, result_ref, h_ref, factor_ref = refs[n_terms:]
-    h_next = high_dot(total(refs[:n_terms]), inverse_ref[...])
+    h_next = stacked_dot(total(refs[:n_terms]), inverse_ref[...])
     result_ref[...] = h_next
     h_ref[...] = h_next
     rank = h_next.shape[0]
@@ -544,7 +554,7 @@
     rank, half = terms_ref.shape
     here = pl.multiple_of((core_of(place) ^ 1 if later else core_of(place)) * half, half)
     features = pl.ds(here, half)
-    v_rows = high_dot(inverse_ref[...], terms_ref[...])
+    v_rows = stacked_dot(inverse_ref[...], terms_ref[...])
     *before, v_ref, sums_ref, v_parts = refs
     v_ref[...] = v_rows
     sums = before[0][...] if later else jnp.zeros((rank, 2 * rank), F32)

time: 81.2 us -> 81.2 us (level)
  no operation moved by 1% of the time
where the time goes in v22:
time: 81.2 us; the launch traced here: 81.1 us
  Pallas kernels  37.2 us (46%)
  starting transfers between devices  30.5 us (38%)
  waiting for transfers between devices  12.2 us (15%)
  between operations  0.84 us (1%)
    ppermute x21, starting transfers between devices, swap(): return lax.ppermute(x, axis, pairs)  30.5 us
    ppermute x21, waiting for transfers between devices, swap(): return lax.ppermute(x, axis, pairs)  12.2 us
    pallas_call x2, Pallas kernels, own_frames(): pl.pallas_call(functools.partial(frames_kernel, layouts, part, share), in...  11.9 us
    pallas_call x1, Pallas kernels, first_projection(): pl.pallas_call(functools.partial(first_projection_kernel, slots, with_gra...  3.73 us
    pallas_call x3, Pallas kernels, next_projection(): pl.pallas_call(functools.partial(next_projection_kernel, slots, first, co...  3.56 us
    pallas_call x4, Pallas kernels, project_frames(): pl.pallas_call(functools.partial(projected_kernel, items), in_specs=[SMEM...  3.49 us
    pallas_call x2, Pallas kernels, half_v(): pl.pallas_call(functools.partial(next_v_kernel, items, share, bool(before...  3.21 us
    pallas_call x1, Pallas kernels, next_w(): pl.pallas_call(functools.partial(next_w_kernel, len(sums)), in_specs=[VME...  2.27 us
  transfers between devices with their start and end apart: 21, of which 12 were waited for; matrix products, arithmetic and copies ran while one was open for 0% of the time, Pallas kernels for 34%

profile of v22, /device:TPU:0, one launch (start us, length us, event | category | flops | bytes accessed | tf_op | source)
XLA Modules:
  0.0 81.1 jit_solution(5797600761540487292)
XLA Ops:
  0.7 3.7 %project_first.1 = s16[528,256]{1,0:T(8,128)(2,1)S(1)} custom-call(s32[1]{0:T(128)} %bitcast.place, bf16[64,1024]{1,0:T(8,128)(2,1)} %bitcast.13, bf16[4,8,256,1024]{3,2,1,0:T(8,128)(2,1)} %bitcast.4), custom_call_target="tpu_custom_call" | custom-call | flops 1000 | bytes 1000 | tf_op jit(solution)/shard_map/project_first/pallas_call | solution.py:171
  4.4 3.0 %collective-permute-start = (s16[528,256]{1,0:T(8,128)(2,1)S(1)}, s16[528,256]{1,0:T(8,128)(2,1)S(1)}, u32[]{:S(2)}, u32[]{:S(2)}) collective-permute-start(s16[528,256]{1,0:T(8,128)(2,1)S(1)} %project_first.1), channel_id=1, source_target_pairs={{0,1},{1,0},{2,3},{3,2},{4,5},{5,4},{6,7},{7,6},{8,9},{9,8},{10,11... | collective-permute-start | bytes 811016 | tf_op jit(solution)/shard_map/ppermute | solution.py:637
  7.8 1.6 %project_next.4 = s16[560,256]{1,0:T(8,128)(2,1)S(1)} custom-call(s32[1]{0:T(128)} %bitcast.place, bf16[64,1024]{1,0:T(8,128)(2,1)S(1)} %bitcast.14, bf16[4,8,256,1024]{3,2,1,0:T(8,128)(2,1)S(1)} %bitcast.5), custom_call_target="tpu_custom_call" | custom-call | flops 1000 | bytes 1000 | tf_op jit(solution)/shard_map/project_next/pallas_call | solution.py:209
  9.4 3.0 %collective-permute-start.3 = (s16[560,256]{1,0:T(8,128)(2,1)S(1)}, s16[560,256]{1,0:T(8,128)(2,1)S(1)}, u32[]{:S(2)}, u32[]{:S(2)}) collective-permute-start(s16[560,256]{1,0:T(8,128)(2,1)S(1)} %project_next.4), channel_id=1, source_target_pairs={{0,1},{1,0},{2,3},{3,2},{4,5},{5,4},{6,7},{7,6},{8,9},{9,8},{10,11... | collective-permute-start | bytes 860168 | tf_op jit(solution)/shard_map/ppermute | solution.py:637
  15.6 3.2 %collective-permute-start.2 = (s16[272,256]{1,0:T(8,128)(2,1)S(1)}, s16[272,256]{1,0:T(8,128)(2,1)S(1)}, u32[]{:S(2)}, u32[]{:S(2)}) collective-permute-start(s16[272,256]{1,0:T(8,128)(2,1)S(1)} %project_next.3), channel_id=1, source_target_pairs={{0,2},{1,3},{2,0},{3,1},{4,6},{5,7},{6,4},{7,5},{8,10},{9,11},{10,... | collective-permute-start | bytes 417800 | tf_op jit(solution)/shard_map/ppermute | solution.py:637
  18.8 1.5 %collective-permute-start.4 = (f32[64,64]{1,0:T(8,128)S(1)}, f32[64,64]{1,0:T(8,128)S(1)}, u32[]{:S(2)}, u32[]{:S(2)}) collective-permute-start(f32[64,64]{1,0:T(8,128)S(1)} %add_terms.5.refs_1_.refs_0_), channel_id=1, source_target_pairs={{0,8},{4,12},{8,0},{12,4},{1,9},{5,13},{9,1},{13,5},{2,10},{6,14},... | collective-permute-start | bytes 49160 | tf_op jit(solution)/shard_map/ppermute | solution.py:637
  24.9 6.0 %own_frames.2 = (bf16[4,64,256]{2,1,0:T(8,128)(2,1)S(1)}, f32[64,64]{1,0:T(8,128)S(1)}, f32[64,64]{1,0:T(8,128)S(1)}) custom-call(s32[1]{0:T(128)} %bitcast.place, s32[32]{0:T(128)S(1)} %copy-done.4, f32[64,64]{1,0:T(8,128)S(1)} %copy-done.3, f32[32,64]{1,0:T(8,128)S(1)} %copy-done.2, f32[64,64]{1,0:T(8,128)S(1)} %get-tuple-element.43.v_gram_ref.before_ref.refs_2_, ...), custom_call_target="tpu_custom_call" | custom-call | flops 1000 | bytes 1000 | tf_op jit(solution)/shard_map/own_frames/pallas_call | solution.py:405
  30.9 2.1 %collective-permute-start.7 = (bf16[4,64,256]{2,1,0:T(8,128)(2,1)S(1)}, bf16[4,64,256]{2,1,0:T(8,128)(2,1)S(1)}, u32[]{:S(2)}, u32[]{:S(2)}) collective-permute-start(bf16[4,64,256]{2,1,0:T(8,128)(2,1)S(1)} %get-tuple-element.50.refs_0_), channel_id=1, source_target_pairs={{0,2},{1,3},{2,0},{3,1},{4,6},{5,7},{6,4},{7,5},{8,10},{9,11},{10,... | collective-permute-start | bytes 393224 | tf_op jit(solution)/shard_map/ppermute | solution.py:637
  33.0 6.0 %own_frames.3 = (bf16[4,64,256]{2,1,0:T(8,128)(2,1)S(1)}, f32[64,64]{1,0:T(8,128)S(1)}, f32[64,64]{1,0:T(8,128)S(1)}) custom-call(s32[1]{0:T(128)} %bitcast.place, s32[32]{0:T(128)S(1)} %copy-done.4, f32[64,64]{1,0:T(8,128)S(1)} %copy-done.3, f32[32,64]{1,0:T(8,128)S(1)} %copy-done.2, f32[64,64]{1,0:T(8,128)S(1)} %get-tuple-element.46.v_gram_ref, ...), custom_call_target="tpu_custom_call" | custom-call | flops 1000 | bytes 1000 | tf_op jit(solution)/shard_map/own_frames/pallas_call | solution.py:405
  40.6 1.7 %collective-permute-start.12 = (bf16[4,64,256]{2,1,0:T(8,128)(2,1)S(1)}, bf16[4,64,256]{2,1,0:T(8,128)(2,1)S(1)}, u32[]{:S(2)}, u32[]{:S(2)}) collective-permute-start(bf16[4,64,256]{2,1,0:T(8,128)(2,1)S(1)} %get-tuple-element.51.refs_2_.refs_1_.refs_0_), channel_id=1, source_target_pairs={{0,2},{1,3},{2,0},{3,1},{4,6},{5,7},{6,4},{7,5},{8,10},{9,11},{10,... | collective-permute-start | bytes 393224 | tf_op jit(solution)/shard_map/ppermute | solution.py:637
  43.6 1.6 %collective-permute-start.8 = (f32[64,64]{1,0:T(8,128)S(1)}, f32[64,64]{1,0:T(8,128)S(1)}, u32[]{:S(2)}, u32[]{:S(2)}) collective-permute-start(f32[64,64]{1,0:T(8,128)S(1)} %add_terms.6.refs_2_.a_ref), channel_id=1, source_target_pairs={{0,8},{4,12},{8,0},{12,4},{1,9},{5,13},{9,1},{13,5},{2,10},{6,14},... | collective-permute-start | bytes 49160 | tf_op jit(solution)/shard_map/ppermute | solution.py:637
  45.1 1.7 %first_inverse.1 = (f32[64,64]{1,0:T(8,128)S(1)}, f32[64,64]{1,0:T(8,128)S(1)}) custom-call(f32[64,64]{1,0:T(8,128)S(1)} %get-tuple-element.53.v_gram_ref, f32[64,64]{1,0:T(8,128)S(1)} %add_terms.5.refs_1_.refs_0_, f32[64,64]{1,0:T(8,128)S(1)} %collective-permute-done.4.refs_1_, f32[64,64]{1,0:T(8,128)S(1)} %add_terms.6.refs_2_.a_ref), custom_call_target="tpu_custom_call" | custom-call | flops 1000 | bytes 1000 | tf_op jit(solution)/shard_map/first_inverse/pallas_call | solution.py:332
  47.7 1.9 %collective-permute-done.13.refs_3_.refs_0_ = bf16[8,64,256]{2,1,0:T(8,128)(2,1)S(1)} collective-permute-done((bf16[8,64,256]{2,1,0:T(8,128)(2,1)S(1)}, bf16[8,64,256]{2,1,0:T(8,128)(2,1)S(1)}, u32[]{:S(2)}, u32[]{:S(2)}) %collective-permute-start.13) | collective-permute-done | bytes 262176 | tf_op jit(solution)/shard_map/ppermute | solution.py:637
  50.6 1.8 %collective-permute-start.11 = (f32[64,64]{1,0:T(8,128)S(1)}, f32[64,64]{1,0:T(8,128)S(1)}, u32[]{:S(2)}, u32[]{:S(2)}) collective-permute-start(f32[64,64]{1,0:T(8,128)S(1)} %add_terms.7.refs_2_.refs_0_), channel_id=1, source_target_pairs={{0,3},{1,2},{2,1},{3,0},{4,7},{5,6},{6,5},{7,4},{8,11},{9,10},{10,... | collective-permute-start | bytes 49160 | tf_op jit(solution)/shard_map/ppermute | solution.py:637
  53.2 1.8 %collective-permute-start.9 = (f32[64,64]{1,0:T(8,128)S(1)}, f32[64,64]{1,0:T(8,128)S(1)}, u32[]{:S(2)}, u32[]{:S(2)}) collective-permute-start(f32[64,64]{1,0:T(8,128)S(1)} %add_terms.7.refs_2_.refs_0_), channel_id=1, source_target_pairs={{0,1},{1,0},{2,3},{3,2},{4,5},{5,4},{6,7},{7,6},{8,9},{9,8},{10,11... | collective-permute-start | bytes 49160 | tf_op jit(solution)/shard_map/ppermute | solution.py:637
  56.3 1.9 %collective-permute-done.14.refs_0_ = bf16[8,64,256]{2,1,0:T(8,128)(2,1)S(1)} collective-permute-done((bf16[8,64,256]{2,1,0:T(8,128)(2,1)S(1)}, bf16[8,64,256]{2,1,0:T(8,128)(2,1)S(1)}, u32[]{:S(2)}, u32[]{:S(2)}) %collective-permute-start.14) | collective-permute-done | bytes 262176 | tf_op jit(solution)/shard_map/ppermute | solution.py:637
  62.3 2.4 %collective-permute-start.16 = (f32[64,512]{1,0:T(8,128)S(1)}, f32[64,512]{1,0:T(8,128)S(1)}, u32[]{:S(2)}, u32[]{:S(2)}) collective-permute-start(f32[64,512]{1,0:T(8,128)S(1)} %add_terms.8.a_ref), channel_id=1, source_target_pairs={{0,8},{4,12},{8,0},{12,4},{1,9},{5,13},{9,1},{13,5},{2,10},{6,14},... | collective-permute-start | bytes 393224 | tf_op jit(solution)/shard_map/ppermute | solution.py:637
  64.6 1.7 %second_inverse.1 = (f32[64,64]{1,0:T(8,128)S(1)}, f32[64,64]{1,0:T(8,128)S(1)}) custom-call(f32[64,64]{1,0:T(8,128)S(1)} %get-tuple-element.73.h_ref, f32[64,64]{1,0:T(8,128)S(1)} %get-tuple-element.74.w_gram_ref), custom_call_target="tpu_custom_call" | custom-call | flops 1000 | bytes 1000 | tf_op jit(solution)/shard_map/second_inverse/pallas_call | solution.py:511
  66.3 2.1 %collective-permute-done.16.b_ref = f32[64,512]{1,0:T(8,128)S(1)} collective-permute-done((f32[64,512]{1,0:T(8,128)S(1)}, f32[64,512]{1,0:T(8,128)S(1)}, u32[]{:S(2)}, u32[]{:S(2)}) %collective-permute-start.16) | collective-permute-done | bytes 131104 | tf_op jit(solution)/shard_map/ppermute | solution.py:637
  68.5 1.6 %next_v.2 = (f32[64,512]{1,0:T(8,128)S(1)}, f32[64,128]{1,0:T(8,128)S(1)}) custom-call(s32[1]{0:T(128)} %bitcast.place, f32[64,512]{1,0:T(8,128)S(1)} %add_terms.9.terms_ref, f32[64,64]{1,0:T(8,128)S(1)} %get-tuple-element.75.refs_0_.inverse_ref, f32[64,64]{1,0:T(8,128)S(1)} %get-tuple-element.73.h_ref, bf16[256,1024]{1,0:T(8,128)(2,1)S(1)} %get-tuple-element.61.refs_0_, ...), custom_call_target="tpu_custom_call" | custom-call | flops 1000 | bytes 1000 | tf_op jit(solution)/shard_map/next_v/pallas_call | solution.py:578
  70.1 1.6 %next_v.3 = (f32[64,512]{1,0:T(8,128)S(1)}, f32[64,128]{1,0:T(8,128)S(1)}) custom-call(s32[1]{0:T(128)} %bitcast.place, f32[64,512]{1,0:T(8,128)S(1)} %collective-permute-done.17.terms_ref, f32[64,64]{1,0:T(8,128)S(1)} %get-tuple-element.75.refs_0_.inverse_ref, f32[64,64]{1,0:T(8,128)S(1)} %get-tuple-element.73.h_ref, ...), custom_call_target="tpu_custom_call" | custom-call | flops 1000 | bytes 1000 | tf_op jit(solution)/shard_map/next_v/pallas_call | solution.py:578
  71.8 1.9 %collective-permute-start.20 = (f32[64,128]{1,0:T(8,128)S(1)}, f32[64,128]{1,0:T(8,128)S(1)}, u32[]{:S(2)}, u32[]{:S(2)}) collective-permute-start(f32[64,128]{1,0:T(8,128)S(1)} %get-tuple-element.80.refs_0_), channel_id=1, source_target_pairs={{0,3},{1,2},{2,1},{3,0},{4,7},{5,6},{6,5},{7,4},{8,11},{9,10},{10,... | collective-permute-start | bytes 98312 | tf_op jit(solution)/shard_map/ppermute | solution.py:637
  73.7 2.5 %collective-permute-start.18 = (f32[64,128]{1,0:T(8,128)S(1)}, f32[64,128]{1,0:T(8,128)S(1)}, u32[]{:S(2)}, u32[]{:S(2)}) collective-permute-start(f32[64,128]{1,0:T(8,128)S(1)} %get-tuple-element.80.refs_0_), channel_id=1, source_target_pairs={{0,1},{1,0},{2,3},{3,2},{4,5},{5,4},{6,7},{7,6},{8,9},{9,8},{10,11... | collective-permute-start | bytes 98312 | tf_op jit(solution)/shard_map/ppermute | solution.py:637
  78.8 2.3 %next_w.1 = f32[32,64]{1,0:T(8,128)} custom-call(f32[64,128]{1,0:T(8,128)S(1)} %get-tuple-element.80.refs_0_, f32[64,128]{1,0:T(8,128)S(1)} %collective-permute-done.18.refs_1_, f32[64,128]{1,0:T(8,128)S(1)} %collective-permute-done.19.refs_2_, f32[64,128]{1,0:T(8,128)S(1)} %collective-permute-done.20.refs_3_, f32[64,64]{1,0:T(8,128)S(1)} %get-tuple-element.81.refs_4_, ...), custom_call_target="tpu_custom_call" | custom-call | flops 1000 | bytes 1000 | tf_op jit(solution)/shard_map/next_w/pallas_call | solution.py:624
  (56 shorter events, 21.6 us)
Async XLA Ops:
  0.7 11.8 %copy-start.2 = (f32[32,64]{1,0:T(8,128)S(1)}, f32[32,64]{1,0:T(8,128)}, u32[]{:S(2)}) copy-start(f32[32,64]{1,0:T(8,128)} %w_ref.5) | copy-start | bytes 24580
  4.4 10.2 %collective-permute-start = (s16[528,256]{1,0:T(8,128)(2,1)S(1)}, s16[528,256]{1,0:T(8,128)(2,1)S(1)}, u32[]{:S(2)}, u32[]{:S(2)}) collective-permute-start(s16[528,256]{1,0:T(8,128)(2,1)S(1)} %project_first.1), channel_id=1, source_target_pairs={{0,1},{1,0},{2,3},{3,2},{4,5},{5,4},{6,7},{7,6},{8,9},{9,8},{10,11... | collective-permute-start | bytes 811016 | tf_op jit(solution)/shard_map/ppermute | solution.py:637
  9.4 13.6 %collective-permute-start.3 = (s16[560,256]{1,0:T(8,128)(2,1)S(1)}, s16[560,256]{1,0:T(8,128)(2,1)S(1)}, u32[]{:S(2)}, u32[]{:S(2)}) collective-permute-start(s16[560,256]{1,0:T(8,128)(2,1)S(1)} %project_next.4), channel_id=1, source_target_pairs={{0,1},{1,0},{2,3},{3,2},{4,5},{5,4},{6,7},{7,6},{8,9},{9,8},{10,11... | collective-permute-start | bytes 860168 | tf_op jit(solution)/shard_map/ppermute | solution.py:637
  13.3 1.3 %collective-permute-start.1 = (f32[64,64]{1,0:T(8,128)S(1)}, f32[64,64]{1,0:T(8,128)S(1)}, u32[]{:S(2)}, u32[]{:S(2)}) collective-permute-start(f32[64,64]{1,0:T(8,128)S(1)} %get-tuple-element.45.a_ref), channel_id=1, source_target_pairs={{0,4},{4,0},{8,12},{12,8},{1,5},{5,1},{9,13},{13,9},{2,6},{6,2},{1... | collective-permute-start | bytes 49160 | tf_op jit(solution)/shard_map/ppermute | solution.py:637
  15.5 9.4 %copy-start.3 = (f32[64,64]{1,0:T(8,128)S(1)}, f32[64,64]{1,0:T(8,128)}, u32[]{:S(2)}) copy-start(f32[64,64]{1,0:T(8,128)} %h_ref.3) | copy-start | bytes 49156
  15.6 9.4 %copy-start.4 = (s32[32]{0:T(128)S(1)}, s32[32]{0:T(128)}, u32[]{:S(2)}) copy-start(s32[32]{0:T(128)} %counts_ref.3) | copy-start | bytes 388
  15.6 9.4 %collective-permute-start.2 = (s16[272,256]{1,0:T(8,128)(2,1)S(1)}, s16[272,256]{1,0:T(8,128)(2,1)S(1)}, u32[]{:S(2)}, u32[]{:S(2)}) collective-permute-start(s16[272,256]{1,0:T(8,128)(2,1)S(1)} %project_next.3), channel_id=1, source_target_pairs={{0,2},{1,3},{2,0},{3,1},{4,6},{5,7},{6,4},{7,5},{8,10},{9,11},{10,... | collective-permute-start | bytes 417800 | tf_op jit(solution)/shard_map/ppermute | solution.py:637
  18.8 3.9 %collective-permute-start.4 = (f32[64,64]{1,0:T(8,128)S(1)}, f32[64,64]{1,0:T(8,128)S(1)}, u32[]{:S(2)}, u32[]{:S(2)}) collective-permute-start(f32[64,64]{1,0:T(8,128)S(1)} %add_terms.5.refs_1_.refs_0_), channel_id=1, source_target_pairs={{0,8},{4,12},{8,0},{12,4},{1,9},{5,13},{9,1},{13,5},{2,10},{6,14},... | collective-permute-start | bytes 49160 | tf_op jit(solution)/shard_map/ppermute | solution.py:637
  24.0 9.0 %collective-permute-start.5 = (s16[304,256]{1,0:T(8,128)(2,1)S(1)}, s16[304,256]{1,0:T(8,128)(2,1)S(1)}, u32[]{:S(2)}, u32[]{:S(2)}) collective-permute-start(s16[304,256]{1,0:T(8,128)(2,1)S(1)} %project_next.5), channel_id=1, source_target_pairs={{0,2},{1,3},{2,0},{3,1},{4,6},{5,7},{6,4},{7,5},{8,10},{9,11},{10,... | collective-permute-start | bytes 466952 | tf_op jit(solution)/shard_map/ppermute | solution.py:637
  30.9 8.5 %collective-permute-start.7 = (bf16[4,64,256]{2,1,0:T(8,128)(2,1)S(1)}, bf16[4,64,256]{2,1,0:T(8,128)(2,1)S(1)}, u32[]{:S(2)}, u32[]{:S(2)}) collective-permute-start(bf16[4,64,256]{2,1,0:T(8,128)(2,1)S(1)} %get-tuple-element.50.refs_0_), channel_id=1, source_target_pairs={{0,2},{1,3},{2,0},{3,1},{4,6},{5,7},{6,4},{7,5},{8,10},{9,11},{10,... | collective-permute-start | bytes 393224 | tf_op jit(solution)/shard_map/ppermute | solution.py:637
  39.5 10.1 %collective-permute-start.13 = (bf16[8,64,256]{2,1,0:T(8,128)(2,1)S(1)}, bf16[8,64,256]{2,1,0:T(8,128)(2,1)S(1)}, u32[]{:S(2)}, u32[]{:S(2)}) collective-permute-start(bf16[8,64,256]{2,1,0:T(8,128)(2,1)S(1)} %join_frames.2.refs_3_), channel_id=1, source_target_pairs={{0,1},{1,0},{2,3},{3,2},{4,5},{5,4},{6,7},{7,6},{8,9},{9,8},{10,11... | collective-permute-start | bytes 786440 | tf_op jit(solution)/shard_map/ppermute | solution.py:637
  40.6 7.1 %collective-permute-start.12 = (bf16[4,64,256]{2,1,0:T(8,128)(2,1)S(1)}, bf16[4,64,256]{2,1,0:T(8,128)(2,1)S(1)}, u32[]{:S(2)}, u32[]{:S(2)}) collective-permute-start(bf16[4,64,256]{2,1,0:T(8,128)(2,1)S(1)} %get-tuple-element.51.refs_2_.refs_1_.refs_0_), channel_id=1, source_target_pairs={{0,2},{1,3},{2,0},{3,1},{4,6},{5,7},{6,4},{7,5},{8,10},{9,11},{10,... | collective-permute-start | bytes 393224 | tf_op jit(solution)/shard_map/ppermute | solution.py:637
  42.3 1.3 %collective-permute-start.6 = (f32[64,64]{1,0:T(8,128)S(1)}, f32[64,64]{1,0:T(8,128)S(1)}, u32[]{:S(2)}, u32[]{:S(2)}) collective-permute-start(f32[64,64]{1,0:T(8,128)S(1)} %get-tuple-element.49.a_ref), channel_id=1, source_target_pairs={{0,4},{4,0},{8,12},{12,8},{1,5},{5,1},{9,13},{13,9},{2,6},{6,2},{1... | collective-permute-start | bytes 49160 | tf_op jit(solution)/shard_map/ppermute | solution.py:637
  43.6 4.0 %collective-permute-start.8 = (f32[64,64]{1,0:T(8,128)S(1)}, f32[64,64]{1,0:T(8,128)S(1)}, u32[]{:S(2)}, u32[]{:S(2)}) collective-permute-start(f32[64,64]{1,0:T(8,128)S(1)} %add_terms.6.refs_2_.a_ref), channel_id=1, source_target_pairs={{0,8},{4,12},{8,0},{12,4},{1,9},{5,13},{9,1},{13,5},{2,10},{6,14},... | collective-permute-start | bytes 49160 | tf_op jit(solution)/shard_map/ppermute | solution.py:637
  49.6 8.7 %collective-permute-start.14 = (bf16[8,64,256]{2,1,0:T(8,128)(2,1)S(1)}, bf16[8,64,256]{2,1,0:T(8,128)(2,1)S(1)}, u32[]{:S(2)}, u32[]{:S(2)}) collective-permute-start(bf16[8,64,256]{2,1,0:T(8,128)(2,1)S(1)} %join_frames.3.refs_1_), channel_id=1, source_target_pairs={{0,1},{1,0},{2,3},{3,2},{4,5},{5,4},{6,7},{7,6},{8,9},{9,8},{10,11... | collective-permute-start | bytes 786440 | tf_op jit(solution)/shard_map/ppermute | solution.py:637
  50.6 8.6 %collective-permute-start.11 = (f32[64,64]{1,0:T(8,128)S(1)}, f32[64,64]{1,0:T(8,128)S(1)}, u32[]{:S(2)}, u32[]{:S(2)}) collective-permute-start(f32[64,64]{1,0:T(8,128)S(1)} %add_terms.7.refs_2_.refs_0_), channel_id=1, source_target_pairs={{0,3},{1,2},{2,1},{3,0},{4,7},{5,6},{6,5},{7,4},{8,11},{9,10},{10,... | collective-permute-start | bytes 49160 | tf_op jit(solution)/shard_map/ppermute | solution.py:637
  52.3 6.8 %collective-permute-start.10 = (f32[64,64]{1,0:T(8,128)S(1)}, f32[64,64]{1,0:T(8,128)S(1)}, u32[]{:S(2)}, u32[]{:S(2)}) collective-permute-start(f32[64,64]{1,0:T(8,128)S(1)} %add_terms.7.refs_2_.refs_0_), channel_id=1, source_target_pairs={{0,2},{1,3},{2,0},{3,1},{4,6},{5,7},{6,4},{7,5},{8,10},{9,11},{10,... | collective-permute-start | bytes 49160 | tf_op jit(solution)/shard_map/ppermute | solution.py:637
  53.2 6.0 %collective-permute-start.9 = (f32[64,64]{1,0:T(8,128)S(1)}, f32[64,64]{1,0:T(8,128)S(1)}, u32[]{:S(2)}, u32[]{:S(2)}) collective-permute-start(f32[64,64]{1,0:T(8,128)S(1)} %add_terms.7.refs_2_.refs_0_), channel_id=1, source_target_pairs={{0,1},{1,0},{2,3},{3,2},{4,5},{5,4},{6,7},{7,6},{8,9},{9,8},{10,11... | collective-permute-start | bytes 49160 | tf_op jit(solution)/shard_map/ppermute | solution.py:637
  60.8 1.4 %collective-permute-start.15 = (f32[64,512]{1,0:T(8,128)S(1)}, f32[64,512]{1,0:T(8,128)S(1)}, u32[]{:S(2)}, u32[]{:S(2)}) collective-permute-start(f32[64,512]{1,0:T(8,128)S(1)} %v_terms.2.refs_12_), channel_id=1, source_target_pairs={{0,4},{4,0},{8,12},{12,8},{1,5},{5,1},{9,13},{13,9},{2,6},{6,2},{1... | collective-permute-start | bytes 393224 | tf_op jit(solution)/shard_map/ppermute | solution.py:637
  62.3 6.2 %collective-permute-start.16 = (f32[64,512]{1,0:T(8,128)S(1)}, f32[64,512]{1,0:T(8,128)S(1)}, u32[]{:S(2)}, u32[]{:S(2)}) collective-permute-start(f32[64,512]{1,0:T(8,128)S(1)} %add_terms.8.a_ref), channel_id=1, source_target_pairs={{0,8},{4,12},{8,0},{12,4},{1,9},{5,13},{9,1},{13,5},{2,10},{6,14},... | collective-permute-start | bytes 393224 | tf_op jit(solution)/shard_map/ppermute | solution.py:637
  68.5 1.7 %collective-permute-start.17 = (f32[64,512]{1,0:T(8,128)S(1)}, f32[64,512]{1,0:T(8,128)S(1)}, u32[]{:S(2)}, u32[]{:S(2)}) collective-permute-start(f32[64,512]{1,0:T(8,128)S(1)} %add_terms.9.terms_ref), channel_id=1, source_target_pairs={{0,4},{4,0},{8,12},{12,8},{1,5},{5,1},{9,13},{13,9},{2,6},{6,2},{1... | collective-permute-start | bytes 393224 | tf_op jit(solution)/shard_map/ppermute | solution.py:637
  71.8 6.0 %collective-permute-start.20 = (f32[64,128]{1,0:T(8,128)S(1)}, f32[64,128]{1,0:T(8,128)S(1)}, u32[]{:S(2)}, u32[]{:S(2)}) collective-permute-start(f32[64,128]{1,0:T(8,128)S(1)} %get-tuple-element.80.refs_0_), channel_id=1, source_target_pairs={{0,3},{1,2},{2,1},{3,0},{4,7},{5,6},{6,5},{7,4},{8,11},{9,10},{10,... | collective-permute-start | bytes 98312 | tf_op jit(solution)/shard_map/ppermute | solution.py:637
  73.6 5.1 %collective-permute-start.19 = (f32[64,128]{1,0:T(8,128)S(1)}, f32[64,128]{1,0:T(8,128)S(1)}, u32[]{:S(2)}, u32[]{:S(2)}) collective-permute-start(f32[64,128]{1,0:T(8,128)S(1)} %get-tuple-element.80.refs_0_), channel_id=1, source_target_pairs={{0,2},{1,3},{2,0},{3,1},{4,6},{5,7},{6,4},{7,5},{8,10},{9,11},{10,... | collective-permute-start | bytes 98312 | tf_op jit(solution)/shard_map/ppermute | solution.py:637
  73.7 5.1 %collective-permute-start.18 = (f32[64,128]{1,0:T(8,128)S(1)}, f32[64,128]{1,0:T(8,128)S(1)}, u32[]{:S(2)}, u32[]{:S(2)}) collective-permute-start(f32[64,128]{1,0:T(8,128)S(1)} %get-tuple-element.80.refs_0_), channel_id=1, source_target_pairs={{0,1},{1,0},{2,3},{3,2},{4,5},{5,4},{6,7},{7,6},{8,9},{9,8},{10,11... | collective-permute-start | bytes 98312 | tf_op jit(solution)/shard_map/ppermute | solution.py:637
  (2 other events, 13.9 us)

commit v23 on v19

--- a/solution.py
+++ b/solution.py
@@ -333,12 +333,11 @@
 def sweep_all(frames, rank, fine):
     patients = range(frames.shape[0])
     if fine:
-        both = [jnp.concatenate(two_parts(frames[p]), axis=0) for p in patients]
-        blocks = [low_dot(x, x, ROWS_BY_ROWS) for x in both]
-        blocks = [x[:rank] + x[rank:] for x in blocks]
-        grams = [x + pltpu.roll(x, rank, 1) for x in blocks]
-        moved = [low_dot(jnp.concatenate(two_parts(g), axis=0), x) for g, x in zip(grams, both)]
-        moved = [x[:rank] + x[rank:] for x in moved]
+        parts = [two_parts(frames[p]) for p in patients]
+        both = [jnp.concatenate(x, axis=0) for x in parts]
+        blocks = [low_dot(x, y, ROWS_BY_ROWS) + low_dot(z, y, ROWS_BY_ROWS) for (x, z), y in zip(parts, both)]
+        grams = [two_parts(x + pltpu.roll(x, rank, 1)) for x in blocks]
+        moved = [low_dot(x, y) + low_dot(z, y) for (x, z), y in zip(grams, both)]
     else:
         first = [frames[p].astype(BF16) for p in patients]
         grams = [low_dot(x, x, ROWS_BY_ROWS).astype(BF16) for x in first]

time: 81.1 us -> 81.8 us (level)
  Pallas kernels: 37.7 us -> 38.6 us
  transfers between devices with their start and end apart: 21 -> 21, of which waited for: 11 -> 11; matrix products, arithmetic and copies ran while one was open for 0% -> 0% of each run, Pallas kernels for 34% -> 35%
where the time goes in v23:
time: 81.8 us; the launch traced here: 81.7 us
  Pallas kernels  38.6 us (47%)
  starting transfers between devices  28.8 us (35%)
  waiting for transfers between devices  13.4 us (16%)
  between operations  0.85 us (1%)
    ppermute x21, starting transfers between devices, swap(): return lax.ppermute(x, axis, pairs)  28.8 us
    ppermute x21, waiting for transfers between devices, swap(): return lax.ppermute(x, axis, pairs)  13.4 us
    pallas_call x2, Pallas kernels, own_frames(): pl.pallas_call(functools.partial(frames_kernel, layouts, part, share), in...  12.7 us
    pallas_call x1, Pallas kernels, first_projection(): pl.pallas_call(functools.partial(first_projection_kernel, slots, with_gra...  4.37 us
    pallas_call x4, Pallas kernels, project_frames(): pl.pallas_call(functools.partial(projected_kernel, items), in_specs=[SMEM...  3.67 us
    pallas_call x3, Pallas kernels, next_projection(): pl.pallas_call(functools.partial(next_projection_kernel, slots, first, co...  3.56 us
    pallas_call x2, Pallas kernels, half_v(): pl.pallas_call(functools.partial(next_v_kernel, items, share, bool(before...  3.24 us
    pallas_call x1, Pallas kernels, next_w(): pl.pallas_call(functools.partial(next_w_kernel, len(sums)), in_specs=[VME...  2.27 us
  transfers between devices with their start and end apart: 21, of which 11 were waited for; matrix products, arithmetic and copies ran while one was open for 0% of the time, Pallas kernels for 35%

profile of v23, /device:TPU:0, one launch (start us, length us, event | category | flops | bytes accessed | tf_op | source)
XLA Modules:
  0.0 81.7 jit_solution(2627677436227401012)
XLA Ops:
  0.7 4.4 %project_first.1 = s16[528,256]{1,0:T(8,128)(2,1)S(1)} custom-call(s32[1]{0:T(128)} %bitcast.place, bf16[64,1024]{1,0:T(8,128)(2,1)} %bitcast.13, bf16[4,8,256,1024]{3,2,1,0:T(8,128)(2,1)} %bitcast.4), custom_call_target="tpu_custom_call" | custom-call | flops 1000 | bytes 1000 | tf_op jit(solution)/shard_map/project_first/pallas_call | solution.py:161
  5.0 3.1 %collective-permute-start = (s16[528,256]{1,0:T(8,128)(2,1)S(1)}, s16[528,256]{1,0:T(8,128)(2,1)S(1)}, u32[]{:S(2)}, u32[]{:S(2)}) collective-permute-start(s16[528,256]{1,0:T(8,128)(2,1)S(1)} %project_first.1), channel_id=1, source_target_pairs={{0,1},{1,0},{2,3},{3,2},{4,5},{5,4},{6,7},{7,6},{8,9},{9,8},{10,11... | collective-permute-start | bytes 811016 | tf_op jit(solution)/shard_map/ppermute | solution.py:626
  8.1 1.6 %project_next.4 = s16[560,256]{1,0:T(8,128)(2,1)S(1)} custom-call(s32[1]{0:T(128)} %bitcast.place, bf16[64,1024]{1,0:T(8,128)(2,1)S(1)} %bitcast.14, bf16[4,8,256,1024]{3,2,1,0:T(8,128)(2,1)S(1)} %bitcast.5), custom_call_target="tpu_custom_call" | custom-call | flops 1000 | bytes 1000 | tf_op jit(solution)/shard_map/project_next/pallas_call | solution.py:199
  9.8 2.7 %collective-permute-start.3 = (s16[560,256]{1,0:T(8,128)(2,1)S(1)}, s16[560,256]{1,0:T(8,128)(2,1)S(1)}, u32[]{:S(2)}, u32[]{:S(2)}) collective-permute-start(s16[560,256]{1,0:T(8,128)(2,1)S(1)} %project_next.4), channel_id=1, source_target_pairs={{0,1},{1,0},{2,3},{3,2},{4,5},{5,4},{6,7},{7,6},{8,9},{9,8},{10,11... | collective-permute-start | bytes 860168 | tf_op jit(solution)/shard_map/ppermute | solution.py:626
  16.4 3.1 %collective-permute-start.2 = (s16[272,256]{1,0:T(8,128)(2,1)S(1)}, s16[272,256]{1,0:T(8,128)(2,1)S(1)}, u32[]{:S(2)}, u32[]{:S(2)}) collective-permute-start(s16[272,256]{1,0:T(8,128)(2,1)S(1)} %project_next.3), channel_id=1, source_target_pairs={{0,2},{1,3},{2,0},{3,1},{4,6},{5,7},{6,4},{7,5},{8,10},{9,11},{10,... | collective-permute-start | bytes 417800 | tf_op jit(solution)/shard_map/ppermute | solution.py:626
  19.5 1.5 %collective-permute-start.4 = (f32[64,64]{1,0:T(8,128)S(1)}, f32[64,64]{1,0:T(8,128)S(1)}, u32[]{:S(2)}, u32[]{:S(2)}) collective-permute-start(f32[64,64]{1,0:T(8,128)S(1)} %add_terms.5.refs_1_.refs_0_), channel_id=1, source_target_pairs={{0,8},{4,12},{8,0},{12,4},{1,9},{5,13},{9,1},{13,5},{2,10},{6,14},... | collective-permute-start | bytes 49160 | tf_op jit(solution)/shard_map/ppermute | solution.py:626
  21.0 1.4 %project_own.1 = (f32[4,64,256]{2,1,0:T(8,128)S(1)}, f32[4,64,256]{2,1,0:T(8,128)S(1)}, f32[64,64]{1,0:T(8,128)S(1)}) custom-call(s32[1]{0:T(128)} %bitcast.place, bf16[64,1024]{1,0:T(8,128)(2,1)S(1)} %bitcast.16, bf16[4,8,256,1024]{3,2,1,0:T(8,128)(2,1)S(1)} %bitcast.7, s16[528,256]{1,0:T(8,128)(2,1)S(1)} %collective-permute-done.arrived_ref.refs_0_), custom_call_target="tpu_custom_call" | custom-call | flops 1000 | bytes 1000 | tf_op jit(solution)/shard_map/project_own/pallas_call | solution.py:254
  25.7 6.3 %own_frames.2 = (bf16[4,64,256]{2,1,0:T(8,128)(2,1)S(1)}, f32[64,64]{1,0:T(8,128)S(1)}, f32[64,64]{1,0:T(8,128)S(1)}) custom-call(s32[1]{0:T(128)} %bitcast.place, s32[32]{0:T(128)S(1)} %copy-done.4, f32[64,64]{1,0:T(8,128)S(1)} %copy-done.3, f32[32,64]{1,0:T(8,128)S(1)} %copy-done.2, f32[64,64]{1,0:T(8,128)S(1)} %get-tuple-element.43.v_gram_ref.before_ref.refs_2_, ...), custom_call_target="tpu_custom_call" | custom-call | flops 1000 | bytes 1000 | tf_op jit(solution)/shard_map/own_frames/pallas_call | solution.py:394
  32.1 2.1 %collective-permute-start.7 = (bf16[4,64,256]{2,1,0:T(8,128)(2,1)S(1)}, bf16[4,64,256]{2,1,0:T(8,128)(2,1)S(1)}, u32[]{:S(2)}, u32[]{:S(2)}) collective-permute-start(bf16[4,64,256]{2,1,0:T(8,128)(2,1)S(1)} %get-tuple-element.50.refs_0_), channel_id=1, source_target_pairs={{0,2},{1,3},{2,0},{3,1},{4,6},{5,7},{6,4},{7,5},{8,10},{9,11},{10,... | collective-permute-start | bytes 393224 | tf_op jit(solution)/shard_map/ppermute | solution.py:626
  34.1 6.3 %own_frames.3 = (bf16[4,64,256]{2,1,0:T(8,128)(2,1)S(1)}, f32[64,64]{1,0:T(8,128)S(1)}, f32[64,64]{1,0:T(8,128)S(1)}) custom-call(s32[1]{0:T(128)} %bitcast.place, s32[32]{0:T(128)S(1)} %copy-done.4, f32[64,64]{1,0:T(8,128)S(1)} %copy-done.3, f32[32,64]{1,0:T(8,128)S(1)} %copy-done.2, f32[64,64]{1,0:T(8,128)S(1)} %get-tuple-element.46.v_gram_ref, ...), custom_call_target="tpu_custom_call" | custom-call | flops 1000 | bytes 1000 | tf_op jit(solution)/shard_map/own_frames/pallas_call | solution.py:394
  40.5 1.5 %collective-permute-start.13 = (bf16[8,64,256]{2,1,0:T(8,128)(2,1)S(1)}, bf16[8,64,256]{2,1,0:T(8,128)(2,1)S(1)}, u32[]{:S(2)}, u32[]{:S(2)}) collective-permute-start(bf16[8,64,256]{2,1,0:T(8,128)(2,1)S(1)} %join_frames.2.refs_3_), channel_id=1, source_target_pairs={{0,1},{1,0},{2,3},{3,2},{4,5},{5,4},{6,7},{7,6},{8,9},{9,8},{10,11... | collective-permute-start | bytes 786440 | tf_op jit(solution)/shard_map/ppermute | solution.py:626
  42.0 1.7 %collective-permute-start.12 = (bf16[4,64,256]{2,1,0:T(8,128)(2,1)S(1)}, bf16[4,64,256]{2,1,0:T(8,128)(2,1)S(1)}, u32[]{:S(2)}, u32[]{:S(2)}) collective-permute-start(bf16[4,64,256]{2,1,0:T(8,128)(2,1)S(1)} %get-tuple-element.51.refs_2_.refs_1_.refs_0_), channel_id=1, source_target_pairs={{0,2},{1,3},{2,0},{3,1},{4,6},{5,7},{6,4},{7,5},{8,10},{9,11},{10,... | collective-permute-start | bytes 393224 | tf_op jit(solution)/shard_map/ppermute | solution.py:626
  43.7 1.4 %project_frames.4 = (bf16[256,1024]{1,0:T(8,128)(2,1)S(1)}, bf16[256,1024]{1,0:T(8,128)(2,1)S(1)}, bf16[256,1024]{1,0:T(8,128)(2,1)S(1)}, bf16[256,1024]{1,0:T(8...) custom-call(s32[1]{0:T(128)} %bitcast.place, ...), custom_call_target="tpu_custom_call" | custom-call | flops 1000 | bytes 1000 | tf_op jit(solution)/shard_map/project_frames/pallas_call | solution.py:451
  45.2 1.6 %collective-permute-start.8 = (f32[64,64]{1,0:T(8,128)S(1)}, f32[64,64]{1,0:T(8,128)S(1)}, u32[]{:S(2)}, u32[]{:S(2)}) collective-permute-start(f32[64,64]{1,0:T(8,128)S(1)} %add_terms.6.refs_2_.a_ref), channel_id=1, source_target_pairs={{0,8},{4,12},{8,0},{12,4},{1,9},{5,13},{9,1},{13,5},{2,10},{6,14},... | collective-permute-start | bytes 49160 | tf_op jit(solution)/shard_map/ppermute | solution.py:626
  46.7 1.6 %first_inverse.1 = (f32[64,64]{1,0:T(8,128)S(1)}, f32[64,64]{1,0:T(8,128)S(1)}) custom-call(f32[64,64]{1,0:T(8,128)S(1)} %get-tuple-element.53.v_gram_ref, f32[64,64]{1,0:T(8,128)S(1)} %add_terms.5.refs_1_.refs_0_, f32[64,64]{1,0:T(8,128)S(1)} %collective-permute-done.4.refs_1_, f32[64,64]{1,0:T(8,128)S(1)} %add_terms.6.refs_2_.a_ref), custom_call_target="tpu_custom_call" | custom-call | flops 1000 | bytes 1000 | tf_op jit(solution)/shard_map/first_inverse/pallas_call | solution.py:322
  51.2 1.9 %collective-permute-start.11 = (f32[64,64]{1,0:T(8,128)S(1)}, f32[64,64]{1,0:T(8,128)S(1)}, u32[]{:S(2)}, u32[]{:S(2)}) collective-permute-start(f32[64,64]{1,0:T(8,128)S(1)} %add_terms.7.refs_2_.refs_0_), channel_id=1, source_target_pairs={{0,3},{1,2},{2,1},{3,0},{4,7},{5,6},{6,5},{7,4},{8,11},{9,10},{10,... | collective-permute-start | bytes 49160 | tf_op jit(solution)/shard_map/ppermute | solution.py:626
  54.0 1.6 %collective-permute-start.9 = (f32[64,64]{1,0:T(8,128)S(1)}, f32[64,64]{1,0:T(8,128)S(1)}, u32[]{:S(2)}, u32[]{:S(2)}) collective-permute-start(f32[64,64]{1,0:T(8,128)S(1)} %add_terms.7.refs_2_.refs_0_), channel_id=1, source_target_pairs={{0,1},{1,0},{2,3},{3,2},{4,5},{5,4},{6,7},{7,6},{8,9},{9,8},{10,11... | collective-permute-start | bytes 49160 | tf_op jit(solution)/shard_map/ppermute | solution.py:626
  57.0 2.4 %collective-permute-done.14.refs_0_ = bf16[8,64,256]{2,1,0:T(8,128)(2,1)S(1)} collective-permute-done((bf16[8,64,256]{2,1,0:T(8,128)(2,1)S(1)}, bf16[8,64,256]{2,1,0:T(8,128)(2,1)S(1)}, u32[]{:S(2)}, u32[]{:S(2)}) %collective-permute-start.14) | collective-permute-done | bytes 262176 | tf_op jit(solution)/shard_map/ppermute | solution.py:626
  64.1 1.7 %second_inverse.1 = (f32[64,64]{1,0:T(8,128)S(1)}, f32[64,64]{1,0:T(8,128)S(1)}) custom-call(f32[64,64]{1,0:T(8,128)S(1)} %get-tuple-element.73.h_ref, f32[64,64]{1,0:T(8,128)S(1)} %get-tuple-element.74.w_gram_ref), custom_call_target="tpu_custom_call" | custom-call | flops 1000 | bytes 1000 | tf_op jit(solution)/shard_map/second_inverse/pallas_call | solution.py:500
  65.8 3.2 %collective-permute-done.16.b_ref = f32[64,512]{1,0:T(8,128)S(1)} collective-permute-done((f32[64,512]{1,0:T(8,128)S(1)}, f32[64,512]{1,0:T(8,128)S(1)}, u32[]{:S(2)}, u32[]{:S(2)}) %collective-permute-start.16) | collective-permute-done | bytes 131104 | tf_op jit(solution)/shard_map/ppermute | solution.py:626
  69.1 1.6 %next_v.2 = (f32[64,512]{1,0:T(8,128)S(1)}, f32[64,128]{1,0:T(8,128)S(1)}) custom-call(s32[1]{0:T(128)} %bitcast.place, f32[64,512]{1,0:T(8,128)S(1)} %add_terms.9.terms_ref, f32[64,64]{1,0:T(8,128)S(1)} %get-tuple-element.75.refs_0_.inverse_ref, f32[64,64]{1,0:T(8,128)S(1)} %get-tuple-element.73.h_ref, bf16[256,1024]{1,0:T(8,128)(2,1)S(1)} %get-tuple-element.61.refs_0_, ...), custom_call_target="tpu_custom_call" | custom-call | flops 1000 | bytes 1000 | tf_op jit(solution)/shard_map/next_v/pallas_call | solution.py:567
  70.7 1.6 %next_v.3 = (f32[64,512]{1,0:T(8,128)S(1)}, f32[64,128]{1,0:T(8,128)S(1)}) custom-call(s32[1]{0:T(128)} %bitcast.place, f32[64,512]{1,0:T(8,128)S(1)} %collective-permute-done.17.terms_ref, f32[64,64]{1,0:T(8,128)S(1)} %get-tuple-element.75.refs_0_.inverse_ref, f32[64,64]{1,0:T(8,128)S(1)} %get-tuple-element.73.h_ref, ...), custom_call_target="tpu_custom_call" | custom-call | flops 1000 | bytes 1000 | tf_op jit(solution)/shard_map/next_v/pallas_call | solution.py:567
  73.6 3.1 %collective-permute-start.18 = (f32[64,128]{1,0:T(8,128)S(1)}, f32[64,128]{1,0:T(8,128)S(1)}, u32[]{:S(2)}, u32[]{:S(2)}) collective-permute-start(f32[64,128]{1,0:T(8,128)S(1)} %get-tuple-element.80.refs_0_), channel_id=1, source_target_pairs={{0,1},{1,0},{2,3},{3,2},{4,5},{5,4},{6,7},{7,6},{8,9},{9,8},{10,11... | collective-permute-start | bytes 98312 | tf_op jit(solution)/shard_map/ppermute | solution.py:626
  79.4 2.3 %next_w.1 = f32[32,64]{1,0:T(8,128)} custom-call(f32[64,128]{1,0:T(8,128)S(1)} %get-tuple-element.80.refs_0_, f32[64,128]{1,0:T(8,128)S(1)} %collective-permute-done.18.refs_1_, f32[64,128]{1,0:T(8,128)S(1)} %collective-permute-done.19.refs_2_, f32[64,128]{1,0:T(8,128)S(1)} %collective-permute-done.20.refs_3_, f32[64,64]{1,0:T(8,128)S(1)} %get-tuple-element.81.refs_4_, ...), custom_call_target="tpu_custom_call" | custom-call | flops 1000 | bytes 1000 | tf_op jit(solution)/shard_map/next_w/pallas_call | solution.py:613
  (56 shorter events, 20.9 us)
Async XLA Ops:
  0.7 11.8 %copy-start.2 = (f32[32,64]{1,0:T(8,128)S(1)}, f32[32,64]{1,0:T(8,128)}, u32[]{:S(2)}) copy-start(f32[32,64]{1,0:T(8,128)} %w_ref.5) | copy-start | bytes 24580
  5.0 10.4 %collective-permute-start = (s16[528,256]{1,0:T(8,128)(2,1)S(1)}, s16[528,256]{1,0:T(8,128)(2,1)S(1)}, u32[]{:S(2)}, u32[]{:S(2)}) collective-permute-start(s16[528,256]{1,0:T(8,128)(2,1)S(1)} %project_first.1), channel_id=1, source_target_pairs={{0,1},{1,0},{2,3},{3,2},{4,5},{5,4},{6,7},{7,6},{8,9},{9,8},{10,11... | collective-permute-start | bytes 811016 | tf_op jit(solution)/shard_map/ppermute | solution.py:626
  9.8 14.0 %collective-permute-start.3 = (s16[560,256]{1,0:T(8,128)(2,1)S(1)}, s16[560,256]{1,0:T(8,128)(2,1)S(1)}, u32[]{:S(2)}, u32[]{:S(2)}) collective-permute-start(s16[560,256]{1,0:T(8,128)(2,1)S(1)} %project_next.4), channel_id=1, source_target_pairs={{0,1},{1,0},{2,3},{3,2},{4,5},{5,4},{6,7},{7,6},{8,9},{9,8},{10,11... | collective-permute-start | bytes 860168 | tf_op jit(solution)/shard_map/ppermute | solution.py:626
  13.3 1.3 %collective-permute-start.1 = (f32[64,64]{1,0:T(8,128)S(1)}, f32[64,64]{1,0:T(8,128)S(1)}, u32[]{:S(2)}, u32[]{:S(2)}) collective-permute-start(f32[64,64]{1,0:T(8,128)S(1)} %get-tuple-element.45.a_ref), channel_id=1, source_target_pairs={{0,4},{4,0},{8,12},{12,8},{1,5},{5,1},{9,13},{13,9},{2,6},{6,2},{1... | collective-permute-start | bytes 49160 | tf_op jit(solution)/shard_map/ppermute | solution.py:626
  16.4 9.3 %copy-start.3 = (f32[64,64]{1,0:T(8,128)S(1)}, f32[64,64]{1,0:T(8,128)}, u32[]{:S(2)}) copy-start(f32[64,64]{1,0:T(8,128)} %h_ref.3) | copy-start | bytes 49156
  16.4 9.3 %copy-start.4 = (s32[32]{0:T(128)S(1)}, s32[32]{0:T(128)}, u32[]{:S(2)}) copy-start(s32[32]{0:T(128)} %counts_ref.3) | copy-start | bytes 388
  16.4 9.3 %collective-permute-start.2 = (s16[272,256]{1,0:T(8,128)(2,1)S(1)}, s16[272,256]{1,0:T(8,128)(2,1)S(1)}, u32[]{:S(2)}, u32[]{:S(2)}) collective-permute-start(s16[272,256]{1,0:T(8,128)(2,1)S(1)} %project_next.3), channel_id=1, source_target_pairs={{0,2},{1,3},{2,0},{3,1},{4,6},{5,7},{6,4},{7,5},{8,10},{9,11},{10,... | collective-permute-start | bytes 417800 | tf_op jit(solution)/shard_map/ppermute | solution.py:626
  19.5 3.9 %collective-permute-start.4 = (f32[64,64]{1,0:T(8,128)S(1)}, f32[64,64]{1,0:T(8,128)S(1)}, u32[]{:S(2)}, u32[]{:S(2)}) collective-permute-start(f32[64,64]{1,0:T(8,128)S(1)} %add_terms.5.refs_1_.refs_0_), channel_id=1, source_target_pairs={{0,8},{4,12},{8,0},{12,4},{1,9},{5,13},{9,1},{13,5},{2,10},{6,14},... | collective-permute-start | bytes 49160 | tf_op jit(solution)/shard_map/ppermute | solution.py:626
  24.7 9.4 %collective-permute-start.5 = (s16[304,256]{1,0:T(8,128)(2,1)S(1)}, s16[304,256]{1,0:T(8,128)(2,1)S(1)}, u32[]{:S(2)}, u32[]{:S(2)}) collective-permute-start(s16[304,256]{1,0:T(8,128)(2,1)S(1)} %project_next.5), channel_id=1, source_target_pairs={{0,2},{1,3},{2,0},{3,1},{4,6},{5,7},{6,4},{7,5},{8,10},{9,11},{10,... | collective-permute-start | bytes 466952 | tf_op jit(solution)/shard_map/ppermute | solution.py:626
  32.1 8.4 %collective-permute-start.7 = (bf16[4,64,256]{2,1,0:T(8,128)(2,1)S(1)}, bf16[4,64,256]{2,1,0:T(8,128)(2,1)S(1)}, u32[]{:S(2)}, u32[]{:S(2)}) collective-permute-start(bf16[4,64,256]{2,1,0:T(8,128)(2,1)S(1)} %get-tuple-element.50.refs_0_), channel_id=1, source_target_pairs={{0,2},{1,3},{2,0},{3,1},{4,6},{5,7},{6,4},{7,5},{8,10},{9,11},{10,... | collective-permute-start | bytes 393224 | tf_op jit(solution)/shard_map/ppermute | solution.py:626
  40.5 9.9 %collective-permute-start.13 = (bf16[8,64,256]{2,1,0:T(8,128)(2,1)S(1)}, bf16[8,64,256]{2,1,0:T(8,128)(2,1)S(1)}, u32[]{:S(2)}, u32[]{:S(2)}) collective-permute-start(bf16[8,64,256]{2,1,0:T(8,128)(2,1)S(1)} %join_frames.2.refs_3_), channel_id=1, source_target_pairs={{0,1},{1,0},{2,3},{3,2},{4,5},{5,4},{6,7},{7,6},{8,9},{9,8},{10,11... | collective-permute-start | bytes 786440 | tf_op jit(solution)/shard_map/ppermute | solution.py:626
  42.0 7.2 %collective-permute-start.12 = (bf16[4,64,256]{2,1,0:T(8,128)(2,1)S(1)}, bf16[4,64,256]{2,1,0:T(8,128)(2,1)S(1)}, u32[]{:S(2)}, u32[]{:S(2)}) collective-permute-start(bf16[4,64,256]{2,1,0:T(8,128)(2,1)S(1)} %get-tuple-element.51.refs_2_.refs_1_.refs_0_), channel_id=1, source_target_pairs={{0,2},{1,3},{2,0},{3,1},{4,6},{5,7},{6,4},{7,5},{8,10},{9,11},{10,... | collective-permute-start | bytes 393224 | tf_op jit(solution)/shard_map/ppermute | solution.py:626
  43.7 1.4 %collective-permute-start.6 = (f32[64,64]{1,0:T(8,128)S(1)}, f32[64,64]{1,0:T(8,128)S(1)}, u32[]{:S(2)}, u32[]{:S(2)}) collective-permute-start(f32[64,64]{1,0:T(8,128)S(1)} %get-tuple-element.49.a_ref), channel_id=1, source_target_pairs={{0,4},{4,0},{8,12},{12,8},{1,5},{5,1},{9,13},{13,9},{2,6},{6,2},{1... | collective-permute-start | bytes 49160 | tf_op jit(solution)/shard_map/ppermute | solution.py:626
  45.2 4.0 %collective-permute-start.8 = (f32[64,64]{1,0:T(8,128)S(1)}, f32[64,64]{1,0:T(8,128)S(1)}, u32[]{:S(2)}, u32[]{:S(2)}) collective-permute-start(f32[64,64]{1,0:T(8,128)S(1)} %add_terms.6.refs_2_.a_ref), channel_id=1, source_target_pairs={{0,8},{4,12},{8,0},{12,4},{1,9},{5,13},{9,1},{13,5},{2,10},{6,14},... | collective-permute-start | bytes 49160 | tf_op jit(solution)/shard_map/ppermute | solution.py:626
  50.4 9.0 %collective-permute-start.14 = (bf16[8,64,256]{2,1,0:T(8,128)(2,1)S(1)}, bf16[8,64,256]{2,1,0:T(8,128)(2,1)S(1)}, u32[]{:S(2)}, u32[]{:S(2)}) collective-permute-start(bf16[8,64,256]{2,1,0:T(8,128)(2,1)S(1)} %join_frames.3.refs_1_), channel_id=1, source_target_pairs={{0,1},{1,0},{2,3},{3,2},{4,5},{5,4},{6,7},{7,6},{8,9},{9,8},{10,11... | collective-permute-start | bytes 786440 | tf_op jit(solution)/shard_map/ppermute | solution.py:626
  51.2 9.1 %collective-permute-start.11 = (f32[64,64]{1,0:T(8,128)S(1)}, f32[64,64]{1,0:T(8,128)S(1)}, u32[]{:S(2)}, u32[]{:S(2)}) collective-permute-start(f32[64,64]{1,0:T(8,128)S(1)} %add_terms.7.refs_2_.refs_0_), channel_id=1, source_target_pairs={{0,3},{1,2},{2,1},{3,0},{4,7},{5,6},{6,5},{7,4},{8,11},{9,10},{10,... | collective-permute-start | bytes 49160 | tf_op jit(solution)/shard_map/ppermute | solution.py:626
  53.1 7.2 %collective-permute-start.10 = (f32[64,64]{1,0:T(8,128)S(1)}, f32[64,64]{1,0:T(8,128)S(1)}, u32[]{:S(2)}, u32[]{:S(2)}) collective-permute-start(f32[64,64]{1,0:T(8,128)S(1)} %add_terms.7.refs_2_.refs_0_), channel_id=1, source_target_pairs={{0,2},{1,3},{2,0},{3,1},{4,6},{5,7},{6,4},{7,5},{8,10},{9,11},{10,... | collective-permute-start | bytes 49160 | tf_op jit(solution)/shard_map/ppermute | solution.py:626
  54.0 6.4 %collective-permute-start.9 = (f32[64,64]{1,0:T(8,128)S(1)}, f32[64,64]{1,0:T(8,128)S(1)}, u32[]{:S(2)}, u32[]{:S(2)}) collective-permute-start(f32[64,64]{1,0:T(8,128)S(1)} %add_terms.7.refs_2_.refs_0_), channel_id=1, source_target_pairs={{0,1},{1,0},{2,3},{3,2},{4,5},{5,4},{6,7},{7,6},{8,9},{9,8},{10,11... | collective-permute-start | bytes 49160 | tf_op jit(solution)/shard_map/ppermute | solution.py:626
  62.0 1.4 %collective-permute-start.15 = (f32[64,512]{1,0:T(8,128)S(1)}, f32[64,512]{1,0:T(8,128)S(1)}, u32[]{:S(2)}, u32[]{:S(2)}) collective-permute-start(f32[64,512]{1,0:T(8,128)S(1)} %v_terms.2.refs_12_), channel_id=1, source_target_pairs={{0,4},{4,0},{8,12},{12,8},{1,5},{5,1},{9,13},{13,9},{2,6},{6,2},{1... | collective-permute-start | bytes 393224 | tf_op jit(solution)/shard_map/ppermute | solution.py:626
  63.4 5.6 %collective-permute-start.16 = (f32[64,512]{1,0:T(8,128)S(1)}, f32[64,512]{1,0:T(8,128)S(1)}, u32[]{:S(2)}, u32[]{:S(2)}) collective-permute-start(f32[64,512]{1,0:T(8,128)S(1)} %add_terms.8.a_ref), channel_id=1, source_target_pairs={{0,8},{4,12},{8,0},{12,4},{1,9},{5,13},{9,1},{13,5},{2,10},{6,14},... | collective-permute-start | bytes 393224 | tf_op jit(solution)/shard_map/ppermute | solution.py:626
  69.0 1.7 %collective-permute-start.17 = (f32[64,512]{1,0:T(8,128)S(1)}, f32[64,512]{1,0:T(8,128)S(1)}, u32[]{:S(2)}, u32[]{:S(2)}) collective-permute-start(f32[64,512]{1,0:T(8,128)S(1)} %add_terms.9.terms_ref), channel_id=1, source_target_pairs={{0,4},{4,0},{8,12},{12,8},{1,5},{5,1},{9,13},{13,9},{2,6},{6,2},{1... | collective-permute-start | bytes 393224 | tf_op jit(solution)/shard_map/ppermute | solution.py:626
  72.3 6.1 %collective-permute-start.20 = (f32[64,128]{1,0:T(8,128)S(1)}, f32[64,128]{1,0:T(8,128)S(1)}, u32[]{:S(2)}, u32[]{:S(2)}) collective-permute-start(f32[64,128]{1,0:T(8,128)S(1)} %get-tuple-element.80.refs_0_), channel_id=1, source_target_pairs={{0,3},{1,2},{2,1},{3,0},{4,7},{5,6},{6,5},{7,4},{8,11},{9,10},{10,... | collective-permute-start | bytes 98312 | tf_op jit(solution)/shard_map/ppermute | solution.py:626
  73.6 5.7 %collective-permute-start.19 = (f32[64,128]{1,0:T(8,128)S(1)}, f32[64,128]{1,0:T(8,128)S(1)}, u32[]{:S(2)}, u32[]{:S(2)}) collective-permute-start(f32[64,128]{1,0:T(8,128)S(1)} %get-tuple-element.80.refs_0_), channel_id=1, source_target_pairs={{0,2},{1,3},{2,0},{3,1},{4,6},{5,7},{6,4},{7,5},{8,10},{9,11},{10,... | collective-permute-start | bytes 98312 | tf_op jit(solution)/shard_map/ppermute | solution.py:626
  73.6 5.7 %collective-permute-start.18 = (f32[64,128]{1,0:T(8,128)S(1)}, f32[64,128]{1,0:T(8,128)S(1)}, u32[]{:S(2)}, u32[]{:S(2)}) collective-permute-start(f32[64,128]{1,0:T(8,128)S(1)} %get-tuple-element.80.refs_0_), channel_id=1, source_target_pairs={{0,1},{1,0},{2,3},{3,2},{4,5},{5,4},{6,7},{7,6},{8,9},{9,8},{10,11... | collective-permute-start | bytes 98312 | tf_op jit(solution)/shard_map/ppermute | solution.py:626
  (2 other events, 15.0 us)
